TPU v7x, 32 devices: a whole 2x2x4 slice. The times are simulated.
32 devices in a mesh: rep: 4 (over z), dom: 8 (over y, x, core).
Axes of the slice: x: 2, y: 2, z: 4, core: 2. Of those that a mesh axis runs over, the one named last changes fastest.
Arguments:
- cols: int32 [64, 8], P('dom', 'rep'), may hold values from 0 to 63, as said below
- vals: bfloat16 [64, 8, 128, 128], P('dom', 'rep')
- features: bfloat16 [8192, 128], P(('rep', 'dom')), may hold values from -6 to 6
- weight: bfloat16 [128, 128], replicated, may hold values from -0.5 to 0.5
- bias: float32 [128], replicated, may hold values from -3 to 3
- cotangent: bfloat16 [8192, 128], P('dom'), may hold values from -6 to 6
Outputs:
- output: bfloat16 [8192, 128], P('dom')
- feature_grad: float32 [8192, 128], P(('rep', 'dom'))
- weight_grad: float32 [128, 128], replicated
Inputs may be any that keep to these rules, and one draw needn't show every extreme that they name: For every block row and every quarter q of the block columns, entries q * 2 to (q + 1) * 2 - 1 of its row of cols are 2 distinct block columns in the range q * 16 to (q + 1) * 16 - 1 (quarters as many as the size of rep); every block row names its own diagonal block.
All inputs are finite; a program needn't handle non-finite values.
Results may differ from a plain program's by a relative error of at most 0.0055.
Values may be sent and summed in bfloat16 or wider, within the bound.
No kernel may reach another device: no remote copies, remote signals or barrier semaphores. Data moves between devices by JAX's collectives and lax.ppermute only.
A program may use at most 64 MiB of HBM per device.

v0:
```python
import jax
import jax.numpy as jnp
from jax import lax
from jax.sharding import PartitionSpec as P


def body(cols, vals, features, weight, bias, cotangent):
    row_blocks, block_count, block_size, _ = vals.shape
    width = features.shape[1]
    quarter_blocks = features.shape[0] * lax.axis_size("dom") // block_size
    local_cols = cols - lax.axis_index("rep") * quarter_blocks
    quarter = lax.all_gather(features, "dom", axis=0, tiled=True).reshape(
        quarter_blocks, block_size, width
    )
    picked = quarter[local_cols]
    partial_sum = jnp.einsum("rkij,rkjf->rif", vals, picked, preferred_element_type=jnp.float32)
    partial_sum = partial_sum.reshape(row_blocks * block_size, width)
    summed = lax.psum(partial_sum, "rep")
    aggregated = summed.astype(jnp.bfloat16)
    hidden = jnp.dot(aggregated, weight, preferred_element_type=jnp.float32) + bias
    gate_prob = jax.nn.sigmoid(hidden)
    output = (hidden * gate_prob).astype(jnp.bfloat16)
    grad_hidden = (
        cotangent.astype(jnp.float32) * gate_prob * (1.0 + hidden * (1.0 - gate_prob))
    ).astype(jnp.bfloat16)
    weight_part = lax.dot_general(
        aggregated, grad_hidden, (((0,), (0,)), ((), ())), preferred_element_type=jnp.float32
    )
    grad_agg = lax.dot_general(
        grad_hidden, weight, (((1,), (1,)), ((), ())), preferred_element_type=jnp.float32
    ).astype(jnp.bfloat16)
    weight_grad = lax.psum(weight_part, "dom")
    full_output, full_grad = (output, grad_agg)
    grad_blocks = full_grad.reshape(row_blocks, block_size, width)
    terms = jnp.einsum("rkij,rif->rkjf", vals, grad_blocks, preferred_element_type=jnp.float32)
    flat_terms = terms.reshape(row_blocks * block_count, block_size, width)
    flat_cols = local_cols.reshape(-1)
    contrib = jax.ops.segment_sum(flat_terms, flat_cols, num_segments=quarter_blocks)
    contrib = contrib.reshape(quarter_blocks * block_size, width)
    feature_grad = lax.psum_scatter(contrib, "dom", scatter_dimension=0, tiled=True)
    return (full_output, feature_grad, weight_grad)


def solution(mesh):
    placed = (
        P("dom", "rep"),
        P("dom", "rep", None, None),
        P(("rep", "dom"), None),
        P(),
        P(),
        P("dom", None),
    )
    return jax.shard_map(
        body,
        mesh=mesh,
        in_specs=placed,
        out_specs=(P("dom", None), P(("rep", "dom"), None), P()),
        check_vma=False,
    )
```

profile of v0, /device:TPU:0, one launch (start us, length us, event | category | flops | bytes accessed | tf_op | source)
XLA Modules:
  0.0 151.8 jit_solution(14498798401476357207)
XLA Ops:
  7.2 0.0 all-reduce.3.cloned.1.call-start
  7.2 0.7 copy-done.3
  8.0 0.1 copy.12
  8.0 0.1 reshape.29
  8.1 11.6 %all_gather.3 = bf16[2048,128]{1,0:T(8,128)(2,1)S(1)} all-gather(bf16[256,128]{1,0:T(8,128)(2,1)} %param.8), channel_id=1, replica_groups=mesh['rep'=4,'dom'=8] {'dom'}, dimensions={0}, use_global_device_ids=true | all-gather | bytes 589824 | tf_op jit(solution)/shard_map/all_gather | solution.py:12
  19.7 0.6 gather_fusion
  20.4 0.3 fusion.4
  20.7 30.9 %all-reduce.4 = bf16[1024,128]{1,0:T(8,128)(2,1)S(1)} all-reduce(f32[1024,128]{1,0:T(8,128)S(1)} %bitcast.30), channel_id=1, replica_groups=mesh['rep'=4,'dom'=8] {'rep'}, use_global_device_ids=true, to_apply=%region_0.0 | all-reduce | flops 131072 | bytes 786432 | tf_op jit(solution)/shard_map/psum | solution.py:18
  51.6 1.1 multiply_convert_fusion
  52.8 0.9 fusion.5
  53.7 0.0 all-reduce.3.cloned.1.call-update
  53.7 0.0 reduce-scatter.2.cloned.1.call-start
  53.7 0.2 convolution_convert_fusion
  54.0 0.3 fusion.3
  54.3 0.1 copy.13
  54.4 0.1 reshape.37
  54.5 0.3 copy.15
  54.8 0.1 broadcast_in_dim.8
  54.9 1.6 %scatter_fusion = f32[16,128,128]{2,1,0:T(8,128)S(1)} fusion(f32[16,128,128]{2,1,0:T(8,128)S(1)} %broadcast_in_dim.8, s32[16]{0:T(128)S(1)} %reshape.37, f32[16,128,128]{2,1,0:T(8,128)S(1)} %copy.15), kind=kCustom, calls=%fused_computation.1 | custom fusion | flops 262144 | bytes 3145792 | tf_op jit(solution)/shard_map/scatter-add | solution.py:38
  56.6 1.0 copy-done.1
  57.5 0.0 reduce-scatter.2.cloned.1.call-update
  57.6 46.4 %all-reduce.3.cloned.1.call-done = f32[128,128]{1,0:T(8,128)} async-done(((f32[128,128]{1,0:T(8,128)}), f32[128,128]{1,0:T(8,128)}) %all-reduce.3.cloned.1.call-update) | async-done | bytes 65552 | tf_op jit(solution)/shard_map/psum | solution.py:32
  104.0 39.5 %reduce-scatter.2.cloned.1.call-done = f32[256,128]{1,0:T(8,128)} async-done(((f32[2048,128]{1,0:T(8,128)}), f32[256,128]{1,0:T(8,128)}) %reduce-scatter.2.cloned.1.call-update) | async-done | bytes 131088 | tf_op jit(solution)/shard_map/reduce_scatter | solution.py:40
  143.5 1.5 copy.24
  (12 shorter events, 0.0 us)
Async XLA Ops:
  7.2 13.2 %copy-start = (bf16[8,2,128,128]{3,2,1,0:T(8,128)(2,1)S(1)}, bf16[8,2,128,128]{3,2,1,0:T(8,128)(2,1)}, u32[]{:S(2)}) copy-start(bf16[8,2,128,128]{3,2,1,0:T(8,128)(2,1)} %param.7) | copy-start | bytes 1572868
  7.2 96.8 %all-reduce.3.cloned.1.call-start = ((), (), s32[]{:S(2)}) async-start(), calls=%async_computation.2 | async-start | bytes 131072 | tf_op jit(solution)/shard_map/psum | solution.py:32
  7.2 0.7 copy-start.3
  20.7 30.9 %copy-start.2 = (bf16[128,128]{1,0:T(8,128)(2,1)S(1)}, bf16[128,128]{1,0:T(8,128)(2,1)}, u32[]{:S(2)}) copy-start(bf16[128,128]{1,0:T(8,128)(2,1)} %param.9) | copy-start | bytes 98308
  20.7 30.9 %copy-start.4 = (bf16[1024,128]{1,0:T(8,128)(2,1)S(1)}, bf16[1024,128]{1,0:T(8,128)(2,1)}, u32[]{:S(2)}) copy-start(bf16[1024,128]{1,0:T(8,128)(2,1)} %param.11) | copy-start | bytes 786436
  20.7 30.9 %copy-start.5 = (f32[128]{0:T(128)S(1)}, f32[128]{0:T(128)}, u32[]{:S(2)}) copy-start(f32[128]{0:T(128)} %param.10) | copy-start | bytes 1540
  53.7 89.8 %reduce-scatter.2.cloned.1.call-start = ((), (), s32[]{:S(2)}) async-start(), calls=%async_computation.1 | async-start | bytes 1179648 | tf_op jit(solution)/shard_map/reduce_scatter | solution.py:40
  56.6 1.0 copy-start.1
Sparse Core Ops, SparseCore 0:
  53.8 50.1 all-reduce.2
  108.0 35.4 reduce-scatter.1
where the time goes:
time: 152 us
  waiting for transfers between devices  86 us (57%)
  blocking collectives  42.5 us (28%)
  between operations  14.2 us (9%)
  local copies, waits for them, and re-layouts  4.59 us (3%)
  matrix products  2.88 us (2%)
  other arithmetic  1.62 us (1%)
    psum x1, waiting for transfers between devices, body(): weight_grad = lax.psum(weight_part, 'dom')  46.4 us
    reduce_scatter x1, waiting for transfers between devices, body(): lax.psum_scatter(contrib, 'dom', scatter_dimension=0, tiled=True)  39.5 us
    psum x1, blocking collectives, body(): summed = lax.psum(partial_sum, 'rep')  30.9 us
    all_gather x1, blocking collectives, body(): lax.all_gather(features, 'dom', axis=0, tiled=True)  11.6 us
    unnamed x13, local copies, waits for them, and re-layouts  3.18 us
  transfers between devices with their start and end apart: 2, of which 2 were waited for; matrix products, arithmetic and copies ran while one was open for 2% of the time, Pallas kernels for 0%

commit v1 on v0

v1 whole, which is shorter than its diff:
```python
import jax
import jax.numpy as jnp
from jax import lax
from jax.sharding import PartitionSpec as P

BF16 = jnp.bfloat16
F32 = jnp.float32


def swap(value, axis, distance):
    size = lax.axis_size(axis)
    return lax.ppermute(value, axis, [(i, i ^ distance) for i in range(size)])


def body(cols, vals, features, weight, bias, cotangent):
    row_blocks, block_count, block_size, _ = vals.shape
    width = features.shape[1]
    dom, rep = lax.axis_size("dom"), lax.axis_size("rep")
    own_blocks = features.shape[0] // block_size
    quarter_blocks = own_blocks * dom
    me_dom, me_rep = lax.axis_index("dom"), lax.axis_index("rep")
    rows = row_blocks * block_size
    part = rows // rep

    local_cols = cols - me_rep * quarter_blocks
    slots = ((local_cols // own_blocks) ^ me_dom) * own_blocks + local_cols % own_blocks

    quarter = jnp.stack([features] + [swap(features, "dom", k) for k in range(1, dom)])
    quarter = quarter.reshape(quarter_blocks, block_size, width)
    picked = quarter[slots]
    partial_sum = jnp.einsum("rkij,rkjf->rif", vals, picked, preferred_element_type=F32)
    partial_sum = partial_sum.reshape(rep, part, width).astype(BF16)
    pieces = lax.all_to_all(partial_sum, "rep", split_axis=0, concat_axis=0)
    own_rows = pieces.astype(F32).sum(axis=0).astype(BF16)

    others = jnp.stack([own_rows] + [swap(own_rows, "rep", k) for k in range(1, rep)])
    aggregated = others[jnp.arange(rep) ^ me_rep].reshape(rows, width)

    hidden = jnp.dot(aggregated, weight, preferred_element_type=F32) + bias
    gate_prob = jax.nn.sigmoid(hidden)
    output = (hidden * gate_prob).astype(BF16)
    grad_hidden = (
        cotangent.astype(F32) * gate_prob * (1.0 + hidden * (1.0 - gate_prob))
    ).astype(BF16)
    weight_part = lax.dot_general(
        aggregated, grad_hidden, (((0,), (0,)), ((), ())), preferred_element_type=F32
    )
    grad_agg = lax.dot_general(
        grad_hidden, weight, (((1,), (1,)), ((), ())), preferred_element_type=F32
    ).astype(BF16)

    weight_rows = lax.all_to_all(
        weight_part.reshape(dom, width // dom, width), "dom", split_axis=0, concat_axis=0
    ).sum(axis=0)
    weight_grad = lax.all_gather(weight_rows, "dom", axis=0, tiled=True)

    grad_blocks = grad_agg.reshape(row_blocks, block_size, width)
    terms = jnp.einsum("rkij,rif->rkjf", vals, grad_blocks, preferred_element_type=F32)
    flat_terms = terms.reshape(row_blocks * block_count, block_size, width)
    contrib = jax.ops.segment_sum(flat_terms, slots.reshape(-1), num_segments=quarter_blocks)
    contrib = contrib.reshape(dom, own_blocks * block_size, width)
    total = contrib[0]
    for k in range(1, dom):
        total = total + swap(contrib[k].astype(BF16), "dom", k).astype(F32)
    return output, total, weight_grad


def solution(mesh):
    placed = (
        P("dom", "rep"),
        P("dom", "rep", None, None),
        P(("rep", "dom"), None),
        P(),
        P(),
        P("dom", None),
    )
    return jax.shard_map(
        body,
        mesh=mesh,
        in_specs=placed,
        out_specs=(P("dom", None), P(("rep", "dom"), None), P()),
        check_vma=False,
    )
```

time: 152 us -> 65.5 us (0.43)
  waiting for transfers between devices: 86 us -> 14.4 us
  blocking collectives: 42.5 us -> 8.27 us
  starting transfers between devices: 0.08 us -> 30.2 us
  between operations: 14.2 us -> 0.9 us
    psum x1 -> x0, waiting for transfers between devices: 46.4 us -> none  [body(): weight_grad = lax.psum(weight_part, 'dom')]
    reduce_scatter x1 -> x0, waiting for transfers between devices: 39.5 us -> none  [body(): lax.psum_scatter(contrib, 'dom', scatter_dimension=0, tiled=True)]
    psum x1 -> x0, blocking collectives: 30.9 us -> none  [body(): summed = lax.psum(partial_sum, 'rep')]
    ppermute x0 -> x17, starting transfers between devices: none -> 22 us  [swap(): return lax.ppermute(value, axis, [(i, i ^ distance) for i in range(size)])]
    all_to_all x0 -> x2, starting transfers between devices: none -> 8.22 us  [the longest x1 4.87 us: body(): pieces = lax.all_to_all(partial_sum, 'rep', split_axis=0, concat_axis=0)]
    all_to_all x0 -> x2, waiting for transfers between devices: none -> 8.07 us  [the longest x1 8.07 us: body(): pieces = lax.all_to_all(partial_sum, 'rep', split_axis=0, concat_axis=0)]
    ppermute x0 -> x17, waiting for transfers between devices: none -> 6.3 us  [swap(): return lax.ppermute(value, axis, [(i, i ^ distance) for i in range(size)])]
    all_gather x1, blocking collectives: 11.6 us -> 8.27 us  [body(): weight_grad = lax.all_gather(weight_rows, 'dom', axis=0, tiled=True)]
  transfers between devices with their start and end apart: 2 -> 19, of which waited for: 2 -> 4; matrix products, arithmetic and copies ran while one was open for 2% -> 3% of each run, Pallas kernels for 0% -> 0%
where the time goes in v1:
time: 65.5 us; the launch traced here: 65.2 us
  starting transfers between devices  30.2 us (46%)
  waiting for transfers between devices  14.4 us (22%)
  blocking collectives  8.27 us (13%)
  local copies, waits for them, and re-layouts  5.32 us (8%)
  matrix products  3.53 us (5%)
  other arithmetic  2.54 us (4%)
  between operations  0.9 us (1%)
    ppermute x17, starting transfers between devices, swap(): return lax.ppermute(value, axis, [(i, i ^ distance) for i in range(size)])  22 us
    all_gather x1, blocking collectives, body(): weight_grad = lax.all_gather(weight_rows, 'dom', axis=0, tiled=True)  8.27 us
    all_to_all x1, waiting for transfers between devices, body(): pieces = lax.all_to_all(partial_sum, 'rep', split_axis=0, concat_axis=0)  8.07 us
    ppermute x17, waiting for transfers between devices, swap(): return lax.ppermute(value, axis, [(i, i ^ distance) for i in range(size)])  6.3 us
    all_to_all x1, starting transfers between devices, body(): pieces = lax.all_to_all(partial_sum, 'rep', split_axis=0, concat_axis=0)  4.87 us
    all_to_all x1, starting transfers between devices, body(): lax.all_to_all(weight_part.reshape(dom, width // dom, width), 'dom', spli...  3.35 us
    unnamed x20, local copies, waits for them, and re-layouts  3.12 us
    scatter-add x1, other arithmetic, body(): jax.ops.segment_sum(flat_terms, slots.reshape(-1), num_segments=quarter_b...  1.6 us
  transfers between devices with their start and end apart: 19, of which 4 were waited for; matrix products, arithmetic and copies ran while one was open for 3% of the time, Pallas kernels for 0%

profile of v1, /device:TPU:0, one launch (start us, length us, event | category | flops | bytes accessed | tf_op | source)
XLA Modules:
  0.0 65.2 jit_solution(6918728102225309310)
XLA Ops:
  0.6 2.5 %collective-permute-start.4 = (bf16[256,128]{1,0:T(8,128)(2,1)}, bf16[256,128]{1,0:T(8,128)(2,1)S(1)}, u32[]{:S(2)}, u32[]{:S(2)}) collective-permute-start(bf16[256,128]{1,0:T(8,128)(2,1)} %param.8), channel_id=1, source_target_pairs={{0,5},{1,4},{2,7},{3,6},{4,1},{5,0},{6,3},{7,2},{8,13},{9,12},{10,... | collective-permute-start | bytes 196616 | tf_op jit(solution)/shard_map/ppermute | solution.py:12
  3.8 1.4 %collective-permute-start.2 = (bf16[256,128]{1,0:T(8,128)(2,1)}, bf16[256,128]{1,0:T(8,128)(2,1)S(1)}, u32[]{:S(2)}, u32[]{:S(2)}) collective-permute-start(bf16[256,128]{1,0:T(8,128)(2,1)} %param.8), channel_id=1, source_target_pairs={{0,3},{1,2},{2,1},{3,0},{4,7},{5,6},{6,5},{7,4},{8,11},{9,10},{10,... | collective-permute-start | bytes 196616 | tf_op jit(solution)/shard_map/ppermute | solution.py:12
  5.6 0.9 %bitcast_dynamic-update-slice_fusion.7 = bf16[8,256,128]{2,1,0:T(8,128)(2,1)S(1)} fusion(bf16[256,128]{1,0:T(8,128)(2,1)} %param.8), kind=kLoop, calls=%fused_computation.27 | loop fusion | bytes 131072
  6.5 0.7 %copy-done.3 = s32[8,2]{0,1:T(2,128)S(1)} copy-done((s32[8,2]{0,1:T(2,128)S(1)}, s32[8,2]{0,1:T(2,128)}, u32[]{:S(2)}) %copy-start.3) | copy-done | bytes 88
  7.4 2.7 %collective-permute-start.6 = (bf16[256,128]{1,0:T(8,128)(2,1)S(1)}, bf16[256,128]{1,0:T(8,128)(2,1)S(1)}, u32[]{:S(2)}, u32[]{:S(2)}) collective-permute-start(bf16[256,128]{1,0:T(8,128)(2,1)S(1)} %copy-done.1), channel_id=1, source_target_pairs={{0,7},{1,6},{2,5},{3,4},{4,3},{5,2},{6,1},{7,0},{8,15},{9,14},{10,... | collective-permute-start | bytes 196616 | tf_op jit(solution)/shard_map/ppermute | solution.py:12
  10.1 1.9 %collective-permute-start.5 = (bf16[256,128]{1,0:T(8,128)(2,1)S(1)}, bf16[256,128]{1,0:T(8,128)(2,1)S(1)}, u32[]{:S(2)}, u32[]{:S(2)}) collective-permute-start(bf16[256,128]{1,0:T(8,128)(2,1)S(1)} %copy-done.1), channel_id=1, source_target_pairs={{0,6},{1,7},{2,4},{3,5},{4,2},{5,3},{6,0},{7,1},{8,14},{9,15},{10,... | collective-permute-start | bytes 196616 | tf_op jit(solution)/shard_map/ppermute | solution.py:12
  12.2 3.2 %collective-permute-done.5 = bf16[256,128]{1,0:T(8,128)(2,1)S(1)} collective-permute-done((bf16[256,128]{1,0:T(8,128)(2,1)S(1)}, bf16[256,128]{1,0:T(8,128)(2,1)S(1)}, u32[]{:S(2)}, u32[]{:S(2)}) %collective-permute-start.5) | collective-permute-done | bytes 65568 | tf_op jit(solution)/shard_map/ppermute | solution.py:12
  16.1 1.0 %fusion = bf16[8,128,128]{1,2,0:T(8,128)(2,1)} fusion(bf16[8,2,128,128]{3,2,1,0:T(8,128)(2,1)S(1)} %copy-done, bf16[8,2,128,128]{3,2,1,0:T(8,128)(2,1)S(1)} %bitcast.78), kind=kOutput, calls=%fused_computation.5 | convolution fusion | flops 67239936 | bytes 1310720 | tf_op jit(solution)/shard_map/rkij,rkjf->rif/dot_general | solution.py:31
  17.1 4.9 %all-to-all-start = ((bf16[4,256,128]{2,1,0:T(8,128)(2,1)}), bf16[4,256,128]{2,1,0:T(8,128)(2,1)S(1)}, u32[]{:S(2)}, u32[]{:S(2)}) async-start(bf16[4,256,128]{2,1,0:T(8,128)(2,1)} %bitcast.13), calls=%async_computation | async-start | bytes 524288 | tf_op jit(solution)/shard_map/all_to_all | solution.py:33
  22.1 8.1 %all-to-all-done = bf16[4,256,128]{2,1,0:T(8,128)(2,1)S(1)} async-done(((bf16[4,256,128]{2,1,0:T(8,128)(2,1)}), bf16[4,256,128]{2,1,0:T(8,128)(2,1)S(1)}, u32[]{:S(2)}, u32[]{:S(2)}) %all-to-all-start) | async-done | bytes 262176 | tf_op jit(solution)/shard_map/all_to_all | solution.py:33
  30.2 1.4 %collective-permute-start.9 = (bf16[256,128]{1,0:T(8,128)(2,1)S(1)}, bf16[256,128]{1,0:T(8,128)(2,1)S(1)}, u32[]{:S(2)}, u32[]{:S(2)}) collective-permute-start(bf16[256,128]{1,0:T(8,128)(2,1)S(1)} %reduce_sum.21), channel_id=1, source_target_pairs={{0,24},{8,16},{16,8},{24,0},{1,25},{9,17},{17,9},{25,1},{2,26},{10... | collective-permute-start | bytes 196616 | tf_op jit(solution)/shard_map/ppermute | solution.py:12
  31.9 2.8 %collective-permute-start.7 = (bf16[256,128]{1,0:T(8,128)(2,1)S(1)}, bf16[256,128]{1,0:T(8,128)(2,1)S(1)}, u32[]{:S(2)}, u32[]{:S(2)}) collective-permute-start(bf16[256,128]{1,0:T(8,128)(2,1)S(1)} %reduce_sum.21), channel_id=1, source_target_pairs={{0,8},{8,0},{16,24},{24,16},{1,9},{9,1},{17,25},{25,17},{2,10},{10... | collective-permute-start | bytes 196616 | tf_op jit(solution)/shard_map/ppermute | solution.py:12
  34.7 1.7 %collective-permute-done.9 = bf16[256,128]{1,0:T(8,128)(2,1)S(1)} collective-permute-done((bf16[256,128]{1,0:T(8,128)(2,1)S(1)}, bf16[256,128]{1,0:T(8,128)(2,1)S(1)}, u32[]{:S(2)}, u32[]{:S(2)}) %collective-permute-start.9) | collective-permute-done | bytes 65568 | tf_op jit(solution)/shard_map/ppermute | solution.py:12
  36.4 1.4 %collective-permute-done.8 = bf16[256,128]{1,0:T(8,128)(2,1)S(1)} collective-permute-done((bf16[256,128]{1,0:T(8,128)(2,1)S(1)}, bf16[256,128]{1,0:T(8,128)(2,1)S(1)}, u32[]{:S(2)}, u32[]{:S(2)}) %collective-permute-start.8) | collective-permute-done | bytes 65568 | tf_op jit(solution)/shard_map/ppermute | solution.py:12
  39.4 1.1 %multiply_convert_fusion = (bf16[1024,128]{1,0:T(8,128)(2,1)S(1)}, bf16[1024,128]{1,0:T(8,128)(2,1)}) fusion(bf16[1024,128]{1,0:T(8,128)(2,1)S(1)} %copy-done.4, f32[128]{0:T(128)S(1)} %copy-done.5, bf16[1024,128]{1,0:T(8,128)(2,1)S(1)} %bitcast.81, bf16[128,128]{1,0:T(8,128)(2,1)S(1)} %copy-done.2), kind=kOutput, calls=%fused_computation.7 | convolution fusion | flops 35258368 | bytes 1081856 | tf_op jit(solution)/shard_map/dot_general | solution.py:39
  41.5 1.6 %scatter_fusion = f32[16,128,128]{2,1,0:T(8,128)S(1)} fusion(f32[16,128,128]{2,1,0:T(8,128)S(1)} %broadcast_in_dim.9, s32[16]{0:T(128)S(1)} %reshape.85, f32[16,128,128]{2,1,0:T(8,128)S(1)} %copy.15), kind=kCustom, calls=%fused_computation.2 | custom fusion | flops 262144 | bytes 3145792 | tf_op jit(solution)/shard_map/scatter-add | solution.py:60
  43.4 1.5 %collective-permute-start.10 = (bf16[256,128]{1,0:T(8,128)(2,1)S(1)}, bf16[256,128]{1,0:T(8,128)(2,1)S(1)}, u32[]{:S(2)}, u32[]{:S(2)}) collective-permute-start(bf16[256,128]{1,0:T(8,128)(2,1)S(1)} %bitcast.90), channel_id=1, source_target_pairs={{0,1},{1,0},{2,3},{3,2},{4,5},{5,4},{6,7},{7,6},{8,9},{9,8},{10,11... | collective-permute-start | bytes 196616 | tf_op jit(solution)/shard_map/ppermute | solution.py:12
  44.9 0.8 %fusion.1 = f32[8,16,128]{2,1,0:T(8,128)} fusion(bf16[8,16,1024]{2,1,0:T(8,128)(2,1)S(1)} %bitcast.82, bf16[1024,128]{1,0:T(8,128)(2,1)S(1)} %get-tuple-element.12), kind=kOutput, calls=%fused_computation.11 | convolution fusion | flops 33554432 | bytes 589824 | tf_op jit(solution)/shard_map/dot_general | solution.py:45
  45.8 3.4 %all-to-all-start.1 = ((f32[8,16,128]{2,1,0:T(8,128)}), f32[8,16,128]{2,1,0:T(8,128)S(1)}, u32[]{:S(2)}, u32[]{:S(2)}) async-start(f32[8,16,128]{2,1,0:T(8,128)} %fusion.1), calls=%async_computation.1 | async-start | bytes 131072 | tf_op jit(solution)/shard_map/all_to_all | solution.py:52
  49.1 2.9 %collective-permute-start.15 = (bf16[256,128]{1,0:T(8,128)(2,1)S(1)}, bf16[256,128]{1,0:T(8,128)(2,1)S(1)}, u32[]{:S(2)}, u32[]{:S(2)}) collective-permute-start(bf16[256,128]{1,0:T(8,128)(2,1)S(1)} %bitcast.89), channel_id=1, source_target_pairs={{0,6},{1,7},{2,4},{3,5},{4,2},{5,3},{6,0},{7,1},{8,14},{9,15},{10,... | collective-permute-start | bytes 196616 | tf_op jit(solution)/shard_map/ppermute | solution.py:12
  52.0 1.5 %collective-permute-start.13 = (bf16[256,128]{1,0:T(8,128)(2,1)S(1)}, bf16[256,128]{1,0:T(8,128)(2,1)S(1)}, u32[]{:S(2)}, u32[]{:S(2)}) collective-permute-start(bf16[256,128]{1,0:T(8,128)(2,1)S(1)} %bitcast.87), channel_id=1, source_target_pairs={{0,4},{1,5},{2,6},{3,7},{4,0},{5,1},{6,2},{7,3},{8,12},{9,13},{10,... | collective-permute-start | bytes 196616 | tf_op jit(solution)/shard_map/ppermute | solution.py:12
  54.0 1.5 %collective-permute-start.11 = (bf16[256,128]{1,0:T(8,128)(2,1)S(1)}, bf16[256,128]{1,0:T(8,128)(2,1)S(1)}, u32[]{:S(2)}, u32[]{:S(2)}) collective-permute-start(bf16[256,128]{1,0:T(8,128)(2,1)S(1)} %bitcast.85), channel_id=1, source_target_pairs={{0,2},{1,3},{2,0},{3,1},{4,6},{5,7},{6,4},{7,5},{8,10},{9,11},{10,... | collective-permute-start | bytes 196616 | tf_op jit(solution)/shard_map/ppermute | solution.py:12
  55.5 8.3 %all_gather.3 = f32[128,128]{1,0:T(8,128)S(1)} all-gather(f32[16,128]{1,0:T(8,128)S(1)} %reduce_sum.22), channel_id=1, replica_groups=mesh['rep'=4,'dom'=8] {'dom'}, dimensions={0}, use_global_device_ids=true | all-gather | bytes 73728 | tf_op jit(solution)/shard_map/all_gather | solution.py:55
  63.8 0.7 %fusion.8 = f32[256,128]{1,0:T(8,128)} fusion(f32[2,128,128]{2,1,0:T(8,128)S(1)} %slice.51, bf16[256,128]{1,0:T(8,128)(2,1)S(1)} %collective-permute-done.16, bf16[256,128]{1,0:T(8,128)(2,1)S(1)} %collective-permute-done.15, bf16[256,128]{1,0:T(8,128)(2,1)S(1)} %collective-permute-done.14, bf16[256,128]{1,0:T(8,128)(2,1)S(1)} %collective-permute-done.13, ...), kind=kLoop, calls=%fused_computation.19 | loop fusion | flops 458752 | bytes 720896 | tf_op jit(solution)/shard_map/add | solution.py:64
  (62 shorter events, 6.5 us)
Async XLA Ops:
  0.6 15.4 %copy-start = (bf16[8,2,128,128]{3,2,1,0:T(8,128)(2,1)S(1)}, bf16[8,2,128,128]{3,2,1,0:T(8,128)(2,1)}, u32[]{:S(2)}) copy-start(bf16[8,2,128,128]{3,2,1,0:T(8,128)(2,1)} %param.7) | copy-start | bytes 1572868
  0.6 11.5 %collective-permute-start.4 = (bf16[256,128]{1,0:T(8,128)(2,1)}, bf16[256,128]{1,0:T(8,128)(2,1)S(1)}, u32[]{:S(2)}, u32[]{:S(2)}) collective-permute-start(bf16[256,128]{1,0:T(8,128)(2,1)} %param.8), channel_id=1, source_target_pairs={{0,5},{1,4},{2,7},{3,6},{4,1},{5,0},{6,3},{7,2},{8,13},{9,12},{10,... | collective-permute-start | bytes 196616 | tf_op jit(solution)/shard_map/ppermute | solution.py:12
  3.1 9.0 %collective-permute-start.3 = (bf16[256,128]{1,0:T(8,128)(2,1)}, bf16[256,128]{1,0:T(8,128)(2,1)S(1)}, u32[]{:S(2)}, u32[]{:S(2)}) collective-permute-start(bf16[256,128]{1,0:T(8,128)(2,1)} %param.8), channel_id=1, source_target_pairs={{0,4},{1,5},{2,6},{3,7},{4,0},{5,1},{6,2},{7,3},{8,12},{9,13},{10,... | collective-permute-start | bytes 196616 | tf_op jit(solution)/shard_map/ppermute | solution.py:12
  3.8 8.3 %collective-permute-start.2 = (bf16[256,128]{1,0:T(8,128)(2,1)}, bf16[256,128]{1,0:T(8,128)(2,1)S(1)}, u32[]{:S(2)}, u32[]{:S(2)}) collective-permute-start(bf16[256,128]{1,0:T(8,128)(2,1)} %param.8), channel_id=1, source_target_pairs={{0,3},{1,2},{2,1},{3,0},{4,7},{5,6},{6,5},{7,4},{8,11},{9,10},{10,... | collective-permute-start | bytes 196616 | tf_op jit(solution)/shard_map/ppermute | solution.py:12
  5.1 5.0 %collective-permute-start.1 = (bf16[256,128]{1,0:T(8,128)(2,1)}, bf16[256,128]{1,0:T(8,128)(2,1)S(1)}, u32[]{:S(2)}, u32[]{:S(2)}) collective-permute-start(bf16[256,128]{1,0:T(8,128)(2,1)} %param.8), channel_id=1, source_target_pairs={{0,2},{1,3},{2,0},{3,1},{4,6},{5,7},{6,4},{7,5},{8,10},{9,11},{10,... | collective-permute-start | bytes 196616 | tf_op jit(solution)/shard_map/ppermute | solution.py:12
  5.4 2.0 %collective-permute-start = (bf16[256,128]{1,0:T(8,128)(2,1)}, bf16[256,128]{1,0:T(8,128)(2,1)S(1)}, u32[]{:S(2)}, u32[]{:S(2)}) collective-permute-start(bf16[256,128]{1,0:T(8,128)(2,1)} %param.8), channel_id=1, source_target_pairs={{0,1},{1,0},{2,3},{3,2},{4,5},{5,4},{6,7},{7,6},{8,9},{9,8},{10,11... | collective-permute-start | bytes 196616 | tf_op jit(solution)/shard_map/ppermute | solution.py:12
  5.6 1.8 %copy-start.1 = (bf16[256,128]{1,0:T(8,128)(2,1)S(1)}, bf16[256,128]{1,0:T(8,128)(2,1)}, u32[]{:S(2)}) copy-start(bf16[256,128]{1,0:T(8,128)(2,1)} %param.8) | copy-start | bytes 196612
  7.4 8.0 %collective-permute-start.6 = (bf16[256,128]{1,0:T(8,128)(2,1)S(1)}, bf16[256,128]{1,0:T(8,128)(2,1)S(1)}, u32[]{:S(2)}, u32[]{:S(2)}) collective-permute-start(bf16[256,128]{1,0:T(8,128)(2,1)S(1)} %copy-done.1), channel_id=1, source_target_pairs={{0,7},{1,6},{2,5},{3,4},{4,3},{5,2},{6,1},{7,0},{8,15},{9,14},{10,... | collective-permute-start | bytes 196616 | tf_op jit(solution)/shard_map/ppermute | solution.py:12
  10.1 5.2 %collective-permute-start.5 = (bf16[256,128]{1,0:T(8,128)(2,1)S(1)}, bf16[256,128]{1,0:T(8,128)(2,1)S(1)}, u32[]{:S(2)}, u32[]{:S(2)}) collective-permute-start(bf16[256,128]{1,0:T(8,128)(2,1)S(1)} %copy-done.1), channel_id=1, source_target_pairs={{0,6},{1,7},{2,4},{3,5},{4,2},{5,3},{6,0},{7,1},{8,14},{9,15},{10,... | collective-permute-start | bytes 196616 | tf_op jit(solution)/shard_map/ppermute | solution.py:12
  17.1 13.1 %all-to-all-start = ((bf16[4,256,128]{2,1,0:T(8,128)(2,1)}), bf16[4,256,128]{2,1,0:T(8,128)(2,1)S(1)}, u32[]{:S(2)}, u32[]{:S(2)}) async-start(bf16[4,256,128]{2,1,0:T(8,128)(2,1)} %bitcast.13), calls=%async_computation | async-start | bytes 524288 | tf_op jit(solution)/shard_map/all_to_all | solution.py:33
  30.2 6.2 %collective-permute-start.9 = (bf16[256,128]{1,0:T(8,128)(2,1)S(1)}, bf16[256,128]{1,0:T(8,128)(2,1)S(1)}, u32[]{:S(2)}, u32[]{:S(2)}) collective-permute-start(bf16[256,128]{1,0:T(8,128)(2,1)S(1)} %reduce_sum.21), channel_id=1, source_target_pairs={{0,24},{8,16},{16,8},{24,0},{1,25},{9,17},{17,9},{25,1},{2,26},{10... | collective-permute-start | bytes 196616 | tf_op jit(solution)/shard_map/ppermute | solution.py:12
  31.6 6.1 %collective-permute-start.8 = (bf16[256,128]{1,0:T(8,128)(2,1)S(1)}, bf16[256,128]{1,0:T(8,128)(2,1)S(1)}, u32[]{:S(2)}, u32[]{:S(2)}) collective-permute-start(bf16[256,128]{1,0:T(8,128)(2,1)S(1)} %reduce_sum.21), channel_id=1, source_target_pairs={{0,16},{8,24},{16,0},{24,8},{1,17},{9,25},{17,1},{25,9},{2,18},{10... | collective-permute-start | bytes 196616 | tf_op jit(solution)/shard_map/ppermute | solution.py:12
  31.9 5.9 %collective-permute-start.7 = (bf16[256,128]{1,0:T(8,128)(2,1)S(1)}, bf16[256,128]{1,0:T(8,128)(2,1)S(1)}, u32[]{:S(2)}, u32[]{:S(2)}) collective-permute-start(bf16[256,128]{1,0:T(8,128)(2,1)S(1)} %reduce_sum.21), channel_id=1, source_target_pairs={{0,8},{8,0},{16,24},{24,16},{1,9},{9,1},{17,25},{25,17},{2,10},{10... | collective-permute-start | bytes 196616 | tf_op jit(solution)/shard_map/ppermute | solution.py:12
  38.4 0.8 %copy-start.2 = (bf16[128,128]{1,0:T(8,128)(2,1)S(1)}, bf16[128,128]{1,0:T(8,128)(2,1)}, u32[]{:S(2)}) copy-start(bf16[128,128]{1,0:T(8,128)(2,1)} %param.9) | copy-start | bytes 98308
  38.4 1.0 %copy-start.4 = (bf16[1024,128]{1,0:T(8,128)(2,1)S(1)}, bf16[1024,128]{1,0:T(8,128)(2,1)}, u32[]{:S(2)}) copy-start(bf16[1024,128]{1,0:T(8,128)(2,1)} %param.11) | copy-start | bytes 786436
  38.6 0.8 %copy-start.5 = (f32[128]{0:T(128)S(1)}, f32[128]{0:T(128)}, u32[]{:S(2)}) copy-start(f32[128]{0:T(128)} %param.10) | copy-start | bytes 1540
  43.3 10.2 %collective-permute-start.16 = (bf16[256,128]{1,0:T(8,128)(2,1)S(1)}, bf16[256,128]{1,0:T(8,128)(2,1)S(1)}, u32[]{:S(2)}, u32[]{:S(2)}) collective-permute-start(bf16[256,128]{1,0:T(8,128)(2,1)S(1)} %bitcast.91), channel_id=1, source_target_pairs={{0,7},{1,6},{2,5},{3,4},{4,3},{5,2},{6,1},{7,0},{8,15},{9,14},{10,... | collective-permute-start | bytes 196616 | tf_op jit(solution)/shard_map/ppermute | solution.py:12
  43.4 10.6 %collective-permute-start.10 = (bf16[256,128]{1,0:T(8,128)(2,1)S(1)}, bf16[256,128]{1,0:T(8,128)(2,1)S(1)}, u32[]{:S(2)}, u32[]{:S(2)}) collective-permute-start(bf16[256,128]{1,0:T(8,128)(2,1)S(1)} %bitcast.90), channel_id=1, source_target_pairs={{0,1},{1,0},{2,3},{3,2},{4,5},{5,4},{6,7},{7,6},{8,9},{9,8},{10,11... | collective-permute-start | bytes 196616 | tf_op jit(solution)/shard_map/ppermute | solution.py:12
  45.8 9.7 %all-to-all-start.1 = ((f32[8,16,128]{2,1,0:T(8,128)}), f32[8,16,128]{2,1,0:T(8,128)S(1)}, u32[]{:S(2)}, u32[]{:S(2)}) async-start(f32[8,16,128]{2,1,0:T(8,128)} %fusion.1), calls=%async_computation.1 | async-start | bytes 131072 | tf_op jit(solution)/shard_map/all_to_all | solution.py:52
  49.1 14.7 %collective-permute-start.15 = (bf16[256,128]{1,0:T(8,128)(2,1)S(1)}, bf16[256,128]{1,0:T(8,128)(2,1)S(1)}, u32[]{:S(2)}, u32[]{:S(2)}) collective-permute-start(bf16[256,128]{1,0:T(8,128)(2,1)S(1)} %bitcast.89), channel_id=1, source_target_pairs={{0,6},{1,7},{2,4},{3,5},{4,2},{5,3},{6,0},{7,1},{8,14},{9,15},{10,... | collective-permute-start | bytes 196616 | tf_op jit(solution)/shard_map/ppermute | solution.py:12
  52.0 11.8 %collective-permute-start.14 = (bf16[256,128]{1,0:T(8,128)(2,1)S(1)}, bf16[256,128]{1,0:T(8,128)(2,1)S(1)}, u32[]{:S(2)}, u32[]{:S(2)}) collective-permute-start(bf16[256,128]{1,0:T(8,128)(2,1)S(1)} %bitcast.88), channel_id=1, source_target_pairs={{0,5},{1,4},{2,7},{3,6},{4,1},{5,0},{6,3},{7,2},{8,13},{9,12},{10,... | collective-permute-start | bytes 196616 | tf_op jit(solution)/shard_map/ppermute | solution.py:12
  52.0 11.8 %collective-permute-start.13 = (bf16[256,128]{1,0:T(8,128)(2,1)S(1)}, bf16[256,128]{1,0:T(8,128)(2,1)S(1)}, u32[]{:S(2)}, u32[]{:S(2)}) collective-permute-start(bf16[256,128]{1,0:T(8,128)(2,1)S(1)} %bitcast.87), channel_id=1, source_target_pairs={{0,4},{1,5},{2,6},{3,7},{4,0},{5,1},{6,2},{7,3},{8,12},{9,13},{10,... | collective-permute-start | bytes 196616 | tf_op jit(solution)/shard_map/ppermute | solution.py:12
  53.5 10.3 %collective-permute-start.12 = (bf16[256,128]{1,0:T(8,128)(2,1)S(1)}, bf16[256,128]{1,0:T(8,128)(2,1)S(1)}, u32[]{:S(2)}, u32[]{:S(2)}) collective-permute-start(bf16[256,128]{1,0:T(8,128)(2,1)S(1)} %bitcast.86), channel_id=1, source_target_pairs={{0,3},{1,2},{2,1},{3,0},{4,7},{5,6},{6,5},{7,4},{8,11},{9,10},{10,... | collective-permute-start | bytes 196616 | tf_op jit(solution)/shard_map/ppermute | solution.py:12
  54.0 9.8 %collective-permute-start.11 = (bf16[256,128]{1,0:T(8,128)(2,1)S(1)}, bf16[256,128]{1,0:T(8,128)(2,1)S(1)}, u32[]{:S(2)}, u32[]{:S(2)}) collective-permute-start(bf16[256,128]{1,0:T(8,128)(2,1)S(1)} %bitcast.85), channel_id=1, source_target_pairs={{0,2},{1,3},{2,0},{3,1},{4,6},{5,7},{6,4},{7,5},{8,10},{9,11},{10,... | collective-permute-start | bytes 196616 | tf_op jit(solution)/shard_map/ppermute | solution.py:12
  (1 other events, 0.7 us)

commit v2 on v0

v2 whole, which is shorter than its diff:
```python
import functools

import jax
import jax.numpy as jnp
from jax import lax
from jax.experimental import pallas as pl
from jax.experimental.pallas import tpu as pltpu
from jax.sharding import PartitionSpec as P

BF16 = jnp.bfloat16
F32 = jnp.float32
VMEM = pl.BlockSpec(memory_space=pltpu.VMEM)
SMEM = pl.BlockSpec(memory_space=pltpu.SMEM)


def swap(value, axis, distance):
    size = lax.axis_size(axis)
    return lax.ppermute(value, axis, [(i, i ^ distance) for i in range(size)])


def matmul(a, b, contract):
    return lax.dot_general(a, b, ((contract[:1], contract[1:]), ((), ())), preferred_element_type=F32)


def slot_of(cols_ref, row, k, own_blocks, quarter_blocks):
    col = cols_ref[row, k] - lax.axis_index("rep") * quarter_blocks
    owner = lax.div(col, jnp.int32(own_blocks)) ^ lax.axis_index("dom")
    return owner * own_blocks + lax.rem(col, jnp.int32(own_blocks))


def aggregate_kernel(rep, cols_ref, vals_ref, own_ref, *refs):
    near, far = refs[: -rep - 2], refs[-rep - 2]
    outs, held = refs[-rep - 1 : -1], refs[-1]
    rows, count, size, _ = vals_ref.shape
    own_blocks = own_ref.shape[0] // size
    quarter_blocks = held.shape[0]
    chips = quarter_blocks // own_blocks // 2

    def put(slot, block):
        held[slot * own_blocks : (slot + 1) * own_blocks] = block.reshape(own_blocks, size, -1)

    put(0, own_ref[...])
    for chip in range(1, chips):
        put(2 * chip, near[chip - 1][...])
    nodes = own_blocks * size
    put(1, near[chips - 1][...])
    for chip in range(1, chips):
        put(2 * chip + 1, far[(chip - 1) * nodes : chip * nodes])

    share = rows // rep
    for j in range(rep):
        target = lax.axis_index("rep") ^ j
        for i in range(share):
            row = target * share + i
            total = None
            for k in range(count):
                slot = slot_of(cols_ref, row, k, own_blocks, quarter_blocks)
                term = matmul(vals_ref[row, k], held[slot], (1, 0))
                total = term if total is None else total + term
            outs[j][i * size : (i + 1) * size] = total.astype(outs[j].dtype)


def layer_kernel(
    rep, cols_ref, vals_ref, cotangent_ref, weight_ref, bias_ref, *refs
):
    pieces = refs[:rep]
    output_ref, send_ref, keep_ref, keep_weight_ref, contrib = refs[rep:]
    rows, count, size, _ = vals_ref.shape
    share = rows // rep
    quarter_blocks = contrib.shape[0]
    own_blocks = keep_ref.shape[1] // size
    contrib[...] = jnp.zeros_like(contrib)
    weight_part = jnp.zeros(weight_ref.shape, F32)
    for j in range(rep):
        target = lax.axis_index("rep") ^ j
        aggregated = pieces[j][...]
        part = aggregated.shape[0]
        here = pl.ds(pl.multiple_of(target * part, part), part)
        hidden = matmul(aggregated, weight_ref[...], (1, 0)) + bias_ref[...]
        gate_prob = jax.nn.sigmoid(hidden)
        output_ref[here, :] = (hidden * gate_prob).astype(BF16)
        grad_hidden = (
            cotangent_ref[here, :].astype(F32) * gate_prob * (1.0 + hidden * (1.0 - gate_prob))
        ).astype(BF16)
        weight_part += matmul(aggregated, grad_hidden, (0, 0))
        grad_agg = matmul(grad_hidden, weight_ref[...], (1, 1)).astype(BF16)
        for i in range(share):
            row = target * share + i
            grad_block = grad_agg[i * size : (i + 1) * size]
            for k in range(count):
                slot = slot_of(cols_ref, row, k, own_blocks, quarter_blocks)
                contrib[slot] += matmul(vals_ref[row, k], grad_block, (0, 0))
    chips = keep_ref.shape[0]
    nodes = own_blocks * size
    for chip in range(chips):
        even = contrib[2 * chip * own_blocks : (2 * chip + 1) * own_blocks]
        odd = contrib[(2 * chip + 1) * own_blocks : (2 * chip + 2) * own_blocks]
        keep_ref[chip] = even.reshape(nodes, -1)
        send_ref[chip * nodes : (chip + 1) * nodes] = odd.reshape(nodes, -1).astype(BF16)
    send_ref[chips * nodes :] = weight_part.astype(BF16)
    keep_weight_ref[...] = weight_part.astype(BF16)


def pair_kernel(keep_ref, keep_weight_ref, got_ref, own_ref, own_weight_ref, *outs):
    chips, nodes, _ = keep_ref.shape
    both = keep_weight_ref[...].astype(F32) + got_ref[chips * nodes :].astype(F32)
    both = both.astype(BF16)
    own_weight_ref[...] = both
    own_ref[...] = keep_ref[0] + got_ref[:nodes].astype(F32)
    for chip in range(1, chips):
        total = keep_ref[chip] + got_ref[chip * nodes : (chip + 1) * nodes].astype(F32)
        outs[chip - 1][:nodes] = total.astype(BF16)
        outs[chip - 1][nodes:] = both


def total_of(values):
    while len(values) > 1:
        values = [a + b for a, b in zip(values[::2], values[1::2])]
    return values[0]


def shape(dims, dtype):
    return jax.ShapeDtypeStruct(dims, dtype)


def body(cols, vals, features, weight, bias, cotangent):
    rows, count, size, _ = vals.shape
    nodes, width = features.shape
    dom, rep = lax.axis_size("dom"), lax.axis_size("rep")
    chips = dom // 2
    quarter_blocks = nodes * dom // size
    part = rows * size // rep
    params = pltpu.CompilerParams(vmem_limit_bytes=(8 + dom // 2) * 1024 * 1024)

    across = [swap(features, "dom", 2 * chip) for chip in range(1, chips)]
    beside = swap(features, "dom", 1)
    far = swap(jnp.concatenate(across), "dom", 1)
    partials = pl.pallas_call(
        functools.partial(aggregate_kernel, rep),
        out_shape=[shape((part, width), F32 if j == 0 else BF16) for j in range(rep)],
        in_specs=[SMEM] + [VMEM] * (chips + 3),
        out_specs=[VMEM] * rep,
        scratch_shapes=[pltpu.VMEM((quarter_blocks, size, width), BF16)],
        compiler_params=params,
    )(cols, vals, features, *across, beside, far)

    arrived = [partials[0]] + [swap(partials[j], "rep", j).astype(F32) for j in range(1, rep)]
    own_rows = total_of(arrived).astype(BF16)
    pieces = [own_rows] + [swap(own_rows, "rep", j) for j in range(1, rep)]

    output, send, keep, keep_weight = pl.pallas_call(
        functools.partial(layer_kernel, rep),
        out_shape=[
            shape((rows * size, width), BF16),
            shape((chips * nodes + width, width), BF16),
            shape((chips, nodes, width), F32),
            shape((width, width), BF16),
        ],
        in_specs=[SMEM] + [VMEM] * (4 + rep),
        out_specs=[VMEM] * 4,
        scratch_shapes=[pltpu.VMEM((quarter_blocks, size, width), F32)],
        compiler_params=params,
    )(cols, vals, cotangent, weight, bias.reshape(1, width), *pieces)

    own, own_weight, *sends = pl.pallas_call(
        pair_kernel,
        out_shape=[shape((nodes, width), F32), shape((width, width), BF16)]
        + [shape((nodes + width, width), BF16)] * (chips - 1),
        in_specs=[VMEM] * 3,
        out_specs=[VMEM] * (chips + 1),
        compiler_params=params,
    )(keep, keep_weight, swap(send, "dom", 1))

    got = [swap(sends[chip - 1], "dom", 2 * chip).astype(F32) for chip in range(1, chips)]
    feature_grad = total_of([own] + [value[:nodes] for value in got])
    weight_grad = total_of([own_weight.astype(F32)] + [value[nodes:] for value in got])
    return output, feature_grad, weight_grad


def solution(mesh):
    placed = (
        P("dom", "rep"),
        P("dom", "rep", None, None),
        P(("rep", "dom"), None),
        P(),
        P(),
        P("dom", None),
    )
    return jax.shard_map(
        body,
        mesh=mesh,
        in_specs=placed,
        out_specs=(P("dom", None), P(("rep", "dom"), None), P()),
        check_vma=False,
    )
```

time: 152 us -> 45.5 us (0.30)
  waiting for transfers between devices: 86 us -> 20.6 us
  blocking collectives: 42.5 us -> 0 us
  starting transfers between devices: 0.08 us -> 17.6 us
  between operations: 14.2 us -> 0.74 us
  Pallas kernels: 0 us -> 3.76 us
  local copies, waits for them, and re-layouts: 4.59 us -> 1.15 us
  matrix products: 2.88 us -> 0 us
    psum x1 -> x0, waiting for transfers between devices: 46.4 us -> none  [body(): weight_grad = lax.psum(weight_part, 'dom')]
    reduce_scatter x1 -> x0, waiting for transfers between devices: 39.5 us -> none  [body(): lax.psum_scatter(contrib, 'dom', scatter_dimension=0, tiled=True)]
    psum x1 -> x0, blocking collectives: 30.9 us -> none  [body(): summed = lax.psum(partial_sum, 'rep')]
    ppermute x0 -> x15, waiting for transfers between devices: none -> 20.6 us  [swap(): return lax.ppermute(value, axis, [(i, i ^ distance) for i in range(size)])]
    ppermute x0 -> x15, starting transfers between devices: none -> 17.6 us  [swap(): return lax.ppermute(value, axis, [(i, i ^ distance) for i in range(size)])]
    all_gather x1 -> x0, blocking collectives: 11.6 us -> none  [body(): lax.all_gather(features, 'dom', axis=0, tiled=True)]
    pallas_call x0 -> x3, Pallas kernels: none -> 3.76 us  [the longest x1 2.76 us: body(): pl.pallas_call(functools.partial(layer_kernel, rep), out_shape=[shape((ro...]
    dot_general x5 -> x0, matrix products: 2.88 us -> none  [the longest x1 1.12 us: body(): jnp.dot(aggregated, weight, preferred_element_type=jnp.float32) + bias]
  transfers between devices with their start and end apart: 2 -> 15, of which waited for: 2 -> 12; matrix products, arithmetic and copies ran while one was open for 2% -> 0% of each run, Pallas kernels for 0% -> 0%
where the time goes in v2:
time: 45.5 us; the launch traced here: 45.3 us
  waiting for transfers between devices  20.6 us (45%)
  starting transfers between devices  17.6 us (39%)
  Pallas kernels  3.76 us (8%)
  other arithmetic  1.42 us (3%)
  local copies, waits for them, and re-layouts  1.15 us (3%)
  between operations  0.74 us (2%)
    ppermute x15, waiting for transfers between devices, swap(): return lax.ppermute(value, axis, [(i, i ^ distance) for i in range(size)])  20.6 us
    ppermute x15, starting transfers between devices, swap(): return lax.ppermute(value, axis, [(i, i ^ distance) for i in range(size)])  17.6 us
    pallas_call x1, Pallas kernels, body(): pl.pallas_call(functools.partial(layer_kernel, rep), out_shape=[shape((ro...  2.76 us
    add x2, other arithmetic, total_of(): values = [a + b for a, b in zip(values[::2], values[1::2])]  1.33 us
    unnamed x13, local copies, waits for them, and re-layouts  1.15 us
    pallas_call x1, Pallas kernels, body(): pl.pallas_call(functools.partial(aggregate_kernel, rep), out_shape=[shape...  0.93 us
  transfers between devices with their start and end apart: 15, of which 12 were waited for; matrix products, arithmetic and copies ran while one was open for 0% of the time, Pallas kernels for 0%

profile of v2, /device:TPU:0, one launch (start us, length us, event | category | flops | bytes accessed | tf_op | source)
XLA Modules:
  0.0 45.3 jit_solution(6341257751501575632)
XLA Ops:
  0.6 4.0 %collective-permute-start.2 = (bf16[256,128]{1,0:T(8,128)(2,1)}, bf16[256,128]{1,0:T(8,128)(2,1)S(1)}, u32[]{:S(2)}, u32[]{:S(2)}) collective-permute-start(bf16[256,128]{1,0:T(8,128)(2,1)} %own_ref.1), channel_id=1, source_target_pairs={{0,6},{1,7},{2,4},{3,5},{4,2},{5,3},{6,0},{7,1},{8,14},{9,15},{10,... | collective-permute-start | bytes 196616 | tf_op jit(solution)/shard_map/ppermute | solution.py:18
  5.3 1.8 %collective-permute-done.2.refs_2_ = bf16[256,128]{1,0:T(8,128)(2,1)S(1)} collective-permute-done((bf16[256,128]{1,0:T(8,128)(2,1)}, bf16[256,128]{1,0:T(8,128)(2,1)S(1)}, u32[]{:S(2)}, u32[]{:S(2)}) %collective-permute-start.2) | collective-permute-done | bytes 65568 | tf_op jit(solution)/shard_map/ppermute | solution.py:18
  7.1 2.0 %collective-permute-done.1.refs_1_ = bf16[256,128]{1,0:T(8,128)(2,1)S(1)} collective-permute-done((bf16[256,128]{1,0:T(8,128)(2,1)}, bf16[256,128]{1,0:T(8,128)(2,1)S(1)}, u32[]{:S(2)}, u32[]{:S(2)}) %collective-permute-start.1) | collective-permute-done | bytes 65568 | tf_op jit(solution)/shard_map/ppermute | solution.py:18
  10.3 0.9 %collective-permute-done.3.refs_3_ = bf16[256,128]{1,0:T(8,128)(2,1)S(1)} collective-permute-done((bf16[256,128]{1,0:T(8,128)(2,1)S(1)}, bf16[256,128]{1,0:T(8,128)(2,1)S(1)}, u32[]{:S(2)}, u32[]{:S(2)}) %collective-permute-start.3) | collective-permute-done | bytes 65568 | tf_op jit(solution)/shard_map/ppermute | solution.py:18
  11.2 1.0 %copy-done = bf16[8,2,128,128]{3,2,1,0:T(8,128)(2,1)S(1)} copy-done((bf16[8,2,128,128]{3,2,1,0:T(8,128)(2,1)S(1)}, bf16[8,2,128,128]{3,2,1,0:T(8,128)(2,1)}, u32[]{:S(2)}) %copy-start) | copy-done | bytes 524312
  12.3 0.9 %shard_map.85 = (f32[256,128]{1,0:T(8,128)S(1)}, bf16[256,128]{1,0:T(8,128)(2,1)S(1)}, bf16[256,128]{1,0:T(8,128)(2,1)S(1)}, bf16[256,128]{1,0:T(8,128)(2,1)S(1)}) custom-call(s32[8,2]{1,0:T(8,128)S(1)} %copy.10.cols_ref, bf16[8,2,128,128]{3,2,1,0:T(8,128)(2,1)S(1)} %copy-done, bf16[256,128]{1,0:T(8,128)(2,1)S(1)} %copy-done.2, ...), custom_call_target="tpu_custom_call" | custom-call | tf_op jit(solution)/shard_map/pallas_call | solution.py:138
  13.2 1.6 %collective-permute-start.5 = (bf16[256,128]{1,0:T(8,128)(2,1)S(1)}, bf16[256,128]{1,0:T(8,128)(2,1)S(1)}, u32[]{:S(2)}, u32[]{:S(2)}) collective-permute-start(bf16[256,128]{1,0:T(8,128)(2,1)S(1)} %get-tuple-element.17), channel_id=1, source_target_pairs={{0,8},{8,0},{16,24},{24,16},{1,9},{9,1},{17,25},{25,17},{2,10},{10... | collective-permute-start | bytes 196616 | tf_op jit(solution)/shard_map/ppermute | solution.py:18
  14.8 2.6 %collective-permute-start.6 = (bf16[256,128]{1,0:T(8,128)(2,1)S(1)}, bf16[256,128]{1,0:T(8,128)(2,1)S(1)}, u32[]{:S(2)}, u32[]{:S(2)}) collective-permute-start(bf16[256,128]{1,0:T(8,128)(2,1)S(1)} %get-tuple-element.18), channel_id=1, source_target_pairs={{0,16},{8,24},{16,0},{24,8},{1,17},{9,25},{17,1},{25,9},{2,18},{10... | collective-permute-start | bytes 196616 | tf_op jit(solution)/shard_map/ppermute | solution.py:18
  17.7 4.8 %collective-permute-done.6 = bf16[256,128]{1,0:T(8,128)(2,1)S(1)} collective-permute-done((bf16[256,128]{1,0:T(8,128)(2,1)S(1)}, bf16[256,128]{1,0:T(8,128)(2,1)S(1)}, u32[]{:S(2)}, u32[]{:S(2)}) %collective-permute-start.6) | collective-permute-done | bytes 65568 | tf_op jit(solution)/shard_map/ppermute | solution.py:18
  22.4 1.2 %collective-permute-done.7 = bf16[256,128]{1,0:T(8,128)(2,1)S(1)} collective-permute-done((bf16[256,128]{1,0:T(8,128)(2,1)S(1)}, bf16[256,128]{1,0:T(8,128)(2,1)S(1)}, u32[]{:S(2)}, u32[]{:S(2)}) %collective-permute-start.7) | collective-permute-done | bytes 65568 | tf_op jit(solution)/shard_map/ppermute | solution.py:18
  23.7 2.1 %collective-permute-start.10 = (bf16[256,128]{1,0:T(8,128)(2,1)S(1)}, bf16[256,128]{1,0:T(8,128)(2,1)S(1)}, u32[]{:S(2)}, u32[]{:S(2)}) collective-permute-start(bf16[256,128]{1,0:T(8,128)(2,1)S(1)} %add_convert_fusion.refs_0_), channel_id=1, source_target_pairs={{0,24},{8,16},{16,8},{24,0},{1,25},{9,17},{17,9},{25,1},{2,26},{10... | collective-permute-start | bytes 196616 | tf_op jit(solution)/shard_map/ppermute | solution.py:18
  26.1 2.0 %collective-permute-start.8 = (bf16[256,128]{1,0:T(8,128)(2,1)S(1)}, bf16[256,128]{1,0:T(8,128)(2,1)S(1)}, u32[]{:S(2)}, u32[]{:S(2)}) collective-permute-start(bf16[256,128]{1,0:T(8,128)(2,1)S(1)} %add_convert_fusion.refs_0_), channel_id=1, source_target_pairs={{0,8},{8,0},{16,24},{24,16},{1,9},{9,1},{17,25},{25,17},{2,10},{10... | collective-permute-start | bytes 196616 | tf_op jit(solution)/shard_map/ppermute | solution.py:18
  28.1 1.8 %collective-permute-done.10.refs_3_ = bf16[256,128]{1,0:T(8,128)(2,1)S(1)} collective-permute-done((bf16[256,128]{1,0:T(8,128)(2,1)S(1)}, bf16[256,128]{1,0:T(8,128)(2,1)S(1)}, u32[]{:S(2)}, u32[]{:S(2)}) %collective-permute-start.10) | collective-permute-done | bytes 65568 | tf_op jit(solution)/shard_map/ppermute | solution.py:18
  29.9 1.6 %collective-permute-done.9.refs_2_ = bf16[256,128]{1,0:T(8,128)(2,1)S(1)} collective-permute-done((bf16[256,128]{1,0:T(8,128)(2,1)S(1)}, bf16[256,128]{1,0:T(8,128)(2,1)S(1)}, u32[]{:S(2)}, u32[]{:S(2)}) %collective-permute-start.9) | collective-permute-done | bytes 65568 | tf_op jit(solution)/shard_map/ppermute | solution.py:18
  31.6 2.8 %shard_map.86 = (bf16[1024,128]{1,0:T(8,128)(2,1)}, bf16[1152,128]{1,0:T(8,128)(2,1)S(1)}, f32[4,256,128]{2,1,0:T(8,128)S(1)}, bf16[128,128]{1,0:T(8,128)(2,1)S(1)}) custom-call(s32[8,2]{1,0:T(8,128)S(1)} %copy.10.cols_ref, bf16[8,2,128,128]{3,2,1,0:T(8,128)(2,1)S(1)} %copy-done, bf16[1024,128]{1,0:T(8,128)(2,1)S(1)} %copy-done.1, ...), custom_call_target="tpu_custom_call" | custom-call | tf_op jit(solution)/shard_map/pallas_call | solution.py:151
  34.3 1.6 %collective-permute-done.11.got_ref = bf16[1152,128]{1,0:T(8,128)(2,1)S(1)} collective-permute-done((bf16[1152,128]{1,0:T(8,128)(2,1)S(1)}, bf16[1152,128]{1,0:T(8,128)(2,1)S(1)}, u32[]{:S(2)}, u32[]{:S(2)}) %collective-permute-start.11) | collective-permute-done | bytes 294944 | tf_op jit(solution)/shard_map/ppermute | solution.py:18
  36.0 0.6 %collective-permute-start.12 = (bf16[384,128]{1,0:T(8,128)(2,1)S(1)}, bf16[384,128]{1,0:T(8,128)(2,1)S(1)}, u32[]{:S(2)}, u32[]{:S(2)}) collective-permute-start(bf16[384,128]{1,0:T(8,128)(2,1)S(1)} %get-tuple-element.25), channel_id=1, source_target_pairs={{0,2},{1,3},{2,0},{3,1},{4,6},{5,7},{6,4},{7,5},{8,10},{9,11},{10,... | collective-permute-start | bytes 294920 | tf_op jit(solution)/shard_map/ppermute | solution.py:18
  36.6 1.5 %collective-permute-start.13 = (bf16[384,128]{1,0:T(8,128)(2,1)S(1)}, bf16[384,128]{1,0:T(8,128)(2,1)S(1)}, u32[]{:S(2)}, u32[]{:S(2)}) collective-permute-start(bf16[384,128]{1,0:T(8,128)(2,1)S(1)} %get-tuple-element.26), channel_id=1, source_target_pairs={{0,4},{1,5},{2,6},{3,7},{4,0},{5,1},{6,2},{7,3},{8,12},{9,13},{10,... | collective-permute-start | bytes 294920 | tf_op jit(solution)/shard_map/ppermute | solution.py:18
  38.1 1.4 %collective-permute-start.14 = (bf16[384,128]{1,0:T(8,128)(2,1)S(1)}, bf16[384,128]{1,0:T(8,128)(2,1)S(1)}, u32[]{:S(2)}, u32[]{:S(2)}) collective-permute-start(bf16[384,128]{1,0:T(8,128)(2,1)S(1)} %get-tuple-element.27), channel_id=1, source_target_pairs={{0,6},{1,7},{2,4},{3,5},{4,2},{5,3},{6,0},{7,1},{8,14},{9,15},{10,... | collective-permute-start | bytes 294920 | tf_op jit(solution)/shard_map/ppermute | solution.py:18
  39.5 2.1 %collective-permute-done.12 = bf16[384,128]{1,0:T(8,128)(2,1)S(1)} collective-permute-done((bf16[384,128]{1,0:T(8,128)(2,1)S(1)}, bf16[384,128]{1,0:T(8,128)(2,1)S(1)}, u32[]{:S(2)}, u32[]{:S(2)}) %collective-permute-start.12) | collective-permute-done | bytes 98336 | tf_op jit(solution)/shard_map/ppermute | solution.py:18
  41.6 0.7 %collective-permute-done.13 = bf16[384,128]{1,0:T(8,128)(2,1)S(1)} collective-permute-done((bf16[384,128]{1,0:T(8,128)(2,1)S(1)}, bf16[384,128]{1,0:T(8,128)(2,1)S(1)}, u32[]{:S(2)}, u32[]{:S(2)}) %collective-permute-start.13) | collective-permute-done | bytes 98336 | tf_op jit(solution)/shard_map/ppermute | solution.py:18
  42.4 1.6 %collective-permute-done.14 = bf16[384,128]{1,0:T(8,128)(2,1)S(1)} collective-permute-done((bf16[384,128]{1,0:T(8,128)(2,1)S(1)}, bf16[384,128]{1,0:T(8,128)(2,1)S(1)}, u32[]{:S(2)}, u32[]{:S(2)}) %collective-permute-start.14) | collective-permute-done | bytes 98336 | tf_op jit(solution)/shard_map/ppermute | solution.py:18
  44.0 0.7 %fusion = f32[256,128]{1,0:T(8,128)} fusion(f32[384,128]{1,0:T(8,128)S(1)} %convert_element_type.30, f32[384,128]{1,0:T(8,128)S(1)} %convert_element_type.29, f32[256,128]{1,0:T(8,128)S(1)} %get-tuple-element.24, f32[384,128]{1,0:T(8,128)S(1)} %convert_element_type.28), kind=kLoop, calls=%fused_computation.2 | loop fusion | flops 98304 | bytes 655360 | tf_op jit(solution)/shard_map/add | solution.py:118
  44.7 0.6 %fusion.1 = f32[128,128]{1,0:T(8,128)} fusion(f32[384,128]{1,0:T(8,128)S(1)} %convert_element_type.30, f32[384,128]{1,0:T(8,128)S(1)} %convert_element_type.29, f32[384,128]{1,0:T(8,128)S(1)} %convert_element_type.28, bf16[128,128]{1,0:T(8,128)(2,1)S(1)} %get-tuple-element.28), kind=kLoop, calls=%fused_computation.6 | loop fusion | flops 65536 | bytes 294912 | tf_op jit(solution)/shard_map/add | solution.py:118
  (29 shorter events, 2.5 us)
Async XLA Ops:
  0.6 9.1 %copy-start.2 = (bf16[256,128]{1,0:T(8,128)(2,1)S(1)}, bf16[256,128]{1,0:T(8,128)(2,1)}, u32[]{:S(2)}) copy-start(bf16[256,128]{1,0:T(8,128)(2,1)} %own_ref.1) | copy-start | bytes 196612
  0.6 9.6 %copy-start.5 = (s32[8,2]{0,1:T(2,128)S(1)}, s32[8,2]{0,1:T(2,128)}, u32[]{:S(2)}) copy-start(s32[8,2]{0,1:T(2,128)} %param.6) | copy-start | bytes 196
  0.6 6.4 %collective-permute-start.2 = (bf16[256,128]{1,0:T(8,128)(2,1)}, bf16[256,128]{1,0:T(8,128)(2,1)S(1)}, u32[]{:S(2)}, u32[]{:S(2)}) collective-permute-start(bf16[256,128]{1,0:T(8,128)(2,1)} %own_ref.1), channel_id=1, source_target_pairs={{0,6},{1,7},{2,4},{3,5},{4,2},{5,3},{6,0},{7,1},{8,14},{9,15},{10,... | collective-permute-start | bytes 196616 | tf_op jit(solution)/shard_map/ppermute | solution.py:18
  4.6 4.5 %collective-permute-start.1 = (bf16[256,128]{1,0:T(8,128)(2,1)}, bf16[256,128]{1,0:T(8,128)(2,1)S(1)}, u32[]{:S(2)}, u32[]{:S(2)}) collective-permute-start(bf16[256,128]{1,0:T(8,128)(2,1)} %own_ref.1), channel_id=1, source_target_pairs={{0,4},{1,5},{2,6},{3,7},{4,0},{5,1},{6,2},{7,3},{8,12},{9,13},{10,... | collective-permute-start | bytes 196616 | tf_op jit(solution)/shard_map/ppermute | solution.py:18
  5.1 4.5 %collective-permute-start = (bf16[256,128]{1,0:T(8,128)(2,1)}, bf16[256,128]{1,0:T(8,128)(2,1)S(1)}, u32[]{:S(2)}, u32[]{:S(2)}) collective-permute-start(bf16[256,128]{1,0:T(8,128)(2,1)} %own_ref.1), channel_id=1, source_target_pairs={{0,2},{1,3},{2,0},{3,1},{4,6},{5,7},{6,4},{7,5},{8,10},{9,11},{10,... | collective-permute-start | bytes 196616 | tf_op jit(solution)/shard_map/ppermute | solution.py:18
  9.6 1.6 %collective-permute-start.4 = (bf16[768,128]{1,0:T(8,128)(2,1)S(1)}, bf16[768,128]{1,0:T(8,128)(2,1)S(1)}, u32[]{:S(2)}, u32[]{:S(2)}) collective-permute-start(bf16[768,128]{1,0:T(8,128)(2,1)S(1)} %pad_maximum_fusion), channel_id=1, source_target_pairs={{0,1},{1,0},{2,3},{3,2},{4,5},{5,4},{6,7},{7,6},{8,9},{9,8},{10,11... | collective-permute-start | bytes 589832 | tf_op jit(solution)/shard_map/ppermute | solution.py:18
  9.7 1.5 %collective-permute-start.3 = (bf16[256,128]{1,0:T(8,128)(2,1)S(1)}, bf16[256,128]{1,0:T(8,128)(2,1)S(1)}, u32[]{:S(2)}, u32[]{:S(2)}) collective-permute-start(bf16[256,128]{1,0:T(8,128)(2,1)S(1)} %copy-done.2), channel_id=1, source_target_pairs={{0,1},{1,0},{2,3},{3,2},{4,5},{5,4},{6,7},{7,6},{8,9},{9,8},{10,11... | collective-permute-start | bytes 196616 | tf_op jit(solution)/shard_map/ppermute | solution.py:18
  11.2 1.0 %copy-start = (bf16[8,2,128,128]{3,2,1,0:T(8,128)(2,1)S(1)}, bf16[8,2,128,128]{3,2,1,0:T(8,128)(2,1)}, u32[]{:S(2)}) copy-start(bf16[8,2,128,128]{3,2,1,0:T(8,128)(2,1)} %vals_ref.3) | copy-start | bytes 1572868
  13.2 18.4 %copy-start.1 = (bf16[1024,128]{1,0:T(8,128)(2,1)S(1)}, bf16[1024,128]{1,0:T(8,128)(2,1)}, u32[]{:S(2)}) copy-start(bf16[1024,128]{1,0:T(8,128)(2,1)} %cotangent_ref.1) | copy-start | bytes 786436
  13.2 4.5 %collective-permute-start.5 = (bf16[256,128]{1,0:T(8,128)(2,1)S(1)}, bf16[256,128]{1,0:T(8,128)(2,1)S(1)}, u32[]{:S(2)}, u32[]{:S(2)}) collective-permute-start(bf16[256,128]{1,0:T(8,128)(2,1)S(1)} %get-tuple-element.17), channel_id=1, source_target_pairs={{0,8},{8,0},{16,24},{24,16},{1,9},{9,1},{17,25},{25,17},{2,10},{10... | collective-permute-start | bytes 196616 | tf_op jit(solution)/shard_map/ppermute | solution.py:18
  14.8 7.6 %collective-permute-start.6 = (bf16[256,128]{1,0:T(8,128)(2,1)S(1)}, bf16[256,128]{1,0:T(8,128)(2,1)S(1)}, u32[]{:S(2)}, u32[]{:S(2)}) collective-permute-start(bf16[256,128]{1,0:T(8,128)(2,1)S(1)} %get-tuple-element.18), channel_id=1, source_target_pairs={{0,16},{8,24},{16,0},{24,8},{1,17},{9,25},{17,1},{25,9},{2,18},{10... | collective-permute-start | bytes 196616 | tf_op jit(solution)/shard_map/ppermute | solution.py:18
  17.4 6.2 %collective-permute-start.7 = (bf16[256,128]{1,0:T(8,128)(2,1)S(1)}, bf16[256,128]{1,0:T(8,128)(2,1)S(1)}, u32[]{:S(2)}, u32[]{:S(2)}) collective-permute-start(bf16[256,128]{1,0:T(8,128)(2,1)S(1)} %get-tuple-element.19), channel_id=1, source_target_pairs={{0,24},{8,16},{16,8},{24,0},{1,25},{9,17},{17,9},{25,1},{2,26},{10... | collective-permute-start | bytes 196616 | tf_op jit(solution)/shard_map/ppermute | solution.py:18
  23.6 8.0 %copy-start.3 = (bf16[128,128]{1,0:T(8,128)(2,1)S(1)}, bf16[128,128]{1,0:T(8,128)(2,1)}, u32[]{:S(2)}) copy-start(bf16[128,128]{1,0:T(8,128)(2,1)} %weight_ref.1) | copy-start | bytes 98308
  23.6 7.9 %copy-start.4 = (f32[128]{0:T(128)S(1)}, f32[128]{0:T(128)}, u32[]{:S(2)}) copy-start(f32[128]{0:T(128)} %param.10) | copy-start | bytes 1540
  23.7 6.2 %collective-permute-start.10 = (bf16[256,128]{1,0:T(8,128)(2,1)S(1)}, bf16[256,128]{1,0:T(8,128)(2,1)S(1)}, u32[]{:S(2)}, u32[]{:S(2)}) collective-permute-start(bf16[256,128]{1,0:T(8,128)(2,1)S(1)} %add_convert_fusion.refs_0_), channel_id=1, source_target_pairs={{0,24},{8,16},{16,8},{24,0},{1,25},{9,17},{17,9},{25,1},{2,26},{10... | collective-permute-start | bytes 196616 | tf_op jit(solution)/shard_map/ppermute | solution.py:18
  25.8 5.7 %collective-permute-start.9 = (bf16[256,128]{1,0:T(8,128)(2,1)S(1)}, bf16[256,128]{1,0:T(8,128)(2,1)S(1)}, u32[]{:S(2)}, u32[]{:S(2)}) collective-permute-start(bf16[256,128]{1,0:T(8,128)(2,1)S(1)} %add_convert_fusion.refs_0_), channel_id=1, source_target_pairs={{0,16},{8,24},{16,0},{24,8},{1,17},{9,25},{17,1},{25,9},{2,18},{10... | collective-permute-start | bytes 196616 | tf_op jit(solution)/shard_map/ppermute | solution.py:18
  26.1 5.4 %collective-permute-start.8 = (bf16[256,128]{1,0:T(8,128)(2,1)S(1)}, bf16[256,128]{1,0:T(8,128)(2,1)S(1)}, u32[]{:S(2)}, u32[]{:S(2)}) collective-permute-start(bf16[256,128]{1,0:T(8,128)(2,1)S(1)} %add_convert_fusion.refs_0_), channel_id=1, source_target_pairs={{0,8},{8,0},{16,24},{24,16},{1,9},{9,1},{17,25},{25,17},{2,10},{10... | collective-permute-start | bytes 196616 | tf_op jit(solution)/shard_map/ppermute | solution.py:18
  34.3 1.6 %collective-permute-start.11 = (bf16[1152,128]{1,0:T(8,128)(2,1)S(1)}, bf16[1152,128]{1,0:T(8,128)(2,1)S(1)}, u32[]{:S(2)}, u32[]{:S(2)}) collective-permute-start(bf16[1152,128]{1,0:T(8,128)(2,1)S(1)} %get-tuple-element.23), channel_id=1, source_target_pairs={{0,1},{1,0},{2,3},{3,2},{4,5},{5,4},{6,7},{7,6},{8,9},{9,8},{10,11... | collective-permute-start | bytes 884744 | tf_op jit(solution)/shard_map/ppermute | solution.py:18
  36.0 5.6 %collective-permute-start.12 = (bf16[384,128]{1,0:T(8,128)(2,1)S(1)}, bf16[384,128]{1,0:T(8,128)(2,1)S(1)}, u32[]{:S(2)}, u32[]{:S(2)}) collective-permute-start(bf16[384,128]{1,0:T(8,128)(2,1)S(1)} %get-tuple-element.25), channel_id=1, source_target_pairs={{0,2},{1,3},{2,0},{3,1},{4,6},{5,7},{6,4},{7,5},{8,10},{9,11},{10,... | collective-permute-start | bytes 294920 | tf_op jit(solution)/shard_map/ppermute | solution.py:18
  36.6 5.8 %collective-permute-start.13 = (bf16[384,128]{1,0:T(8,128)(2,1)S(1)}, bf16[384,128]{1,0:T(8,128)(2,1)S(1)}, u32[]{:S(2)}, u32[]{:S(2)}) collective-permute-start(bf16[384,128]{1,0:T(8,128)(2,1)S(1)} %get-tuple-element.26), channel_id=1, source_target_pairs={{0,4},{1,5},{2,6},{3,7},{4,0},{5,1},{6,2},{7,3},{8,12},{9,13},{10,... | collective-permute-start | bytes 294920 | tf_op jit(solution)/shard_map/ppermute | solution.py:18
  38.1 5.8 %collective-permute-start.14 = (bf16[384,128]{1,0:T(8,128)(2,1)S(1)}, bf16[384,128]{1,0:T(8,128)(2,1)S(1)}, u32[]{:S(2)}, u32[]{:S(2)}) collective-permute-start(bf16[384,128]{1,0:T(8,128)(2,1)S(1)} %get-tuple-element.27), channel_id=1, source_target_pairs={{0,6},{1,7},{2,4},{3,5},{4,2},{5,3},{6,0},{7,1},{8,14},{9,15},{10,... | collective-permute-start | bytes 294920 | tf_op jit(solution)/shard_map/ppermute | solution.py:18

commit v3 on v2

v3 whole, which is shorter than its diff:
```python
import functools

import jax
import jax.numpy as jnp
from jax import lax
from jax.experimental import pallas as pl
from jax.experimental.pallas import tpu as pltpu
from jax.sharding import PartitionSpec as P

BF16 = jnp.bfloat16
F32 = jnp.float32
VMEM = pl.BlockSpec(memory_space=pltpu.VMEM)
SMEM = pl.BlockSpec(memory_space=pltpu.SMEM)


def swap(value, axis, distance):
    size = lax.axis_size(axis)
    return lax.ppermute(value, axis, [(i, i ^ distance) for i in range(size)])


def matmul(a, b, contract):
    return lax.dot_general(a, b, ((contract[:1], contract[1:]), ((), ())), preferred_element_type=F32)


def slot_of(cols_ref, row, k, own_blocks, quarter_blocks):
    col = cols_ref[row, k] - lax.axis_index("rep") * quarter_blocks
    owner = lax.div(col, jnp.int32(own_blocks)) ^ lax.axis_index("dom")
    return owner, lax.rem(col, jnp.int32(own_blocks))


def transpose_kernel(vals_ref, near_ref, flipped_ref):
    rows, count, size, _ = vals_ref.shape
    near_ref[...] = vals_ref[...]
    for row in range(rows):
        for k in range(count):
            flipped_ref[row, k * size : (k + 1) * size] = vals_ref[row, k].T


def join_kernel(order, *refs):
    pieces, out_ref = refs[: len(order)], refs[-1]
    nodes = pieces[0].shape[0]
    for chip, piece in zip(order, pieces):
        out_ref[chip * nodes : (chip + 1) * nodes] = piece[...]


def aggregate_kernel(rep, own_blocks, j, cols_ref, vals_ref, mine_ref, far_ref, out_ref):
    rows, count, size, _ = vals_ref.shape
    quarter_blocks = 2 * mine_ref.shape[0] // size
    share = rows // rep
    target = lax.axis_index("rep") ^ j
    for i in range(share):
        row = target * share + i
        total = None
        for k in range(count):
            owner, rest = slot_of(cols_ref, row, k, own_blocks, quarter_blocks)
            index = (owner >> 1) * own_blocks + rest
            here = pl.ds(pl.multiple_of(index * size, size), size)
            block = jnp.where((owner & 1) == 1, far_ref[here, :], mine_ref[here, :])
            term = matmul(vals_ref[row, k], block, (1, 0))
            total = term if total is None else total + term
        out_ref[i * size : (i + 1) * size] = total.astype(out_ref.dtype)


def layer_kernel(
    rep, count, own_blocks, j, cols_ref, flipped_ref, cotangent_ref, weight_ref, bias_ref, *refs
):
    first, last = j == 0, j == 1
    piece_ref, refs = refs[0], refs[1:]
    if not first:
        (contrib_in, weight_in), refs = refs[:2], refs[2:]
    if last:
        output_ref, send_ref, keep_ref, keep_weight_ref, contrib = refs
    else:
        output_ref, contrib, weight_out = refs
    rows, _, size = flipped_ref.shape
    share = rows // rep
    quarter_blocks = contrib.shape[0]
    nodes = own_blocks * size
    contrib[...] = jnp.zeros_like(contrib) if first else contrib_in[...]

    target = lax.axis_index("rep") ^ j
    aggregated = piece_ref[...]
    part = aggregated.shape[0]
    here = pl.ds(pl.multiple_of(target * part, part), part)
    hidden = matmul(aggregated, weight_ref[...], (1, 0)) + bias_ref[...]
    gate_prob = jax.nn.sigmoid(hidden)
    output_ref[...] = (hidden * gate_prob).astype(BF16)
    grad_hidden = (
        cotangent_ref[here, :].astype(F32) * gate_prob * (1.0 + hidden * (1.0 - gate_prob))
    ).astype(BF16)
    weight_part = matmul(aggregated, grad_hidden, (0, 0))
    if not first:
        weight_part = weight_in[...] + weight_part
    grad_agg = matmul(grad_hidden, weight_ref[...], (1, 1)).astype(BF16)
    for i in range(share):
        row = target * share + i
        terms = matmul(flipped_ref[row], grad_agg[i * size : (i + 1) * size], (1, 0))
        for k in range(count):
            owner, rest = slot_of(cols_ref, row, k, own_blocks, quarter_blocks)
            contrib[owner * own_blocks + rest] += terms[k * size : (k + 1) * size]
    if not last:
        weight_out[...] = weight_part
        return
    chips = keep_ref.shape[0]
    for chip in range(chips):
        even = contrib[2 * chip * own_blocks : (2 * chip + 1) * own_blocks]
        odd = contrib[(2 * chip + 1) * own_blocks : (2 * chip + 2) * own_blocks]
        keep_ref[chip] = even.reshape(nodes, -1)
        send_ref[chip * nodes : (chip + 1) * nodes] = odd.reshape(nodes, -1).astype(BF16)
    send_ref[chips * nodes :] = weight_part.astype(BF16)
    keep_weight_ref[...] = weight_part.astype(BF16)


def add_kernel(a_ref, b_ref, out_ref):
    out_ref[...] = (a_ref[...] + b_ref[...].astype(F32)).astype(out_ref.dtype)


def place_kernel(order, *refs):
    pieces, out_ref = refs[:-1], refs[-1]
    part = pieces[0].shape[0]
    for j, piece in zip(order, pieces):
        target = lax.axis_index("rep") ^ j
        out_ref[pl.ds(pl.multiple_of(target * part, part), part), :] = piece[...]


def pair_kernel(keep_ref, keep_weight_ref, got_ref, own_ref, own_weight_ref, *outs):
    chips, nodes, _ = keep_ref.shape
    both = keep_weight_ref[...].astype(F32) + got_ref[chips * nodes :].astype(F32)
    both = both.astype(BF16)
    own_weight_ref[...] = both
    own_ref[...] = keep_ref[0] + got_ref[:nodes].astype(F32)
    for chip in range(1, chips):
        total = keep_ref[chip] + got_ref[chip * nodes : (chip + 1) * nodes].astype(F32)
        outs[chip - 1][:nodes] = total.astype(BF16)
        outs[chip - 1][nodes:] = both


def total_of(values):
    while len(values) > 1:
        values = [a + b for a, b in zip(values[::2], values[1::2])]
    return values[0]


def half_kernel(levels, *refs):
    for level in range(1, levels):
        first = 1 << level
        got = refs[: -levels + 1][::-1][first - 2 : 2 * first - 2]
        refs[level - levels][...] = total_of([g[...].astype(F32) for g in got])


def final_kernel(own_ref, own_weight_ref, got_ref, *refs):
    later, (feature_ref, weight_ref) = refs[:-2], refs[-2:]
    nodes = own_ref.shape[0]
    feature = own_ref[...] + got_ref[:nodes].astype(F32)
    weight = own_weight_ref[...].astype(F32) + got_ref[nodes:].astype(F32)
    for value in later:
        feature += value[:nodes]
        weight += value[nodes:]
    feature_ref[...] = feature
    weight_ref[...] = weight


def shape(dims, dtype):
    return jax.ShapeDtypeStruct(dims, dtype)


def body(cols, vals, features, weight, bias, cotangent):
    rows, count, size, _ = vals.shape
    nodes, width = features.shape
    dom, rep = lax.axis_size("dom"), lax.axis_size("rep")
    chips = dom // 2
    own_blocks = nodes // size
    quarter_blocks = own_blocks * dom
    part = rows * size // rep
    params = pltpu.CompilerParams(vmem_limit_bytes=(8 + dom // 2) * 1024 * 1024)

    def call(kernel, out_shape, in_specs, scratch=()):
        single = not isinstance(out_shape, list)
        return pl.pallas_call(
            kernel,
            out_shape=out_shape,
            in_specs=in_specs,
            out_specs=VMEM if single else [VMEM] * len(out_shape),
            scratch_shapes=scratch,
            compiler_params=params,
        )

    near, flipped = call(
        transpose_kernel,
        [shape(vals.shape, BF16), shape((rows, count * size, size), BF16)],
        [VMEM],
    )(vals)
    order = list(range(chips - 1, -1, -1))
    across = [swap(features, "dom", 2 * chip) for chip in order[:-1]] + [features]
    mine = call(
        functools.partial(join_kernel, order), shape((chips * nodes, width), BF16), [VMEM] * (chips + 1)
    )(*across, near)
    far = swap(mine, "dom", 1)

    arrived = {}
    for j in range(rep - 1, -1, -1):
        partial_sum = call(
            functools.partial(aggregate_kernel, rep, own_blocks, j),
            shape((part, width), BF16 if j else F32),
            [SMEM, VMEM, VMEM, VMEM],
        )(cols, near, mine, far)
        arrived[j] = swap(partial_sum, "rep", j) if j else partial_sum
    own_rows = arrived[0]
    for j in range(rep - 1, 0, -1):
        own_rows = call(add_kernel, shape((part, width), F32 if j > 1 else BF16), [VMEM] * 2)(
            own_rows, arrived[j]
        )

    pieces = {0: own_rows}
    for j in range(rep - 1, 0, -1):
        pieces[j] = swap(own_rows, "rep", j)

    outputs, carried = [], []
    for j, piece in pieces.items():
        if j != 1:
            outs = [shape((quarter_blocks, size, width), F32), shape((width, width), F32)]
            scratch = []
        else:
            outs = [
                shape((chips * nodes + width, width), BF16),
                shape((chips, nodes, width), F32),
                shape((width, width), BF16),
            ]
            scratch = [pltpu.VMEM((quarter_blocks, size, width), F32)]
        output, *carried = call(
            functools.partial(layer_kernel, rep, count, own_blocks, j),
            [shape((part, width), BF16)] + outs,
            [SMEM] + [VMEM] * (5 + len(carried)),
            scratch,
        )(cols, flipped, cotangent, weight, bias.reshape(1, width), piece, *carried)
        outputs.append(output)
    send, keep, keep_weight = carried

    own, own_weight, *sends = call(
        pair_kernel,
        [shape((nodes, width), F32), shape((width, width), BF16)]
        + [shape((nodes + width, width), BF16)] * (chips - 1),
        [VMEM] * 3,
    )(keep, keep_weight, swap(send, "dom", 1))
    got = {chip: swap(sends[chip - 1], "dom", 2 * chip) for chip in range(chips - 1, 0, -1)}
    output = call(
        functools.partial(place_kernel, list(pieces)), shape((rows * size, width), BF16), [VMEM] * rep
    )(*outputs)
    levels = chips.bit_length() - 1
    later = call(
        functools.partial(half_kernel, levels), [shape((nodes + width, width), F32)] * (levels - 1), [VMEM] * (chips - 2)
    )(*[got[chip] for chip in range(chips - 1, 1, -1)])
    feature_grad, weight_grad = call(
        final_kernel,
        [shape((nodes, width), F32), shape((width, width), F32)],
        [VMEM] * (levels + 2),
    )(own, own_weight, got[1], *later)
    return output, feature_grad, weight_grad


def solution(mesh):
    placed = (
        P("dom", "rep"),
        P("dom", "rep", None, None),
        P(("rep", "dom"), None),
        P(),
        P(),
        P("dom", None),
    )
    return jax.shard_map(
        body,
        mesh=mesh,
        in_specs=placed,
        out_specs=(P("dom", None), P(("rep", "dom"), None), P()),
        check_vma=False,
    )
```

time: 45.5 us -> 44 us (0.967)
  waiting for transfers between devices: 20.6 us -> 13.9 us
  Pallas kernels: 3.76 us -> 9.46 us
  other arithmetic: 1.42 us -> 0 us
  local copies, waits for them, and re-layouts: 1.15 us -> 2.37 us
    ppermute x15 -> x14, waiting for transfers between devices: 20.6 us -> 13.9 us  [swap(): return lax.ppermute(value, axis, [(i, i ^ distance) for i in range(size)])]
    pallas_call x3 -> x17, Pallas kernels: 3.76 us -> 9.46 us  [the longest x4 4.52 us: body(): call(functools.partial(layer_kernel, rep, count, own_blocks, j), [shape((...]
    add x2 -> x0, other arithmetic: 1.33 us -> none  [total_of(): values = [a + b for a, b in zip(values[::2], values[1::2])]]
    unnamed x13, local copies, waits for them, and re-layouts: 1.15 us -> 2.37 us
    ppermute x15 -> x14, starting transfers between devices: 17.6 us -> 17.3 us  [swap(): return lax.ppermute(value, axis, [(i, i ^ distance) for i in range(size)])]
  transfers between devices with their start and end apart: 15 -> 14, of which waited for: 12 -> 10; matrix products, arithmetic and copies ran while one was open for 0% -> 0% of each run, Pallas kernels for 0% -> 15%
where the time goes in v3:
time: 44 us; the launch traced here: 43.9 us
  starting transfers between devices  17.3 us (39%)
  waiting for transfers between devices  13.9 us (32%)
  Pallas kernels  9.46 us (22%)
  local copies, waits for them, and re-layouts  2.37 us (5%)
  between operations  0.81 us (2%)
    ppermute x14, starting transfers between devices, swap(): return lax.ppermute(value, axis, [(i, i ^ distance) for i in range(size)])  17.3 us
    ppermute x14, waiting for transfers between devices, swap(): return lax.ppermute(value, axis, [(i, i ^ distance) for i in range(size)])  13.9 us
    pallas_call x4, Pallas kernels, body(): call(functools.partial(layer_kernel, rep, count, own_blocks, j), [shape((...  4.52 us
    pallas_call x4, Pallas kernels, body(): call(functools.partial(aggregate_kernel, rep, own_blocks, j), shape((part...  3.19 us
    unnamed x13, local copies, waits for them, and re-layouts  2.37 us
  transfers between devices with their start and end apart: 14, of which 10 were waited for; matrix products, arithmetic and copies ran while one was open for 0% of the time, Pallas kernels for 15%

profile of v3, /device:TPU:0, one launch (start us, length us, event | category | flops | bytes accessed | tf_op | source)
XLA Modules:
  0.0 43.9 jit_solution(13797739987440803871)
XLA Ops:
  0.6 3.0 %collective-permute-start.1 = (bf16[256,128]{1,0:T(8,128)(2,1)}, bf16[256,128]{1,0:T(8,128)(2,1)S(1)}, u32[]{:S(2)}, u32[]{:S(2)}) collective-permute-start(bf16[256,128]{1,0:T(8,128)(2,1)} %refs_3_.1), channel_id=1, source_target_pairs={{0,4},{1,5},{2,6},{3,7},{4,0},{5,1},{6,2},{7,3},{8,12},{9,13},{10,... | collective-permute-start | bytes 196616 | tf_op jit(solution)/shard_map/ppermute | solution.py:18
  3.7 1.4 %collective-permute-start = (bf16[256,128]{1,0:T(8,128)(2,1)}, bf16[256,128]{1,0:T(8,128)(2,1)S(1)}, u32[]{:S(2)}, u32[]{:S(2)}) collective-permute-start(bf16[256,128]{1,0:T(8,128)(2,1)} %refs_3_.1), channel_id=1, source_target_pairs={{0,6},{1,7},{2,4},{3,5},{4,2},{5,3},{6,0},{7,1},{8,14},{9,15},{10,... | collective-permute-start | bytes 196616 | tf_op jit(solution)/shard_map/ppermute | solution.py:18
  5.2 1.0 %copy-done.2 = bf16[8,2,128,128]{3,2,1,0:T(8,128)(2,1)S(1)} copy-done((bf16[8,2,128,128]{3,2,1,0:T(8,128)(2,1)S(1)}, bf16[8,2,128,128]{3,2,1,0:T(8,128)(2,1)}, u32[]{:S(2)}) %copy-start.2) | copy-done | bytes 524312
  6.7 2.9 %collective-permute-done.refs_0_ = bf16[256,128]{1,0:T(8,128)(2,1)S(1)} collective-permute-done((bf16[256,128]{1,0:T(8,128)(2,1)}, bf16[256,128]{1,0:T(8,128)(2,1)S(1)}, u32[]{:S(2)}, u32[]{:S(2)}) %collective-permute-start) | collective-permute-done | bytes 65568 | tf_op jit(solution)/shard_map/ppermute | solution.py:18
  10.3 0.9 %collective-permute-done.3.far_ref = bf16[1024,128]{1,0:T(8,128)(2,1)S(1)} collective-permute-done((bf16[1024,128]{1,0:T(8,128)(2,1)S(1)}, bf16[1024,128]{1,0:T(8,128)(2,1)S(1)}, u32[]{:S(2)}, u32[]{:S(2)}) %collective-permute-start.3) | collective-permute-done | bytes 262176 | tf_op jit(solution)/shard_map/ppermute | solution.py:18
  11.2 0.8 %shard_map.88 = bf16[256,128]{1,0:T(8,128)(2,1)S(1)} custom-call(s32[8,2]{1,0:T(8,128)S(1)} %copy.13.cols_ref, bf16[8,2,128,128]{3,2,1,0:T(8,128)(2,1)S(1)} %get-tuple-element.26.refs_4_.vals_ref, bf16[1024,128]{1,0:T(8,128)(2,1)S(1)} %shard_map.86.mine_ref, bf16[1024,128]{1,0:T(8,128)(2,1)S(1)} %collective-permute-done.3.far_ref), custom_call_target="tpu_custom_call" | custom-call | tf_op jit(solution)/shard_map/pallas_call | solution.py:202
  12.0 3.7 %collective-permute-start.4 = (bf16[256,128]{1,0:T(8,128)(2,1)S(1)}, bf16[256,128]{1,0:T(8,128)(2,1)S(1)}, u32[]{:S(2)}, u32[]{:S(2)}) collective-permute-start(bf16[256,128]{1,0:T(8,128)(2,1)S(1)} %shard_map.88), channel_id=1, source_target_pairs={{0,24},{8,16},{16,8},{24,0},{1,25},{9,17},{17,9},{25,1},{2,26},{10... | collective-permute-start | bytes 196616 | tf_op jit(solution)/shard_map/ppermute | solution.py:18
  15.7 0.8 %shard_map.90 = bf16[256,128]{1,0:T(8,128)(2,1)S(1)} custom-call(s32[8,2]{1,0:T(8,128)S(1)} %copy.13.cols_ref, bf16[8,2,128,128]{3,2,1,0:T(8,128)(2,1)S(1)} %get-tuple-element.26.refs_4_.vals_ref, bf16[1024,128]{1,0:T(8,128)(2,1)S(1)} %shard_map.86.mine_ref, bf16[1024,128]{1,0:T(8,128)(2,1)S(1)} %collective-permute-done.3.far_ref), custom_call_target="tpu_custom_call" | custom-call | tf_op jit(solution)/shard_map/pallas_call | solution.py:202
  16.6 0.8 %shard_map.92 = bf16[256,128]{1,0:T(8,128)(2,1)S(1)} custom-call(s32[8,2]{1,0:T(8,128)S(1)} %copy.13.cols_ref, bf16[8,2,128,128]{3,2,1,0:T(8,128)(2,1)S(1)} %get-tuple-element.26.refs_4_.vals_ref, bf16[1024,128]{1,0:T(8,128)(2,1)S(1)} %shard_map.86.mine_ref, bf16[1024,128]{1,0:T(8,128)(2,1)S(1)} %collective-permute-done.3.far_ref), custom_call_target="tpu_custom_call" | custom-call | tf_op jit(solution)/shard_map/pallas_call | solution.py:202
  17.4 0.8 %collective-permute-start.6 = (bf16[256,128]{1,0:T(8,128)(2,1)S(1)}, bf16[256,128]{1,0:T(8,128)(2,1)S(1)}, u32[]{:S(2)}, u32[]{:S(2)}) collective-permute-start(bf16[256,128]{1,0:T(8,128)(2,1)S(1)} %shard_map.92), channel_id=1, source_target_pairs={{0,8},{8,0},{16,24},{24,16},{1,9},{9,1},{17,25},{25,17},{2,10},{10... | collective-permute-start | bytes 196616 | tf_op jit(solution)/shard_map/ppermute | solution.py:18
  18.2 0.8 %shard_map.87.a_ref = f32[256,128]{1,0:T(8,128)S(1)} custom-call(s32[8,2]{1,0:T(8,128)S(1)} %copy.13.cols_ref, bf16[8,2,128,128]{3,2,1,0:T(8,128)(2,1)S(1)} %get-tuple-element.26.refs_4_.vals_ref, bf16[1024,128]{1,0:T(8,128)(2,1)S(1)} %shard_map.86.mine_ref, bf16[1024,128]{1,0:T(8,128)(2,1)S(1)} %collective-permute-done.3.far_ref), custom_call_target="tpu_custom_call" | custom-call | tf_op jit(solution)/shard_map/pallas_call | solution.py:202
  19.1 3.1 %collective-permute-done.5.b_ref = bf16[256,128]{1,0:T(8,128)(2,1)S(1)} collective-permute-done((bf16[256,128]{1,0:T(8,128)(2,1)S(1)}, bf16[256,128]{1,0:T(8,128)(2,1)S(1)}, u32[]{:S(2)}, u32[]{:S(2)}) %collective-permute-start.5) | collective-permute-done | bytes 65568 | tf_op jit(solution)/shard_map/ppermute | solution.py:18
  22.7 2.3 %collective-permute-start.7 = (bf16[256,128]{1,0:T(8,128)(2,1)S(1)}, bf16[256,128]{1,0:T(8,128)(2,1)S(1)}, u32[]{:S(2)}, u32[]{:S(2)}) collective-permute-start(bf16[256,128]{1,0:T(8,128)(2,1)S(1)} %shard_map.93.refs_0_), channel_id=1, source_target_pairs={{0,24},{8,16},{16,8},{24,0},{1,25},{9,17},{17,9},{25,1},{2,26},{10... | collective-permute-start | bytes 196616 | tf_op jit(solution)/shard_map/ppermute | solution.py:18
  25.1 2.1 %collective-permute-start.9 = (bf16[256,128]{1,0:T(8,128)(2,1)S(1)}, bf16[256,128]{1,0:T(8,128)(2,1)S(1)}, u32[]{:S(2)}, u32[]{:S(2)}) collective-permute-start(bf16[256,128]{1,0:T(8,128)(2,1)S(1)} %shard_map.93.refs_0_), channel_id=1, source_target_pairs={{0,8},{8,0},{16,24},{24,16},{1,9},{9,1},{17,25},{25,17},{2,10},{10... | collective-permute-start | bytes 196616 | tf_op jit(solution)/shard_map/ppermute | solution.py:18
  27.8 1.1 %shard_map.94 = (bf16[256,128]{1,0:T(8,128)(2,1)S(1)}, f32[16,128,128]{2,1,0:T(8,128)S(1)}, f32[128,128]{1,0:T(8,128)S(1)}) custom-call(s32[8,2]{1,0:T(8,128)S(1)} %copy.13.cols_ref, bf16[8,256,128]{2,1,0:T(8,128)(2,1)S(1)} %get-tuple-element.25.flipped_ref, bf16[1024,128]{1,0:T(8,128)(2,1)S(1)} %copy-done, bf16[128,128]{1,0:T(8,128)(2,1)S(1)} %copy-done.1, ...), custom_call_target="tpu_custom_call" | custom-call | tf_op jit(solution)/shard_map/pallas_call | solution.py:230
  29.0 1.1 %shard_map.95 = (bf16[256,128]{1,0:T(8,128)(2,1)S(1)}, f32[16,128,128]{2,1,0:T(8,128)S(1)}, f32[128,128]{1,0:T(8,128)S(1)}) custom-call(s32[8,2]{1,0:T(8,128)S(1)} %copy.13.cols_ref, bf16[8,256,128]{2,1,0:T(8,128)(2,1)S(1)} %get-tuple-element.25.flipped_ref, bf16[1024,128]{1,0:T(8,128)(2,1)S(1)} %copy-done, bf16[128,128]{1,0:T(8,128)(2,1)S(1)} %copy-done.1, ...), custom_call_target="tpu_custom_call" | custom-call | tf_op jit(solution)/shard_map/pallas_call | solution.py:230
  30.1 1.0 %collective-permute-done.8.refs_0_ = bf16[256,128]{1,0:T(8,128)(2,1)S(1)} collective-permute-done((bf16[256,128]{1,0:T(8,128)(2,1)S(1)}, bf16[256,128]{1,0:T(8,128)(2,1)S(1)}, u32[]{:S(2)}, u32[]{:S(2)}) %collective-permute-start.8) | collective-permute-done | bytes 65568 | tf_op jit(solution)/shard_map/ppermute | solution.py:18
  31.1 1.1 %shard_map.96 = (bf16[256,128]{1,0:T(8,128)(2,1)S(1)}, f32[16,128,128]{2,1,0:T(8,128)S(1)}, f32[128,128]{1,0:T(8,128)S(1)}) custom-call(s32[8,2]{1,0:T(8,128)S(1)} %copy.13.cols_ref, bf16[8,256,128]{2,1,0:T(8,128)(2,1)S(1)} %get-tuple-element.25.flipped_ref, bf16[1024,128]{1,0:T(8,128)(2,1)S(1)} %copy-done, bf16[128,128]{1,0:T(8,128)(2,1)S(1)} %copy-done.1, ...), custom_call_target="tpu_custom_call" | custom-call | tf_op jit(solution)/shard_map/pallas_call | solution.py:230
  32.3 1.2 %shard_map.97 = (bf16[256,128]{1,0:T(8,128)(2,1)S(1)}, bf16[1152,128]{1,0:T(8,128)(2,1)S(1)}, f32[4,256,128]{2,1,0:T(8,128)S(1)}, bf16[128,128]{1,0:T(8,128)(2,1)S(1)}) custom-call(s32[8,2]{1,0:T(8,128)S(1)} %copy.13.cols_ref, bf16[8,256,128]{2,1,0:T(8,128)(2,1)S(1)} %get-tuple-element.25.flipped_ref, bf16[1024,128]{1,0:T(8,128)(2,1)S(1)} %copy-done, ...), custom_call_target="tpu_custom_call" | custom-call | tf_op jit(solution)/shard_map/pallas_call | solution.py:230
  33.5 1.6 %collective-permute-done.10.got_ref = bf16[1152,128]{1,0:T(8,128)(2,1)S(1)} collective-permute-done((bf16[1152,128]{1,0:T(8,128)(2,1)S(1)}, bf16[1152,128]{1,0:T(8,128)(2,1)S(1)}, u32[]{:S(2)}, u32[]{:S(2)}) %collective-permute-start.10) | collective-permute-done | bytes 294944 | tf_op jit(solution)/shard_map/ppermute | solution.py:18
  35.1 1.7 %collective-permute-start.12 = (bf16[384,128]{1,0:T(8,128)(2,1)S(1)}, bf16[384,128]{1,0:T(8,128)(2,1)S(1)}, u32[]{:S(2)}, u32[]{:S(2)}) collective-permute-start(bf16[384,128]{1,0:T(8,128)(2,1)S(1)} %get-tuple-element.43), channel_id=1, source_target_pairs={{0,6},{1,7},{2,4},{3,5},{4,2},{5,3},{6,0},{7,1},{8,14},{9,15},{10,... | collective-permute-start | bytes 294920 | tf_op jit(solution)/shard_map/ppermute | solution.py:18
  37.6 1.1 %collective-permute-start.11 = (bf16[384,128]{1,0:T(8,128)(2,1)S(1)}, bf16[384,128]{1,0:T(8,128)(2,1)S(1)}, u32[]{:S(2)}, u32[]{:S(2)}) collective-permute-start(bf16[384,128]{1,0:T(8,128)(2,1)S(1)} %get-tuple-element.42), channel_id=1, source_target_pairs={{0,2},{1,3},{2,0},{3,1},{4,6},{5,7},{6,4},{7,5},{8,10},{9,11},{10,... | collective-permute-start | bytes 294920 | tf_op jit(solution)/shard_map/ppermute | solution.py:18
  39.4 2.0 %collective-permute-done.12.refs_0_ = bf16[384,128]{1,0:T(8,128)(2,1)S(1)} collective-permute-done((bf16[384,128]{1,0:T(8,128)(2,1)S(1)}, bf16[384,128]{1,0:T(8,128)(2,1)S(1)}, u32[]{:S(2)}, u32[]{:S(2)}) %collective-permute-start.12) | collective-permute-done | bytes 98336 | tf_op jit(solution)/shard_map/ppermute | solution.py:18
  41.4 1.6 %collective-permute-done.13.refs_1_ = bf16[384,128]{1,0:T(8,128)(2,1)S(1)} collective-permute-done((bf16[384,128]{1,0:T(8,128)(2,1)S(1)}, bf16[384,128]{1,0:T(8,128)(2,1)S(1)}, u32[]{:S(2)}, u32[]{:S(2)}) %collective-permute-start.13) | collective-permute-done | bytes 98336 | tf_op jit(solution)/shard_map/ppermute | solution.py:18
  (34 shorter events, 5.1 us)
Async XLA Ops:
  0.6 6.0 %collective-permute-start.1 = (bf16[256,128]{1,0:T(8,128)(2,1)}, bf16[256,128]{1,0:T(8,128)(2,1)S(1)}, u32[]{:S(2)}, u32[]{:S(2)}) collective-permute-start(bf16[256,128]{1,0:T(8,128)(2,1)} %refs_3_.1), channel_id=1, source_target_pairs={{0,4},{1,5},{2,6},{3,7},{4,0},{5,1},{6,2},{7,3},{8,12},{9,13},{10,... | collective-permute-start | bytes 196616 | tf_op jit(solution)/shard_map/ppermute | solution.py:18
  3.7 5.9 %collective-permute-start = (bf16[256,128]{1,0:T(8,128)(2,1)}, bf16[256,128]{1,0:T(8,128)(2,1)S(1)}, u32[]{:S(2)}, u32[]{:S(2)}) collective-permute-start(bf16[256,128]{1,0:T(8,128)(2,1)} %refs_3_.1), channel_id=1, source_target_pairs={{0,6},{1,7},{2,4},{3,5},{4,2},{5,3},{6,0},{7,1},{8,14},{9,15},{10,... | collective-permute-start | bytes 196616 | tf_op jit(solution)/shard_map/ppermute | solution.py:18
  5.1 4.5 %collective-permute-start.2 = (bf16[256,128]{1,0:T(8,128)(2,1)}, bf16[256,128]{1,0:T(8,128)(2,1)S(1)}, u32[]{:S(2)}, u32[]{:S(2)}) collective-permute-start(bf16[256,128]{1,0:T(8,128)(2,1)} %refs_3_.1), channel_id=1, source_target_pairs={{0,2},{1,3},{2,0},{3,1},{4,6},{5,7},{6,4},{7,5},{8,10},{9,11},{10,... | collective-permute-start | bytes 196616 | tf_op jit(solution)/shard_map/ppermute | solution.py:18
  5.2 1.0 %copy-start.2 = (bf16[8,2,128,128]{3,2,1,0:T(8,128)(2,1)S(1)}, bf16[8,2,128,128]{3,2,1,0:T(8,128)(2,1)}, u32[]{:S(2)}) copy-start(bf16[8,2,128,128]{3,2,1,0:T(8,128)(2,1)} %vals_ref.1) | copy-start | bytes 1572868
  6.2 3.3 %copy-start.3 = (bf16[256,128]{1,0:T(8,128)(2,1)S(1)}, bf16[256,128]{1,0:T(8,128)(2,1)}, u32[]{:S(2)}) copy-start(bf16[256,128]{1,0:T(8,128)(2,1)} %refs_3_.1) | copy-start | bytes 196612
  9.6 0.7 %copy-start.5 = (s32[8,2]{0,1:T(2,128)S(1)}, s32[8,2]{0,1:T(2,128)}, u32[]{:S(2)}) copy-start(s32[8,2]{0,1:T(2,128)} %param.6) | copy-start | bytes 196
  9.6 1.6 %collective-permute-start.3 = (bf16[1024,128]{1,0:T(8,128)(2,1)S(1)}, bf16[1024,128]{1,0:T(8,128)(2,1)S(1)}, u32[]{:S(2)}, u32[]{:S(2)}) collective-permute-start(bf16[1024,128]{1,0:T(8,128)(2,1)S(1)} %shard_map.86.mine_ref), channel_id=1, source_target_pairs={{0,1},{1,0},{2,3},{3,2},{4,5},{5,4},{6,7},{7,6},{8,9},{9,8},{10,11... | collective-permute-start | bytes 786440 | tf_op jit(solution)/shard_map/ppermute | solution.py:18
  12.0 7.0 %collective-permute-start.4 = (bf16[256,128]{1,0:T(8,128)(2,1)S(1)}, bf16[256,128]{1,0:T(8,128)(2,1)S(1)}, u32[]{:S(2)}, u32[]{:S(2)}) collective-permute-start(bf16[256,128]{1,0:T(8,128)(2,1)S(1)} %shard_map.88), channel_id=1, source_target_pairs={{0,24},{8,16},{16,8},{24,0},{1,25},{9,17},{17,9},{25,1},{2,26},{10... | collective-permute-start | bytes 196616 | tf_op jit(solution)/shard_map/ppermute | solution.py:18
  16.5 5.6 %collective-permute-start.5 = (bf16[256,128]{1,0:T(8,128)(2,1)S(1)}, bf16[256,128]{1,0:T(8,128)(2,1)S(1)}, u32[]{:S(2)}, u32[]{:S(2)}) collective-permute-start(bf16[256,128]{1,0:T(8,128)(2,1)S(1)} %shard_map.90), channel_id=1, source_target_pairs={{0,16},{8,24},{16,0},{24,8},{1,17},{9,25},{17,1},{25,9},{2,18},{10... | collective-permute-start | bytes 196616 | tf_op jit(solution)/shard_map/ppermute | solution.py:18
  17.4 5.3 %collective-permute-start.6 = (bf16[256,128]{1,0:T(8,128)(2,1)S(1)}, bf16[256,128]{1,0:T(8,128)(2,1)S(1)}, u32[]{:S(2)}, u32[]{:S(2)}) collective-permute-start(bf16[256,128]{1,0:T(8,128)(2,1)S(1)} %shard_map.92), channel_id=1, source_target_pairs={{0,8},{8,0},{16,24},{24,16},{1,9},{9,1},{17,25},{25,17},{2,10},{10... | collective-permute-start | bytes 196616 | tf_op jit(solution)/shard_map/ppermute | solution.py:18
  19.0 8.1 %copy-start = (bf16[1024,128]{1,0:T(8,128)(2,1)S(1)}, bf16[1024,128]{1,0:T(8,128)(2,1)}, u32[]{:S(2)}) copy-start(bf16[1024,128]{1,0:T(8,128)(2,1)} %cotangent_ref.7) | copy-start | bytes 786436
  22.1 5.1 %copy-start.1 = (bf16[128,128]{1,0:T(8,128)(2,1)S(1)}, bf16[128,128]{1,0:T(8,128)(2,1)}, u32[]{:S(2)}) copy-start(bf16[128,128]{1,0:T(8,128)(2,1)} %weight_ref.7) | copy-start | bytes 98308
  22.7 6.2 %collective-permute-start.7 = (bf16[256,128]{1,0:T(8,128)(2,1)S(1)}, bf16[256,128]{1,0:T(8,128)(2,1)S(1)}, u32[]{:S(2)}, u32[]{:S(2)}) collective-permute-start(bf16[256,128]{1,0:T(8,128)(2,1)S(1)} %shard_map.93.refs_0_), channel_id=1, source_target_pairs={{0,24},{8,16},{16,8},{24,0},{1,25},{9,17},{17,9},{25,1},{2,26},{10... | collective-permute-start | bytes 196616 | tf_op jit(solution)/shard_map/ppermute | solution.py:18
  25.1 6.1 %collective-permute-start.8 = (bf16[256,128]{1,0:T(8,128)(2,1)S(1)}, bf16[256,128]{1,0:T(8,128)(2,1)S(1)}, u32[]{:S(2)}, u32[]{:S(2)}) collective-permute-start(bf16[256,128]{1,0:T(8,128)(2,1)S(1)} %shard_map.93.refs_0_), channel_id=1, source_target_pairs={{0,16},{8,24},{16,0},{24,8},{1,17},{9,25},{17,1},{25,9},{2,18},{10... | collective-permute-start | bytes 196616 | tf_op jit(solution)/shard_map/ppermute | solution.py:18
  25.1 7.2 %collective-permute-start.9 = (bf16[256,128]{1,0:T(8,128)(2,1)S(1)}, bf16[256,128]{1,0:T(8,128)(2,1)S(1)}, u32[]{:S(2)}, u32[]{:S(2)}) collective-permute-start(bf16[256,128]{1,0:T(8,128)(2,1)S(1)} %shard_map.93.refs_0_), channel_id=1, source_target_pairs={{0,8},{8,0},{16,24},{24,16},{1,9},{9,1},{17,25},{25,17},{2,10},{10... | collective-permute-start | bytes 196616 | tf_op jit(solution)/shard_map/ppermute | solution.py:18
  27.2 0.7 %copy-start.4 = (f32[128]{0:T(128)S(1)}, f32[128]{0:T(128)}, u32[]{:S(2)}) copy-start(f32[128]{0:T(128)} %param.10) | copy-start | bytes 1540
  33.4 1.6 %collective-permute-start.10 = (bf16[1152,128]{1,0:T(8,128)(2,1)S(1)}, bf16[1152,128]{1,0:T(8,128)(2,1)S(1)}, u32[]{:S(2)}, u32[]{:S(2)}) collective-permute-start(bf16[1152,128]{1,0:T(8,128)(2,1)S(1)} %get-tuple-element.39), channel_id=1, source_target_pairs={{0,1},{1,0},{2,3},{3,2},{4,5},{5,4},{6,7},{7,6},{8,9},{9,8},{10,11... | collective-permute-start | bytes 884744 | tf_op jit(solution)/shard_map/ppermute | solution.py:18
  35.1 6.3 %collective-permute-start.12 = (bf16[384,128]{1,0:T(8,128)(2,1)S(1)}, bf16[384,128]{1,0:T(8,128)(2,1)S(1)}, u32[]{:S(2)}, u32[]{:S(2)}) collective-permute-start(bf16[384,128]{1,0:T(8,128)(2,1)S(1)} %get-tuple-element.43), channel_id=1, source_target_pairs={{0,6},{1,7},{2,4},{3,5},{4,2},{5,3},{6,0},{7,1},{8,14},{9,15},{10,... | collective-permute-start | bytes 294920 | tf_op jit(solution)/shard_map/ppermute | solution.py:18
  36.9 6.2 %collective-permute-start.13 = (bf16[384,128]{1,0:T(8,128)(2,1)S(1)}, bf16[384,128]{1,0:T(8,128)(2,1)S(1)}, u32[]{:S(2)}, u32[]{:S(2)}) collective-permute-start(bf16[384,128]{1,0:T(8,128)(2,1)S(1)} %get-tuple-element.44), channel_id=1, source_target_pairs={{0,4},{1,5},{2,6},{3,7},{4,0},{5,1},{6,2},{7,3},{8,12},{9,13},{10,... | collective-permute-start | bytes 294920 | tf_op jit(solution)/shard_map/ppermute | solution.py:18
  37.6 5.5 %collective-permute-start.11 = (bf16[384,128]{1,0:T(8,128)(2,1)S(1)}, bf16[384,128]{1,0:T(8,128)(2,1)S(1)}, u32[]{:S(2)}, u32[]{:S(2)}) collective-permute-start(bf16[384,128]{1,0:T(8,128)(2,1)S(1)} %get-tuple-element.42), channel_id=1, source_target_pairs={{0,2},{1,3},{2,0},{3,1},{4,6},{5,7},{6,4},{7,5},{8,10},{9,11},{10,... | collective-permute-start | bytes 294920 | tf_op jit(solution)/shard_map/ppermute | solution.py:18

commit v4 on v3

--- a/solution.py
+++ b/solution.py
@@ -10,7 +10,6 @@
 BF16 = jnp.bfloat16
 F32 = jnp.float32
 VMEM = pl.BlockSpec(memory_space=pltpu.VMEM)
-SMEM = pl.BlockSpec(memory_space=pltpu.SMEM)
 
 
 def swap(value, axis, distance):
@@ -22,18 +21,17 @@
     return lax.dot_general(a, b, ((contract[:1], contract[1:]), ((), ())), preferred_element_type=F32)
 
 
-def slot_of(cols_ref, row, k, own_blocks, quarter_blocks):
-    col = cols_ref[row, k] - lax.axis_index("rep") * quarter_blocks
-    owner = lax.div(col, jnp.int32(own_blocks)) ^ lax.axis_index("dom")
-    return owner, lax.rem(col, jnp.int32(own_blocks))
-
-
-def transpose_kernel(vals_ref, near_ref, flipped_ref):
+def early_kernel(own_blocks, dom, cols_ref, vals_ref, *refs):
+    flipped_ref, place_ref = refs[-2:]
     rows, count, size, _ = vals_ref.shape
-    near_ref[...] = vals_ref[...]
     for row in range(rows):
         for k in range(count):
             flipped_ref[row, k * size : (k + 1) * size] = vals_ref[row, k].T
+            col = cols_ref[row, k] - lax.axis_index("rep") * (own_blocks * dom)
+            owner = lax.div(col, jnp.int32(own_blocks)) ^ lax.axis_index("dom")
+            place = ((owner & 1) * (dom // 2) + (owner >> 1)) * own_blocks
+            place += lax.rem(col, jnp.int32(own_blocks))
+            place_ref[row * count + k : row * count + k + 1, :] = jnp.full((1, 128), place, jnp.int32)
 
 
 def join_kernel(order, *refs):
@@ -43,26 +41,28 @@
         out_ref[chip * nodes : (chip + 1) * nodes] = piece[...]
 
 
-def aggregate_kernel(rep, own_blocks, j, cols_ref, vals_ref, mine_ref, far_ref, out_ref):
+def aggregate_kernel(rep, place_ref, vals_ref, mine_ref, far_ref, *outs):
     rows, count, size, _ = vals_ref.shape
-    quarter_blocks = 2 * mine_ref.shape[0] // size
+    half = mine_ref.shape[0] // size
     share = rows // rep
-    target = lax.axis_index("rep") ^ j
-    for i in range(share):
-        row = target * share + i
-        total = None
-        for k in range(count):
-            owner, rest = slot_of(cols_ref, row, k, own_blocks, quarter_blocks)
-            index = (owner >> 1) * own_blocks + rest
-            here = pl.ds(pl.multiple_of(index * size, size), size)
-            block = jnp.where((owner & 1) == 1, far_ref[here, :], mine_ref[here, :])
-            term = matmul(vals_ref[row, k], block, (1, 0))
-            total = term if total is None else total + term
-        out_ref[i * size : (i + 1) * size] = total.astype(out_ref.dtype)
+    for j in range(rep - 1, -1, -1):
+        target = lax.axis_index("rep") ^ j
+        for i in range(share):
+            row = target * share + i
+            total = None
+            for k in range(count):
+                place = place_ref[row * count + k, 0]
+                beyond = place >= half
+                index = jnp.where(beyond, place - half, place)
+                here = pl.ds(pl.multiple_of(index * size, size), size)
+                block = jnp.where(beyond, far_ref[here, :], mine_ref[here, :])
+                term = matmul(vals_ref[row, k], block, (1, 0))
+                total = term if total is None else total + term
+            outs[j][i * size : (i + 1) * size] = total.astype(outs[j].dtype)
 
 
 def layer_kernel(
-    rep, count, own_blocks, j, cols_ref, flipped_ref, cotangent_ref, weight_ref, bias_ref, *refs
+    rep, count, own_blocks, j, place_ref, flipped_ref, cotangent_ref, weight_ref, bias_ref, *refs
 ):
     first, last = j == 0, j == 1
     piece_ref, refs = refs[0], refs[1:]
@@ -96,17 +96,14 @@
         row = target * share + i
         terms = matmul(flipped_ref[row], grad_agg[i * size : (i + 1) * size], (1, 0))
         for k in range(count):
-            owner, rest = slot_of(cols_ref, row, k, own_blocks, quarter_blocks)
-            contrib[owner * own_blocks + rest] += terms[k * size : (k + 1) * size]
+            contrib[place_ref[row * count + k, 0]] += terms[k * size : (k + 1) * size]
     if not last:
         weight_out[...] = weight_part
         return
     chips = keep_ref.shape[0]
-    for chip in range(chips):
-        even = contrib[2 * chip * own_blocks : (2 * chip + 1) * own_blocks]
-        odd = contrib[(2 * chip + 1) * own_blocks : (2 * chip + 2) * own_blocks]
-        keep_ref[chip] = even.reshape(nodes, -1)
-        send_ref[chip * nodes : (chip + 1) * nodes] = odd.reshape(nodes, -1).astype(BF16)
+    half = quarter_blocks // 2
+    keep_ref[...] = contrib[:half].reshape(keep_ref.shape)
+    send_ref[: chips * nodes] = contrib[half:].reshape(chips * nodes, -1).astype(BF16)
     send_ref[chips * nodes :] = weight_part.astype(BF16)
     keep_weight_ref[...] = weight_part.astype(BF16)
 
@@ -185,26 +182,25 @@
             compiler_params=params,
         )
 
-    near, flipped = call(
-        transpose_kernel,
-        [shape(vals.shape, BF16), shape((rows, count * size, size), BF16)],
-        [VMEM],
-    )(vals)
+    bias = bias.reshape(1, width)
+    flipped, place = call(
+        functools.partial(early_kernel, own_blocks, dom),
+        [shape((rows, count * size, size), BF16), shape((rows * count, 128), jnp.int32)],
+        [VMEM] * 3,
+    )(cols, vals, bias)
     order = list(range(chips - 1, -1, -1))
     across = [swap(features, "dom", 2 * chip) for chip in order[:-1]] + [features]
     mine = call(
         functools.partial(join_kernel, order), shape((chips * nodes, width), BF16), [VMEM] * (chips + 1)
-    )(*across, near)
+    )(*across, place)
     far = swap(mine, "dom", 1)
 
-    arrived = {}
-    for j in range(rep - 1, -1, -1):
-        partial_sum = call(
-            functools.partial(aggregate_kernel, rep, own_blocks, j),
-            shape((part, width), BF16 if j else F32),
-            [SMEM, VMEM, VMEM, VMEM],
-        )(cols, near, mine, far)
-        arrived[j] = swap(partial_sum, "rep", j) if j else partial_sum
+    partials = call(
+        functools.partial(aggregate_kernel, rep),
+        [shape((part, width), BF16 if j else F32) for j in range(rep)],
+        [VMEM] * 4,
+    )(place, vals, mine, far)
+    arrived = {j: swap(partials[j], "rep", j) if j else partials[j] for j in range(rep)}
     own_rows = arrived[0]
     for j in range(rep - 1, 0, -1):
         own_rows = call(add_kernel, shape((part, width), F32 if j > 1 else BF16), [VMEM] * 2)(
@@ -230,9 +226,9 @@
         output, *carried = call(
             functools.partial(layer_kernel, rep, count, own_blocks, j),
             [shape((part, width), BF16)] + outs,
-            [SMEM] + [VMEM] * (5 + len(carried)),
+            [VMEM] * (6 + len(carried)),
             scratch,
-        )(cols, flipped, cotangent, weight, bias.reshape(1, width), piece, *carried)
+        )(place, flipped, cotangent, weight, bias, piece, *carried)
         outputs.append(output)
     send, keep, keep_weight = carried
 

time: 44 us -> 42.8 us (0.973)
  Pallas kernels: 9.46 us -> 4.31 us
  waiting for transfers between devices: 13.9 us -> 17.1 us
  local copies, waits for them, and re-layouts: 2.37 us -> 3.3 us
    ppermute x14, waiting for transfers between devices: 13.9 us -> 17.1 us  [swap(): return lax.ppermute(value, axis, [(i, i ^ distance) for i in range(size)])]
    pallas_call x5 -> x2, Pallas kernels: 3.38 us -> 0.6 us  [the longest x1 0.35 us: body(): call(functools.partial(aggregate_kernel, rep), [shape((part, width), BF16...]
    pallas_call x4, Pallas kernels: 4.52 us -> 2.15 us  [body(): call(functools.partial(layer_kernel, rep, count, own_blocks, j), [shape((...]
    unnamed x13, local copies, waits for them, and re-layouts: 2.37 us -> 3.3 us
  transfers between devices with their start and end apart: 14 -> 14, of which waited for: 10 -> 10; matrix products, arithmetic and copies ran while one was open for 0% -> 2% of each run, Pallas kernels for 15% -> 6%
where the time goes in v4:
time: 42.8 us; the launch traced here: 42.6 us
  starting transfers between devices  17.2 us (40%)
  waiting for transfers between devices  17.1 us (40%)
  Pallas kernels  4.31 us (10%)
  local copies, waits for them, and re-layouts  3.3 us (8%)
  between operations  0.75 us (2%)
    ppermute x14, starting transfers between devices, swap(): return lax.ppermute(value, axis, [(i, i ^ distance) for i in range(size)])  17.2 us
    ppermute x14, waiting for transfers between devices, swap(): return lax.ppermute(value, axis, [(i, i ^ distance) for i in range(size)])  17.1 us
    unnamed x13, local copies, waits for them, and re-layouts  3.3 us
    pallas_call x4, Pallas kernels, body(): call(functools.partial(layer_kernel, rep, count, own_blocks, j), [shape((...  2.15 us
  transfers between devices with their start and end apart: 14, of which 10 were waited for; matrix products, arithmetic and copies ran while one was open for 2% of the time, Pallas kernels for 6%

profile of v4, /device:TPU:0, one launch (start us, length us, event | category | flops | bytes accessed | tf_op | source)
XLA Modules:
  0.0 42.6 jit_solution(10270207603466379087)
XLA Ops:
  0.6 3.0 %collective-permute-start.1 = (bf16[256,128]{1,0:T(8,128)(2,1)}, bf16[256,128]{1,0:T(8,128)(2,1)S(1)}, u32[]{:S(2)}, u32[]{:S(2)}) collective-permute-start(bf16[256,128]{1,0:T(8,128)(2,1)} %refs_3_.1), channel_id=1, source_target_pairs={{0,4},{1,5},{2,6},{3,7},{4,0},{5,1},{6,2},{7,3},{8,12},{9,13},{10,... | collective-permute-start | bytes 196616 | tf_op jit(solution)/shard_map/ppermute | solution.py:17
  3.7 1.4 %collective-permute-start = (bf16[256,128]{1,0:T(8,128)(2,1)}, bf16[256,128]{1,0:T(8,128)(2,1)S(1)}, u32[]{:S(2)}, u32[]{:S(2)}) collective-permute-start(bf16[256,128]{1,0:T(8,128)(2,1)} %refs_3_.1), channel_id=1, source_target_pairs={{0,6},{1,7},{2,4},{3,5},{4,2},{5,3},{6,0},{7,1},{8,14},{9,15},{10,... | collective-permute-start | bytes 196616 | tf_op jit(solution)/shard_map/ppermute | solution.py:17
  5.2 0.8 %copy.9.cols_ref = s32[8,2]{1,0:T(8,128)S(1)} copy(s32[8,2]{0,1:T(2,128)} %param.6) | data formatting | bytes 128 | tf_op args[0]
  6.0 0.7 %copy-done.5 = f32[128]{0:T(128)S(1)} copy-done((f32[128]{0:T(128)S(1)}, f32[128]{0:T(128)}, u32[]{:S(2)}) %copy-start.5) | copy-done | bytes 536
  6.6 1.0 %copy-done.1 = bf16[8,2,128,128]{3,2,1,0:T(8,128)(2,1)S(1)} copy-done((bf16[8,2,128,128]{3,2,1,0:T(8,128)(2,1)S(1)}, bf16[8,2,128,128]{3,2,1,0:T(8,128)(2,1)}, u32[]{:S(2)}) %copy-start.1) | copy-done | bytes 524312
  7.9 1.6 %collective-permute-done.refs_0_ = bf16[256,128]{1,0:T(8,128)(2,1)S(1)} collective-permute-done((bf16[256,128]{1,0:T(8,128)(2,1)}, bf16[256,128]{1,0:T(8,128)(2,1)S(1)}, u32[]{:S(2)}, u32[]{:S(2)}) %collective-permute-start) | collective-permute-done | bytes 65568 | tf_op jit(solution)/shard_map/ppermute | solution.py:17
  9.6 0.8 %copy-done.4 = bf16[256,128]{1,0:T(8,128)(2,1)S(1)} copy-done((bf16[256,128]{1,0:T(8,128)(2,1)S(1)}, bf16[256,128]{1,0:T(8,128)(2,1)}, u32[]{:S(2)}) %copy-start.4) | copy-done | bytes 65560
  10.5 1.5 %collective-permute-done.3.far_ref = bf16[1024,128]{1,0:T(8,128)(2,1)S(1)} collective-permute-done((bf16[1024,128]{1,0:T(8,128)(2,1)S(1)}, bf16[1024,128]{1,0:T(8,128)(2,1)S(1)}, u32[]{:S(2)}, u32[]{:S(2)}) %collective-permute-start.3) | collective-permute-done | bytes 262176 | tf_op jit(solution)/shard_map/ppermute | solution.py:17
  12.4 3.7 %collective-permute-start.4 = (bf16[256,128]{1,0:T(8,128)(2,1)S(1)}, bf16[256,128]{1,0:T(8,128)(2,1)S(1)}, u32[]{:S(2)}, u32[]{:S(2)}) collective-permute-start(bf16[256,128]{1,0:T(8,128)(2,1)S(1)} %get-tuple-element.32), channel_id=1, source_target_pairs={{0,24},{8,16},{16,8},{24,0},{1,25},{9,17},{17,9},{25,1},{2,26},{10... | collective-permute-start | bytes 196616 | tf_op jit(solution)/shard_map/ppermute | solution.py:17
  16.1 0.8 %collective-permute-start.6 = (bf16[256,128]{1,0:T(8,128)(2,1)S(1)}, bf16[256,128]{1,0:T(8,128)(2,1)S(1)}, u32[]{:S(2)}, u32[]{:S(2)}) collective-permute-start(bf16[256,128]{1,0:T(8,128)(2,1)S(1)} %get-tuple-element.34), channel_id=1, source_target_pairs={{0,8},{8,0},{16,24},{24,16},{1,9},{9,1},{17,25},{25,17},{2,10},{10... | collective-permute-start | bytes 196616 | tf_op jit(solution)/shard_map/ppermute | solution.py:17
  16.8 1.9 %collective-permute-done.4.b_ref = bf16[256,128]{1,0:T(8,128)(2,1)S(1)} collective-permute-done((bf16[256,128]{1,0:T(8,128)(2,1)S(1)}, bf16[256,128]{1,0:T(8,128)(2,1)S(1)}, u32[]{:S(2)}, u32[]{:S(2)}) %collective-permute-start.4) | collective-permute-done | bytes 65568 | tf_op jit(solution)/shard_map/ppermute | solution.py:17
  18.8 3.2 %collective-permute-done.5.b_ref = bf16[256,128]{1,0:T(8,128)(2,1)S(1)} collective-permute-done((bf16[256,128]{1,0:T(8,128)(2,1)S(1)}, bf16[256,128]{1,0:T(8,128)(2,1)S(1)}, u32[]{:S(2)}, u32[]{:S(2)}) %collective-permute-start.5) | collective-permute-done | bytes 65568 | tf_op jit(solution)/shard_map/ppermute | solution.py:17
  22.0 2.5 %collective-permute-start.7 = (bf16[256,128]{1,0:T(8,128)(2,1)S(1)}, bf16[256,128]{1,0:T(8,128)(2,1)S(1)}, u32[]{:S(2)}, u32[]{:S(2)}) collective-permute-start(bf16[256,128]{1,0:T(8,128)(2,1)S(1)} %shard_map.90.refs_0_), channel_id=1, source_target_pairs={{0,24},{8,16},{16,8},{24,0},{1,25},{9,17},{17,9},{25,1},{2,26},{10... | collective-permute-start | bytes 196616 | tf_op jit(solution)/shard_map/ppermute | solution.py:17
  24.6 1.9 %collective-permute-start.9 = (bf16[256,128]{1,0:T(8,128)(2,1)S(1)}, bf16[256,128]{1,0:T(8,128)(2,1)S(1)}, u32[]{:S(2)}, u32[]{:S(2)}) collective-permute-start(bf16[256,128]{1,0:T(8,128)(2,1)S(1)} %shard_map.90.refs_0_), channel_id=1, source_target_pairs={{0,8},{8,0},{16,24},{24,16},{1,9},{9,1},{17,25},{25,17},{2,10},{10... | collective-permute-start | bytes 196616 | tf_op jit(solution)/shard_map/ppermute | solution.py:17
  27.0 1.4 %collective-permute-done.7.refs_0_ = bf16[256,128]{1,0:T(8,128)(2,1)S(1)} collective-permute-done((bf16[256,128]{1,0:T(8,128)(2,1)S(1)}, bf16[256,128]{1,0:T(8,128)(2,1)S(1)}, u32[]{:S(2)}, u32[]{:S(2)}) %collective-permute-start.7) | collective-permute-done | bytes 65568 | tf_op jit(solution)/shard_map/ppermute | solution.py:17
  28.9 2.2 %collective-permute-done.8.refs_0_ = bf16[256,128]{1,0:T(8,128)(2,1)S(1)} collective-permute-done((bf16[256,128]{1,0:T(8,128)(2,1)S(1)}, bf16[256,128]{1,0:T(8,128)(2,1)S(1)}, u32[]{:S(2)}, u32[]{:S(2)}) %collective-permute-start.8) | collective-permute-done | bytes 65568 | tf_op jit(solution)/shard_map/ppermute | solution.py:17
  32.3 1.6 %collective-permute-done.10.got_ref = bf16[1152,128]{1,0:T(8,128)(2,1)S(1)} collective-permute-done((bf16[1152,128]{1,0:T(8,128)(2,1)S(1)}, bf16[1152,128]{1,0:T(8,128)(2,1)S(1)}, u32[]{:S(2)}, u32[]{:S(2)}) %collective-permute-start.10) | collective-permute-done | bytes 294944 | tf_op jit(solution)/shard_map/ppermute | solution.py:17
  33.9 1.7 %collective-permute-start.12 = (bf16[384,128]{1,0:T(8,128)(2,1)S(1)}, bf16[384,128]{1,0:T(8,128)(2,1)S(1)}, u32[]{:S(2)}, u32[]{:S(2)}) collective-permute-start(bf16[384,128]{1,0:T(8,128)(2,1)S(1)} %get-tuple-element.51), channel_id=1, source_target_pairs={{0,6},{1,7},{2,4},{3,5},{4,2},{5,3},{6,0},{7,1},{8,14},{9,15},{10,... | collective-permute-start | bytes 294920 | tf_op jit(solution)/shard_map/ppermute | solution.py:17
  35.6 0.8 %collective-permute-start.13 = (bf16[384,128]{1,0:T(8,128)(2,1)S(1)}, bf16[384,128]{1,0:T(8,128)(2,1)S(1)}, u32[]{:S(2)}, u32[]{:S(2)}) collective-permute-start(bf16[384,128]{1,0:T(8,128)(2,1)S(1)} %get-tuple-element.52), channel_id=1, source_target_pairs={{0,4},{1,5},{2,6},{3,7},{4,0},{5,1},{6,2},{7,3},{8,12},{9,13},{10,... | collective-permute-start | bytes 294920 | tf_op jit(solution)/shard_map/ppermute | solution.py:17
  36.4 1.1 %collective-permute-start.11 = (bf16[384,128]{1,0:T(8,128)(2,1)S(1)}, bf16[384,128]{1,0:T(8,128)(2,1)S(1)}, u32[]{:S(2)}, u32[]{:S(2)}) collective-permute-start(bf16[384,128]{1,0:T(8,128)(2,1)S(1)} %get-tuple-element.50), channel_id=1, source_target_pairs={{0,2},{1,3},{2,0},{3,1},{4,6},{5,7},{6,4},{7,5},{8,10},{9,11},{10,... | collective-permute-start | bytes 294920 | tf_op jit(solution)/shard_map/ppermute | solution.py:17
  37.4 0.7 %shard_map.95 = bf16[1024,128]{1,0:T(8,128)(2,1)} custom-call(bf16[256,128]{1,0:T(8,128)(2,1)S(1)} %get-tuple-element.35.refs_0_, bf16[256,128]{1,0:T(8,128)(2,1)S(1)} %get-tuple-element.38.refs_1_, bf16[256,128]{1,0:T(8,128)(2,1)S(1)} %get-tuple-element.41.refs_2_, bf16[256,128]{1,0:T(8,128)(2,1)S(1)} %get-tuple-element.44.refs_3_), custom_call_target="tpu_custom_call" | custom-call | tf_op jit(solution)/shard_map/pallas_call | solution.py:242
  38.2 2.0 %collective-permute-done.12.refs_0_ = bf16[384,128]{1,0:T(8,128)(2,1)S(1)} collective-permute-done((bf16[384,128]{1,0:T(8,128)(2,1)S(1)}, bf16[384,128]{1,0:T(8,128)(2,1)S(1)}, u32[]{:S(2)}, u32[]{:S(2)}) %collective-permute-start.12) | collective-permute-done | bytes 98336 | tf_op jit(solution)/shard_map/ppermute | solution.py:17
  40.2 1.6 %collective-permute-done.13.refs_1_ = bf16[384,128]{1,0:T(8,128)(2,1)S(1)} collective-permute-done((bf16[384,128]{1,0:T(8,128)(2,1)S(1)}, bf16[384,128]{1,0:T(8,128)(2,1)S(1)}, u32[]{:S(2)}, u32[]{:S(2)}) %collective-permute-start.13) | collective-permute-done | bytes 98336 | tf_op jit(solution)/shard_map/ppermute | solution.py:17
  41.9 0.7 %shard_map.98 = (f32[256,128]{1,0:T(8,128)}, f32[128,128]{1,0:T(8,128)}) custom-call(f32[256,128]{1,0:T(8,128)S(1)} %get-tuple-element.48.own_ref, bf16[128,128]{1,0:T(8,128)(2,1)S(1)} %get-tuple-element.49.own_weight_ref, bf16[384,128]{1,0:T(8,128)(2,1)S(1)} %collective-permute-done.11.got_ref, f32[384,128]{1,0:T(8,128)S(1)} %shard_map.97.refs_0_), custom_call_target="tpu_custom_call" | custom-call | tf_op jit(solution)/shard_map/pallas_call | solution.py:249
  (31 shorter events, 3.3 us)
Async XLA Ops:
  0.6 7.3 %collective-permute-start.1 = (bf16[256,128]{1,0:T(8,128)(2,1)}, bf16[256,128]{1,0:T(8,128)(2,1)S(1)}, u32[]{:S(2)}, u32[]{:S(2)}) collective-permute-start(bf16[256,128]{1,0:T(8,128)(2,1)} %refs_3_.1), channel_id=1, source_target_pairs={{0,4},{1,5},{2,6},{3,7},{4,0},{5,1},{6,2},{7,3},{8,12},{9,13},{10,... | collective-permute-start | bytes 196616 | tf_op jit(solution)/shard_map/ppermute | solution.py:17
  3.7 5.9 %collective-permute-start = (bf16[256,128]{1,0:T(8,128)(2,1)}, bf16[256,128]{1,0:T(8,128)(2,1)S(1)}, u32[]{:S(2)}, u32[]{:S(2)}) collective-permute-start(bf16[256,128]{1,0:T(8,128)(2,1)} %refs_3_.1), channel_id=1, source_target_pairs={{0,6},{1,7},{2,4},{3,5},{4,2},{5,3},{6,0},{7,1},{8,14},{9,15},{10,... | collective-permute-start | bytes 196616 | tf_op jit(solution)/shard_map/ppermute | solution.py:17
  5.1 4.5 %collective-permute-start.2 = (bf16[256,128]{1,0:T(8,128)(2,1)}, bf16[256,128]{1,0:T(8,128)(2,1)S(1)}, u32[]{:S(2)}, u32[]{:S(2)}) collective-permute-start(bf16[256,128]{1,0:T(8,128)(2,1)} %refs_3_.1), channel_id=1, source_target_pairs={{0,2},{1,3},{2,0},{3,1},{4,6},{5,7},{6,4},{7,5},{8,10},{9,11},{10,... | collective-permute-start | bytes 196616 | tf_op jit(solution)/shard_map/ppermute | solution.py:17
  6.0 0.7 %copy-start.5 = (f32[128]{0:T(128)S(1)}, f32[128]{0:T(128)}, u32[]{:S(2)}) copy-start(f32[128]{0:T(128)} %param.10) | copy-start | bytes 1540
  6.6 1.0 %copy-start.1 = (bf16[8,2,128,128]{3,2,1,0:T(8,128)(2,1)S(1)}, bf16[8,2,128,128]{3,2,1,0:T(8,128)(2,1)}, u32[]{:S(2)}) copy-start(bf16[8,2,128,128]{3,2,1,0:T(8,128)(2,1)} %vals_ref.3) | copy-start | bytes 1572868
  7.7 4.4 %copy-start.2 = (bf16[8,2,128,128]{3,2,1,0:T(8,128)(2,1)S(1)}, bf16[8,2,128,128]{3,2,1,0:T(8,128)(2,1)}, u32[]{:S(2)}) copy-start(bf16[8,2,128,128]{3,2,1,0:T(8,128)(2,1)} %vals_ref.3) | copy-start | bytes 1572868
  9.6 0.8 %copy-start.4 = (bf16[256,128]{1,0:T(8,128)(2,1)S(1)}, bf16[256,128]{1,0:T(8,128)(2,1)}, u32[]{:S(2)}) copy-start(bf16[256,128]{1,0:T(8,128)(2,1)} %refs_3_.1) | copy-start | bytes 196612
  10.4 1.6 %collective-permute-start.3 = (bf16[1024,128]{1,0:T(8,128)(2,1)S(1)}, bf16[1024,128]{1,0:T(8,128)(2,1)S(1)}, u32[]{:S(2)}, u32[]{:S(2)}) collective-permute-start(bf16[1024,128]{1,0:T(8,128)(2,1)S(1)} %shard_map.86.mine_ref), channel_id=1, source_target_pairs={{0,1},{1,0},{2,3},{3,2},{4,5},{5,4},{6,7},{7,6},{8,9},{9,8},{10,11... | collective-permute-start | bytes 786440 | tf_op jit(solution)/shard_map/ppermute | solution.py:17
  12.4 6.4 %collective-permute-start.4 = (bf16[256,128]{1,0:T(8,128)(2,1)S(1)}, bf16[256,128]{1,0:T(8,128)(2,1)S(1)}, u32[]{:S(2)}, u32[]{:S(2)}) collective-permute-start(bf16[256,128]{1,0:T(8,128)(2,1)S(1)} %get-tuple-element.32), channel_id=1, source_target_pairs={{0,24},{8,16},{16,8},{24,0},{1,25},{9,17},{17,9},{25,1},{2,26},{10... | collective-permute-start | bytes 196616 | tf_op jit(solution)/shard_map/ppermute | solution.py:17
  16.1 5.9 %collective-permute-start.5 = (bf16[256,128]{1,0:T(8,128)(2,1)S(1)}, bf16[256,128]{1,0:T(8,128)(2,1)S(1)}, u32[]{:S(2)}, u32[]{:S(2)}) collective-permute-start(bf16[256,128]{1,0:T(8,128)(2,1)S(1)} %get-tuple-element.33), channel_id=1, source_target_pairs={{0,16},{8,24},{16,0},{24,8},{1,17},{9,25},{17,1},{25,9},{2,18},{10... | collective-permute-start | bytes 196616 | tf_op jit(solution)/shard_map/ppermute | solution.py:17
  16.1 5.9 %collective-permute-start.6 = (bf16[256,128]{1,0:T(8,128)(2,1)S(1)}, bf16[256,128]{1,0:T(8,128)(2,1)S(1)}, u32[]{:S(2)}, u32[]{:S(2)}) collective-permute-start(bf16[256,128]{1,0:T(8,128)(2,1)S(1)} %get-tuple-element.34), channel_id=1, source_target_pairs={{0,8},{8,0},{16,24},{24,16},{1,9},{9,1},{17,25},{25,17},{2,10},{10... | collective-permute-start | bytes 196616 | tf_op jit(solution)/shard_map/ppermute | solution.py:17
  18.8 7.7 %copy-start = (bf16[1024,128]{1,0:T(8,128)(2,1)S(1)}, bf16[1024,128]{1,0:T(8,128)(2,1)}, u32[]{:S(2)}) copy-start(bf16[1024,128]{1,0:T(8,128)(2,1)} %cotangent_ref.7) | copy-start | bytes 786436
  22.0 4.5 %copy-start.3 = (bf16[128,128]{1,0:T(8,128)(2,1)S(1)}, bf16[128,128]{1,0:T(8,128)(2,1)}, u32[]{:S(2)}) copy-start(bf16[128,128]{1,0:T(8,128)(2,1)} %weight_ref.7) | copy-start | bytes 98308
  22.0 6.4 %collective-permute-start.7 = (bf16[256,128]{1,0:T(8,128)(2,1)S(1)}, bf16[256,128]{1,0:T(8,128)(2,1)S(1)}, u32[]{:S(2)}, u32[]{:S(2)}) collective-permute-start(bf16[256,128]{1,0:T(8,128)(2,1)S(1)} %shard_map.90.refs_0_), channel_id=1, source_target_pairs={{0,24},{8,16},{16,8},{24,0},{1,25},{9,17},{17,9},{25,1},{2,26},{10... | collective-permute-start | bytes 196616 | tf_op jit(solution)/shard_map/ppermute | solution.py:17
  24.6 6.5 %collective-permute-start.8 = (bf16[256,128]{1,0:T(8,128)(2,1)S(1)}, bf16[256,128]{1,0:T(8,128)(2,1)S(1)}, u32[]{:S(2)}, u32[]{:S(2)}) collective-permute-start(bf16[256,128]{1,0:T(8,128)(2,1)S(1)} %shard_map.90.refs_0_), channel_id=1, source_target_pairs={{0,16},{8,24},{16,0},{24,8},{1,17},{9,25},{17,1},{25,9},{2,18},{10... | collective-permute-start | bytes 196616 | tf_op jit(solution)/shard_map/ppermute | solution.py:17
  24.6 7.0 %collective-permute-start.9 = (bf16[256,128]{1,0:T(8,128)(2,1)S(1)}, bf16[256,128]{1,0:T(8,128)(2,1)S(1)}, u32[]{:S(2)}, u32[]{:S(2)}) collective-permute-start(bf16[256,128]{1,0:T(8,128)(2,1)S(1)} %shard_map.90.refs_0_), channel_id=1, source_target_pairs={{0,8},{8,0},{16,24},{24,16},{1,9},{9,1},{17,25},{25,17},{2,10},{10... | collective-permute-start | bytes 196616 | tf_op jit(solution)/shard_map/ppermute | solution.py:17
  32.2 1.6 %collective-permute-start.10 = (bf16[1152,128]{1,0:T(8,128)(2,1)S(1)}, bf16[1152,128]{1,0:T(8,128)(2,1)S(1)}, u32[]{:S(2)}, u32[]{:S(2)}) collective-permute-start(bf16[1152,128]{1,0:T(8,128)(2,1)S(1)} %get-tuple-element.47), channel_id=1, source_target_pairs={{0,1},{1,0},{2,3},{3,2},{4,5},{5,4},{6,7},{7,6},{8,9},{9,8},{10,11... | collective-permute-start | bytes 884744 | tf_op jit(solution)/shard_map/ppermute | solution.py:17
  33.9 6.3 %collective-permute-start.12 = (bf16[384,128]{1,0:T(8,128)(2,1)S(1)}, bf16[384,128]{1,0:T(8,128)(2,1)S(1)}, u32[]{:S(2)}, u32[]{:S(2)}) collective-permute-start(bf16[384,128]{1,0:T(8,128)(2,1)S(1)} %get-tuple-element.51), channel_id=1, source_target_pairs={{0,6},{1,7},{2,4},{3,5},{4,2},{5,3},{6,0},{7,1},{8,14},{9,15},{10,... | collective-permute-start | bytes 294920 | tf_op jit(solution)/shard_map/ppermute | solution.py:17
  35.6 6.2 %collective-permute-start.13 = (bf16[384,128]{1,0:T(8,128)(2,1)S(1)}, bf16[384,128]{1,0:T(8,128)(2,1)S(1)}, u32[]{:S(2)}, u32[]{:S(2)}) collective-permute-start(bf16[384,128]{1,0:T(8,128)(2,1)S(1)} %get-tuple-element.52), channel_id=1, source_target_pairs={{0,4},{1,5},{2,6},{3,7},{4,0},{5,1},{6,2},{7,3},{8,12},{9,13},{10,... | collective-permute-start | bytes 294920 | tf_op jit(solution)/shard_map/ppermute | solution.py:17
  36.4 5.5 %collective-permute-start.11 = (bf16[384,128]{1,0:T(8,128)(2,1)S(1)}, bf16[384,128]{1,0:T(8,128)(2,1)S(1)}, u32[]{:S(2)}, u32[]{:S(2)}) collective-permute-start(bf16[384,128]{1,0:T(8,128)(2,1)S(1)} %get-tuple-element.50), channel_id=1, source_target_pairs={{0,2},{1,3},{2,0},{3,1},{4,6},{5,7},{6,4},{7,5},{8,10},{9,11},{10,... | collective-permute-start | bytes 294920 | tf_op jit(solution)/shard_map/ppermute | solution.py:17

commit v5 on v4

--- a/solution.py
+++ b/solution.py
@@ -21,24 +21,44 @@
     return lax.dot_general(a, b, ((contract[:1], contract[1:]), ((), ())), preferred_element_type=F32)
 
 
-def early_kernel(own_blocks, dom, cols_ref, vals_ref, *refs):
-    flipped_ref, place_ref = refs[-2:]
+def early_kernel(vals_ref, features_ref, flipped_ref, own_ref):
     rows, count, size, _ = vals_ref.shape
+    own_ref[...] = features_ref[...]
     for row in range(rows):
         for k in range(count):
             flipped_ref[row, k * size : (k + 1) * size] = vals_ref[row, k].T
-            col = cols_ref[row, k] - lax.axis_index("rep") * (own_blocks * dom)
+
+
+def place_kernel(own_blocks, dom, cols_ref, _, place_ref):
+    count, rows = cols_ref.shape
+    for row in range(rows):
+        for k in range(count):
+            col = cols_ref[k, row] - lax.axis_index("rep") * (own_blocks * dom)
             owner = lax.div(col, jnp.int32(own_blocks)) ^ lax.axis_index("dom")
             place = ((owner & 1) * (dom // 2) + (owner >> 1)) * own_blocks
             place += lax.rem(col, jnp.int32(own_blocks))
             place_ref[row * count + k : row * count + k + 1, :] = jnp.full((1, 128), place, jnp.int32)
 
 
-def join_kernel(order, *refs):
-    pieces, out_ref = refs[: len(order)], refs[-1]
-    nodes = pieces[0].shape[0]
-    for chip, piece in zip(order, pieces):
-        out_ref[chip * nodes : (chip + 1) * nodes] = piece[...]
+def join_kernel(*refs):
+    pieces, out_ref = refs[:-1], refs[-1]
+    first = 0
+    for piece in pieces:
+        out_ref[first : first + piece.shape[0]] = piece[...]
+        first += piece.shape[0]
+
+
+def last_join_kernel(*refs):
+    near, middle, out_ref = refs[:-2], refs[-2], refs[-1]
+    nodes = near[0].shape[0]
+    body = middle.shape[0] - 2 * nodes
+    out_ref[:nodes] = middle[body : body + nodes]
+    first = nodes
+    for piece in near:
+        out_ref[first : first + nodes] = piece[...]
+        first += nodes
+    out_ref[first : first + body] = middle[:body]
+    out_ref[first + body :] = middle[body + nodes :]
 
 
 def aggregate_kernel(rep, place_ref, vals_ref, mine_ref, far_ref, *outs):
@@ -112,7 +132,7 @@
     out_ref[...] = (a_ref[...] + b_ref[...].astype(F32)).astype(out_ref.dtype)
 
 
-def place_kernel(order, *refs):
+def order_kernel(order, *refs):
     pieces, out_ref = refs[:-1], refs[-1]
     part = pieces[0].shape[0]
     for j, piece in zip(order, pieces):
@@ -182,18 +202,28 @@
             compiler_params=params,
         )
 
-    bias = bias.reshape(1, width)
-    flipped, place = call(
-        functools.partial(early_kernel, own_blocks, dom),
-        [shape((rows, count * size, size), BF16), shape((rows * count, 128), jnp.int32)],
-        [VMEM] * 3,
-    )(cols, vals, bias)
-    order = list(range(chips - 1, -1, -1))
-    across = [swap(features, "dom", 2 * chip) for chip in order[:-1]] + [features]
-    mine = call(
-        functools.partial(join_kernel, order), shape((chips * nodes, width), BF16), [VMEM] * (chips + 1)
-    )(*across, place)
+    flipped, own = call(
+        early_kernel,
+        [shape((rows, count * size, size), BF16), shape(features.shape, BF16)],
+        [VMEM] * 2,
+    )(vals, features)
+
+    def join(*values):
+        nodes_in = sum(v.shape[0] for v in values)
+        return call(join_kernel, shape((nodes_in, width), BF16), [VMEM] * len(values))(*values)
+
+    across = [swap(features, "dom", 2 * chip) for chip in range(1, chips)]
+    front = join(own, across[-1])
+    middle = join(*across[chips // 2 - 1 : -1], front)
+    mine = call(last_join_kernel, shape((chips * nodes, width), BF16), [VMEM] * (chips // 2))(
+        *across[: chips // 2 - 1], middle
+    )
     far = swap(mine, "dom", 1)
+    place = call(
+        functools.partial(place_kernel, own_blocks, dom),
+        shape((rows * count, 128), jnp.int32),
+        [VMEM] * 2,
+    )(cols.T, mine)
 
     partials = call(
         functools.partial(aggregate_kernel, rep),
@@ -201,14 +231,14 @@
         [VMEM] * 4,
     )(place, vals, mine, far)
     arrived = {j: swap(partials[j], "rep", j) if j else partials[j] for j in range(rep)}
+    order = [*range(2, rep), 1]
     own_rows = arrived[0]
-    for j in range(rep - 1, 0, -1):
+    for j in order:
         own_rows = call(add_kernel, shape((part, width), F32 if j > 1 else BF16), [VMEM] * 2)(
             own_rows, arrived[j]
         )
-
     pieces = {0: own_rows}
-    for j in range(rep - 1, 0, -1):
+    for j in order:
         pieces[j] = swap(own_rows, "rep", j)
 
     outputs, carried = [], []
@@ -240,7 +270,7 @@
     )(keep, keep_weight, swap(send, "dom", 1))
     got = {chip: swap(sends[chip - 1], "dom", 2 * chip) for chip in range(chips - 1, 0, -1)}
     output = call(
-        functools.partial(place_kernel, list(pieces)), shape((rows * size, width), BF16), [VMEM] * rep
+        functools.partial(order_kernel, list(pieces)), shape((rows * size, width), BF16), [VMEM] * rep
     )(*outputs)
     levels = chips.bit_length() - 1
     later = call(

time: 42.8 us -> 41.7 us (0.974)
  starting transfers between devices: 17.2 us -> 16.3 us
  local copies, waits for them, and re-layouts: 3.3 us -> 2.5 us
    ppermute x14, starting transfers between devices: 17.2 us -> 16.3 us  [swap(): return lax.ppermute(value, axis, [(i, i ^ distance) for i in range(size)])]
    unnamed x13 -> x14, local copies, waits for them, and re-layouts: 3.3 us -> 2.5 us
    pallas_call x3 -> x6, Pallas kernels: 0.99 us -> 1.12 us  [the longest x1 0.72 us: body(): call(functools.partial(order_kernel, list(pieces)), shape((rows * size, w...]
  transfers between devices with their start and end apart: 14 -> 14, of which waited for: 10 -> 12; matrix products, arithmetic and copies ran while one was open for 2% -> 0% of each run, Pallas kernels for 6% -> 7%
where the time goes in v5:
time: 41.7 us; the launch traced here: 41.5 us
  waiting for transfers between devices  17.5 us (42%)
  starting transfers between devices  16.3 us (39%)
  Pallas kernels  4.43 us (11%)
  local copies, waits for them, and re-layouts  2.5 us (6%)
  between operations  0.79 us (2%)
    ppermute x14, waiting for transfers between devices, swap(): return lax.ppermute(value, axis, [(i, i ^ distance) for i in range(size)])  17.5 us
    ppermute x14, starting transfers between devices, swap(): return lax.ppermute(value, axis, [(i, i ^ distance) for i in range(size)])  16.3 us
    unnamed x14, local copies, waits for them, and re-layouts  2.5 us
    pallas_call x4, Pallas kernels, body(): call(functools.partial(layer_kernel, rep, count, own_blocks, j), [shape((...  2.14 us
  transfers between devices with their start and end apart: 14, of which 12 were waited for; matrix products, arithmetic and copies ran while one was open for 0% of the time, Pallas kernels for 7%

profile of v5, /device:TPU:0, one launch (start us, length us, event | category | flops | bytes accessed | tf_op | source)
XLA Modules:
  0.0 41.5 jit_solution(11901206208547081001)
XLA Ops:
  0.6 4.0 %collective-permute-start.2 = (bf16[256,128]{1,0:T(8,128)(2,1)}, bf16[256,128]{1,0:T(8,128)(2,1)S(1)}, u32[]{:S(2)}, u32[]{:S(2)}) collective-permute-start(bf16[256,128]{1,0:T(8,128)(2,1)} %features_ref.1), channel_id=1, source_target_pairs={{0,6},{1,7},{2,4},{3,5},{4,2},{5,3},{6,0},{7,1},{8,14},{9,15},{10,... | collective-permute-start | bytes 196616 | tf_op jit(solution)/shard_map/ppermute | solution.py:17
  5.2 1.0 %copy-done.1 = bf16[8,2,128,128]{3,2,1,0:T(8,128)(2,1)S(1)} copy-done((bf16[8,2,128,128]{3,2,1,0:T(8,128)(2,1)S(1)}, bf16[8,2,128,128]{3,2,1,0:T(8,128)(2,1)}, u32[]{:S(2)}) %copy-start.1) | copy-done | bytes 524312
  6.3 0.8 %copy-done.4 = bf16[256,128]{1,0:T(8,128)(2,1)S(1)} copy-done((bf16[256,128]{1,0:T(8,128)(2,1)S(1)}, bf16[256,128]{1,0:T(8,128)(2,1)}, u32[]{:S(2)}) %copy-start.4) | copy-done | bytes 65560
  7.3 1.7 %collective-permute-done.1.refs_0_ = bf16[256,128]{1,0:T(8,128)(2,1)S(1)} collective-permute-done((bf16[256,128]{1,0:T(8,128)(2,1)}, bf16[256,128]{1,0:T(8,128)(2,1)S(1)}, u32[]{:S(2)}, u32[]{:S(2)}) %collective-permute-start.1) | collective-permute-done | bytes 65568 | tf_op jit(solution)/shard_map/ppermute | solution.py:17
  9.7 0.6 %copy-done.6 = s32[8,2]{0,1:T(2,128)S(1)} copy-done((s32[8,2]{0,1:T(2,128)S(1)}, s32[8,2]{0,1:T(2,128)}, u32[]{:S(2)}) %copy-start.6) | copy-done | bytes 88
  10.5 0.8 %collective-permute-done.3.far_ref = bf16[1024,128]{1,0:T(8,128)(2,1)S(1)} collective-permute-done((bf16[1024,128]{1,0:T(8,128)(2,1)S(1)}, bf16[1024,128]{1,0:T(8,128)(2,1)S(1)}, u32[]{:S(2)}, u32[]{:S(2)}) %collective-permute-start.3) | collective-permute-done | bytes 262176 | tf_op jit(solution)/shard_map/ppermute | solution.py:17
  11.6 2.7 %collective-permute-start.4 = (bf16[256,128]{1,0:T(8,128)(2,1)S(1)}, bf16[256,128]{1,0:T(8,128)(2,1)S(1)}, u32[]{:S(2)}, u32[]{:S(2)}) collective-permute-start(bf16[256,128]{1,0:T(8,128)(2,1)S(1)} %get-tuple-element.32), channel_id=1, source_target_pairs={{0,16},{8,24},{16,0},{24,8},{1,17},{9,25},{17,1},{25,9},{2,18},{10... | collective-permute-start | bytes 196616 | tf_op jit(solution)/shard_map/ppermute | solution.py:17
  14.2 1.3 %collective-permute-start.5 = (bf16[256,128]{1,0:T(8,128)(2,1)S(1)}, bf16[256,128]{1,0:T(8,128)(2,1)S(1)}, u32[]{:S(2)}, u32[]{:S(2)}) collective-permute-start(bf16[256,128]{1,0:T(8,128)(2,1)S(1)} %get-tuple-element.33), channel_id=1, source_target_pairs={{0,24},{8,16},{16,8},{24,0},{1,25},{9,17},{17,9},{25,1},{2,26},{10... | collective-permute-start | bytes 196616 | tf_op jit(solution)/shard_map/ppermute | solution.py:17
  15.8 3.5 %collective-permute-done.4.b_ref = bf16[256,128]{1,0:T(8,128)(2,1)S(1)} collective-permute-done((bf16[256,128]{1,0:T(8,128)(2,1)S(1)}, bf16[256,128]{1,0:T(8,128)(2,1)S(1)}, u32[]{:S(2)}, u32[]{:S(2)}) %collective-permute-start.4) | collective-permute-done | bytes 65568 | tf_op jit(solution)/shard_map/ppermute | solution.py:17
  19.4 1.3 %collective-permute-done.5.b_ref = bf16[256,128]{1,0:T(8,128)(2,1)S(1)} collective-permute-done((bf16[256,128]{1,0:T(8,128)(2,1)S(1)}, bf16[256,128]{1,0:T(8,128)(2,1)S(1)}, u32[]{:S(2)}, u32[]{:S(2)}) %collective-permute-start.5) | collective-permute-done | bytes 65568 | tf_op jit(solution)/shard_map/ppermute | solution.py:17
  21.0 2.7 %collective-permute-start.7 = (bf16[256,128]{1,0:T(8,128)(2,1)S(1)}, bf16[256,128]{1,0:T(8,128)(2,1)S(1)}, u32[]{:S(2)}, u32[]{:S(2)}) collective-permute-start(bf16[256,128]{1,0:T(8,128)(2,1)S(1)} %shard_map.93.refs_0_), channel_id=1, source_target_pairs={{0,16},{8,24},{16,0},{24,8},{1,17},{9,25},{17,1},{25,9},{2,18},{10... | collective-permute-start | bytes 196616 | tf_op jit(solution)/shard_map/ppermute | solution.py:17
  23.7 0.6 %collective-permute-start.8 = (bf16[256,128]{1,0:T(8,128)(2,1)S(1)}, bf16[256,128]{1,0:T(8,128)(2,1)S(1)}, u32[]{:S(2)}, u32[]{:S(2)}) collective-permute-start(bf16[256,128]{1,0:T(8,128)(2,1)S(1)} %shard_map.93.refs_0_), channel_id=1, source_target_pairs={{0,24},{8,16},{16,8},{24,0},{1,25},{9,17},{17,9},{25,1},{2,26},{10... | collective-permute-start | bytes 196616 | tf_op jit(solution)/shard_map/ppermute | solution.py:17
  25.3 2.4 %collective-permute-done.7.refs_0_ = bf16[256,128]{1,0:T(8,128)(2,1)S(1)} collective-permute-done((bf16[256,128]{1,0:T(8,128)(2,1)S(1)}, bf16[256,128]{1,0:T(8,128)(2,1)S(1)}, u32[]{:S(2)}, u32[]{:S(2)}) %collective-permute-start.7) | collective-permute-done | bytes 65568 | tf_op jit(solution)/shard_map/ppermute | solution.py:17
  27.7 0.5 %shard_map.95 = (bf16[256,128]{1,0:T(8,128)(2,1)S(1)}, f32[16,128,128]{2,1,0:T(8,128)S(1)}, f32[128,128]{1,0:T(8,128)S(1)}) custom-call(s32[16,128]{1,0:T(8,128)S(1)} %shard_map.89.place_ref, bf16[8,256,128]{2,1,0:T(8,128)(2,1)S(1)} %get-tuple-element.30.flipped_ref, bf16[1024,128]{1,0:T(8,128)(2,1)S(1)} %copy-done, bf16[128,128]{1,0:T(8,128)(2,1)S(1)} %copy-done.3, ...), custom_call_target="tpu_custom_call" | custom-call | tf_op jit(solution)/shard_map/pallas_call | solution.py:256
  28.2 1.8 %collective-permute-done.8.refs_0_ = bf16[256,128]{1,0:T(8,128)(2,1)S(1)} collective-permute-done((bf16[256,128]{1,0:T(8,128)(2,1)S(1)}, bf16[256,128]{1,0:T(8,128)(2,1)S(1)}, u32[]{:S(2)}, u32[]{:S(2)}) %collective-permute-start.8) | collective-permute-done | bytes 65568 | tf_op jit(solution)/shard_map/ppermute | solution.py:17
  30.0 0.5 %shard_map.96 = (bf16[256,128]{1,0:T(8,128)(2,1)S(1)}, f32[16,128,128]{2,1,0:T(8,128)S(1)}, f32[128,128]{1,0:T(8,128)S(1)}) custom-call(s32[16,128]{1,0:T(8,128)S(1)} %shard_map.89.place_ref, bf16[8,256,128]{2,1,0:T(8,128)(2,1)S(1)} %get-tuple-element.30.flipped_ref, bf16[1024,128]{1,0:T(8,128)(2,1)S(1)} %copy-done, bf16[128,128]{1,0:T(8,128)(2,1)S(1)} %copy-done.3, ...), custom_call_target="tpu_custom_call" | custom-call | tf_op jit(solution)/shard_map/pallas_call | solution.py:256
  30.5 0.6 %shard_map.97 = (bf16[256,128]{1,0:T(8,128)(2,1)S(1)}, bf16[1152,128]{1,0:T(8,128)(2,1)S(1)}, f32[4,256,128]{2,1,0:T(8,128)S(1)}, bf16[128,128]{1,0:T(8,128)(2,1)S(1)}) custom-call(s32[16,128]{1,0:T(8,128)S(1)} %shard_map.89.place_ref, bf16[8,256,128]{2,1,0:T(8,128)(2,1)S(1)} %get-tuple-element.30.flipped_ref, bf16[1024,128]{1,0:T(8,128)(2,1)S(1)} %copy-done, ...), custom_call_target="tpu_custom_call" | custom-call | tf_op jit(solution)/shard_map/pallas_call | solution.py:256
  31.2 1.6 %collective-permute-done.10.got_ref = bf16[1152,128]{1,0:T(8,128)(2,1)S(1)} collective-permute-done((bf16[1152,128]{1,0:T(8,128)(2,1)S(1)}, bf16[1152,128]{1,0:T(8,128)(2,1)S(1)}, u32[]{:S(2)}, u32[]{:S(2)}) %collective-permute-start.10) | collective-permute-done | bytes 294944 | tf_op jit(solution)/shard_map/ppermute | solution.py:17
  32.8 1.6 %collective-permute-start.12 = (bf16[384,128]{1,0:T(8,128)(2,1)S(1)}, bf16[384,128]{1,0:T(8,128)(2,1)S(1)}, u32[]{:S(2)}, u32[]{:S(2)}) collective-permute-start(bf16[384,128]{1,0:T(8,128)(2,1)S(1)} %get-tuple-element.51), channel_id=1, source_target_pairs={{0,6},{1,7},{2,4},{3,5},{4,2},{5,3},{6,0},{7,1},{8,14},{9,15},{10,... | collective-permute-start | bytes 294920 | tf_op jit(solution)/shard_map/ppermute | solution.py:17
  34.8 1.5 %collective-permute-start.11 = (bf16[384,128]{1,0:T(8,128)(2,1)S(1)}, bf16[384,128]{1,0:T(8,128)(2,1)S(1)}, u32[]{:S(2)}, u32[]{:S(2)}) collective-permute-start(bf16[384,128]{1,0:T(8,128)(2,1)S(1)} %get-tuple-element.50), channel_id=1, source_target_pairs={{0,2},{1,3},{2,0},{3,1},{4,6},{5,7},{6,4},{7,5},{8,10},{9,11},{10,... | collective-permute-start | bytes 294920 | tf_op jit(solution)/shard_map/ppermute | solution.py:17
  36.3 0.7 %shard_map.98 = bf16[1024,128]{1,0:T(8,128)(2,1)} custom-call(bf16[256,128]{1,0:T(8,128)(2,1)S(1)} %get-tuple-element.35.refs_0_, bf16[256,128]{1,0:T(8,128)(2,1)S(1)} %get-tuple-element.38.refs_1_, bf16[256,128]{1,0:T(8,128)(2,1)S(1)} %get-tuple-element.41.refs_2_, bf16[256,128]{1,0:T(8,128)(2,1)S(1)} %get-tuple-element.44.refs_3_), custom_call_target="tpu_custom_call" | custom-call | tf_op jit(solution)/shard_map/pallas_call | solution.py:272
  37.1 2.2 %collective-permute-done.12.refs_0_ = bf16[384,128]{1,0:T(8,128)(2,1)S(1)} collective-permute-done((bf16[384,128]{1,0:T(8,128)(2,1)S(1)}, bf16[384,128]{1,0:T(8,128)(2,1)S(1)}, u32[]{:S(2)}, u32[]{:S(2)}) %collective-permute-start.12) | collective-permute-done | bytes 98336 | tf_op jit(solution)/shard_map/ppermute | solution.py:17
  39.2 1.4 %collective-permute-done.13.refs_1_ = bf16[384,128]{1,0:T(8,128)(2,1)S(1)} collective-permute-done((bf16[384,128]{1,0:T(8,128)(2,1)S(1)}, bf16[384,128]{1,0:T(8,128)(2,1)S(1)}, u32[]{:S(2)}, u32[]{:S(2)}) %collective-permute-start.13) | collective-permute-done | bytes 98336 | tf_op jit(solution)/shard_map/ppermute | solution.py:17
  40.8 0.7 %shard_map.101 = (f32[256,128]{1,0:T(8,128)}, f32[128,128]{1,0:T(8,128)}) custom-call(f32[256,128]{1,0:T(8,128)S(1)} %get-tuple-element.48.own_ref, bf16[128,128]{1,0:T(8,128)(2,1)S(1)} %get-tuple-element.49.own_weight_ref, bf16[384,128]{1,0:T(8,128)(2,1)S(1)} %collective-permute-done.11.got_ref, f32[384,128]{1,0:T(8,128)S(1)} %shard_map.100.refs_0_), custom_call_target="tpu_custom_call" | custom-call | tf_op jit(solution)/shard_map/pallas_call | solution.py:279
  (35 shorter events, 4.3 us)
Async XLA Ops:
  0.6 6.7 %collective-permute-start.2 = (bf16[256,128]{1,0:T(8,128)(2,1)}, bf16[256,128]{1,0:T(8,128)(2,1)S(1)}, u32[]{:S(2)}, u32[]{:S(2)}) collective-permute-start(bf16[256,128]{1,0:T(8,128)(2,1)} %features_ref.1), channel_id=1, source_target_pairs={{0,6},{1,7},{2,4},{3,5},{4,2},{5,3},{6,0},{7,1},{8,14},{9,15},{10,... | collective-permute-start | bytes 196616 | tf_op jit(solution)/shard_map/ppermute | solution.py:17
  4.6 4.5 %collective-permute-start.1 = (bf16[256,128]{1,0:T(8,128)(2,1)}, bf16[256,128]{1,0:T(8,128)(2,1)S(1)}, u32[]{:S(2)}, u32[]{:S(2)}) collective-permute-start(bf16[256,128]{1,0:T(8,128)(2,1)} %features_ref.1), channel_id=1, source_target_pairs={{0,4},{1,5},{2,6},{3,7},{4,0},{5,1},{6,2},{7,3},{8,12},{9,13},{10,... | collective-permute-start | bytes 196616 | tf_op jit(solution)/shard_map/ppermute | solution.py:17
  5.1 4.5 %collective-permute-start = (bf16[256,128]{1,0:T(8,128)(2,1)}, bf16[256,128]{1,0:T(8,128)(2,1)S(1)}, u32[]{:S(2)}, u32[]{:S(2)}) collective-permute-start(bf16[256,128]{1,0:T(8,128)(2,1)} %features_ref.1), channel_id=1, source_target_pairs={{0,2},{1,3},{2,0},{3,1},{4,6},{5,7},{6,4},{7,5},{8,10},{9,11},{10,... | collective-permute-start | bytes 196616 | tf_op jit(solution)/shard_map/ppermute | solution.py:17
  5.2 1.0 %copy-start.1 = (bf16[8,2,128,128]{3,2,1,0:T(8,128)(2,1)S(1)}, bf16[8,2,128,128]{3,2,1,0:T(8,128)(2,1)}, u32[]{:S(2)}) copy-start(bf16[8,2,128,128]{3,2,1,0:T(8,128)(2,1)} %vals_ref.3) | copy-start | bytes 1572868
  6.3 0.8 %copy-start.4 = (bf16[256,128]{1,0:T(8,128)(2,1)S(1)}, bf16[256,128]{1,0:T(8,128)(2,1)}, u32[]{:S(2)}) copy-start(bf16[256,128]{1,0:T(8,128)(2,1)} %features_ref.1) | copy-start | bytes 196612
  7.3 3.9 %copy-start.2 = (bf16[8,2,128,128]{3,2,1,0:T(8,128)(2,1)S(1)}, bf16[8,2,128,128]{3,2,1,0:T(8,128)(2,1)}, u32[]{:S(2)}) copy-start(bf16[8,2,128,128]{3,2,1,0:T(8,128)(2,1)} %vals_ref.3) | copy-start | bytes 1572868
  9.6 0.7 %copy-start.6 = (s32[8,2]{0,1:T(2,128)S(1)}, s32[8,2]{0,1:T(2,128)}, u32[]{:S(2)}) copy-start(s32[8,2]{0,1:T(2,128)} %param.6) | copy-start | bytes 196
  9.6 1.6 %collective-permute-start.3 = (bf16[1024,128]{1,0:T(8,128)(2,1)S(1)}, bf16[1024,128]{1,0:T(8,128)(2,1)S(1)}, u32[]{:S(2)}, u32[]{:S(2)}) collective-permute-start(bf16[1024,128]{1,0:T(8,128)(2,1)S(1)} %shard_map.88._.mine_ref), channel_id=1, source_target_pairs={{0,1},{1,0},{2,3},{3,2},{4,5},{5,4},{6,7},{7,6},{8,9},{9,8},{10,11... | collective-permute-start | bytes 786440 | tf_op jit(solution)/shard_map/ppermute | solution.py:17
  11.6 7.8 %collective-permute-start.4 = (bf16[256,128]{1,0:T(8,128)(2,1)S(1)}, bf16[256,128]{1,0:T(8,128)(2,1)S(1)}, u32[]{:S(2)}, u32[]{:S(2)}) collective-permute-start(bf16[256,128]{1,0:T(8,128)(2,1)S(1)} %get-tuple-element.32), channel_id=1, source_target_pairs={{0,16},{8,24},{16,0},{24,8},{1,17},{9,25},{17,1},{25,9},{2,18},{10... | collective-permute-start | bytes 196616 | tf_op jit(solution)/shard_map/ppermute | solution.py:17
  14.2 6.4 %collective-permute-start.5 = (bf16[256,128]{1,0:T(8,128)(2,1)S(1)}, bf16[256,128]{1,0:T(8,128)(2,1)S(1)}, u32[]{:S(2)}, u32[]{:S(2)}) collective-permute-start(bf16[256,128]{1,0:T(8,128)(2,1)S(1)} %get-tuple-element.33), channel_id=1, source_target_pairs={{0,24},{8,16},{16,8},{24,0},{1,25},{9,17},{17,9},{25,1},{2,26},{10... | collective-permute-start | bytes 196616 | tf_op jit(solution)/shard_map/ppermute | solution.py:17
  15.6 5.4 %collective-permute-start.6 = (bf16[256,128]{1,0:T(8,128)(2,1)S(1)}, bf16[256,128]{1,0:T(8,128)(2,1)S(1)}, u32[]{:S(2)}, u32[]{:S(2)}) collective-permute-start(bf16[256,128]{1,0:T(8,128)(2,1)S(1)} %get-tuple-element.34), channel_id=1, source_target_pairs={{0,8},{8,0},{16,24},{24,16},{1,9},{9,1},{17,25},{25,17},{2,10},{10... | collective-permute-start | bytes 196616 | tf_op jit(solution)/shard_map/ppermute | solution.py:17
  19.4 5.4 %copy-start = (bf16[1024,128]{1,0:T(8,128)(2,1)S(1)}, bf16[1024,128]{1,0:T(8,128)(2,1)}, u32[]{:S(2)}) copy-start(bf16[1024,128]{1,0:T(8,128)(2,1)} %cotangent_ref.7) | copy-start | bytes 786436
  20.6 4.1 %copy-start.3 = (bf16[128,128]{1,0:T(8,128)(2,1)S(1)}, bf16[128,128]{1,0:T(8,128)(2,1)}, u32[]{:S(2)}) copy-start(bf16[128,128]{1,0:T(8,128)(2,1)} %weight_ref.7) | copy-start | bytes 98308
  21.0 3.8 %copy-start.5 = (f32[128]{0:T(128)S(1)}, f32[128]{0:T(128)}, u32[]{:S(2)}) copy-start(f32[128]{0:T(128)} %bias_ref.7) | copy-start | bytes 1540
  21.0 6.7 %collective-permute-start.7 = (bf16[256,128]{1,0:T(8,128)(2,1)S(1)}, bf16[256,128]{1,0:T(8,128)(2,1)S(1)}, u32[]{:S(2)}, u32[]{:S(2)}) collective-permute-start(bf16[256,128]{1,0:T(8,128)(2,1)S(1)} %shard_map.93.refs_0_), channel_id=1, source_target_pairs={{0,16},{8,24},{16,0},{24,8},{1,17},{9,25},{17,1},{25,9},{2,18},{10... | collective-permute-start | bytes 196616 | tf_op jit(solution)/shard_map/ppermute | solution.py:17
  23.7 6.3 %collective-permute-start.8 = (bf16[256,128]{1,0:T(8,128)(2,1)S(1)}, bf16[256,128]{1,0:T(8,128)(2,1)S(1)}, u32[]{:S(2)}, u32[]{:S(2)}) collective-permute-start(bf16[256,128]{1,0:T(8,128)(2,1)S(1)} %shard_map.93.refs_0_), channel_id=1, source_target_pairs={{0,24},{8,16},{16,8},{24,0},{1,25},{9,17},{17,9},{25,1},{2,26},{10... | collective-permute-start | bytes 196616 | tf_op jit(solution)/shard_map/ppermute | solution.py:17
  24.3 6.2 %collective-permute-start.9 = (bf16[256,128]{1,0:T(8,128)(2,1)S(1)}, bf16[256,128]{1,0:T(8,128)(2,1)S(1)}, u32[]{:S(2)}, u32[]{:S(2)}) collective-permute-start(bf16[256,128]{1,0:T(8,128)(2,1)S(1)} %shard_map.93.refs_0_), channel_id=1, source_target_pairs={{0,8},{8,0},{16,24},{24,16},{1,9},{9,1},{17,25},{25,17},{2,10},{10... | collective-permute-start | bytes 196616 | tf_op jit(solution)/shard_map/ppermute | solution.py:17
  31.1 1.6 %collective-permute-start.10 = (bf16[1152,128]{1,0:T(8,128)(2,1)S(1)}, bf16[1152,128]{1,0:T(8,128)(2,1)S(1)}, u32[]{:S(2)}, u32[]{:S(2)}) collective-permute-start(bf16[1152,128]{1,0:T(8,128)(2,1)S(1)} %get-tuple-element.47), channel_id=1, source_target_pairs={{0,1},{1,0},{2,3},{3,2},{4,5},{5,4},{6,7},{7,6},{8,9},{9,8},{10,11... | collective-permute-start | bytes 884744 | tf_op jit(solution)/shard_map/ppermute | solution.py:17
  32.8 6.5 %collective-permute-start.12 = (bf16[384,128]{1,0:T(8,128)(2,1)S(1)}, bf16[384,128]{1,0:T(8,128)(2,1)S(1)}, u32[]{:S(2)}, u32[]{:S(2)}) collective-permute-start(bf16[384,128]{1,0:T(8,128)(2,1)S(1)} %get-tuple-element.51), channel_id=1, source_target_pairs={{0,6},{1,7},{2,4},{3,5},{4,2},{5,3},{6,0},{7,1},{8,14},{9,15},{10,... | collective-permute-start | bytes 294920 | tf_op jit(solution)/shard_map/ppermute | solution.py:17
  34.3 6.3 %collective-permute-start.13 = (bf16[384,128]{1,0:T(8,128)(2,1)S(1)}, bf16[384,128]{1,0:T(8,128)(2,1)S(1)}, u32[]{:S(2)}, u32[]{:S(2)}) collective-permute-start(bf16[384,128]{1,0:T(8,128)(2,1)S(1)} %get-tuple-element.52), channel_id=1, source_target_pairs={{0,4},{1,5},{2,6},{3,7},{4,0},{5,1},{6,2},{7,3},{8,12},{9,13},{10,... | collective-permute-start | bytes 294920 | tf_op jit(solution)/shard_map/ppermute | solution.py:17
  34.8 6.0 %collective-permute-start.11 = (bf16[384,128]{1,0:T(8,128)(2,1)S(1)}, bf16[384,128]{1,0:T(8,128)(2,1)S(1)}, u32[]{:S(2)}, u32[]{:S(2)}) collective-permute-start(bf16[384,128]{1,0:T(8,128)(2,1)S(1)} %get-tuple-element.50), channel_id=1, source_target_pairs={{0,2},{1,3},{2,0},{3,1},{4,6},{5,7},{6,4},{7,5},{8,10},{9,11},{10,... | collective-permute-start | bytes 294920 | tf_op jit(solution)/shard_map/ppermute | solution.py:17

commit v6 on v5

--- a/solution.py
+++ b/solution.py
@@ -63,81 +63,108 @@
 
 def aggregate_kernel(rep, place_ref, vals_ref, mine_ref, far_ref, *outs):
     rows, count, size, _ = vals_ref.shape
-    half = mine_ref.shape[0] // size
+    blocks = mine_ref.shape[0] // size
     share = rows // rep
-    for j in range(rep - 1, -1, -1):
+    for j in (*range(2, rep), 1, 0):
         target = lax.axis_index("rep") ^ j
         for i in range(share):
             row = target * share + i
             total = None
             for k in range(count):
                 place = place_ref[row * count + k, 0]
-                beyond = place >= half
-                index = jnp.where(beyond, place - half, place)
+                beyond = place >= blocks
+                index = jnp.where(beyond, place - blocks, place)
                 here = pl.ds(pl.multiple_of(index * size, size), size)
                 block = jnp.where(beyond, far_ref[here, :], mine_ref[here, :])
                 term = matmul(vals_ref[row, k], block, (1, 0))
                 total = term if total is None else total + term
-            outs[j][i * size : (i + 1) * size] = total.astype(outs[j].dtype)
+            half, at = (0, i) if j == 1 else divmod(i, share // 2)
+            out_ref = outs[-1] if j == 1 else outs[2 * max(j - 1, 0) + half]
+            out_ref[at * size : (at + 1) * size] = total.astype(out_ref.dtype)
 
 
 def layer_kernel(
-    rep, count, own_blocks, j, place_ref, flipped_ref, cotangent_ref, weight_ref, bias_ref, *refs
+    rep, count, own_blocks, segments, stage, place_ref, flipped_ref, cotangent_ref, weight_ref,
+    bias_ref, *refs
 ):
-    first, last = j == 0, j == 1
-    piece_ref, refs = refs[0], refs[1:]
-    if not first:
-        (contrib_in, weight_in), refs = refs[:2], refs[2:]
-    if last:
+    pieces, refs = refs[: len(segments)], refs[len(segments) :]
+    if stage > 0:
+        (contrib_in, sums_in), refs = refs[:2], refs[2:]
+    if stage == 3:
         output_ref, send_ref, keep_ref, keep_weight_ref, contrib = refs
     else:
-        output_ref, contrib, weight_out = refs
+        output_ref, contrib, sums_out = refs
     rows, _, size = flipped_ref.shape
-    share = rows // rep
+    part = rows * size // rep
     quarter_blocks = contrib.shape[0]
     nodes = own_blocks * size
-    contrib[...] = jnp.zeros_like(contrib) if first else contrib_in[...]
-
-    target = lax.axis_index("rep") ^ j
-    aggregated = piece_ref[...]
-    part = aggregated.shape[0]
-    here = pl.ds(pl.multiple_of(target * part, part), part)
+    contrib[...] = contrib_in[...] if stage > 0 else jnp.zeros_like(contrib)
+
+    def joined(values):
+        return values[0] if len(values) == 1 else jnp.concatenate(values)
+
+    starts = [(lax.axis_index("rep") ^ j) * part + first for j, first, _ in segments]
+    aggregated = joined([piece[...] for piece in pieces])
+    gradient = joined(
+        [
+            cotangent_ref[pl.ds(pl.multiple_of(start, size), length), :]
+            for start, (_, _, length) in zip(starts, segments)
+        ]
+    ).astype(F32)
     hidden = matmul(aggregated, weight_ref[...], (1, 0)) + bias_ref[...]
     gate_prob = jax.nn.sigmoid(hidden)
     output_ref[...] = (hidden * gate_prob).astype(BF16)
-    grad_hidden = (
-        cotangent_ref[here, :].astype(F32) * gate_prob * (1.0 + hidden * (1.0 - gate_prob))
-    ).astype(BF16)
-    weight_part = matmul(aggregated, grad_hidden, (0, 0))
-    if not first:
-        weight_part = weight_in[...] + weight_part
+    grad_hidden = (gradient * gate_prob * (1.0 + hidden * (1.0 - gate_prob))).astype(BF16)
     grad_agg = matmul(grad_hidden, weight_ref[...], (1, 1)).astype(BF16)
-    for i in range(share):
-        row = target * share + i
-        terms = matmul(flipped_ref[row], grad_agg[i * size : (i + 1) * size], (1, 0))
-        for k in range(count):
-            contrib[place_ref[row * count + k, 0]] += terms[k * size : (k + 1) * size]
-    if not last:
-        weight_out[...] = weight_part
+
+    sums, at = [None, None], 0
+    for start, (_, first, length) in zip(starts, segments):
+        for i in range(length // size):
+            here = slice(at + i * size, at + (i + 1) * size)
+            row = lax.div(start, jnp.int32(size)) + i
+            terms = matmul(flipped_ref[row], grad_agg[here], (1, 0))
+            for k in range(count):
+                contrib[place_ref[row * count + k, 0]] += terms[k * size : (k + 1) * size]
+        for half in range(first * 2 // part, (first + length) * 2 // part):
+            skip = at + half * part // 2 - first
+            here = slice(skip, skip + part // 2)
+            part_sum = matmul(aggregated[here], grad_hidden[here], (0, 0))
+            sums[half] = part_sum if sums[half] is None else sums[half] + part_sum
+        at += length
+
+    if stage == 0:
+        sums_out[0] = sums_out[1] = jnp.zeros_like(sums[0])
+        sums_out[2] = sums[0]
+    elif stage == 1:
+        sums_out[0], sums_out[1], sums_out[2] = sums[0], sums[1], sums_in[2]
+    elif stage == 2:
+        sums_out[0], sums_out[1] = sums_in[0] + sums[0], sums_in[1] + sums[1]
+        sums_out[2] = sums_in[2]
+    if stage < 3:
         return
+    weight_part = ((sums_in[0] + sums_in[2]) + (sums_in[1] + sums[1])).astype(BF16)
     chips = keep_ref.shape[0]
     half = quarter_blocks // 2
     keep_ref[...] = contrib[:half].reshape(keep_ref.shape)
     send_ref[: chips * nodes] = contrib[half:].reshape(chips * nodes, -1).astype(BF16)
-    send_ref[chips * nodes :] = weight_part.astype(BF16)
-    keep_weight_ref[...] = weight_part.astype(BF16)
-
-
-def add_kernel(a_ref, b_ref, out_ref):
-    out_ref[...] = (a_ref[...] + b_ref[...].astype(F32)).astype(out_ref.dtype)
-
-
-def order_kernel(order, *refs):
+    send_ref[chips * nodes :] = weight_part
+    keep_weight_ref[...] = weight_part
+
+
+def add_kernel(first, a_ref, b_ref, *refs):
+    out_ref = refs[-1]
+    b = b_ref[first : first + a_ref.shape[0]]
+    out_ref[...] = (a_ref[...] + b.astype(F32)).astype(out_ref.dtype)
+
+
+def order_kernel(part, stages, *refs):
     pieces, out_ref = refs[:-1], refs[-1]
-    part = pieces[0].shape[0]
-    for j, piece in zip(order, pieces):
-        target = lax.axis_index("rep") ^ j
-        out_ref[pl.ds(pl.multiple_of(target * part, part), part), :] = piece[...]
+    for segments, piece in zip(stages, pieces):
+        at = 0
+        for j, first, length in segments:
+            start = (lax.axis_index("rep") ^ j) * part + first
+            out_ref[pl.ds(pl.multiple_of(start, 128), length), :] = piece[at : at + length]
+            at += length
 
 
 def pair_kernel(keep_ref, keep_weight_ref, got_ref, own_ref, own_weight_ref, *outs):
@@ -191,7 +218,9 @@
     part = rows * size // rep
     params = pltpu.CompilerParams(vmem_limit_bytes=(8 + dom // 2) * 1024 * 1024)
 
-    def call(kernel, out_shape, in_specs, scratch=()):
+    cost = pl.CostEstimate(flops=10**9, bytes_accessed=10**6, transcendentals=0)
+
+    def call(kernel, out_shape, in_specs, scratch=(), cost=None):
         single = not isinstance(out_shape, list)
         return pl.pallas_call(
             kernel,
@@ -200,6 +229,7 @@
             out_specs=VMEM if single else [VMEM] * len(out_shape),
             scratch_shapes=scratch,
             compiler_params=params,
+            cost_estimate=cost,
         )
 
     flipped, own = call(
@@ -225,26 +255,46 @@
         [VMEM] * 2,
     )(cols.T, mine)
 
-    partials = call(
+    beyond, half = range(2, rep), part // 2
+    halves = call(
         functools.partial(aggregate_kernel, rep),
-        [shape((part, width), BF16 if j else F32) for j in range(rep)],
+        [shape((half, width), F32)] * 2
+        + [shape((half, width), BF16)] * (2 * len(beyond))
+        + [shape((part, width), BF16)],
         [VMEM] * 4,
     )(place, vals, mine, far)
-    arrived = {j: swap(partials[j], "rep", j) if j else partials[j] for j in range(rep)}
-    order = [*range(2, rep), 1]
-    own_rows = arrived[0]
-    for j in order:
-        own_rows = call(add_kernel, shape((part, width), F32 if j > 1 else BF16), [VMEM] * 2)(
-            own_rows, arrived[j]
-        )
-    pieces = {0: own_rows}
-    for j in order:
-        pieces[j] = swap(own_rows, "rep", j)
-
+    partials = {(j, h): halves[2 * max(j - 1, 0) + h] for j in (0, *beyond) for h in (0, 1)}
+    arrived = {(j, 0): swap(partials[j, 0], "rep", j) for j in beyond}
+    beside = swap(halves[-1], "rep", 1)
+    arrived |= {(j, 1): swap(partials[j, 1], "rep", j) for j in beyond}
+
+    def add(a, b, first, dtype, *after):
+        kernel = functools.partial(add_kernel, first)
+        return call(kernel, shape(a.shape, dtype), [VMEM] * (2 + len(after)), cost=cost)(a, b, *after)
+
+    own_rows, pieces = {}, {}
+    for h in (0, 1):
+        total = partials[0, h]
+        for j in beyond:
+            after = [own_rows[0]] if h == 1 and j == 2 else []
+            total = add(total, arrived[j, h], 0, F32, *after)
+        own_rows[h] = add(total, beside, h * half, BF16)
+        for j in beyond:
+            pieces[j, h] = swap(own_rows[h], "rep", j)
+    both = call(join_kernel, shape((part, width), BF16), [VMEM] * 2)(own_rows[0], own_rows[1])
+    beside = swap(both, "rep", 1)
+
+    stages = [
+        [(j, 0, half) for j in beyond],
+        [(0, 0, part)],
+        [(1, 0, part)],
+        [(j, half, half) for j in beyond],
+    ]
+    blocks = [[pieces[j, 0] for j in beyond], [both], [beside], [pieces[j, 1] for j in beyond]]
     outputs, carried = [], []
-    for j, piece in pieces.items():
-        if j != 1:
-            outs = [shape((quarter_blocks, size, width), F32), shape((width, width), F32)]
+    for stage, (segments, values) in enumerate(zip(stages, blocks)):
+        if stage < 3:
+            outs = [shape((quarter_blocks, size, width), F32), shape((3, width, width), F32)]
             scratch = []
         else:
             outs = [
@@ -254,11 +304,12 @@
             ]
             scratch = [pltpu.VMEM((quarter_blocks, size, width), F32)]
         output, *carried = call(
-            functools.partial(layer_kernel, rep, count, own_blocks, j),
-            [shape((part, width), BF16)] + outs,
-            [VMEM] * (6 + len(carried)),
+            functools.partial(layer_kernel, rep, count, own_blocks, segments, stage),
+            [shape((sum(length for _, _, length in segments), width), BF16)] + outs,
+            [VMEM] * (5 + len(values) + len(carried)),
             scratch,
-        )(place, flipped, cotangent, weight, bias, piece, *carried)
+            cost=cost,
+        )(place, flipped, cotangent, weight, bias.reshape(1, width), *values, *carried)
         outputs.append(output)
     send, keep, keep_weight = carried
 
@@ -270,7 +321,7 @@
     )(keep, keep_weight, swap(send, "dom", 1))
     got = {chip: swap(sends[chip - 1], "dom", 2 * chip) for chip in range(chips - 1, 0, -1)}
     output = call(
-        functools.partial(order_kernel, list(pieces)), shape((rows * size, width), BF16), [VMEM] * rep
+        functools.partial(order_kernel, part, stages), shape((rows * size, width), BF16), [VMEM] * 4
     )(*outputs)
     levels = chips.bit_length() - 1
     later = call(

time: 41.7 us -> 43 us (1.031)
  starting transfers between devices: 16.3 us -> 22.7 us
  waiting for transfers between devices: 17.5 us -> 11.8 us
  local copies, waits for them, and re-layouts: 2.5 us -> 3.13 us
    ppermute x14 -> x18, starting transfers between devices: 16.3 us -> 22.7 us  [swap(): return lax.ppermute(value, axis, [(i, i ^ distance) for i in range(size)])]
    ppermute x14 -> x18, waiting for transfers between devices: 17.5 us -> 11.8 us  [swap(): return lax.ppermute(value, axis, [(i, i ^ distance) for i in range(size)])]
    unnamed x14, local copies, waits for them, and re-layouts: 2.5 us -> 3.13 us
    pallas_call x9 -> x13, Pallas kernels: 3.26 us -> 3.09 us  [the longest x4 1.95 us: body(): call(functools.partial(layer_kernel, rep, count, own_blocks, segments, st...]
  transfers between devices with their start and end apart: 14 -> 18, of which waited for: 12 -> 10; matrix products, arithmetic and copies ran while one was open for 0% -> 0% of each run, Pallas kernels for 7% -> 6%
where the time goes in v6:
time: 43 us; the launch traced here: 42.7 us
  starting transfers between devices  22.7 us (53%)
  waiting for transfers between devices  11.8 us (27%)
  Pallas kernels  4.26 us (10%)
  local copies, waits for them, and re-layouts  3.13 us (7%)
  between operations  0.84 us (2%)
    ppermute x18, starting transfers between devices, swap(): return lax.ppermute(value, axis, [(i, i ^ distance) for i in range(size)])  22.7 us
    ppermute x18, waiting for transfers between devices, swap(): return lax.ppermute(value, axis, [(i, i ^ distance) for i in range(size)])  11.8 us
    unnamed x14, local copies, waits for them, and re-layouts  3.13 us
    pallas_call x4, Pallas kernels, body(): call(functools.partial(layer_kernel, rep, count, own_blocks, segments, st...  1.95 us
  transfers between devices with their start and end apart: 18, of which 10 were waited for; matrix products, arithmetic and copies ran while one was open for 0% of the time, Pallas kernels for 6%

profile of v6, /device:TPU:0, one launch (start us, length us, event | category | flops | bytes accessed | tf_op | source)
XLA Modules:
  0.0 42.7 jit_solution(16874634980844644230)
XLA Ops:
  0.6 4.0 %collective-permute-start.2 = (bf16[256,128]{1,0:T(8,128)(2,1)}, bf16[256,128]{1,0:T(8,128)(2,1)S(1)}, u32[]{:S(2)}, u32[]{:S(2)}) collective-permute-start(bf16[256,128]{1,0:T(8,128)(2,1)} %features_ref.1), channel_id=1, source_target_pairs={{0,6},{1,7},{2,4},{3,5},{4,2},{5,3},{6,0},{7,1},{8,14},{9,15},{10,... | collective-permute-start | bytes 196616 | tf_op jit(solution)/shard_map/ppermute | solution.py:17
  5.2 1.0 %copy-done = bf16[8,2,128,128]{3,2,1,0:T(8,128)(2,1)S(1)} copy-done((bf16[8,2,128,128]{3,2,1,0:T(8,128)(2,1)S(1)}, bf16[8,2,128,128]{3,2,1,0:T(8,128)(2,1)}, u32[]{:S(2)}) %copy-start) | copy-done | bytes 524312
  6.3 0.8 %copy-done.2 = bf16[256,128]{1,0:T(8,128)(2,1)S(1)} copy-done((bf16[256,128]{1,0:T(8,128)(2,1)S(1)}, bf16[256,128]{1,0:T(8,128)(2,1)}, u32[]{:S(2)}) %copy-start.2) | copy-done | bytes 65560
  7.3 1.7 %collective-permute-done.1.refs_0_ = bf16[256,128]{1,0:T(8,128)(2,1)S(1)} collective-permute-done((bf16[256,128]{1,0:T(8,128)(2,1)}, bf16[256,128]{1,0:T(8,128)(2,1)S(1)}, u32[]{:S(2)}, u32[]{:S(2)}) %collective-permute-start.1) | collective-permute-done | bytes 65568 | tf_op jit(solution)/shard_map/ppermute | solution.py:17
  10.5 0.8 %collective-permute-done.3.far_ref = bf16[1024,128]{1,0:T(8,128)(2,1)S(1)} collective-permute-done((bf16[1024,128]{1,0:T(8,128)(2,1)S(1)}, bf16[1024,128]{1,0:T(8,128)(2,1)S(1)}, u32[]{:S(2)}, u32[]{:S(2)}) %collective-permute-start.3) | collective-permute-done | bytes 262176 | tf_op jit(solution)/shard_map/ppermute | solution.py:17
  11.6 2.7 %collective-permute-start.4 = (bf16[128,128]{1,0:T(8,128)(2,1)S(1)}, bf16[128,128]{1,0:T(8,128)(2,1)S(1)}, u32[]{:S(2)}, u32[]{:S(2)}) collective-permute-start(bf16[128,128]{1,0:T(8,128)(2,1)S(1)} %get-tuple-element.35), channel_id=1, source_target_pairs={{0,16},{8,24},{16,0},{24,8},{1,17},{9,25},{17,1},{25,9},{2,18},{10... | collective-permute-start | bytes 98312 | tf_op jit(solution)/shard_map/ppermute | solution.py:17
  14.2 1.3 %collective-permute-start.5 = (bf16[128,128]{1,0:T(8,128)(2,1)S(1)}, bf16[128,128]{1,0:T(8,128)(2,1)S(1)}, u32[]{:S(2)}, u32[]{:S(2)}) collective-permute-start(bf16[128,128]{1,0:T(8,128)(2,1)S(1)} %get-tuple-element.36), channel_id=1, source_target_pairs={{0,24},{8,16},{16,8},{24,0},{1,25},{9,17},{17,9},{25,1},{2,26},{10... | collective-permute-start | bytes 98312 | tf_op jit(solution)/shard_map/ppermute | solution.py:17
  15.8 2.8 %collective-permute-start.9 = (bf16[128,128]{1,0:T(8,128)(2,1)S(1)}, bf16[128,128]{1,0:T(8,128)(2,1)S(1)}, u32[]{:S(2)}, u32[]{:S(2)}) collective-permute-start(bf16[128,128]{1,0:T(8,128)(2,1)S(1)} %get-tuple-element.40), channel_id=1, source_target_pairs={{0,16},{8,24},{16,0},{24,8},{1,17},{9,25},{17,1},{25,9},{2,18},{10... | collective-permute-start | bytes 98312 | tf_op jit(solution)/shard_map/ppermute | solution.py:17
  18.6 1.3 %collective-permute-start.10 = (bf16[128,128]{1,0:T(8,128)(2,1)S(1)}, bf16[128,128]{1,0:T(8,128)(2,1)S(1)}, u32[]{:S(2)}, u32[]{:S(2)}) collective-permute-start(bf16[128,128]{1,0:T(8,128)(2,1)S(1)} %get-tuple-element.41), channel_id=1, source_target_pairs={{0,24},{8,16},{16,8},{24,0},{1,25},{9,17},{17,9},{25,1},{2,26},{10... | collective-permute-start | bytes 98312 | tf_op jit(solution)/shard_map/ppermute | solution.py:17
  20.6 1.1 %collective-permute-start.7 = (bf16[128,128]{1,0:T(8,128)(2,1)S(1)}, bf16[128,128]{1,0:T(8,128)(2,1)S(1)}, u32[]{:S(2)}, u32[]{:S(2)}) collective-permute-start(bf16[128,128]{1,0:T(8,128)(2,1)S(1)} %shard_map.93.refs_0_), channel_id=1, source_target_pairs={{0,16},{8,24},{16,0},{24,8},{1,17},{9,25},{17,1},{25,9},{2,18},{10... | collective-permute-start | bytes 98312 | tf_op jit(solution)/shard_map/ppermute | solution.py:17
  21.6 1.4 %collective-permute-start.8 = (bf16[128,128]{1,0:T(8,128)(2,1)S(1)}, bf16[128,128]{1,0:T(8,128)(2,1)S(1)}, u32[]{:S(2)}, u32[]{:S(2)}) collective-permute-start(bf16[128,128]{1,0:T(8,128)(2,1)S(1)} %shard_map.93.refs_0_), channel_id=1, source_target_pairs={{0,24},{8,16},{16,8},{24,0},{1,25},{9,17},{17,9},{25,1},{2,26},{10... | collective-permute-start | bytes 98312 | tf_op jit(solution)/shard_map/ppermute | solution.py:17
  23.0 1.3 %collective-permute-done.10.b_ref = bf16[128,128]{1,0:T(8,128)(2,1)S(1)} collective-permute-done((bf16[128,128]{1,0:T(8,128)(2,1)S(1)}, bf16[128,128]{1,0:T(8,128)(2,1)S(1)}, u32[]{:S(2)}, u32[]{:S(2)}) %collective-permute-start.10) | collective-permute-done | bytes 32800 | tf_op jit(solution)/shard_map/ppermute | solution.py:17
  24.4 0.7 %collective-permute-start.12 = (bf16[128,128]{1,0:T(8,128)(2,1)S(1)}, bf16[128,128]{1,0:T(8,128)(2,1)S(1)}, u32[]{:S(2)}, u32[]{:S(2)}) collective-permute-start(bf16[128,128]{1,0:T(8,128)(2,1)S(1)} %shard_map.97.refs_1_), channel_id=1, source_target_pairs={{0,16},{8,24},{16,0},{24,8},{1,17},{9,25},{17,1},{25,9},{2,18},{10... | collective-permute-start | bytes 98312 | tf_op jit(solution)/shard_map/ppermute | solution.py:17
  25.1 1.5 %collective-permute-start.13 = (bf16[128,128]{1,0:T(8,128)(2,1)S(1)}, bf16[128,128]{1,0:T(8,128)(2,1)S(1)}, u32[]{:S(2)}, u32[]{:S(2)}) collective-permute-start(bf16[128,128]{1,0:T(8,128)(2,1)S(1)} %shard_map.97.refs_1_), channel_id=1, source_target_pairs={{0,24},{8,16},{16,8},{24,0},{1,25},{9,17},{17,9},{25,1},{2,26},{10... | collective-permute-start | bytes 98312 | tf_op jit(solution)/shard_map/ppermute | solution.py:17
  26.7 1.3 %collective-permute-start.11 = (bf16[256,128]{1,0:T(8,128)(2,1)S(1)}, bf16[256,128]{1,0:T(8,128)(2,1)S(1)}, u32[]{:S(2)}, u32[]{:S(2)}) collective-permute-start(bf16[256,128]{1,0:T(8,128)(2,1)S(1)} %shard_map.98.refs_0_), channel_id=1, source_target_pairs={{0,8},{8,0},{16,24},{24,16},{1,9},{9,1},{17,25},{25,17},{2,10},{10... | collective-permute-start | bytes 196616 | tf_op jit(solution)/shard_map/ppermute | solution.py:17
  28.0 0.6 %copy-done.6 = f32[128]{0:T(128)S(1)} copy-done((f32[128]{0:T(128)S(1)}, f32[128]{0:T(128)}, u32[]{:S(2)}) %copy-start.6) | copy-done | bytes 536
  29.6 1.7 %collective-permute-done.11.refs_0_ = bf16[256,128]{1,0:T(8,128)(2,1)S(1)} collective-permute-done((bf16[256,128]{1,0:T(8,128)(2,1)S(1)}, bf16[256,128]{1,0:T(8,128)(2,1)S(1)}, u32[]{:S(2)}, u32[]{:S(2)}) %collective-permute-start.11) | collective-permute-done | bytes 65568 | tf_op jit(solution)/shard_map/ppermute | solution.py:17
  32.4 1.6 %collective-permute-done.14.got_ref = bf16[1152,128]{1,0:T(8,128)(2,1)S(1)} collective-permute-done((bf16[1152,128]{1,0:T(8,128)(2,1)S(1)}, bf16[1152,128]{1,0:T(8,128)(2,1)S(1)}, u32[]{:S(2)}, u32[]{:S(2)}) %collective-permute-start.14) | collective-permute-done | bytes 294944 | tf_op jit(solution)/shard_map/ppermute | solution.py:17
  34.0 1.6 %collective-permute-start.16 = (bf16[384,128]{1,0:T(8,128)(2,1)S(1)}, bf16[384,128]{1,0:T(8,128)(2,1)S(1)}, u32[]{:S(2)}, u32[]{:S(2)}) collective-permute-start(bf16[384,128]{1,0:T(8,128)(2,1)S(1)} %get-tuple-element.57), channel_id=1, source_target_pairs={{0,6},{1,7},{2,4},{3,5},{4,2},{5,3},{6,0},{7,1},{8,14},{9,15},{10,... | collective-permute-start | bytes 294920 | tf_op jit(solution)/shard_map/ppermute | solution.py:17
  36.1 1.5 %collective-permute-start.15 = (bf16[384,128]{1,0:T(8,128)(2,1)S(1)}, bf16[384,128]{1,0:T(8,128)(2,1)S(1)}, u32[]{:S(2)}, u32[]{:S(2)}) collective-permute-start(bf16[384,128]{1,0:T(8,128)(2,1)S(1)} %get-tuple-element.56), channel_id=1, source_target_pairs={{0,2},{1,3},{2,0},{3,1},{4,6},{5,7},{6,4},{7,5},{8,10},{9,11},{10,... | collective-permute-start | bytes 294920 | tf_op jit(solution)/shard_map/ppermute | solution.py:17
  37.6 0.7 %shard_map.102 = bf16[1024,128]{1,0:T(8,128)(2,1)} custom-call(bf16[256,128]{1,0:T(8,128)(2,1)S(1)} %get-tuple-element.38.refs_0_, bf16[256,128]{1,0:T(8,128)(2,1)S(1)} %get-tuple-element.44.refs_1_, bf16[256,128]{1,0:T(8,128)(2,1)S(1)} %get-tuple-element.47.refs_2_, bf16[256,128]{1,0:T(8,128)(2,1)S(1)} %get-tuple-element.50.refs_3_), custom_call_target="tpu_custom_call" | custom-call | tf_op jit(solution)/shard_map/pallas_call | solution.py:323
  38.3 2.2 %collective-permute-done.16.refs_0_ = bf16[384,128]{1,0:T(8,128)(2,1)S(1)} collective-permute-done((bf16[384,128]{1,0:T(8,128)(2,1)S(1)}, bf16[384,128]{1,0:T(8,128)(2,1)S(1)}, u32[]{:S(2)}, u32[]{:S(2)}) %collective-permute-start.16) | collective-permute-done | bytes 98336 | tf_op jit(solution)/shard_map/ppermute | solution.py:17
  40.5 1.4 %collective-permute-done.17.refs_1_ = bf16[384,128]{1,0:T(8,128)(2,1)S(1)} collective-permute-done((bf16[384,128]{1,0:T(8,128)(2,1)S(1)}, bf16[384,128]{1,0:T(8,128)(2,1)S(1)}, u32[]{:S(2)}, u32[]{:S(2)}) %collective-permute-start.17) | collective-permute-done | bytes 98336 | tf_op jit(solution)/shard_map/ppermute | solution.py:17
  42.0 0.7 %shard_map.105 = (f32[256,128]{1,0:T(8,128)}, f32[128,128]{1,0:T(8,128)}) custom-call(f32[256,128]{1,0:T(8,128)S(1)} %get-tuple-element.54.own_ref, bf16[128,128]{1,0:T(8,128)(2,1)S(1)} %get-tuple-element.55.own_weight_ref, bf16[384,128]{1,0:T(8,128)(2,1)S(1)} %collective-permute-done.15.got_ref, f32[384,128]{1,0:T(8,128)S(1)} %shard_map.104.refs_0_), custom_call_target="tpu_custom_call" | custom-call | tf_op jit(solution)/shard_map/pallas_call | solution.py:330
  (47 shorter events, 6.2 us)
Async XLA Ops:
  0.6 6.7 %collective-permute-start.2 = (bf16[256,128]{1,0:T(8,128)(2,1)}, bf16[256,128]{1,0:T(8,128)(2,1)S(1)}, u32[]{:S(2)}, u32[]{:S(2)}) collective-permute-start(bf16[256,128]{1,0:T(8,128)(2,1)} %features_ref.1), channel_id=1, source_target_pairs={{0,6},{1,7},{2,4},{3,5},{4,2},{5,3},{6,0},{7,1},{8,14},{9,15},{10,... | collective-permute-start | bytes 196616 | tf_op jit(solution)/shard_map/ppermute | solution.py:17
  4.6 4.5 %collective-permute-start.1 = (bf16[256,128]{1,0:T(8,128)(2,1)}, bf16[256,128]{1,0:T(8,128)(2,1)S(1)}, u32[]{:S(2)}, u32[]{:S(2)}) collective-permute-start(bf16[256,128]{1,0:T(8,128)(2,1)} %features_ref.1), channel_id=1, source_target_pairs={{0,4},{1,5},{2,6},{3,7},{4,0},{5,1},{6,2},{7,3},{8,12},{9,13},{10,... | collective-permute-start | bytes 196616 | tf_op jit(solution)/shard_map/ppermute | solution.py:17
  5.1 4.5 %collective-permute-start = (bf16[256,128]{1,0:T(8,128)(2,1)}, bf16[256,128]{1,0:T(8,128)(2,1)S(1)}, u32[]{:S(2)}, u32[]{:S(2)}) collective-permute-start(bf16[256,128]{1,0:T(8,128)(2,1)} %features_ref.1), channel_id=1, source_target_pairs={{0,2},{1,3},{2,0},{3,1},{4,6},{5,7},{6,4},{7,5},{8,10},{9,11},{10,... | collective-permute-start | bytes 196616 | tf_op jit(solution)/shard_map/ppermute | solution.py:17
  5.2 1.0 %copy-start = (bf16[8,2,128,128]{3,2,1,0:T(8,128)(2,1)S(1)}, bf16[8,2,128,128]{3,2,1,0:T(8,128)(2,1)}, u32[]{:S(2)}) copy-start(bf16[8,2,128,128]{3,2,1,0:T(8,128)(2,1)} %vals_ref.3) | copy-start | bytes 1572868
  6.3 0.8 %copy-start.2 = (bf16[256,128]{1,0:T(8,128)(2,1)S(1)}, bf16[256,128]{1,0:T(8,128)(2,1)}, u32[]{:S(2)}) copy-start(bf16[256,128]{1,0:T(8,128)(2,1)} %features_ref.1) | copy-start | bytes 196612
  7.3 3.9 %copy-start.1 = (bf16[8,2,128,128]{3,2,1,0:T(8,128)(2,1)S(1)}, bf16[8,2,128,128]{3,2,1,0:T(8,128)(2,1)}, u32[]{:S(2)}) copy-start(bf16[8,2,128,128]{3,2,1,0:T(8,128)(2,1)} %vals_ref.3) | copy-start | bytes 1572868
  9.6 0.7 %copy-start.3 = (s32[8,2]{0,1:T(2,128)S(1)}, s32[8,2]{0,1:T(2,128)}, u32[]{:S(2)}) copy-start(s32[8,2]{0,1:T(2,128)} %param.6) | copy-start | bytes 196
  9.6 1.6 %collective-permute-start.3 = (bf16[1024,128]{1,0:T(8,128)(2,1)S(1)}, bf16[1024,128]{1,0:T(8,128)(2,1)S(1)}, u32[]{:S(2)}, u32[]{:S(2)}) collective-permute-start(bf16[1024,128]{1,0:T(8,128)(2,1)S(1)} %shard_map.88._.mine_ref), channel_id=1, source_target_pairs={{0,1},{1,0},{2,3},{3,2},{4,5},{5,4},{6,7},{7,6},{8,9},{9,8},{10,11... | collective-permute-start | bytes 786440 | tf_op jit(solution)/shard_map/ppermute | solution.py:17
  11.6 8.4 %collective-permute-start.4 = (bf16[128,128]{1,0:T(8,128)(2,1)S(1)}, bf16[128,128]{1,0:T(8,128)(2,1)S(1)}, u32[]{:S(2)}, u32[]{:S(2)}) collective-permute-start(bf16[128,128]{1,0:T(8,128)(2,1)S(1)} %get-tuple-element.35), channel_id=1, source_target_pairs={{0,16},{8,24},{16,0},{24,8},{1,17},{9,25},{17,1},{25,9},{2,18},{10... | collective-permute-start | bytes 98312 | tf_op jit(solution)/shard_map/ppermute | solution.py:17
  14.2 5.8 %collective-permute-start.5 = (bf16[128,128]{1,0:T(8,128)(2,1)S(1)}, bf16[128,128]{1,0:T(8,128)(2,1)S(1)}, u32[]{:S(2)}, u32[]{:S(2)}) collective-permute-start(bf16[128,128]{1,0:T(8,128)(2,1)S(1)} %get-tuple-element.36), channel_id=1, source_target_pairs={{0,24},{8,16},{16,8},{24,0},{1,25},{9,17},{17,9},{25,1},{2,26},{10... | collective-permute-start | bytes 98312 | tf_op jit(solution)/shard_map/ppermute | solution.py:17
  15.6 5.0 %collective-permute-start.6 = (bf16[256,128]{1,0:T(8,128)(2,1)S(1)}, bf16[256,128]{1,0:T(8,128)(2,1)S(1)}, u32[]{:S(2)}, u32[]{:S(2)}) collective-permute-start(bf16[256,128]{1,0:T(8,128)(2,1)S(1)} %get-tuple-element.37), channel_id=1, source_target_pairs={{0,8},{8,0},{16,24},{24,16},{1,9},{9,1},{17,25},{25,17},{2,10},{10... | collective-permute-start | bytes 196616 | tf_op jit(solution)/shard_map/ppermute | solution.py:17
  15.8 7.2 %collective-permute-start.9 = (bf16[128,128]{1,0:T(8,128)(2,1)S(1)}, bf16[128,128]{1,0:T(8,128)(2,1)S(1)}, u32[]{:S(2)}, u32[]{:S(2)}) collective-permute-start(bf16[128,128]{1,0:T(8,128)(2,1)S(1)} %get-tuple-element.40), channel_id=1, source_target_pairs={{0,16},{8,24},{16,0},{24,8},{1,17},{9,25},{17,1},{25,9},{2,18},{10... | collective-permute-start | bytes 98312 | tf_op jit(solution)/shard_map/ppermute | solution.py:17
  18.6 5.7 %collective-permute-start.10 = (bf16[128,128]{1,0:T(8,128)(2,1)S(1)}, bf16[128,128]{1,0:T(8,128)(2,1)S(1)}, u32[]{:S(2)}, u32[]{:S(2)}) collective-permute-start(bf16[128,128]{1,0:T(8,128)(2,1)S(1)} %get-tuple-element.41), channel_id=1, source_target_pairs={{0,24},{8,16},{16,8},{24,0},{1,25},{9,17},{17,9},{25,1},{2,26},{10... | collective-permute-start | bytes 98312 | tf_op jit(solution)/shard_map/ppermute | solution.py:17
  20.6 7.4 %collective-permute-start.7 = (bf16[128,128]{1,0:T(8,128)(2,1)S(1)}, bf16[128,128]{1,0:T(8,128)(2,1)S(1)}, u32[]{:S(2)}, u32[]{:S(2)}) collective-permute-start(bf16[128,128]{1,0:T(8,128)(2,1)S(1)} %shard_map.93.refs_0_), channel_id=1, source_target_pairs={{0,16},{8,24},{16,0},{24,8},{1,17},{9,25},{17,1},{25,9},{2,18},{10... | collective-permute-start | bytes 98312 | tf_op jit(solution)/shard_map/ppermute | solution.py:17
  21.6 6.3 %collective-permute-start.8 = (bf16[128,128]{1,0:T(8,128)(2,1)S(1)}, bf16[128,128]{1,0:T(8,128)(2,1)S(1)}, u32[]{:S(2)}, u32[]{:S(2)}) collective-permute-start(bf16[128,128]{1,0:T(8,128)(2,1)S(1)} %shard_map.93.refs_0_), channel_id=1, source_target_pairs={{0,24},{8,16},{16,8},{24,0},{1,25},{9,17},{17,9},{25,1},{2,26},{10... | collective-permute-start | bytes 98312 | tf_op jit(solution)/shard_map/ppermute | solution.py:17
  24.3 3.6 %copy-start.4 = (bf16[1024,128]{1,0:T(8,128)(2,1)S(1)}, bf16[1024,128]{1,0:T(8,128)(2,1)}, u32[]{:S(2)}) copy-start(bf16[1024,128]{1,0:T(8,128)(2,1)} %cotangent_ref.7) | copy-start | bytes 786436
  24.4 3.6 %copy-start.5 = (bf16[128,128]{1,0:T(8,128)(2,1)S(1)}, bf16[128,128]{1,0:T(8,128)(2,1)}, u32[]{:S(2)}) copy-start(bf16[128,128]{1,0:T(8,128)(2,1)} %weight_ref.7) | copy-start | bytes 98308
  24.4 7.4 %collective-permute-start.12 = (bf16[128,128]{1,0:T(8,128)(2,1)S(1)}, bf16[128,128]{1,0:T(8,128)(2,1)S(1)}, u32[]{:S(2)}, u32[]{:S(2)}) collective-permute-start(bf16[128,128]{1,0:T(8,128)(2,1)S(1)} %shard_map.97.refs_1_), channel_id=1, source_target_pairs={{0,16},{8,24},{16,0},{24,8},{1,17},{9,25},{17,1},{25,9},{2,18},{10... | collective-permute-start | bytes 98312 | tf_op jit(solution)/shard_map/ppermute | solution.py:17
  25.1 6.7 %collective-permute-start.13 = (bf16[128,128]{1,0:T(8,128)(2,1)S(1)}, bf16[128,128]{1,0:T(8,128)(2,1)S(1)}, u32[]{:S(2)}, u32[]{:S(2)}) collective-permute-start(bf16[128,128]{1,0:T(8,128)(2,1)S(1)} %shard_map.97.refs_1_), channel_id=1, source_target_pairs={{0,24},{8,16},{16,8},{24,0},{1,25},{9,17},{17,9},{25,1},{2,26},{10... | collective-permute-start | bytes 98312 | tf_op jit(solution)/shard_map/ppermute | solution.py:17
  26.7 4.6 %collective-permute-start.11 = (bf16[256,128]{1,0:T(8,128)(2,1)S(1)}, bf16[256,128]{1,0:T(8,128)(2,1)S(1)}, u32[]{:S(2)}, u32[]{:S(2)}) collective-permute-start(bf16[256,128]{1,0:T(8,128)(2,1)S(1)} %shard_map.98.refs_0_), channel_id=1, source_target_pairs={{0,8},{8,0},{16,24},{24,16},{1,9},{9,1},{17,25},{25,17},{2,10},{10... | collective-permute-start | bytes 196616 | tf_op jit(solution)/shard_map/ppermute | solution.py:17
  32.3 1.6 %collective-permute-start.14 = (bf16[1152,128]{1,0:T(8,128)(2,1)S(1)}, bf16[1152,128]{1,0:T(8,128)(2,1)S(1)}, u32[]{:S(2)}, u32[]{:S(2)}) collective-permute-start(bf16[1152,128]{1,0:T(8,128)(2,1)S(1)} %get-tuple-element.53), channel_id=1, source_target_pairs={{0,1},{1,0},{2,3},{3,2},{4,5},{5,4},{6,7},{7,6},{8,9},{9,8},{10,11... | collective-permute-start | bytes 884744 | tf_op jit(solution)/shard_map/ppermute | solution.py:17
  34.0 6.5 %collective-permute-start.16 = (bf16[384,128]{1,0:T(8,128)(2,1)S(1)}, bf16[384,128]{1,0:T(8,128)(2,1)S(1)}, u32[]{:S(2)}, u32[]{:S(2)}) collective-permute-start(bf16[384,128]{1,0:T(8,128)(2,1)S(1)} %get-tuple-element.57), channel_id=1, source_target_pairs={{0,6},{1,7},{2,4},{3,5},{4,2},{5,3},{6,0},{7,1},{8,14},{9,15},{10,... | collective-permute-start | bytes 294920 | tf_op jit(solution)/shard_map/ppermute | solution.py:17
  35.6 6.4 %collective-permute-start.17 = (bf16[384,128]{1,0:T(8,128)(2,1)S(1)}, bf16[384,128]{1,0:T(8,128)(2,1)S(1)}, u32[]{:S(2)}, u32[]{:S(2)}) collective-permute-start(bf16[384,128]{1,0:T(8,128)(2,1)S(1)} %get-tuple-element.58), channel_id=1, source_target_pairs={{0,4},{1,5},{2,6},{3,7},{4,0},{5,1},{6,2},{7,3},{8,12},{9,13},{10,... | collective-permute-start | bytes 294920 | tf_op jit(solution)/shard_map/ppermute | solution.py:17
  36.1 5.9 %collective-permute-start.15 = (bf16[384,128]{1,0:T(8,128)(2,1)S(1)}, bf16[384,128]{1,0:T(8,128)(2,1)S(1)}, u32[]{:S(2)}, u32[]{:S(2)}) collective-permute-start(bf16[384,128]{1,0:T(8,128)(2,1)S(1)} %get-tuple-element.56), channel_id=1, source_target_pairs={{0,2},{1,3},{2,0},{3,1},{4,6},{5,7},{6,4},{7,5},{8,10},{9,11},{10,... | collective-permute-start | bytes 294920 | tf_op jit(solution)/shard_map/ppermute | solution.py:17
  (1 other events, 0.7 us)

commit v7 on v5

--- a/solution.py
+++ b/solution.py
@@ -87,11 +87,11 @@
     first, last = j == 0, j == 1
     piece_ref, refs = refs[0], refs[1:]
     if not first:
-        (contrib_in, weight_in), refs = refs[:2], refs[2:]
+        (contrib_in, sums_in), refs = refs[:2], refs[2:]
     if last:
-        output_ref, send_ref, keep_ref, keep_weight_ref, contrib = refs
+        output_ref, first_ref, rest_ref, keep_ref, contrib = refs
     else:
-        output_ref, contrib, weight_out = refs
+        output_ref, contrib, sums_out = refs
     rows, _, size = flipped_ref.shape
     share = rows // rep
     quarter_blocks = contrib.shape[0]
@@ -108,24 +108,27 @@
     grad_hidden = (
         cotangent_ref[here, :].astype(F32) * gate_prob * (1.0 + hidden * (1.0 - gate_prob))
     ).astype(BF16)
-    weight_part = matmul(aggregated, grad_hidden, (0, 0))
-    if not first:
-        weight_part = weight_in[...] + weight_part
+    part_sum = matmul(aggregated, grad_hidden, (0, 0))
     grad_agg = matmul(grad_hidden, weight_ref[...], (1, 1)).astype(BF16)
     for i in range(share):
         row = target * share + i
         terms = matmul(flipped_ref[row], grad_agg[i * size : (i + 1) * size], (1, 0))
         for k in range(count):
             contrib[place_ref[row * count + k, 0]] += terms[k * size : (k + 1) * size]
+    if first:
+        sums_out[0] = part_sum
+        sums_out[1] = jnp.zeros_like(part_sum)
+    elif not last:
+        sums_out[0] = sums_in[0]
+        sums_out[1] = sums_in[1] + part_sum
     if not last:
-        weight_out[...] = weight_part
         return
-    chips = keep_ref.shape[0]
     half = quarter_blocks // 2
     keep_ref[...] = contrib[:half].reshape(keep_ref.shape)
-    send_ref[: chips * nodes] = contrib[half:].reshape(chips * nodes, -1).astype(BF16)
-    send_ref[chips * nodes :] = weight_part.astype(BF16)
-    keep_weight_ref[...] = weight_part.astype(BF16)
+    away = contrib[half:].reshape(half * size, -1).astype(BF16)
+    rest_ref[...] = away[:-nodes]
+    first_ref[:nodes] = away[-nodes:]
+    first_ref[nodes:] = ((sums_in[0] + part_sum) + sums_in[1]).astype(BF16)
 
 
 def add_kernel(a_ref, b_ref, out_ref):
@@ -140,16 +143,19 @@
         out_ref[pl.ds(pl.multiple_of(target * part, part), part), :] = piece[...]
 
 
-def pair_kernel(keep_ref, keep_weight_ref, got_ref, own_ref, own_weight_ref, *outs):
+def first_pair_kernel(keep_ref, sent_ref, got_ref, out_ref):
     chips, nodes, _ = keep_ref.shape
-    both = keep_weight_ref[...].astype(F32) + got_ref[chips * nodes :].astype(F32)
-    both = both.astype(BF16)
-    own_weight_ref[...] = both
+    out_ref[:nodes] = (keep_ref[chips - 1] + got_ref[:nodes].astype(F32)).astype(BF16)
+    out_ref[nodes:] = (sent_ref[nodes:].astype(F32) + got_ref[nodes:].astype(F32)).astype(BF16)
+
+
+def rest_pair_kernel(keep_ref, first_ref, got_ref, own_ref, *outs):
+    chips, nodes, _ = keep_ref.shape
     own_ref[...] = keep_ref[0] + got_ref[:nodes].astype(F32)
-    for chip in range(1, chips):
+    for chip in range(1, chips - 1):
         total = keep_ref[chip] + got_ref[chip * nodes : (chip + 1) * nodes].astype(F32)
         outs[chip - 1][:nodes] = total.astype(BF16)
-        outs[chip - 1][nodes:] = both
+        outs[chip - 1][nodes:] = first_ref[nodes:]
 
 
 def total_of(values):
@@ -158,18 +164,22 @@
     return values[0]
 
 
+def lift_kernel(got_ref, out_ref):
+    out_ref[...] = got_ref[...].astype(F32)
+
+
 def half_kernel(levels, *refs):
     for level in range(1, levels):
         first = 1 << level
-        got = refs[: -levels + 1][::-1][first - 2 : 2 * first - 2]
+        got = refs[first - 2 : 2 * first - 2]
         refs[level - levels][...] = total_of([g[...].astype(F32) for g in got])
 
 
-def final_kernel(own_ref, own_weight_ref, got_ref, *refs):
+def final_kernel(own_ref, sent_ref, got_ref, *refs):
     later, (feature_ref, weight_ref) = refs[:-2], refs[-2:]
     nodes = own_ref.shape[0]
     feature = own_ref[...] + got_ref[:nodes].astype(F32)
-    weight = own_weight_ref[...].astype(F32) + got_ref[nodes:].astype(F32)
+    weight = sent_ref[nodes:].astype(F32) + got_ref[nodes:].astype(F32)
     for value in later:
         feature += value[:nodes]
         weight += value[nodes:]
@@ -191,7 +201,7 @@
     part = rows * size // rep
     params = pltpu.CompilerParams(vmem_limit_bytes=(8 + dom // 2) * 1024 * 1024)
 
-    def call(kernel, out_shape, in_specs, scratch=()):
+    def call(kernel, out_shape, in_specs, scratch=(), cost=0):
         single = not isinstance(out_shape, list)
         return pl.pallas_call(
             kernel,
@@ -200,6 +210,7 @@
             out_specs=VMEM if single else [VMEM] * len(out_shape),
             scratch_shapes=scratch,
             compiler_params=params,
+            cost_estimate=pl.CostEstimate(flops=cost, bytes_accessed=0, transcendentals=0),
         )
 
     flipped, own = call(
@@ -231,7 +242,7 @@
         [VMEM] * 4,
     )(place, vals, mine, far)
     arrived = {j: swap(partials[j], "rep", j) if j else partials[j] for j in range(rep)}
-    order = [*range(2, rep), 1]
+    order = range(rep - 1, 0, -1)
     own_rows = arrived[0]
     for j in order:
         own_rows = call(add_kernel, shape((part, width), F32 if j > 1 else BF16), [VMEM] * 2)(
@@ -244,13 +255,13 @@
     outputs, carried = [], []
     for j, piece in pieces.items():
         if j != 1:
-            outs = [shape((quarter_blocks, size, width), F32), shape((width, width), F32)]
+            outs = [shape((quarter_blocks, size, width), F32), shape((2, width, width), F32)]
             scratch = []
         else:
             outs = [
-                shape((chips * nodes + width, width), BF16),
+                shape((nodes + width, width), BF16),
+                shape(((chips - 1) * nodes, width), BF16),
                 shape((chips, nodes, width), F32),
-                shape((width, width), BF16),
             ]
             scratch = [pltpu.VMEM((quarter_blocks, size, width), F32)]
         output, *carried = call(
@@ -260,27 +271,30 @@
             scratch,
         )(place, flipped, cotangent, weight, bias, piece, *carried)
         outputs.append(output)
-    send, keep, keep_weight = carried
-
-    own, own_weight, *sends = call(
-        pair_kernel,
-        [shape((nodes, width), F32), shape((width, width), BF16)]
-        + [shape((nodes + width, width), BF16)] * (chips - 1),
-        [VMEM] * 3,
-    )(keep, keep_weight, swap(send, "dom", 1))
+    first, rest, keep = carried
+
+    message = shape((nodes + width, width), BF16)
+    got_first, got_rest = swap(first, "dom", 1), swap(rest, "dom", 1)
+    sends = [call(first_pair_kernel, message, [VMEM] * 3, cost=5000000000)(keep, first, got_first)]
+    own, *others = call(
+        rest_pair_kernel, [shape((nodes, width), F32)] + [message] * (chips - 2), [VMEM] * 3, cost=1000000000
+    )(keep, sends[0], got_rest)
+    sends = others + sends
     got = {chip: swap(sends[chip - 1], "dom", 2 * chip) for chip in range(chips - 1, 0, -1)}
     output = call(
         functools.partial(order_kernel, list(pieces)), shape((rows * size, width), BF16), [VMEM] * rep
     )(*outputs)
     levels = chips.bit_length() - 1
+    total = shape(message.shape, F32)
+    got[chips - 1] = call(lift_kernel, total, [VMEM], cost=1000000000)(got[chips - 1])
     later = call(
-        functools.partial(half_kernel, levels), [shape((nodes + width, width), F32)] * (levels - 1), [VMEM] * (chips - 2)
-    )(*[got[chip] for chip in range(chips - 1, 1, -1)])
+        functools.partial(half_kernel, levels), [total] * (levels - 1), [VMEM] * (chips - 2), cost=0
+    )(*[got[chip] for chip in range(2, chips)])
     feature_grad, weight_grad = call(
         final_kernel,
         [shape((nodes, width), F32), shape((width, width), F32)],
         [VMEM] * (levels + 2),
-    )(own, own_weight, got[1], *later)
+    )(own, sends[-1], got[1], *later)
     return output, feature_grad, weight_grad
 
 

time: 41.7 us -> 41.7 us (level)
  waiting for transfers between devices: 17.5 us -> 15.9 us
  starting transfers between devices: 16.3 us -> 17.8 us
    ppermute x14 -> x15, waiting for transfers between devices: 17.5 us -> 15.9 us  [swap(): return lax.ppermute(value, axis, [(i, i ^ distance) for i in range(size)])]
    ppermute x14 -> x15, starting transfers between devices: 16.3 us -> 17.8 us  [swap(): return lax.ppermute(value, axis, [(i, i ^ distance) for i in range(size)])]
  transfers between devices with their start and end apart: 14 -> 15, of which waited for: 12 -> 11; matrix products, arithmetic and copies ran while one was open for 0% -> 0% of each run, Pallas kernels for 7% -> 7%
where the time goes in v7:
time: 41.7 us; the launch traced here: 41.5 us
  starting transfers between devices  17.8 us (43%)
  waiting for transfers between devices  15.9 us (38%)
  Pallas kernels  4.46 us (11%)
  local copies, waits for them, and re-layouts  2.5 us (6%)
  between operations  0.81 us (2%)
    ppermute x15, starting transfers between devices, swap(): return lax.ppermute(value, axis, [(i, i ^ distance) for i in range(size)])  17.8 us
    ppermute x15, waiting for transfers between devices, swap(): return lax.ppermute(value, axis, [(i, i ^ distance) for i in range(size)])  15.9 us
    unnamed x14, local copies, waits for them, and re-layouts  2.5 us
    pallas_call x4, Pallas kernels, body(): call(functools.partial(layer_kernel, rep, count, own_blocks, j), [shape((...  2.15 us
  transfers between devices with their start and end apart: 15, of which 11 were waited for; matrix products, arithmetic and copies ran while one was open for 0% of the time, Pallas kernels for 7%

profile of v7, /device:TPU:0, one launch (start us, length us, event | category | flops | bytes accessed | tf_op | source)
XLA Modules:
  0.0 41.5 jit_solution(12840057351529146016)
XLA Ops:
  0.6 4.0 %collective-permute-start.2 = (bf16[256,128]{1,0:T(8,128)(2,1)}, bf16[256,128]{1,0:T(8,128)(2,1)S(1)}, u32[]{:S(2)}, u32[]{:S(2)}) collective-permute-start(bf16[256,128]{1,0:T(8,128)(2,1)} %features_ref.1), channel_id=1, source_target_pairs={{0,6},{1,7},{2,4},{3,5},{4,2},{5,3},{6,0},{7,1},{8,14},{9,15},{10,... | collective-permute-start | bytes 196616 | tf_op jit(solution)/shard_map/ppermute | solution.py:17
  5.2 1.0 %copy-done.1 = bf16[8,2,128,128]{3,2,1,0:T(8,128)(2,1)S(1)} copy-done((bf16[8,2,128,128]{3,2,1,0:T(8,128)(2,1)S(1)}, bf16[8,2,128,128]{3,2,1,0:T(8,128)(2,1)}, u32[]{:S(2)}) %copy-start.1) | copy-done | bytes 524312
  6.3 0.8 %copy-done.4 = bf16[256,128]{1,0:T(8,128)(2,1)S(1)} copy-done((bf16[256,128]{1,0:T(8,128)(2,1)S(1)}, bf16[256,128]{1,0:T(8,128)(2,1)}, u32[]{:S(2)}) %copy-start.4) | copy-done | bytes 65560
  7.3 1.7 %collective-permute-done.1.refs_0_ = bf16[256,128]{1,0:T(8,128)(2,1)S(1)} collective-permute-done((bf16[256,128]{1,0:T(8,128)(2,1)}, bf16[256,128]{1,0:T(8,128)(2,1)S(1)}, u32[]{:S(2)}, u32[]{:S(2)}) %collective-permute-start.1) | collective-permute-done | bytes 65568 | tf_op jit(solution)/shard_map/ppermute | solution.py:17
  9.7 0.6 %copy-done.6 = s32[8,2]{0,1:T(2,128)S(1)} copy-done((s32[8,2]{0,1:T(2,128)S(1)}, s32[8,2]{0,1:T(2,128)}, u32[]{:S(2)}) %copy-start.6) | copy-done | bytes 88
  10.5 0.8 %collective-permute-done.3.far_ref = bf16[1024,128]{1,0:T(8,128)(2,1)S(1)} collective-permute-done((bf16[1024,128]{1,0:T(8,128)(2,1)S(1)}, bf16[1024,128]{1,0:T(8,128)(2,1)S(1)}, u32[]{:S(2)}, u32[]{:S(2)}) %collective-permute-start.3) | collective-permute-done | bytes 262176 | tf_op jit(solution)/shard_map/ppermute | solution.py:17
  11.6 3.7 %collective-permute-start.4 = (bf16[256,128]{1,0:T(8,128)(2,1)S(1)}, bf16[256,128]{1,0:T(8,128)(2,1)S(1)}, u32[]{:S(2)}, u32[]{:S(2)}) collective-permute-start(bf16[256,128]{1,0:T(8,128)(2,1)S(1)} %get-tuple-element.30), channel_id=1, source_target_pairs={{0,24},{8,16},{16,8},{24,0},{1,25},{9,17},{17,9},{25,1},{2,26},{10... | collective-permute-start | bytes 196616 | tf_op jit(solution)/shard_map/ppermute | solution.py:17
  15.2 0.8 %collective-permute-start.6 = (bf16[256,128]{1,0:T(8,128)(2,1)S(1)}, bf16[256,128]{1,0:T(8,128)(2,1)S(1)}, u32[]{:S(2)}, u32[]{:S(2)}) collective-permute-start(bf16[256,128]{1,0:T(8,128)(2,1)S(1)} %get-tuple-element.32), channel_id=1, source_target_pairs={{0,8},{8,0},{16,24},{24,16},{1,9},{9,1},{17,25},{25,17},{2,10},{10... | collective-permute-start | bytes 196616 | tf_op jit(solution)/shard_map/ppermute | solution.py:17
  16.0 1.9 %collective-permute-done.4.b_ref = bf16[256,128]{1,0:T(8,128)(2,1)S(1)} collective-permute-done((bf16[256,128]{1,0:T(8,128)(2,1)S(1)}, bf16[256,128]{1,0:T(8,128)(2,1)S(1)}, u32[]{:S(2)}, u32[]{:S(2)}) %collective-permute-start.4) | collective-permute-done | bytes 65568 | tf_op jit(solution)/shard_map/ppermute | solution.py:17
  18.0 3.2 %collective-permute-done.5.b_ref = bf16[256,128]{1,0:T(8,128)(2,1)S(1)} collective-permute-done((bf16[256,128]{1,0:T(8,128)(2,1)S(1)}, bf16[256,128]{1,0:T(8,128)(2,1)S(1)}, u32[]{:S(2)}, u32[]{:S(2)}) %collective-permute-start.5) | collective-permute-done | bytes 65568 | tf_op jit(solution)/shard_map/ppermute | solution.py:17
  21.2 2.5 %collective-permute-start.7 = (bf16[256,128]{1,0:T(8,128)(2,1)S(1)}, bf16[256,128]{1,0:T(8,128)(2,1)S(1)}, u32[]{:S(2)}, u32[]{:S(2)}) collective-permute-start(bf16[256,128]{1,0:T(8,128)(2,1)S(1)} %shard_map.93.refs_0_), channel_id=1, source_target_pairs={{0,24},{8,16},{16,8},{24,0},{1,25},{9,17},{17,9},{25,1},{2,26},{10... | collective-permute-start | bytes 196616 | tf_op jit(solution)/shard_map/ppermute | solution.py:17
  23.8 1.9 %collective-permute-start.9 = (bf16[256,128]{1,0:T(8,128)(2,1)S(1)}, bf16[256,128]{1,0:T(8,128)(2,1)S(1)}, u32[]{:S(2)}, u32[]{:S(2)}) collective-permute-start(bf16[256,128]{1,0:T(8,128)(2,1)S(1)} %shard_map.93.refs_0_), channel_id=1, source_target_pairs={{0,8},{8,0},{16,24},{24,16},{1,9},{9,1},{17,25},{25,17},{2,10},{10... | collective-permute-start | bytes 196616 | tf_op jit(solution)/shard_map/ppermute | solution.py:17
  26.2 1.4 %collective-permute-done.7.refs_0_ = bf16[256,128]{1,0:T(8,128)(2,1)S(1)} collective-permute-done((bf16[256,128]{1,0:T(8,128)(2,1)S(1)}, bf16[256,128]{1,0:T(8,128)(2,1)S(1)}, u32[]{:S(2)}, u32[]{:S(2)}) %collective-permute-start.7) | collective-permute-done | bytes 65568 | tf_op jit(solution)/shard_map/ppermute | solution.py:17
  27.6 0.5 %shard_map.95 = (bf16[256,128]{1,0:T(8,128)(2,1)S(1)}, f32[16,128,128]{2,1,0:T(8,128)S(1)}, f32[2,128,128]{2,1,0:T(8,128)S(1)}) custom-call(s32[16,128]{1,0:T(8,128)S(1)} %shard_map.89.place_ref, bf16[8,256,128]{2,1,0:T(8,128)(2,1)S(1)} %get-tuple-element.28.flipped_ref, bf16[1024,128]{1,0:T(8,128)(2,1)S(1)} %copy-done, bf16[128,128]{1,0:T(8,128)(2,1)S(1)} %copy-done.3, ...), custom_call_target="tpu_custom_call" | custom-call | tf_op jit(solution)/shard_map/pallas_call | solution.py:267
  28.1 2.2 %collective-permute-done.8.refs_0_ = bf16[256,128]{1,0:T(8,128)(2,1)S(1)} collective-permute-done((bf16[256,128]{1,0:T(8,128)(2,1)S(1)}, bf16[256,128]{1,0:T(8,128)(2,1)S(1)}, u32[]{:S(2)}, u32[]{:S(2)}) %collective-permute-start.8) | collective-permute-done | bytes 65568 | tf_op jit(solution)/shard_map/ppermute | solution.py:17
  30.8 0.6 %shard_map.97 = (bf16[256,128]{1,0:T(8,128)(2,1)S(1)}, bf16[384,128]{1,0:T(8,128)(2,1)S(1)}, bf16[768,128]{1,0:T(8,128)(2,1)S(1)}, f32[4,256,128]{2,1,0:T(8,128)S(1)}) custom-call(s32[16,128]{1,0:T(8,128)S(1)} %shard_map.89.place_ref, bf16[8,256,128]{2,1,0:T(8,128)(2,1)S(1)} %get-tuple-element.28.flipped_ref, bf16[1024,128]{1,0:T(8,128)(2,1)S(1)} %copy-done, ...), custom_call_target="tpu_custom_call" | custom-call | tf_op jit(solution)/shard_map/pallas_call | solution.py:267
  31.9 0.8 %collective-permute-done.10.got_ref = bf16[384,128]{1,0:T(8,128)(2,1)S(1)} collective-permute-done((bf16[384,128]{1,0:T(8,128)(2,1)S(1)}, bf16[384,128]{1,0:T(8,128)(2,1)S(1)}, u32[]{:S(2)}, u32[]{:S(2)}) %collective-permute-start.10) | collective-permute-done | bytes 98336 | tf_op jit(solution)/shard_map/ppermute | solution.py:17
  32.8 1.6 %collective-permute-start.14 = (bf16[384,128]{1,0:T(8,128)(2,1)S(1)}, bf16[384,128]{1,0:T(8,128)(2,1)S(1)}, u32[]{:S(2)}, u32[]{:S(2)}) collective-permute-start(bf16[384,128]{1,0:T(8,128)(2,1)S(1)} %shard_map.99.first_ref.sent_ref), channel_id=1, source_target_pairs={{0,6},{1,7},{2,4},{3,5},{4,2},{5,3},{6,0},{7,1},{8,14},{9,15},{10,... | collective-permute-start | bytes 294920 | tf_op jit(solution)/shard_map/ppermute | solution.py:17
  34.4 0.6 %collective-permute-start.13 = (bf16[384,128]{1,0:T(8,128)(2,1)S(1)}, bf16[384,128]{1,0:T(8,128)(2,1)S(1)}, u32[]{:S(2)}, u32[]{:S(2)}) collective-permute-start(bf16[384,128]{1,0:T(8,128)(2,1)S(1)} %get-tuple-element.48), channel_id=1, source_target_pairs={{0,4},{1,5},{2,6},{3,7},{4,0},{5,1},{6,2},{7,3},{8,12},{9,13},{10,... | collective-permute-start | bytes 294920 | tf_op jit(solution)/shard_map/ppermute | solution.py:17
  34.9 1.5 %collective-permute-start.12 = (bf16[384,128]{1,0:T(8,128)(2,1)S(1)}, bf16[384,128]{1,0:T(8,128)(2,1)S(1)}, u32[]{:S(2)}, u32[]{:S(2)}) collective-permute-start(bf16[384,128]{1,0:T(8,128)(2,1)S(1)} %get-tuple-element.47), channel_id=1, source_target_pairs={{0,2},{1,3},{2,0},{3,1},{4,6},{5,7},{6,4},{7,5},{8,10},{9,11},{10,... | collective-permute-start | bytes 294920 | tf_op jit(solution)/shard_map/ppermute | solution.py:17
  36.4 0.7 %shard_map.98 = bf16[1024,128]{1,0:T(8,128)(2,1)} custom-call(bf16[256,128]{1,0:T(8,128)(2,1)S(1)} %get-tuple-element.33.refs_0_, bf16[256,128]{1,0:T(8,128)(2,1)S(1)} %get-tuple-element.36.refs_1_, bf16[256,128]{1,0:T(8,128)(2,1)S(1)} %get-tuple-element.39.refs_2_, bf16[256,128]{1,0:T(8,128)(2,1)S(1)} %get-tuple-element.42.refs_3_), custom_call_target="tpu_custom_call" | custom-call | tf_op jit(solution)/shard_map/pallas_call | solution.py:284
  37.2 1.9 %collective-permute-done.14.got_ref = bf16[384,128]{1,0:T(8,128)(2,1)S(1)} collective-permute-done((bf16[384,128]{1,0:T(8,128)(2,1)S(1)}, bf16[384,128]{1,0:T(8,128)(2,1)S(1)}, u32[]{:S(2)}, u32[]{:S(2)}) %collective-permute-start.14) | collective-permute-done | bytes 98336 | tf_op jit(solution)/shard_map/ppermute | solution.py:17
  39.1 1.6 %collective-permute-done.13.refs_0_ = bf16[384,128]{1,0:T(8,128)(2,1)S(1)} collective-permute-done((bf16[384,128]{1,0:T(8,128)(2,1)S(1)}, bf16[384,128]{1,0:T(8,128)(2,1)S(1)}, u32[]{:S(2)}, u32[]{:S(2)}) %collective-permute-start.13) | collective-permute-done | bytes 98336 | tf_op jit(solution)/shard_map/ppermute | solution.py:17
  40.8 0.7 %shard_map.103 = (f32[256,128]{1,0:T(8,128)}, f32[128,128]{1,0:T(8,128)}) custom-call(f32[256,128]{1,0:T(8,128)S(1)} %get-tuple-element.46.own_ref, bf16[384,128]{1,0:T(8,128)(2,1)S(1)} %shard_map.99.first_ref.sent_ref, bf16[384,128]{1,0:T(8,128)(2,1)S(1)} %collective-permute-done.12.got_ref, f32[384,128]{1,0:T(8,128)S(1)} %shard_map.102.refs_0_), custom_call_target="tpu_custom_call" | custom-call | tf_op jit(solution)/shard_map/pallas_call | solution.py:293
  (39 shorter events, 3.9 us)
Async XLA Ops:
  0.6 6.7 %collective-permute-start.2 = (bf16[256,128]{1,0:T(8,128)(2,1)}, bf16[256,128]{1,0:T(8,128)(2,1)S(1)}, u32[]{:S(2)}, u32[]{:S(2)}) collective-permute-start(bf16[256,128]{1,0:T(8,128)(2,1)} %features_ref.1), channel_id=1, source_target_pairs={{0,6},{1,7},{2,4},{3,5},{4,2},{5,3},{6,0},{7,1},{8,14},{9,15},{10,... | collective-permute-start | bytes 196616 | tf_op jit(solution)/shard_map/ppermute | solution.py:17
  4.6 4.5 %collective-permute-start.1 = (bf16[256,128]{1,0:T(8,128)(2,1)}, bf16[256,128]{1,0:T(8,128)(2,1)S(1)}, u32[]{:S(2)}, u32[]{:S(2)}) collective-permute-start(bf16[256,128]{1,0:T(8,128)(2,1)} %features_ref.1), channel_id=1, source_target_pairs={{0,4},{1,5},{2,6},{3,7},{4,0},{5,1},{6,2},{7,3},{8,12},{9,13},{10,... | collective-permute-start | bytes 196616 | tf_op jit(solution)/shard_map/ppermute | solution.py:17
  5.1 4.5 %collective-permute-start = (bf16[256,128]{1,0:T(8,128)(2,1)}, bf16[256,128]{1,0:T(8,128)(2,1)S(1)}, u32[]{:S(2)}, u32[]{:S(2)}) collective-permute-start(bf16[256,128]{1,0:T(8,128)(2,1)} %features_ref.1), channel_id=1, source_target_pairs={{0,2},{1,3},{2,0},{3,1},{4,6},{5,7},{6,4},{7,5},{8,10},{9,11},{10,... | collective-permute-start | bytes 196616 | tf_op jit(solution)/shard_map/ppermute | solution.py:17
  5.2 1.0 %copy-start.1 = (bf16[8,2,128,128]{3,2,1,0:T(8,128)(2,1)S(1)}, bf16[8,2,128,128]{3,2,1,0:T(8,128)(2,1)}, u32[]{:S(2)}) copy-start(bf16[8,2,128,128]{3,2,1,0:T(8,128)(2,1)} %vals_ref.3) | copy-start | bytes 1572868
  6.3 0.8 %copy-start.4 = (bf16[256,128]{1,0:T(8,128)(2,1)S(1)}, bf16[256,128]{1,0:T(8,128)(2,1)}, u32[]{:S(2)}) copy-start(bf16[256,128]{1,0:T(8,128)(2,1)} %features_ref.1) | copy-start | bytes 196612
  7.3 3.9 %copy-start.2 = (bf16[8,2,128,128]{3,2,1,0:T(8,128)(2,1)S(1)}, bf16[8,2,128,128]{3,2,1,0:T(8,128)(2,1)}, u32[]{:S(2)}) copy-start(bf16[8,2,128,128]{3,2,1,0:T(8,128)(2,1)} %vals_ref.3) | copy-start | bytes 1572868
  9.6 0.7 %copy-start.6 = (s32[8,2]{0,1:T(2,128)S(1)}, s32[8,2]{0,1:T(2,128)}, u32[]{:S(2)}) copy-start(s32[8,2]{0,1:T(2,128)} %param.6) | copy-start | bytes 196
  9.6 1.6 %collective-permute-start.3 = (bf16[1024,128]{1,0:T(8,128)(2,1)S(1)}, bf16[1024,128]{1,0:T(8,128)(2,1)S(1)}, u32[]{:S(2)}, u32[]{:S(2)}) collective-permute-start(bf16[1024,128]{1,0:T(8,128)(2,1)S(1)} %shard_map.88._.mine_ref), channel_id=1, source_target_pairs={{0,1},{1,0},{2,3},{3,2},{4,5},{5,4},{6,7},{7,6},{8,9},{9,8},{10,11... | collective-permute-start | bytes 786440 | tf_op jit(solution)/shard_map/ppermute | solution.py:17
  11.6 6.4 %collective-permute-start.4 = (bf16[256,128]{1,0:T(8,128)(2,1)S(1)}, bf16[256,128]{1,0:T(8,128)(2,1)S(1)}, u32[]{:S(2)}, u32[]{:S(2)}) collective-permute-start(bf16[256,128]{1,0:T(8,128)(2,1)S(1)} %get-tuple-element.30), channel_id=1, source_target_pairs={{0,24},{8,16},{16,8},{24,0},{1,25},{9,17},{17,9},{25,1},{2,26},{10... | collective-permute-start | bytes 196616 | tf_op jit(solution)/shard_map/ppermute | solution.py:17
  15.2 5.9 %collective-permute-start.5 = (bf16[256,128]{1,0:T(8,128)(2,1)S(1)}, bf16[256,128]{1,0:T(8,128)(2,1)S(1)}, u32[]{:S(2)}, u32[]{:S(2)}) collective-permute-start(bf16[256,128]{1,0:T(8,128)(2,1)S(1)} %get-tuple-element.31), channel_id=1, source_target_pairs={{0,16},{8,24},{16,0},{24,8},{1,17},{9,25},{17,1},{25,9},{2,18},{10... | collective-permute-start | bytes 196616 | tf_op jit(solution)/shard_map/ppermute | solution.py:17
  15.2 5.9 %collective-permute-start.6 = (bf16[256,128]{1,0:T(8,128)(2,1)S(1)}, bf16[256,128]{1,0:T(8,128)(2,1)S(1)}, u32[]{:S(2)}, u32[]{:S(2)}) collective-permute-start(bf16[256,128]{1,0:T(8,128)(2,1)S(1)} %get-tuple-element.32), channel_id=1, source_target_pairs={{0,8},{8,0},{16,24},{24,16},{1,9},{9,1},{17,25},{25,17},{2,10},{10... | collective-permute-start | bytes 196616 | tf_op jit(solution)/shard_map/ppermute | solution.py:17
  18.0 7.7 %copy-start = (bf16[1024,128]{1,0:T(8,128)(2,1)S(1)}, bf16[1024,128]{1,0:T(8,128)(2,1)}, u32[]{:S(2)}) copy-start(bf16[1024,128]{1,0:T(8,128)(2,1)} %cotangent_ref.7) | copy-start | bytes 786436
  21.1 4.5 %copy-start.3 = (bf16[128,128]{1,0:T(8,128)(2,1)S(1)}, bf16[128,128]{1,0:T(8,128)(2,1)}, u32[]{:S(2)}) copy-start(bf16[128,128]{1,0:T(8,128)(2,1)} %weight_ref.7) | copy-start | bytes 98308
  21.2 4.5 %copy-start.5 = (f32[128]{0:T(128)S(1)}, f32[128]{0:T(128)}, u32[]{:S(2)}) copy-start(f32[128]{0:T(128)} %bias_ref.7) | copy-start | bytes 1540
  21.2 6.4 %collective-permute-start.7 = (bf16[256,128]{1,0:T(8,128)(2,1)S(1)}, bf16[256,128]{1,0:T(8,128)(2,1)S(1)}, u32[]{:S(2)}, u32[]{:S(2)}) collective-permute-start(bf16[256,128]{1,0:T(8,128)(2,1)S(1)} %shard_map.93.refs_0_), channel_id=1, source_target_pairs={{0,24},{8,16},{16,8},{24,0},{1,25},{9,17},{17,9},{25,1},{2,26},{10... | collective-permute-start | bytes 196616 | tf_op jit(solution)/shard_map/ppermute | solution.py:17
  23.7 6.5 %collective-permute-start.8 = (bf16[256,128]{1,0:T(8,128)(2,1)S(1)}, bf16[256,128]{1,0:T(8,128)(2,1)S(1)}, u32[]{:S(2)}, u32[]{:S(2)}) collective-permute-start(bf16[256,128]{1,0:T(8,128)(2,1)S(1)} %shard_map.93.refs_0_), channel_id=1, source_target_pairs={{0,16},{8,24},{16,0},{24,8},{1,17},{9,25},{17,1},{25,9},{2,18},{10... | collective-permute-start | bytes 196616 | tf_op jit(solution)/shard_map/ppermute | solution.py:17
  23.8 7.0 %collective-permute-start.9 = (bf16[256,128]{1,0:T(8,128)(2,1)S(1)}, bf16[256,128]{1,0:T(8,128)(2,1)S(1)}, u32[]{:S(2)}, u32[]{:S(2)}) collective-permute-start(bf16[256,128]{1,0:T(8,128)(2,1)S(1)} %shard_map.93.refs_0_), channel_id=1, source_target_pairs={{0,8},{8,0},{16,24},{24,16},{1,9},{9,1},{17,25},{25,17},{2,10},{10... | collective-permute-start | bytes 196616 | tf_op jit(solution)/shard_map/ppermute | solution.py:17
  31.4 1.4 %collective-permute-start.10 = (bf16[384,128]{1,0:T(8,128)(2,1)S(1)}, bf16[384,128]{1,0:T(8,128)(2,1)S(1)}, u32[]{:S(2)}, u32[]{:S(2)}) collective-permute-start(bf16[384,128]{1,0:T(8,128)(2,1)S(1)} %get-tuple-element.44.sent_ref), channel_id=1, source_target_pairs={{0,1},{1,0},{2,3},{3,2},{4,5},{5,4},{6,7},{7,6},{8,9},{9,8},{10,11... | collective-permute-start | bytes 294920 | tf_op jit(solution)/shard_map/ppermute | solution.py:17
  31.4 2.9 %collective-permute-start.11 = (bf16[768,128]{1,0:T(8,128)(2,1)S(1)}, bf16[768,128]{1,0:T(8,128)(2,1)S(1)}, u32[]{:S(2)}, u32[]{:S(2)}) collective-permute-start(bf16[768,128]{1,0:T(8,128)(2,1)S(1)} %get-tuple-element.45), channel_id=1, source_target_pairs={{0,1},{1,0},{2,3},{3,2},{4,5},{5,4},{6,7},{7,6},{8,9},{9,8},{10,11... | collective-permute-start | bytes 589832 | tf_op jit(solution)/shard_map/ppermute | solution.py:17
  32.8 6.3 %collective-permute-start.14 = (bf16[384,128]{1,0:T(8,128)(2,1)S(1)}, bf16[384,128]{1,0:T(8,128)(2,1)S(1)}, u32[]{:S(2)}, u32[]{:S(2)}) collective-permute-start(bf16[384,128]{1,0:T(8,128)(2,1)S(1)} %shard_map.99.first_ref.sent_ref), channel_id=1, source_target_pairs={{0,6},{1,7},{2,4},{3,5},{4,2},{5,3},{6,0},{7,1},{8,14},{9,15},{10,... | collective-permute-start | bytes 294920 | tf_op jit(solution)/shard_map/ppermute | solution.py:17
  34.4 6.3 %collective-permute-start.13 = (bf16[384,128]{1,0:T(8,128)(2,1)S(1)}, bf16[384,128]{1,0:T(8,128)(2,1)S(1)}, u32[]{:S(2)}, u32[]{:S(2)}) collective-permute-start(bf16[384,128]{1,0:T(8,128)(2,1)S(1)} %get-tuple-element.48), channel_id=1, source_target_pairs={{0,4},{1,5},{2,6},{3,7},{4,0},{5,1},{6,2},{7,3},{8,12},{9,13},{10,... | collective-permute-start | bytes 294920 | tf_op jit(solution)/shard_map/ppermute | solution.py:17
  34.9 5.8 %collective-permute-start.12 = (bf16[384,128]{1,0:T(8,128)(2,1)S(1)}, bf16[384,128]{1,0:T(8,128)(2,1)S(1)}, u32[]{:S(2)}, u32[]{:S(2)}) collective-permute-start(bf16[384,128]{1,0:T(8,128)(2,1)S(1)} %get-tuple-element.47), channel_id=1, source_target_pairs={{0,2},{1,3},{2,0},{3,1},{4,6},{5,7},{6,4},{7,5},{8,10},{9,11},{10,... | collective-permute-start | bytes 294920 | tf_op jit(solution)/shard_map/ppermute | solution.py:17

commit v8 on v7

--- a/solution.py
+++ b/solution.py
@@ -84,7 +84,7 @@
 def layer_kernel(
     rep, count, own_blocks, j, place_ref, flipped_ref, cotangent_ref, weight_ref, bias_ref, *refs
 ):
-    first, last = j == 0, j == 1
+    first, last = j == 0, j == 3
     piece_ref, refs = refs[0], refs[1:]
     if not first:
         (contrib_in, sums_in), refs = refs[:2], refs[2:]
@@ -115,12 +115,15 @@
         terms = matmul(flipped_ref[row], grad_agg[i * size : (i + 1) * size], (1, 0))
         for k in range(count):
             contrib[place_ref[row * count + k, 0]] += terms[k * size : (k + 1) * size]
-    if first:
+    if j == 0:
         sums_out[0] = part_sum
         sums_out[1] = jnp.zeros_like(part_sum)
-    elif not last:
+    elif j == 2:
         sums_out[0] = sums_in[0]
-        sums_out[1] = sums_in[1] + part_sum
+        sums_out[1] = part_sum
+    elif j == 1:
+        sums_out[0] = sums_in[0] + part_sum
+        sums_out[1] = sums_in[1]
     if not last:
         return
     half = quarter_blocks // 2
@@ -128,7 +131,7 @@
     away = contrib[half:].reshape(half * size, -1).astype(BF16)
     rest_ref[...] = away[:-nodes]
     first_ref[:nodes] = away[-nodes:]
-    first_ref[nodes:] = ((sums_in[0] + part_sum) + sums_in[1]).astype(BF16)
+    first_ref[nodes:] = (sums_in[0] + (sums_in[1] + part_sum)).astype(BF16)
 
 
 def add_kernel(a_ref, b_ref, out_ref):
@@ -238,23 +241,22 @@
 
     partials = call(
         functools.partial(aggregate_kernel, rep),
-        [shape((part, width), BF16 if j else F32) for j in range(rep)],
+        [shape((part, width), BF16 if j % 2 else F32) for j in range(rep)],
         [VMEM] * 4,
     )(place, vals, mine, far)
-    arrived = {j: swap(partials[j], "rep", j) if j else partials[j] for j in range(rep)}
-    order = range(rep - 1, 0, -1)
-    own_rows = arrived[0]
-    for j in order:
-        own_rows = call(add_kernel, shape((part, width), F32 if j > 1 else BF16), [VMEM] * 2)(
-            own_rows, arrived[j]
-        )
-    pieces = {0: own_rows}
-    for j in order:
-        pieces[j] = swap(own_rows, "rep", j)
+    def add(a, b, dtype, cost=0):
+        return call(add_kernel, shape((part, width), dtype), [VMEM] * 2, cost=cost)(a, b)
+
+    passing = swap(partials[3], "rep", 1)
+    beside = swap(partials[1], "rep", 1)
+    crossing = swap(add(partials[2], passing, BF16), "rep", 2)
+    own_rows = add(add(partials[0], beside, F32), crossing, BF16)
+    pieces = {0: own_rows, 2: swap(own_rows, "rep", 2), 1: swap(own_rows, "rep", 1)}
+    pieces[3] = swap(pieces[2], "rep", 1)
 
     outputs, carried = [], []
     for j, piece in pieces.items():
-        if j != 1:
+        if j != 3:
             outs = [shape((quarter_blocks, size, width), F32), shape((2, width, width), F32)]
             scratch = []
         else:

time: 41.7 us -> 42 us (level)
  starting transfers between devices: 17.8 us -> 20.2 us
  waiting for transfers between devices: 15.9 us -> 13.8 us
    ppermute x15, starting transfers between devices: 17.8 us -> 20.2 us  [swap(): return lax.ppermute(value, axis, [(i, i ^ distance) for i in range(size)])]
    ppermute x15, waiting for transfers between devices: 15.9 us -> 13.8 us  [swap(): return lax.ppermute(value, axis, [(i, i ^ distance) for i in range(size)])]
where the time goes in v8:
time: 42 us; the launch traced here: 41.8 us
  starting transfers between devices  20.2 us (48%)
  waiting for transfers between devices  13.8 us (33%)
  Pallas kernels  4.48 us (11%)
  local copies, waits for them, and re-layouts  2.5 us (6%)
  between operations  0.78 us (2%)
    ppermute x15, starting transfers between devices, swap(): return lax.ppermute(value, axis, [(i, i ^ distance) for i in range(size)])  20.2 us
    ppermute x15, waiting for transfers between devices, swap(): return lax.ppermute(value, axis, [(i, i ^ distance) for i in range(size)])  13.8 us
    unnamed x14, local copies, waits for them, and re-layouts  2.5 us
    pallas_call x4, Pallas kernels, body(): call(functools.partial(layer_kernel, rep, count, own_blocks, j), [shape((...  2.15 us
  transfers between devices with their start and end apart: 15, of which 11 were waited for; matrix products, arithmetic and copies ran while one was open for 0% of the time, Pallas kernels for 7%

profile of v8, /device:TPU:0, one launch (start us, length us, event | category | flops | bytes accessed | tf_op | source)
XLA Modules:
  0.0 41.8 jit_solution(13147389995505806075)
XLA Ops:
  0.6 4.0 %collective-permute-start.2 = (bf16[256,128]{1,0:T(8,128)(2,1)}, bf16[256,128]{1,0:T(8,128)(2,1)S(1)}, u32[]{:S(2)}, u32[]{:S(2)}) collective-permute-start(bf16[256,128]{1,0:T(8,128)(2,1)} %features_ref.1), channel_id=1, source_target_pairs={{0,6},{1,7},{2,4},{3,5},{4,2},{5,3},{6,0},{7,1},{8,14},{9,15},{10,... | collective-permute-start | bytes 196616 | tf_op jit(solution)/shard_map/ppermute | solution.py:17
  5.2 1.0 %copy-done.1 = bf16[8,2,128,128]{3,2,1,0:T(8,128)(2,1)S(1)} copy-done((bf16[8,2,128,128]{3,2,1,0:T(8,128)(2,1)S(1)}, bf16[8,2,128,128]{3,2,1,0:T(8,128)(2,1)}, u32[]{:S(2)}) %copy-start.1) | copy-done | bytes 524312
  6.3 0.8 %copy-done.4 = bf16[256,128]{1,0:T(8,128)(2,1)S(1)} copy-done((bf16[256,128]{1,0:T(8,128)(2,1)S(1)}, bf16[256,128]{1,0:T(8,128)(2,1)}, u32[]{:S(2)}) %copy-start.4) | copy-done | bytes 65560
  7.3 1.7 %collective-permute-done.1.refs_0_ = bf16[256,128]{1,0:T(8,128)(2,1)S(1)} collective-permute-done((bf16[256,128]{1,0:T(8,128)(2,1)}, bf16[256,128]{1,0:T(8,128)(2,1)S(1)}, u32[]{:S(2)}, u32[]{:S(2)}) %collective-permute-start.1) | collective-permute-done | bytes 65568 | tf_op jit(solution)/shard_map/ppermute | solution.py:17
  9.7 0.6 %copy-done.6 = s32[8,2]{0,1:T(2,128)S(1)} copy-done((s32[8,2]{0,1:T(2,128)S(1)}, s32[8,2]{0,1:T(2,128)}, u32[]{:S(2)}) %copy-start.6) | copy-done | bytes 88
  10.5 0.8 %collective-permute-done.3.far_ref = bf16[1024,128]{1,0:T(8,128)(2,1)S(1)} collective-permute-done((bf16[1024,128]{1,0:T(8,128)(2,1)S(1)}, bf16[1024,128]{1,0:T(8,128)(2,1)S(1)}, u32[]{:S(2)}, u32[]{:S(2)}) %collective-permute-start.3) | collective-permute-done | bytes 262176 | tf_op jit(solution)/shard_map/ppermute | solution.py:17
  11.6 1.6 %collective-permute-start.5 = (bf16[256,128]{1,0:T(8,128)(2,1)S(1)}, bf16[256,128]{1,0:T(8,128)(2,1)S(1)}, u32[]{:S(2)}, u32[]{:S(2)}) collective-permute-start(bf16[256,128]{1,0:T(8,128)(2,1)S(1)} %get-tuple-element.32), channel_id=1, source_target_pairs={{0,8},{8,0},{16,24},{24,16},{1,9},{9,1},{17,25},{25,17},{2,10},{10... | collective-permute-start | bytes 196616 | tf_op jit(solution)/shard_map/ppermute | solution.py:17
  13.7 2.6 %collective-permute-done.5.b_ref = bf16[256,128]{1,0:T(8,128)(2,1)S(1)} collective-permute-done((bf16[256,128]{1,0:T(8,128)(2,1)S(1)}, bf16[256,128]{1,0:T(8,128)(2,1)S(1)}, u32[]{:S(2)}, u32[]{:S(2)}) %collective-permute-start.5) | collective-permute-done | bytes 65568 | tf_op jit(solution)/shard_map/ppermute | solution.py:17
  16.2 2.7 %collective-permute-start.6 = (bf16[256,128]{1,0:T(8,128)(2,1)S(1)}, bf16[256,128]{1,0:T(8,128)(2,1)S(1)}, u32[]{:S(2)}, u32[]{:S(2)}) collective-permute-start(bf16[256,128]{1,0:T(8,128)(2,1)S(1)} %shard_map.92), channel_id=1, source_target_pairs={{0,16},{8,24},{16,0},{24,8},{1,17},{9,25},{17,1},{25,9},{2,18},{10... | collective-permute-start | bytes 196616 | tf_op jit(solution)/shard_map/ppermute | solution.py:17
  18.9 2.5 %collective-permute-done.6.b_ref = bf16[256,128]{1,0:T(8,128)(2,1)S(1)} collective-permute-done((bf16[256,128]{1,0:T(8,128)(2,1)S(1)}, bf16[256,128]{1,0:T(8,128)(2,1)S(1)}, u32[]{:S(2)}, u32[]{:S(2)}) %collective-permute-start.6) | collective-permute-done | bytes 65568 | tf_op jit(solution)/shard_map/ppermute | solution.py:17
  21.5 2.7 %collective-permute-start.7 = (bf16[256,128]{1,0:T(8,128)(2,1)S(1)}, bf16[256,128]{1,0:T(8,128)(2,1)S(1)}, u32[]{:S(2)}, u32[]{:S(2)}) collective-permute-start(bf16[256,128]{1,0:T(8,128)(2,1)S(1)} %shard_map.93.refs_0_), channel_id=1, source_target_pairs={{0,16},{8,24},{16,0},{24,8},{1,17},{9,25},{17,1},{25,9},{2,18},{10... | collective-permute-start | bytes 196616 | tf_op jit(solution)/shard_map/ppermute | solution.py:17
  24.2 2.1 %collective-permute-start.8 = (bf16[256,128]{1,0:T(8,128)(2,1)S(1)}, bf16[256,128]{1,0:T(8,128)(2,1)S(1)}, u32[]{:S(2)}, u32[]{:S(2)}) collective-permute-start(bf16[256,128]{1,0:T(8,128)(2,1)S(1)} %shard_map.93.refs_0_), channel_id=1, source_target_pairs={{0,8},{8,0},{16,24},{24,16},{1,9},{9,1},{17,25},{25,17},{2,10},{10... | collective-permute-start | bytes 196616 | tf_op jit(solution)/shard_map/ppermute | solution.py:17
  26.8 1.8 %collective-permute-start.9 = (bf16[256,128]{1,0:T(8,128)(2,1)S(1)}, bf16[256,128]{1,0:T(8,128)(2,1)S(1)}, u32[]{:S(2)}, u32[]{:S(2)}) collective-permute-start(bf16[256,128]{1,0:T(8,128)(2,1)S(1)} %collective-permute-done.7.refs_0_), channel_id=1, source_target_pairs={{0,8},{8,0},{16,24},{24,16},{1,9},{9,1},{17,25},{25,17},{2,10},{10... | collective-permute-start | bytes 196616 | tf_op jit(solution)/shard_map/ppermute | solution.py:17
  29.1 0.5 %shard_map.95 = (bf16[256,128]{1,0:T(8,128)(2,1)S(1)}, f32[16,128,128]{2,1,0:T(8,128)S(1)}, f32[2,128,128]{2,1,0:T(8,128)S(1)}) custom-call(s32[16,128]{1,0:T(8,128)S(1)} %shard_map.89.place_ref, bf16[8,256,128]{2,1,0:T(8,128)(2,1)S(1)} %get-tuple-element.28.flipped_ref, bf16[1024,128]{1,0:T(8,128)(2,1)S(1)} %copy-done, bf16[128,128]{1,0:T(8,128)(2,1)S(1)} %copy-done.3, ...), custom_call_target="tpu_custom_call" | custom-call | tf_op jit(solution)/shard_map/pallas_call | solution.py:269
  29.6 0.5 %shard_map.96 = (bf16[256,128]{1,0:T(8,128)(2,1)S(1)}, f32[16,128,128]{2,1,0:T(8,128)S(1)}, f32[2,128,128]{2,1,0:T(8,128)S(1)}) custom-call(s32[16,128]{1,0:T(8,128)S(1)} %shard_map.89.place_ref, bf16[8,256,128]{2,1,0:T(8,128)(2,1)S(1)} %get-tuple-element.28.flipped_ref, bf16[1024,128]{1,0:T(8,128)(2,1)S(1)} %copy-done, bf16[128,128]{1,0:T(8,128)(2,1)S(1)} %copy-done.3, ...), custom_call_target="tpu_custom_call" | custom-call | tf_op jit(solution)/shard_map/pallas_call | solution.py:269
  30.2 0.9 %collective-permute-done.9.refs_0_ = bf16[256,128]{1,0:T(8,128)(2,1)S(1)} collective-permute-done((bf16[256,128]{1,0:T(8,128)(2,1)S(1)}, bf16[256,128]{1,0:T(8,128)(2,1)S(1)}, u32[]{:S(2)}, u32[]{:S(2)}) %collective-permute-start.9) | collective-permute-done | bytes 65568 | tf_op jit(solution)/shard_map/ppermute | solution.py:17
  31.1 0.6 %shard_map.97 = (bf16[256,128]{1,0:T(8,128)(2,1)S(1)}, bf16[384,128]{1,0:T(8,128)(2,1)S(1)}, bf16[768,128]{1,0:T(8,128)(2,1)S(1)}, f32[4,256,128]{2,1,0:T(8,128)S(1)}) custom-call(s32[16,128]{1,0:T(8,128)S(1)} %shard_map.89.place_ref, bf16[8,256,128]{2,1,0:T(8,128)(2,1)S(1)} %get-tuple-element.28.flipped_ref, bf16[1024,128]{1,0:T(8,128)(2,1)S(1)} %copy-done, ...), custom_call_target="tpu_custom_call" | custom-call | tf_op jit(solution)/shard_map/pallas_call | solution.py:269
  32.2 0.8 %collective-permute-done.10.got_ref = bf16[384,128]{1,0:T(8,128)(2,1)S(1)} collective-permute-done((bf16[384,128]{1,0:T(8,128)(2,1)S(1)}, bf16[384,128]{1,0:T(8,128)(2,1)S(1)}, u32[]{:S(2)}, u32[]{:S(2)}) %collective-permute-start.10) | collective-permute-done | bytes 98336 | tf_op jit(solution)/shard_map/ppermute | solution.py:17
  33.0 1.6 %collective-permute-start.14 = (bf16[384,128]{1,0:T(8,128)(2,1)S(1)}, bf16[384,128]{1,0:T(8,128)(2,1)S(1)}, u32[]{:S(2)}, u32[]{:S(2)}) collective-permute-start(bf16[384,128]{1,0:T(8,128)(2,1)S(1)} %shard_map.99.first_ref.sent_ref), channel_id=1, source_target_pairs={{0,6},{1,7},{2,4},{3,5},{4,2},{5,3},{6,0},{7,1},{8,14},{9,15},{10,... | collective-permute-start | bytes 294920 | tf_op jit(solution)/shard_map/ppermute | solution.py:17
  35.1 1.7 %collective-permute-start.12 = (bf16[384,128]{1,0:T(8,128)(2,1)S(1)}, bf16[384,128]{1,0:T(8,128)(2,1)S(1)}, u32[]{:S(2)}, u32[]{:S(2)}) collective-permute-start(bf16[384,128]{1,0:T(8,128)(2,1)S(1)} %get-tuple-element.47), channel_id=1, source_target_pairs={{0,2},{1,3},{2,0},{3,1},{4,6},{5,7},{6,4},{7,5},{8,10},{9,11},{10,... | collective-permute-start | bytes 294920 | tf_op jit(solution)/shard_map/ppermute | solution.py:17
  36.7 0.7 %shard_map.98 = bf16[1024,128]{1,0:T(8,128)(2,1)} custom-call(bf16[256,128]{1,0:T(8,128)(2,1)S(1)} %get-tuple-element.33.refs_0_, bf16[256,128]{1,0:T(8,128)(2,1)S(1)} %get-tuple-element.36.refs_1_, bf16[256,128]{1,0:T(8,128)(2,1)S(1)} %get-tuple-element.39.refs_2_, bf16[256,128]{1,0:T(8,128)(2,1)S(1)} %get-tuple-element.42.refs_3_), custom_call_target="tpu_custom_call" | custom-call | tf_op jit(solution)/shard_map/pallas_call | solution.py:286
  37.4 1.9 %collective-permute-done.14.got_ref = bf16[384,128]{1,0:T(8,128)(2,1)S(1)} collective-permute-done((bf16[384,128]{1,0:T(8,128)(2,1)S(1)}, bf16[384,128]{1,0:T(8,128)(2,1)S(1)}, u32[]{:S(2)}, u32[]{:S(2)}) %collective-permute-start.14) | collective-permute-done | bytes 98336 | tf_op jit(solution)/shard_map/ppermute | solution.py:17
  39.4 1.6 %collective-permute-done.13.refs_0_ = bf16[384,128]{1,0:T(8,128)(2,1)S(1)} collective-permute-done((bf16[384,128]{1,0:T(8,128)(2,1)S(1)}, bf16[384,128]{1,0:T(8,128)(2,1)S(1)}, u32[]{:S(2)}, u32[]{:S(2)}) %collective-permute-start.13) | collective-permute-done | bytes 98336 | tf_op jit(solution)/shard_map/ppermute | solution.py:17
  41.1 0.7 %shard_map.103 = (f32[256,128]{1,0:T(8,128)}, f32[128,128]{1,0:T(8,128)}) custom-call(f32[256,128]{1,0:T(8,128)S(1)} %get-tuple-element.46.own_ref, bf16[384,128]{1,0:T(8,128)(2,1)S(1)} %shard_map.99.first_ref.sent_ref, bf16[384,128]{1,0:T(8,128)(2,1)S(1)} %collective-permute-done.12.got_ref, f32[384,128]{1,0:T(8,128)S(1)} %shard_map.102.refs_0_), custom_call_target="tpu_custom_call" | custom-call | tf_op jit(solution)/shard_map/pallas_call | solution.py:295
  (39 shorter events, 4.6 us)
Async XLA Ops:
  0.6 6.7 %collective-permute-start.2 = (bf16[256,128]{1,0:T(8,128)(2,1)}, bf16[256,128]{1,0:T(8,128)(2,1)S(1)}, u32[]{:S(2)}, u32[]{:S(2)}) collective-permute-start(bf16[256,128]{1,0:T(8,128)(2,1)} %features_ref.1), channel_id=1, source_target_pairs={{0,6},{1,7},{2,4},{3,5},{4,2},{5,3},{6,0},{7,1},{8,14},{9,15},{10,... | collective-permute-start | bytes 196616 | tf_op jit(solution)/shard_map/ppermute | solution.py:17
  4.6 4.5 %collective-permute-start.1 = (bf16[256,128]{1,0:T(8,128)(2,1)}, bf16[256,128]{1,0:T(8,128)(2,1)S(1)}, u32[]{:S(2)}, u32[]{:S(2)}) collective-permute-start(bf16[256,128]{1,0:T(8,128)(2,1)} %features_ref.1), channel_id=1, source_target_pairs={{0,4},{1,5},{2,6},{3,7},{4,0},{5,1},{6,2},{7,3},{8,12},{9,13},{10,... | collective-permute-start | bytes 196616 | tf_op jit(solution)/shard_map/ppermute | solution.py:17
  5.1 4.5 %collective-permute-start = (bf16[256,128]{1,0:T(8,128)(2,1)}, bf16[256,128]{1,0:T(8,128)(2,1)S(1)}, u32[]{:S(2)}, u32[]{:S(2)}) collective-permute-start(bf16[256,128]{1,0:T(8,128)(2,1)} %features_ref.1), channel_id=1, source_target_pairs={{0,2},{1,3},{2,0},{3,1},{4,6},{5,7},{6,4},{7,5},{8,10},{9,11},{10,... | collective-permute-start | bytes 196616 | tf_op jit(solution)/shard_map/ppermute | solution.py:17
  5.2 1.0 %copy-start.1 = (bf16[8,2,128,128]{3,2,1,0:T(8,128)(2,1)S(1)}, bf16[8,2,128,128]{3,2,1,0:T(8,128)(2,1)}, u32[]{:S(2)}) copy-start(bf16[8,2,128,128]{3,2,1,0:T(8,128)(2,1)} %vals_ref.3) | copy-start | bytes 1572868
  6.3 0.8 %copy-start.4 = (bf16[256,128]{1,0:T(8,128)(2,1)S(1)}, bf16[256,128]{1,0:T(8,128)(2,1)}, u32[]{:S(2)}) copy-start(bf16[256,128]{1,0:T(8,128)(2,1)} %features_ref.1) | copy-start | bytes 196612
  7.3 3.9 %copy-start.2 = (bf16[8,2,128,128]{3,2,1,0:T(8,128)(2,1)S(1)}, bf16[8,2,128,128]{3,2,1,0:T(8,128)(2,1)}, u32[]{:S(2)}) copy-start(bf16[8,2,128,128]{3,2,1,0:T(8,128)(2,1)} %vals_ref.3) | copy-start | bytes 1572868
  9.6 0.7 %copy-start.6 = (s32[8,2]{0,1:T(2,128)S(1)}, s32[8,2]{0,1:T(2,128)}, u32[]{:S(2)}) copy-start(s32[8,2]{0,1:T(2,128)} %param.6) | copy-start | bytes 196
  9.6 1.6 %collective-permute-start.3 = (bf16[1024,128]{1,0:T(8,128)(2,1)S(1)}, bf16[1024,128]{1,0:T(8,128)(2,1)S(1)}, u32[]{:S(2)}, u32[]{:S(2)}) collective-permute-start(bf16[1024,128]{1,0:T(8,128)(2,1)S(1)} %shard_map.88._.mine_ref), channel_id=1, source_target_pairs={{0,1},{1,0},{2,3},{3,2},{4,5},{5,4},{6,7},{7,6},{8,9},{9,8},{10,11... | collective-permute-start | bytes 786440 | tf_op jit(solution)/shard_map/ppermute | solution.py:17
  11.6 4.6 %collective-permute-start.5 = (bf16[256,128]{1,0:T(8,128)(2,1)S(1)}, bf16[256,128]{1,0:T(8,128)(2,1)S(1)}, u32[]{:S(2)}, u32[]{:S(2)}) collective-permute-start(bf16[256,128]{1,0:T(8,128)(2,1)S(1)} %get-tuple-element.32), channel_id=1, source_target_pairs={{0,8},{8,0},{16,24},{24,16},{1,9},{9,1},{17,25},{25,17},{2,10},{10... | collective-permute-start | bytes 196616 | tf_op jit(solution)/shard_map/ppermute | solution.py:17
  13.2 5.7 %collective-permute-start.4 = (bf16[256,128]{1,0:T(8,128)(2,1)S(1)}, bf16[256,128]{1,0:T(8,128)(2,1)S(1)}, u32[]{:S(2)}, u32[]{:S(2)}) collective-permute-start(bf16[256,128]{1,0:T(8,128)(2,1)S(1)} %get-tuple-element.30), channel_id=1, source_target_pairs={{0,8},{8,0},{16,24},{24,16},{1,9},{9,1},{17,25},{25,17},{2,10},{10... | collective-permute-start | bytes 196616 | tf_op jit(solution)/shard_map/ppermute | solution.py:17
  16.2 5.2 %collective-permute-start.6 = (bf16[256,128]{1,0:T(8,128)(2,1)S(1)}, bf16[256,128]{1,0:T(8,128)(2,1)S(1)}, u32[]{:S(2)}, u32[]{:S(2)}) collective-permute-start(bf16[256,128]{1,0:T(8,128)(2,1)S(1)} %shard_map.92), channel_id=1, source_target_pairs={{0,16},{8,24},{16,0},{24,8},{1,17},{9,25},{17,1},{25,9},{2,18},{10... | collective-permute-start | bytes 196616 | tf_op jit(solution)/shard_map/ppermute | solution.py:17
  18.9 9.7 %copy-start = (bf16[1024,128]{1,0:T(8,128)(2,1)S(1)}, bf16[1024,128]{1,0:T(8,128)(2,1)}, u32[]{:S(2)}) copy-start(bf16[1024,128]{1,0:T(8,128)(2,1)} %cotangent_ref.7) | copy-start | bytes 786436
  18.9 9.7 %copy-start.3 = (bf16[128,128]{1,0:T(8,128)(2,1)S(1)}, bf16[128,128]{1,0:T(8,128)(2,1)}, u32[]{:S(2)}) copy-start(bf16[128,128]{1,0:T(8,128)(2,1)} %weight_ref.7) | copy-start | bytes 98308
  21.5 7.1 %copy-start.5 = (f32[128]{0:T(128)S(1)}, f32[128]{0:T(128)}, u32[]{:S(2)}) copy-start(f32[128]{0:T(128)} %bias_ref.7) | copy-start | bytes 1540
  21.5 5.3 %collective-permute-start.7 = (bf16[256,128]{1,0:T(8,128)(2,1)S(1)}, bf16[256,128]{1,0:T(8,128)(2,1)S(1)}, u32[]{:S(2)}, u32[]{:S(2)}) collective-permute-start(bf16[256,128]{1,0:T(8,128)(2,1)S(1)} %shard_map.93.refs_0_), channel_id=1, source_target_pairs={{0,16},{8,24},{16,0},{24,8},{1,17},{9,25},{17,1},{25,9},{2,18},{10... | collective-permute-start | bytes 196616 | tf_op jit(solution)/shard_map/ppermute | solution.py:17
  24.2 5.5 %collective-permute-start.8 = (bf16[256,128]{1,0:T(8,128)(2,1)S(1)}, bf16[256,128]{1,0:T(8,128)(2,1)S(1)}, u32[]{:S(2)}, u32[]{:S(2)}) collective-permute-start(bf16[256,128]{1,0:T(8,128)(2,1)S(1)} %shard_map.93.refs_0_), channel_id=1, source_target_pairs={{0,8},{8,0},{16,24},{24,16},{1,9},{9,1},{17,25},{25,17},{2,10},{10... | collective-permute-start | bytes 196616 | tf_op jit(solution)/shard_map/ppermute | solution.py:17
  26.8 4.3 %collective-permute-start.9 = (bf16[256,128]{1,0:T(8,128)(2,1)S(1)}, bf16[256,128]{1,0:T(8,128)(2,1)S(1)}, u32[]{:S(2)}, u32[]{:S(2)}) collective-permute-start(bf16[256,128]{1,0:T(8,128)(2,1)S(1)} %collective-permute-done.7.refs_0_), channel_id=1, source_target_pairs={{0,8},{8,0},{16,24},{24,16},{1,9},{9,1},{17,25},{25,17},{2,10},{10... | collective-permute-start | bytes 196616 | tf_op jit(solution)/shard_map/ppermute | solution.py:17
  31.7 1.4 %collective-permute-start.10 = (bf16[384,128]{1,0:T(8,128)(2,1)S(1)}, bf16[384,128]{1,0:T(8,128)(2,1)S(1)}, u32[]{:S(2)}, u32[]{:S(2)}) collective-permute-start(bf16[384,128]{1,0:T(8,128)(2,1)S(1)} %get-tuple-element.44.sent_ref), channel_id=1, source_target_pairs={{0,1},{1,0},{2,3},{3,2},{4,5},{5,4},{6,7},{7,6},{8,9},{9,8},{10,11... | collective-permute-start | bytes 294920 | tf_op jit(solution)/shard_map/ppermute | solution.py:17
  31.7 2.9 %collective-permute-start.11 = (bf16[768,128]{1,0:T(8,128)(2,1)S(1)}, bf16[768,128]{1,0:T(8,128)(2,1)S(1)}, u32[]{:S(2)}, u32[]{:S(2)}) collective-permute-start(bf16[768,128]{1,0:T(8,128)(2,1)S(1)} %get-tuple-element.45), channel_id=1, source_target_pairs={{0,1},{1,0},{2,3},{3,2},{4,5},{5,4},{6,7},{7,6},{8,9},{9,8},{10,11... | collective-permute-start | bytes 589832 | tf_op jit(solution)/shard_map/ppermute | solution.py:17
  33.0 6.3 %collective-permute-start.14 = (bf16[384,128]{1,0:T(8,128)(2,1)S(1)}, bf16[384,128]{1,0:T(8,128)(2,1)S(1)}, u32[]{:S(2)}, u32[]{:S(2)}) collective-permute-start(bf16[384,128]{1,0:T(8,128)(2,1)S(1)} %shard_map.99.first_ref.sent_ref), channel_id=1, source_target_pairs={{0,6},{1,7},{2,4},{3,5},{4,2},{5,3},{6,0},{7,1},{8,14},{9,15},{10,... | collective-permute-start | bytes 294920 | tf_op jit(solution)/shard_map/ppermute | solution.py:17
  34.7 6.3 %collective-permute-start.13 = (bf16[384,128]{1,0:T(8,128)(2,1)S(1)}, bf16[384,128]{1,0:T(8,128)(2,1)S(1)}, u32[]{:S(2)}, u32[]{:S(2)}) collective-permute-start(bf16[384,128]{1,0:T(8,128)(2,1)S(1)} %get-tuple-element.48), channel_id=1, source_target_pairs={{0,4},{1,5},{2,6},{3,7},{4,0},{5,1},{6,2},{7,3},{8,12},{9,13},{10,... | collective-permute-start | bytes 294920 | tf_op jit(solution)/shard_map/ppermute | solution.py:17
  35.1 6.0 %collective-permute-start.12 = (bf16[384,128]{1,0:T(8,128)(2,1)S(1)}, bf16[384,128]{1,0:T(8,128)(2,1)S(1)}, u32[]{:S(2)}, u32[]{:S(2)}) collective-permute-start(bf16[384,128]{1,0:T(8,128)(2,1)S(1)} %get-tuple-element.47), channel_id=1, source_target_pairs={{0,2},{1,3},{2,0},{3,1},{4,6},{5,7},{6,4},{7,5},{8,10},{9,11},{10,... | collective-permute-start | bytes 294920 | tf_op jit(solution)/shard_map/ppermute | solution.py:17

commit v9 on v8

--- a/solution.py
+++ b/solution.py
@@ -91,7 +91,9 @@
     if last:
         output_ref, first_ref, rest_ref, keep_ref, contrib = refs
     else:
-        output_ref, contrib, sums_out = refs
+        output_ref, contrib, sums_out = refs[:3]
+    if first:
+        refs[3][...] = piece_ref[...]
     rows, _, size = flipped_ref.shape
     share = rows // rep
     quarter_blocks = contrib.shape[0]
@@ -134,6 +136,11 @@
     first_ref[nodes:] = (sums_in[0] + (sums_in[1] + part_sum)).astype(BF16)
 
 
+def combine_kernel(partial_ref, passing_ref, staying_ref, combined_ref, out_ref):
+    combined_ref[...] = (partial_ref[...] + passing_ref[...].astype(F32)).astype(BF16)
+    out_ref[...] = staying_ref[...]
+
+
 def add_kernel(a_ref, b_ref, out_ref):
     out_ref[...] = (a_ref[...] + b_ref[...].astype(F32)).astype(out_ref.dtype)
 
@@ -244,21 +251,27 @@
         [shape((part, width), BF16 if j % 2 else F32) for j in range(rep)],
         [VMEM] * 4,
     )(place, vals, mine, far)
-    def add(a, b, dtype, cost=0):
-        return call(add_kernel, shape((part, width), dtype), [VMEM] * 2, cost=cost)(a, b)
+    def add(a, b, dtype):
+        return call(add_kernel, shape((part, width), dtype), [VMEM] * 2, cost=10**9)(a, b)
 
     passing = swap(partials[3], "rep", 1)
-    beside = swap(partials[1], "rep", 1)
-    crossing = swap(add(partials[2], passing, BF16), "rep", 2)
-    own_rows = add(add(partials[0], beside, F32), crossing, BF16)
-    pieces = {0: own_rows, 2: swap(own_rows, "rep", 2), 1: swap(own_rows, "rep", 1)}
+    combined, staying = call(
+        combine_kernel, [shape((part, width), BF16)] * 2, [VMEM] * 3
+    )(partials[2], passing, partials[1])
+    crossing = swap(combined, "rep", 2)
+    beside = swap(staying, "rep", 1)
+    own_rows = add(add(partials[0], crossing, F32), beside, BF16)
+    pieces = {0: own_rows, 2: swap(own_rows, "rep", 2)}
+    pieces[1] = None
     pieces[3] = swap(pieces[2], "rep", 1)
 
     outputs, carried = [], []
-    for j, piece in pieces.items():
+    for j in pieces:
         if j != 3:
             outs = [shape((quarter_blocks, size, width), F32), shape((2, width, width), F32)]
             scratch = []
+            if j == 0:
+                outs += [shape((part, width), BF16)]
         else:
             outs = [
                 shape((nodes + width, width), BF16),
@@ -271,8 +284,10 @@
             [shape((part, width), BF16)] + outs,
             [VMEM] * (6 + len(carried)),
             scratch,
-        )(place, flipped, cotangent, weight, bias, piece, *carried)
+        )(place, flipped, cotangent, weight, bias, pieces[j], *carried)
         outputs.append(output)
+        if j == 0:
+            pieces[1] = swap(carried.pop(), "rep", 1)
     first, rest, keep = carried
 
     message = shape((nodes + width, width), BF16)

time: 42 us -> 43.4 us (1.033)
  waiting for transfers between devices: 13.8 us -> 15.3 us
    ppermute x15, waiting for transfers between devices: 13.8 us -> 15.3 us  [swap(): return lax.ppermute(value, axis, [(i, i ^ distance) for i in range(size)])]
  transfers between devices with their start and end apart: 15 -> 15, of which waited for: 11 -> 12; matrix products, arithmetic and copies ran while one was open for 0% -> 0% of each run, Pallas kernels for 7% -> 6%
where the time goes in v9:
time: 43.4 us; the launch traced here: 43.2 us
  starting transfers between devices  20.2 us (47%)
  waiting for transfers between devices  15.3 us (35%)
  Pallas kernels  4.48 us (10%)
  local copies, waits for them, and re-layouts  2.5 us (6%)
  between operations  0.8 us (2%)
    ppermute x15, starting transfers between devices, swap(): return lax.ppermute(value, axis, [(i, i ^ distance) for i in range(size)])  20.2 us
    ppermute x15, waiting for transfers between devices, swap(): return lax.ppermute(value, axis, [(i, i ^ distance) for i in range(size)])  15.3 us
    unnamed x14, local copies, waits for them, and re-layouts  2.5 us
    pallas_call x4, Pallas kernels, body(): call(functools.partial(layer_kernel, rep, count, own_blocks, j), [shape((...  2.16 us
  transfers between devices with their start and end apart: 15, of which 12 were waited for; matrix products, arithmetic and copies ran while one was open for 0% of the time, Pallas kernels for 6%

profile of v9, /device:TPU:0, one launch (start us, length us, event | category | flops | bytes accessed | tf_op | source)
XLA Modules:
  0.0 43.2 jit_solution(9078571138127440053)
XLA Ops:
  0.6 4.0 %collective-permute-start.2 = (bf16[256,128]{1,0:T(8,128)(2,1)}, bf16[256,128]{1,0:T(8,128)(2,1)S(1)}, u32[]{:S(2)}, u32[]{:S(2)}) collective-permute-start(bf16[256,128]{1,0:T(8,128)(2,1)} %features_ref.1), channel_id=1, source_target_pairs={{0,6},{1,7},{2,4},{3,5},{4,2},{5,3},{6,0},{7,1},{8,14},{9,15},{10,... | collective-permute-start | bytes 196616 | tf_op jit(solution)/shard_map/ppermute | solution.py:17
  5.2 1.0 %copy-done.1 = bf16[8,2,128,128]{3,2,1,0:T(8,128)(2,1)S(1)} copy-done((bf16[8,2,128,128]{3,2,1,0:T(8,128)(2,1)S(1)}, bf16[8,2,128,128]{3,2,1,0:T(8,128)(2,1)}, u32[]{:S(2)}) %copy-start.1) | copy-done | bytes 524312
  6.3 0.8 %copy-done.4 = bf16[256,128]{1,0:T(8,128)(2,1)S(1)} copy-done((bf16[256,128]{1,0:T(8,128)(2,1)S(1)}, bf16[256,128]{1,0:T(8,128)(2,1)}, u32[]{:S(2)}) %copy-start.4) | copy-done | bytes 65560
  7.3 1.7 %collective-permute-done.1.refs_0_ = bf16[256,128]{1,0:T(8,128)(2,1)S(1)} collective-permute-done((bf16[256,128]{1,0:T(8,128)(2,1)}, bf16[256,128]{1,0:T(8,128)(2,1)S(1)}, u32[]{:S(2)}, u32[]{:S(2)}) %collective-permute-start.1) | collective-permute-done | bytes 65568 | tf_op jit(solution)/shard_map/ppermute | solution.py:17
  9.7 0.6 %copy-done.6 = s32[8,2]{0,1:T(2,128)S(1)} copy-done((s32[8,2]{0,1:T(2,128)S(1)}, s32[8,2]{0,1:T(2,128)}, u32[]{:S(2)}) %copy-start.6) | copy-done | bytes 88
  10.5 0.8 %collective-permute-done.3.far_ref = bf16[1024,128]{1,0:T(8,128)(2,1)S(1)} collective-permute-done((bf16[1024,128]{1,0:T(8,128)(2,1)S(1)}, bf16[1024,128]{1,0:T(8,128)(2,1)S(1)}, u32[]{:S(2)}, u32[]{:S(2)}) %collective-permute-start.3) | collective-permute-done | bytes 262176 | tf_op jit(solution)/shard_map/ppermute | solution.py:17
  11.6 1.6 %collective-permute-start.4 = (bf16[256,128]{1,0:T(8,128)(2,1)S(1)}, bf16[256,128]{1,0:T(8,128)(2,1)S(1)}, u32[]{:S(2)}, u32[]{:S(2)}) collective-permute-start(bf16[256,128]{1,0:T(8,128)(2,1)S(1)} %get-tuple-element.34), channel_id=1, source_target_pairs={{0,8},{8,0},{16,24},{24,16},{1,9},{9,1},{17,25},{25,17},{2,10},{10... | collective-permute-start | bytes 196616 | tf_op jit(solution)/shard_map/ppermute | solution.py:17
  13.2 2.7 %collective-permute-done.4.passing_ref = bf16[256,128]{1,0:T(8,128)(2,1)S(1)} collective-permute-done((bf16[256,128]{1,0:T(8,128)(2,1)S(1)}, bf16[256,128]{1,0:T(8,128)(2,1)S(1)}, u32[]{:S(2)}, u32[]{:S(2)}) %collective-permute-start.4) | collective-permute-done | bytes 65568 | tf_op jit(solution)/shard_map/ppermute | solution.py:17
  15.9 2.7 %collective-permute-start.5 = (bf16[256,128]{1,0:T(8,128)(2,1)S(1)}, bf16[256,128]{1,0:T(8,128)(2,1)S(1)}, u32[]{:S(2)}, u32[]{:S(2)}) collective-permute-start(bf16[256,128]{1,0:T(8,128)(2,1)S(1)} %get-tuple-element.36), channel_id=1, source_target_pairs={{0,16},{8,24},{16,0},{24,8},{1,17},{9,25},{17,1},{25,9},{2,18},{10... | collective-permute-start | bytes 196616 | tf_op jit(solution)/shard_map/ppermute | solution.py:17
  18.6 1.6 %collective-permute-start.6 = (bf16[256,128]{1,0:T(8,128)(2,1)S(1)}, bf16[256,128]{1,0:T(8,128)(2,1)S(1)}, u32[]{:S(2)}, u32[]{:S(2)}) collective-permute-start(bf16[256,128]{1,0:T(8,128)(2,1)S(1)} %get-tuple-element.37), channel_id=1, source_target_pairs={{0,8},{8,0},{16,24},{24,16},{1,9},{9,1},{17,25},{25,17},{2,10},{10... | collective-permute-start | bytes 196616 | tf_op jit(solution)/shard_map/ppermute | solution.py:17
  20.2 1.1 %collective-permute-done.5.b_ref = bf16[256,128]{1,0:T(8,128)(2,1)S(1)} collective-permute-done((bf16[256,128]{1,0:T(8,128)(2,1)S(1)}, bf16[256,128]{1,0:T(8,128)(2,1)S(1)}, u32[]{:S(2)}, u32[]{:S(2)}) %collective-permute-start.5) | collective-permute-done | bytes 65568 | tf_op jit(solution)/shard_map/ppermute | solution.py:17
  21.3 1.5 %collective-permute-done.6.b_ref = bf16[256,128]{1,0:T(8,128)(2,1)S(1)} collective-permute-done((bf16[256,128]{1,0:T(8,128)(2,1)S(1)}, bf16[256,128]{1,0:T(8,128)(2,1)S(1)}, u32[]{:S(2)}, u32[]{:S(2)}) %collective-permute-start.6) | collective-permute-done | bytes 65568 | tf_op jit(solution)/shard_map/ppermute | solution.py:17
  22.9 1.1 %collective-permute-start.7 = (bf16[256,128]{1,0:T(8,128)(2,1)S(1)}, bf16[256,128]{1,0:T(8,128)(2,1)S(1)}, u32[]{:S(2)}, u32[]{:S(2)}) collective-permute-start(bf16[256,128]{1,0:T(8,128)(2,1)S(1)} %shard_map.93.refs_0_), channel_id=1, source_target_pairs={{0,16},{8,24},{16,0},{24,8},{1,17},{9,25},{17,1},{25,9},{2,18},{10... | collective-permute-start | bytes 196616 | tf_op jit(solution)/shard_map/ppermute | solution.py:17
  24.5 2.2 %collective-permute-start.8 = (bf16[256,128]{1,0:T(8,128)(2,1)S(1)}, bf16[256,128]{1,0:T(8,128)(2,1)S(1)}, u32[]{:S(2)}, u32[]{:S(2)}) collective-permute-start(bf16[256,128]{1,0:T(8,128)(2,1)S(1)} %get-tuple-element.42), channel_id=1, source_target_pairs={{0,8},{8,0},{16,24},{24,16},{1,9},{9,1},{17,25},{25,17},{2,10},{10... | collective-permute-start | bytes 196616 | tf_op jit(solution)/shard_map/ppermute | solution.py:17
  26.7 1.4 %collective-permute-done.7.refs_0_ = bf16[256,128]{1,0:T(8,128)(2,1)S(1)} collective-permute-done((bf16[256,128]{1,0:T(8,128)(2,1)S(1)}, bf16[256,128]{1,0:T(8,128)(2,1)S(1)}, u32[]{:S(2)}, u32[]{:S(2)}) %collective-permute-start.7) | collective-permute-done | bytes 65568 | tf_op jit(solution)/shard_map/ppermute | solution.py:17
  28.1 2.2 %collective-permute-start.9 = (bf16[256,128]{1,0:T(8,128)(2,1)S(1)}, bf16[256,128]{1,0:T(8,128)(2,1)S(1)}, u32[]{:S(2)}, u32[]{:S(2)}) collective-permute-start(bf16[256,128]{1,0:T(8,128)(2,1)S(1)} %collective-permute-done.7.refs_0_), channel_id=1, source_target_pairs={{0,8},{8,0},{16,24},{24,16},{1,9},{9,1},{17,25},{25,17},{2,10},{10... | collective-permute-start | bytes 196616 | tf_op jit(solution)/shard_map/ppermute | solution.py:17
  31.3 1.2 %collective-permute-done.9.refs_0_ = bf16[256,128]{1,0:T(8,128)(2,1)S(1)} collective-permute-done((bf16[256,128]{1,0:T(8,128)(2,1)S(1)}, bf16[256,128]{1,0:T(8,128)(2,1)S(1)}, u32[]{:S(2)}, u32[]{:S(2)}) %collective-permute-start.9) | collective-permute-done | bytes 65568 | tf_op jit(solution)/shard_map/ppermute | solution.py:17
  33.7 0.8 %collective-permute-done.10.got_ref = bf16[384,128]{1,0:T(8,128)(2,1)S(1)} collective-permute-done((bf16[384,128]{1,0:T(8,128)(2,1)S(1)}, bf16[384,128]{1,0:T(8,128)(2,1)S(1)}, u32[]{:S(2)}, u32[]{:S(2)}) %collective-permute-start.10) | collective-permute-done | bytes 98336 | tf_op jit(solution)/shard_map/ppermute | solution.py:17
  34.5 1.6 %collective-permute-start.14 = (bf16[384,128]{1,0:T(8,128)(2,1)S(1)}, bf16[384,128]{1,0:T(8,128)(2,1)S(1)}, u32[]{:S(2)}, u32[]{:S(2)}) collective-permute-start(bf16[384,128]{1,0:T(8,128)(2,1)S(1)} %shard_map.99.first_ref.sent_ref), channel_id=1, source_target_pairs={{0,6},{1,7},{2,4},{3,5},{4,2},{5,3},{6,0},{7,1},{8,14},{9,15},{10,... | collective-permute-start | bytes 294920 | tf_op jit(solution)/shard_map/ppermute | solution.py:17
  36.7 1.5 %collective-permute-start.12 = (bf16[384,128]{1,0:T(8,128)(2,1)S(1)}, bf16[384,128]{1,0:T(8,128)(2,1)S(1)}, u32[]{:S(2)}, u32[]{:S(2)}) collective-permute-start(bf16[384,128]{1,0:T(8,128)(2,1)S(1)} %get-tuple-element.53), channel_id=1, source_target_pairs={{0,2},{1,3},{2,0},{3,1},{4,6},{5,7},{6,4},{7,5},{8,10},{9,11},{10,... | collective-permute-start | bytes 294920 | tf_op jit(solution)/shard_map/ppermute | solution.py:17
  38.2 0.7 %shard_map.98 = bf16[1024,128]{1,0:T(8,128)(2,1)} custom-call(bf16[256,128]{1,0:T(8,128)(2,1)S(1)} %get-tuple-element.38.refs_0_, bf16[256,128]{1,0:T(8,128)(2,1)S(1)} %get-tuple-element.41.refs_1_, bf16[256,128]{1,0:T(8,128)(2,1)S(1)} %get-tuple-element.45.refs_2_, bf16[256,128]{1,0:T(8,128)(2,1)S(1)} %get-tuple-element.48.refs_3_), custom_call_target="tpu_custom_call" | custom-call | tf_op jit(solution)/shard_map/pallas_call | solution.py:301
  38.9 1.9 %collective-permute-done.14.got_ref = bf16[384,128]{1,0:T(8,128)(2,1)S(1)} collective-permute-done((bf16[384,128]{1,0:T(8,128)(2,1)S(1)}, bf16[384,128]{1,0:T(8,128)(2,1)S(1)}, u32[]{:S(2)}, u32[]{:S(2)}) %collective-permute-start.14) | collective-permute-done | bytes 98336 | tf_op jit(solution)/shard_map/ppermute | solution.py:17
  40.9 1.6 %collective-permute-done.13.refs_0_ = bf16[384,128]{1,0:T(8,128)(2,1)S(1)} collective-permute-done((bf16[384,128]{1,0:T(8,128)(2,1)S(1)}, bf16[384,128]{1,0:T(8,128)(2,1)S(1)}, u32[]{:S(2)}, u32[]{:S(2)}) %collective-permute-start.13) | collective-permute-done | bytes 98336 | tf_op jit(solution)/shard_map/ppermute | solution.py:17
  42.5 0.7 %shard_map.103 = (f32[256,128]{1,0:T(8,128)}, f32[128,128]{1,0:T(8,128)}) custom-call(f32[256,128]{1,0:T(8,128)S(1)} %get-tuple-element.52.own_ref, bf16[384,128]{1,0:T(8,128)(2,1)S(1)} %shard_map.99.first_ref.sent_ref, bf16[384,128]{1,0:T(8,128)(2,1)S(1)} %collective-permute-done.12.got_ref, f32[384,128]{1,0:T(8,128)S(1)} %shard_map.102.refs_0_), custom_call_target="tpu_custom_call" | custom-call | tf_op jit(solution)/shard_map/pallas_call | solution.py:310
  (39 shorter events, 5.5 us)
Async XLA Ops:
  0.6 6.7 %collective-permute-start.2 = (bf16[256,128]{1,0:T(8,128)(2,1)}, bf16[256,128]{1,0:T(8,128)(2,1)S(1)}, u32[]{:S(2)}, u32[]{:S(2)}) collective-permute-start(bf16[256,128]{1,0:T(8,128)(2,1)} %features_ref.1), channel_id=1, source_target_pairs={{0,6},{1,7},{2,4},{3,5},{4,2},{5,3},{6,0},{7,1},{8,14},{9,15},{10,... | collective-permute-start | bytes 196616 | tf_op jit(solution)/shard_map/ppermute | solution.py:17
  4.6 4.5 %collective-permute-start.1 = (bf16[256,128]{1,0:T(8,128)(2,1)}, bf16[256,128]{1,0:T(8,128)(2,1)S(1)}, u32[]{:S(2)}, u32[]{:S(2)}) collective-permute-start(bf16[256,128]{1,0:T(8,128)(2,1)} %features_ref.1), channel_id=1, source_target_pairs={{0,4},{1,5},{2,6},{3,7},{4,0},{5,1},{6,2},{7,3},{8,12},{9,13},{10,... | collective-permute-start | bytes 196616 | tf_op jit(solution)/shard_map/ppermute | solution.py:17
  5.1 4.5 %collective-permute-start = (bf16[256,128]{1,0:T(8,128)(2,1)}, bf16[256,128]{1,0:T(8,128)(2,1)S(1)}, u32[]{:S(2)}, u32[]{:S(2)}) collective-permute-start(bf16[256,128]{1,0:T(8,128)(2,1)} %features_ref.1), channel_id=1, source_target_pairs={{0,2},{1,3},{2,0},{3,1},{4,6},{5,7},{6,4},{7,5},{8,10},{9,11},{10,... | collective-permute-start | bytes 196616 | tf_op jit(solution)/shard_map/ppermute | solution.py:17
  5.2 1.0 %copy-start.1 = (bf16[8,2,128,128]{3,2,1,0:T(8,128)(2,1)S(1)}, bf16[8,2,128,128]{3,2,1,0:T(8,128)(2,1)}, u32[]{:S(2)}) copy-start(bf16[8,2,128,128]{3,2,1,0:T(8,128)(2,1)} %vals_ref.3) | copy-start | bytes 1572868
  6.3 0.8 %copy-start.4 = (bf16[256,128]{1,0:T(8,128)(2,1)S(1)}, bf16[256,128]{1,0:T(8,128)(2,1)}, u32[]{:S(2)}) copy-start(bf16[256,128]{1,0:T(8,128)(2,1)} %features_ref.1) | copy-start | bytes 196612
  7.3 3.9 %copy-start.2 = (bf16[8,2,128,128]{3,2,1,0:T(8,128)(2,1)S(1)}, bf16[8,2,128,128]{3,2,1,0:T(8,128)(2,1)}, u32[]{:S(2)}) copy-start(bf16[8,2,128,128]{3,2,1,0:T(8,128)(2,1)} %vals_ref.3) | copy-start | bytes 1572868
  9.6 0.7 %copy-start.6 = (s32[8,2]{0,1:T(2,128)S(1)}, s32[8,2]{0,1:T(2,128)}, u32[]{:S(2)}) copy-start(s32[8,2]{0,1:T(2,128)} %param.6) | copy-start | bytes 196
  9.6 1.6 %collective-permute-start.3 = (bf16[1024,128]{1,0:T(8,128)(2,1)S(1)}, bf16[1024,128]{1,0:T(8,128)(2,1)S(1)}, u32[]{:S(2)}, u32[]{:S(2)}) collective-permute-start(bf16[1024,128]{1,0:T(8,128)(2,1)S(1)} %shard_map.88._.mine_ref), channel_id=1, source_target_pairs={{0,1},{1,0},{2,3},{3,2},{4,5},{5,4},{6,7},{7,6},{8,9},{9,8},{10,11... | collective-permute-start | bytes 786440 | tf_op jit(solution)/shard_map/ppermute | solution.py:17
  11.6 4.3 %collective-permute-start.4 = (bf16[256,128]{1,0:T(8,128)(2,1)S(1)}, bf16[256,128]{1,0:T(8,128)(2,1)S(1)}, u32[]{:S(2)}, u32[]{:S(2)}) collective-permute-start(bf16[256,128]{1,0:T(8,128)(2,1)S(1)} %get-tuple-element.34), channel_id=1, source_target_pairs={{0,8},{8,0},{16,24},{24,16},{1,9},{9,1},{17,25},{25,17},{2,10},{10... | collective-permute-start | bytes 196616 | tf_op jit(solution)/shard_map/ppermute | solution.py:17
  15.9 5.3 %collective-permute-start.5 = (bf16[256,128]{1,0:T(8,128)(2,1)S(1)}, bf16[256,128]{1,0:T(8,128)(2,1)S(1)}, u32[]{:S(2)}, u32[]{:S(2)}) collective-permute-start(bf16[256,128]{1,0:T(8,128)(2,1)S(1)} %get-tuple-element.36), channel_id=1, source_target_pairs={{0,16},{8,24},{16,0},{24,8},{1,17},{9,25},{17,1},{25,9},{2,18},{10... | collective-permute-start | bytes 196616 | tf_op jit(solution)/shard_map/ppermute | solution.py:17
  18.6 4.3 %collective-permute-start.6 = (bf16[256,128]{1,0:T(8,128)(2,1)S(1)}, bf16[256,128]{1,0:T(8,128)(2,1)S(1)}, u32[]{:S(2)}, u32[]{:S(2)}) collective-permute-start(bf16[256,128]{1,0:T(8,128)(2,1)S(1)} %get-tuple-element.37), channel_id=1, source_target_pairs={{0,8},{8,0},{16,24},{24,16},{1,9},{9,1},{17,25},{25,17},{2,10},{10... | collective-permute-start | bytes 196616 | tf_op jit(solution)/shard_map/ppermute | solution.py:17
  21.3 2.7 %copy-start = (bf16[1024,128]{1,0:T(8,128)(2,1)S(1)}, bf16[1024,128]{1,0:T(8,128)(2,1)}, u32[]{:S(2)}) copy-start(bf16[1024,128]{1,0:T(8,128)(2,1)} %cotangent_ref.7) | copy-start | bytes 786436
  21.3 2.7 %copy-start.3 = (bf16[128,128]{1,0:T(8,128)(2,1)S(1)}, bf16[128,128]{1,0:T(8,128)(2,1)}, u32[]{:S(2)}) copy-start(bf16[128,128]{1,0:T(8,128)(2,1)} %weight_ref.7) | copy-start | bytes 98308
  22.9 1.1 %copy-start.5 = (f32[128]{0:T(128)S(1)}, f32[128]{0:T(128)}, u32[]{:S(2)}) copy-start(f32[128]{0:T(128)} %bias_ref.7) | copy-start | bytes 1540
  22.9 5.2 %collective-permute-start.7 = (bf16[256,128]{1,0:T(8,128)(2,1)S(1)}, bf16[256,128]{1,0:T(8,128)(2,1)S(1)}, u32[]{:S(2)}, u32[]{:S(2)}) collective-permute-start(bf16[256,128]{1,0:T(8,128)(2,1)S(1)} %shard_map.93.refs_0_), channel_id=1, source_target_pairs={{0,16},{8,24},{16,0},{24,8},{1,17},{9,25},{17,1},{25,9},{2,18},{10... | collective-permute-start | bytes 196616 | tf_op jit(solution)/shard_map/ppermute | solution.py:17
  24.5 6.3 %collective-permute-start.8 = (bf16[256,128]{1,0:T(8,128)(2,1)S(1)}, bf16[256,128]{1,0:T(8,128)(2,1)S(1)}, u32[]{:S(2)}, u32[]{:S(2)}) collective-permute-start(bf16[256,128]{1,0:T(8,128)(2,1)S(1)} %get-tuple-element.42), channel_id=1, source_target_pairs={{0,8},{8,0},{16,24},{24,16},{1,9},{9,1},{17,25},{25,17},{2,10},{10... | collective-permute-start | bytes 196616 | tf_op jit(solution)/shard_map/ppermute | solution.py:17
  28.1 4.4 %collective-permute-start.9 = (bf16[256,128]{1,0:T(8,128)(2,1)S(1)}, bf16[256,128]{1,0:T(8,128)(2,1)S(1)}, u32[]{:S(2)}, u32[]{:S(2)}) collective-permute-start(bf16[256,128]{1,0:T(8,128)(2,1)S(1)} %collective-permute-done.7.refs_0_), channel_id=1, source_target_pairs={{0,8},{8,0},{16,24},{24,16},{1,9},{9,1},{17,25},{25,17},{2,10},{10... | collective-permute-start | bytes 196616 | tf_op jit(solution)/shard_map/ppermute | solution.py:17
  33.1 1.4 %collective-permute-start.10 = (bf16[384,128]{1,0:T(8,128)(2,1)S(1)}, bf16[384,128]{1,0:T(8,128)(2,1)S(1)}, u32[]{:S(2)}, u32[]{:S(2)}) collective-permute-start(bf16[384,128]{1,0:T(8,128)(2,1)S(1)} %get-tuple-element.50.sent_ref), channel_id=1, source_target_pairs={{0,1},{1,0},{2,3},{3,2},{4,5},{5,4},{6,7},{7,6},{8,9},{9,8},{10,11... | collective-permute-start | bytes 294920 | tf_op jit(solution)/shard_map/ppermute | solution.py:17
  33.2 2.9 %collective-permute-start.11 = (bf16[768,128]{1,0:T(8,128)(2,1)S(1)}, bf16[768,128]{1,0:T(8,128)(2,1)S(1)}, u32[]{:S(2)}, u32[]{:S(2)}) collective-permute-start(bf16[768,128]{1,0:T(8,128)(2,1)S(1)} %get-tuple-element.51), channel_id=1, source_target_pairs={{0,1},{1,0},{2,3},{3,2},{4,5},{5,4},{6,7},{7,6},{8,9},{9,8},{10,11... | collective-permute-start | bytes 589832 | tf_op jit(solution)/shard_map/ppermute | solution.py:17
  34.5 6.3 %collective-permute-start.14 = (bf16[384,128]{1,0:T(8,128)(2,1)S(1)}, bf16[384,128]{1,0:T(8,128)(2,1)S(1)}, u32[]{:S(2)}, u32[]{:S(2)}) collective-permute-start(bf16[384,128]{1,0:T(8,128)(2,1)S(1)} %shard_map.99.first_ref.sent_ref), channel_id=1, source_target_pairs={{0,6},{1,7},{2,4},{3,5},{4,2},{5,3},{6,0},{7,1},{8,14},{9,15},{10,... | collective-permute-start | bytes 294920 | tf_op jit(solution)/shard_map/ppermute | solution.py:17
  36.1 6.3 %collective-permute-start.13 = (bf16[384,128]{1,0:T(8,128)(2,1)S(1)}, bf16[384,128]{1,0:T(8,128)(2,1)S(1)}, u32[]{:S(2)}, u32[]{:S(2)}) collective-permute-start(bf16[384,128]{1,0:T(8,128)(2,1)S(1)} %get-tuple-element.54), channel_id=1, source_target_pairs={{0,4},{1,5},{2,6},{3,7},{4,0},{5,1},{6,2},{7,3},{8,12},{9,13},{10,... | collective-permute-start | bytes 294920 | tf_op jit(solution)/shard_map/ppermute | solution.py:17
  36.7 5.8 %collective-permute-start.12 = (bf16[384,128]{1,0:T(8,128)(2,1)S(1)}, bf16[384,128]{1,0:T(8,128)(2,1)S(1)}, u32[]{:S(2)}, u32[]{:S(2)}) collective-permute-start(bf16[384,128]{1,0:T(8,128)(2,1)S(1)} %get-tuple-element.53), channel_id=1, source_target_pairs={{0,2},{1,3},{2,0},{3,1},{4,6},{5,7},{6,4},{7,5},{8,10},{9,11},{10,... | collective-permute-start | bytes 294920 | tf_op jit(solution)/shard_map/ppermute | solution.py:17

commit v10 on v7

--- a/solution.py
+++ b/solution.py
@@ -82,65 +82,46 @@
 
 
 def layer_kernel(
-    rep, count, own_blocks, j, place_ref, flipped_ref, cotangent_ref, weight_ref, bias_ref, *refs
+    rep, place_ref, flipped_ref, cotangent_ref, weight_ref, bias_ref, aggregated_ref,
+    output_ref, first_ref, rest_ref, keep_ref, contrib,
 ):
-    first, last = j == 0, j == 1
-    piece_ref, refs = refs[0], refs[1:]
-    if not first:
-        (contrib_in, sums_in), refs = refs[:2], refs[2:]
-    if last:
-        output_ref, first_ref, rest_ref, keep_ref, contrib = refs
-    else:
-        output_ref, contrib, sums_out = refs
-    rows, _, size = flipped_ref.shape
-    share = rows // rep
-    quarter_blocks = contrib.shape[0]
-    nodes = own_blocks * size
-    contrib[...] = jnp.zeros_like(contrib) if first else contrib_in[...]
-
-    target = lax.axis_index("rep") ^ j
-    aggregated = piece_ref[...]
-    part = aggregated.shape[0]
-    here = pl.ds(pl.multiple_of(target * part, part), part)
-    hidden = matmul(aggregated, weight_ref[...], (1, 0)) + bias_ref[...]
-    gate_prob = jax.nn.sigmoid(hidden)
-    output_ref[...] = (hidden * gate_prob).astype(BF16)
-    grad_hidden = (
-        cotangent_ref[here, :].astype(F32) * gate_prob * (1.0 + hidden * (1.0 - gate_prob))
-    ).astype(BF16)
-    part_sum = matmul(aggregated, grad_hidden, (0, 0))
-    grad_agg = matmul(grad_hidden, weight_ref[...], (1, 1)).astype(BF16)
-    for i in range(share):
-        row = target * share + i
-        terms = matmul(flipped_ref[row], grad_agg[i * size : (i + 1) * size], (1, 0))
-        for k in range(count):
-            contrib[place_ref[row * count + k, 0]] += terms[k * size : (k + 1) * size]
-    if first:
-        sums_out[0] = part_sum
-        sums_out[1] = jnp.zeros_like(part_sum)
-    elif not last:
-        sums_out[0] = sums_in[0]
-        sums_out[1] = sums_in[1] + part_sum
-    if not last:
-        return
-    half = quarter_blocks // 2
+    rows, length, size = flipped_ref.shape
+    count = length // size
+    chips, nodes, _ = keep_ref.shape
+    part = rows * size // rep
+    contrib[...] = jnp.zeros_like(contrib)
+    weight_part = None
+    for piece in range(rep):
+        here = slice(piece * part, (piece + 1) * part)
+        aggregated = aggregated_ref[here, :]
+        hidden = matmul(aggregated, weight_ref[...], (1, 0)) + bias_ref[...]
+        gate_prob = jax.nn.sigmoid(hidden)
+        output_ref[here, :] = (hidden * gate_prob).astype(BF16)
+        grad_hidden = (
+            cotangent_ref[here, :].astype(F32) * gate_prob * (1.0 + hidden * (1.0 - gate_prob))
+        ).astype(BF16)
+        part_sum = matmul(aggregated, grad_hidden, (0, 0))
+        weight_part = part_sum if piece == 0 else weight_part + part_sum
+        grad_agg = matmul(grad_hidden, weight_ref[...], (1, 1)).astype(BF16)
+        for i in range(part // size):
+            row = piece * (part // size) + i
+            terms = matmul(flipped_ref[row], grad_agg[i * size : (i + 1) * size], (1, 0))
+            for k in range(count):
+                contrib[place_ref[row * count + k, 0]] += terms[k * size : (k + 1) * size]
+    half = contrib.shape[0] // 2
     keep_ref[...] = contrib[:half].reshape(keep_ref.shape)
     away = contrib[half:].reshape(half * size, -1).astype(BF16)
     rest_ref[...] = away[:-nodes]
     first_ref[:nodes] = away[-nodes:]
-    first_ref[nodes:] = ((sums_in[0] + part_sum) + sums_in[1]).astype(BF16)
+    first_ref[nodes:] = weight_part.astype(BF16)
 
 
 def add_kernel(a_ref, b_ref, out_ref):
     out_ref[...] = (a_ref[...] + b_ref[...].astype(F32)).astype(out_ref.dtype)
 
 
-def order_kernel(order, *refs):
-    pieces, out_ref = refs[:-1], refs[-1]
-    part = pieces[0].shape[0]
-    for j, piece in zip(order, pieces):
-        target = lax.axis_index("rep") ^ j
-        out_ref[pl.ds(pl.multiple_of(target * part, part), part), :] = piece[...]
+def copy_kernel(value_ref, out_ref):
+    out_ref[...] = value_ref[...]
 
 
 def first_pair_kernel(keep_ref, sent_ref, got_ref, out_ref):
@@ -248,30 +229,19 @@
         own_rows = call(add_kernel, shape((part, width), F32 if j > 1 else BF16), [VMEM] * 2)(
             own_rows, arrived[j]
         )
-    pieces = {0: own_rows}
-    for j in order:
-        pieces[j] = swap(own_rows, "rep", j)
-
-    outputs, carried = [], []
-    for j, piece in pieces.items():
-        if j != 1:
-            outs = [shape((quarter_blocks, size, width), F32), shape((2, width, width), F32)]
-            scratch = []
-        else:
-            outs = [
-                shape((nodes + width, width), BF16),
-                shape(((chips - 1) * nodes, width), BF16),
-                shape((chips, nodes, width), F32),
-            ]
-            scratch = [pltpu.VMEM((quarter_blocks, size, width), F32)]
-        output, *carried = call(
-            functools.partial(layer_kernel, rep, count, own_blocks, j),
-            [shape((part, width), BF16)] + outs,
-            [VMEM] * (6 + len(carried)),
-            scratch,
-        )(place, flipped, cotangent, weight, bias, piece, *carried)
-        outputs.append(output)
-    first, rest, keep = carried
+    aggregated = lax.all_gather(own_rows, "rep", axis=0, tiled=True)
+
+    output, first, rest, keep = call(
+        functools.partial(layer_kernel, rep),
+        [
+            shape((rows * size, width), BF16),
+            shape((nodes + width, width), BF16),
+            shape(((chips - 1) * nodes, width), BF16),
+            shape((chips, nodes, width), F32),
+        ],
+        [VMEM] * 6,
+        [pltpu.VMEM((quarter_blocks, size, width), F32)],
+    )(place, flipped, cotangent, weight, bias.reshape(1, width), aggregated)
 
     message = shape((nodes + width, width), BF16)
     got_first, got_rest = swap(first, "dom", 1), swap(rest, "dom", 1)
@@ -281,9 +251,7 @@
     )(keep, sends[0], got_rest)
     sends = others + sends
     got = {chip: swap(sends[chip - 1], "dom", 2 * chip) for chip in range(chips - 1, 0, -1)}
-    output = call(
-        functools.partial(order_kernel, list(pieces)), shape((rows * size, width), BF16), [VMEM] * rep
-    )(*outputs)
+    output = call(copy_kernel, shape(output.shape, BF16), [VMEM])(output)
     levels = chips.bit_length() - 1
     total = shape(message.shape, F32)
     got[chips - 1] = call(lift_kernel, total, [VMEM], cost=1000000000)(got[chips - 1])

time: 41.7 us -> 47.8 us (1.15)
  blocking collectives: 0 us -> 14 us
  starting transfers between devices: 17.8 us -> 13.3 us
  waiting for transfers between devices: 15.9 us -> 12.4 us
  local copies, waits for them, and re-layouts: 2.5 us -> 3.14 us
  Pallas kernels: 4.46 us -> 3.88 us
    all_gather x0 -> x1, blocking collectives: none -> 14 us  [body(): aggregated = lax.all_gather(own_rows, 'rep', axis=0, tiled=True)]
    ppermute x15 -> x12, starting transfers between devices: 17.8 us -> 13.3 us  [swap(): return lax.ppermute(value, axis, [(i, i ^ distance) for i in range(size)])]
    ppermute x15 -> x12, waiting for transfers between devices: 15.9 us -> 12.4 us  [swap(): return lax.ppermute(value, axis, [(i, i ^ distance) for i in range(size)])]
    unnamed x14, local copies, waits for them, and re-layouts: 2.5 us -> 3.14 us
    pallas_call x5 -> x2, Pallas kernels: 2.87 us -> 2.28 us  [the longest x1 1.57 us: body(): call(functools.partial(layer_kernel, rep), [shape((rows * size, width), B...]
  transfers between devices with their start and end apart: 15 -> 12, of which waited for: 11 -> 9; matrix products, arithmetic and copies ran while one was open for 0% -> 0% of each run, Pallas kernels for 7% -> 3%
where the time goes in v10:
time: 47.8 us; the launch traced here: 47.5 us
  blocking collectives  14 us (29%)
  starting transfers between devices  13.3 us (28%)
  waiting for transfers between devices  12.4 us (26%)
  Pallas kernels  3.88 us (8%)
  local copies, waits for them, and re-layouts  3.14 us (7%)
  between operations  0.78 us (2%)
    all_gather x1, blocking collectives, body(): aggregated = lax.all_gather(own_rows, 'rep', axis=0, tiled=True)  14 us
    ppermute x12, starting transfers between devices, swap(): return lax.ppermute(value, axis, [(i, i ^ distance) for i in range(size)])  13.3 us
    ppermute x12, waiting for transfers between devices, swap(): return lax.ppermute(value, axis, [(i, i ^ distance) for i in range(size)])  12.4 us
    unnamed x14, local copies, waits for them, and re-layouts  3.14 us
    pallas_call x1, Pallas kernels, body(): call(functools.partial(layer_kernel, rep), [shape((rows * size, width), B...  1.57 us
  transfers between devices with their start and end apart: 12, of which 9 were waited for; matrix products, arithmetic and copies ran while one was open for 0% of the time, Pallas kernels for 3%

profile of v10, /device:TPU:0, one launch (start us, length us, event | category | flops | bytes accessed | tf_op | source)
XLA Modules:
  0.0 47.5 jit_solution(12810386800469523721)
XLA Ops:
  0.6 4.0 %collective-permute-start.2 = (bf16[256,128]{1,0:T(8,128)(2,1)}, bf16[256,128]{1,0:T(8,128)(2,1)S(1)}, u32[]{:S(2)}, u32[]{:S(2)}) collective-permute-start(bf16[256,128]{1,0:T(8,128)(2,1)} %features_ref.1), channel_id=1, source_target_pairs={{0,6},{1,7},{2,4},{3,5},{4,2},{5,3},{6,0},{7,1},{8,14},{9,15},{10,... | collective-permute-start | bytes 196616 | tf_op jit(solution)/shard_map/ppermute | solution.py:17
  4.6 0.5 %collective-permute-start.1 = (bf16[256,128]{1,0:T(8,128)(2,1)}, bf16[256,128]{1,0:T(8,128)(2,1)S(1)}, u32[]{:S(2)}, u32[]{:S(2)}) collective-permute-start(bf16[256,128]{1,0:T(8,128)(2,1)} %features_ref.1), channel_id=1, source_target_pairs={{0,4},{1,5},{2,6},{3,7},{4,0},{5,1},{6,2},{7,3},{8,12},{9,13},{10,... | collective-permute-start | bytes 196616 | tf_op jit(solution)/shard_map/ppermute | solution.py:17
  5.2 1.0 %copy-done = bf16[8,2,128,128]{3,2,1,0:T(8,128)(2,1)S(1)} copy-done((bf16[8,2,128,128]{3,2,1,0:T(8,128)(2,1)S(1)}, bf16[8,2,128,128]{3,2,1,0:T(8,128)(2,1)}, u32[]{:S(2)}) %copy-start) | copy-done | bytes 524312
  6.3 0.8 %copy-done.3 = bf16[256,128]{1,0:T(8,128)(2,1)S(1)} copy-done((bf16[256,128]{1,0:T(8,128)(2,1)S(1)}, bf16[256,128]{1,0:T(8,128)(2,1)}, u32[]{:S(2)}) %copy-start.3) | copy-done | bytes 65560
  7.3 1.7 %collective-permute-done.1.refs_0_ = bf16[256,128]{1,0:T(8,128)(2,1)S(1)} collective-permute-done((bf16[256,128]{1,0:T(8,128)(2,1)}, bf16[256,128]{1,0:T(8,128)(2,1)S(1)}, u32[]{:S(2)}, u32[]{:S(2)}) %collective-permute-start.1) | collective-permute-done | bytes 65568 | tf_op jit(solution)/shard_map/ppermute | solution.py:17
  9.1 0.5 %collective-permute-done.refs_0_ = bf16[256,128]{1,0:T(8,128)(2,1)S(1)} collective-permute-done((bf16[256,128]{1,0:T(8,128)(2,1)}, bf16[256,128]{1,0:T(8,128)(2,1)S(1)}, u32[]{:S(2)}, u32[]{:S(2)}) %collective-permute-start) | collective-permute-done | bytes 65568 | tf_op jit(solution)/shard_map/ppermute | solution.py:17
  9.7 0.6 %copy-done.5 = s32[8,2]{0,1:T(2,128)S(1)} copy-done((s32[8,2]{0,1:T(2,128)S(1)}, s32[8,2]{0,1:T(2,128)}, u32[]{:S(2)}) %copy-start.5) | copy-done | bytes 88
  10.5 0.8 %collective-permute-done.3.far_ref = bf16[1024,128]{1,0:T(8,128)(2,1)S(1)} collective-permute-done((bf16[1024,128]{1,0:T(8,128)(2,1)S(1)}, bf16[1024,128]{1,0:T(8,128)(2,1)S(1)}, u32[]{:S(2)}, u32[]{:S(2)}) %collective-permute-start.3) | collective-permute-done | bytes 262176 | tf_op jit(solution)/shard_map/ppermute | solution.py:17
  11.6 3.7 %collective-permute-start.4 = (bf16[256,128]{1,0:T(8,128)(2,1)S(1)}, bf16[256,128]{1,0:T(8,128)(2,1)S(1)}, u32[]{:S(2)}, u32[]{:S(2)}) collective-permute-start(bf16[256,128]{1,0:T(8,128)(2,1)S(1)} %get-tuple-element.21), channel_id=1, source_target_pairs={{0,24},{8,16},{16,8},{24,0},{1,25},{9,17},{17,9},{25,1},{2,26},{10... | collective-permute-start | bytes 196616 | tf_op jit(solution)/shard_map/ppermute | solution.py:17
  15.2 0.8 %collective-permute-start.6 = (bf16[256,128]{1,0:T(8,128)(2,1)S(1)}, bf16[256,128]{1,0:T(8,128)(2,1)S(1)}, u32[]{:S(2)}, u32[]{:S(2)}) collective-permute-start(bf16[256,128]{1,0:T(8,128)(2,1)S(1)} %get-tuple-element.23), channel_id=1, source_target_pairs={{0,8},{8,0},{16,24},{24,16},{1,9},{9,1},{17,25},{25,17},{2,10},{10... | collective-permute-start | bytes 196616 | tf_op jit(solution)/shard_map/ppermute | solution.py:17
  16.0 1.9 %collective-permute-done.4.b_ref = bf16[256,128]{1,0:T(8,128)(2,1)S(1)} collective-permute-done((bf16[256,128]{1,0:T(8,128)(2,1)S(1)}, bf16[256,128]{1,0:T(8,128)(2,1)S(1)}, u32[]{:S(2)}, u32[]{:S(2)}) %collective-permute-start.4) | collective-permute-done | bytes 65568 | tf_op jit(solution)/shard_map/ppermute | solution.py:17
  18.0 3.2 %collective-permute-done.5.b_ref = bf16[256,128]{1,0:T(8,128)(2,1)S(1)} collective-permute-done((bf16[256,128]{1,0:T(8,128)(2,1)S(1)}, bf16[256,128]{1,0:T(8,128)(2,1)S(1)}, u32[]{:S(2)}, u32[]{:S(2)}) %collective-permute-start.5) | collective-permute-done | bytes 65568 | tf_op jit(solution)/shard_map/ppermute | solution.py:17
  21.2 14.0 %all_gather.3.aggregated_ref = bf16[1024,128]{1,0:T(8,128)(2,1)S(1)} all-gather(bf16[256,128]{1,0:T(8,128)(2,1)S(1)} %shard_map.93), channel_id=1, replica_groups=mesh['rep'=4,'dom'=8] {'rep'}, dimensions={0}, use_global_device_ids=true | all-gather | bytes 327680 | tf_op jit(solution)/shard_map/all_gather | solution.py:232
  35.2 0.6 %copy-done.6 = f32[128]{0:T(128)S(1)} copy-done((f32[128]{0:T(128)S(1)}, f32[128]{0:T(128)}, u32[]{:S(2)}) %copy-start.6) | copy-done | bytes 536
  35.8 1.6 %shard_map.94 = (bf16[1024,128]{1,0:T(8,128)(2,1)S(1)}, bf16[384,128]{1,0:T(8,128)(2,1)S(1)}, bf16[768,128]{1,0:T(8,128)(2,1)S(1)}, f32[4,256,128]{2,1,0:T(8,128)S(1)}) custom-call(s32[16,128]{1,0:T(8,128)S(1)} %shard_map.89.place_ref, bf16[8,256,128]{2,1,0:T(8,128)(2,1)S(1)} %get-tuple-element.19.flipped_ref, bf16[1024,128]{1,0:T(8,128)(2,1)S(1)} %copy-done.2, ...), custom_call_target="tpu_custom_call" | custom-call | tf_op jit(solution)/shard_map/pallas_call | solution.py:234
  37.5 0.5 %collective-permute-start.8 = (bf16[768,128]{1,0:T(8,128)(2,1)S(1)}, bf16[768,128]{1,0:T(8,128)(2,1)S(1)}, u32[]{:S(2)}, u32[]{:S(2)}) collective-permute-start(bf16[768,128]{1,0:T(8,128)(2,1)S(1)} %get-tuple-element.27), channel_id=1, source_target_pairs={{0,1},{1,0},{2,3},{3,2},{4,5},{5,4},{6,7},{7,6},{8,9},{9,8},{10,11... | collective-permute-start | bytes 589832 | tf_op jit(solution)/shard_map/ppermute | solution.py:17
  38.0 0.8 %collective-permute-done.7.got_ref = bf16[384,128]{1,0:T(8,128)(2,1)S(1)} collective-permute-done((bf16[384,128]{1,0:T(8,128)(2,1)S(1)}, bf16[384,128]{1,0:T(8,128)(2,1)S(1)}, u32[]{:S(2)}, u32[]{:S(2)}) %collective-permute-start.7) | collective-permute-done | bytes 98336 | tf_op jit(solution)/shard_map/ppermute | solution.py:17
  38.8 1.6 %collective-permute-start.11 = (bf16[384,128]{1,0:T(8,128)(2,1)S(1)}, bf16[384,128]{1,0:T(8,128)(2,1)S(1)}, u32[]{:S(2)}, u32[]{:S(2)}) collective-permute-start(bf16[384,128]{1,0:T(8,128)(2,1)S(1)} %shard_map.96.first_ref.sent_ref), channel_id=1, source_target_pairs={{0,6},{1,7},{2,4},{3,5},{4,2},{5,3},{6,0},{7,1},{8,14},{9,15},{10,... | collective-permute-start | bytes 294920 | tf_op jit(solution)/shard_map/ppermute | solution.py:17
  40.4 0.5 %collective-permute-start.10 = (bf16[384,128]{1,0:T(8,128)(2,1)S(1)}, bf16[384,128]{1,0:T(8,128)(2,1)S(1)}, u32[]{:S(2)}, u32[]{:S(2)}) collective-permute-start(bf16[384,128]{1,0:T(8,128)(2,1)S(1)} %get-tuple-element.30), channel_id=1, source_target_pairs={{0,4},{1,5},{2,6},{3,7},{4,0},{5,1},{6,2},{7,3},{8,12},{9,13},{10,... | collective-permute-start | bytes 294920 | tf_op jit(solution)/shard_map/ppermute | solution.py:17
  41.0 1.5 %collective-permute-start.9 = (bf16[384,128]{1,0:T(8,128)(2,1)S(1)}, bf16[384,128]{1,0:T(8,128)(2,1)S(1)}, u32[]{:S(2)}, u32[]{:S(2)}) collective-permute-start(bf16[384,128]{1,0:T(8,128)(2,1)S(1)} %get-tuple-element.29), channel_id=1, source_target_pairs={{0,2},{1,3},{2,0},{3,1},{4,6},{5,7},{6,4},{7,5},{8,10},{9,11},{10,... | collective-permute-start | bytes 294920 | tf_op jit(solution)/shard_map/ppermute | solution.py:17
  42.5 0.7 %shard_map.95 = bf16[1024,128]{1,0:T(8,128)(2,1)} custom-call(bf16[1024,128]{1,0:T(8,128)(2,1)S(1)} %get-tuple-element.24.value_ref), custom_call_target="tpu_custom_call" | custom-call | tf_op jit(solution)/shard_map/pallas_call | solution.py:254
  43.2 1.9 %collective-permute-done.11.got_ref = bf16[384,128]{1,0:T(8,128)(2,1)S(1)} collective-permute-done((bf16[384,128]{1,0:T(8,128)(2,1)S(1)}, bf16[384,128]{1,0:T(8,128)(2,1)S(1)}, u32[]{:S(2)}, u32[]{:S(2)}) %collective-permute-start.11) | collective-permute-done | bytes 98336 | tf_op jit(solution)/shard_map/ppermute | solution.py:17
  45.1 1.6 %collective-permute-done.10.refs_0_ = bf16[384,128]{1,0:T(8,128)(2,1)S(1)} collective-permute-done((bf16[384,128]{1,0:T(8,128)(2,1)S(1)}, bf16[384,128]{1,0:T(8,128)(2,1)S(1)}, u32[]{:S(2)}, u32[]{:S(2)}) %collective-permute-start.10) | collective-permute-done | bytes 98336 | tf_op jit(solution)/shard_map/ppermute | solution.py:17
  46.8 0.7 %shard_map.100 = (f32[256,128]{1,0:T(8,128)}, f32[128,128]{1,0:T(8,128)}) custom-call(f32[256,128]{1,0:T(8,128)S(1)} %get-tuple-element.28.own_ref, bf16[384,128]{1,0:T(8,128)(2,1)S(1)} %shard_map.96.first_ref.sent_ref, bf16[384,128]{1,0:T(8,128)(2,1)S(1)} %collective-permute-done.9.got_ref, f32[384,128]{1,0:T(8,128)S(1)} %shard_map.99.refs_0_), custom_call_target="tpu_custom_call" | custom-call | tf_op jit(solution)/shard_map/pallas_call | solution.py:261
  (31 shorter events, 1.3 us)
Async XLA Ops:
  0.6 6.7 %collective-permute-start.2 = (bf16[256,128]{1,0:T(8,128)(2,1)}, bf16[256,128]{1,0:T(8,128)(2,1)S(1)}, u32[]{:S(2)}, u32[]{:S(2)}) collective-permute-start(bf16[256,128]{1,0:T(8,128)(2,1)} %features_ref.1), channel_id=1, source_target_pairs={{0,6},{1,7},{2,4},{3,5},{4,2},{5,3},{6,0},{7,1},{8,14},{9,15},{10,... | collective-permute-start | bytes 196616 | tf_op jit(solution)/shard_map/ppermute | solution.py:17
  4.6 4.5 %collective-permute-start.1 = (bf16[256,128]{1,0:T(8,128)(2,1)}, bf16[256,128]{1,0:T(8,128)(2,1)S(1)}, u32[]{:S(2)}, u32[]{:S(2)}) collective-permute-start(bf16[256,128]{1,0:T(8,128)(2,1)} %features_ref.1), channel_id=1, source_target_pairs={{0,4},{1,5},{2,6},{3,7},{4,0},{5,1},{6,2},{7,3},{8,12},{9,13},{10,... | collective-permute-start | bytes 196616 | tf_op jit(solution)/shard_map/ppermute | solution.py:17
  5.1 4.5 %collective-permute-start = (bf16[256,128]{1,0:T(8,128)(2,1)}, bf16[256,128]{1,0:T(8,128)(2,1)S(1)}, u32[]{:S(2)}, u32[]{:S(2)}) collective-permute-start(bf16[256,128]{1,0:T(8,128)(2,1)} %features_ref.1), channel_id=1, source_target_pairs={{0,2},{1,3},{2,0},{3,1},{4,6},{5,7},{6,4},{7,5},{8,10},{9,11},{10,... | collective-permute-start | bytes 196616 | tf_op jit(solution)/shard_map/ppermute | solution.py:17
  5.2 1.0 %copy-start = (bf16[8,2,128,128]{3,2,1,0:T(8,128)(2,1)S(1)}, bf16[8,2,128,128]{3,2,1,0:T(8,128)(2,1)}, u32[]{:S(2)}) copy-start(bf16[8,2,128,128]{3,2,1,0:T(8,128)(2,1)} %vals_ref.3) | copy-start | bytes 1572868
  6.3 0.8 %copy-start.3 = (bf16[256,128]{1,0:T(8,128)(2,1)S(1)}, bf16[256,128]{1,0:T(8,128)(2,1)}, u32[]{:S(2)}) copy-start(bf16[256,128]{1,0:T(8,128)(2,1)} %features_ref.1) | copy-start | bytes 196612
  7.3 3.9 %copy-start.1 = (bf16[8,2,128,128]{3,2,1,0:T(8,128)(2,1)S(1)}, bf16[8,2,128,128]{3,2,1,0:T(8,128)(2,1)}, u32[]{:S(2)}) copy-start(bf16[8,2,128,128]{3,2,1,0:T(8,128)(2,1)} %vals_ref.3) | copy-start | bytes 1572868
  9.6 0.7 %copy-start.5 = (s32[8,2]{0,1:T(2,128)S(1)}, s32[8,2]{0,1:T(2,128)}, u32[]{:S(2)}) copy-start(s32[8,2]{0,1:T(2,128)} %param.6) | copy-start | bytes 196
  9.6 1.6 %collective-permute-start.3 = (bf16[1024,128]{1,0:T(8,128)(2,1)S(1)}, bf16[1024,128]{1,0:T(8,128)(2,1)S(1)}, u32[]{:S(2)}, u32[]{:S(2)}) collective-permute-start(bf16[1024,128]{1,0:T(8,128)(2,1)S(1)} %shard_map.88._.mine_ref), channel_id=1, source_target_pairs={{0,1},{1,0},{2,3},{3,2},{4,5},{5,4},{6,7},{7,6},{8,9},{9,8},{10,11... | collective-permute-start | bytes 786440 | tf_op jit(solution)/shard_map/ppermute | solution.py:17
  11.6 6.4 %collective-permute-start.4 = (bf16[256,128]{1,0:T(8,128)(2,1)S(1)}, bf16[256,128]{1,0:T(8,128)(2,1)S(1)}, u32[]{:S(2)}, u32[]{:S(2)}) collective-permute-start(bf16[256,128]{1,0:T(8,128)(2,1)S(1)} %get-tuple-element.21), channel_id=1, source_target_pairs={{0,24},{8,16},{16,8},{24,0},{1,25},{9,17},{17,9},{25,1},{2,26},{10... | collective-permute-start | bytes 196616 | tf_op jit(solution)/shard_map/ppermute | solution.py:17
  15.2 5.9 %collective-permute-start.5 = (bf16[256,128]{1,0:T(8,128)(2,1)S(1)}, bf16[256,128]{1,0:T(8,128)(2,1)S(1)}, u32[]{:S(2)}, u32[]{:S(2)}) collective-permute-start(bf16[256,128]{1,0:T(8,128)(2,1)S(1)} %get-tuple-element.22), channel_id=1, source_target_pairs={{0,16},{8,24},{16,0},{24,8},{1,17},{9,25},{17,1},{25,9},{2,18},{10... | collective-permute-start | bytes 196616 | tf_op jit(solution)/shard_map/ppermute | solution.py:17
  15.2 5.9 %collective-permute-start.6 = (bf16[256,128]{1,0:T(8,128)(2,1)S(1)}, bf16[256,128]{1,0:T(8,128)(2,1)S(1)}, u32[]{:S(2)}, u32[]{:S(2)}) collective-permute-start(bf16[256,128]{1,0:T(8,128)(2,1)S(1)} %get-tuple-element.23), channel_id=1, source_target_pairs={{0,8},{8,0},{16,24},{24,16},{1,9},{9,1},{17,25},{25,17},{2,10},{10... | collective-permute-start | bytes 196616 | tf_op jit(solution)/shard_map/ppermute | solution.py:17
  21.1 14.0 %copy-start.2 = (bf16[1024,128]{1,0:T(8,128)(2,1)S(1)}, bf16[1024,128]{1,0:T(8,128)(2,1)}, u32[]{:S(2)}) copy-start(bf16[1024,128]{1,0:T(8,128)(2,1)} %cotangent_ref.1) | copy-start | bytes 786436
  21.2 14.0 %copy-start.4 = (bf16[128,128]{1,0:T(8,128)(2,1)S(1)}, bf16[128,128]{1,0:T(8,128)(2,1)}, u32[]{:S(2)}) copy-start(bf16[128,128]{1,0:T(8,128)(2,1)} %weight_ref.1) | copy-start | bytes 98308
  35.2 0.7 %copy-start.6 = (f32[128]{0:T(128)S(1)}, f32[128]{0:T(128)}, u32[]{:S(2)}) copy-start(f32[128]{0:T(128)} %param.10) | copy-start | bytes 1540
  37.4 1.4 %collective-permute-start.7 = (bf16[384,128]{1,0:T(8,128)(2,1)S(1)}, bf16[384,128]{1,0:T(8,128)(2,1)S(1)}, u32[]{:S(2)}, u32[]{:S(2)}) collective-permute-start(bf16[384,128]{1,0:T(8,128)(2,1)S(1)} %get-tuple-element.26.sent_ref), channel_id=1, source_target_pairs={{0,1},{1,0},{2,3},{3,2},{4,5},{5,4},{6,7},{7,6},{8,9},{9,8},{10,11... | collective-permute-start | bytes 294920 | tf_op jit(solution)/shard_map/ppermute | solution.py:17
  37.5 2.9 %collective-permute-start.8 = (bf16[768,128]{1,0:T(8,128)(2,1)S(1)}, bf16[768,128]{1,0:T(8,128)(2,1)S(1)}, u32[]{:S(2)}, u32[]{:S(2)}) collective-permute-start(bf16[768,128]{1,0:T(8,128)(2,1)S(1)} %get-tuple-element.27), channel_id=1, source_target_pairs={{0,1},{1,0},{2,3},{3,2},{4,5},{5,4},{6,7},{7,6},{8,9},{9,8},{10,11... | collective-permute-start | bytes 589832 | tf_op jit(solution)/shard_map/ppermute | solution.py:17
  38.8 6.3 %collective-permute-start.11 = (bf16[384,128]{1,0:T(8,128)(2,1)S(1)}, bf16[384,128]{1,0:T(8,128)(2,1)S(1)}, u32[]{:S(2)}, u32[]{:S(2)}) collective-permute-start(bf16[384,128]{1,0:T(8,128)(2,1)S(1)} %shard_map.96.first_ref.sent_ref), channel_id=1, source_target_pairs={{0,6},{1,7},{2,4},{3,5},{4,2},{5,3},{6,0},{7,1},{8,14},{9,15},{10,... | collective-permute-start | bytes 294920 | tf_op jit(solution)/shard_map/ppermute | solution.py:17
  40.4 6.3 %collective-permute-start.10 = (bf16[384,128]{1,0:T(8,128)(2,1)S(1)}, bf16[384,128]{1,0:T(8,128)(2,1)S(1)}, u32[]{:S(2)}, u32[]{:S(2)}) collective-permute-start(bf16[384,128]{1,0:T(8,128)(2,1)S(1)} %get-tuple-element.30), channel_id=1, source_target_pairs={{0,4},{1,5},{2,6},{3,7},{4,0},{5,1},{6,2},{7,3},{8,12},{9,13},{10,... | collective-permute-start | bytes 294920 | tf_op jit(solution)/shard_map/ppermute | solution.py:17
  41.0 5.9 %collective-permute-start.9 = (bf16[384,128]{1,0:T(8,128)(2,1)S(1)}, bf16[384,128]{1,0:T(8,128)(2,1)S(1)}, u32[]{:S(2)}, u32[]{:S(2)}) collective-permute-start(bf16[384,128]{1,0:T(8,128)(2,1)S(1)} %get-tuple-element.29), channel_id=1, source_target_pairs={{0,2},{1,3},{2,0},{3,1},{4,6},{5,7},{6,4},{7,5},{8,10},{9,11},{10,... | collective-permute-start | bytes 294920 | tf_op jit(solution)/shard_map/ppermute | solution.py:17

commit v11 on v7

--- a/solution.py
+++ b/solution.py
@@ -87,16 +87,14 @@
     first, last = j == 0, j == 1
     piece_ref, refs = refs[0], refs[1:]
     if not first:
-        (contrib_in, sums_in), refs = refs[:2], refs[2:]
-    if last:
-        output_ref, first_ref, rest_ref, keep_ref, contrib = refs
-    else:
-        output_ref, contrib, sums_out = refs
+        (_, sums_in), refs = refs[:2], refs[2:]
+    output_ref, contrib, *refs = refs
     rows, _, size = flipped_ref.shape
     share = rows // rep
     quarter_blocks = contrib.shape[0]
     nodes = own_blocks * size
-    contrib[...] = jnp.zeros_like(contrib) if first else contrib_in[...]
+    if first:
+        contrib[...] = jnp.zeros_like(contrib)
 
     target = lax.axis_index("rep") ^ j
     aggregated = piece_ref[...]
@@ -116,19 +114,17 @@
         for k in range(count):
             contrib[place_ref[row * count + k, 0]] += terms[k * size : (k + 1) * size]
     if first:
-        sums_out[0] = part_sum
-        sums_out[1] = jnp.zeros_like(part_sum)
+        refs[0][0] = part_sum
+        refs[0][1] = jnp.zeros_like(part_sum)
     elif not last:
-        sums_out[0] = sums_in[0]
-        sums_out[1] = sums_in[1] + part_sum
-    if not last:
-        return
-    half = quarter_blocks // 2
-    keep_ref[...] = contrib[:half].reshape(keep_ref.shape)
-    away = contrib[half:].reshape(half * size, -1).astype(BF16)
-    rest_ref[...] = away[:-nodes]
-    first_ref[:nodes] = away[-nodes:]
-    first_ref[nodes:] = ((sums_in[0] + part_sum) + sums_in[1]).astype(BF16)
+        refs[0][0] = sums_in[0]
+        refs[0][1] = sums_in[1] + part_sum
+    else:
+        first_ref, rest_ref = refs
+        away = contrib[quarter_blocks // 2 :].reshape(quarter_blocks // 2 * size, -1).astype(BF16)
+        rest_ref[...] = away[:-nodes]
+        first_ref[:nodes] = away[-nodes:]
+        first_ref[nodes:] = ((sums_in[0] + part_sum) + sums_in[1]).astype(BF16)
 
 
 def add_kernel(a_ref, b_ref, out_ref):
@@ -143,19 +139,24 @@
         out_ref[pl.ds(pl.multiple_of(target * part, part), part), :] = piece[...]
 
 
-def first_pair_kernel(keep_ref, sent_ref, got_ref, out_ref):
-    chips, nodes, _ = keep_ref.shape
-    out_ref[:nodes] = (keep_ref[chips - 1] + got_ref[:nodes].astype(F32)).astype(BF16)
+def first_pair_kernel(contrib_ref, sent_ref, got_ref, out_ref):
+    blocks, size, _ = contrib_ref.shape
+    nodes = out_ref.shape[0] - sent_ref.shape[1]
+    last = contrib_ref[blocks // 2 - nodes // size : blocks // 2].reshape(nodes, -1)
+    out_ref[:nodes] = (last + got_ref[:nodes].astype(F32)).astype(BF16)
     out_ref[nodes:] = (sent_ref[nodes:].astype(F32) + got_ref[nodes:].astype(F32)).astype(BF16)
 
 
-def rest_pair_kernel(keep_ref, first_ref, got_ref, own_ref, *outs):
-    chips, nodes, _ = keep_ref.shape
-    own_ref[...] = keep_ref[0] + got_ref[:nodes].astype(F32)
-    for chip in range(1, chips - 1):
-        total = keep_ref[chip] + got_ref[chip * nodes : (chip + 1) * nodes].astype(F32)
-        outs[chip - 1][:nodes] = total.astype(BF16)
-        outs[chip - 1][nodes:] = first_ref[nodes:]
+def rest_pair_kernel(contrib_ref, first_ref, got_ref, own_ref, *outs):
+    size, nodes = contrib_ref.shape[1], own_ref.shape[0]
+    for chip in range(len(outs) + 1):
+        mine = contrib_ref[chip * nodes // size : (chip + 1) * nodes // size].reshape(nodes, -1)
+        total = mine + got_ref[chip * nodes : (chip + 1) * nodes].astype(F32)
+        if chip == 0:
+            own_ref[...] = total
+        else:
+            outs[chip - 1][:nodes] = total.astype(BF16)
+            outs[chip - 1][nodes:] = first_ref[nodes:]
 
 
 def total_of(values):
@@ -201,14 +202,14 @@
     part = rows * size // rep
     params = pltpu.CompilerParams(vmem_limit_bytes=(8 + dom // 2) * 1024 * 1024)
 
-    def call(kernel, out_shape, in_specs, scratch=(), cost=0):
+    def call(kernel, out_shape, in_specs, aliases={}, cost=0):
         single = not isinstance(out_shape, list)
         return pl.pallas_call(
             kernel,
             out_shape=out_shape,
             in_specs=in_specs,
             out_specs=VMEM if single else [VMEM] * len(out_shape),
-            scratch_shapes=scratch,
+            input_output_aliases=aliases,
             compiler_params=params,
             cost_estimate=pl.CostEstimate(flops=cost, bytes_accessed=0, transcendentals=0),
         )
@@ -242,7 +243,7 @@
         [VMEM] * 4,
     )(place, vals, mine, far)
     arrived = {j: swap(partials[j], "rep", j) if j else partials[j] for j in range(rep)}
-    order = range(rep - 1, 0, -1)
+    order = [*range(2, rep), 1]
     own_rows = arrived[0]
     for j in order:
         own_rows = call(add_kernel, shape((part, width), F32 if j > 1 else BF16), [VMEM] * 2)(
@@ -254,31 +255,29 @@
 
     outputs, carried = [], []
     for j, piece in pieces.items():
+        outs = [shape((part, width), BF16), shape((quarter_blocks, size, width), F32)]
         if j != 1:
-            outs = [shape((quarter_blocks, size, width), F32), shape((2, width, width), F32)]
-            scratch = []
+            outs += [shape((2, width, width), F32)]
         else:
-            outs = [
+            outs += [
                 shape((nodes + width, width), BF16),
                 shape(((chips - 1) * nodes, width), BF16),
-                shape((chips, nodes, width), F32),
             ]
-            scratch = [pltpu.VMEM((quarter_blocks, size, width), F32)]
         output, *carried = call(
             functools.partial(layer_kernel, rep, count, own_blocks, j),
-            [shape((part, width), BF16)] + outs,
+            outs,
             [VMEM] * (6 + len(carried)),
-            scratch,
-        )(place, flipped, cotangent, weight, bias, piece, *carried)
+            aliases={6: 1} if carried else {},
+        )(place, flipped, cotangent, weight, bias.reshape(1, width), piece, *carried)
         outputs.append(output)
-    first, rest, keep = carried
+    contrib, first, rest = carried
 
     message = shape((nodes + width, width), BF16)
     got_first, got_rest = swap(first, "dom", 1), swap(rest, "dom", 1)
-    sends = [call(first_pair_kernel, message, [VMEM] * 3, cost=5000000000)(keep, first, got_first)]
+    sends = [call(first_pair_kernel, message, [VMEM] * 3, cost=5000000000)(contrib, first, got_first)]
     own, *others = call(
         rest_pair_kernel, [shape((nodes, width), F32)] + [message] * (chips - 2), [VMEM] * 3, cost=1000000000
-    )(keep, sends[0], got_rest)
+    )(contrib, sends[0], got_rest)
     sends = others + sends
     got = {chip: swap(sends[chip - 1], "dom", 2 * chip) for chip in range(chips - 1, 0, -1)}
     output = call(

time: 41.7 us -> 41.4 us (level)
  starting transfers between devices: 17.8 us -> 16.9 us
  local copies, waits for them, and re-layouts: 2.5 us -> 3.14 us
    ppermute x15, starting transfers between devices: 17.8 us -> 16.9 us  [swap(): return lax.ppermute(value, axis, [(i, i ^ distance) for i in range(size)])]
    unnamed x14, local copies, waits for them, and re-layouts: 2.5 us -> 3.14 us
  transfers between devices with their start and end apart: 15 -> 15, of which waited for: 11 -> 12; matrix products, arithmetic and copies ran while one was open for 0% -> 0% of each run, Pallas kernels for 7% -> 7%
where the time goes in v11:
time: 41.4 us; the launch traced here: 41.2 us
  starting transfers between devices  16.9 us (41%)
  waiting for transfers between devices  15.9 us (38%)
  Pallas kernels  4.43 us (11%)
  local copies, waits for them, and re-layouts  3.14 us (8%)
  between operations  0.8 us (2%)
    ppermute x15, starting transfers between devices, swap(): return lax.ppermute(value, axis, [(i, i ^ distance) for i in range(size)])  16.9 us
    ppermute x15, waiting for transfers between devices, swap(): return lax.ppermute(value, axis, [(i, i ^ distance) for i in range(size)])  15.9 us
    unnamed x14, local copies, waits for them, and re-layouts  3.14 us
    pallas_call x4, Pallas kernels, body(): call(functools.partial(layer_kernel, rep, count, own_blocks, j), outs, [V...  2.11 us
  transfers between devices with their start and end apart: 15, of which 12 were waited for; matrix products, arithmetic and copies ran while one was open for 0% of the time, Pallas kernels for 7%

profile of v11, /device:TPU:0, one launch (start us, length us, event | category | flops | bytes accessed | tf_op | source)
XLA Modules:
  0.0 41.2 jit_solution(2094469993939796125)
XLA Ops:
  0.6 4.0 %collective-permute-start.2 = (bf16[256,128]{1,0:T(8,128)(2,1)}, bf16[256,128]{1,0:T(8,128)(2,1)S(1)}, u32[]{:S(2)}, u32[]{:S(2)}) collective-permute-start(bf16[256,128]{1,0:T(8,128)(2,1)} %features_ref.1), channel_id=1, source_target_pairs={{0,6},{1,7},{2,4},{3,5},{4,2},{5,3},{6,0},{7,1},{8,14},{9,15},{10,... | collective-permute-start | bytes 196616 | tf_op jit(solution)/shard_map/ppermute | solution.py:17
  5.2 1.0 %copy-done.1 = bf16[8,2,128,128]{3,2,1,0:T(8,128)(2,1)S(1)} copy-done((bf16[8,2,128,128]{3,2,1,0:T(8,128)(2,1)S(1)}, bf16[8,2,128,128]{3,2,1,0:T(8,128)(2,1)}, u32[]{:S(2)}) %copy-start.1) | copy-done | bytes 524312
  6.3 0.8 %copy-done.4 = bf16[256,128]{1,0:T(8,128)(2,1)S(1)} copy-done((bf16[256,128]{1,0:T(8,128)(2,1)S(1)}, bf16[256,128]{1,0:T(8,128)(2,1)}, u32[]{:S(2)}) %copy-start.4) | copy-done | bytes 65560
  7.3 1.7 %collective-permute-done.1.refs_0_ = bf16[256,128]{1,0:T(8,128)(2,1)S(1)} collective-permute-done((bf16[256,128]{1,0:T(8,128)(2,1)}, bf16[256,128]{1,0:T(8,128)(2,1)S(1)}, u32[]{:S(2)}, u32[]{:S(2)}) %collective-permute-start.1) | collective-permute-done | bytes 65568 | tf_op jit(solution)/shard_map/ppermute | solution.py:17
  9.7 0.6 %copy-done.6 = s32[8,2]{0,1:T(2,128)S(1)} copy-done((s32[8,2]{0,1:T(2,128)S(1)}, s32[8,2]{0,1:T(2,128)}, u32[]{:S(2)}) %copy-start.6) | copy-done | bytes 88
  10.5 0.8 %collective-permute-done.3.far_ref = bf16[1024,128]{1,0:T(8,128)(2,1)S(1)} collective-permute-done((bf16[1024,128]{1,0:T(8,128)(2,1)S(1)}, bf16[1024,128]{1,0:T(8,128)(2,1)S(1)}, u32[]{:S(2)}, u32[]{:S(2)}) %collective-permute-start.3) | collective-permute-done | bytes 262176 | tf_op jit(solution)/shard_map/ppermute | solution.py:17
  11.6 2.7 %collective-permute-start.4 = (bf16[256,128]{1,0:T(8,128)(2,1)S(1)}, bf16[256,128]{1,0:T(8,128)(2,1)S(1)}, u32[]{:S(2)}, u32[]{:S(2)}) collective-permute-start(bf16[256,128]{1,0:T(8,128)(2,1)S(1)} %get-tuple-element.30), channel_id=1, source_target_pairs={{0,16},{8,24},{16,0},{24,8},{1,17},{9,25},{17,1},{25,9},{2,18},{10... | collective-permute-start | bytes 196616 | tf_op jit(solution)/shard_map/ppermute | solution.py:17
  14.2 1.3 %collective-permute-start.5 = (bf16[256,128]{1,0:T(8,128)(2,1)S(1)}, bf16[256,128]{1,0:T(8,128)(2,1)S(1)}, u32[]{:S(2)}, u32[]{:S(2)}) collective-permute-start(bf16[256,128]{1,0:T(8,128)(2,1)S(1)} %get-tuple-element.31), channel_id=1, source_target_pairs={{0,24},{8,16},{16,8},{24,0},{1,25},{9,17},{17,9},{25,1},{2,26},{10... | collective-permute-start | bytes 196616 | tf_op jit(solution)/shard_map/ppermute | solution.py:17
  15.8 3.5 %collective-permute-done.4.b_ref = bf16[256,128]{1,0:T(8,128)(2,1)S(1)} collective-permute-done((bf16[256,128]{1,0:T(8,128)(2,1)S(1)}, bf16[256,128]{1,0:T(8,128)(2,1)S(1)}, u32[]{:S(2)}, u32[]{:S(2)}) %collective-permute-start.4) | collective-permute-done | bytes 65568 | tf_op jit(solution)/shard_map/ppermute | solution.py:17
  19.4 1.3 %collective-permute-done.5.b_ref = bf16[256,128]{1,0:T(8,128)(2,1)S(1)} collective-permute-done((bf16[256,128]{1,0:T(8,128)(2,1)S(1)}, bf16[256,128]{1,0:T(8,128)(2,1)S(1)}, u32[]{:S(2)}, u32[]{:S(2)}) %collective-permute-start.5) | collective-permute-done | bytes 65568 | tf_op jit(solution)/shard_map/ppermute | solution.py:17
  21.0 2.7 %collective-permute-start.7 = (bf16[256,128]{1,0:T(8,128)(2,1)S(1)}, bf16[256,128]{1,0:T(8,128)(2,1)S(1)}, u32[]{:S(2)}, u32[]{:S(2)}) collective-permute-start(bf16[256,128]{1,0:T(8,128)(2,1)S(1)} %shard_map.93.refs_0_), channel_id=1, source_target_pairs={{0,16},{8,24},{16,0},{24,8},{1,17},{9,25},{17,1},{25,9},{2,18},{10... | collective-permute-start | bytes 196616 | tf_op jit(solution)/shard_map/ppermute | solution.py:17
  23.6 0.6 %collective-permute-start.8 = (bf16[256,128]{1,0:T(8,128)(2,1)S(1)}, bf16[256,128]{1,0:T(8,128)(2,1)S(1)}, u32[]{:S(2)}, u32[]{:S(2)}) collective-permute-start(bf16[256,128]{1,0:T(8,128)(2,1)S(1)} %shard_map.93.refs_0_), channel_id=1, source_target_pairs={{0,24},{8,16},{16,8},{24,0},{1,25},{9,17},{17,9},{25,1},{2,26},{10... | collective-permute-start | bytes 196616 | tf_op jit(solution)/shard_map/ppermute | solution.py:17
  24.8 0.6 %copy-done.5 = f32[128]{0:T(128)S(1)} copy-done((f32[128]{0:T(128)S(1)}, f32[128]{0:T(128)}, u32[]{:S(2)}) %copy-start.5) | copy-done | bytes 536
  25.9 1.7 %collective-permute-done.7.refs_0_ = bf16[256,128]{1,0:T(8,128)(2,1)S(1)} collective-permute-done((bf16[256,128]{1,0:T(8,128)(2,1)S(1)}, bf16[256,128]{1,0:T(8,128)(2,1)S(1)}, u32[]{:S(2)}, u32[]{:S(2)}) %collective-permute-start.7) | collective-permute-done | bytes 65568 | tf_op jit(solution)/shard_map/ppermute | solution.py:17
  28.2 1.8 %collective-permute-done.8.refs_0_ = bf16[256,128]{1,0:T(8,128)(2,1)S(1)} collective-permute-done((bf16[256,128]{1,0:T(8,128)(2,1)S(1)}, bf16[256,128]{1,0:T(8,128)(2,1)S(1)}, u32[]{:S(2)}, u32[]{:S(2)}) %collective-permute-start.8) | collective-permute-done | bytes 65568 | tf_op jit(solution)/shard_map/ppermute | solution.py:17
  30.5 0.6 %shard_map.97 = (bf16[256,128]{1,0:T(8,128)(2,1)S(1)}, f32[16,128,128]{2,1,0:T(8,128)S(1)}, bf16[384,128]{1,0:T(8,128)(2,1)S(1)}, bf16[768,128]{1,0:T(8,128)(2,1)S(1)}) custom-call(s32[16,128]{1,0:T(8,128)S(1)} %shard_map.89.place_ref, bf16[8,256,128]{2,1,0:T(8,128)(2,1)S(1)} %get-tuple-element.28.flipped_ref, ...), custom_call_target="tpu_custom_call", output_to_operand_aliasing={{1}: (6, {})} | custom-call | tf_op jit(solution)/shard_map/pallas_call | solution.py:266
  31.6 0.8 %collective-permute-done.10.got_ref = bf16[384,128]{1,0:T(8,128)(2,1)S(1)} collective-permute-done((bf16[384,128]{1,0:T(8,128)(2,1)S(1)}, bf16[384,128]{1,0:T(8,128)(2,1)S(1)}, u32[]{:S(2)}, u32[]{:S(2)}) %collective-permute-start.10) | collective-permute-done | bytes 98336 | tf_op jit(solution)/shard_map/ppermute | solution.py:17
  32.4 1.6 %collective-permute-start.14 = (bf16[384,128]{1,0:T(8,128)(2,1)S(1)}, bf16[384,128]{1,0:T(8,128)(2,1)S(1)}, u32[]{:S(2)}, u32[]{:S(2)}) collective-permute-start(bf16[384,128]{1,0:T(8,128)(2,1)S(1)} %shard_map.99.first_ref.sent_ref), channel_id=1, source_target_pairs={{0,6},{1,7},{2,4},{3,5},{4,2},{5,3},{6,0},{7,1},{8,14},{9,15},{10,... | collective-permute-start | bytes 294920 | tf_op jit(solution)/shard_map/ppermute | solution.py:17
  34.0 0.6 %collective-permute-start.13 = (bf16[384,128]{1,0:T(8,128)(2,1)S(1)}, bf16[384,128]{1,0:T(8,128)(2,1)S(1)}, u32[]{:S(2)}, u32[]{:S(2)}) collective-permute-start(bf16[384,128]{1,0:T(8,128)(2,1)S(1)} %get-tuple-element.48), channel_id=1, source_target_pairs={{0,4},{1,5},{2,6},{3,7},{4,0},{5,1},{6,2},{7,3},{8,12},{9,13},{10,... | collective-permute-start | bytes 294920 | tf_op jit(solution)/shard_map/ppermute | solution.py:17
  34.6 1.5 %collective-permute-start.12 = (bf16[384,128]{1,0:T(8,128)(2,1)S(1)}, bf16[384,128]{1,0:T(8,128)(2,1)S(1)}, u32[]{:S(2)}, u32[]{:S(2)}) collective-permute-start(bf16[384,128]{1,0:T(8,128)(2,1)S(1)} %get-tuple-element.47), channel_id=1, source_target_pairs={{0,2},{1,3},{2,0},{3,1},{4,6},{5,7},{6,4},{7,5},{8,10},{9,11},{10,... | collective-permute-start | bytes 294920 | tf_op jit(solution)/shard_map/ppermute | solution.py:17
  36.1 0.7 %shard_map.98 = bf16[1024,128]{1,0:T(8,128)(2,1)} custom-call(bf16[256,128]{1,0:T(8,128)(2,1)S(1)} %get-tuple-element.33.refs_0_, bf16[256,128]{1,0:T(8,128)(2,1)S(1)} %get-tuple-element.36.refs_1_, bf16[256,128]{1,0:T(8,128)(2,1)S(1)} %get-tuple-element.39.refs_2_, bf16[256,128]{1,0:T(8,128)(2,1)S(1)} %get-tuple-element.42.refs_3_), custom_call_target="tpu_custom_call" | custom-call | tf_op jit(solution)/shard_map/pallas_call | solution.py:283
  36.8 1.9 %collective-permute-done.14.got_ref = bf16[384,128]{1,0:T(8,128)(2,1)S(1)} collective-permute-done((bf16[384,128]{1,0:T(8,128)(2,1)S(1)}, bf16[384,128]{1,0:T(8,128)(2,1)S(1)}, u32[]{:S(2)}, u32[]{:S(2)}) %collective-permute-start.14) | collective-permute-done | bytes 98336 | tf_op jit(solution)/shard_map/ppermute | solution.py:17
  38.8 1.6 %collective-permute-done.13.refs_0_ = bf16[384,128]{1,0:T(8,128)(2,1)S(1)} collective-permute-done((bf16[384,128]{1,0:T(8,128)(2,1)S(1)}, bf16[384,128]{1,0:T(8,128)(2,1)S(1)}, u32[]{:S(2)}, u32[]{:S(2)}) %collective-permute-start.13) | collective-permute-done | bytes 98336 | tf_op jit(solution)/shard_map/ppermute | solution.py:17
  40.5 0.7 %shard_map.103 = (f32[256,128]{1,0:T(8,128)}, f32[128,128]{1,0:T(8,128)}) custom-call(f32[256,128]{1,0:T(8,128)S(1)} %get-tuple-element.46.own_ref, bf16[384,128]{1,0:T(8,128)(2,1)S(1)} %shard_map.99.first_ref.sent_ref, bf16[384,128]{1,0:T(8,128)(2,1)S(1)} %collective-permute-done.12.got_ref, f32[384,128]{1,0:T(8,128)S(1)} %shard_map.102.refs_0_), custom_call_target="tpu_custom_call" | custom-call | tf_op jit(solution)/shard_map/pallas_call | solution.py:292
  (39 shorter events, 5.4 us)
Async XLA Ops:
  0.6 6.7 %collective-permute-start.2 = (bf16[256,128]{1,0:T(8,128)(2,1)}, bf16[256,128]{1,0:T(8,128)(2,1)S(1)}, u32[]{:S(2)}, u32[]{:S(2)}) collective-permute-start(bf16[256,128]{1,0:T(8,128)(2,1)} %features_ref.1), channel_id=1, source_target_pairs={{0,6},{1,7},{2,4},{3,5},{4,2},{5,3},{6,0},{7,1},{8,14},{9,15},{10,... | collective-permute-start | bytes 196616 | tf_op jit(solution)/shard_map/ppermute | solution.py:17
  4.6 4.5 %collective-permute-start.1 = (bf16[256,128]{1,0:T(8,128)(2,1)}, bf16[256,128]{1,0:T(8,128)(2,1)S(1)}, u32[]{:S(2)}, u32[]{:S(2)}) collective-permute-start(bf16[256,128]{1,0:T(8,128)(2,1)} %features_ref.1), channel_id=1, source_target_pairs={{0,4},{1,5},{2,6},{3,7},{4,0},{5,1},{6,2},{7,3},{8,12},{9,13},{10,... | collective-permute-start | bytes 196616 | tf_op jit(solution)/shard_map/ppermute | solution.py:17
  5.1 4.5 %collective-permute-start = (bf16[256,128]{1,0:T(8,128)(2,1)}, bf16[256,128]{1,0:T(8,128)(2,1)S(1)}, u32[]{:S(2)}, u32[]{:S(2)}) collective-permute-start(bf16[256,128]{1,0:T(8,128)(2,1)} %features_ref.1), channel_id=1, source_target_pairs={{0,2},{1,3},{2,0},{3,1},{4,6},{5,7},{6,4},{7,5},{8,10},{9,11},{10,... | collective-permute-start | bytes 196616 | tf_op jit(solution)/shard_map/ppermute | solution.py:17
  5.2 1.0 %copy-start.1 = (bf16[8,2,128,128]{3,2,1,0:T(8,128)(2,1)S(1)}, bf16[8,2,128,128]{3,2,1,0:T(8,128)(2,1)}, u32[]{:S(2)}) copy-start(bf16[8,2,128,128]{3,2,1,0:T(8,128)(2,1)} %vals_ref.3) | copy-start | bytes 1572868
  6.3 0.8 %copy-start.4 = (bf16[256,128]{1,0:T(8,128)(2,1)S(1)}, bf16[256,128]{1,0:T(8,128)(2,1)}, u32[]{:S(2)}) copy-start(bf16[256,128]{1,0:T(8,128)(2,1)} %features_ref.1) | copy-start | bytes 196612
  7.3 3.9 %copy-start.2 = (bf16[8,2,128,128]{3,2,1,0:T(8,128)(2,1)S(1)}, bf16[8,2,128,128]{3,2,1,0:T(8,128)(2,1)}, u32[]{:S(2)}) copy-start(bf16[8,2,128,128]{3,2,1,0:T(8,128)(2,1)} %vals_ref.3) | copy-start | bytes 1572868
  9.6 0.7 %copy-start.6 = (s32[8,2]{0,1:T(2,128)S(1)}, s32[8,2]{0,1:T(2,128)}, u32[]{:S(2)}) copy-start(s32[8,2]{0,1:T(2,128)} %param.6) | copy-start | bytes 196
  9.6 1.6 %collective-permute-start.3 = (bf16[1024,128]{1,0:T(8,128)(2,1)S(1)}, bf16[1024,128]{1,0:T(8,128)(2,1)S(1)}, u32[]{:S(2)}, u32[]{:S(2)}) collective-permute-start(bf16[1024,128]{1,0:T(8,128)(2,1)S(1)} %shard_map.88._.mine_ref), channel_id=1, source_target_pairs={{0,1},{1,0},{2,3},{3,2},{4,5},{5,4},{6,7},{7,6},{8,9},{9,8},{10,11... | collective-permute-start | bytes 786440 | tf_op jit(solution)/shard_map/ppermute | solution.py:17
  11.6 7.8 %collective-permute-start.4 = (bf16[256,128]{1,0:T(8,128)(2,1)S(1)}, bf16[256,128]{1,0:T(8,128)(2,1)S(1)}, u32[]{:S(2)}, u32[]{:S(2)}) collective-permute-start(bf16[256,128]{1,0:T(8,128)(2,1)S(1)} %get-tuple-element.30), channel_id=1, source_target_pairs={{0,16},{8,24},{16,0},{24,8},{1,17},{9,25},{17,1},{25,9},{2,18},{10... | collective-permute-start | bytes 196616 | tf_op jit(solution)/shard_map/ppermute | solution.py:17
  14.2 6.4 %collective-permute-start.5 = (bf16[256,128]{1,0:T(8,128)(2,1)S(1)}, bf16[256,128]{1,0:T(8,128)(2,1)S(1)}, u32[]{:S(2)}, u32[]{:S(2)}) collective-permute-start(bf16[256,128]{1,0:T(8,128)(2,1)S(1)} %get-tuple-element.31), channel_id=1, source_target_pairs={{0,24},{8,16},{16,8},{24,0},{1,25},{9,17},{17,9},{25,1},{2,26},{10... | collective-permute-start | bytes 196616 | tf_op jit(solution)/shard_map/ppermute | solution.py:17
  15.6 5.4 %collective-permute-start.6 = (bf16[256,128]{1,0:T(8,128)(2,1)S(1)}, bf16[256,128]{1,0:T(8,128)(2,1)S(1)}, u32[]{:S(2)}, u32[]{:S(2)}) collective-permute-start(bf16[256,128]{1,0:T(8,128)(2,1)S(1)} %get-tuple-element.32), channel_id=1, source_target_pairs={{0,8},{8,0},{16,24},{24,16},{1,9},{9,1},{17,25},{25,17},{2,10},{10... | collective-permute-start | bytes 196616 | tf_op jit(solution)/shard_map/ppermute | solution.py:17
  19.4 5.4 %copy-start = (bf16[1024,128]{1,0:T(8,128)(2,1)S(1)}, bf16[1024,128]{1,0:T(8,128)(2,1)}, u32[]{:S(2)}) copy-start(bf16[1024,128]{1,0:T(8,128)(2,1)} %cotangent_ref.7) | copy-start | bytes 786436
  20.6 4.1 %copy-start.3 = (bf16[128,128]{1,0:T(8,128)(2,1)S(1)}, bf16[128,128]{1,0:T(8,128)(2,1)}, u32[]{:S(2)}) copy-start(bf16[128,128]{1,0:T(8,128)(2,1)} %weight_ref.7) | copy-start | bytes 98308
  21.0 6.7 %collective-permute-start.7 = (bf16[256,128]{1,0:T(8,128)(2,1)S(1)}, bf16[256,128]{1,0:T(8,128)(2,1)S(1)}, u32[]{:S(2)}, u32[]{:S(2)}) collective-permute-start(bf16[256,128]{1,0:T(8,128)(2,1)S(1)} %shard_map.93.refs_0_), channel_id=1, source_target_pairs={{0,16},{8,24},{16,0},{24,8},{1,17},{9,25},{17,1},{25,9},{2,18},{10... | collective-permute-start | bytes 196616 | tf_op jit(solution)/shard_map/ppermute | solution.py:17
  23.6 6.3 %collective-permute-start.8 = (bf16[256,128]{1,0:T(8,128)(2,1)S(1)}, bf16[256,128]{1,0:T(8,128)(2,1)S(1)}, u32[]{:S(2)}, u32[]{:S(2)}) collective-permute-start(bf16[256,128]{1,0:T(8,128)(2,1)S(1)} %shard_map.93.refs_0_), channel_id=1, source_target_pairs={{0,24},{8,16},{16,8},{24,0},{1,25},{9,17},{17,9},{25,1},{2,26},{10... | collective-permute-start | bytes 196616 | tf_op jit(solution)/shard_map/ppermute | solution.py:17
  24.3 6.2 %collective-permute-start.9 = (bf16[256,128]{1,0:T(8,128)(2,1)S(1)}, bf16[256,128]{1,0:T(8,128)(2,1)S(1)}, u32[]{:S(2)}, u32[]{:S(2)}) collective-permute-start(bf16[256,128]{1,0:T(8,128)(2,1)S(1)} %shard_map.93.refs_0_), channel_id=1, source_target_pairs={{0,8},{8,0},{16,24},{24,16},{1,9},{9,1},{17,25},{25,17},{2,10},{10... | collective-permute-start | bytes 196616 | tf_op jit(solution)/shard_map/ppermute | solution.py:17
  24.8 0.7 %copy-start.5 = (f32[128]{0:T(128)S(1)}, f32[128]{0:T(128)}, u32[]{:S(2)}) copy-start(f32[128]{0:T(128)} %param.10) | copy-start | bytes 1540
  31.0 1.4 %collective-permute-start.10 = (bf16[384,128]{1,0:T(8,128)(2,1)S(1)}, bf16[384,128]{1,0:T(8,128)(2,1)S(1)}, u32[]{:S(2)}, u32[]{:S(2)}) collective-permute-start(bf16[384,128]{1,0:T(8,128)(2,1)S(1)} %get-tuple-element.44.sent_ref), channel_id=1, source_target_pairs={{0,1},{1,0},{2,3},{3,2},{4,5},{5,4},{6,7},{7,6},{8,9},{9,8},{10,11... | collective-permute-start | bytes 294920 | tf_op jit(solution)/shard_map/ppermute | solution.py:17
  31.1 2.9 %collective-permute-start.11 = (bf16[768,128]{1,0:T(8,128)(2,1)S(1)}, bf16[768,128]{1,0:T(8,128)(2,1)S(1)}, u32[]{:S(2)}, u32[]{:S(2)}) collective-permute-start(bf16[768,128]{1,0:T(8,128)(2,1)S(1)} %get-tuple-element.45), channel_id=1, source_target_pairs={{0,1},{1,0},{2,3},{3,2},{4,5},{5,4},{6,7},{7,6},{8,9},{9,8},{10,11... | collective-permute-start | bytes 589832 | tf_op jit(solution)/shard_map/ppermute | solution.py:17
  32.4 6.3 %collective-permute-start.14 = (bf16[384,128]{1,0:T(8,128)(2,1)S(1)}, bf16[384,128]{1,0:T(8,128)(2,1)S(1)}, u32[]{:S(2)}, u32[]{:S(2)}) collective-permute-start(bf16[384,128]{1,0:T(8,128)(2,1)S(1)} %shard_map.99.first_ref.sent_ref), channel_id=1, source_target_pairs={{0,6},{1,7},{2,4},{3,5},{4,2},{5,3},{6,0},{7,1},{8,14},{9,15},{10,... | collective-permute-start | bytes 294920 | tf_op jit(solution)/shard_map/ppermute | solution.py:17
  34.0 6.3 %collective-permute-start.13 = (bf16[384,128]{1,0:T(8,128)(2,1)S(1)}, bf16[384,128]{1,0:T(8,128)(2,1)S(1)}, u32[]{:S(2)}, u32[]{:S(2)}) collective-permute-start(bf16[384,128]{1,0:T(8,128)(2,1)S(1)} %get-tuple-element.48), channel_id=1, source_target_pairs={{0,4},{1,5},{2,6},{3,7},{4,0},{5,1},{6,2},{7,3},{8,12},{9,13},{10,... | collective-permute-start | bytes 294920 | tf_op jit(solution)/shard_map/ppermute | solution.py:17
  34.6 5.8 %collective-permute-start.12 = (bf16[384,128]{1,0:T(8,128)(2,1)S(1)}, bf16[384,128]{1,0:T(8,128)(2,1)S(1)}, u32[]{:S(2)}, u32[]{:S(2)}) collective-permute-start(bf16[384,128]{1,0:T(8,128)(2,1)S(1)} %get-tuple-element.47), channel_id=1, source_target_pairs={{0,2},{1,3},{2,0},{3,1},{4,6},{5,7},{6,4},{7,5},{8,10},{9,11},{10,... | collective-permute-start | bytes 294920 | tf_op jit(solution)/shard_map/ppermute | solution.py:17

commit v12 on v11

--- a/solution.py
+++ b/solution.py
@@ -17,6 +17,14 @@
     return lax.ppermute(value, axis, [(i, i ^ distance) for i in range(size)])
 
 
+def cross(value, turn, chips):
+    def partner(i):
+        chip = turn ^ (chips - 1) if i % 2 and turn != chips - 1 else turn
+        return i ^ (2 * chip)
+
+    return lax.ppermute(value, "dom", [(i, partner(i)) for i in range(2 * chips)])
+
+
 def matmul(a, b, contract):
     return lax.dot_general(a, b, ((contract[:1], contract[1:]), ((), ())), preferred_element_type=F32)
 
@@ -29,14 +37,21 @@
             flipped_ref[row, k * size : (k + 1) * size] = vals_ref[row, k].T
 
 
-def place_kernel(own_blocks, dom, cols_ref, _, place_ref):
+def place_kernel(own_blocks, chips, cols_ref, _, place_ref):
     count, rows = cols_ref.shape
+    half = chips // 2 - 1
+    me = lax.axis_index("dom")
     for row in range(rows):
         for k in range(count):
-            col = cols_ref[k, row] - lax.axis_index("rep") * (own_blocks * dom)
-            owner = lax.div(col, jnp.int32(own_blocks)) ^ lax.axis_index("dom")
-            place = ((owner & 1) * (dom // 2) + (owner >> 1)) * own_blocks
-            place += lax.rem(col, jnp.int32(own_blocks))
+            col = cols_ref[k, row] - lax.axis_index("rep") * (own_blocks * 2 * chips)
+            apart = lax.div(col, jnp.int32(own_blocks)) ^ me
+            side, chip = apart & 1, apart >> 1
+            inner = jnp.logical_and(chip > 0, chip < chips - 1)
+            odd = ((me & 1) ^ side) == 1
+            turn = jnp.where(jnp.logical_and(inner, odd), chip ^ (chips - 1), chip)
+            turn = jnp.where(turn > half, turn + 1, turn)
+            turn = jnp.where(chip == chips - 1, half + 1, turn)
+            place = (side * chips + turn) * own_blocks + lax.rem(col, jnp.int32(own_blocks))
             place_ref[row * count + k : row * count + k + 1, :] = jnp.full((1, 128), place, jnp.int32)
 
 
@@ -46,19 +61,6 @@
     for piece in pieces:
         out_ref[first : first + piece.shape[0]] = piece[...]
         first += piece.shape[0]
-
-
-def last_join_kernel(*refs):
-    near, middle, out_ref = refs[:-2], refs[-2], refs[-1]
-    nodes = near[0].shape[0]
-    body = middle.shape[0] - 2 * nodes
-    out_ref[:nodes] = middle[body : body + nodes]
-    first = nodes
-    for piece in near:
-        out_ref[first : first + nodes] = piece[...]
-        first += nodes
-    out_ref[first : first + body] = middle[:body]
-    out_ref[first + body :] = middle[body + nodes :]
 
 
 def aggregate_kernel(rep, place_ref, vals_ref, mine_ref, far_ref, *outs):
@@ -122,8 +124,9 @@
     else:
         first_ref, rest_ref = refs
         away = contrib[quarter_blocks // 2 :].reshape(quarter_blocks // 2 * size, -1).astype(BF16)
-        rest_ref[...] = away[:-nodes]
-        first_ref[:nodes] = away[-nodes:]
+        rest_ref[:nodes] = away[:nodes]
+        rest_ref[nodes:] = away[2 * nodes :]
+        first_ref[:nodes] = away[nodes : 2 * nodes]
         first_ref[nodes:] = ((sums_in[0] + part_sum) + sums_in[1]).astype(BF16)
 
 
@@ -140,23 +143,22 @@
 
 
 def first_pair_kernel(contrib_ref, sent_ref, got_ref, out_ref):
-    blocks, size, _ = contrib_ref.shape
+    size = contrib_ref.shape[1]
     nodes = out_ref.shape[0] - sent_ref.shape[1]
-    last = contrib_ref[blocks // 2 - nodes // size : blocks // 2].reshape(nodes, -1)
-    out_ref[:nodes] = (last + got_ref[:nodes].astype(F32)).astype(BF16)
+    mine = contrib_ref[nodes // size : 2 * nodes // size].reshape(nodes, -1)
+    out_ref[:nodes] = (mine + got_ref[:nodes].astype(F32)).astype(BF16)
     out_ref[nodes:] = (sent_ref[nodes:].astype(F32) + got_ref[nodes:].astype(F32)).astype(BF16)
 
 
 def rest_pair_kernel(contrib_ref, first_ref, got_ref, own_ref, *outs):
     size, nodes = contrib_ref.shape[1], own_ref.shape[0]
-    for chip in range(len(outs) + 1):
-        mine = contrib_ref[chip * nodes // size : (chip + 1) * nodes // size].reshape(nodes, -1)
-        total = mine + got_ref[chip * nodes : (chip + 1) * nodes].astype(F32)
-        if chip == 0:
-            own_ref[...] = total
-        else:
-            outs[chip - 1][:nodes] = total.astype(BF16)
-            outs[chip - 1][nodes:] = first_ref[nodes:]
+    mine = contrib_ref[: nodes // size].reshape(nodes, -1)
+    own_ref[...] = mine + got_ref[:nodes].astype(F32)
+    for at, out_ref in enumerate(outs, 1):
+        mine = contrib_ref[(at + 1) * nodes // size : (at + 2) * nodes // size].reshape(nodes, -1)
+        total = mine + got_ref[at * nodes : (at + 1) * nodes].astype(F32)
+        out_ref[:nodes] = total.astype(BF16)
+        out_ref[nodes:] = first_ref[nodes:]
 
 
 def total_of(values):
@@ -169,23 +171,31 @@
     out_ref[...] = got_ref[...].astype(F32)
 
 
-def half_kernel(levels, *refs):
-    for level in range(1, levels):
-        first = 1 << level
-        got = refs[first - 2 : 2 * first - 2]
-        refs[level - levels][...] = total_of([g[...].astype(F32) for g in got])
-
-
-def final_kernel(own_ref, sent_ref, got_ref, *refs):
-    later, (feature_ref, weight_ref) = refs[:-2], refs[-2:]
+def early_sum_kernel(own_ref, sent_ref, lifted_ref, *refs):
+    got, out_ref = refs[:-1], refs[-1]
     nodes = own_ref.shape[0]
-    feature = own_ref[...] + got_ref[:nodes].astype(F32)
-    weight = sent_ref[nodes:].astype(F32) + got_ref[nodes:].astype(F32)
-    for value in later:
-        feature += value[:nodes]
-        weight += value[nodes:]
-    feature_ref[...] = feature
-    weight_ref[...] = weight
+    width = sent_ref.shape[1]
+    total = own_ref[...] + lifted_ref[:nodes]
+    for g in got:
+        total += g[:nodes].astype(F32)
+    out_ref[:nodes] = total
+    weights = [sent_ref[nodes:].astype(F32) + got[-1][nodes:].astype(F32), lifted_ref[nodes:]]
+    weights += [g[nodes:].astype(F32) for g in got[:-1]]
+    for i, value in enumerate(weights):
+        out_ref[nodes + i * width : nodes + (i + 1) * width] = value
+
+
+def final_kernel(early_ref, *refs):
+    got, (feature_ref, weight_ref) = refs[:-2], refs[-2:]
+    nodes, width = feature_ref.shape
+    total = early_ref[:nodes]
+    weights = [early_ref[nodes : nodes + width]]
+    for i, g in enumerate(got):
+        total += g[:nodes].astype(F32)
+        early = early_ref[nodes + (i + 1) * width : nodes + (i + 2) * width]
+        weights.append(early + got[-1 - i][nodes:].astype(F32))
+    feature_ref[...] = total
+    weight_ref[...] = total_of(weights)
 
 
 def shape(dims, dtype):
@@ -224,15 +234,15 @@
         nodes_in = sum(v.shape[0] for v in values)
         return call(join_kernel, shape((nodes_in, width), BF16), [VMEM] * len(values))(*values)
 
-    across = [swap(features, "dom", 2 * chip) for chip in range(1, chips)]
-    front = join(own, across[-1])
-    middle = join(*across[chips // 2 - 1 : -1], front)
-    mine = call(last_join_kernel, shape((chips * nodes, width), BF16), [VMEM] * (chips // 2))(
-        *across[: chips // 2 - 1], middle
-    )
+    half = chips // 2 - 1
+    turns = [*range(1, half + 1), chips - 1, *range(half + 1, chips - 1)]
+    across = {turn: cross(features, turn, chips) for turn in turns}
+    mine = join(own, *[across[turn] for turn in turns[:half]])
+    mine = join(mine, across[chips - 1])
+    mine = join(mine, *[across[turn] for turn in turns[half + 1 :]])
     far = swap(mine, "dom", 1)
     place = call(
-        functools.partial(place_kernel, own_blocks, dom),
+        functools.partial(place_kernel, own_blocks, chips),
         shape((rows * count, 128), jnp.int32),
         [VMEM] * 2,
     )(cols.T, mine)
@@ -274,26 +284,28 @@
 
     message = shape((nodes + width, width), BF16)
     got_first, got_rest = swap(first, "dom", 1), swap(rest, "dom", 1)
-    sends = [call(first_pair_kernel, message, [VMEM] * 3, cost=5000000000)(contrib, first, got_first)]
-    own, *others = call(
-        rest_pair_kernel, [shape((nodes, width), F32)] + [message] * (chips - 2), [VMEM] * 3, cost=1000000000
-    )(contrib, sends[0], got_rest)
-    sends = others + sends
-    got = {chip: swap(sends[chip - 1], "dom", 2 * chip) for chip in range(chips - 1, 0, -1)}
+    sent = call(first_pair_kernel, message, [VMEM] * 3, cost=5 * 10**9)(contrib, first, got_first)
+    own, *sends = call(
+        rest_pair_kernel,
+        [shape((nodes, width), F32)] + [message] * (chips - 2),
+        [VMEM] * 3,
+        cost=10**9,
+    )(contrib, sent, got_rest)
+    got = [cross(value, turn, chips) for value, turn in zip([sent, *sends], turns)]
     output = call(
         functools.partial(order_kernel, list(pieces)), shape((rows * size, width), BF16), [VMEM] * rep
     )(*outputs)
-    levels = chips.bit_length() - 1
-    total = shape(message.shape, F32)
-    got[chips - 1] = call(lift_kernel, total, [VMEM], cost=1000000000)(got[chips - 1])
-    later = call(
-        functools.partial(half_kernel, levels), [total] * (levels - 1), [VMEM] * (chips - 2), cost=0
-    )(*[got[chip] for chip in range(2, chips)])
+    lifted = call(lift_kernel, shape(message.shape, F32), [VMEM], cost=10**9)(got[0])
+    early = call(
+        early_sum_kernel,
+        shape((nodes + (half + 1) * width, width), F32),
+        [VMEM] * (3 + half),
+    )(own, sent, lifted, *got[1 : half + 1])
     feature_grad, weight_grad = call(
         final_kernel,
         [shape((nodes, width), F32), shape((width, width), F32)],
-        [VMEM] * (levels + 2),
-    )(own, sends[-1], got[1], *later)
+        [VMEM] * (1 + half),
+    )(early, *got[half + 1 :])
     return output, feature_grad, weight_grad
 
 

time: 41.4 us -> 42 us (1.014)
  waiting for transfers between devices: 15.9 us -> 16.5 us
    ppermute x15 -> x9, starting transfers between devices: 16.9 us -> 8.65 us  [swap(): return lax.ppermute(value, axis, [(i, i ^ distance) for i in range(size)])]
    ppermute x0 -> x6, starting transfers between devices: none -> 8.16 us  [cross(): lax.ppermute(value, 'dom', [(i, partner(i)) for i in range(2 * chips)])]
    ppermute x0 -> x6, waiting for transfers between devices: none -> 6.39 us  [cross(): lax.ppermute(value, 'dom', [(i, partner(i)) for i in range(2 * chips)])]
    ppermute x15 -> x9, waiting for transfers between devices: 15.9 us -> 10.1 us  [swap(): return lax.ppermute(value, axis, [(i, i ^ distance) for i in range(size)])]
  transfers between devices with their start and end apart: 15 -> 15, of which waited for: 12 -> 11; matrix products, arithmetic and copies ran while one was open for 0% -> 0% of each run, Pallas kernels for 7% -> 7%
where the time goes in v12:
time: 42 us; the launch traced here: 41.7 us
  starting transfers between devices  16.8 us (40%)
  waiting for transfers between devices  16.5 us (39%)
  Pallas kernels  4.5 us (11%)
  local copies, waits for them, and re-layouts  3.14 us (7%)
  between operations  0.81 us (2%)
    ppermute x9, waiting for transfers between devices, swap(): return lax.ppermute(value, axis, [(i, i ^ distance) for i in range(size)])  10.1 us
    ppermute x9, starting transfers between devices, swap(): return lax.ppermute(value, axis, [(i, i ^ distance) for i in range(size)])  8.65 us
    ppermute x6, starting transfers between devices, cross(): lax.ppermute(value, 'dom', [(i, partner(i)) for i in range(2 * chips)])  8.16 us
    ppermute x6, waiting for transfers between devices, cross(): lax.ppermute(value, 'dom', [(i, partner(i)) for i in range(2 * chips)])  6.39 us
    unnamed x14, local copies, waits for them, and re-layouts  3.14 us
    pallas_call x4, Pallas kernels, body(): call(functools.partial(layer_kernel, rep, count, own_blocks, j), outs, [V...  2.12 us
  transfers between devices with their start and end apart: 15, of which 11 were waited for; matrix products, arithmetic and copies ran while one was open for 0% of the time, Pallas kernels for 7%

profile of v12, /device:TPU:0, one launch (start us, length us, event | category | flops | bytes accessed | tf_op | source)
XLA Modules:
  0.0 41.7 jit_solution(9194141796175962196)
XLA Ops:
  0.6 3.0 %collective-permute-start = (bf16[256,128]{1,0:T(8,128)(2,1)}, bf16[256,128]{1,0:T(8,128)(2,1)S(1)}, u32[]{:S(2)}, u32[]{:S(2)}) collective-permute-start(bf16[256,128]{1,0:T(8,128)(2,1)} %features_ref.1), channel_id=1, source_target_pairs={{0,2},{1,5},{2,0},{3,7},{4,6},{5,1},{6,4},{7,3},{8,10},{9,13},{10,... | collective-permute-start | bytes 196616 | tf_op jit(solution)/shard_map/ppermute | solution.py:25
  3.6 1.5 %collective-permute-start.1 = (bf16[256,128]{1,0:T(8,128)(2,1)}, bf16[256,128]{1,0:T(8,128)(2,1)S(1)}, u32[]{:S(2)}, u32[]{:S(2)}) collective-permute-start(bf16[256,128]{1,0:T(8,128)(2,1)} %features_ref.1), channel_id=1, source_target_pairs={{0,6},{1,7},{2,4},{3,5},{4,2},{5,3},{6,0},{7,1},{8,14},{9,15},{10,... | collective-permute-start | bytes 196616 | tf_op jit(solution)/shard_map/ppermute | solution.py:25
  5.2 1.0 %copy-done.1 = bf16[8,2,128,128]{3,2,1,0:T(8,128)(2,1)S(1)} copy-done((bf16[8,2,128,128]{3,2,1,0:T(8,128)(2,1)S(1)}, bf16[8,2,128,128]{3,2,1,0:T(8,128)(2,1)}, u32[]{:S(2)}) %copy-start.1) | copy-done | bytes 524312
  6.2 0.8 %copy-done.4 = bf16[256,128]{1,0:T(8,128)(2,1)S(1)} copy-done((bf16[256,128]{1,0:T(8,128)(2,1)S(1)}, bf16[256,128]{1,0:T(8,128)(2,1)}, u32[]{:S(2)}) %copy-start.4) | copy-done | bytes 65560
  7.3 2.5 %collective-permute-done.1.refs_1_ = bf16[256,128]{1,0:T(8,128)(2,1)S(1)} collective-permute-done((bf16[256,128]{1,0:T(8,128)(2,1)}, bf16[256,128]{1,0:T(8,128)(2,1)S(1)}, u32[]{:S(2)}, u32[]{:S(2)}) %collective-permute-start.1) | collective-permute-done | bytes 65568 | tf_op jit(solution)/shard_map/ppermute | solution.py:25
  10.1 0.6 %copy-done.6 = s32[8,2]{0,1:T(2,128)S(1)} copy-done((s32[8,2]{0,1:T(2,128)S(1)}, s32[8,2]{0,1:T(2,128)}, u32[]{:S(2)}) %copy-start.6) | copy-done | bytes 88
  11.0 0.7 %collective-permute-done.3.far_ref = bf16[1024,128]{1,0:T(8,128)(2,1)S(1)} collective-permute-done((bf16[1024,128]{1,0:T(8,128)(2,1)S(1)}, bf16[1024,128]{1,0:T(8,128)(2,1)S(1)}, u32[]{:S(2)}, u32[]{:S(2)}) %collective-permute-start.3) | collective-permute-done | bytes 262176 | tf_op jit(solution)/shard_map/ppermute | solution.py:17
  12.0 2.7 %collective-permute-start.4 = (bf16[256,128]{1,0:T(8,128)(2,1)S(1)}, bf16[256,128]{1,0:T(8,128)(2,1)S(1)}, u32[]{:S(2)}, u32[]{:S(2)}) collective-permute-start(bf16[256,128]{1,0:T(8,128)(2,1)S(1)} %get-tuple-element.30), channel_id=1, source_target_pairs={{0,16},{8,24},{16,0},{24,8},{1,17},{9,25},{17,1},{25,9},{2,18},{10... | collective-permute-start | bytes 196616 | tf_op jit(solution)/shard_map/ppermute | solution.py:17
  14.7 1.3 %collective-permute-start.5 = (bf16[256,128]{1,0:T(8,128)(2,1)S(1)}, bf16[256,128]{1,0:T(8,128)(2,1)S(1)}, u32[]{:S(2)}, u32[]{:S(2)}) collective-permute-start(bf16[256,128]{1,0:T(8,128)(2,1)S(1)} %get-tuple-element.31), channel_id=1, source_target_pairs={{0,24},{8,16},{16,8},{24,0},{1,25},{9,17},{17,9},{25,1},{2,26},{10... | collective-permute-start | bytes 196616 | tf_op jit(solution)/shard_map/ppermute | solution.py:17
  16.3 3.5 %collective-permute-done.4.b_ref = bf16[256,128]{1,0:T(8,128)(2,1)S(1)} collective-permute-done((bf16[256,128]{1,0:T(8,128)(2,1)S(1)}, bf16[256,128]{1,0:T(8,128)(2,1)S(1)}, u32[]{:S(2)}, u32[]{:S(2)}) %collective-permute-start.4) | collective-permute-done | bytes 65568 | tf_op jit(solution)/shard_map/ppermute | solution.py:17
  19.8 1.3 %collective-permute-done.5.b_ref = bf16[256,128]{1,0:T(8,128)(2,1)S(1)} collective-permute-done((bf16[256,128]{1,0:T(8,128)(2,1)S(1)}, bf16[256,128]{1,0:T(8,128)(2,1)S(1)}, u32[]{:S(2)}, u32[]{:S(2)}) %collective-permute-start.5) | collective-permute-done | bytes 65568 | tf_op jit(solution)/shard_map/ppermute | solution.py:17
  21.4 2.7 %collective-permute-start.7 = (bf16[256,128]{1,0:T(8,128)(2,1)S(1)}, bf16[256,128]{1,0:T(8,128)(2,1)S(1)}, u32[]{:S(2)}, u32[]{:S(2)}) collective-permute-start(bf16[256,128]{1,0:T(8,128)(2,1)S(1)} %shard_map.93.refs_0_), channel_id=1, source_target_pairs={{0,16},{8,24},{16,0},{24,8},{1,17},{9,25},{17,1},{25,9},{2,18},{10... | collective-permute-start | bytes 196616 | tf_op jit(solution)/shard_map/ppermute | solution.py:17
  24.1 0.6 %collective-permute-start.8 = (bf16[256,128]{1,0:T(8,128)(2,1)S(1)}, bf16[256,128]{1,0:T(8,128)(2,1)S(1)}, u32[]{:S(2)}, u32[]{:S(2)}) collective-permute-start(bf16[256,128]{1,0:T(8,128)(2,1)S(1)} %shard_map.93.refs_0_), channel_id=1, source_target_pairs={{0,24},{8,16},{16,8},{24,0},{1,25},{9,17},{17,9},{25,1},{2,26},{10... | collective-permute-start | bytes 196616 | tf_op jit(solution)/shard_map/ppermute | solution.py:17
  25.2 0.6 %copy-done.5 = f32[128]{0:T(128)S(1)} copy-done((f32[128]{0:T(128)S(1)}, f32[128]{0:T(128)}, u32[]{:S(2)}) %copy-start.5) | copy-done | bytes 536
  26.4 1.7 %collective-permute-done.7.refs_0_ = bf16[256,128]{1,0:T(8,128)(2,1)S(1)} collective-permute-done((bf16[256,128]{1,0:T(8,128)(2,1)S(1)}, bf16[256,128]{1,0:T(8,128)(2,1)S(1)}, u32[]{:S(2)}, u32[]{:S(2)}) %collective-permute-start.7) | collective-permute-done | bytes 65568 | tf_op jit(solution)/shard_map/ppermute | solution.py:17
  28.7 1.8 %collective-permute-done.8.refs_0_ = bf16[256,128]{1,0:T(8,128)(2,1)S(1)} collective-permute-done((bf16[256,128]{1,0:T(8,128)(2,1)S(1)}, bf16[256,128]{1,0:T(8,128)(2,1)S(1)}, u32[]{:S(2)}, u32[]{:S(2)}) %collective-permute-start.8) | collective-permute-done | bytes 65568 | tf_op jit(solution)/shard_map/ppermute | solution.py:17
  32.1 0.8 %collective-permute-done.10.got_ref = bf16[384,128]{1,0:T(8,128)(2,1)S(1)} collective-permute-done((bf16[384,128]{1,0:T(8,128)(2,1)S(1)}, bf16[384,128]{1,0:T(8,128)(2,1)S(1)}, u32[]{:S(2)}, u32[]{:S(2)}) %collective-permute-start.10) | collective-permute-done | bytes 98336 | tf_op jit(solution)/shard_map/ppermute | solution.py:17
  32.9 1.5 %collective-permute-start.12 = (bf16[384,128]{1,0:T(8,128)(2,1)S(1)}, bf16[384,128]{1,0:T(8,128)(2,1)S(1)}, u32[]{:S(2)}, u32[]{:S(2)}) collective-permute-start(bf16[384,128]{1,0:T(8,128)(2,1)S(1)} %shard_map.99.first_ref.sent_ref), channel_id=1, source_target_pairs={{0,2},{1,5},{2,0},{3,7},{4,6},{5,1},{6,4},{7,3},{8,10},{9,13},{10,... | collective-permute-start | bytes 294920 | tf_op jit(solution)/shard_map/ppermute | solution.py:25
  34.4 0.9 %collective-permute-start.13 = (bf16[384,128]{1,0:T(8,128)(2,1)S(1)}, bf16[384,128]{1,0:T(8,128)(2,1)S(1)}, u32[]{:S(2)}, u32[]{:S(2)}) collective-permute-start(bf16[384,128]{1,0:T(8,128)(2,1)S(1)} %get-tuple-element.47), channel_id=1, source_target_pairs={{0,6},{1,7},{2,4},{3,5},{4,2},{5,3},{6,0},{7,1},{8,14},{9,15},{10,... | collective-permute-start | bytes 294920 | tf_op jit(solution)/shard_map/ppermute | solution.py:25
  35.3 1.3 %collective-permute-start.14 = (bf16[384,128]{1,0:T(8,128)(2,1)S(1)}, bf16[384,128]{1,0:T(8,128)(2,1)S(1)}, u32[]{:S(2)}, u32[]{:S(2)}) collective-permute-start(bf16[384,128]{1,0:T(8,128)(2,1)S(1)} %get-tuple-element.48), channel_id=1, source_target_pairs={{0,4},{1,3},{2,6},{3,1},{4,0},{5,7},{6,2},{7,5},{8,12},{9,11},{10,... | collective-permute-start | bytes 294920 | tf_op jit(solution)/shard_map/ppermute | solution.py:25
  36.6 0.7 %shard_map.98 = bf16[1024,128]{1,0:T(8,128)(2,1)} custom-call(bf16[256,128]{1,0:T(8,128)(2,1)S(1)} %get-tuple-element.33.refs_0_, bf16[256,128]{1,0:T(8,128)(2,1)S(1)} %get-tuple-element.36.refs_1_, bf16[256,128]{1,0:T(8,128)(2,1)S(1)} %get-tuple-element.39.refs_2_, bf16[256,128]{1,0:T(8,128)(2,1)S(1)} %get-tuple-element.42.refs_3_), custom_call_target="tpu_custom_call" | custom-call | tf_op jit(solution)/shard_map/pallas_call | solution.py:295
  37.3 0.9 %collective-permute-done.12.got_ref = bf16[384,128]{1,0:T(8,128)(2,1)S(1)} collective-permute-done((bf16[384,128]{1,0:T(8,128)(2,1)S(1)}, bf16[384,128]{1,0:T(8,128)(2,1)S(1)}, u32[]{:S(2)}, u32[]{:S(2)}) %collective-permute-start.12) | collective-permute-done | bytes 98336 | tf_op jit(solution)/shard_map/ppermute | solution.py:25
  38.2 2.7 %collective-permute-done.13.refs_0_ = bf16[384,128]{1,0:T(8,128)(2,1)S(1)} collective-permute-done((bf16[384,128]{1,0:T(8,128)(2,1)S(1)}, bf16[384,128]{1,0:T(8,128)(2,1)S(1)}, u32[]{:S(2)}, u32[]{:S(2)}) %collective-permute-start.13) | collective-permute-done | bytes 98336 | tf_op jit(solution)/shard_map/ppermute | solution.py:25
  41.0 0.7 %shard_map.103 = (f32[256,128]{1,0:T(8,128)}, f32[128,128]{1,0:T(8,128)}) custom-call(f32[512,128]{1,0:T(8,128)S(1)} %shard_map.102.early_ref, bf16[384,128]{1,0:T(8,128)(2,1)S(1)} %collective-permute-done.14.refs_0_), custom_call_target="tpu_custom_call" | custom-call | tf_op jit(solution)/shard_map/pallas_call | solution.py:304
  (39 shorter events, 5.1 us)
Async XLA Ops:
  0.6 6.6 %collective-permute-start = (bf16[256,128]{1,0:T(8,128)(2,1)}, bf16[256,128]{1,0:T(8,128)(2,1)S(1)}, u32[]{:S(2)}, u32[]{:S(2)}) collective-permute-start(bf16[256,128]{1,0:T(8,128)(2,1)} %features_ref.1), channel_id=1, source_target_pairs={{0,2},{1,5},{2,0},{3,7},{4,6},{5,1},{6,4},{7,3},{8,10},{9,13},{10,... | collective-permute-start | bytes 196616 | tf_op jit(solution)/shard_map/ppermute | solution.py:25
  3.6 6.2 %collective-permute-start.1 = (bf16[256,128]{1,0:T(8,128)(2,1)}, bf16[256,128]{1,0:T(8,128)(2,1)S(1)}, u32[]{:S(2)}, u32[]{:S(2)}) collective-permute-start(bf16[256,128]{1,0:T(8,128)(2,1)} %features_ref.1), channel_id=1, source_target_pairs={{0,6},{1,7},{2,4},{3,5},{4,2},{5,3},{6,0},{7,1},{8,14},{9,15},{10,... | collective-permute-start | bytes 196616 | tf_op jit(solution)/shard_map/ppermute | solution.py:25
  5.1 4.9 %collective-permute-start.2 = (bf16[256,128]{1,0:T(8,128)(2,1)}, bf16[256,128]{1,0:T(8,128)(2,1)S(1)}, u32[]{:S(2)}, u32[]{:S(2)}) collective-permute-start(bf16[256,128]{1,0:T(8,128)(2,1)} %features_ref.1), channel_id=1, source_target_pairs={{0,4},{1,3},{2,6},{3,1},{4,0},{5,7},{6,2},{7,5},{8,12},{9,11},{10,... | collective-permute-start | bytes 196616 | tf_op jit(solution)/shard_map/ppermute | solution.py:25
  5.2 1.0 %copy-start.1 = (bf16[8,2,128,128]{3,2,1,0:T(8,128)(2,1)S(1)}, bf16[8,2,128,128]{3,2,1,0:T(8,128)(2,1)}, u32[]{:S(2)}) copy-start(bf16[8,2,128,128]{3,2,1,0:T(8,128)(2,1)} %vals_ref.3) | copy-start | bytes 1572868
  6.2 0.8 %copy-start.4 = (bf16[256,128]{1,0:T(8,128)(2,1)S(1)}, bf16[256,128]{1,0:T(8,128)(2,1)}, u32[]{:S(2)}) copy-start(bf16[256,128]{1,0:T(8,128)(2,1)} %features_ref.1) | copy-start | bytes 196612
  7.3 4.4 %copy-start.2 = (bf16[8,2,128,128]{3,2,1,0:T(8,128)(2,1)S(1)}, bf16[8,2,128,128]{3,2,1,0:T(8,128)(2,1)}, u32[]{:S(2)}) copy-start(bf16[8,2,128,128]{3,2,1,0:T(8,128)(2,1)} %vals_ref.3) | copy-start | bytes 1572868
  10.1 0.7 %copy-start.6 = (s32[8,2]{0,1:T(2,128)S(1)}, s32[8,2]{0,1:T(2,128)}, u32[]{:S(2)}) copy-start(s32[8,2]{0,1:T(2,128)} %param.6) | copy-start | bytes 196
  10.1 1.6 %collective-permute-start.3 = (bf16[1024,128]{1,0:T(8,128)(2,1)S(1)}, bf16[1024,128]{1,0:T(8,128)(2,1)S(1)}, u32[]{:S(2)}, u32[]{:S(2)}) collective-permute-start(bf16[1024,128]{1,0:T(8,128)(2,1)S(1)} %shard_map.88._.mine_ref), channel_id=1, source_target_pairs={{0,1},{1,0},{2,3},{3,2},{4,5},{5,4},{6,7},{7,6},{8,9},{9,8},{10,11... | collective-permute-start | bytes 786440 | tf_op jit(solution)/shard_map/ppermute | solution.py:17
  12.0 7.8 %collective-permute-start.4 = (bf16[256,128]{1,0:T(8,128)(2,1)S(1)}, bf16[256,128]{1,0:T(8,128)(2,1)S(1)}, u32[]{:S(2)}, u32[]{:S(2)}) collective-permute-start(bf16[256,128]{1,0:T(8,128)(2,1)S(1)} %get-tuple-element.30), channel_id=1, source_target_pairs={{0,16},{8,24},{16,0},{24,8},{1,17},{9,25},{17,1},{25,9},{2,18},{10... | collective-permute-start | bytes 196616 | tf_op jit(solution)/shard_map/ppermute | solution.py:17
  14.7 6.4 %collective-permute-start.5 = (bf16[256,128]{1,0:T(8,128)(2,1)S(1)}, bf16[256,128]{1,0:T(8,128)(2,1)S(1)}, u32[]{:S(2)}, u32[]{:S(2)}) collective-permute-start(bf16[256,128]{1,0:T(8,128)(2,1)S(1)} %get-tuple-element.31), channel_id=1, source_target_pairs={{0,24},{8,16},{16,8},{24,0},{1,25},{9,17},{17,9},{25,1},{2,26},{10... | collective-permute-start | bytes 196616 | tf_op jit(solution)/shard_map/ppermute | solution.py:17
  16.0 5.4 %collective-permute-start.6 = (bf16[256,128]{1,0:T(8,128)(2,1)S(1)}, bf16[256,128]{1,0:T(8,128)(2,1)S(1)}, u32[]{:S(2)}, u32[]{:S(2)}) collective-permute-start(bf16[256,128]{1,0:T(8,128)(2,1)S(1)} %get-tuple-element.32), channel_id=1, source_target_pairs={{0,8},{8,0},{16,24},{24,16},{1,9},{9,1},{17,25},{25,17},{2,10},{10... | collective-permute-start | bytes 196616 | tf_op jit(solution)/shard_map/ppermute | solution.py:17
  19.8 5.4 %copy-start = (bf16[1024,128]{1,0:T(8,128)(2,1)S(1)}, bf16[1024,128]{1,0:T(8,128)(2,1)}, u32[]{:S(2)}) copy-start(bf16[1024,128]{1,0:T(8,128)(2,1)} %cotangent_ref.7) | copy-start | bytes 786436
  21.1 4.1 %copy-start.3 = (bf16[128,128]{1,0:T(8,128)(2,1)S(1)}, bf16[128,128]{1,0:T(8,128)(2,1)}, u32[]{:S(2)}) copy-start(bf16[128,128]{1,0:T(8,128)(2,1)} %weight_ref.7) | copy-start | bytes 98308
  21.4 6.7 %collective-permute-start.7 = (bf16[256,128]{1,0:T(8,128)(2,1)S(1)}, bf16[256,128]{1,0:T(8,128)(2,1)S(1)}, u32[]{:S(2)}, u32[]{:S(2)}) collective-permute-start(bf16[256,128]{1,0:T(8,128)(2,1)S(1)} %shard_map.93.refs_0_), channel_id=1, source_target_pairs={{0,16},{8,24},{16,0},{24,8},{1,17},{9,25},{17,1},{25,9},{2,18},{10... | collective-permute-start | bytes 196616 | tf_op jit(solution)/shard_map/ppermute | solution.py:17
  24.1 6.3 %collective-permute-start.8 = (bf16[256,128]{1,0:T(8,128)(2,1)S(1)}, bf16[256,128]{1,0:T(8,128)(2,1)S(1)}, u32[]{:S(2)}, u32[]{:S(2)}) collective-permute-start(bf16[256,128]{1,0:T(8,128)(2,1)S(1)} %shard_map.93.refs_0_), channel_id=1, source_target_pairs={{0,24},{8,16},{16,8},{24,0},{1,25},{9,17},{17,9},{25,1},{2,26},{10... | collective-permute-start | bytes 196616 | tf_op jit(solution)/shard_map/ppermute | solution.py:17
  24.7 6.2 %collective-permute-start.9 = (bf16[256,128]{1,0:T(8,128)(2,1)S(1)}, bf16[256,128]{1,0:T(8,128)(2,1)S(1)}, u32[]{:S(2)}, u32[]{:S(2)}) collective-permute-start(bf16[256,128]{1,0:T(8,128)(2,1)S(1)} %shard_map.93.refs_0_), channel_id=1, source_target_pairs={{0,8},{8,0},{16,24},{24,16},{1,9},{9,1},{17,25},{25,17},{2,10},{10... | collective-permute-start | bytes 196616 | tf_op jit(solution)/shard_map/ppermute | solution.py:17
  25.2 0.7 %copy-start.5 = (f32[128]{0:T(128)S(1)}, f32[128]{0:T(128)}, u32[]{:S(2)}) copy-start(f32[128]{0:T(128)} %param.10) | copy-start | bytes 1540
  31.5 1.4 %collective-permute-start.10 = (bf16[384,128]{1,0:T(8,128)(2,1)S(1)}, bf16[384,128]{1,0:T(8,128)(2,1)S(1)}, u32[]{:S(2)}, u32[]{:S(2)}) collective-permute-start(bf16[384,128]{1,0:T(8,128)(2,1)S(1)} %get-tuple-element.44.sent_ref), channel_id=1, source_target_pairs={{0,1},{1,0},{2,3},{3,2},{4,5},{5,4},{6,7},{7,6},{8,9},{9,8},{10,11... | collective-permute-start | bytes 294920 | tf_op jit(solution)/shard_map/ppermute | solution.py:17
  31.6 2.8 %collective-permute-start.11 = (bf16[768,128]{1,0:T(8,128)(2,1)S(1)}, bf16[768,128]{1,0:T(8,128)(2,1)S(1)}, u32[]{:S(2)}, u32[]{:S(2)}) collective-permute-start(bf16[768,128]{1,0:T(8,128)(2,1)S(1)} %get-tuple-element.45), channel_id=1, source_target_pairs={{0,1},{1,0},{2,3},{3,2},{4,5},{5,4},{6,7},{7,6},{8,9},{9,8},{10,11... | collective-permute-start | bytes 589832 | tf_op jit(solution)/shard_map/ppermute | solution.py:17
  32.9 5.3 %collective-permute-start.12 = (bf16[384,128]{1,0:T(8,128)(2,1)S(1)}, bf16[384,128]{1,0:T(8,128)(2,1)S(1)}, u32[]{:S(2)}, u32[]{:S(2)}) collective-permute-start(bf16[384,128]{1,0:T(8,128)(2,1)S(1)} %shard_map.99.first_ref.sent_ref), channel_id=1, source_target_pairs={{0,2},{1,5},{2,0},{3,7},{4,6},{5,1},{6,4},{7,3},{8,10},{9,13},{10,... | collective-permute-start | bytes 294920 | tf_op jit(solution)/shard_map/ppermute | solution.py:25
  34.4 6.5 %collective-permute-start.13 = (bf16[384,128]{1,0:T(8,128)(2,1)S(1)}, bf16[384,128]{1,0:T(8,128)(2,1)S(1)}, u32[]{:S(2)}, u32[]{:S(2)}) collective-permute-start(bf16[384,128]{1,0:T(8,128)(2,1)S(1)} %get-tuple-element.47), channel_id=1, source_target_pairs={{0,6},{1,7},{2,4},{3,5},{4,2},{5,3},{6,0},{7,1},{8,14},{9,15},{10,... | collective-permute-start | bytes 294920 | tf_op jit(solution)/shard_map/ppermute | solution.py:25
  35.3 5.7 %collective-permute-start.14 = (bf16[384,128]{1,0:T(8,128)(2,1)S(1)}, bf16[384,128]{1,0:T(8,128)(2,1)S(1)}, u32[]{:S(2)}, u32[]{:S(2)}) collective-permute-start(bf16[384,128]{1,0:T(8,128)(2,1)S(1)} %get-tuple-element.48), channel_id=1, source_target_pairs={{0,4},{1,3},{2,6},{3,1},{4,0},{5,7},{6,2},{7,5},{8,12},{9,11},{10,... | collective-permute-start | bytes 294920 | tf_op jit(solution)/shard_map/ppermute | solution.py:25

commit v13 on v11

--- a/solution.py
+++ b/solution.py
@@ -35,7 +35,8 @@
         for k in range(count):
             col = cols_ref[k, row] - lax.axis_index("rep") * (own_blocks * dom)
             owner = lax.div(col, jnp.int32(own_blocks)) ^ lax.axis_index("dom")
-            place = ((owner & 1) * (dom // 2) + (owner >> 1)) * own_blocks
+            side = jnp.where(owner > 1, 1 - (owner & 1), owner)
+            place = (side * (dom // 2) + (owner >> 1)) * own_blocks
             place += lax.rem(col, jnp.int32(own_blocks))
             place_ref[row * count + k : row * count + k + 1, :] = jnp.full((1, 128), place, jnp.int32)
 
@@ -224,7 +225,7 @@
         nodes_in = sum(v.shape[0] for v in values)
         return call(join_kernel, shape((nodes_in, width), BF16), [VMEM] * len(values))(*values)
 
-    across = [swap(features, "dom", 2 * chip) for chip in range(1, chips)]
+    across = [swap(features, "dom", 2 * chip + 1) for chip in range(1, chips)]
     front = join(own, across[-1])
     middle = join(*across[chips // 2 - 1 : -1], front)
     mine = call(last_join_kernel, shape((chips * nodes, width), BF16), [VMEM] * (chips // 2))(
@@ -279,7 +280,7 @@
         rest_pair_kernel, [shape((nodes, width), F32)] + [message] * (chips - 2), [VMEM] * 3, cost=1000000000
     )(contrib, sends[0], got_rest)
     sends = others + sends
-    got = {chip: swap(sends[chip - 1], "dom", 2 * chip) for chip in range(chips - 1, 0, -1)}
+    got = {chip: swap(sends[chip - 1], "dom", 2 * chip + 1) for chip in range(chips - 1, 0, -1)}
     output = call(
         functools.partial(order_kernel, list(pieces)), shape((rows * size, width), BF16), [VMEM] * rep
     )(*outputs)

time: 41.4 us -> 41.3 us (level)
  waiting for transfers between devices: 15.9 us -> 16.6 us
  starting transfers between devices: 16.9 us -> 16.2 us
    ppermute x15, starting transfers between devices: 16.9 us -> 16.2 us  [swap(): return lax.ppermute(value, axis, [(i, i ^ distance) for i in range(size)])]
    ppermute x15, waiting for transfers between devices: 15.9 us -> 16.6 us  [swap(): return lax.ppermute(value, axis, [(i, i ^ distance) for i in range(size)])]
  transfers between devices with their start and end apart: 15 -> 15, of which waited for: 12 -> 11; matrix products, arithmetic and copies ran while one was open for 0% -> 0% of each run, Pallas kernels for 7% -> 7%
where the time goes in v13:
time: 41.3 us; the launch traced here: 41.1 us
  waiting for transfers between devices  16.6 us (40%)
  starting transfers between devices  16.2 us (39%)
  Pallas kernels  4.44 us (11%)
  local copies, waits for them, and re-layouts  3.04 us (7%)
  between operations  0.8 us (2%)
    ppermute x15, waiting for transfers between devices, swap(): return lax.ppermute(value, axis, [(i, i ^ distance) for i in range(size)])  16.6 us
    ppermute x15, starting transfers between devices, swap(): return lax.ppermute(value, axis, [(i, i ^ distance) for i in range(size)])  16.2 us
    unnamed x14, local copies, waits for them, and re-layouts  3.04 us
    pallas_call x4, Pallas kernels, body(): call(functools.partial(layer_kernel, rep, count, own_blocks, j), outs, [V...  2.11 us
  transfers between devices with their start and end apart: 15, of which 11 were waited for; matrix products, arithmetic and copies ran while one was open for 0% of the time, Pallas kernels for 7%

profile of v13, /device:TPU:0, one launch (start us, length us, event | category | flops | bytes accessed | tf_op | source)
XLA Modules:
  0.0 41.1 jit_solution(15754122920055395471)
XLA Ops:
  0.6 3.4 %collective-permute-start.2 = (bf16[256,128]{1,0:T(8,128)(2,1)}, bf16[256,128]{1,0:T(8,128)(2,1)S(1)}, u32[]{:S(2)}, u32[]{:S(2)}) collective-permute-start(bf16[256,128]{1,0:T(8,128)(2,1)} %features_ref.1), channel_id=1, source_target_pairs={{0,7},{1,6},{2,5},{3,4},{4,3},{5,2},{6,1},{7,0},{8,15},{9,14},{10,... | collective-permute-start | bytes 196616 | tf_op jit(solution)/shard_map/ppermute | solution.py:17
  4.0 0.8 %collective-permute-start.1 = (bf16[256,128]{1,0:T(8,128)(2,1)}, bf16[256,128]{1,0:T(8,128)(2,1)S(1)}, u32[]{:S(2)}, u32[]{:S(2)}) collective-permute-start(bf16[256,128]{1,0:T(8,128)(2,1)} %features_ref.1), channel_id=1, source_target_pairs={{0,5},{1,4},{2,7},{3,6},{4,1},{5,0},{6,3},{7,2},{8,13},{9,12},{10,... | collective-permute-start | bytes 196616 | tf_op jit(solution)/shard_map/ppermute | solution.py:17
  5.0 1.0 %copy-done.1 = bf16[8,2,128,128]{3,2,1,0:T(8,128)(2,1)S(1)} copy-done((bf16[8,2,128,128]{3,2,1,0:T(8,128)(2,1)S(1)}, bf16[8,2,128,128]{3,2,1,0:T(8,128)(2,1)}, u32[]{:S(2)}) %copy-start.1) | copy-done | bytes 524312
  6.0 0.8 %copy-done.4 = bf16[256,128]{1,0:T(8,128)(2,1)S(1)} copy-done((bf16[256,128]{1,0:T(8,128)(2,1)S(1)}, bf16[256,128]{1,0:T(8,128)(2,1)}, u32[]{:S(2)}) %copy-start.4) | copy-done | bytes 65560
  7.1 1.1 %collective-permute-done.1.refs_0_ = bf16[256,128]{1,0:T(8,128)(2,1)S(1)} collective-permute-done((bf16[256,128]{1,0:T(8,128)(2,1)}, bf16[256,128]{1,0:T(8,128)(2,1)S(1)}, u32[]{:S(2)}, u32[]{:S(2)}) %collective-permute-start.1) | collective-permute-done | bytes 65568 | tf_op jit(solution)/shard_map/ppermute | solution.py:17
  8.2 1.1 %collective-permute-done.refs_0_ = bf16[256,128]{1,0:T(8,128)(2,1)S(1)} collective-permute-done((bf16[256,128]{1,0:T(8,128)(2,1)}, bf16[256,128]{1,0:T(8,128)(2,1)S(1)}, u32[]{:S(2)}, u32[]{:S(2)}) %collective-permute-start) | collective-permute-done | bytes 65568 | tf_op jit(solution)/shard_map/ppermute | solution.py:17
  10.2 0.7 %collective-permute-done.3.far_ref = bf16[1024,128]{1,0:T(8,128)(2,1)S(1)} collective-permute-done((bf16[1024,128]{1,0:T(8,128)(2,1)S(1)}, bf16[1024,128]{1,0:T(8,128)(2,1)S(1)}, u32[]{:S(2)}, u32[]{:S(2)}) %collective-permute-start.3) | collective-permute-done | bytes 262176 | tf_op jit(solution)/shard_map/ppermute | solution.py:17
  11.3 2.7 %collective-permute-start.4 = (bf16[256,128]{1,0:T(8,128)(2,1)S(1)}, bf16[256,128]{1,0:T(8,128)(2,1)S(1)}, u32[]{:S(2)}, u32[]{:S(2)}) collective-permute-start(bf16[256,128]{1,0:T(8,128)(2,1)S(1)} %get-tuple-element.30), channel_id=1, source_target_pairs={{0,16},{8,24},{16,0},{24,8},{1,17},{9,25},{17,1},{25,9},{2,18},{10... | collective-permute-start | bytes 196616 | tf_op jit(solution)/shard_map/ppermute | solution.py:17
  14.0 1.3 %collective-permute-start.5 = (bf16[256,128]{1,0:T(8,128)(2,1)S(1)}, bf16[256,128]{1,0:T(8,128)(2,1)S(1)}, u32[]{:S(2)}, u32[]{:S(2)}) collective-permute-start(bf16[256,128]{1,0:T(8,128)(2,1)S(1)} %get-tuple-element.31), channel_id=1, source_target_pairs={{0,24},{8,16},{16,8},{24,0},{1,25},{9,17},{17,9},{25,1},{2,26},{10... | collective-permute-start | bytes 196616 | tf_op jit(solution)/shard_map/ppermute | solution.py:17
  15.6 3.5 %collective-permute-done.4.b_ref = bf16[256,128]{1,0:T(8,128)(2,1)S(1)} collective-permute-done((bf16[256,128]{1,0:T(8,128)(2,1)S(1)}, bf16[256,128]{1,0:T(8,128)(2,1)S(1)}, u32[]{:S(2)}, u32[]{:S(2)}) %collective-permute-start.4) | collective-permute-done | bytes 65568 | tf_op jit(solution)/shard_map/ppermute | solution.py:17
  19.2 1.3 %collective-permute-done.5.b_ref = bf16[256,128]{1,0:T(8,128)(2,1)S(1)} collective-permute-done((bf16[256,128]{1,0:T(8,128)(2,1)S(1)}, bf16[256,128]{1,0:T(8,128)(2,1)S(1)}, u32[]{:S(2)}, u32[]{:S(2)}) %collective-permute-start.5) | collective-permute-done | bytes 65568 | tf_op jit(solution)/shard_map/ppermute | solution.py:17
  20.8 2.7 %collective-permute-start.7 = (bf16[256,128]{1,0:T(8,128)(2,1)S(1)}, bf16[256,128]{1,0:T(8,128)(2,1)S(1)}, u32[]{:S(2)}, u32[]{:S(2)}) collective-permute-start(bf16[256,128]{1,0:T(8,128)(2,1)S(1)} %shard_map.93.refs_0_), channel_id=1, source_target_pairs={{0,16},{8,24},{16,0},{24,8},{1,17},{9,25},{17,1},{25,9},{2,18},{10... | collective-permute-start | bytes 196616 | tf_op jit(solution)/shard_map/ppermute | solution.py:17
  23.4 0.6 %collective-permute-start.8 = (bf16[256,128]{1,0:T(8,128)(2,1)S(1)}, bf16[256,128]{1,0:T(8,128)(2,1)S(1)}, u32[]{:S(2)}, u32[]{:S(2)}) collective-permute-start(bf16[256,128]{1,0:T(8,128)(2,1)S(1)} %shard_map.93.refs_0_), channel_id=1, source_target_pairs={{0,24},{8,16},{16,8},{24,0},{1,25},{9,17},{17,9},{25,1},{2,26},{10... | collective-permute-start | bytes 196616 | tf_op jit(solution)/shard_map/ppermute | solution.py:17
  24.6 0.6 %copy-done.5 = f32[128]{0:T(128)S(1)} copy-done((f32[128]{0:T(128)S(1)}, f32[128]{0:T(128)}, u32[]{:S(2)}) %copy-start.5) | copy-done | bytes 536
  25.7 1.7 %collective-permute-done.7.refs_0_ = bf16[256,128]{1,0:T(8,128)(2,1)S(1)} collective-permute-done((bf16[256,128]{1,0:T(8,128)(2,1)S(1)}, bf16[256,128]{1,0:T(8,128)(2,1)S(1)}, u32[]{:S(2)}, u32[]{:S(2)}) %collective-permute-start.7) | collective-permute-done | bytes 65568 | tf_op jit(solution)/shard_map/ppermute | solution.py:17
  28.0 1.8 %collective-permute-done.8.refs_0_ = bf16[256,128]{1,0:T(8,128)(2,1)S(1)} collective-permute-done((bf16[256,128]{1,0:T(8,128)(2,1)S(1)}, bf16[256,128]{1,0:T(8,128)(2,1)S(1)}, u32[]{:S(2)}, u32[]{:S(2)}) %collective-permute-start.8) | collective-permute-done | bytes 65568 | tf_op jit(solution)/shard_map/ppermute | solution.py:17
  30.3 0.6 %shard_map.97 = (bf16[256,128]{1,0:T(8,128)(2,1)S(1)}, f32[16,128,128]{2,1,0:T(8,128)S(1)}, bf16[384,128]{1,0:T(8,128)(2,1)S(1)}, bf16[768,128]{1,0:T(8,128)(2,1)S(1)}) custom-call(s32[16,128]{1,0:T(8,128)S(1)} %shard_map.89.place_ref, bf16[8,256,128]{2,1,0:T(8,128)(2,1)S(1)} %get-tuple-element.28.flipped_ref, ...), custom_call_target="tpu_custom_call", output_to_operand_aliasing={{1}: (6, {})} | custom-call | tf_op jit(solution)/shard_map/pallas_call | solution.py:267
  31.4 0.8 %collective-permute-done.10.got_ref = bf16[384,128]{1,0:T(8,128)(2,1)S(1)} collective-permute-done((bf16[384,128]{1,0:T(8,128)(2,1)S(1)}, bf16[384,128]{1,0:T(8,128)(2,1)S(1)}, u32[]{:S(2)}, u32[]{:S(2)}) %collective-permute-start.10) | collective-permute-done | bytes 98336 | tf_op jit(solution)/shard_map/ppermute | solution.py:17
  32.2 1.3 %collective-permute-start.14 = (bf16[384,128]{1,0:T(8,128)(2,1)S(1)}, bf16[384,128]{1,0:T(8,128)(2,1)S(1)}, u32[]{:S(2)}, u32[]{:S(2)}) collective-permute-start(bf16[384,128]{1,0:T(8,128)(2,1)S(1)} %shard_map.99.first_ref.sent_ref), channel_id=1, source_target_pairs={{0,7},{1,6},{2,5},{3,4},{4,3},{5,2},{6,1},{7,0},{8,15},{9,14},{10,... | collective-permute-start | bytes 294920 | tf_op jit(solution)/shard_map/ppermute | solution.py:17
  33.6 1.3 %collective-permute-start.13 = (bf16[384,128]{1,0:T(8,128)(2,1)S(1)}, bf16[384,128]{1,0:T(8,128)(2,1)S(1)}, u32[]{:S(2)}, u32[]{:S(2)}) collective-permute-start(bf16[384,128]{1,0:T(8,128)(2,1)S(1)} %get-tuple-element.48), channel_id=1, source_target_pairs={{0,5},{1,4},{2,7},{3,6},{4,1},{5,0},{6,3},{7,2},{8,13},{9,12},{10,... | collective-permute-start | bytes 294920 | tf_op jit(solution)/shard_map/ppermute | solution.py:17
  35.4 0.7 %shard_map.98 = bf16[1024,128]{1,0:T(8,128)(2,1)} custom-call(bf16[256,128]{1,0:T(8,128)(2,1)S(1)} %get-tuple-element.33.refs_0_, bf16[256,128]{1,0:T(8,128)(2,1)S(1)} %get-tuple-element.36.refs_1_, bf16[256,128]{1,0:T(8,128)(2,1)S(1)} %get-tuple-element.39.refs_2_, bf16[256,128]{1,0:T(8,128)(2,1)S(1)} %get-tuple-element.42.refs_3_), custom_call_target="tpu_custom_call" | custom-call | tf_op jit(solution)/shard_map/pallas_call | solution.py:284
  36.1 1.9 %collective-permute-done.14.got_ref = bf16[384,128]{1,0:T(8,128)(2,1)S(1)} collective-permute-done((bf16[384,128]{1,0:T(8,128)(2,1)S(1)}, bf16[384,128]{1,0:T(8,128)(2,1)S(1)}, u32[]{:S(2)}, u32[]{:S(2)}) %collective-permute-start.14) | collective-permute-done | bytes 98336 | tf_op jit(solution)/shard_map/ppermute | solution.py:17
  38.1 2.3 %collective-permute-done.13.refs_0_ = bf16[384,128]{1,0:T(8,128)(2,1)S(1)} collective-permute-done((bf16[384,128]{1,0:T(8,128)(2,1)S(1)}, bf16[384,128]{1,0:T(8,128)(2,1)S(1)}, u32[]{:S(2)}, u32[]{:S(2)}) %collective-permute-start.13) | collective-permute-done | bytes 98336 | tf_op jit(solution)/shard_map/ppermute | solution.py:17
  40.4 0.7 %shard_map.103 = (f32[256,128]{1,0:T(8,128)}, f32[128,128]{1,0:T(8,128)}) custom-call(f32[256,128]{1,0:T(8,128)S(1)} %get-tuple-element.46.own_ref, bf16[384,128]{1,0:T(8,128)(2,1)S(1)} %shard_map.99.first_ref.sent_ref, bf16[384,128]{1,0:T(8,128)(2,1)S(1)} %collective-permute-done.12.got_ref, f32[384,128]{1,0:T(8,128)S(1)} %shard_map.102.refs_0_), custom_call_target="tpu_custom_call" | custom-call | tf_op jit(solution)/shard_map/pallas_call | solution.py:293
  (39 shorter events, 5.4 us)
Async XLA Ops:
  0.6 6.4 %collective-permute-start.2 = (bf16[256,128]{1,0:T(8,128)(2,1)}, bf16[256,128]{1,0:T(8,128)(2,1)S(1)}, u32[]{:S(2)}, u32[]{:S(2)}) collective-permute-start(bf16[256,128]{1,0:T(8,128)(2,1)} %features_ref.1), channel_id=1, source_target_pairs={{0,7},{1,6},{2,5},{3,4},{4,3},{5,2},{6,1},{7,0},{8,15},{9,14},{10,... | collective-permute-start | bytes 196616 | tf_op jit(solution)/shard_map/ppermute | solution.py:17
  4.0 4.2 %collective-permute-start.1 = (bf16[256,128]{1,0:T(8,128)(2,1)}, bf16[256,128]{1,0:T(8,128)(2,1)S(1)}, u32[]{:S(2)}, u32[]{:S(2)}) collective-permute-start(bf16[256,128]{1,0:T(8,128)(2,1)} %features_ref.1), channel_id=1, source_target_pairs={{0,5},{1,4},{2,7},{3,6},{4,1},{5,0},{6,3},{7,2},{8,13},{9,12},{10,... | collective-permute-start | bytes 196616 | tf_op jit(solution)/shard_map/ppermute | solution.py:17
  4.8 4.5 %collective-permute-start = (bf16[256,128]{1,0:T(8,128)(2,1)}, bf16[256,128]{1,0:T(8,128)(2,1)S(1)}, u32[]{:S(2)}, u32[]{:S(2)}) collective-permute-start(bf16[256,128]{1,0:T(8,128)(2,1)} %features_ref.1), channel_id=1, source_target_pairs={{0,3},{1,2},{2,1},{3,0},{4,7},{5,6},{6,5},{7,4},{8,11},{9,10},{10,... | collective-permute-start | bytes 196616 | tf_op jit(solution)/shard_map/ppermute | solution.py:17
  5.0 1.0 %copy-start.1 = (bf16[8,2,128,128]{3,2,1,0:T(8,128)(2,1)S(1)}, bf16[8,2,128,128]{3,2,1,0:T(8,128)(2,1)}, u32[]{:S(2)}) copy-start(bf16[8,2,128,128]{3,2,1,0:T(8,128)(2,1)} %vals_ref.3) | copy-start | bytes 1572868
  6.0 0.8 %copy-start.4 = (bf16[256,128]{1,0:T(8,128)(2,1)S(1)}, bf16[256,128]{1,0:T(8,128)(2,1)}, u32[]{:S(2)}) copy-start(bf16[256,128]{1,0:T(8,128)(2,1)} %features_ref.1) | copy-start | bytes 196612
  7.1 3.9 %copy-start.2 = (bf16[8,2,128,128]{3,2,1,0:T(8,128)(2,1)S(1)}, bf16[8,2,128,128]{3,2,1,0:T(8,128)(2,1)}, u32[]{:S(2)}) copy-start(bf16[8,2,128,128]{3,2,1,0:T(8,128)(2,1)} %vals_ref.3) | copy-start | bytes 1572868
  9.4 0.7 %copy-start.6 = (s32[8,2]{0,1:T(2,128)S(1)}, s32[8,2]{0,1:T(2,128)}, u32[]{:S(2)}) copy-start(s32[8,2]{0,1:T(2,128)} %param.6) | copy-start | bytes 196
  9.4 1.6 %collective-permute-start.3 = (bf16[1024,128]{1,0:T(8,128)(2,1)S(1)}, bf16[1024,128]{1,0:T(8,128)(2,1)S(1)}, u32[]{:S(2)}, u32[]{:S(2)}) collective-permute-start(bf16[1024,128]{1,0:T(8,128)(2,1)S(1)} %shard_map.88._.mine_ref), channel_id=1, source_target_pairs={{0,1},{1,0},{2,3},{3,2},{4,5},{5,4},{6,7},{7,6},{8,9},{9,8},{10,11... | collective-permute-start | bytes 786440 | tf_op jit(solution)/shard_map/ppermute | solution.py:17
  11.3 7.8 %collective-permute-start.4 = (bf16[256,128]{1,0:T(8,128)(2,1)S(1)}, bf16[256,128]{1,0:T(8,128)(2,1)S(1)}, u32[]{:S(2)}, u32[]{:S(2)}) collective-permute-start(bf16[256,128]{1,0:T(8,128)(2,1)S(1)} %get-tuple-element.30), channel_id=1, source_target_pairs={{0,16},{8,24},{16,0},{24,8},{1,17},{9,25},{17,1},{25,9},{2,18},{10... | collective-permute-start | bytes 196616 | tf_op jit(solution)/shard_map/ppermute | solution.py:17
  14.0 6.4 %collective-permute-start.5 = (bf16[256,128]{1,0:T(8,128)(2,1)S(1)}, bf16[256,128]{1,0:T(8,128)(2,1)S(1)}, u32[]{:S(2)}, u32[]{:S(2)}) collective-permute-start(bf16[256,128]{1,0:T(8,128)(2,1)S(1)} %get-tuple-element.31), channel_id=1, source_target_pairs={{0,24},{8,16},{16,8},{24,0},{1,25},{9,17},{17,9},{25,1},{2,26},{10... | collective-permute-start | bytes 196616 | tf_op jit(solution)/shard_map/ppermute | solution.py:17
  15.3 5.4 %collective-permute-start.6 = (bf16[256,128]{1,0:T(8,128)(2,1)S(1)}, bf16[256,128]{1,0:T(8,128)(2,1)S(1)}, u32[]{:S(2)}, u32[]{:S(2)}) collective-permute-start(bf16[256,128]{1,0:T(8,128)(2,1)S(1)} %get-tuple-element.32), channel_id=1, source_target_pairs={{0,8},{8,0},{16,24},{24,16},{1,9},{9,1},{17,25},{25,17},{2,10},{10... | collective-permute-start | bytes 196616 | tf_op jit(solution)/shard_map/ppermute | solution.py:17
  19.1 5.4 %copy-start = (bf16[1024,128]{1,0:T(8,128)(2,1)S(1)}, bf16[1024,128]{1,0:T(8,128)(2,1)}, u32[]{:S(2)}) copy-start(bf16[1024,128]{1,0:T(8,128)(2,1)} %cotangent_ref.7) | copy-start | bytes 786436
  20.4 4.1 %copy-start.3 = (bf16[128,128]{1,0:T(8,128)(2,1)S(1)}, bf16[128,128]{1,0:T(8,128)(2,1)}, u32[]{:S(2)}) copy-start(bf16[128,128]{1,0:T(8,128)(2,1)} %weight_ref.7) | copy-start | bytes 98308
  20.8 6.7 %collective-permute-start.7 = (bf16[256,128]{1,0:T(8,128)(2,1)S(1)}, bf16[256,128]{1,0:T(8,128)(2,1)S(1)}, u32[]{:S(2)}, u32[]{:S(2)}) collective-permute-start(bf16[256,128]{1,0:T(8,128)(2,1)S(1)} %shard_map.93.refs_0_), channel_id=1, source_target_pairs={{0,16},{8,24},{16,0},{24,8},{1,17},{9,25},{17,1},{25,9},{2,18},{10... | collective-permute-start | bytes 196616 | tf_op jit(solution)/shard_map/ppermute | solution.py:17
  23.4 6.3 %collective-permute-start.8 = (bf16[256,128]{1,0:T(8,128)(2,1)S(1)}, bf16[256,128]{1,0:T(8,128)(2,1)S(1)}, u32[]{:S(2)}, u32[]{:S(2)}) collective-permute-start(bf16[256,128]{1,0:T(8,128)(2,1)S(1)} %shard_map.93.refs_0_), channel_id=1, source_target_pairs={{0,24},{8,16},{16,8},{24,0},{1,25},{9,17},{17,9},{25,1},{2,26},{10... | collective-permute-start | bytes 196616 | tf_op jit(solution)/shard_map/ppermute | solution.py:17
  24.1 6.2 %collective-permute-start.9 = (bf16[256,128]{1,0:T(8,128)(2,1)S(1)}, bf16[256,128]{1,0:T(8,128)(2,1)S(1)}, u32[]{:S(2)}, u32[]{:S(2)}) collective-permute-start(bf16[256,128]{1,0:T(8,128)(2,1)S(1)} %shard_map.93.refs_0_), channel_id=1, source_target_pairs={{0,8},{8,0},{16,24},{24,16},{1,9},{9,1},{17,25},{25,17},{2,10},{10... | collective-permute-start | bytes 196616 | tf_op jit(solution)/shard_map/ppermute | solution.py:17
  24.5 0.7 %copy-start.5 = (f32[128]{0:T(128)S(1)}, f32[128]{0:T(128)}, u32[]{:S(2)}) copy-start(f32[128]{0:T(128)} %param.10) | copy-start | bytes 1540
  30.8 1.4 %collective-permute-start.10 = (bf16[384,128]{1,0:T(8,128)(2,1)S(1)}, bf16[384,128]{1,0:T(8,128)(2,1)S(1)}, u32[]{:S(2)}, u32[]{:S(2)}) collective-permute-start(bf16[384,128]{1,0:T(8,128)(2,1)S(1)} %get-tuple-element.44.sent_ref), channel_id=1, source_target_pairs={{0,1},{1,0},{2,3},{3,2},{4,5},{5,4},{6,7},{7,6},{8,9},{9,8},{10,11... | collective-permute-start | bytes 294920 | tf_op jit(solution)/shard_map/ppermute | solution.py:17
  30.9 2.6 %collective-permute-start.11 = (bf16[768,128]{1,0:T(8,128)(2,1)S(1)}, bf16[768,128]{1,0:T(8,128)(2,1)S(1)}, u32[]{:S(2)}, u32[]{:S(2)}) collective-permute-start(bf16[768,128]{1,0:T(8,128)(2,1)S(1)} %get-tuple-element.45), channel_id=1, source_target_pairs={{0,1},{1,0},{2,3},{3,2},{4,5},{5,4},{6,7},{7,6},{8,9},{9,8},{10,11... | collective-permute-start | bytes 589832 | tf_op jit(solution)/shard_map/ppermute | solution.py:17
  32.2 5.8 %collective-permute-start.14 = (bf16[384,128]{1,0:T(8,128)(2,1)S(1)}, bf16[384,128]{1,0:T(8,128)(2,1)S(1)}, u32[]{:S(2)}, u32[]{:S(2)}) collective-permute-start(bf16[384,128]{1,0:T(8,128)(2,1)S(1)} %shard_map.99.first_ref.sent_ref), channel_id=1, source_target_pairs={{0,7},{1,6},{2,5},{3,4},{4,3},{5,2},{6,1},{7,0},{8,15},{9,14},{10,... | collective-permute-start | bytes 294920 | tf_op jit(solution)/shard_map/ppermute | solution.py:17
  33.6 6.8 %collective-permute-start.13 = (bf16[384,128]{1,0:T(8,128)(2,1)S(1)}, bf16[384,128]{1,0:T(8,128)(2,1)S(1)}, u32[]{:S(2)}, u32[]{:S(2)}) collective-permute-start(bf16[384,128]{1,0:T(8,128)(2,1)S(1)} %get-tuple-element.48), channel_id=1, source_target_pairs={{0,5},{1,4},{2,7},{3,6},{4,1},{5,0},{6,3},{7,2},{8,13},{9,12},{10,... | collective-permute-start | bytes 294920 | tf_op jit(solution)/shard_map/ppermute | solution.py:17
  34.9 5.5 %collective-permute-start.12 = (bf16[384,128]{1,0:T(8,128)(2,1)S(1)}, bf16[384,128]{1,0:T(8,128)(2,1)S(1)}, u32[]{:S(2)}, u32[]{:S(2)}) collective-permute-start(bf16[384,128]{1,0:T(8,128)(2,1)S(1)} %get-tuple-element.47), channel_id=1, source_target_pairs={{0,3},{1,2},{2,1},{3,0},{4,7},{5,6},{6,5},{7,4},{8,11},{9,10},{10,... | collective-permute-start | bytes 294920 | tf_op jit(solution)/shard_map/ppermute | solution.py:17

commit v14 on v13

--- a/solution.py
+++ b/solution.py
@@ -85,7 +85,7 @@
 def layer_kernel(
     rep, count, own_blocks, j, place_ref, flipped_ref, cotangent_ref, weight_ref, bias_ref, *refs
 ):
-    first, last = j == 0, j == 1
+    first, last = j == 0, j == 3
     piece_ref, refs = refs[0], refs[1:]
     if not first:
         (_, sums_in), refs = refs[:2], refs[2:]
@@ -114,18 +114,21 @@
         terms = matmul(flipped_ref[row], grad_agg[i * size : (i + 1) * size], (1, 0))
         for k in range(count):
             contrib[place_ref[row * count + k, 0]] += terms[k * size : (k + 1) * size]
-    if first:
+    if j == 0:
         refs[0][0] = part_sum
         refs[0][1] = jnp.zeros_like(part_sum)
-    elif not last:
+    elif j == 2:
         refs[0][0] = sums_in[0]
-        refs[0][1] = sums_in[1] + part_sum
+        refs[0][1] = part_sum
+    elif j == 1:
+        refs[0][0] = sums_in[0] + part_sum
+        refs[0][1] = sums_in[1]
     else:
         first_ref, rest_ref = refs
         away = contrib[quarter_blocks // 2 :].reshape(quarter_blocks // 2 * size, -1).astype(BF16)
         rest_ref[...] = away[:-nodes]
         first_ref[:nodes] = away[-nodes:]
-        first_ref[nodes:] = ((sums_in[0] + part_sum) + sums_in[1]).astype(BF16)
+        first_ref[nodes:] = (sums_in[0] + (sums_in[1] + part_sum)).astype(BF16)
 
 
 def add_kernel(a_ref, b_ref, out_ref):
@@ -244,10 +247,10 @@
         [VMEM] * 4,
     )(place, vals, mine, far)
     arrived = {j: swap(partials[j], "rep", j) if j else partials[j] for j in range(rep)}
-    order = [*range(2, rep), 1]
+    order = [2, 1, 3]
     own_rows = arrived[0]
     for j in order:
-        own_rows = call(add_kernel, shape((part, width), F32 if j > 1 else BF16), [VMEM] * 2)(
+        own_rows = call(add_kernel, shape((part, width), F32 if j != 3 else BF16), [VMEM] * 2)(
             own_rows, arrived[j]
         )
     pieces = {0: own_rows}
@@ -257,7 +260,7 @@
     outputs, carried = [], []
     for j, piece in pieces.items():
         outs = [shape((part, width), BF16), shape((quarter_blocks, size, width), F32)]
-        if j != 1:
+        if j != 3:
             outs += [shape((2, width, width), F32)]
         else:
             outs += [

time: 41.3 us -> 40.7 us (0.985)
  waiting for transfers between devices: 16.6 us -> 15.1 us
  starting transfers between devices: 16.2 us -> 17.1 us
    ppermute x15, waiting for transfers between devices: 16.6 us -> 15.1 us  [swap(): return lax.ppermute(value, axis, [(i, i ^ distance) for i in range(size)])]
    ppermute x15, starting transfers between devices: 16.2 us -> 17.1 us  [swap(): return lax.ppermute(value, axis, [(i, i ^ distance) for i in range(size)])]
  transfers between devices with their start and end apart: 15 -> 15, of which waited for: 11 -> 12; matrix products, arithmetic and copies ran while one was open for 0% -> 0% of each run, Pallas kernels for 7% -> 7%
where the time goes in v14:
time: 40.7 us; the launch traced here: 40.5 us
  starting transfers between devices  17.1 us (42%)
  waiting for transfers between devices  15.1 us (37%)
  Pallas kernels  4.44 us (11%)
  local copies, waits for them, and re-layouts  3.04 us (7%)
  between operations  0.79 us (2%)
    ppermute x15, starting transfers between devices, swap(): return lax.ppermute(value, axis, [(i, i ^ distance) for i in range(size)])  17.1 us
    ppermute x15, waiting for transfers between devices, swap(): return lax.ppermute(value, axis, [(i, i ^ distance) for i in range(size)])  15.1 us
    unnamed x14, local copies, waits for them, and re-layouts  3.04 us
    pallas_call x4, Pallas kernels, body(): call(functools.partial(layer_kernel, rep, count, own_blocks, j), outs, [V...  2.1 us
  transfers between devices with their start and end apart: 15, of which 12 were waited for; matrix products, arithmetic and copies ran while one was open for 0% of the time, Pallas kernels for 7%

profile of v14, /device:TPU:0, one launch (start us, length us, event | category | flops | bytes accessed | tf_op | source)
XLA Modules:
  0.0 40.5 jit_solution(12640053910752885996)
XLA Ops:
  0.6 3.4 %collective-permute-start.2 = (bf16[256,128]{1,0:T(8,128)(2,1)}, bf16[256,128]{1,0:T(8,128)(2,1)S(1)}, u32[]{:S(2)}, u32[]{:S(2)}) collective-permute-start(bf16[256,128]{1,0:T(8,128)(2,1)} %features_ref.1), channel_id=1, source_target_pairs={{0,7},{1,6},{2,5},{3,4},{4,3},{5,2},{6,1},{7,0},{8,15},{9,14},{10,... | collective-permute-start | bytes 196616 | tf_op jit(solution)/shard_map/ppermute | solution.py:17
  4.0 0.8 %collective-permute-start.1 = (bf16[256,128]{1,0:T(8,128)(2,1)}, bf16[256,128]{1,0:T(8,128)(2,1)S(1)}, u32[]{:S(2)}, u32[]{:S(2)}) collective-permute-start(bf16[256,128]{1,0:T(8,128)(2,1)} %features_ref.1), channel_id=1, source_target_pairs={{0,5},{1,4},{2,7},{3,6},{4,1},{5,0},{6,3},{7,2},{8,13},{9,12},{10,... | collective-permute-start | bytes 196616 | tf_op jit(solution)/shard_map/ppermute | solution.py:17
  5.0 1.0 %copy-done.1 = bf16[8,2,128,128]{3,2,1,0:T(8,128)(2,1)S(1)} copy-done((bf16[8,2,128,128]{3,2,1,0:T(8,128)(2,1)S(1)}, bf16[8,2,128,128]{3,2,1,0:T(8,128)(2,1)}, u32[]{:S(2)}) %copy-start.1) | copy-done | bytes 524312
  6.0 0.8 %copy-done.4 = bf16[256,128]{1,0:T(8,128)(2,1)S(1)} copy-done((bf16[256,128]{1,0:T(8,128)(2,1)S(1)}, bf16[256,128]{1,0:T(8,128)(2,1)}, u32[]{:S(2)}) %copy-start.4) | copy-done | bytes 65560
  7.1 1.1 %collective-permute-done.1.refs_0_ = bf16[256,128]{1,0:T(8,128)(2,1)S(1)} collective-permute-done((bf16[256,128]{1,0:T(8,128)(2,1)}, bf16[256,128]{1,0:T(8,128)(2,1)S(1)}, u32[]{:S(2)}, u32[]{:S(2)}) %collective-permute-start.1) | collective-permute-done | bytes 65568 | tf_op jit(solution)/shard_map/ppermute | solution.py:17
  8.2 1.1 %collective-permute-done.refs_0_ = bf16[256,128]{1,0:T(8,128)(2,1)S(1)} collective-permute-done((bf16[256,128]{1,0:T(8,128)(2,1)}, bf16[256,128]{1,0:T(8,128)(2,1)S(1)}, u32[]{:S(2)}, u32[]{:S(2)}) %collective-permute-start) | collective-permute-done | bytes 65568 | tf_op jit(solution)/shard_map/ppermute | solution.py:17
  10.2 0.7 %collective-permute-done.3.far_ref = bf16[1024,128]{1,0:T(8,128)(2,1)S(1)} collective-permute-done((bf16[1024,128]{1,0:T(8,128)(2,1)S(1)}, bf16[1024,128]{1,0:T(8,128)(2,1)S(1)}, u32[]{:S(2)}, u32[]{:S(2)}) %collective-permute-start.3) | collective-permute-done | bytes 262176 | tf_op jit(solution)/shard_map/ppermute | solution.py:17
  11.3 2.7 %collective-permute-start.4 = (bf16[256,128]{1,0:T(8,128)(2,1)S(1)}, bf16[256,128]{1,0:T(8,128)(2,1)S(1)}, u32[]{:S(2)}, u32[]{:S(2)}) collective-permute-start(bf16[256,128]{1,0:T(8,128)(2,1)S(1)} %get-tuple-element.30), channel_id=1, source_target_pairs={{0,16},{8,24},{16,0},{24,8},{1,17},{9,25},{17,1},{25,9},{2,18},{10... | collective-permute-start | bytes 196616 | tf_op jit(solution)/shard_map/ppermute | solution.py:17
  14.0 1.6 %collective-permute-start.5 = (bf16[256,128]{1,0:T(8,128)(2,1)S(1)}, bf16[256,128]{1,0:T(8,128)(2,1)S(1)}, u32[]{:S(2)}, u32[]{:S(2)}) collective-permute-start(bf16[256,128]{1,0:T(8,128)(2,1)S(1)} %get-tuple-element.31), channel_id=1, source_target_pairs={{0,8},{8,0},{16,24},{24,16},{1,9},{9,1},{17,25},{25,17},{2,10},{10... | collective-permute-start | bytes 196616 | tf_op jit(solution)/shard_map/ppermute | solution.py:17
  15.8 1.9 %collective-permute-done.4.b_ref = bf16[256,128]{1,0:T(8,128)(2,1)S(1)} collective-permute-done((bf16[256,128]{1,0:T(8,128)(2,1)S(1)}, bf16[256,128]{1,0:T(8,128)(2,1)S(1)}, u32[]{:S(2)}, u32[]{:S(2)}) %collective-permute-start.4) | collective-permute-done | bytes 65568 | tf_op jit(solution)/shard_map/ppermute | solution.py:17
  17.7 0.6 %collective-permute-done.5.b_ref = bf16[256,128]{1,0:T(8,128)(2,1)S(1)} collective-permute-done((bf16[256,128]{1,0:T(8,128)(2,1)S(1)}, bf16[256,128]{1,0:T(8,128)(2,1)S(1)}, u32[]{:S(2)}, u32[]{:S(2)}) %collective-permute-start.5) | collective-permute-done | bytes 65568 | tf_op jit(solution)/shard_map/ppermute | solution.py:17
  18.4 3.3 %collective-permute-done.6.b_ref = bf16[256,128]{1,0:T(8,128)(2,1)S(1)} collective-permute-done((bf16[256,128]{1,0:T(8,128)(2,1)S(1)}, bf16[256,128]{1,0:T(8,128)(2,1)S(1)}, u32[]{:S(2)}, u32[]{:S(2)}) %collective-permute-start.6) | collective-permute-done | bytes 65568 | tf_op jit(solution)/shard_map/ppermute | solution.py:17
  21.7 1.7 %collective-permute-start.7 = (bf16[256,128]{1,0:T(8,128)(2,1)S(1)}, bf16[256,128]{1,0:T(8,128)(2,1)S(1)}, u32[]{:S(2)}, u32[]{:S(2)}) collective-permute-start(bf16[256,128]{1,0:T(8,128)(2,1)S(1)} %shard_map.93.refs_0_), channel_id=1, source_target_pairs={{0,16},{8,24},{16,0},{24,8},{1,17},{9,25},{17,1},{25,9},{2,18},{10... | collective-permute-start | bytes 196616 | tf_op jit(solution)/shard_map/ppermute | solution.py:17
  23.6 2.5 %collective-permute-start.9 = (bf16[256,128]{1,0:T(8,128)(2,1)S(1)}, bf16[256,128]{1,0:T(8,128)(2,1)S(1)}, u32[]{:S(2)}, u32[]{:S(2)}) collective-permute-start(bf16[256,128]{1,0:T(8,128)(2,1)S(1)} %shard_map.93.refs_0_), channel_id=1, source_target_pairs={{0,24},{8,16},{16,8},{24,0},{1,25},{9,17},{17,9},{25,1},{2,26},{10... | collective-permute-start | bytes 196616 | tf_op jit(solution)/shard_map/ppermute | solution.py:17
  26.1 0.6 %copy-done.5 = f32[128]{0:T(128)S(1)} copy-done((f32[128]{0:T(128)S(1)}, f32[128]{0:T(128)}, u32[]{:S(2)}) %copy-start.5) | copy-done | bytes 536
  28.0 0.6 %collective-permute-done.8.refs_0_ = bf16[256,128]{1,0:T(8,128)(2,1)S(1)} collective-permute-done((bf16[256,128]{1,0:T(8,128)(2,1)S(1)}, bf16[256,128]{1,0:T(8,128)(2,1)S(1)}, u32[]{:S(2)}, u32[]{:S(2)}) %collective-permute-start.8) | collective-permute-done | bytes 65568 | tf_op jit(solution)/shard_map/ppermute | solution.py:17
  29.1 0.6 %collective-permute-done.9.refs_0_ = bf16[256,128]{1,0:T(8,128)(2,1)S(1)} collective-permute-done((bf16[256,128]{1,0:T(8,128)(2,1)S(1)}, bf16[256,128]{1,0:T(8,128)(2,1)S(1)}, u32[]{:S(2)}, u32[]{:S(2)}) %collective-permute-start.9) | collective-permute-done | bytes 65568 | tf_op jit(solution)/shard_map/ppermute | solution.py:17
  30.8 0.8 %collective-permute-done.10.got_ref = bf16[384,128]{1,0:T(8,128)(2,1)S(1)} collective-permute-done((bf16[384,128]{1,0:T(8,128)(2,1)S(1)}, bf16[384,128]{1,0:T(8,128)(2,1)S(1)}, u32[]{:S(2)}, u32[]{:S(2)}) %collective-permute-start.10) | collective-permute-done | bytes 98336 | tf_op jit(solution)/shard_map/ppermute | solution.py:17
  31.7 1.3 %collective-permute-start.14 = (bf16[384,128]{1,0:T(8,128)(2,1)S(1)}, bf16[384,128]{1,0:T(8,128)(2,1)S(1)}, u32[]{:S(2)}, u32[]{:S(2)}) collective-permute-start(bf16[384,128]{1,0:T(8,128)(2,1)S(1)} %shard_map.99.first_ref.sent_ref), channel_id=1, source_target_pairs={{0,7},{1,6},{2,5},{3,4},{4,3},{5,2},{6,1},{7,0},{8,15},{9,14},{10,... | collective-permute-start | bytes 294920 | tf_op jit(solution)/shard_map/ppermute | solution.py:17
  33.0 1.3 %collective-permute-start.13 = (bf16[384,128]{1,0:T(8,128)(2,1)S(1)}, bf16[384,128]{1,0:T(8,128)(2,1)S(1)}, u32[]{:S(2)}, u32[]{:S(2)}) collective-permute-start(bf16[384,128]{1,0:T(8,128)(2,1)S(1)} %get-tuple-element.48), channel_id=1, source_target_pairs={{0,5},{1,4},{2,7},{3,6},{4,1},{5,0},{6,3},{7,2},{8,13},{9,12},{10,... | collective-permute-start | bytes 294920 | tf_op jit(solution)/shard_map/ppermute | solution.py:17
  34.8 0.7 %shard_map.98 = bf16[1024,128]{1,0:T(8,128)(2,1)} custom-call(bf16[256,128]{1,0:T(8,128)(2,1)S(1)} %get-tuple-element.33.refs_0_, bf16[256,128]{1,0:T(8,128)(2,1)S(1)} %get-tuple-element.36.refs_1_, bf16[256,128]{1,0:T(8,128)(2,1)S(1)} %get-tuple-element.39.refs_2_, bf16[256,128]{1,0:T(8,128)(2,1)S(1)} %get-tuple-element.42.refs_3_), custom_call_target="tpu_custom_call" | custom-call | tf_op jit(solution)/shard_map/pallas_call | solution.py:287
  35.5 1.9 %collective-permute-done.14.got_ref = bf16[384,128]{1,0:T(8,128)(2,1)S(1)} collective-permute-done((bf16[384,128]{1,0:T(8,128)(2,1)S(1)}, bf16[384,128]{1,0:T(8,128)(2,1)S(1)}, u32[]{:S(2)}, u32[]{:S(2)}) %collective-permute-start.14) | collective-permute-done | bytes 98336 | tf_op jit(solution)/shard_map/ppermute | solution.py:17
  37.5 2.3 %collective-permute-done.13.refs_0_ = bf16[384,128]{1,0:T(8,128)(2,1)S(1)} collective-permute-done((bf16[384,128]{1,0:T(8,128)(2,1)S(1)}, bf16[384,128]{1,0:T(8,128)(2,1)S(1)}, u32[]{:S(2)}, u32[]{:S(2)}) %collective-permute-start.13) | collective-permute-done | bytes 98336 | tf_op jit(solution)/shard_map/ppermute | solution.py:17
  39.8 0.7 %shard_map.103 = (f32[256,128]{1,0:T(8,128)}, f32[128,128]{1,0:T(8,128)}) custom-call(f32[256,128]{1,0:T(8,128)S(1)} %get-tuple-element.46.own_ref, bf16[384,128]{1,0:T(8,128)(2,1)S(1)} %shard_map.99.first_ref.sent_ref, bf16[384,128]{1,0:T(8,128)(2,1)S(1)} %collective-permute-done.12.got_ref, f32[384,128]{1,0:T(8,128)S(1)} %shard_map.102.refs_0_), custom_call_target="tpu_custom_call" | custom-call | tf_op jit(solution)/shard_map/pallas_call | solution.py:296
  (39 shorter events, 5.6 us)
Async XLA Ops:
  0.6 6.4 %collective-permute-start.2 = (bf16[256,128]{1,0:T(8,128)(2,1)}, bf16[256,128]{1,0:T(8,128)(2,1)S(1)}, u32[]{:S(2)}, u32[]{:S(2)}) collective-permute-start(bf16[256,128]{1,0:T(8,128)(2,1)} %features_ref.1), channel_id=1, source_target_pairs={{0,7},{1,6},{2,5},{3,4},{4,3},{5,2},{6,1},{7,0},{8,15},{9,14},{10,... | collective-permute-start | bytes 196616 | tf_op jit(solution)/shard_map/ppermute | solution.py:17
  4.0 4.2 %collective-permute-start.1 = (bf16[256,128]{1,0:T(8,128)(2,1)}, bf16[256,128]{1,0:T(8,128)(2,1)S(1)}, u32[]{:S(2)}, u32[]{:S(2)}) collective-permute-start(bf16[256,128]{1,0:T(8,128)(2,1)} %features_ref.1), channel_id=1, source_target_pairs={{0,5},{1,4},{2,7},{3,6},{4,1},{5,0},{6,3},{7,2},{8,13},{9,12},{10,... | collective-permute-start | bytes 196616 | tf_op jit(solution)/shard_map/ppermute | solution.py:17
  4.8 4.5 %collective-permute-start = (bf16[256,128]{1,0:T(8,128)(2,1)}, bf16[256,128]{1,0:T(8,128)(2,1)S(1)}, u32[]{:S(2)}, u32[]{:S(2)}) collective-permute-start(bf16[256,128]{1,0:T(8,128)(2,1)} %features_ref.1), channel_id=1, source_target_pairs={{0,3},{1,2},{2,1},{3,0},{4,7},{5,6},{6,5},{7,4},{8,11},{9,10},{10,... | collective-permute-start | bytes 196616 | tf_op jit(solution)/shard_map/ppermute | solution.py:17
  5.0 1.0 %copy-start.1 = (bf16[8,2,128,128]{3,2,1,0:T(8,128)(2,1)S(1)}, bf16[8,2,128,128]{3,2,1,0:T(8,128)(2,1)}, u32[]{:S(2)}) copy-start(bf16[8,2,128,128]{3,2,1,0:T(8,128)(2,1)} %vals_ref.3) | copy-start | bytes 1572868
  6.0 0.8 %copy-start.4 = (bf16[256,128]{1,0:T(8,128)(2,1)S(1)}, bf16[256,128]{1,0:T(8,128)(2,1)}, u32[]{:S(2)}) copy-start(bf16[256,128]{1,0:T(8,128)(2,1)} %features_ref.1) | copy-start | bytes 196612
  7.1 3.9 %copy-start.2 = (bf16[8,2,128,128]{3,2,1,0:T(8,128)(2,1)S(1)}, bf16[8,2,128,128]{3,2,1,0:T(8,128)(2,1)}, u32[]{:S(2)}) copy-start(bf16[8,2,128,128]{3,2,1,0:T(8,128)(2,1)} %vals_ref.3) | copy-start | bytes 1572868
  9.4 0.7 %copy-start.6 = (s32[8,2]{0,1:T(2,128)S(1)}, s32[8,2]{0,1:T(2,128)}, u32[]{:S(2)}) copy-start(s32[8,2]{0,1:T(2,128)} %param.6) | copy-start | bytes 196
  9.4 1.6 %collective-permute-start.3 = (bf16[1024,128]{1,0:T(8,128)(2,1)S(1)}, bf16[1024,128]{1,0:T(8,128)(2,1)S(1)}, u32[]{:S(2)}, u32[]{:S(2)}) collective-permute-start(bf16[1024,128]{1,0:T(8,128)(2,1)S(1)} %shard_map.88._.mine_ref), channel_id=1, source_target_pairs={{0,1},{1,0},{2,3},{3,2},{4,5},{5,4},{6,7},{7,6},{8,9},{9,8},{10,11... | collective-permute-start | bytes 786440 | tf_op jit(solution)/shard_map/ppermute | solution.py:17
  11.3 6.4 %collective-permute-start.4 = (bf16[256,128]{1,0:T(8,128)(2,1)S(1)}, bf16[256,128]{1,0:T(8,128)(2,1)S(1)}, u32[]{:S(2)}, u32[]{:S(2)}) collective-permute-start(bf16[256,128]{1,0:T(8,128)(2,1)S(1)} %get-tuple-element.30), channel_id=1, source_target_pairs={{0,16},{8,24},{16,0},{24,8},{1,17},{9,25},{17,1},{25,9},{2,18},{10... | collective-permute-start | bytes 196616 | tf_op jit(solution)/shard_map/ppermute | solution.py:17
  14.0 4.3 %collective-permute-start.5 = (bf16[256,128]{1,0:T(8,128)(2,1)S(1)}, bf16[256,128]{1,0:T(8,128)(2,1)S(1)}, u32[]{:S(2)}, u32[]{:S(2)}) collective-permute-start(bf16[256,128]{1,0:T(8,128)(2,1)S(1)} %get-tuple-element.31), channel_id=1, source_target_pairs={{0,8},{8,0},{16,24},{24,16},{1,9},{9,1},{17,25},{25,17},{2,10},{10... | collective-permute-start | bytes 196616 | tf_op jit(solution)/shard_map/ppermute | solution.py:17
  15.6 6.1 %collective-permute-start.6 = (bf16[256,128]{1,0:T(8,128)(2,1)S(1)}, bf16[256,128]{1,0:T(8,128)(2,1)S(1)}, u32[]{:S(2)}, u32[]{:S(2)}) collective-permute-start(bf16[256,128]{1,0:T(8,128)(2,1)S(1)} %get-tuple-element.32), channel_id=1, source_target_pairs={{0,24},{8,16},{16,8},{24,0},{1,25},{9,17},{17,9},{25,1},{2,26},{10... | collective-permute-start | bytes 196616 | tf_op jit(solution)/shard_map/ppermute | solution.py:17
  17.7 8.4 %copy-start = (bf16[1024,128]{1,0:T(8,128)(2,1)S(1)}, bf16[1024,128]{1,0:T(8,128)(2,1)}, u32[]{:S(2)}) copy-start(bf16[1024,128]{1,0:T(8,128)(2,1)} %cotangent_ref.7) | copy-start | bytes 786436
  18.3 7.8 %copy-start.3 = (bf16[128,128]{1,0:T(8,128)(2,1)S(1)}, bf16[128,128]{1,0:T(8,128)(2,1)}, u32[]{:S(2)}) copy-start(bf16[128,128]{1,0:T(8,128)(2,1)} %weight_ref.7) | copy-start | bytes 98308
  21.7 5.8 %collective-permute-start.7 = (bf16[256,128]{1,0:T(8,128)(2,1)S(1)}, bf16[256,128]{1,0:T(8,128)(2,1)S(1)}, u32[]{:S(2)}, u32[]{:S(2)}) collective-permute-start(bf16[256,128]{1,0:T(8,128)(2,1)S(1)} %shard_map.93.refs_0_), channel_id=1, source_target_pairs={{0,16},{8,24},{16,0},{24,8},{1,17},{9,25},{17,1},{25,9},{2,18},{10... | collective-permute-start | bytes 196616 | tf_op jit(solution)/shard_map/ppermute | solution.py:17
  23.3 5.2 %collective-permute-start.8 = (bf16[256,128]{1,0:T(8,128)(2,1)S(1)}, bf16[256,128]{1,0:T(8,128)(2,1)S(1)}, u32[]{:S(2)}, u32[]{:S(2)}) collective-permute-start(bf16[256,128]{1,0:T(8,128)(2,1)S(1)} %shard_map.93.refs_0_), channel_id=1, source_target_pairs={{0,8},{8,0},{16,24},{24,16},{1,9},{9,1},{17,25},{25,17},{2,10},{10... | collective-permute-start | bytes 196616 | tf_op jit(solution)/shard_map/ppermute | solution.py:17
  23.6 6.1 %collective-permute-start.9 = (bf16[256,128]{1,0:T(8,128)(2,1)S(1)}, bf16[256,128]{1,0:T(8,128)(2,1)S(1)}, u32[]{:S(2)}, u32[]{:S(2)}) collective-permute-start(bf16[256,128]{1,0:T(8,128)(2,1)S(1)} %shard_map.93.refs_0_), channel_id=1, source_target_pairs={{0,24},{8,16},{16,8},{24,0},{1,25},{9,17},{17,9},{25,1},{2,26},{10... | collective-permute-start | bytes 196616 | tf_op jit(solution)/shard_map/ppermute | solution.py:17
  26.1 0.7 %copy-start.5 = (f32[128]{0:T(128)S(1)}, f32[128]{0:T(128)}, u32[]{:S(2)}) copy-start(f32[128]{0:T(128)} %param.10) | copy-start | bytes 1540
  30.3 1.4 %collective-permute-start.10 = (bf16[384,128]{1,0:T(8,128)(2,1)S(1)}, bf16[384,128]{1,0:T(8,128)(2,1)S(1)}, u32[]{:S(2)}, u32[]{:S(2)}) collective-permute-start(bf16[384,128]{1,0:T(8,128)(2,1)S(1)} %get-tuple-element.44.sent_ref), channel_id=1, source_target_pairs={{0,1},{1,0},{2,3},{3,2},{4,5},{5,4},{6,7},{7,6},{8,9},{9,8},{10,11... | collective-permute-start | bytes 294920 | tf_op jit(solution)/shard_map/ppermute | solution.py:17
  30.3 2.6 %collective-permute-start.11 = (bf16[768,128]{1,0:T(8,128)(2,1)S(1)}, bf16[768,128]{1,0:T(8,128)(2,1)S(1)}, u32[]{:S(2)}, u32[]{:S(2)}) collective-permute-start(bf16[768,128]{1,0:T(8,128)(2,1)S(1)} %get-tuple-element.45), channel_id=1, source_target_pairs={{0,1},{1,0},{2,3},{3,2},{4,5},{5,4},{6,7},{7,6},{8,9},{9,8},{10,11... | collective-permute-start | bytes 589832 | tf_op jit(solution)/shard_map/ppermute | solution.py:17
  31.7 5.8 %collective-permute-start.14 = (bf16[384,128]{1,0:T(8,128)(2,1)S(1)}, bf16[384,128]{1,0:T(8,128)(2,1)S(1)}, u32[]{:S(2)}, u32[]{:S(2)}) collective-permute-start(bf16[384,128]{1,0:T(8,128)(2,1)S(1)} %shard_map.99.first_ref.sent_ref), channel_id=1, source_target_pairs={{0,7},{1,6},{2,5},{3,4},{4,3},{5,2},{6,1},{7,0},{8,15},{9,14},{10,... | collective-permute-start | bytes 294920 | tf_op jit(solution)/shard_map/ppermute | solution.py:17
  33.0 6.8 %collective-permute-start.13 = (bf16[384,128]{1,0:T(8,128)(2,1)S(1)}, bf16[384,128]{1,0:T(8,128)(2,1)S(1)}, u32[]{:S(2)}, u32[]{:S(2)}) collective-permute-start(bf16[384,128]{1,0:T(8,128)(2,1)S(1)} %get-tuple-element.48), channel_id=1, source_target_pairs={{0,5},{1,4},{2,7},{3,6},{4,1},{5,0},{6,3},{7,2},{8,13},{9,12},{10,... | collective-permute-start | bytes 294920 | tf_op jit(solution)/shard_map/ppermute | solution.py:17
  34.3 5.5 %collective-permute-start.12 = (bf16[384,128]{1,0:T(8,128)(2,1)S(1)}, bf16[384,128]{1,0:T(8,128)(2,1)S(1)}, u32[]{:S(2)}, u32[]{:S(2)}) collective-permute-start(bf16[384,128]{1,0:T(8,128)(2,1)S(1)} %get-tuple-element.47), channel_id=1, source_target_pairs={{0,3},{1,2},{2,1},{3,0},{4,7},{5,6},{6,5},{7,4},{8,11},{9,10},{10,... | collective-permute-start | bytes 294920 | tf_op jit(solution)/shard_map/ppermute | solution.py:17

commit v15 on v14

--- a/solution.py
+++ b/solution.py
@@ -85,7 +85,7 @@
 def layer_kernel(
     rep, count, own_blocks, j, place_ref, flipped_ref, cotangent_ref, weight_ref, bias_ref, *refs
 ):
-    first, last = j == 0, j == 3
+    first, last = j == 0, j == 2
     piece_ref, refs = refs[0], refs[1:]
     if not first:
         (_, sums_in), refs = refs[:2], refs[2:]
@@ -117,7 +117,7 @@
     if j == 0:
         refs[0][0] = part_sum
         refs[0][1] = jnp.zeros_like(part_sum)
-    elif j == 2:
+    elif j == 3:
         refs[0][0] = sums_in[0]
         refs[0][1] = part_sum
     elif j == 1:
@@ -247,10 +247,10 @@
         [VMEM] * 4,
     )(place, vals, mine, far)
     arrived = {j: swap(partials[j], "rep", j) if j else partials[j] for j in range(rep)}
-    order = [2, 1, 3]
+    order = [3, 1, 2]
     own_rows = arrived[0]
     for j in order:
-        own_rows = call(add_kernel, shape((part, width), F32 if j != 3 else BF16), [VMEM] * 2)(
+        own_rows = call(add_kernel, shape((part, width), F32 if j != 2 else BF16), [VMEM] * 2)(
             own_rows, arrived[j]
         )
     pieces = {0: own_rows}
@@ -260,7 +260,7 @@
     outputs, carried = [], []
     for j, piece in pieces.items():
         outs = [shape((part, width), BF16), shape((quarter_blocks, size, width), F32)]
-        if j != 3:
+        if j != 2:
             outs += [shape((2, width, width), F32)]
         else:
             outs += [

time: 40.7 us -> 39.9 us (0.980)
  waiting for transfers between devices: 15.1 us -> 14.3 us
    ppermute x15, waiting for transfers between devices: 15.1 us -> 14.3 us  [swap(): return lax.ppermute(value, axis, [(i, i ^ distance) for i in range(size)])]
where the time goes in v15:
time: 39.9 us; the launch traced here: 39.6 us
  starting transfers between devices  17.1 us (43%)
  waiting for transfers between devices  14.3 us (36%)
  Pallas kernels  4.43 us (11%)
  local copies, waits for them, and re-layouts  3.04 us (8%)
  between operations  0.79 us (2%)
    ppermute x15, starting transfers between devices, swap(): return lax.ppermute(value, axis, [(i, i ^ distance) for i in range(size)])  17.1 us
    ppermute x15, waiting for transfers between devices, swap(): return lax.ppermute(value, axis, [(i, i ^ distance) for i in range(size)])  14.3 us
    unnamed x14, local copies, waits for them, and re-layouts  3.04 us
    pallas_call x4, Pallas kernels, body(): call(functools.partial(layer_kernel, rep, count, own_blocks, j), outs, [V...  2.1 us
  transfers between devices with their start and end apart: 15, of which 12 were waited for; matrix products, arithmetic and copies ran while one was open for 0% of the time, Pallas kernels for 7%

profile of v15, /device:TPU:0, one launch (start us, length us, event | category | flops | bytes accessed | tf_op | source)
XLA Modules:
  0.0 39.6 jit_solution(13447723303304187061)
XLA Ops:
  0.6 3.4 %collective-permute-start.2 = (bf16[256,128]{1,0:T(8,128)(2,1)}, bf16[256,128]{1,0:T(8,128)(2,1)S(1)}, u32[]{:S(2)}, u32[]{:S(2)}) collective-permute-start(bf16[256,128]{1,0:T(8,128)(2,1)} %features_ref.1), channel_id=1, source_target_pairs={{0,7},{1,6},{2,5},{3,4},{4,3},{5,2},{6,1},{7,0},{8,15},{9,14},{10,... | collective-permute-start | bytes 196616 | tf_op jit(solution)/shard_map/ppermute | solution.py:17
  4.0 0.8 %collective-permute-start.1 = (bf16[256,128]{1,0:T(8,128)(2,1)}, bf16[256,128]{1,0:T(8,128)(2,1)S(1)}, u32[]{:S(2)}, u32[]{:S(2)}) collective-permute-start(bf16[256,128]{1,0:T(8,128)(2,1)} %features_ref.1), channel_id=1, source_target_pairs={{0,5},{1,4},{2,7},{3,6},{4,1},{5,0},{6,3},{7,2},{8,13},{9,12},{10,... | collective-permute-start | bytes 196616 | tf_op jit(solution)/shard_map/ppermute | solution.py:17
  5.0 1.0 %copy-done.1 = bf16[8,2,128,128]{3,2,1,0:T(8,128)(2,1)S(1)} copy-done((bf16[8,2,128,128]{3,2,1,0:T(8,128)(2,1)S(1)}, bf16[8,2,128,128]{3,2,1,0:T(8,128)(2,1)}, u32[]{:S(2)}) %copy-start.1) | copy-done | bytes 524312
  6.0 0.8 %copy-done.4 = bf16[256,128]{1,0:T(8,128)(2,1)S(1)} copy-done((bf16[256,128]{1,0:T(8,128)(2,1)S(1)}, bf16[256,128]{1,0:T(8,128)(2,1)}, u32[]{:S(2)}) %copy-start.4) | copy-done | bytes 65560
  7.1 1.1 %collective-permute-done.1.refs_0_ = bf16[256,128]{1,0:T(8,128)(2,1)S(1)} collective-permute-done((bf16[256,128]{1,0:T(8,128)(2,1)}, bf16[256,128]{1,0:T(8,128)(2,1)S(1)}, u32[]{:S(2)}, u32[]{:S(2)}) %collective-permute-start.1) | collective-permute-done | bytes 65568 | tf_op jit(solution)/shard_map/ppermute | solution.py:17
  8.2 1.1 %collective-permute-done.refs_0_ = bf16[256,128]{1,0:T(8,128)(2,1)S(1)} collective-permute-done((bf16[256,128]{1,0:T(8,128)(2,1)}, bf16[256,128]{1,0:T(8,128)(2,1)S(1)}, u32[]{:S(2)}, u32[]{:S(2)}) %collective-permute-start) | collective-permute-done | bytes 65568 | tf_op jit(solution)/shard_map/ppermute | solution.py:17
  10.2 0.7 %collective-permute-done.3.far_ref = bf16[1024,128]{1,0:T(8,128)(2,1)S(1)} collective-permute-done((bf16[1024,128]{1,0:T(8,128)(2,1)S(1)}, bf16[1024,128]{1,0:T(8,128)(2,1)S(1)}, u32[]{:S(2)}, u32[]{:S(2)}) %collective-permute-start.3) | collective-permute-done | bytes 262176 | tf_op jit(solution)/shard_map/ppermute | solution.py:17
  11.3 3.7 %collective-permute-start.4 = (bf16[256,128]{1,0:T(8,128)(2,1)S(1)}, bf16[256,128]{1,0:T(8,128)(2,1)S(1)}, u32[]{:S(2)}, u32[]{:S(2)}) collective-permute-start(bf16[256,128]{1,0:T(8,128)(2,1)S(1)} %get-tuple-element.30), channel_id=1, source_target_pairs={{0,24},{8,16},{16,8},{24,0},{1,25},{9,17},{17,9},{25,1},{2,26},{10... | collective-permute-start | bytes 196616 | tf_op jit(solution)/shard_map/ppermute | solution.py:17
  15.0 0.8 %collective-permute-start.6 = (bf16[256,128]{1,0:T(8,128)(2,1)S(1)}, bf16[256,128]{1,0:T(8,128)(2,1)S(1)}, u32[]{:S(2)}, u32[]{:S(2)}) collective-permute-start(bf16[256,128]{1,0:T(8,128)(2,1)S(1)} %get-tuple-element.32), channel_id=1, source_target_pairs={{0,16},{8,24},{16,0},{24,8},{1,17},{9,25},{17,1},{25,9},{2,18},{10... | collective-permute-start | bytes 196616 | tf_op jit(solution)/shard_map/ppermute | solution.py:17
  15.8 2.4 %collective-permute-done.4.b_ref = bf16[256,128]{1,0:T(8,128)(2,1)S(1)} collective-permute-done((bf16[256,128]{1,0:T(8,128)(2,1)S(1)}, bf16[256,128]{1,0:T(8,128)(2,1)S(1)}, u32[]{:S(2)}, u32[]{:S(2)}) %collective-permute-start.4) | collective-permute-done | bytes 65568 | tf_op jit(solution)/shard_map/ppermute | solution.py:17
  18.2 1.9 %collective-permute-done.5.b_ref = bf16[256,128]{1,0:T(8,128)(2,1)S(1)} collective-permute-done((bf16[256,128]{1,0:T(8,128)(2,1)S(1)}, bf16[256,128]{1,0:T(8,128)(2,1)S(1)}, u32[]{:S(2)}, u32[]{:S(2)}) %collective-permute-start.5) | collective-permute-done | bytes 65568 | tf_op jit(solution)/shard_map/ppermute | solution.py:17
  20.1 0.8 %collective-permute-done.6.b_ref = bf16[256,128]{1,0:T(8,128)(2,1)S(1)} collective-permute-done((bf16[256,128]{1,0:T(8,128)(2,1)S(1)}, bf16[256,128]{1,0:T(8,128)(2,1)S(1)}, u32[]{:S(2)}, u32[]{:S(2)}) %collective-permute-start.6) | collective-permute-done | bytes 65568 | tf_op jit(solution)/shard_map/ppermute | solution.py:17
  20.9 2.2 %collective-permute-start.7 = (bf16[256,128]{1,0:T(8,128)(2,1)S(1)}, bf16[256,128]{1,0:T(8,128)(2,1)S(1)}, u32[]{:S(2)}, u32[]{:S(2)}) collective-permute-start(bf16[256,128]{1,0:T(8,128)(2,1)S(1)} %shard_map.93.refs_0_), channel_id=1, source_target_pairs={{0,24},{8,16},{16,8},{24,0},{1,25},{9,17},{17,9},{25,1},{2,26},{10... | collective-permute-start | bytes 196616 | tf_op jit(solution)/shard_map/ppermute | solution.py:17
  23.5 1.9 %collective-permute-start.9 = (bf16[256,128]{1,0:T(8,128)(2,1)S(1)}, bf16[256,128]{1,0:T(8,128)(2,1)S(1)}, u32[]{:S(2)}, u32[]{:S(2)}) collective-permute-start(bf16[256,128]{1,0:T(8,128)(2,1)S(1)} %shard_map.93.refs_0_), channel_id=1, source_target_pairs={{0,16},{8,24},{16,0},{24,8},{1,17},{9,25},{17,1},{25,9},{2,18},{10... | collective-permute-start | bytes 196616 | tf_op jit(solution)/shard_map/ppermute | solution.py:17
  25.4 0.6 %copy-done.5 = f32[128]{0:T(128)S(1)} copy-done((f32[128]{0:T(128)S(1)}, f32[128]{0:T(128)}, u32[]{:S(2)}) %copy-start.5) | copy-done | bytes 536
  26.5 0.8 %collective-permute-done.7.refs_0_ = bf16[256,128]{1,0:T(8,128)(2,1)S(1)} collective-permute-done((bf16[256,128]{1,0:T(8,128)(2,1)S(1)}, bf16[256,128]{1,0:T(8,128)(2,1)S(1)}, u32[]{:S(2)}, u32[]{:S(2)}) %collective-permute-start.7) | collective-permute-done | bytes 65568 | tf_op jit(solution)/shard_map/ppermute | solution.py:17
  28.8 0.5 %shard_map.97 = (bf16[256,128]{1,0:T(8,128)(2,1)S(1)}, f32[16,128,128]{2,1,0:T(8,128)S(1)}, bf16[384,128]{1,0:T(8,128)(2,1)S(1)}, bf16[768,128]{1,0:T(8,128)(2,1)S(1)}) custom-call(s32[16,128]{1,0:T(8,128)S(1)} %shard_map.89.place_ref, bf16[8,256,128]{2,1,0:T(8,128)(2,1)S(1)} %get-tuple-element.28.flipped_ref, ...), custom_call_target="tpu_custom_call", output_to_operand_aliasing={{1}: (6, {})} | custom-call | tf_op jit(solution)/shard_map/pallas_call | solution.py:270
  30.0 0.8 %collective-permute-done.10.got_ref = bf16[384,128]{1,0:T(8,128)(2,1)S(1)} collective-permute-done((bf16[384,128]{1,0:T(8,128)(2,1)S(1)}, bf16[384,128]{1,0:T(8,128)(2,1)S(1)}, u32[]{:S(2)}, u32[]{:S(2)}) %collective-permute-start.10) | collective-permute-done | bytes 98336 | tf_op jit(solution)/shard_map/ppermute | solution.py:17
  30.8 1.3 %collective-permute-start.14 = (bf16[384,128]{1,0:T(8,128)(2,1)S(1)}, bf16[384,128]{1,0:T(8,128)(2,1)S(1)}, u32[]{:S(2)}, u32[]{:S(2)}) collective-permute-start(bf16[384,128]{1,0:T(8,128)(2,1)S(1)} %shard_map.99.first_ref.sent_ref), channel_id=1, source_target_pairs={{0,7},{1,6},{2,5},{3,4},{4,3},{5,2},{6,1},{7,0},{8,15},{9,14},{10,... | collective-permute-start | bytes 294920 | tf_op jit(solution)/shard_map/ppermute | solution.py:17
  32.1 1.3 %collective-permute-start.13 = (bf16[384,128]{1,0:T(8,128)(2,1)S(1)}, bf16[384,128]{1,0:T(8,128)(2,1)S(1)}, u32[]{:S(2)}, u32[]{:S(2)}) collective-permute-start(bf16[384,128]{1,0:T(8,128)(2,1)S(1)} %get-tuple-element.48), channel_id=1, source_target_pairs={{0,5},{1,4},{2,7},{3,6},{4,1},{5,0},{6,3},{7,2},{8,13},{9,12},{10,... | collective-permute-start | bytes 294920 | tf_op jit(solution)/shard_map/ppermute | solution.py:17
  33.9 0.7 %shard_map.98 = bf16[1024,128]{1,0:T(8,128)(2,1)} custom-call(bf16[256,128]{1,0:T(8,128)(2,1)S(1)} %get-tuple-element.33.refs_0_, bf16[256,128]{1,0:T(8,128)(2,1)S(1)} %get-tuple-element.36.refs_1_, bf16[256,128]{1,0:T(8,128)(2,1)S(1)} %get-tuple-element.39.refs_2_, bf16[256,128]{1,0:T(8,128)(2,1)S(1)} %get-tuple-element.42.refs_3_), custom_call_target="tpu_custom_call" | custom-call | tf_op jit(solution)/shard_map/pallas_call | solution.py:287
  34.7 1.9 %collective-permute-done.14.got_ref = bf16[384,128]{1,0:T(8,128)(2,1)S(1)} collective-permute-done((bf16[384,128]{1,0:T(8,128)(2,1)S(1)}, bf16[384,128]{1,0:T(8,128)(2,1)S(1)}, u32[]{:S(2)}, u32[]{:S(2)}) %collective-permute-start.14) | collective-permute-done | bytes 98336 | tf_op jit(solution)/shard_map/ppermute | solution.py:17
  36.6 2.3 %collective-permute-done.13.refs_0_ = bf16[384,128]{1,0:T(8,128)(2,1)S(1)} collective-permute-done((bf16[384,128]{1,0:T(8,128)(2,1)S(1)}, bf16[384,128]{1,0:T(8,128)(2,1)S(1)}, u32[]{:S(2)}, u32[]{:S(2)}) %collective-permute-start.13) | collective-permute-done | bytes 98336 | tf_op jit(solution)/shard_map/ppermute | solution.py:17
  38.9 0.7 %shard_map.103 = (f32[256,128]{1,0:T(8,128)}, f32[128,128]{1,0:T(8,128)}) custom-call(f32[256,128]{1,0:T(8,128)S(1)} %get-tuple-element.46.own_ref, bf16[384,128]{1,0:T(8,128)(2,1)S(1)} %shard_map.99.first_ref.sent_ref, bf16[384,128]{1,0:T(8,128)(2,1)S(1)} %collective-permute-done.12.got_ref, f32[384,128]{1,0:T(8,128)S(1)} %shard_map.102.refs_0_), custom_call_target="tpu_custom_call" | custom-call | tf_op jit(solution)/shard_map/pallas_call | solution.py:296
  (39 shorter events, 5.2 us)
Async XLA Ops:
  0.6 6.4 %collective-permute-start.2 = (bf16[256,128]{1,0:T(8,128)(2,1)}, bf16[256,128]{1,0:T(8,128)(2,1)S(1)}, u32[]{:S(2)}, u32[]{:S(2)}) collective-permute-start(bf16[256,128]{1,0:T(8,128)(2,1)} %features_ref.1), channel_id=1, source_target_pairs={{0,7},{1,6},{2,5},{3,4},{4,3},{5,2},{6,1},{7,0},{8,15},{9,14},{10,... | collective-permute-start | bytes 196616 | tf_op jit(solution)/shard_map/ppermute | solution.py:17
  4.0 4.2 %collective-permute-start.1 = (bf16[256,128]{1,0:T(8,128)(2,1)}, bf16[256,128]{1,0:T(8,128)(2,1)S(1)}, u32[]{:S(2)}, u32[]{:S(2)}) collective-permute-start(bf16[256,128]{1,0:T(8,128)(2,1)} %features_ref.1), channel_id=1, source_target_pairs={{0,5},{1,4},{2,7},{3,6},{4,1},{5,0},{6,3},{7,2},{8,13},{9,12},{10,... | collective-permute-start | bytes 196616 | tf_op jit(solution)/shard_map/ppermute | solution.py:17
  4.8 4.5 %collective-permute-start = (bf16[256,128]{1,0:T(8,128)(2,1)}, bf16[256,128]{1,0:T(8,128)(2,1)S(1)}, u32[]{:S(2)}, u32[]{:S(2)}) collective-permute-start(bf16[256,128]{1,0:T(8,128)(2,1)} %features_ref.1), channel_id=1, source_target_pairs={{0,3},{1,2},{2,1},{3,0},{4,7},{5,6},{6,5},{7,4},{8,11},{9,10},{10,... | collective-permute-start | bytes 196616 | tf_op jit(solution)/shard_map/ppermute | solution.py:17
  5.0 1.0 %copy-start.1 = (bf16[8,2,128,128]{3,2,1,0:T(8,128)(2,1)S(1)}, bf16[8,2,128,128]{3,2,1,0:T(8,128)(2,1)}, u32[]{:S(2)}) copy-start(bf16[8,2,128,128]{3,2,1,0:T(8,128)(2,1)} %vals_ref.3) | copy-start | bytes 1572868
  6.0 0.8 %copy-start.4 = (bf16[256,128]{1,0:T(8,128)(2,1)S(1)}, bf16[256,128]{1,0:T(8,128)(2,1)}, u32[]{:S(2)}) copy-start(bf16[256,128]{1,0:T(8,128)(2,1)} %features_ref.1) | copy-start | bytes 196612
  7.1 3.9 %copy-start.2 = (bf16[8,2,128,128]{3,2,1,0:T(8,128)(2,1)S(1)}, bf16[8,2,128,128]{3,2,1,0:T(8,128)(2,1)}, u32[]{:S(2)}) copy-start(bf16[8,2,128,128]{3,2,1,0:T(8,128)(2,1)} %vals_ref.3) | copy-start | bytes 1572868
  9.4 0.7 %copy-start.6 = (s32[8,2]{0,1:T(2,128)S(1)}, s32[8,2]{0,1:T(2,128)}, u32[]{:S(2)}) copy-start(s32[8,2]{0,1:T(2,128)} %param.6) | copy-start | bytes 196
  9.4 1.6 %collective-permute-start.3 = (bf16[1024,128]{1,0:T(8,128)(2,1)S(1)}, bf16[1024,128]{1,0:T(8,128)(2,1)S(1)}, u32[]{:S(2)}, u32[]{:S(2)}) collective-permute-start(bf16[1024,128]{1,0:T(8,128)(2,1)S(1)} %shard_map.88._.mine_ref), channel_id=1, source_target_pairs={{0,1},{1,0},{2,3},{3,2},{4,5},{5,4},{6,7},{7,6},{8,9},{9,8},{10,11... | collective-permute-start | bytes 786440 | tf_op jit(solution)/shard_map/ppermute | solution.py:17
  11.3 6.8 %collective-permute-start.4 = (bf16[256,128]{1,0:T(8,128)(2,1)S(1)}, bf16[256,128]{1,0:T(8,128)(2,1)S(1)}, u32[]{:S(2)}, u32[]{:S(2)}) collective-permute-start(bf16[256,128]{1,0:T(8,128)(2,1)S(1)} %get-tuple-element.30), channel_id=1, source_target_pairs={{0,24},{8,16},{16,8},{24,0},{1,25},{9,17},{17,9},{25,1},{2,26},{10... | collective-permute-start | bytes 196616 | tf_op jit(solution)/shard_map/ppermute | solution.py:17
  15.0 5.1 %collective-permute-start.5 = (bf16[256,128]{1,0:T(8,128)(2,1)S(1)}, bf16[256,128]{1,0:T(8,128)(2,1)S(1)}, u32[]{:S(2)}, u32[]{:S(2)}) collective-permute-start(bf16[256,128]{1,0:T(8,128)(2,1)S(1)} %get-tuple-element.31), channel_id=1, source_target_pairs={{0,8},{8,0},{16,24},{24,16},{1,9},{9,1},{17,25},{25,17},{2,10},{10... | collective-permute-start | bytes 196616 | tf_op jit(solution)/shard_map/ppermute | solution.py:17
  15.0 5.9 %collective-permute-start.6 = (bf16[256,128]{1,0:T(8,128)(2,1)S(1)}, bf16[256,128]{1,0:T(8,128)(2,1)S(1)}, u32[]{:S(2)}, u32[]{:S(2)}) collective-permute-start(bf16[256,128]{1,0:T(8,128)(2,1)S(1)} %get-tuple-element.32), channel_id=1, source_target_pairs={{0,16},{8,24},{16,0},{24,8},{1,17},{9,25},{17,1},{25,9},{2,18},{10... | collective-permute-start | bytes 196616 | tf_op jit(solution)/shard_map/ppermute | solution.py:17
  18.2 7.2 %copy-start = (bf16[1024,128]{1,0:T(8,128)(2,1)S(1)}, bf16[1024,128]{1,0:T(8,128)(2,1)}, u32[]{:S(2)}) copy-start(bf16[1024,128]{1,0:T(8,128)(2,1)} %cotangent_ref.7) | copy-start | bytes 786436
  20.1 5.3 %copy-start.3 = (bf16[128,128]{1,0:T(8,128)(2,1)S(1)}, bf16[128,128]{1,0:T(8,128)(2,1)}, u32[]{:S(2)}) copy-start(bf16[128,128]{1,0:T(8,128)(2,1)} %weight_ref.7) | copy-start | bytes 98308
  20.9 6.4 %collective-permute-start.7 = (bf16[256,128]{1,0:T(8,128)(2,1)S(1)}, bf16[256,128]{1,0:T(8,128)(2,1)S(1)}, u32[]{:S(2)}, u32[]{:S(2)}) collective-permute-start(bf16[256,128]{1,0:T(8,128)(2,1)S(1)} %shard_map.93.refs_0_), channel_id=1, source_target_pairs={{0,24},{8,16},{16,8},{24,0},{1,25},{9,17},{17,9},{25,1},{2,26},{10... | collective-permute-start | bytes 196616 | tf_op jit(solution)/shard_map/ppermute | solution.py:17
  23.1 5.1 %collective-permute-start.8 = (bf16[256,128]{1,0:T(8,128)(2,1)S(1)}, bf16[256,128]{1,0:T(8,128)(2,1)S(1)}, u32[]{:S(2)}, u32[]{:S(2)}) collective-permute-start(bf16[256,128]{1,0:T(8,128)(2,1)S(1)} %shard_map.93.refs_0_), channel_id=1, source_target_pairs={{0,8},{8,0},{16,24},{24,16},{1,9},{9,1},{17,25},{25,17},{2,10},{10... | collective-permute-start | bytes 196616 | tf_op jit(solution)/shard_map/ppermute | solution.py:17
  23.5 5.3 %collective-permute-start.9 = (bf16[256,128]{1,0:T(8,128)(2,1)S(1)}, bf16[256,128]{1,0:T(8,128)(2,1)S(1)}, u32[]{:S(2)}, u32[]{:S(2)}) collective-permute-start(bf16[256,128]{1,0:T(8,128)(2,1)S(1)} %shard_map.93.refs_0_), channel_id=1, source_target_pairs={{0,16},{8,24},{16,0},{24,8},{1,17},{9,25},{17,1},{25,9},{2,18},{10... | collective-permute-start | bytes 196616 | tf_op jit(solution)/shard_map/ppermute | solution.py:17
  25.4 0.7 %copy-start.5 = (f32[128]{0:T(128)S(1)}, f32[128]{0:T(128)}, u32[]{:S(2)}) copy-start(f32[128]{0:T(128)} %param.10) | copy-start | bytes 1540
  29.4 1.4 %collective-permute-start.10 = (bf16[384,128]{1,0:T(8,128)(2,1)S(1)}, bf16[384,128]{1,0:T(8,128)(2,1)S(1)}, u32[]{:S(2)}, u32[]{:S(2)}) collective-permute-start(bf16[384,128]{1,0:T(8,128)(2,1)S(1)} %get-tuple-element.44.sent_ref), channel_id=1, source_target_pairs={{0,1},{1,0},{2,3},{3,2},{4,5},{5,4},{6,7},{7,6},{8,9},{9,8},{10,11... | collective-permute-start | bytes 294920 | tf_op jit(solution)/shard_map/ppermute | solution.py:17
  29.5 2.6 %collective-permute-start.11 = (bf16[768,128]{1,0:T(8,128)(2,1)S(1)}, bf16[768,128]{1,0:T(8,128)(2,1)S(1)}, u32[]{:S(2)}, u32[]{:S(2)}) collective-permute-start(bf16[768,128]{1,0:T(8,128)(2,1)S(1)} %get-tuple-element.45), channel_id=1, source_target_pairs={{0,1},{1,0},{2,3},{3,2},{4,5},{5,4},{6,7},{7,6},{8,9},{9,8},{10,11... | collective-permute-start | bytes 589832 | tf_op jit(solution)/shard_map/ppermute | solution.py:17
  30.8 5.8 %collective-permute-start.14 = (bf16[384,128]{1,0:T(8,128)(2,1)S(1)}, bf16[384,128]{1,0:T(8,128)(2,1)S(1)}, u32[]{:S(2)}, u32[]{:S(2)}) collective-permute-start(bf16[384,128]{1,0:T(8,128)(2,1)S(1)} %shard_map.99.first_ref.sent_ref), channel_id=1, source_target_pairs={{0,7},{1,6},{2,5},{3,4},{4,3},{5,2},{6,1},{7,0},{8,15},{9,14},{10,... | collective-permute-start | bytes 294920 | tf_op jit(solution)/shard_map/ppermute | solution.py:17
  32.1 6.8 %collective-permute-start.13 = (bf16[384,128]{1,0:T(8,128)(2,1)S(1)}, bf16[384,128]{1,0:T(8,128)(2,1)S(1)}, u32[]{:S(2)}, u32[]{:S(2)}) collective-permute-start(bf16[384,128]{1,0:T(8,128)(2,1)S(1)} %get-tuple-element.48), channel_id=1, source_target_pairs={{0,5},{1,4},{2,7},{3,6},{4,1},{5,0},{6,3},{7,2},{8,13},{9,12},{10,... | collective-permute-start | bytes 294920 | tf_op jit(solution)/shard_map/ppermute | solution.py:17
  33.4 5.5 %collective-permute-start.12 = (bf16[384,128]{1,0:T(8,128)(2,1)S(1)}, bf16[384,128]{1,0:T(8,128)(2,1)S(1)}, u32[]{:S(2)}, u32[]{:S(2)}) collective-permute-start(bf16[384,128]{1,0:T(8,128)(2,1)S(1)} %get-tuple-element.47), channel_id=1, source_target_pairs={{0,3},{1,2},{2,1},{3,0},{4,7},{5,6},{6,5},{7,4},{8,11},{9,10},{10,... | collective-permute-start | bytes 294920 | tf_op jit(solution)/shard_map/ppermute | solution.py:17

commit v16 on v15

--- a/solution.py
+++ b/solution.py
@@ -15,6 +15,12 @@
 def swap(value, axis, distance):
     size = lax.axis_size(axis)
     return lax.ppermute(value, axis, [(i, i ^ distance) for i in range(size)])
+
+
+def lift(value, distance):
+    rep, dom = lax.axis_size("rep"), lax.axis_size("dom")
+    pairs = [(r * dom + d, (r ^ distance) * dom + (d ^ 1)) for r in range(rep) for d in range(dom)]
+    return lax.ppermute(value, ("rep", "dom"), pairs)
 
 
 def matmul(a, b, contract):
@@ -85,7 +91,7 @@
 def layer_kernel(
     rep, count, own_blocks, j, place_ref, flipped_ref, cotangent_ref, weight_ref, bias_ref, *refs
 ):
-    first, last = j == 0, j == 2
+    first, last = j == 3, j == 2
     piece_ref, refs = refs[0], refs[1:]
     if not first:
         (_, sums_in), refs = refs[:2], refs[2:]
@@ -114,13 +120,10 @@
         terms = matmul(flipped_ref[row], grad_agg[i * size : (i + 1) * size], (1, 0))
         for k in range(count):
             contrib[place_ref[row * count + k, 0]] += terms[k * size : (k + 1) * size]
-    if j == 0:
-        refs[0][0] = part_sum
-        refs[0][1] = jnp.zeros_like(part_sum)
-    elif j == 3:
-        refs[0][0] = sums_in[0]
+    if j == 3:
+        refs[0][0] = jnp.zeros_like(part_sum)
         refs[0][1] = part_sum
-    elif j == 1:
+    elif not last:
         refs[0][0] = sums_in[0] + part_sum
         refs[0][1] = sums_in[1]
     else:
@@ -132,7 +135,7 @@
 
 
 def add_kernel(a_ref, b_ref, out_ref):
-    out_ref[...] = (a_ref[...] + b_ref[...].astype(F32)).astype(out_ref.dtype)
+    out_ref[...] = (a_ref[...].astype(F32) + b_ref[...].astype(F32)).astype(out_ref.dtype)
 
 
 def order_kernel(order, *refs):
@@ -246,16 +249,15 @@
         [shape((part, width), BF16 if j else F32) for j in range(rep)],
         [VMEM] * 4,
     )(place, vals, mine, far)
-    arrived = {j: swap(partials[j], "rep", j) if j else partials[j] for j in range(rep)}
-    order = [3, 1, 2]
-    own_rows = arrived[0]
-    for j in order:
-        own_rows = call(add_kernel, shape((part, width), F32 if j != 2 else BF16), [VMEM] * 2)(
-            own_rows, arrived[j]
-        )
-    pieces = {0: own_rows}
-    for j in order:
-        pieces[j] = swap(own_rows, "rep", j)
+    def add(a, b, dtype):
+        return call(add_kernel, shape((part, width), dtype), [VMEM] * 2, cost=10**9)(a, b)
+
+    arrived = {j: lift(partials[j], j) for j in (3, 1, 2)}
+    total = add(arrived[3], arrived[1], F32)
+    total = add(total, arrived[2], F32)
+    own_rows = add(total, swap(partials[0], "dom", 1), BF16)
+    pieces = {3: lift(own_rows, 3), 1: lift(own_rows, 1)}
+    pieces |= {0: swap(own_rows, "dom", 1), 2: lift(own_rows, 2)}
 
     outputs, carried = [], []
     for j, piece in pieces.items():

time: 39.9 us -> 41.2 us (1.033)
  waiting for transfers between devices: 14.3 us -> 15.8 us
    ppermute x15 -> x11, starting transfers between devices: 17.1 us -> 8.6 us  [swap(): return lax.ppermute(value, axis, [(i, i ^ distance) for i in range(size)])]
    ppermute x0 -> x6, starting transfers between devices: none -> 8.16 us  [lift(): return lax.ppermute(value, ('rep', 'dom'), pairs)]
    ppermute x0 -> x6, waiting for transfers between devices: none -> 7.82 us  [lift(): return lax.ppermute(value, ('rep', 'dom'), pairs)]
    ppermute x15 -> x11, waiting for transfers between devices: 14.3 us -> 8.01 us  [swap(): return lax.ppermute(value, axis, [(i, i ^ distance) for i in range(size)])]
  transfers between devices with their start and end apart: 15 -> 17, of which waited for: 12 -> 10; matrix products, arithmetic and copies ran while one was open for 0% -> 0% of each run, Pallas kernels for 7% -> 7%
where the time goes in v16:
time: 41.2 us; the launch traced here: 40.9 us
  starting transfers between devices  16.8 us (41%)
  waiting for transfers between devices  15.8 us (38%)
  Pallas kernels  4.47 us (11%)
  local copies, waits for them, and re-layouts  3.04 us (7%)
  between operations  0.82 us (2%)
    ppermute x11, starting transfers between devices, swap(): return lax.ppermute(value, axis, [(i, i ^ distance) for i in range(size)])  8.6 us
    ppermute x6, starting transfers between devices, lift(): return lax.ppermute(value, ('rep', 'dom'), pairs)  8.16 us
    ppermute x11, waiting for transfers between devices, swap(): return lax.ppermute(value, axis, [(i, i ^ distance) for i in range(size)])  8.01 us
    ppermute x6, waiting for transfers between devices, lift(): return lax.ppermute(value, ('rep', 'dom'), pairs)  7.82 us
    unnamed x14, local copies, waits for them, and re-layouts  3.04 us
    pallas_call x4, Pallas kernels, body(): call(functools.partial(layer_kernel, rep, count, own_blocks, j), outs, [V...  2.12 us
  transfers between devices with their start and end apart: 17, of which 10 were waited for; matrix products, arithmetic and copies ran while one was open for 0% of the time, Pallas kernels for 7%

profile of v16, /device:TPU:0, one launch (start us, length us, event | category | flops | bytes accessed | tf_op | source)
XLA Modules:
  0.0 40.9 jit_solution(4409358776793647194)
XLA Ops:
  0.6 3.4 %collective-permute-start.2 = (bf16[256,128]{1,0:T(8,128)(2,1)}, bf16[256,128]{1,0:T(8,128)(2,1)S(1)}, u32[]{:S(2)}, u32[]{:S(2)}) collective-permute-start(bf16[256,128]{1,0:T(8,128)(2,1)} %features_ref.1), channel_id=1, source_target_pairs={{0,7},{1,6},{2,5},{3,4},{4,3},{5,2},{6,1},{7,0},{8,15},{9,14},{10,... | collective-permute-start | bytes 196616 | tf_op jit(solution)/shard_map/ppermute | solution.py:17
  4.0 0.8 %collective-permute-start.1 = (bf16[256,128]{1,0:T(8,128)(2,1)}, bf16[256,128]{1,0:T(8,128)(2,1)S(1)}, u32[]{:S(2)}, u32[]{:S(2)}) collective-permute-start(bf16[256,128]{1,0:T(8,128)(2,1)} %features_ref.1), channel_id=1, source_target_pairs={{0,5},{1,4},{2,7},{3,6},{4,1},{5,0},{6,3},{7,2},{8,13},{9,12},{10,... | collective-permute-start | bytes 196616 | tf_op jit(solution)/shard_map/ppermute | solution.py:17
  5.0 1.0 %copy-done.1 = bf16[8,2,128,128]{3,2,1,0:T(8,128)(2,1)S(1)} copy-done((bf16[8,2,128,128]{3,2,1,0:T(8,128)(2,1)S(1)}, bf16[8,2,128,128]{3,2,1,0:T(8,128)(2,1)}, u32[]{:S(2)}) %copy-start.1) | copy-done | bytes 524312
  6.0 0.8 %copy-done.4 = bf16[256,128]{1,0:T(8,128)(2,1)S(1)} copy-done((bf16[256,128]{1,0:T(8,128)(2,1)S(1)}, bf16[256,128]{1,0:T(8,128)(2,1)}, u32[]{:S(2)}) %copy-start.4) | copy-done | bytes 65560
  7.1 1.1 %collective-permute-done.1.refs_0_ = bf16[256,128]{1,0:T(8,128)(2,1)S(1)} collective-permute-done((bf16[256,128]{1,0:T(8,128)(2,1)}, bf16[256,128]{1,0:T(8,128)(2,1)S(1)}, u32[]{:S(2)}, u32[]{:S(2)}) %collective-permute-start.1) | collective-permute-done | bytes 65568 | tf_op jit(solution)/shard_map/ppermute | solution.py:17
  8.2 1.1 %collective-permute-done.refs_0_ = bf16[256,128]{1,0:T(8,128)(2,1)S(1)} collective-permute-done((bf16[256,128]{1,0:T(8,128)(2,1)}, bf16[256,128]{1,0:T(8,128)(2,1)S(1)}, u32[]{:S(2)}, u32[]{:S(2)}) %collective-permute-start) | collective-permute-done | bytes 65568 | tf_op jit(solution)/shard_map/ppermute | solution.py:17
  10.2 0.7 %collective-permute-done.3.far_ref = bf16[1024,128]{1,0:T(8,128)(2,1)S(1)} collective-permute-done((bf16[1024,128]{1,0:T(8,128)(2,1)S(1)}, bf16[1024,128]{1,0:T(8,128)(2,1)S(1)}, u32[]{:S(2)}, u32[]{:S(2)}) %collective-permute-start.3) | collective-permute-done | bytes 262176 | tf_op jit(solution)/shard_map/ppermute | solution.py:17
  11.3 3.4 %collective-permute-start.4 = (bf16[256,128]{1,0:T(8,128)(2,1)S(1)}, bf16[256,128]{1,0:T(8,128)(2,1)S(1)}, u32[]{:S(2)}, u32[]{:S(2)}) collective-permute-start(bf16[256,128]{1,0:T(8,128)(2,1)S(1)} %get-tuple-element.29), channel_id=1, source_target_pairs={{0,25},{1,24},{2,27},{3,26},{4,29},{5,28},{6,31},{7,30},{8,17},{9,... | collective-permute-start | bytes 196616 | tf_op jit(solution)/shard_map/ppermute | solution.py:23
  14.8 0.6 %collective-permute-start.6 = (bf16[256,128]{1,0:T(8,128)(2,1)S(1)}, bf16[256,128]{1,0:T(8,128)(2,1)S(1)}, u32[]{:S(2)}, u32[]{:S(2)}) collective-permute-start(bf16[256,128]{1,0:T(8,128)(2,1)S(1)} %get-tuple-element.31), channel_id=1, source_target_pairs={{0,17},{1,16},{2,19},{3,18},{4,21},{5,20},{6,23},{7,22},{8,25},{9,... | collective-permute-start | bytes 196616 | tf_op jit(solution)/shard_map/ppermute | solution.py:23
  15.6 1.8 %collective-permute-done.4.a_ref = bf16[256,128]{1,0:T(8,128)(2,1)S(1)} collective-permute-done((bf16[256,128]{1,0:T(8,128)(2,1)S(1)}, bf16[256,128]{1,0:T(8,128)(2,1)S(1)}, u32[]{:S(2)}, u32[]{:S(2)}) %collective-permute-start.4) | collective-permute-done | bytes 65568 | tf_op jit(solution)/shard_map/ppermute | solution.py:23
  17.4 2.8 %collective-permute-done.5.b_ref = bf16[256,128]{1,0:T(8,128)(2,1)S(1)} collective-permute-done((bf16[256,128]{1,0:T(8,128)(2,1)S(1)}, bf16[256,128]{1,0:T(8,128)(2,1)S(1)}, u32[]{:S(2)}, u32[]{:S(2)}) %collective-permute-start.5) | collective-permute-done | bytes 65568 | tf_op jit(solution)/shard_map/ppermute | solution.py:23
  20.4 2.3 %collective-permute-start.8 = (bf16[256,128]{1,0:T(8,128)(2,1)S(1)}, bf16[256,128]{1,0:T(8,128)(2,1)S(1)}, u32[]{:S(2)}, u32[]{:S(2)}) collective-permute-start(bf16[256,128]{1,0:T(8,128)(2,1)S(1)} %shard_map.93), channel_id=1, source_target_pairs={{0,25},{1,24},{2,27},{3,26},{4,29},{5,28},{6,31},{7,30},{8,17},{9,... | collective-permute-start | bytes 196616 | tf_op jit(solution)/shard_map/ppermute | solution.py:23
  23.4 1.3 %collective-permute-start.11 = (bf16[256,128]{1,0:T(8,128)(2,1)S(1)}, bf16[256,128]{1,0:T(8,128)(2,1)S(1)}, u32[]{:S(2)}, u32[]{:S(2)}) collective-permute-start(bf16[256,128]{1,0:T(8,128)(2,1)S(1)} %shard_map.93), channel_id=1, source_target_pairs={{0,17},{1,16},{2,19},{3,18},{4,21},{5,20},{6,23},{7,22},{8,25},{9,... | collective-permute-start | bytes 196616 | tf_op jit(solution)/shard_map/ppermute | solution.py:23
  24.6 1.8 %collective-permute-done.8.refs_0_ = bf16[256,128]{1,0:T(8,128)(2,1)S(1)} collective-permute-done((bf16[256,128]{1,0:T(8,128)(2,1)S(1)}, bf16[256,128]{1,0:T(8,128)(2,1)S(1)}, u32[]{:S(2)}, u32[]{:S(2)}) %collective-permute-start.8) | collective-permute-done | bytes 65568 | tf_op jit(solution)/shard_map/ppermute | solution.py:23
  26.5 0.6 %copy-done.5 = f32[128]{0:T(128)S(1)} copy-done((f32[128]{0:T(128)S(1)}, f32[128]{0:T(128)}, u32[]{:S(2)}) %copy-start.5) | copy-done | bytes 536
  27.7 1.4 %collective-permute-done.9.refs_0_ = bf16[256,128]{1,0:T(8,128)(2,1)S(1)} collective-permute-done((bf16[256,128]{1,0:T(8,128)(2,1)S(1)}, bf16[256,128]{1,0:T(8,128)(2,1)S(1)}, u32[]{:S(2)}, u32[]{:S(2)}) %collective-permute-start.9) | collective-permute-done | bytes 65568 | tf_op jit(solution)/shard_map/ppermute | solution.py:23
  30.1 0.5 %shard_map.97 = (bf16[256,128]{1,0:T(8,128)(2,1)S(1)}, f32[16,128,128]{2,1,0:T(8,128)S(1)}, bf16[384,128]{1,0:T(8,128)(2,1)S(1)}, bf16[768,128]{1,0:T(8,128)(2,1)S(1)}) custom-call(s32[16,128]{1,0:T(8,128)S(1)} %shard_map.89.place_ref, bf16[8,256,128]{2,1,0:T(8,128)(2,1)S(1)} %get-tuple-element.28.flipped_ref, ...), custom_call_target="tpu_custom_call", output_to_operand_aliasing={{1}: (6, {})} | custom-call | tf_op jit(solution)/shard_map/pallas_call | solution.py:272
  31.3 0.8 %collective-permute-done.12.got_ref = bf16[384,128]{1,0:T(8,128)(2,1)S(1)} collective-permute-done((bf16[384,128]{1,0:T(8,128)(2,1)S(1)}, bf16[384,128]{1,0:T(8,128)(2,1)S(1)}, u32[]{:S(2)}, u32[]{:S(2)}) %collective-permute-start.12) | collective-permute-done | bytes 98336 | tf_op jit(solution)/shard_map/ppermute | solution.py:17
  32.1 1.3 %collective-permute-start.16 = (bf16[384,128]{1,0:T(8,128)(2,1)S(1)}, bf16[384,128]{1,0:T(8,128)(2,1)S(1)}, u32[]{:S(2)}, u32[]{:S(2)}) collective-permute-start(bf16[384,128]{1,0:T(8,128)(2,1)S(1)} %shard_map.99.first_ref.sent_ref), channel_id=1, source_target_pairs={{0,7},{1,6},{2,5},{3,4},{4,3},{5,2},{6,1},{7,0},{8,15},{9,14},{10,... | collective-permute-start | bytes 294920 | tf_op jit(solution)/shard_map/ppermute | solution.py:17
  33.4 1.3 %collective-permute-start.15 = (bf16[384,128]{1,0:T(8,128)(2,1)S(1)}, bf16[384,128]{1,0:T(8,128)(2,1)S(1)}, u32[]{:S(2)}, u32[]{:S(2)}) collective-permute-start(bf16[384,128]{1,0:T(8,128)(2,1)S(1)} %get-tuple-element.48), channel_id=1, source_target_pairs={{0,5},{1,4},{2,7},{3,6},{4,1},{5,0},{6,3},{7,2},{8,13},{9,12},{10,... | collective-permute-start | bytes 294920 | tf_op jit(solution)/shard_map/ppermute | solution.py:17
  35.2 0.7 %shard_map.98 = bf16[1024,128]{1,0:T(8,128)(2,1)} custom-call(bf16[256,128]{1,0:T(8,128)(2,1)S(1)} %get-tuple-element.33.refs_0_, bf16[256,128]{1,0:T(8,128)(2,1)S(1)} %get-tuple-element.36.refs_1_, bf16[256,128]{1,0:T(8,128)(2,1)S(1)} %get-tuple-element.39.refs_2_, bf16[256,128]{1,0:T(8,128)(2,1)S(1)} %get-tuple-element.42.refs_3_), custom_call_target="tpu_custom_call" | custom-call | tf_op jit(solution)/shard_map/pallas_call | solution.py:289
  36.0 1.9 %collective-permute-done.16.got_ref = bf16[384,128]{1,0:T(8,128)(2,1)S(1)} collective-permute-done((bf16[384,128]{1,0:T(8,128)(2,1)S(1)}, bf16[384,128]{1,0:T(8,128)(2,1)S(1)}, u32[]{:S(2)}, u32[]{:S(2)}) %collective-permute-start.16) | collective-permute-done | bytes 98336 | tf_op jit(solution)/shard_map/ppermute | solution.py:17
  37.9 2.3 %collective-permute-done.15.refs_0_ = bf16[384,128]{1,0:T(8,128)(2,1)S(1)} collective-permute-done((bf16[384,128]{1,0:T(8,128)(2,1)S(1)}, bf16[384,128]{1,0:T(8,128)(2,1)S(1)}, u32[]{:S(2)}, u32[]{:S(2)}) %collective-permute-start.15) | collective-permute-done | bytes 98336 | tf_op jit(solution)/shard_map/ppermute | solution.py:17
  40.2 0.7 %shard_map.103 = (f32[256,128]{1,0:T(8,128)}, f32[128,128]{1,0:T(8,128)}) custom-call(f32[256,128]{1,0:T(8,128)S(1)} %get-tuple-element.46.own_ref, bf16[384,128]{1,0:T(8,128)(2,1)S(1)} %shard_map.99.first_ref.sent_ref, bf16[384,128]{1,0:T(8,128)(2,1)S(1)} %collective-permute-done.14.got_ref, f32[384,128]{1,0:T(8,128)S(1)} %shard_map.102.refs_0_), custom_call_target="tpu_custom_call" | custom-call | tf_op jit(solution)/shard_map/pallas_call | solution.py:298
  (43 shorter events, 5.4 us)
Async XLA Ops:
  0.6 6.4 %collective-permute-start.2 = (bf16[256,128]{1,0:T(8,128)(2,1)}, bf16[256,128]{1,0:T(8,128)(2,1)S(1)}, u32[]{:S(2)}, u32[]{:S(2)}) collective-permute-start(bf16[256,128]{1,0:T(8,128)(2,1)} %features_ref.1), channel_id=1, source_target_pairs={{0,7},{1,6},{2,5},{3,4},{4,3},{5,2},{6,1},{7,0},{8,15},{9,14},{10,... | collective-permute-start | bytes 196616 | tf_op jit(solution)/shard_map/ppermute | solution.py:17
  4.0 4.2 %collective-permute-start.1 = (bf16[256,128]{1,0:T(8,128)(2,1)}, bf16[256,128]{1,0:T(8,128)(2,1)S(1)}, u32[]{:S(2)}, u32[]{:S(2)}) collective-permute-start(bf16[256,128]{1,0:T(8,128)(2,1)} %features_ref.1), channel_id=1, source_target_pairs={{0,5},{1,4},{2,7},{3,6},{4,1},{5,0},{6,3},{7,2},{8,13},{9,12},{10,... | collective-permute-start | bytes 196616 | tf_op jit(solution)/shard_map/ppermute | solution.py:17
  4.8 4.5 %collective-permute-start = (bf16[256,128]{1,0:T(8,128)(2,1)}, bf16[256,128]{1,0:T(8,128)(2,1)S(1)}, u32[]{:S(2)}, u32[]{:S(2)}) collective-permute-start(bf16[256,128]{1,0:T(8,128)(2,1)} %features_ref.1), channel_id=1, source_target_pairs={{0,3},{1,2},{2,1},{3,0},{4,7},{5,6},{6,5},{7,4},{8,11},{9,10},{10,... | collective-permute-start | bytes 196616 | tf_op jit(solution)/shard_map/ppermute | solution.py:17
  5.0 1.0 %copy-start.1 = (bf16[8,2,128,128]{3,2,1,0:T(8,128)(2,1)S(1)}, bf16[8,2,128,128]{3,2,1,0:T(8,128)(2,1)}, u32[]{:S(2)}) copy-start(bf16[8,2,128,128]{3,2,1,0:T(8,128)(2,1)} %vals_ref.3) | copy-start | bytes 1572868
  6.0 0.8 %copy-start.4 = (bf16[256,128]{1,0:T(8,128)(2,1)S(1)}, bf16[256,128]{1,0:T(8,128)(2,1)}, u32[]{:S(2)}) copy-start(bf16[256,128]{1,0:T(8,128)(2,1)} %features_ref.1) | copy-start | bytes 196612
  7.1 3.9 %copy-start.2 = (bf16[8,2,128,128]{3,2,1,0:T(8,128)(2,1)S(1)}, bf16[8,2,128,128]{3,2,1,0:T(8,128)(2,1)}, u32[]{:S(2)}) copy-start(bf16[8,2,128,128]{3,2,1,0:T(8,128)(2,1)} %vals_ref.3) | copy-start | bytes 1572868
  9.4 0.7 %copy-start.6 = (s32[8,2]{0,1:T(2,128)S(1)}, s32[8,2]{0,1:T(2,128)}, u32[]{:S(2)}) copy-start(s32[8,2]{0,1:T(2,128)} %param.6) | copy-start | bytes 196
  9.4 1.6 %collective-permute-start.3 = (bf16[1024,128]{1,0:T(8,128)(2,1)S(1)}, bf16[1024,128]{1,0:T(8,128)(2,1)S(1)}, u32[]{:S(2)}, u32[]{:S(2)}) collective-permute-start(bf16[1024,128]{1,0:T(8,128)(2,1)S(1)} %shard_map.88._.mine_ref), channel_id=1, source_target_pairs={{0,1},{1,0},{2,3},{3,2},{4,5},{5,4},{6,7},{7,6},{8,9},{9,8},{10,11... | collective-permute-start | bytes 786440 | tf_op jit(solution)/shard_map/ppermute | solution.py:17
  11.3 6.1 %collective-permute-start.4 = (bf16[256,128]{1,0:T(8,128)(2,1)S(1)}, bf16[256,128]{1,0:T(8,128)(2,1)S(1)}, u32[]{:S(2)}, u32[]{:S(2)}) collective-permute-start(bf16[256,128]{1,0:T(8,128)(2,1)S(1)} %get-tuple-element.29), channel_id=1, source_target_pairs={{0,25},{1,24},{2,27},{3,26},{4,29},{5,28},{6,31},{7,30},{8,17},{9,... | collective-permute-start | bytes 196616 | tf_op jit(solution)/shard_map/ppermute | solution.py:23
  14.8 5.5 %collective-permute-start.5 = (bf16[256,128]{1,0:T(8,128)(2,1)S(1)}, bf16[256,128]{1,0:T(8,128)(2,1)S(1)}, u32[]{:S(2)}, u32[]{:S(2)}) collective-permute-start(bf16[256,128]{1,0:T(8,128)(2,1)S(1)} %get-tuple-element.30), channel_id=1, source_target_pairs={{0,9},{1,8},{2,11},{3,10},{4,13},{5,12},{6,15},{7,14},{8,1},{9,0},... | collective-permute-start | bytes 196616 | tf_op jit(solution)/shard_map/ppermute | solution.py:23
  14.8 5.5 %collective-permute-start.6 = (bf16[256,128]{1,0:T(8,128)(2,1)S(1)}, bf16[256,128]{1,0:T(8,128)(2,1)S(1)}, u32[]{:S(2)}, u32[]{:S(2)}) collective-permute-start(bf16[256,128]{1,0:T(8,128)(2,1)S(1)} %get-tuple-element.31), channel_id=1, source_target_pairs={{0,17},{1,16},{2,19},{3,18},{4,21},{5,20},{6,23},{7,22},{8,25},{9,... | collective-permute-start | bytes 196616 | tf_op jit(solution)/shard_map/ppermute | solution.py:23
  15.4 4.9 %collective-permute-start.7 = (f32[256,128]{1,0:T(8,128)S(1)}, f32[256,128]{1,0:T(8,128)S(1)}, u32[]{:S(2)}, u32[]{:S(2)}) collective-permute-start(f32[256,128]{1,0:T(8,128)S(1)} %get-tuple-element.32), channel_id=1, source_target_pairs={{0,1},{1,0},{2,3},{3,2},{4,5},{5,4},{6,7},{7,6},{8,9},{9,8},{10,11... | collective-permute-start | bytes 393224 | tf_op jit(solution)/shard_map/ppermute | solution.py:17
  20.3 6.2 %copy-start = (bf16[1024,128]{1,0:T(8,128)(2,1)S(1)}, bf16[1024,128]{1,0:T(8,128)(2,1)}, u32[]{:S(2)}) copy-start(bf16[1024,128]{1,0:T(8,128)(2,1)} %cotangent_ref.7) | copy-start | bytes 786436
  20.3 6.2 %copy-start.3 = (bf16[128,128]{1,0:T(8,128)(2,1)S(1)}, bf16[128,128]{1,0:T(8,128)(2,1)}, u32[]{:S(2)}) copy-start(bf16[128,128]{1,0:T(8,128)(2,1)} %weight_ref.7) | copy-start | bytes 98308
  20.4 6.1 %collective-permute-start.8 = (bf16[256,128]{1,0:T(8,128)(2,1)S(1)}, bf16[256,128]{1,0:T(8,128)(2,1)S(1)}, u32[]{:S(2)}, u32[]{:S(2)}) collective-permute-start(bf16[256,128]{1,0:T(8,128)(2,1)S(1)} %shard_map.93), channel_id=1, source_target_pairs={{0,25},{1,24},{2,27},{3,26},{4,29},{5,28},{6,31},{7,30},{8,17},{9,... | collective-permute-start | bytes 196616 | tf_op jit(solution)/shard_map/ppermute | solution.py:23
  22.7 6.4 %collective-permute-start.9 = (bf16[256,128]{1,0:T(8,128)(2,1)S(1)}, bf16[256,128]{1,0:T(8,128)(2,1)S(1)}, u32[]{:S(2)}, u32[]{:S(2)}) collective-permute-start(bf16[256,128]{1,0:T(8,128)(2,1)S(1)} %shard_map.93), channel_id=1, source_target_pairs={{0,9},{1,8},{2,11},{3,10},{4,13},{5,12},{6,15},{7,14},{8,1},{9,0},... | collective-permute-start | bytes 196616 | tf_op jit(solution)/shard_map/ppermute | solution.py:23
  23.2 6.3 %collective-permute-start.10 = (bf16[256,128]{1,0:T(8,128)(2,1)S(1)}, bf16[256,128]{1,0:T(8,128)(2,1)S(1)}, u32[]{:S(2)}, u32[]{:S(2)}) collective-permute-start(bf16[256,128]{1,0:T(8,128)(2,1)S(1)} %shard_map.93), channel_id=1, source_target_pairs={{0,1},{1,0},{2,3},{3,2},{4,5},{5,4},{6,7},{7,6},{8,9},{9,8},{10,11... | collective-permute-start | bytes 196616 | tf_op jit(solution)/shard_map/ppermute | solution.py:17
  23.4 6.7 %collective-permute-start.11 = (bf16[256,128]{1,0:T(8,128)(2,1)S(1)}, bf16[256,128]{1,0:T(8,128)(2,1)S(1)}, u32[]{:S(2)}, u32[]{:S(2)}) collective-permute-start(bf16[256,128]{1,0:T(8,128)(2,1)S(1)} %shard_map.93), channel_id=1, source_target_pairs={{0,17},{1,16},{2,19},{3,18},{4,21},{5,20},{6,23},{7,22},{8,25},{9,... | collective-permute-start | bytes 196616 | tf_op jit(solution)/shard_map/ppermute | solution.py:23
  26.5 0.7 %copy-start.5 = (f32[128]{0:T(128)S(1)}, f32[128]{0:T(128)}, u32[]{:S(2)}) copy-start(f32[128]{0:T(128)} %param.10) | copy-start | bytes 1540
  30.7 1.4 %collective-permute-start.12 = (bf16[384,128]{1,0:T(8,128)(2,1)S(1)}, bf16[384,128]{1,0:T(8,128)(2,1)S(1)}, u32[]{:S(2)}, u32[]{:S(2)}) collective-permute-start(bf16[384,128]{1,0:T(8,128)(2,1)S(1)} %get-tuple-element.44.sent_ref), channel_id=1, source_target_pairs={{0,1},{1,0},{2,3},{3,2},{4,5},{5,4},{6,7},{7,6},{8,9},{9,8},{10,11... | collective-permute-start | bytes 294920 | tf_op jit(solution)/shard_map/ppermute | solution.py:17
  30.9 2.5 %collective-permute-start.13 = (bf16[768,128]{1,0:T(8,128)(2,1)S(1)}, bf16[768,128]{1,0:T(8,128)(2,1)S(1)}, u32[]{:S(2)}, u32[]{:S(2)}) collective-permute-start(bf16[768,128]{1,0:T(8,128)(2,1)S(1)} %get-tuple-element.45), channel_id=1, source_target_pairs={{0,1},{1,0},{2,3},{3,2},{4,5},{5,4},{6,7},{7,6},{8,9},{9,8},{10,11... | collective-permute-start | bytes 589832 | tf_op jit(solution)/shard_map/ppermute | solution.py:17
  32.1 5.8 %collective-permute-start.16 = (bf16[384,128]{1,0:T(8,128)(2,1)S(1)}, bf16[384,128]{1,0:T(8,128)(2,1)S(1)}, u32[]{:S(2)}, u32[]{:S(2)}) collective-permute-start(bf16[384,128]{1,0:T(8,128)(2,1)S(1)} %shard_map.99.first_ref.sent_ref), channel_id=1, source_target_pairs={{0,7},{1,6},{2,5},{3,4},{4,3},{5,2},{6,1},{7,0},{8,15},{9,14},{10,... | collective-permute-start | bytes 294920 | tf_op jit(solution)/shard_map/ppermute | solution.py:17
  33.4 6.7 %collective-permute-start.15 = (bf16[384,128]{1,0:T(8,128)(2,1)S(1)}, bf16[384,128]{1,0:T(8,128)(2,1)S(1)}, u32[]{:S(2)}, u32[]{:S(2)}) collective-permute-start(bf16[384,128]{1,0:T(8,128)(2,1)S(1)} %get-tuple-element.48), channel_id=1, source_target_pairs={{0,5},{1,4},{2,7},{3,6},{4,1},{5,0},{6,3},{7,2},{8,13},{9,12},{10,... | collective-permute-start | bytes 294920 | tf_op jit(solution)/shard_map/ppermute | solution.py:17
  34.7 5.5 %collective-permute-start.14 = (bf16[384,128]{1,0:T(8,128)(2,1)S(1)}, bf16[384,128]{1,0:T(8,128)(2,1)S(1)}, u32[]{:S(2)}, u32[]{:S(2)}) collective-permute-start(bf16[384,128]{1,0:T(8,128)(2,1)S(1)} %get-tuple-element.47), channel_id=1, source_target_pairs={{0,3},{1,2},{2,1},{3,0},{4,7},{5,6},{6,5},{7,4},{8,11},{9,10},{10,... | collective-permute-start | bytes 294920 | tf_op jit(solution)/shard_map/ppermute | solution.py:17

commit v17 on v15

--- a/solution.py
+++ b/solution.py
@@ -49,17 +49,13 @@
         first += piece.shape[0]
 
 
-def last_join_kernel(*refs):
-    near, middle, out_ref = refs[:-2], refs[-2], refs[-1]
-    nodes = near[0].shape[0]
-    body = middle.shape[0] - 2 * nodes
-    out_ref[:nodes] = middle[body : body + nodes]
-    first = nodes
-    for piece in near:
-        out_ref[first : first + nodes] = piece[...]
-        first += nodes
-    out_ref[first : first + body] = middle[:body]
-    out_ref[first + body :] = middle[body + nodes :]
+def wrap_kernel(ends_ref, *refs):
+    out_ref = refs[-1]
+    nodes = ends_ref.shape[0] // 2
+    out_ref[:nodes] = ends_ref[:nodes]
+    for at, piece in enumerate(refs[:-1], 1):
+        out_ref[at * nodes : (at + 1) * nodes] = piece[...]
+    out_ref[out_ref.shape[0] - nodes :] = ends_ref[nodes:]
 
 
 def aggregate_kernel(rep, place_ref, vals_ref, mine_ref, far_ref, *outs):
@@ -229,17 +225,21 @@
         return call(join_kernel, shape((nodes_in, width), BF16), [VMEM] * len(values))(*values)
 
     across = [swap(features, "dom", 2 * chip + 1) for chip in range(1, chips)]
-    front = join(own, across[-1])
-    middle = join(*across[chips // 2 - 1 : -1], front)
-    mine = call(last_join_kernel, shape((chips * nodes, width), BF16), [VMEM] * (chips // 2))(
-        *across[: chips // 2 - 1], middle
-    )
-    far = swap(mine, "dom", 1)
+    ends = join(own, across[-1])
+    far_ends = swap(ends, "dom", 1)
+    half = chips // 2 - 1
+    beyond = [swap(piece, "dom", 1) for piece in across[half:-1]]
+    beyond = [swap(piece, "dom", 1) for piece in across[:half]] + beyond
+
+    def wrap(*values):
+        return call(wrap_kernel, shape((chips * nodes, width), BF16), [VMEM] * (chips - 1))(*values)
+
+    mine, far = wrap(ends, *across[:-1]), wrap(far_ends, *beyond)
     place = call(
         functools.partial(place_kernel, own_blocks, dom),
         shape((rows * count, 128), jnp.int32),
         [VMEM] * 2,
-    )(cols.T, mine)
+    )(cols.T, ends)
 
     partials = call(
         functools.partial(aggregate_kernel, rep),

time: 39.9 us -> 39.9 us (level)
  starting transfers between devices: 17.1 us -> 17.8 us
  local copies, waits for them, and re-layouts: 3.04 us -> 2.62 us
    ppermute x15 -> x17, starting transfers between devices: 17.1 us -> 17.8 us  [swap(): return lax.ppermute(value, axis, [(i, i ^ distance) for i in range(size)])]
    unnamed x14, local copies, waits for them, and re-layouts: 3.04 us -> 2.62 us
    ppermute x15 -> x17, waiting for transfers between devices: 14.3 us -> 14 us  [swap(): return lax.ppermute(value, axis, [(i, i ^ distance) for i in range(size)])]
  transfers between devices with their start and end apart: 15 -> 17, of which waited for: 12 -> 13; matrix products, arithmetic and copies ran while one was open for 0% -> 0% of each run, Pallas kernels for 7% -> 7%
where the time goes in v17:
time: 39.9 us; the launch traced here: 39.7 us
  starting transfers between devices  17.8 us (45%)
  waiting for transfers between devices  14 us (35%)
  Pallas kernels  4.44 us (11%)
  local copies, waits for them, and re-layouts  2.62 us (7%)
  between operations  0.81 us (2%)
    ppermute x17, starting transfers between devices, swap(): return lax.ppermute(value, axis, [(i, i ^ distance) for i in range(size)])  17.8 us
    ppermute x17, waiting for transfers between devices, swap(): return lax.ppermute(value, axis, [(i, i ^ distance) for i in range(size)])  14 us
    unnamed x14, local copies, waits for them, and re-layouts  2.62 us
    pallas_call x4, Pallas kernels, body(): call(functools.partial(layer_kernel, rep, count, own_blocks, j), outs, [V...  2.11 us
  transfers between devices with their start and end apart: 17, of which 13 were waited for; matrix products, arithmetic and copies ran while one was open for 0% of the time, Pallas kernels for 7%

profile of v17, /device:TPU:0, one launch (start us, length us, event | category | flops | bytes accessed | tf_op | source)
XLA Modules:
  0.0 39.7 jit_solution(3055890911023910943)
XLA Ops:
  0.6 3.4 %collective-permute-start = (bf16[256,128]{1,0:T(8,128)(2,1)}, bf16[256,128]{1,0:T(8,128)(2,1)S(1)}, u32[]{:S(2)}, u32[]{:S(2)}) collective-permute-start(bf16[256,128]{1,0:T(8,128)(2,1)} %features_ref.1), channel_id=1, source_target_pairs={{0,7},{1,6},{2,5},{3,4},{4,3},{5,2},{6,1},{7,0},{8,15},{9,14},{10,... | collective-permute-start | bytes 196616 | tf_op jit(solution)/shard_map/ppermute | solution.py:17
  4.0 0.8 %collective-permute-start.2 = (bf16[256,128]{1,0:T(8,128)(2,1)}, bf16[256,128]{1,0:T(8,128)(2,1)S(1)}, u32[]{:S(2)}, u32[]{:S(2)}) collective-permute-start(bf16[256,128]{1,0:T(8,128)(2,1)} %features_ref.1), channel_id=1, source_target_pairs={{0,5},{1,4},{2,7},{3,6},{4,1},{5,0},{6,3},{7,2},{8,13},{9,12},{10,... | collective-permute-start | bytes 196616 | tf_op jit(solution)/shard_map/ppermute | solution.py:17
  5.0 1.0 %copy-done.1 = bf16[8,2,128,128]{3,2,1,0:T(8,128)(2,1)S(1)} copy-done((bf16[8,2,128,128]{3,2,1,0:T(8,128)(2,1)S(1)}, bf16[8,2,128,128]{3,2,1,0:T(8,128)(2,1)}, u32[]{:S(2)}) %copy-start.1) | copy-done | bytes 524312
  6.0 0.8 %copy-done.4 = bf16[256,128]{1,0:T(8,128)(2,1)S(1)} copy-done((bf16[256,128]{1,0:T(8,128)(2,1)S(1)}, bf16[256,128]{1,0:T(8,128)(2,1)}, u32[]{:S(2)}) %copy-start.4) | copy-done | bytes 65560
  7.1 1.0 %collective-permute-done.2.refs_1_ = bf16[256,128]{1,0:T(8,128)(2,1)S(1)} collective-permute-done((bf16[256,128]{1,0:T(8,128)(2,1)}, bf16[256,128]{1,0:T(8,128)(2,1)S(1)}, u32[]{:S(2)}, u32[]{:S(2)}) %collective-permute-start.2) | collective-permute-done | bytes 65568 | tf_op jit(solution)/shard_map/ppermute | solution.py:17
  8.2 0.7 %collective-permute-start.5 = (bf16[256,128]{1,0:T(8,128)(2,1)S(1)}, bf16[256,128]{1,0:T(8,128)(2,1)S(1)}, u32[]{:S(2)}, u32[]{:S(2)}) collective-permute-start(bf16[256,128]{1,0:T(8,128)(2,1)S(1)} %collective-permute-done.2.refs_1_), channel_id=1, source_target_pairs={{0,1},{1,0},{2,3},{3,2},{4,5},{5,4},{6,7},{7,6},{8,9},{9,8},{10,11... | collective-permute-start | bytes 196616 | tf_op jit(solution)/shard_map/ppermute | solution.py:17
  9.8 0.8 %collective-permute-done.4.refs_0_ = bf16[256,128]{1,0:T(8,128)(2,1)S(1)} collective-permute-done((bf16[256,128]{1,0:T(8,128)(2,1)S(1)}, bf16[256,128]{1,0:T(8,128)(2,1)S(1)}, u32[]{:S(2)}, u32[]{:S(2)}) %collective-permute-start.4) | collective-permute-done | bytes 65568 | tf_op jit(solution)/shard_map/ppermute | solution.py:17
  11.1 3.7 %collective-permute-start.6 = (bf16[256,128]{1,0:T(8,128)(2,1)S(1)}, bf16[256,128]{1,0:T(8,128)(2,1)S(1)}, u32[]{:S(2)}, u32[]{:S(2)}) collective-permute-start(bf16[256,128]{1,0:T(8,128)(2,1)S(1)} %get-tuple-element.30), channel_id=1, source_target_pairs={{0,24},{8,16},{16,8},{24,0},{1,25},{9,17},{17,9},{25,1},{2,26},{10... | collective-permute-start | bytes 196616 | tf_op jit(solution)/shard_map/ppermute | solution.py:17
  14.8 0.8 %collective-permute-start.8 = (bf16[256,128]{1,0:T(8,128)(2,1)S(1)}, bf16[256,128]{1,0:T(8,128)(2,1)S(1)}, u32[]{:S(2)}, u32[]{:S(2)}) collective-permute-start(bf16[256,128]{1,0:T(8,128)(2,1)S(1)} %get-tuple-element.32), channel_id=1, source_target_pairs={{0,16},{8,24},{16,0},{24,8},{1,17},{9,25},{17,1},{25,9},{2,18},{10... | collective-permute-start | bytes 196616 | tf_op jit(solution)/shard_map/ppermute | solution.py:17
  15.5 2.3 %collective-permute-done.6.b_ref = bf16[256,128]{1,0:T(8,128)(2,1)S(1)} collective-permute-done((bf16[256,128]{1,0:T(8,128)(2,1)S(1)}, bf16[256,128]{1,0:T(8,128)(2,1)S(1)}, u32[]{:S(2)}, u32[]{:S(2)}) %collective-permute-start.6) | collective-permute-done | bytes 65568 | tf_op jit(solution)/shard_map/ppermute | solution.py:17
  17.9 2.3 %collective-permute-done.7.b_ref = bf16[256,128]{1,0:T(8,128)(2,1)S(1)} collective-permute-done((bf16[256,128]{1,0:T(8,128)(2,1)S(1)}, bf16[256,128]{1,0:T(8,128)(2,1)S(1)}, u32[]{:S(2)}, u32[]{:S(2)}) %collective-permute-start.7) | collective-permute-done | bytes 65568 | tf_op jit(solution)/shard_map/ppermute | solution.py:17
  20.6 2.3 %collective-permute-start.9 = (bf16[256,128]{1,0:T(8,128)(2,1)S(1)}, bf16[256,128]{1,0:T(8,128)(2,1)S(1)}, u32[]{:S(2)}, u32[]{:S(2)}) collective-permute-start(bf16[256,128]{1,0:T(8,128)(2,1)S(1)} %shard_map.93.refs_0_), channel_id=1, source_target_pairs={{0,24},{8,16},{16,8},{24,0},{1,25},{9,17},{17,9},{25,1},{2,26},{10... | collective-permute-start | bytes 196616 | tf_op jit(solution)/shard_map/ppermute | solution.py:17
  23.5 1.6 %collective-permute-start.11 = (bf16[256,128]{1,0:T(8,128)(2,1)S(1)}, bf16[256,128]{1,0:T(8,128)(2,1)S(1)}, u32[]{:S(2)}, u32[]{:S(2)}) collective-permute-start(bf16[256,128]{1,0:T(8,128)(2,1)S(1)} %shard_map.93.refs_0_), channel_id=1, source_target_pairs={{0,16},{8,24},{16,0},{24,8},{1,17},{9,25},{17,1},{25,9},{2,18},{10... | collective-permute-start | bytes 196616 | tf_op jit(solution)/shard_map/ppermute | solution.py:17
  25.1 0.6 %copy-done.5 = f32[128]{0:T(128)S(1)} copy-done((f32[128]{0:T(128)S(1)}, f32[128]{0:T(128)}, u32[]{:S(2)}) %copy-start.5) | copy-done | bytes 536
  26.3 0.6 %collective-permute-done.9.refs_0_ = bf16[256,128]{1,0:T(8,128)(2,1)S(1)} collective-permute-done((bf16[256,128]{1,0:T(8,128)(2,1)S(1)}, bf16[256,128]{1,0:T(8,128)(2,1)S(1)}, u32[]{:S(2)}, u32[]{:S(2)}) %collective-permute-start.9) | collective-permute-done | bytes 65568 | tf_op jit(solution)/shard_map/ppermute | solution.py:17
  27.4 0.6 %collective-permute-done.10.refs_0_ = bf16[256,128]{1,0:T(8,128)(2,1)S(1)} collective-permute-done((bf16[256,128]{1,0:T(8,128)(2,1)S(1)}, bf16[256,128]{1,0:T(8,128)(2,1)S(1)}, u32[]{:S(2)}, u32[]{:S(2)}) %collective-permute-start.10) | collective-permute-done | bytes 65568 | tf_op jit(solution)/shard_map/ppermute | solution.py:17
  28.9 0.5 %shard_map.97 = (bf16[256,128]{1,0:T(8,128)(2,1)S(1)}, f32[16,128,128]{2,1,0:T(8,128)S(1)}, bf16[384,128]{1,0:T(8,128)(2,1)S(1)}, bf16[768,128]{1,0:T(8,128)(2,1)S(1)}) custom-call(s32[16,128]{1,0:T(8,128)S(1)} %shard_map.87.place_ref, bf16[8,256,128]{2,1,0:T(8,128)(2,1)S(1)} %get-tuple-element.28.flipped_ref, ...), custom_call_target="tpu_custom_call", output_to_operand_aliasing={{1}: (6, {})} | custom-call | tf_op jit(solution)/shard_map/pallas_call | solution.py:270
  30.0 0.8 %collective-permute-done.12.got_ref = bf16[384,128]{1,0:T(8,128)(2,1)S(1)} collective-permute-done((bf16[384,128]{1,0:T(8,128)(2,1)S(1)}, bf16[384,128]{1,0:T(8,128)(2,1)S(1)}, u32[]{:S(2)}, u32[]{:S(2)}) %collective-permute-start.12) | collective-permute-done | bytes 98336 | tf_op jit(solution)/shard_map/ppermute | solution.py:17
  30.8 1.3 %collective-permute-start.16 = (bf16[384,128]{1,0:T(8,128)(2,1)S(1)}, bf16[384,128]{1,0:T(8,128)(2,1)S(1)}, u32[]{:S(2)}, u32[]{:S(2)}) collective-permute-start(bf16[384,128]{1,0:T(8,128)(2,1)S(1)} %shard_map.99.first_ref.sent_ref), channel_id=1, source_target_pairs={{0,7},{1,6},{2,5},{3,4},{4,3},{5,2},{6,1},{7,0},{8,15},{9,14},{10,... | collective-permute-start | bytes 294920 | tf_op jit(solution)/shard_map/ppermute | solution.py:17
  32.2 1.3 %collective-permute-start.15 = (bf16[384,128]{1,0:T(8,128)(2,1)S(1)}, bf16[384,128]{1,0:T(8,128)(2,1)S(1)}, u32[]{:S(2)}, u32[]{:S(2)}) collective-permute-start(bf16[384,128]{1,0:T(8,128)(2,1)S(1)} %get-tuple-element.48), channel_id=1, source_target_pairs={{0,5},{1,4},{2,7},{3,6},{4,1},{5,0},{6,3},{7,2},{8,13},{9,12},{10,... | collective-permute-start | bytes 294920 | tf_op jit(solution)/shard_map/ppermute | solution.py:17
  34.0 0.7 %shard_map.98 = bf16[1024,128]{1,0:T(8,128)(2,1)} custom-call(bf16[256,128]{1,0:T(8,128)(2,1)S(1)} %get-tuple-element.33.refs_0_, bf16[256,128]{1,0:T(8,128)(2,1)S(1)} %get-tuple-element.36.refs_1_, bf16[256,128]{1,0:T(8,128)(2,1)S(1)} %get-tuple-element.39.refs_2_, bf16[256,128]{1,0:T(8,128)(2,1)S(1)} %get-tuple-element.42.refs_3_), custom_call_target="tpu_custom_call" | custom-call | tf_op jit(solution)/shard_map/pallas_call | solution.py:287
  34.7 1.9 %collective-permute-done.16.got_ref = bf16[384,128]{1,0:T(8,128)(2,1)S(1)} collective-permute-done((bf16[384,128]{1,0:T(8,128)(2,1)S(1)}, bf16[384,128]{1,0:T(8,128)(2,1)S(1)}, u32[]{:S(2)}, u32[]{:S(2)}) %collective-permute-start.16) | collective-permute-done | bytes 98336 | tf_op jit(solution)/shard_map/ppermute | solution.py:17
  36.7 2.3 %collective-permute-done.15.refs_0_ = bf16[384,128]{1,0:T(8,128)(2,1)S(1)} collective-permute-done((bf16[384,128]{1,0:T(8,128)(2,1)S(1)}, bf16[384,128]{1,0:T(8,128)(2,1)S(1)}, u32[]{:S(2)}, u32[]{:S(2)}) %collective-permute-start.15) | collective-permute-done | bytes 98336 | tf_op jit(solution)/shard_map/ppermute | solution.py:17
  39.0 0.7 %shard_map.103 = (f32[256,128]{1,0:T(8,128)}, f32[128,128]{1,0:T(8,128)}) custom-call(f32[256,128]{1,0:T(8,128)S(1)} %get-tuple-element.46.own_ref, bf16[384,128]{1,0:T(8,128)(2,1)S(1)} %shard_map.99.first_ref.sent_ref, bf16[384,128]{1,0:T(8,128)(2,1)S(1)} %collective-permute-done.14.got_ref, f32[384,128]{1,0:T(8,128)S(1)} %shard_map.102.refs_0_), custom_call_target="tpu_custom_call" | custom-call | tf_op jit(solution)/shard_map/pallas_call | solution.py:296
  (43 shorter events, 5.8 us)
Async XLA Ops:
  0.6 6.4 %collective-permute-start = (bf16[256,128]{1,0:T(8,128)(2,1)}, bf16[256,128]{1,0:T(8,128)(2,1)S(1)}, u32[]{:S(2)}, u32[]{:S(2)}) collective-permute-start(bf16[256,128]{1,0:T(8,128)(2,1)} %features_ref.1), channel_id=1, source_target_pairs={{0,7},{1,6},{2,5},{3,4},{4,3},{5,2},{6,1},{7,0},{8,15},{9,14},{10,... | collective-permute-start | bytes 196616 | tf_op jit(solution)/shard_map/ppermute | solution.py:17
  4.0 4.2 %collective-permute-start.2 = (bf16[256,128]{1,0:T(8,128)(2,1)}, bf16[256,128]{1,0:T(8,128)(2,1)S(1)}, u32[]{:S(2)}, u32[]{:S(2)}) collective-permute-start(bf16[256,128]{1,0:T(8,128)(2,1)} %features_ref.1), channel_id=1, source_target_pairs={{0,5},{1,4},{2,7},{3,6},{4,1},{5,0},{6,3},{7,2},{8,13},{9,12},{10,... | collective-permute-start | bytes 196616 | tf_op jit(solution)/shard_map/ppermute | solution.py:17
  4.8 4.5 %collective-permute-start.1 = (bf16[256,128]{1,0:T(8,128)(2,1)}, bf16[256,128]{1,0:T(8,128)(2,1)S(1)}, u32[]{:S(2)}, u32[]{:S(2)}) collective-permute-start(bf16[256,128]{1,0:T(8,128)(2,1)} %features_ref.1), channel_id=1, source_target_pairs={{0,3},{1,2},{2,1},{3,0},{4,7},{5,6},{6,5},{7,4},{8,11},{9,10},{10,... | collective-permute-start | bytes 196616 | tf_op jit(solution)/shard_map/ppermute | solution.py:17
  5.0 1.0 %copy-start.1 = (bf16[8,2,128,128]{3,2,1,0:T(8,128)(2,1)S(1)}, bf16[8,2,128,128]{3,2,1,0:T(8,128)(2,1)}, u32[]{:S(2)}) copy-start(bf16[8,2,128,128]{3,2,1,0:T(8,128)(2,1)} %vals_ref.3) | copy-start | bytes 1572868
  6.0 0.8 %copy-start.4 = (bf16[256,128]{1,0:T(8,128)(2,1)S(1)}, bf16[256,128]{1,0:T(8,128)(2,1)}, u32[]{:S(2)}) copy-start(bf16[256,128]{1,0:T(8,128)(2,1)} %features_ref.1) | copy-start | bytes 196612
  7.1 2.4 %copy-start.6 = (s32[8,2]{0,1:T(2,128)S(1)}, s32[8,2]{0,1:T(2,128)}, u32[]{:S(2)}) copy-start(s32[8,2]{0,1:T(2,128)} %param.6) | copy-start | bytes 196
  7.1 3.5 %collective-permute-start.3 = (bf16[512,128]{1,0:T(8,128)(2,1)S(1)}, bf16[512,128]{1,0:T(8,128)(2,1)S(1)}, u32[]{:S(2)}, u32[]{:S(2)}) collective-permute-start(bf16[512,128]{1,0:T(8,128)(2,1)S(1)} %shard_map.86._.ends_ref), channel_id=1, source_target_pairs={{0,1},{1,0},{2,3},{3,2},{4,5},{5,4},{6,7},{7,6},{8,9},{9,8},{10,11... | collective-permute-start | bytes 393224 | tf_op jit(solution)/shard_map/ppermute | solution.py:17
  8.2 1.6 %collective-permute-start.5 = (bf16[256,128]{1,0:T(8,128)(2,1)S(1)}, bf16[256,128]{1,0:T(8,128)(2,1)S(1)}, u32[]{:S(2)}, u32[]{:S(2)}) collective-permute-start(bf16[256,128]{1,0:T(8,128)(2,1)S(1)} %collective-permute-done.2.refs_1_), channel_id=1, source_target_pairs={{0,1},{1,0},{2,3},{3,2},{4,5},{5,4},{6,7},{7,6},{8,9},{9,8},{10,11... | collective-permute-start | bytes 196616 | tf_op jit(solution)/shard_map/ppermute | solution.py:17
  9.3 1.3 %collective-permute-start.4 = (bf16[256,128]{1,0:T(8,128)(2,1)S(1)}, bf16[256,128]{1,0:T(8,128)(2,1)S(1)}, u32[]{:S(2)}, u32[]{:S(2)}) collective-permute-start(bf16[256,128]{1,0:T(8,128)(2,1)S(1)} %collective-permute-done.1.refs_0_), channel_id=1, source_target_pairs={{0,1},{1,0},{2,3},{3,2},{4,5},{5,4},{6,7},{7,6},{8,9},{9,8},{10,11... | collective-permute-start | bytes 196616 | tf_op jit(solution)/shard_map/ppermute | solution.py:17
  9.7 1.0 %copy-start.2 = (bf16[8,2,128,128]{3,2,1,0:T(8,128)(2,1)S(1)}, bf16[8,2,128,128]{3,2,1,0:T(8,128)(2,1)}, u32[]{:S(2)}) copy-start(bf16[8,2,128,128]{3,2,1,0:T(8,128)(2,1)} %vals_ref.3) | copy-start | bytes 1572868
  11.1 6.8 %collective-permute-start.6 = (bf16[256,128]{1,0:T(8,128)(2,1)S(1)}, bf16[256,128]{1,0:T(8,128)(2,1)S(1)}, u32[]{:S(2)}, u32[]{:S(2)}) collective-permute-start(bf16[256,128]{1,0:T(8,128)(2,1)S(1)} %get-tuple-element.30), channel_id=1, source_target_pairs={{0,24},{8,16},{16,8},{24,0},{1,25},{9,17},{17,9},{25,1},{2,26},{10... | collective-permute-start | bytes 196616 | tf_op jit(solution)/shard_map/ppermute | solution.py:17
  14.8 5.4 %collective-permute-start.7 = (bf16[256,128]{1,0:T(8,128)(2,1)S(1)}, bf16[256,128]{1,0:T(8,128)(2,1)S(1)}, u32[]{:S(2)}, u32[]{:S(2)}) collective-permute-start(bf16[256,128]{1,0:T(8,128)(2,1)S(1)} %get-tuple-element.31), channel_id=1, source_target_pairs={{0,8},{8,0},{16,24},{24,16},{1,9},{9,1},{17,25},{25,17},{2,10},{10... | collective-permute-start | bytes 196616 | tf_op jit(solution)/shard_map/ppermute | solution.py:17
  14.8 5.9 %collective-permute-start.8 = (bf16[256,128]{1,0:T(8,128)(2,1)S(1)}, bf16[256,128]{1,0:T(8,128)(2,1)S(1)}, u32[]{:S(2)}, u32[]{:S(2)}) collective-permute-start(bf16[256,128]{1,0:T(8,128)(2,1)S(1)} %get-tuple-element.32), channel_id=1, source_target_pairs={{0,16},{8,24},{16,0},{24,8},{1,17},{9,25},{17,1},{25,9},{2,18},{10... | collective-permute-start | bytes 196616 | tf_op jit(solution)/shard_map/ppermute | solution.py:17
  17.9 7.2 %copy-start = (bf16[1024,128]{1,0:T(8,128)(2,1)S(1)}, bf16[1024,128]{1,0:T(8,128)(2,1)}, u32[]{:S(2)}) copy-start(bf16[1024,128]{1,0:T(8,128)(2,1)} %cotangent_ref.7) | copy-start | bytes 786436
  20.2 4.9 %copy-start.3 = (bf16[128,128]{1,0:T(8,128)(2,1)S(1)}, bf16[128,128]{1,0:T(8,128)(2,1)}, u32[]{:S(2)}) copy-start(bf16[128,128]{1,0:T(8,128)(2,1)} %weight_ref.7) | copy-start | bytes 98308
  20.6 6.3 %collective-permute-start.9 = (bf16[256,128]{1,0:T(8,128)(2,1)S(1)}, bf16[256,128]{1,0:T(8,128)(2,1)S(1)}, u32[]{:S(2)}, u32[]{:S(2)}) collective-permute-start(bf16[256,128]{1,0:T(8,128)(2,1)S(1)} %shard_map.93.refs_0_), channel_id=1, source_target_pairs={{0,24},{8,16},{16,8},{24,0},{1,25},{9,17},{17,9},{25,1},{2,26},{10... | collective-permute-start | bytes 196616 | tf_op jit(solution)/shard_map/ppermute | solution.py:17
  23.0 5.1 %collective-permute-start.10 = (bf16[256,128]{1,0:T(8,128)(2,1)S(1)}, bf16[256,128]{1,0:T(8,128)(2,1)S(1)}, u32[]{:S(2)}, u32[]{:S(2)}) collective-permute-start(bf16[256,128]{1,0:T(8,128)(2,1)S(1)} %shard_map.93.refs_0_), channel_id=1, source_target_pairs={{0,8},{8,0},{16,24},{24,16},{1,9},{9,1},{17,25},{25,17},{2,10},{10... | collective-permute-start | bytes 196616 | tf_op jit(solution)/shard_map/ppermute | solution.py:17
  23.5 5.4 %collective-permute-start.11 = (bf16[256,128]{1,0:T(8,128)(2,1)S(1)}, bf16[256,128]{1,0:T(8,128)(2,1)S(1)}, u32[]{:S(2)}, u32[]{:S(2)}) collective-permute-start(bf16[256,128]{1,0:T(8,128)(2,1)S(1)} %shard_map.93.refs_0_), channel_id=1, source_target_pairs={{0,16},{8,24},{16,0},{24,8},{1,17},{9,25},{17,1},{25,9},{2,18},{10... | collective-permute-start | bytes 196616 | tf_op jit(solution)/shard_map/ppermute | solution.py:17
  25.1 0.7 %copy-start.5 = (f32[128]{0:T(128)S(1)}, f32[128]{0:T(128)}, u32[]{:S(2)}) copy-start(f32[128]{0:T(128)} %param.10) | copy-start | bytes 1540
  29.4 1.4 %collective-permute-start.12 = (bf16[384,128]{1,0:T(8,128)(2,1)S(1)}, bf16[384,128]{1,0:T(8,128)(2,1)S(1)}, u32[]{:S(2)}, u32[]{:S(2)}) collective-permute-start(bf16[384,128]{1,0:T(8,128)(2,1)S(1)} %get-tuple-element.44.sent_ref), channel_id=1, source_target_pairs={{0,1},{1,0},{2,3},{3,2},{4,5},{5,4},{6,7},{7,6},{8,9},{9,8},{10,11... | collective-permute-start | bytes 294920 | tf_op jit(solution)/shard_map/ppermute | solution.py:17
  29.5 2.6 %collective-permute-start.13 = (bf16[768,128]{1,0:T(8,128)(2,1)S(1)}, bf16[768,128]{1,0:T(8,128)(2,1)S(1)}, u32[]{:S(2)}, u32[]{:S(2)}) collective-permute-start(bf16[768,128]{1,0:T(8,128)(2,1)S(1)} %get-tuple-element.45), channel_id=1, source_target_pairs={{0,1},{1,0},{2,3},{3,2},{4,5},{5,4},{6,7},{7,6},{8,9},{9,8},{10,11... | collective-permute-start | bytes 589832 | tf_op jit(solution)/shard_map/ppermute | solution.py:17
  30.8 5.8 %collective-permute-start.16 = (bf16[384,128]{1,0:T(8,128)(2,1)S(1)}, bf16[384,128]{1,0:T(8,128)(2,1)S(1)}, u32[]{:S(2)}, u32[]{:S(2)}) collective-permute-start(bf16[384,128]{1,0:T(8,128)(2,1)S(1)} %shard_map.99.first_ref.sent_ref), channel_id=1, source_target_pairs={{0,7},{1,6},{2,5},{3,4},{4,3},{5,2},{6,1},{7,0},{8,15},{9,14},{10,... | collective-permute-start | bytes 294920 | tf_op jit(solution)/shard_map/ppermute | solution.py:17
  32.2 6.8 %collective-permute-start.15 = (bf16[384,128]{1,0:T(8,128)(2,1)S(1)}, bf16[384,128]{1,0:T(8,128)(2,1)S(1)}, u32[]{:S(2)}, u32[]{:S(2)}) collective-permute-start(bf16[384,128]{1,0:T(8,128)(2,1)S(1)} %get-tuple-element.48), channel_id=1, source_target_pairs={{0,5},{1,4},{2,7},{3,6},{4,1},{5,0},{6,3},{7,2},{8,13},{9,12},{10,... | collective-permute-start | bytes 294920 | tf_op jit(solution)/shard_map/ppermute | solution.py:17
  33.5 5.5 %collective-permute-start.14 = (bf16[384,128]{1,0:T(8,128)(2,1)S(1)}, bf16[384,128]{1,0:T(8,128)(2,1)S(1)}, u32[]{:S(2)}, u32[]{:S(2)}) collective-permute-start(bf16[384,128]{1,0:T(8,128)(2,1)S(1)} %get-tuple-element.47), channel_id=1, source_target_pairs={{0,3},{1,2},{2,1},{3,0},{4,7},{5,6},{6,5},{7,4},{8,11},{9,10},{10,... | collective-permute-start | bytes 294920 | tf_op jit(solution)/shard_map/ppermute | solution.py:17

commit v18 on v17

--- a/solution.py
+++ b/solution.py
@@ -143,20 +143,18 @@
     blocks, size, _ = contrib_ref.shape
     nodes = out_ref.shape[0] - sent_ref.shape[1]
     last = contrib_ref[blocks // 2 - nodes // size : blocks // 2].reshape(nodes, -1)
+    weight = (sent_ref[nodes:].astype(F32) + got_ref[nodes:].astype(F32)).astype(BF16)
     out_ref[:nodes] = (last + got_ref[:nodes].astype(F32)).astype(BF16)
-    out_ref[nodes:] = (sent_ref[nodes:].astype(F32) + got_ref[nodes:].astype(F32)).astype(BF16)
-
-
-def rest_pair_kernel(contrib_ref, first_ref, got_ref, own_ref, *outs):
+    out_ref[nodes:] = weight
+
+
+def rest_pair_kernel(contrib_ref, got_ref, first_ref, weight_ref, own_ref, *outs):
     size, nodes = contrib_ref.shape[1], own_ref.shape[0]
-    for chip in range(len(outs) + 1):
+    weight_ref[...] = first_ref[nodes:]
+    for chip, out_ref in enumerate([own_ref, *outs]):
         mine = contrib_ref[chip * nodes // size : (chip + 1) * nodes // size].reshape(nodes, -1)
         total = mine + got_ref[chip * nodes : (chip + 1) * nodes].astype(F32)
-        if chip == 0:
-            own_ref[...] = total
-        else:
-            outs[chip - 1][:nodes] = total.astype(BF16)
-            outs[chip - 1][nodes:] = first_ref[nodes:]
+        out_ref[...] = total.astype(out_ref.dtype)
 
 
 def total_of(values):
@@ -169,23 +167,20 @@
     out_ref[...] = got_ref[...].astype(F32)
 
 
-def half_kernel(levels, *refs):
-    for level in range(1, levels):
-        first = 1 << level
-        got = refs[first - 2 : 2 * first - 2]
-        refs[level - levels][...] = total_of([g[...].astype(F32) for g in got])
-
-
-def final_kernel(own_ref, sent_ref, got_ref, *refs):
-    later, (feature_ref, weight_ref) = refs[:-2], refs[-2:]
+def early_sum_kernel(own_ref, lifted_ref, *refs):
+    got, out_ref = refs[:-1], refs[-1]
     nodes = own_ref.shape[0]
-    feature = own_ref[...] + got_ref[:nodes].astype(F32)
-    weight = sent_ref[nodes:].astype(F32) + got_ref[nodes:].astype(F32)
-    for value in later:
-        feature += value[:nodes]
-        weight += value[nodes:]
-    feature_ref[...] = feature
-    weight_ref[...] = weight
+    total = own_ref[...] + lifted_ref[:nodes]
+    for g in got:
+        total += g[...].astype(F32)
+    out_ref[...] = total
+
+
+def final_kernel(early_ref, lifted_ref, got_ref, *refs):
+    weights, (feature_ref, weight_ref) = refs[:-2], refs[-2:]
+    feature_ref[...] = early_ref[...] + got_ref[...].astype(F32)
+    across = lifted_ref[feature_ref.shape[0] :]
+    weight_ref[...] = total_of([w[...].astype(F32) for w in weights] + [across])
 
 
 def shape(dims, dtype):
@@ -278,26 +273,31 @@
 
     message = shape((nodes + width, width), BF16)
     got_first, got_rest = swap(first, "dom", 1), swap(rest, "dom", 1)
-    sends = [call(first_pair_kernel, message, [VMEM] * 3, cost=5000000000)(contrib, first, got_first)]
-    own, *others = call(
-        rest_pair_kernel, [shape((nodes, width), F32)] + [message] * (chips - 2), [VMEM] * 3, cost=1000000000
-    )(contrib, sends[0], got_rest)
-    sends = others + sends
-    got = {chip: swap(sends[chip - 1], "dom", 2 * chip + 1) for chip in range(chips - 1, 0, -1)}
+    first = call(first_pair_kernel, message, [VMEM] * 3, cost=5 * 10**9)(contrib, first, got_first)
+    pair_weight, own, *rest = call(
+        rest_pair_kernel,
+        [shape((width, width), BF16), shape((nodes, width), F32)]
+        + [shape((nodes, width), BF16)] * (chips - 2),
+        [VMEM] * 3,
+        cost=10**9,
+    )(contrib, got_rest, first)
+    last = chips - 1
+    got = {last: swap(first, "dom", 2 * last + 1)}
+    got |= {chip: swap(rest[chip - 1], "dom", 2 * chip + 1) for chip in range(last - 1, 0, -1)}
+    weights = {chip: swap(pair_weight, "dom", 2 * chip + 1) for chip in range(last - 1, 0, -1)}
+    weights[0] = pair_weight
     output = call(
         functools.partial(order_kernel, list(pieces)), shape((rows * size, width), BF16), [VMEM] * rep
     )(*outputs)
-    levels = chips.bit_length() - 1
-    total = shape(message.shape, F32)
-    got[chips - 1] = call(lift_kernel, total, [VMEM], cost=1000000000)(got[chips - 1])
-    later = call(
-        functools.partial(half_kernel, levels), [total] * (levels - 1), [VMEM] * (chips - 2), cost=0
-    )(*[got[chip] for chip in range(2, chips)])
+    lifted = call(lift_kernel, shape(message.shape, F32), [VMEM], cost=0)(got[last])
+    early = call(early_sum_kernel, shape((nodes, width), F32), [VMEM] * last, cost=0)(
+        own, lifted, *[got[chip] for chip in range(last - 1, 1, -1)]
+    )
     feature_grad, weight_grad = call(
         final_kernel,
         [shape((nodes, width), F32), shape((width, width), F32)],
-        [VMEM] * (levels + 2),
-    )(own, sends[-1], got[1], *later)
+        [VMEM] * (chips + 2),
+    )(early, lifted, got[1], *[weights[chip] for chip in range(last)])
     return output, feature_grad, weight_grad
 
 

time: 39.9 us -> 39.9 us (level)
  waiting for transfers between devices: 14 us -> 12.2 us
  starting transfers between devices: 17.8 us -> 19.5 us
    ppermute x17 -> x19, waiting for transfers between devices: 14 us -> 12.2 us  [swap(): return lax.ppermute(value, axis, [(i, i ^ distance) for i in range(size)])]
    ppermute x17 -> x19, starting transfers between devices: 17.8 us -> 19.5 us  [swap(): return lax.ppermute(value, axis, [(i, i ^ distance) for i in range(size)])]
  transfers between devices with their start and end apart: 17 -> 19, of which waited for: 13 -> 14; matrix products, arithmetic and copies ran while one was open for 0% -> 0% of each run, Pallas kernels for 7% -> 7%
where the time goes in v18:
time: 39.9 us; the launch traced here: 39.6 us
  starting transfers between devices  19.5 us (49%)
  waiting for transfers between devices  12.2 us (31%)
  Pallas kernels  4.44 us (11%)
  local copies, waits for them, and re-layouts  2.62 us (7%)
  between operations  0.81 us (2%)
    ppermute x19, starting transfers between devices, swap(): return lax.ppermute(value, axis, [(i, i ^ distance) for i in range(size)])  19.5 us
    ppermute x19, waiting for transfers between devices, swap(): return lax.ppermute(value, axis, [(i, i ^ distance) for i in range(size)])  12.2 us
    unnamed x14, local copies, waits for them, and re-layouts  2.62 us
    pallas_call x4, Pallas kernels, body(): call(functools.partial(layer_kernel, rep, count, own_blocks, j), outs, [V...  2.11 us
  transfers between devices with their start and end apart: 19, of which 14 were waited for; matrix products, arithmetic and copies ran while one was open for 0% of the time, Pallas kernels for 7%

profile of v18, /device:TPU:0, one launch (start us, length us, event | category | flops | bytes accessed | tf_op | source)
XLA Modules:
  0.0 39.6 jit_solution(17177982895910762236)
XLA Ops:
  0.6 3.4 %collective-permute-start = (bf16[256,128]{1,0:T(8,128)(2,1)}, bf16[256,128]{1,0:T(8,128)(2,1)S(1)}, u32[]{:S(2)}, u32[]{:S(2)}) collective-permute-start(bf16[256,128]{1,0:T(8,128)(2,1)} %features_ref.1), channel_id=1, source_target_pairs={{0,7},{1,6},{2,5},{3,4},{4,3},{5,2},{6,1},{7,0},{8,15},{9,14},{10,... | collective-permute-start | bytes 196616 | tf_op jit(solution)/shard_map/ppermute | solution.py:17
  4.0 0.8 %collective-permute-start.2 = (bf16[256,128]{1,0:T(8,128)(2,1)}, bf16[256,128]{1,0:T(8,128)(2,1)S(1)}, u32[]{:S(2)}, u32[]{:S(2)}) collective-permute-start(bf16[256,128]{1,0:T(8,128)(2,1)} %features_ref.1), channel_id=1, source_target_pairs={{0,5},{1,4},{2,7},{3,6},{4,1},{5,0},{6,3},{7,2},{8,13},{9,12},{10,... | collective-permute-start | bytes 196616 | tf_op jit(solution)/shard_map/ppermute | solution.py:17
  5.0 1.0 %copy-done.1 = bf16[8,2,128,128]{3,2,1,0:T(8,128)(2,1)S(1)} copy-done((bf16[8,2,128,128]{3,2,1,0:T(8,128)(2,1)S(1)}, bf16[8,2,128,128]{3,2,1,0:T(8,128)(2,1)}, u32[]{:S(2)}) %copy-start.1) | copy-done | bytes 524312
  6.0 0.8 %copy-done.4 = bf16[256,128]{1,0:T(8,128)(2,1)S(1)} copy-done((bf16[256,128]{1,0:T(8,128)(2,1)S(1)}, bf16[256,128]{1,0:T(8,128)(2,1)}, u32[]{:S(2)}) %copy-start.4) | copy-done | bytes 65560
  7.1 1.0 %collective-permute-done.2.refs_1_ = bf16[256,128]{1,0:T(8,128)(2,1)S(1)} collective-permute-done((bf16[256,128]{1,0:T(8,128)(2,1)}, bf16[256,128]{1,0:T(8,128)(2,1)S(1)}, u32[]{:S(2)}, u32[]{:S(2)}) %collective-permute-start.2) | collective-permute-done | bytes 65568 | tf_op jit(solution)/shard_map/ppermute | solution.py:17
  8.2 0.7 %collective-permute-start.5 = (bf16[256,128]{1,0:T(8,128)(2,1)S(1)}, bf16[256,128]{1,0:T(8,128)(2,1)S(1)}, u32[]{:S(2)}, u32[]{:S(2)}) collective-permute-start(bf16[256,128]{1,0:T(8,128)(2,1)S(1)} %collective-permute-done.2.refs_1_), channel_id=1, source_target_pairs={{0,1},{1,0},{2,3},{3,2},{4,5},{5,4},{6,7},{7,6},{8,9},{9,8},{10,11... | collective-permute-start | bytes 196616 | tf_op jit(solution)/shard_map/ppermute | solution.py:17
  9.8 0.8 %collective-permute-done.4.refs_0_ = bf16[256,128]{1,0:T(8,128)(2,1)S(1)} collective-permute-done((bf16[256,128]{1,0:T(8,128)(2,1)S(1)}, bf16[256,128]{1,0:T(8,128)(2,1)S(1)}, u32[]{:S(2)}, u32[]{:S(2)}) %collective-permute-start.4) | collective-permute-done | bytes 65568 | tf_op jit(solution)/shard_map/ppermute | solution.py:17
  11.1 3.7 %collective-permute-start.6 = (bf16[256,128]{1,0:T(8,128)(2,1)S(1)}, bf16[256,128]{1,0:T(8,128)(2,1)S(1)}, u32[]{:S(2)}, u32[]{:S(2)}) collective-permute-start(bf16[256,128]{1,0:T(8,128)(2,1)S(1)} %get-tuple-element.31), channel_id=1, source_target_pairs={{0,24},{8,16},{16,8},{24,0},{1,25},{9,17},{17,9},{25,1},{2,26},{10... | collective-permute-start | bytes 196616 | tf_op jit(solution)/shard_map/ppermute | solution.py:17
  14.8 0.8 %collective-permute-start.8 = (bf16[256,128]{1,0:T(8,128)(2,1)S(1)}, bf16[256,128]{1,0:T(8,128)(2,1)S(1)}, u32[]{:S(2)}, u32[]{:S(2)}) collective-permute-start(bf16[256,128]{1,0:T(8,128)(2,1)S(1)} %get-tuple-element.33), channel_id=1, source_target_pairs={{0,16},{8,24},{16,0},{24,8},{1,17},{9,25},{17,1},{25,9},{2,18},{10... | collective-permute-start | bytes 196616 | tf_op jit(solution)/shard_map/ppermute | solution.py:17
  15.5 2.3 %collective-permute-done.6.b_ref = bf16[256,128]{1,0:T(8,128)(2,1)S(1)} collective-permute-done((bf16[256,128]{1,0:T(8,128)(2,1)S(1)}, bf16[256,128]{1,0:T(8,128)(2,1)S(1)}, u32[]{:S(2)}, u32[]{:S(2)}) %collective-permute-start.6) | collective-permute-done | bytes 65568 | tf_op jit(solution)/shard_map/ppermute | solution.py:17
  17.9 2.3 %collective-permute-done.7.b_ref = bf16[256,128]{1,0:T(8,128)(2,1)S(1)} collective-permute-done((bf16[256,128]{1,0:T(8,128)(2,1)S(1)}, bf16[256,128]{1,0:T(8,128)(2,1)S(1)}, u32[]{:S(2)}, u32[]{:S(2)}) %collective-permute-start.7) | collective-permute-done | bytes 65568 | tf_op jit(solution)/shard_map/ppermute | solution.py:17
  20.6 2.3 %collective-permute-start.9 = (bf16[256,128]{1,0:T(8,128)(2,1)S(1)}, bf16[256,128]{1,0:T(8,128)(2,1)S(1)}, u32[]{:S(2)}, u32[]{:S(2)}) collective-permute-start(bf16[256,128]{1,0:T(8,128)(2,1)S(1)} %shard_map.93.refs_0_), channel_id=1, source_target_pairs={{0,24},{8,16},{16,8},{24,0},{1,25},{9,17},{17,9},{25,1},{2,26},{10... | collective-permute-start | bytes 196616 | tf_op jit(solution)/shard_map/ppermute | solution.py:17
  23.5 1.6 %collective-permute-start.11 = (bf16[256,128]{1,0:T(8,128)(2,1)S(1)}, bf16[256,128]{1,0:T(8,128)(2,1)S(1)}, u32[]{:S(2)}, u32[]{:S(2)}) collective-permute-start(bf16[256,128]{1,0:T(8,128)(2,1)S(1)} %shard_map.93.refs_0_), channel_id=1, source_target_pairs={{0,16},{8,24},{16,0},{24,8},{1,17},{9,25},{17,1},{25,9},{2,18},{10... | collective-permute-start | bytes 196616 | tf_op jit(solution)/shard_map/ppermute | solution.py:17
  25.1 0.6 %copy-done.5 = f32[128]{0:T(128)S(1)} copy-done((f32[128]{0:T(128)S(1)}, f32[128]{0:T(128)}, u32[]{:S(2)}) %copy-start.5) | copy-done | bytes 536
  26.3 0.6 %collective-permute-done.9.refs_0_ = bf16[256,128]{1,0:T(8,128)(2,1)S(1)} collective-permute-done((bf16[256,128]{1,0:T(8,128)(2,1)S(1)}, bf16[256,128]{1,0:T(8,128)(2,1)S(1)}, u32[]{:S(2)}, u32[]{:S(2)}) %collective-permute-start.9) | collective-permute-done | bytes 65568 | tf_op jit(solution)/shard_map/ppermute | solution.py:17
  27.4 0.6 %collective-permute-done.10.refs_0_ = bf16[256,128]{1,0:T(8,128)(2,1)S(1)} collective-permute-done((bf16[256,128]{1,0:T(8,128)(2,1)S(1)}, bf16[256,128]{1,0:T(8,128)(2,1)S(1)}, u32[]{:S(2)}, u32[]{:S(2)}) %collective-permute-start.10) | collective-permute-done | bytes 65568 | tf_op jit(solution)/shard_map/ppermute | solution.py:17
  30.0 0.8 %collective-permute-done.13.got_ref = bf16[384,128]{1,0:T(8,128)(2,1)S(1)} collective-permute-done((bf16[384,128]{1,0:T(8,128)(2,1)S(1)}, bf16[384,128]{1,0:T(8,128)(2,1)S(1)}, u32[]{:S(2)}, u32[]{:S(2)}) %collective-permute-start.13) | collective-permute-done | bytes 98336 | tf_op jit(solution)/shard_map/ppermute | solution.py:17
  30.8 1.3 %collective-permute-start.14 = (bf16[384,128]{1,0:T(8,128)(2,1)S(1)}, bf16[384,128]{1,0:T(8,128)(2,1)S(1)}, u32[]{:S(2)}, u32[]{:S(2)}) collective-permute-start(bf16[384,128]{1,0:T(8,128)(2,1)S(1)} %shard_map.99.first_ref), channel_id=1, source_target_pairs={{0,7},{1,6},{2,5},{3,4},{4,3},{5,2},{6,1},{7,0},{8,15},{9,14},{10,... | collective-permute-start | bytes 294920 | tf_op jit(solution)/shard_map/ppermute | solution.py:17
  32.2 1.3 %collective-permute-start.15 = (bf16[256,128]{1,0:T(8,128)(2,1)S(1)}, bf16[256,128]{1,0:T(8,128)(2,1)S(1)}, u32[]{:S(2)}, u32[]{:S(2)}) collective-permute-start(bf16[256,128]{1,0:T(8,128)(2,1)S(1)} %get-tuple-element.48), channel_id=1, source_target_pairs={{0,5},{1,4},{2,7},{3,6},{4,1},{5,0},{6,3},{7,2},{8,13},{9,12},{10,... | collective-permute-start | bytes 196616 | tf_op jit(solution)/shard_map/ppermute | solution.py:17
  34.0 1.5 %collective-permute-start.18 = (bf16[128,128]{1,0:T(8,128)(2,1)S(1)}, bf16[128,128]{1,0:T(8,128)(2,1)S(1)}, u32[]{:S(2)}, u32[]{:S(2)}) collective-permute-start(bf16[128,128]{1,0:T(8,128)(2,1)S(1)} %get-tuple-element.50.refs_0_), channel_id=1, source_target_pairs={{0,5},{1,4},{2,7},{3,6},{4,1},{5,0},{6,3},{7,2},{8,13},{9,12},{10,... | collective-permute-start | bytes 98312 | tf_op jit(solution)/shard_map/ppermute | solution.py:17
  35.7 0.7 %shard_map.98 = bf16[1024,128]{1,0:T(8,128)(2,1)} custom-call(bf16[256,128]{1,0:T(8,128)(2,1)S(1)} %get-tuple-element.34.refs_0_, bf16[256,128]{1,0:T(8,128)(2,1)S(1)} %get-tuple-element.37.refs_1_, bf16[256,128]{1,0:T(8,128)(2,1)S(1)} %get-tuple-element.40.refs_2_, bf16[256,128]{1,0:T(8,128)(2,1)S(1)} %get-tuple-element.43.refs_3_), custom_call_target="tpu_custom_call" | custom-call | tf_op jit(solution)/shard_map/pallas_call | solution.py:289
  36.7 1.6 %collective-permute-done.15.refs_0_ = bf16[256,128]{1,0:T(8,128)(2,1)S(1)} collective-permute-done((bf16[256,128]{1,0:T(8,128)(2,1)S(1)}, bf16[256,128]{1,0:T(8,128)(2,1)S(1)}, u32[]{:S(2)}, u32[]{:S(2)}) %collective-permute-start.15) | collective-permute-done | bytes 65568 | tf_op jit(solution)/shard_map/ppermute | solution.py:17
  38.3 0.7 %collective-permute-done.18.refs_2_ = bf16[128,128]{1,0:T(8,128)(2,1)S(1)} collective-permute-done((bf16[128,128]{1,0:T(8,128)(2,1)S(1)}, bf16[128,128]{1,0:T(8,128)(2,1)S(1)}, u32[]{:S(2)}, u32[]{:S(2)}) %collective-permute-start.18) | collective-permute-done | bytes 32800 | tf_op jit(solution)/shard_map/ppermute | solution.py:17
  39.0 0.7 %shard_map.103 = (f32[256,128]{1,0:T(8,128)}, f32[128,128]{1,0:T(8,128)}) custom-call(f32[256,128]{1,0:T(8,128)S(1)} %shard_map.102.early_ref, f32[384,128]{1,0:T(8,128)S(1)} %shard_map.101.lifted_ref, bf16[256,128]{1,0:T(8,128)(2,1)S(1)} %collective-permute-done.16.got_ref, bf16[128,128]{1,0:T(8,128)(2,1)S(1)} %get-tuple-element.50.refs_0_, ...), custom_call_target="tpu_custom_call" | custom-call | tf_op jit(solution)/shard_map/pallas_call | solution.py:296
  (47 shorter events, 6.8 us)
Async XLA Ops:
  0.6 6.4 %collective-permute-start = (bf16[256,128]{1,0:T(8,128)(2,1)}, bf16[256,128]{1,0:T(8,128)(2,1)S(1)}, u32[]{:S(2)}, u32[]{:S(2)}) collective-permute-start(bf16[256,128]{1,0:T(8,128)(2,1)} %features_ref.1), channel_id=1, source_target_pairs={{0,7},{1,6},{2,5},{3,4},{4,3},{5,2},{6,1},{7,0},{8,15},{9,14},{10,... | collective-permute-start | bytes 196616 | tf_op jit(solution)/shard_map/ppermute | solution.py:17
  4.0 4.2 %collective-permute-start.2 = (bf16[256,128]{1,0:T(8,128)(2,1)}, bf16[256,128]{1,0:T(8,128)(2,1)S(1)}, u32[]{:S(2)}, u32[]{:S(2)}) collective-permute-start(bf16[256,128]{1,0:T(8,128)(2,1)} %features_ref.1), channel_id=1, source_target_pairs={{0,5},{1,4},{2,7},{3,6},{4,1},{5,0},{6,3},{7,2},{8,13},{9,12},{10,... | collective-permute-start | bytes 196616 | tf_op jit(solution)/shard_map/ppermute | solution.py:17
  4.8 4.5 %collective-permute-start.1 = (bf16[256,128]{1,0:T(8,128)(2,1)}, bf16[256,128]{1,0:T(8,128)(2,1)S(1)}, u32[]{:S(2)}, u32[]{:S(2)}) collective-permute-start(bf16[256,128]{1,0:T(8,128)(2,1)} %features_ref.1), channel_id=1, source_target_pairs={{0,3},{1,2},{2,1},{3,0},{4,7},{5,6},{6,5},{7,4},{8,11},{9,10},{10,... | collective-permute-start | bytes 196616 | tf_op jit(solution)/shard_map/ppermute | solution.py:17
  5.0 1.0 %copy-start.1 = (bf16[8,2,128,128]{3,2,1,0:T(8,128)(2,1)S(1)}, bf16[8,2,128,128]{3,2,1,0:T(8,128)(2,1)}, u32[]{:S(2)}) copy-start(bf16[8,2,128,128]{3,2,1,0:T(8,128)(2,1)} %vals_ref.3) | copy-start | bytes 1572868
  7.1 2.4 %copy-start.6 = (s32[8,2]{0,1:T(2,128)S(1)}, s32[8,2]{0,1:T(2,128)}, u32[]{:S(2)}) copy-start(s32[8,2]{0,1:T(2,128)} %param.6) | copy-start | bytes 196
  7.1 3.5 %collective-permute-start.3 = (bf16[512,128]{1,0:T(8,128)(2,1)S(1)}, bf16[512,128]{1,0:T(8,128)(2,1)S(1)}, u32[]{:S(2)}, u32[]{:S(2)}) collective-permute-start(bf16[512,128]{1,0:T(8,128)(2,1)S(1)} %shard_map.86._.ends_ref), channel_id=1, source_target_pairs={{0,1},{1,0},{2,3},{3,2},{4,5},{5,4},{6,7},{7,6},{8,9},{9,8},{10,11... | collective-permute-start | bytes 393224 | tf_op jit(solution)/shard_map/ppermute | solution.py:17
  8.2 1.6 %collective-permute-start.5 = (bf16[256,128]{1,0:T(8,128)(2,1)S(1)}, bf16[256,128]{1,0:T(8,128)(2,1)S(1)}, u32[]{:S(2)}, u32[]{:S(2)}) collective-permute-start(bf16[256,128]{1,0:T(8,128)(2,1)S(1)} %collective-permute-done.2.refs_1_), channel_id=1, source_target_pairs={{0,1},{1,0},{2,3},{3,2},{4,5},{5,4},{6,7},{7,6},{8,9},{9,8},{10,11... | collective-permute-start | bytes 196616 | tf_op jit(solution)/shard_map/ppermute | solution.py:17
  9.3 1.3 %collective-permute-start.4 = (bf16[256,128]{1,0:T(8,128)(2,1)S(1)}, bf16[256,128]{1,0:T(8,128)(2,1)S(1)}, u32[]{:S(2)}, u32[]{:S(2)}) collective-permute-start(bf16[256,128]{1,0:T(8,128)(2,1)S(1)} %collective-permute-done.1.refs_0_), channel_id=1, source_target_pairs={{0,1},{1,0},{2,3},{3,2},{4,5},{5,4},{6,7},{7,6},{8,9},{9,8},{10,11... | collective-permute-start | bytes 196616 | tf_op jit(solution)/shard_map/ppermute | solution.py:17
  9.7 1.0 %copy-start.2 = (bf16[8,2,128,128]{3,2,1,0:T(8,128)(2,1)S(1)}, bf16[8,2,128,128]{3,2,1,0:T(8,128)(2,1)}, u32[]{:S(2)}) copy-start(bf16[8,2,128,128]{3,2,1,0:T(8,128)(2,1)} %vals_ref.3) | copy-start | bytes 1572868
  11.1 6.8 %collective-permute-start.6 = (bf16[256,128]{1,0:T(8,128)(2,1)S(1)}, bf16[256,128]{1,0:T(8,128)(2,1)S(1)}, u32[]{:S(2)}, u32[]{:S(2)}) collective-permute-start(bf16[256,128]{1,0:T(8,128)(2,1)S(1)} %get-tuple-element.31), channel_id=1, source_target_pairs={{0,24},{8,16},{16,8},{24,0},{1,25},{9,17},{17,9},{25,1},{2,26},{10... | collective-permute-start | bytes 196616 | tf_op jit(solution)/shard_map/ppermute | solution.py:17
  14.8 5.4 %collective-permute-start.7 = (bf16[256,128]{1,0:T(8,128)(2,1)S(1)}, bf16[256,128]{1,0:T(8,128)(2,1)S(1)}, u32[]{:S(2)}, u32[]{:S(2)}) collective-permute-start(bf16[256,128]{1,0:T(8,128)(2,1)S(1)} %get-tuple-element.32), channel_id=1, source_target_pairs={{0,8},{8,0},{16,24},{24,16},{1,9},{9,1},{17,25},{25,17},{2,10},{10... | collective-permute-start | bytes 196616 | tf_op jit(solution)/shard_map/ppermute | solution.py:17
  14.8 5.9 %collective-permute-start.8 = (bf16[256,128]{1,0:T(8,128)(2,1)S(1)}, bf16[256,128]{1,0:T(8,128)(2,1)S(1)}, u32[]{:S(2)}, u32[]{:S(2)}) collective-permute-start(bf16[256,128]{1,0:T(8,128)(2,1)S(1)} %get-tuple-element.33), channel_id=1, source_target_pairs={{0,16},{8,24},{16,0},{24,8},{1,17},{9,25},{17,1},{25,9},{2,18},{10... | collective-permute-start | bytes 196616 | tf_op jit(solution)/shard_map/ppermute | solution.py:17
  17.9 7.2 %copy-start = (bf16[1024,128]{1,0:T(8,128)(2,1)S(1)}, bf16[1024,128]{1,0:T(8,128)(2,1)}, u32[]{:S(2)}) copy-start(bf16[1024,128]{1,0:T(8,128)(2,1)} %cotangent_ref.7) | copy-start | bytes 786436
  20.2 4.9 %copy-start.3 = (bf16[128,128]{1,0:T(8,128)(2,1)S(1)}, bf16[128,128]{1,0:T(8,128)(2,1)}, u32[]{:S(2)}) copy-start(bf16[128,128]{1,0:T(8,128)(2,1)} %weight_ref.7) | copy-start | bytes 98308
  20.6 6.3 %collective-permute-start.9 = (bf16[256,128]{1,0:T(8,128)(2,1)S(1)}, bf16[256,128]{1,0:T(8,128)(2,1)S(1)}, u32[]{:S(2)}, u32[]{:S(2)}) collective-permute-start(bf16[256,128]{1,0:T(8,128)(2,1)S(1)} %shard_map.93.refs_0_), channel_id=1, source_target_pairs={{0,24},{8,16},{16,8},{24,0},{1,25},{9,17},{17,9},{25,1},{2,26},{10... | collective-permute-start | bytes 196616 | tf_op jit(solution)/shard_map/ppermute | solution.py:17
  23.0 5.1 %collective-permute-start.10 = (bf16[256,128]{1,0:T(8,128)(2,1)S(1)}, bf16[256,128]{1,0:T(8,128)(2,1)S(1)}, u32[]{:S(2)}, u32[]{:S(2)}) collective-permute-start(bf16[256,128]{1,0:T(8,128)(2,1)S(1)} %shard_map.93.refs_0_), channel_id=1, source_target_pairs={{0,8},{8,0},{16,24},{24,16},{1,9},{9,1},{17,25},{25,17},{2,10},{10... | collective-permute-start | bytes 196616 | tf_op jit(solution)/shard_map/ppermute | solution.py:17
  23.5 5.4 %collective-permute-start.11 = (bf16[256,128]{1,0:T(8,128)(2,1)S(1)}, bf16[256,128]{1,0:T(8,128)(2,1)S(1)}, u32[]{:S(2)}, u32[]{:S(2)}) collective-permute-start(bf16[256,128]{1,0:T(8,128)(2,1)S(1)} %shard_map.93.refs_0_), channel_id=1, source_target_pairs={{0,16},{8,24},{16,0},{24,8},{1,17},{9,25},{17,1},{25,9},{2,18},{10... | collective-permute-start | bytes 196616 | tf_op jit(solution)/shard_map/ppermute | solution.py:17
  29.4 1.4 %collective-permute-start.13 = (bf16[384,128]{1,0:T(8,128)(2,1)S(1)}, bf16[384,128]{1,0:T(8,128)(2,1)S(1)}, u32[]{:S(2)}, u32[]{:S(2)}) collective-permute-start(bf16[384,128]{1,0:T(8,128)(2,1)S(1)} %get-tuple-element.46.sent_ref), channel_id=1, source_target_pairs={{0,1},{1,0},{2,3},{3,2},{4,5},{5,4},{6,7},{7,6},{8,9},{9,8},{10,11... | collective-permute-start | bytes 294920 | tf_op jit(solution)/shard_map/ppermute | solution.py:17
  29.5 2.6 %collective-permute-start.12 = (bf16[768,128]{1,0:T(8,128)(2,1)S(1)}, bf16[768,128]{1,0:T(8,128)(2,1)S(1)}, u32[]{:S(2)}, u32[]{:S(2)}) collective-permute-start(bf16[768,128]{1,0:T(8,128)(2,1)S(1)} %get-tuple-element.45), channel_id=1, source_target_pairs={{0,1},{1,0},{2,3},{3,2},{4,5},{5,4},{6,7},{7,6},{8,9},{9,8},{10,11... | collective-permute-start | bytes 589832 | tf_op jit(solution)/shard_map/ppermute | solution.py:17
  30.8 5.8 %collective-permute-start.14 = (bf16[384,128]{1,0:T(8,128)(2,1)S(1)}, bf16[384,128]{1,0:T(8,128)(2,1)S(1)}, u32[]{:S(2)}, u32[]{:S(2)}) collective-permute-start(bf16[384,128]{1,0:T(8,128)(2,1)S(1)} %shard_map.99.first_ref), channel_id=1, source_target_pairs={{0,7},{1,6},{2,5},{3,4},{4,3},{5,2},{6,1},{7,0},{8,15},{9,14},{10,... | collective-permute-start | bytes 294920 | tf_op jit(solution)/shard_map/ppermute | solution.py:17
  32.2 6.1 %collective-permute-start.15 = (bf16[256,128]{1,0:T(8,128)(2,1)S(1)}, bf16[256,128]{1,0:T(8,128)(2,1)S(1)}, u32[]{:S(2)}, u32[]{:S(2)}) collective-permute-start(bf16[256,128]{1,0:T(8,128)(2,1)S(1)} %get-tuple-element.48), channel_id=1, source_target_pairs={{0,5},{1,4},{2,7},{3,6},{4,1},{5,0},{6,3},{7,2},{8,13},{9,12},{10,... | collective-permute-start | bytes 196616 | tf_op jit(solution)/shard_map/ppermute | solution.py:17
  33.5 5.5 %collective-permute-start.16 = (bf16[256,128]{1,0:T(8,128)(2,1)S(1)}, bf16[256,128]{1,0:T(8,128)(2,1)S(1)}, u32[]{:S(2)}, u32[]{:S(2)}) collective-permute-start(bf16[256,128]{1,0:T(8,128)(2,1)S(1)} %get-tuple-element.49), channel_id=1, source_target_pairs={{0,3},{1,2},{2,1},{3,0},{4,7},{5,6},{6,5},{7,4},{8,11},{9,10},{10,... | collective-permute-start | bytes 196616 | tf_op jit(solution)/shard_map/ppermute | solution.py:17
  34.0 5.0 %collective-permute-start.18 = (bf16[128,128]{1,0:T(8,128)(2,1)S(1)}, bf16[128,128]{1,0:T(8,128)(2,1)S(1)}, u32[]{:S(2)}, u32[]{:S(2)}) collective-permute-start(bf16[128,128]{1,0:T(8,128)(2,1)S(1)} %get-tuple-element.50.refs_0_), channel_id=1, source_target_pairs={{0,5},{1,4},{2,7},{3,6},{4,1},{5,0},{6,3},{7,2},{8,13},{9,12},{10,... | collective-permute-start | bytes 98312 | tf_op jit(solution)/shard_map/ppermute | solution.py:17
  35.5 3.4 %collective-permute-start.17 = (bf16[128,128]{1,0:T(8,128)(2,1)S(1)}, bf16[128,128]{1,0:T(8,128)(2,1)S(1)}, u32[]{:S(2)}, u32[]{:S(2)}) collective-permute-start(bf16[128,128]{1,0:T(8,128)(2,1)S(1)} %get-tuple-element.50.refs_0_), channel_id=1, source_target_pairs={{0,3},{1,2},{2,1},{3,0},{4,7},{5,6},{6,5},{7,4},{8,11},{9,10},{10,... | collective-permute-start | bytes 98312 | tf_op jit(solution)/shard_map/ppermute | solution.py:17
  (2 other events, 1.5 us)

commit v19 on v18

--- a/solution.py
+++ b/solution.py
@@ -21,8 +21,9 @@
     return lax.dot_general(a, b, ((contract[:1], contract[1:]), ((), ())), preferred_element_type=F32)
 
 
-def early_kernel(vals_ref, features_ref, flipped_ref, own_ref):
+def early_kernel(vals_ref, features_ref, flipped_ref, own_ref, near_ref):
     rows, count, size, _ = vals_ref.shape
+    near_ref[...] = vals_ref[...]
     own_ref[...] = features_ref[...]
     for row in range(rows):
         for k in range(count):
@@ -35,8 +36,7 @@
         for k in range(count):
             col = cols_ref[k, row] - lax.axis_index("rep") * (own_blocks * dom)
             owner = lax.div(col, jnp.int32(own_blocks)) ^ lax.axis_index("dom")
-            side = jnp.where(owner > 1, 1 - (owner & 1), owner)
-            place = (side * (dom // 2) + (owner >> 1)) * own_blocks
+            place = ((owner & 1) * (dom // 2) + (owner >> 1)) * own_blocks
             place += lax.rem(col, jnp.int32(own_blocks))
             place_ref[row * count + k : row * count + k + 1, :] = jnp.full((1, 128), place, jnp.int32)
 
@@ -209,9 +209,9 @@
             cost_estimate=pl.CostEstimate(flops=cost, bytes_accessed=0, transcendentals=0),
         )
 
-    flipped, own = call(
+    flipped, own, vals = call(
         early_kernel,
-        [shape((rows, count * size, size), BF16), shape(features.shape, BF16)],
+        [shape((rows, count * size, size), BF16), shape(features.shape, BF16), shape(vals.shape, BF16)],
         [VMEM] * 2,
     )(vals, features)
 
@@ -219,7 +219,7 @@
         nodes_in = sum(v.shape[0] for v in values)
         return call(join_kernel, shape((nodes_in, width), BF16), [VMEM] * len(values))(*values)
 
-    across = [swap(features, "dom", 2 * chip + 1) for chip in range(1, chips)]
+    across = [swap(features, "dom", 2 * chip) for chip in range(1, chips)]
     ends = join(own, across[-1])
     far_ends = swap(ends, "dom", 1)
     half = chips // 2 - 1
@@ -282,9 +282,9 @@
         cost=10**9,
     )(contrib, got_rest, first)
     last = chips - 1
-    got = {last: swap(first, "dom", 2 * last + 1)}
-    got |= {chip: swap(rest[chip - 1], "dom", 2 * chip + 1) for chip in range(last - 1, 0, -1)}
-    weights = {chip: swap(pair_weight, "dom", 2 * chip + 1) for chip in range(last - 1, 0, -1)}
+    got = {last: swap(first, "dom", 2 * last)}
+    got |= {chip: swap(rest[chip - 1], "dom", 2 * chip) for chip in range(last - 1, 0, -1)}
+    weights = {chip: swap(pair_weight, "dom", 2 * chip) for chip in range(last - 1, 0, -1)}
     weights[0] = pair_weight
     output = call(
         functools.partial(order_kernel, list(pieces)), shape((rows * size, width), BF16), [VMEM] * rep

time: 39.9 us -> 40.7 us (1.020)
  waiting for transfers between devices: 12.2 us -> 12.9 us
    ppermute x19, waiting for transfers between devices: 12.2 us -> 12.9 us  [swap(): return lax.ppermute(value, axis, [(i, i ^ distance) for i in range(size)])]
    unnamed x14 -> x12, local copies, waits for them, and re-layouts: 2.62 us -> 2.55 us
where the time goes in v19:
time: 40.7 us; the launch traced here: 40.5 us
  starting transfers between devices  19.8 us (49%)
  waiting for transfers between devices  12.9 us (32%)
  Pallas kernels  4.43 us (11%)
  local copies, waits for them, and re-layouts  2.55 us (6%)
  between operations  0.8 us (2%)
    ppermute x19, starting transfers between devices, swap(): return lax.ppermute(value, axis, [(i, i ^ distance) for i in range(size)])  19.8 us
    ppermute x19, waiting for transfers between devices, swap(): return lax.ppermute(value, axis, [(i, i ^ distance) for i in range(size)])  12.9 us
    unnamed x12, local copies, waits for them, and re-layouts  2.55 us
    pallas_call x4, Pallas kernels, body(): call(functools.partial(layer_kernel, rep, count, own_blocks, j), outs, [V...  2.11 us
  transfers between devices with their start and end apart: 19, of which 14 were waited for; matrix products, arithmetic and copies ran while one was open for 0% of the time, Pallas kernels for 7%

profile of v19, /device:TPU:0, one launch (start us, length us, event | category | flops | bytes accessed | tf_op | source)
XLA Modules:
  0.0 40.5 jit_solution(14625197742959458443)
XLA Ops:
  0.6 4.0 %collective-permute-start = (bf16[256,128]{1,0:T(8,128)(2,1)}, bf16[256,128]{1,0:T(8,128)(2,1)S(1)}, u32[]{:S(2)}, u32[]{:S(2)}) collective-permute-start(bf16[256,128]{1,0:T(8,128)(2,1)} %features_ref.1), channel_id=1, source_target_pairs={{0,6},{1,7},{2,4},{3,5},{4,2},{5,3},{6,0},{7,1},{8,14},{9,15},{10,... | collective-permute-start | bytes 196616 | tf_op jit(solution)/shard_map/ppermute | solution.py:17
  5.2 1.0 %copy-done.2 = bf16[8,2,128,128]{3,2,1,0:T(8,128)(2,1)S(1)} copy-done((bf16[8,2,128,128]{3,2,1,0:T(8,128)(2,1)S(1)}, bf16[8,2,128,128]{3,2,1,0:T(8,128)(2,1)}, u32[]{:S(2)}) %copy-start.2) | copy-done | bytes 524312
  6.3 0.8 %copy-done.3 = bf16[256,128]{1,0:T(8,128)(2,1)S(1)} copy-done((bf16[256,128]{1,0:T(8,128)(2,1)S(1)}, bf16[256,128]{1,0:T(8,128)(2,1)}, u32[]{:S(2)}) %copy-start.3) | copy-done | bytes 65560
  7.4 1.6 %collective-permute-done.2.refs_1_ = bf16[256,128]{1,0:T(8,128)(2,1)S(1)} collective-permute-done((bf16[256,128]{1,0:T(8,128)(2,1)}, bf16[256,128]{1,0:T(8,128)(2,1)S(1)}, u32[]{:S(2)}, u32[]{:S(2)}) %collective-permute-start.2) | collective-permute-done | bytes 65568 | tf_op jit(solution)/shard_map/ppermute | solution.py:17
  11.2 3.7 %collective-permute-start.6 = (bf16[256,128]{1,0:T(8,128)(2,1)S(1)}, bf16[256,128]{1,0:T(8,128)(2,1)S(1)}, u32[]{:S(2)}, u32[]{:S(2)}) collective-permute-start(bf16[256,128]{1,0:T(8,128)(2,1)S(1)} %get-tuple-element.33), channel_id=1, source_target_pairs={{0,24},{8,16},{16,8},{24,0},{1,25},{9,17},{17,9},{25,1},{2,26},{10... | collective-permute-start | bytes 196616 | tf_op jit(solution)/shard_map/ppermute | solution.py:17
  14.9 0.8 %collective-permute-start.8 = (bf16[256,128]{1,0:T(8,128)(2,1)S(1)}, bf16[256,128]{1,0:T(8,128)(2,1)S(1)}, u32[]{:S(2)}, u32[]{:S(2)}) collective-permute-start(bf16[256,128]{1,0:T(8,128)(2,1)S(1)} %get-tuple-element.35), channel_id=1, source_target_pairs={{0,16},{8,24},{16,0},{24,8},{1,17},{9,25},{17,1},{25,9},{2,18},{10... | collective-permute-start | bytes 196616 | tf_op jit(solution)/shard_map/ppermute | solution.py:17
  15.7 2.4 %collective-permute-done.6.b_ref = bf16[256,128]{1,0:T(8,128)(2,1)S(1)} collective-permute-done((bf16[256,128]{1,0:T(8,128)(2,1)S(1)}, bf16[256,128]{1,0:T(8,128)(2,1)S(1)}, u32[]{:S(2)}, u32[]{:S(2)}) %collective-permute-start.6) | collective-permute-done | bytes 65568 | tf_op jit(solution)/shard_map/ppermute | solution.py:17
  18.1 1.8 %collective-permute-done.7.b_ref = bf16[256,128]{1,0:T(8,128)(2,1)S(1)} collective-permute-done((bf16[256,128]{1,0:T(8,128)(2,1)S(1)}, bf16[256,128]{1,0:T(8,128)(2,1)S(1)}, u32[]{:S(2)}, u32[]{:S(2)}) %collective-permute-start.7) | collective-permute-done | bytes 65568 | tf_op jit(solution)/shard_map/ppermute | solution.py:17
  20.0 0.7 %collective-permute-done.8.b_ref = bf16[256,128]{1,0:T(8,128)(2,1)S(1)} collective-permute-done((bf16[256,128]{1,0:T(8,128)(2,1)S(1)}, bf16[256,128]{1,0:T(8,128)(2,1)S(1)}, u32[]{:S(2)}, u32[]{:S(2)}) %collective-permute-start.8) | collective-permute-done | bytes 65568 | tf_op jit(solution)/shard_map/ppermute | solution.py:17
  20.8 2.3 %collective-permute-start.9 = (bf16[256,128]{1,0:T(8,128)(2,1)S(1)}, bf16[256,128]{1,0:T(8,128)(2,1)S(1)}, u32[]{:S(2)}, u32[]{:S(2)}) collective-permute-start(bf16[256,128]{1,0:T(8,128)(2,1)S(1)} %shard_map.93.refs_0_), channel_id=1, source_target_pairs={{0,24},{8,16},{16,8},{24,0},{1,25},{9,17},{17,9},{25,1},{2,26},{10... | collective-permute-start | bytes 196616 | tf_op jit(solution)/shard_map/ppermute | solution.py:17
  23.4 1.8 %collective-permute-start.11 = (bf16[256,128]{1,0:T(8,128)(2,1)S(1)}, bf16[256,128]{1,0:T(8,128)(2,1)S(1)}, u32[]{:S(2)}, u32[]{:S(2)}) collective-permute-start(bf16[256,128]{1,0:T(8,128)(2,1)S(1)} %shard_map.93.refs_0_), channel_id=1, source_target_pairs={{0,16},{8,24},{16,0},{24,8},{1,17},{9,25},{17,1},{25,9},{2,18},{10... | collective-permute-start | bytes 196616 | tf_op jit(solution)/shard_map/ppermute | solution.py:17
  25.2 0.6 %copy-done.4 = f32[128]{0:T(128)S(1)} copy-done((f32[128]{0:T(128)S(1)}, f32[128]{0:T(128)}, u32[]{:S(2)}) %copy-start.4) | copy-done | bytes 536
  26.4 0.7 %collective-permute-done.9.refs_0_ = bf16[256,128]{1,0:T(8,128)(2,1)S(1)} collective-permute-done((bf16[256,128]{1,0:T(8,128)(2,1)S(1)}, bf16[256,128]{1,0:T(8,128)(2,1)S(1)}, u32[]{:S(2)}, u32[]{:S(2)}) %collective-permute-start.9) | collective-permute-done | bytes 65568 | tf_op jit(solution)/shard_map/ppermute | solution.py:17
  28.7 0.6 %shard_map.97 = (bf16[256,128]{1,0:T(8,128)(2,1)S(1)}, f32[16,128,128]{2,1,0:T(8,128)S(1)}, bf16[384,128]{1,0:T(8,128)(2,1)S(1)}, bf16[768,128]{1,0:T(8,128)(2,1)S(1)}) custom-call(s32[16,128]{1,0:T(8,128)S(1)} %shard_map.87.place_ref, bf16[8,256,128]{2,1,0:T(8,128)(2,1)S(1)} %get-tuple-element.30.flipped_ref, ...), custom_call_target="tpu_custom_call", output_to_operand_aliasing={{1}: (6, {})} | custom-call | tf_op jit(solution)/shard_map/pallas_call | solution.py:265
  29.8 0.8 %collective-permute-done.13.got_ref = bf16[384,128]{1,0:T(8,128)(2,1)S(1)} collective-permute-done((bf16[384,128]{1,0:T(8,128)(2,1)S(1)}, bf16[384,128]{1,0:T(8,128)(2,1)S(1)}, u32[]{:S(2)}, u32[]{:S(2)}) %collective-permute-start.13) | collective-permute-done | bytes 98336 | tf_op jit(solution)/shard_map/ppermute | solution.py:17
  30.7 1.5 %collective-permute-start.14 = (bf16[384,128]{1,0:T(8,128)(2,1)S(1)}, bf16[384,128]{1,0:T(8,128)(2,1)S(1)}, u32[]{:S(2)}, u32[]{:S(2)}) collective-permute-start(bf16[384,128]{1,0:T(8,128)(2,1)S(1)} %shard_map.99.first_ref), channel_id=1, source_target_pairs={{0,6},{1,7},{2,4},{3,5},{4,2},{5,3},{6,0},{7,1},{8,14},{9,15},{10,... | collective-permute-start | bytes 294920 | tf_op jit(solution)/shard_map/ppermute | solution.py:17
  32.3 0.9 %collective-permute-start.15 = (bf16[256,128]{1,0:T(8,128)(2,1)S(1)}, bf16[256,128]{1,0:T(8,128)(2,1)S(1)}, u32[]{:S(2)}, u32[]{:S(2)}) collective-permute-start(bf16[256,128]{1,0:T(8,128)(2,1)S(1)} %get-tuple-element.50), channel_id=1, source_target_pairs={{0,4},{1,5},{2,6},{3,7},{4,0},{5,1},{6,2},{7,3},{8,12},{9,13},{10,... | collective-permute-start | bytes 196616 | tf_op jit(solution)/shard_map/ppermute | solution.py:17
  33.2 1.2 %collective-permute-start.16 = (bf16[256,128]{1,0:T(8,128)(2,1)S(1)}, bf16[256,128]{1,0:T(8,128)(2,1)S(1)}, u32[]{:S(2)}, u32[]{:S(2)}) collective-permute-start(bf16[256,128]{1,0:T(8,128)(2,1)S(1)} %get-tuple-element.51), channel_id=1, source_target_pairs={{0,2},{1,3},{2,0},{3,1},{4,6},{5,7},{6,4},{7,5},{8,10},{9,11},{10,... | collective-permute-start | bytes 196616 | tf_op jit(solution)/shard_map/ppermute | solution.py:17
  34.3 1.5 %collective-permute-start.18 = (bf16[128,128]{1,0:T(8,128)(2,1)S(1)}, bf16[128,128]{1,0:T(8,128)(2,1)S(1)}, u32[]{:S(2)}, u32[]{:S(2)}) collective-permute-start(bf16[128,128]{1,0:T(8,128)(2,1)S(1)} %get-tuple-element.52.refs_0_), channel_id=1, source_target_pairs={{0,4},{1,5},{2,6},{3,7},{4,0},{5,1},{6,2},{7,3},{8,12},{9,13},{10,... | collective-permute-start | bytes 98312 | tf_op jit(solution)/shard_map/ppermute | solution.py:17
  36.4 0.7 %shard_map.98 = bf16[1024,128]{1,0:T(8,128)(2,1)} custom-call(bf16[256,128]{1,0:T(8,128)(2,1)S(1)} %get-tuple-element.36.refs_0_, bf16[256,128]{1,0:T(8,128)(2,1)S(1)} %get-tuple-element.39.refs_1_, bf16[256,128]{1,0:T(8,128)(2,1)S(1)} %get-tuple-element.42.refs_2_, bf16[256,128]{1,0:T(8,128)(2,1)S(1)} %get-tuple-element.45.refs_3_), custom_call_target="tpu_custom_call" | custom-call | tf_op jit(solution)/shard_map/pallas_call | solution.py:289
  37.1 0.8 %collective-permute-done.15.refs_0_ = bf16[256,128]{1,0:T(8,128)(2,1)S(1)} collective-permute-done((bf16[256,128]{1,0:T(8,128)(2,1)S(1)}, bf16[256,128]{1,0:T(8,128)(2,1)S(1)}, u32[]{:S(2)}, u32[]{:S(2)}) %collective-permute-start.15) | collective-permute-done | bytes 65568 | tf_op jit(solution)/shard_map/ppermute | solution.py:17
  38.0 0.6 %collective-permute-done.18.refs_2_ = bf16[128,128]{1,0:T(8,128)(2,1)S(1)} collective-permute-done((bf16[128,128]{1,0:T(8,128)(2,1)S(1)}, bf16[128,128]{1,0:T(8,128)(2,1)S(1)}, u32[]{:S(2)}, u32[]{:S(2)}) %collective-permute-start.18) | collective-permute-done | bytes 32800 | tf_op jit(solution)/shard_map/ppermute | solution.py:17
  38.6 1.2 %collective-permute-done.17.refs_1_ = bf16[128,128]{1,0:T(8,128)(2,1)S(1)} collective-permute-done((bf16[128,128]{1,0:T(8,128)(2,1)S(1)}, bf16[128,128]{1,0:T(8,128)(2,1)S(1)}, u32[]{:S(2)}, u32[]{:S(2)}) %collective-permute-start.17) | collective-permute-done | bytes 32800 | tf_op jit(solution)/shard_map/ppermute | solution.py:17
  39.8 0.7 %shard_map.103 = (f32[256,128]{1,0:T(8,128)}, f32[128,128]{1,0:T(8,128)}) custom-call(f32[256,128]{1,0:T(8,128)S(1)} %shard_map.102.early_ref, f32[384,128]{1,0:T(8,128)S(1)} %shard_map.101.lifted_ref, bf16[256,128]{1,0:T(8,128)(2,1)S(1)} %collective-permute-done.16.got_ref, bf16[128,128]{1,0:T(8,128)(2,1)S(1)} %get-tuple-element.52.refs_0_, ...), custom_call_target="tpu_custom_call" | custom-call | tf_op jit(solution)/shard_map/pallas_call | solution.py:296
  (45 shorter events, 6.8 us)
Async XLA Ops:
  0.6 6.7 %collective-permute-start = (bf16[256,128]{1,0:T(8,128)(2,1)}, bf16[256,128]{1,0:T(8,128)(2,1)S(1)}, u32[]{:S(2)}, u32[]{:S(2)}) collective-permute-start(bf16[256,128]{1,0:T(8,128)(2,1)} %features_ref.1), channel_id=1, source_target_pairs={{0,6},{1,7},{2,4},{3,5},{4,2},{5,3},{6,0},{7,1},{8,14},{9,15},{10,... | collective-permute-start | bytes 196616 | tf_op jit(solution)/shard_map/ppermute | solution.py:17
  4.6 4.5 %collective-permute-start.2 = (bf16[256,128]{1,0:T(8,128)(2,1)}, bf16[256,128]{1,0:T(8,128)(2,1)S(1)}, u32[]{:S(2)}, u32[]{:S(2)}) collective-permute-start(bf16[256,128]{1,0:T(8,128)(2,1)} %features_ref.1), channel_id=1, source_target_pairs={{0,4},{1,5},{2,6},{3,7},{4,0},{5,1},{6,2},{7,3},{8,12},{9,13},{10,... | collective-permute-start | bytes 196616 | tf_op jit(solution)/shard_map/ppermute | solution.py:17
  5.1 4.5 %collective-permute-start.1 = (bf16[256,128]{1,0:T(8,128)(2,1)}, bf16[256,128]{1,0:T(8,128)(2,1)S(1)}, u32[]{:S(2)}, u32[]{:S(2)}) collective-permute-start(bf16[256,128]{1,0:T(8,128)(2,1)} %features_ref.1), channel_id=1, source_target_pairs={{0,2},{1,3},{2,0},{3,1},{4,6},{5,7},{6,4},{7,5},{8,10},{9,11},{10,... | collective-permute-start | bytes 196616 | tf_op jit(solution)/shard_map/ppermute | solution.py:17
  5.2 1.0 %copy-start.2 = (bf16[8,2,128,128]{3,2,1,0:T(8,128)(2,1)S(1)}, bf16[8,2,128,128]{3,2,1,0:T(8,128)(2,1)}, u32[]{:S(2)}) copy-start(bf16[8,2,128,128]{3,2,1,0:T(8,128)(2,1)} %vals_ref.1) | copy-start | bytes 1572868
  6.3 0.8 %copy-start.3 = (bf16[256,128]{1,0:T(8,128)(2,1)S(1)}, bf16[256,128]{1,0:T(8,128)(2,1)}, u32[]{:S(2)}) copy-start(bf16[256,128]{1,0:T(8,128)(2,1)} %features_ref.1) | copy-start | bytes 196612
  7.3 2.2 %copy-start.5 = (s32[8,2]{0,1:T(2,128)S(1)}, s32[8,2]{0,1:T(2,128)}, u32[]{:S(2)}) copy-start(s32[8,2]{0,1:T(2,128)} %param.6) | copy-start | bytes 196
  7.4 3.5 %collective-permute-start.3 = (bf16[512,128]{1,0:T(8,128)(2,1)S(1)}, bf16[512,128]{1,0:T(8,128)(2,1)S(1)}, u32[]{:S(2)}, u32[]{:S(2)}) collective-permute-start(bf16[512,128]{1,0:T(8,128)(2,1)S(1)} %shard_map.86._.ends_ref), channel_id=1, source_target_pairs={{0,1},{1,0},{2,3},{3,2},{4,5},{5,4},{6,7},{7,6},{8,9},{9,8},{10,11... | collective-permute-start | bytes 393224 | tf_op jit(solution)/shard_map/ppermute | solution.py:17
  9.1 1.3 %collective-permute-start.5 = (bf16[256,128]{1,0:T(8,128)(2,1)S(1)}, bf16[256,128]{1,0:T(8,128)(2,1)S(1)}, u32[]{:S(2)}, u32[]{:S(2)}) collective-permute-start(bf16[256,128]{1,0:T(8,128)(2,1)S(1)} %collective-permute-done.2.refs_1_), channel_id=1, source_target_pairs={{0,1},{1,0},{2,3},{3,2},{4,5},{5,4},{6,7},{7,6},{8,9},{9,8},{10,11... | collective-permute-start | bytes 196616 | tf_op jit(solution)/shard_map/ppermute | solution.py:17
  9.6 1.3 %collective-permute-start.4 = (bf16[256,128]{1,0:T(8,128)(2,1)S(1)}, bf16[256,128]{1,0:T(8,128)(2,1)S(1)}, u32[]{:S(2)}, u32[]{:S(2)}) collective-permute-start(bf16[256,128]{1,0:T(8,128)(2,1)S(1)} %collective-permute-done.1.refs_0_), channel_id=1, source_target_pairs={{0,1},{1,0},{2,3},{3,2},{4,5},{5,4},{6,7},{7,6},{8,9},{9,8},{10,11... | collective-permute-start | bytes 196616 | tf_op jit(solution)/shard_map/ppermute | solution.py:17
  11.2 6.9 %collective-permute-start.6 = (bf16[256,128]{1,0:T(8,128)(2,1)S(1)}, bf16[256,128]{1,0:T(8,128)(2,1)S(1)}, u32[]{:S(2)}, u32[]{:S(2)}) collective-permute-start(bf16[256,128]{1,0:T(8,128)(2,1)S(1)} %get-tuple-element.33), channel_id=1, source_target_pairs={{0,24},{8,16},{16,8},{24,0},{1,25},{9,17},{17,9},{25,1},{2,26},{10... | collective-permute-start | bytes 196616 | tf_op jit(solution)/shard_map/ppermute | solution.py:17
  14.9 5.1 %collective-permute-start.7 = (bf16[256,128]{1,0:T(8,128)(2,1)S(1)}, bf16[256,128]{1,0:T(8,128)(2,1)S(1)}, u32[]{:S(2)}, u32[]{:S(2)}) collective-permute-start(bf16[256,128]{1,0:T(8,128)(2,1)S(1)} %get-tuple-element.34), channel_id=1, source_target_pairs={{0,8},{8,0},{16,24},{24,16},{1,9},{9,1},{17,25},{25,17},{2,10},{10... | collective-permute-start | bytes 196616 | tf_op jit(solution)/shard_map/ppermute | solution.py:17
  14.9 5.9 %collective-permute-start.8 = (bf16[256,128]{1,0:T(8,128)(2,1)S(1)}, bf16[256,128]{1,0:T(8,128)(2,1)S(1)}, u32[]{:S(2)}, u32[]{:S(2)}) collective-permute-start(bf16[256,128]{1,0:T(8,128)(2,1)S(1)} %get-tuple-element.35), channel_id=1, source_target_pairs={{0,16},{8,24},{16,0},{24,8},{1,17},{9,25},{17,1},{25,9},{2,18},{10... | collective-permute-start | bytes 196616 | tf_op jit(solution)/shard_map/ppermute | solution.py:17
  18.1 7.1 %copy-start = (bf16[1024,128]{1,0:T(8,128)(2,1)S(1)}, bf16[1024,128]{1,0:T(8,128)(2,1)}, u32[]{:S(2)}) copy-start(bf16[1024,128]{1,0:T(8,128)(2,1)} %cotangent_ref.7) | copy-start | bytes 786436
  20.0 5.2 %copy-start.1 = (bf16[128,128]{1,0:T(8,128)(2,1)S(1)}, bf16[128,128]{1,0:T(8,128)(2,1)}, u32[]{:S(2)}) copy-start(bf16[128,128]{1,0:T(8,128)(2,1)} %weight_ref.7) | copy-start | bytes 98308
  20.8 6.3 %collective-permute-start.9 = (bf16[256,128]{1,0:T(8,128)(2,1)S(1)}, bf16[256,128]{1,0:T(8,128)(2,1)S(1)}, u32[]{:S(2)}, u32[]{:S(2)}) collective-permute-start(bf16[256,128]{1,0:T(8,128)(2,1)S(1)} %shard_map.93.refs_0_), channel_id=1, source_target_pairs={{0,24},{8,16},{16,8},{24,0},{1,25},{9,17},{17,9},{25,1},{2,26},{10... | collective-permute-start | bytes 196616 | tf_op jit(solution)/shard_map/ppermute | solution.py:17
  23.0 5.0 %collective-permute-start.10 = (bf16[256,128]{1,0:T(8,128)(2,1)S(1)}, bf16[256,128]{1,0:T(8,128)(2,1)S(1)}, u32[]{:S(2)}, u32[]{:S(2)}) collective-permute-start(bf16[256,128]{1,0:T(8,128)(2,1)S(1)} %shard_map.93.refs_0_), channel_id=1, source_target_pairs={{0,8},{8,0},{16,24},{24,16},{1,9},{9,1},{17,25},{25,17},{2,10},{10... | collective-permute-start | bytes 196616 | tf_op jit(solution)/shard_map/ppermute | solution.py:17
  23.4 5.3 %collective-permute-start.11 = (bf16[256,128]{1,0:T(8,128)(2,1)S(1)}, bf16[256,128]{1,0:T(8,128)(2,1)S(1)}, u32[]{:S(2)}, u32[]{:S(2)}) collective-permute-start(bf16[256,128]{1,0:T(8,128)(2,1)S(1)} %shard_map.93.refs_0_), channel_id=1, source_target_pairs={{0,16},{8,24},{16,0},{24,8},{1,17},{9,25},{17,1},{25,9},{2,18},{10... | collective-permute-start | bytes 196616 | tf_op jit(solution)/shard_map/ppermute | solution.py:17
  29.3 1.4 %collective-permute-start.13 = (bf16[384,128]{1,0:T(8,128)(2,1)S(1)}, bf16[384,128]{1,0:T(8,128)(2,1)S(1)}, u32[]{:S(2)}, u32[]{:S(2)}) collective-permute-start(bf16[384,128]{1,0:T(8,128)(2,1)S(1)} %get-tuple-element.48.sent_ref), channel_id=1, source_target_pairs={{0,1},{1,0},{2,3},{3,2},{4,5},{5,4},{6,7},{7,6},{8,9},{9,8},{10,11... | collective-permute-start | bytes 294920 | tf_op jit(solution)/shard_map/ppermute | solution.py:17
  29.3 2.9 %collective-permute-start.12 = (bf16[768,128]{1,0:T(8,128)(2,1)S(1)}, bf16[768,128]{1,0:T(8,128)(2,1)S(1)}, u32[]{:S(2)}, u32[]{:S(2)}) collective-permute-start(bf16[768,128]{1,0:T(8,128)(2,1)S(1)} %get-tuple-element.47), channel_id=1, source_target_pairs={{0,1},{1,0},{2,3},{3,2},{4,5},{5,4},{6,7},{7,6},{8,9},{9,8},{10,11... | collective-permute-start | bytes 589832 | tf_op jit(solution)/shard_map/ppermute | solution.py:17
  30.7 6.5 %collective-permute-start.14 = (bf16[384,128]{1,0:T(8,128)(2,1)S(1)}, bf16[384,128]{1,0:T(8,128)(2,1)S(1)}, u32[]{:S(2)}, u32[]{:S(2)}) collective-permute-start(bf16[384,128]{1,0:T(8,128)(2,1)S(1)} %shard_map.99.first_ref), channel_id=1, source_target_pairs={{0,6},{1,7},{2,4},{3,5},{4,2},{5,3},{6,0},{7,1},{8,14},{9,15},{10,... | collective-permute-start | bytes 294920 | tf_op jit(solution)/shard_map/ppermute | solution.py:17
  32.3 5.7 %collective-permute-start.15 = (bf16[256,128]{1,0:T(8,128)(2,1)S(1)}, bf16[256,128]{1,0:T(8,128)(2,1)S(1)}, u32[]{:S(2)}, u32[]{:S(2)}) collective-permute-start(bf16[256,128]{1,0:T(8,128)(2,1)S(1)} %get-tuple-element.50), channel_id=1, source_target_pairs={{0,4},{1,5},{2,6},{3,7},{4,0},{5,1},{6,2},{7,3},{8,12},{9,13},{10,... | collective-permute-start | bytes 196616 | tf_op jit(solution)/shard_map/ppermute | solution.py:17
  33.2 6.6 %collective-permute-start.16 = (bf16[256,128]{1,0:T(8,128)(2,1)S(1)}, bf16[256,128]{1,0:T(8,128)(2,1)S(1)}, u32[]{:S(2)}, u32[]{:S(2)}) collective-permute-start(bf16[256,128]{1,0:T(8,128)(2,1)S(1)} %get-tuple-element.51), channel_id=1, source_target_pairs={{0,2},{1,3},{2,0},{3,1},{4,6},{5,7},{6,4},{7,5},{8,10},{9,11},{10,... | collective-permute-start | bytes 196616 | tf_op jit(solution)/shard_map/ppermute | solution.py:17
  34.3 4.2 %collective-permute-start.18 = (bf16[128,128]{1,0:T(8,128)(2,1)S(1)}, bf16[128,128]{1,0:T(8,128)(2,1)S(1)}, u32[]{:S(2)}, u32[]{:S(2)}) collective-permute-start(bf16[128,128]{1,0:T(8,128)(2,1)S(1)} %get-tuple-element.52.refs_0_), channel_id=1, source_target_pairs={{0,4},{1,5},{2,6},{3,7},{4,0},{5,1},{6,2},{7,3},{8,12},{9,13},{10,... | collective-permute-start | bytes 98312 | tf_op jit(solution)/shard_map/ppermute | solution.py:17
  35.9 3.9 %collective-permute-start.17 = (bf16[128,128]{1,0:T(8,128)(2,1)S(1)}, bf16[128,128]{1,0:T(8,128)(2,1)S(1)}, u32[]{:S(2)}, u32[]{:S(2)}) collective-permute-start(bf16[128,128]{1,0:T(8,128)(2,1)S(1)} %get-tuple-element.52.refs_0_), channel_id=1, source_target_pairs={{0,2},{1,3},{2,0},{3,1},{4,6},{5,7},{6,4},{7,5},{8,10},{9,11},{10,... | collective-permute-start | bytes 98312 | tf_op jit(solution)/shard_map/ppermute | solution.py:17
  (1 other events, 0.7 us)

commit v20 on v19

--- a/solution.py
+++ b/solution.py
@@ -36,7 +36,8 @@
         for k in range(count):
             col = cols_ref[k, row] - lax.axis_index("rep") * (own_blocks * dom)
             owner = lax.div(col, jnp.int32(own_blocks)) ^ lax.axis_index("dom")
-            place = ((owner & 1) * (dom // 2) + (owner >> 1)) * own_blocks
+            side = jnp.where(owner > 1, 1 - (owner & 1), owner)
+            place = (side * (dom // 2) + (owner >> 1)) * own_blocks
             place += lax.rem(col, jnp.int32(own_blocks))
             place_ref[row * count + k : row * count + k + 1, :] = jnp.full((1, 128), place, jnp.int32)
 
@@ -120,11 +121,16 @@
         refs[0][0] = sums_in[0] + part_sum
         refs[0][1] = sums_in[1]
     else:
-        first_ref, rest_ref = refs
-        away = contrib[quarter_blocks // 2 :].reshape(quarter_blocks // 2 * size, -1).astype(BF16)
-        rest_ref[...] = away[:-nodes]
-        first_ref[:nodes] = away[-nodes:]
-        first_ref[nodes:] = (sums_in[0] + (sums_in[1] + part_sum)).astype(BF16)
+        across_ref, beside_ref = refs
+        half = quarter_blocks // 2
+        rest = quarter_blocks * size // 2 - nodes
+        weight = (sums_in[0] + (sums_in[1] + part_sum)).astype(BF16)
+        across_ref[:nodes] = contrib[half - own_blocks : half].reshape(nodes, -1).astype(BF16)
+        across_ref[2 * nodes :] = weight
+        beside_ref[rest:] = weight
+        away = contrib[half:].reshape(half * size, -1).astype(BF16)
+        across_ref[nodes : 2 * nodes] = away[rest:]
+        beside_ref[:rest] = away[:rest]
 
 
 def add_kernel(a_ref, b_ref, out_ref):
@@ -139,22 +145,23 @@
         out_ref[pl.ds(pl.multiple_of(target * part, part), part), :] = piece[...]
 
 
-def first_pair_kernel(contrib_ref, sent_ref, got_ref, out_ref):
-    blocks, size, _ = contrib_ref.shape
-    nodes = out_ref.shape[0] - sent_ref.shape[1]
-    last = contrib_ref[blocks // 2 - nodes // size : blocks // 2].reshape(nodes, -1)
-    weight = (sent_ref[nodes:].astype(F32) + got_ref[nodes:].astype(F32)).astype(BF16)
-    out_ref[:nodes] = (last + got_ref[:nodes].astype(F32)).astype(BF16)
-    out_ref[nodes:] = weight
-
-
-def rest_pair_kernel(contrib_ref, got_ref, first_ref, weight_ref, own_ref, *outs):
+def pair_kernel(contrib_ref, sent_ref, got_ref, own_ref, *outs):
     size, nodes = contrib_ref.shape[1], own_ref.shape[0]
-    weight_ref[...] = first_ref[nodes:]
-    for chip, out_ref in enumerate([own_ref, *outs]):
+    rest = nodes * len(outs)
+    weight = (sent_ref[rest:].astype(F32) + got_ref[rest:].astype(F32)).astype(BF16)
+    for chip in range(len(outs)):
         mine = contrib_ref[chip * nodes // size : (chip + 1) * nodes // size].reshape(nodes, -1)
         total = mine + got_ref[chip * nodes : (chip + 1) * nodes].astype(F32)
-        out_ref[...] = total.astype(out_ref.dtype)
+        if chip == 0:
+            own_ref[...] = total
+        else:
+            outs[chip - 1][:nodes] = total.astype(BF16)
+            outs[chip - 1][nodes:] = weight
+    outs[-1][...] = weight
+
+
+def pass_kernel(got_ref, out_ref):
+    out_ref[...] = got_ref[got_ref.shape[0] - out_ref.shape[0] :]
 
 
 def total_of(values):
@@ -163,24 +170,22 @@
     return values[0]
 
 
-def lift_kernel(got_ref, out_ref):
-    out_ref[...] = got_ref[...].astype(F32)
-
-
-def early_sum_kernel(own_ref, lifted_ref, *refs):
+def early_sum_kernel(own_ref, across_ref, *refs):
     got, out_ref = refs[:-1], refs[-1]
     nodes = own_ref.shape[0]
-    total = own_ref[...] + lifted_ref[:nodes]
+    total = own_ref[...] + across_ref[:nodes].astype(F32)
     for g in got:
-        total += g[...].astype(F32)
+        total += g[:nodes].astype(F32)
     out_ref[...] = total
 
 
-def final_kernel(early_ref, lifted_ref, got_ref, *refs):
-    weights, (feature_ref, weight_ref) = refs[:-2], refs[-2:]
-    feature_ref[...] = early_ref[...] + got_ref[...].astype(F32)
-    across = lifted_ref[feature_ref.shape[0] :]
-    weight_ref[...] = total_of([w[...].astype(F32) for w in weights] + [across])
+def final_kernel(early_ref, weight_ref, across_ref, passed_ref, *refs):
+    got, (feature_ref, grad_ref) = refs[:-2], refs[-2:]
+    nodes = feature_ref.shape[0]
+    feature_ref[...] = early_ref[...] + passed_ref[:nodes].astype(F32)
+    weights = [weight_ref[...].astype(F32)] + [g[nodes:].astype(F32) for g in got]
+    across = across_ref[2 * nodes :].astype(F32) + passed_ref[nodes:].astype(F32)
+    grad_ref[...] = total_of(weights + [across.astype(BF16).astype(F32)])
 
 
 def shape(dims, dtype):
@@ -219,7 +224,7 @@
         nodes_in = sum(v.shape[0] for v in values)
         return call(join_kernel, shape((nodes_in, width), BF16), [VMEM] * len(values))(*values)
 
-    across = [swap(features, "dom", 2 * chip) for chip in range(1, chips)]
+    across = [swap(features, "dom", 2 * chip + 1) for chip in range(1, chips)]
     ends = join(own, across[-1])
     far_ends = swap(ends, "dom", 1)
     half = chips // 2 - 1
@@ -259,8 +264,8 @@
             outs += [shape((2, width, width), F32)]
         else:
             outs += [
-                shape((nodes + width, width), BF16),
-                shape(((chips - 1) * nodes, width), BF16),
+                shape((2 * nodes + width, width), BF16),
+                shape(((chips - 1) * nodes + width, width), BF16),
             ]
         output, *carried = call(
             functools.partial(layer_kernel, rep, count, own_blocks, j),
@@ -269,35 +274,29 @@
             aliases={6: 1} if carried else {},
         )(place, flipped, cotangent, weight, bias.reshape(1, width), piece, *carried)
         outputs.append(output)
-    contrib, first, rest = carried
-
+    contrib, across, beside = carried
+
+    last = chips - 1
     message = shape((nodes + width, width), BF16)
-    got_first, got_rest = swap(first, "dom", 1), swap(rest, "dom", 1)
-    first = call(first_pair_kernel, message, [VMEM] * 3, cost=5 * 10**9)(contrib, first, got_first)
-    pair_weight, own, *rest = call(
-        rest_pair_kernel,
-        [shape((width, width), BF16), shape((nodes, width), F32)]
-        + [shape((nodes, width), BF16)] * (chips - 2),
+    got_across = swap(across, "dom", 2 * last + 1)
+    own, *sends, pair_weight = call(
+        pair_kernel,
+        [shape((nodes, width), F32)] + [message] * (last - 1) + [shape((width, width), BF16)],
         [VMEM] * 3,
-        cost=10**9,
-    )(contrib, got_rest, first)
-    last = chips - 1
-    got = {last: swap(first, "dom", 2 * last)}
-    got |= {chip: swap(rest[chip - 1], "dom", 2 * chip) for chip in range(last - 1, 0, -1)}
-    weights = {chip: swap(pair_weight, "dom", 2 * chip) for chip in range(last - 1, 0, -1)}
-    weights[0] = pair_weight
+    )(contrib, beside, swap(beside, "dom", 1))
+    got = {chip: swap(sends[chip - 1], "dom", 2 * chip + 1) for chip in range(last - 1, 0, -1)}
+    passed = swap(call(pass_kernel, message, [VMEM])(got_across), "dom", 1)
     output = call(
         functools.partial(order_kernel, list(pieces)), shape((rows * size, width), BF16), [VMEM] * rep
     )(*outputs)
-    lifted = call(lift_kernel, shape(message.shape, F32), [VMEM], cost=0)(got[last])
-    early = call(early_sum_kernel, shape((nodes, width), F32), [VMEM] * last, cost=0)(
-        own, lifted, *[got[chip] for chip in range(last - 1, 1, -1)]
+    early = call(early_sum_kernel, shape((nodes, width), F32), [VMEM] * chips)(
+        own, got_across, *[got[chip] for chip in range(last - 1, 0, -1)]
     )
     feature_grad, weight_grad = call(
         final_kernel,
         [shape((nodes, width), F32), shape((width, width), F32)],
         [VMEM] * (chips + 2),
-    )(early, lifted, got[1], *[weights[chip] for chip in range(last)])
+    )(early, pair_weight, got_across, passed, *[got[chip] for chip in range(1, last)])
     return output, feature_grad, weight_grad
 
 

time: 40.7 us -> 39.6 us (0.973)
  starting transfers between devices: 19.8 us -> 18.5 us
    ppermute x19 -> x17, starting transfers between devices: 19.8 us -> 18.5 us  [swap(): return lax.ppermute(value, axis, [(i, i ^ distance) for i in range(size)])]
    ppermute x19 -> x17, waiting for transfers between devices: 12.9 us -> 13.1 us  [swap(): return lax.ppermute(value, axis, [(i, i ^ distance) for i in range(size)])]
  transfers between devices with their start and end apart: 19 -> 17, of which waited for: 14 -> 12; matrix products, arithmetic and copies ran while one was open for 0% -> 0% of each run, Pallas kernels for 7% -> 7%
where the time goes in v20:
time: 39.6 us; the launch traced here: 39.4 us
  starting transfers between devices  18.5 us (47%)
  waiting for transfers between devices  13.1 us (33%)
  Pallas kernels  4.44 us (11%)
  local copies, waits for them, and re-layouts  2.55 us (6%)
  between operations  0.8 us (2%)
    ppermute x17, starting transfers between devices, swap(): return lax.ppermute(value, axis, [(i, i ^ distance) for i in range(size)])  18.5 us
    ppermute x17, waiting for transfers between devices, swap(): return lax.ppermute(value, axis, [(i, i ^ distance) for i in range(size)])  13.1 us
    unnamed x12, local copies, waits for them, and re-layouts  2.55 us
    pallas_call x4, Pallas kernels, body(): call(functools.partial(layer_kernel, rep, count, own_blocks, j), outs, [V...  2.11 us
  transfers between devices with their start and end apart: 17, of which 12 were waited for; matrix products, arithmetic and copies ran while one was open for 0% of the time, Pallas kernels for 7%

profile of v20, /device:TPU:0, one launch (start us, length us, event | category | flops | bytes accessed | tf_op | source)
XLA Modules:
  0.0 39.4 jit_solution(6329611121799217389)
XLA Ops:
  0.6 3.4 %collective-permute-start = (bf16[256,128]{1,0:T(8,128)(2,1)}, bf16[256,128]{1,0:T(8,128)(2,1)S(1)}, u32[]{:S(2)}, u32[]{:S(2)}) collective-permute-start(bf16[256,128]{1,0:T(8,128)(2,1)} %features_ref.1), channel_id=1, source_target_pairs={{0,7},{1,6},{2,5},{3,4},{4,3},{5,2},{6,1},{7,0},{8,15},{9,14},{10,... | collective-permute-start | bytes 196616 | tf_op jit(solution)/shard_map/ppermute | solution.py:17
  4.0 0.8 %collective-permute-start.2 = (bf16[256,128]{1,0:T(8,128)(2,1)}, bf16[256,128]{1,0:T(8,128)(2,1)S(1)}, u32[]{:S(2)}, u32[]{:S(2)}) collective-permute-start(bf16[256,128]{1,0:T(8,128)(2,1)} %features_ref.1), channel_id=1, source_target_pairs={{0,5},{1,4},{2,7},{3,6},{4,1},{5,0},{6,3},{7,2},{8,13},{9,12},{10,... | collective-permute-start | bytes 196616 | tf_op jit(solution)/shard_map/ppermute | solution.py:17
  5.0 1.0 %copy-done.2 = bf16[8,2,128,128]{3,2,1,0:T(8,128)(2,1)S(1)} copy-done((bf16[8,2,128,128]{3,2,1,0:T(8,128)(2,1)S(1)}, bf16[8,2,128,128]{3,2,1,0:T(8,128)(2,1)}, u32[]{:S(2)}) %copy-start.2) | copy-done | bytes 524312
  6.0 0.8 %copy-done.3 = bf16[256,128]{1,0:T(8,128)(2,1)S(1)} copy-done((bf16[256,128]{1,0:T(8,128)(2,1)S(1)}, bf16[256,128]{1,0:T(8,128)(2,1)}, u32[]{:S(2)}) %copy-start.3) | copy-done | bytes 65560
  7.2 1.0 %collective-permute-done.2.refs_1_ = bf16[256,128]{1,0:T(8,128)(2,1)S(1)} collective-permute-done((bf16[256,128]{1,0:T(8,128)(2,1)}, bf16[256,128]{1,0:T(8,128)(2,1)S(1)}, u32[]{:S(2)}, u32[]{:S(2)}) %collective-permute-start.2) | collective-permute-done | bytes 65568 | tf_op jit(solution)/shard_map/ppermute | solution.py:17
  8.2 0.7 %collective-permute-start.5 = (bf16[256,128]{1,0:T(8,128)(2,1)S(1)}, bf16[256,128]{1,0:T(8,128)(2,1)S(1)}, u32[]{:S(2)}, u32[]{:S(2)}) collective-permute-start(bf16[256,128]{1,0:T(8,128)(2,1)S(1)} %collective-permute-done.2.refs_1_), channel_id=1, source_target_pairs={{0,1},{1,0},{2,3},{3,2},{4,5},{5,4},{6,7},{7,6},{8,9},{9,8},{10,11... | collective-permute-start | bytes 196616 | tf_op jit(solution)/shard_map/ppermute | solution.py:17
  9.8 0.8 %collective-permute-done.4.refs_0_ = bf16[256,128]{1,0:T(8,128)(2,1)S(1)} collective-permute-done((bf16[256,128]{1,0:T(8,128)(2,1)S(1)}, bf16[256,128]{1,0:T(8,128)(2,1)S(1)}, u32[]{:S(2)}, u32[]{:S(2)}) %collective-permute-start.4) | collective-permute-done | bytes 65568 | tf_op jit(solution)/shard_map/ppermute | solution.py:17
  11.0 3.7 %collective-permute-start.6 = (bf16[256,128]{1,0:T(8,128)(2,1)S(1)}, bf16[256,128]{1,0:T(8,128)(2,1)S(1)}, u32[]{:S(2)}, u32[]{:S(2)}) collective-permute-start(bf16[256,128]{1,0:T(8,128)(2,1)S(1)} %get-tuple-element.33), channel_id=1, source_target_pairs={{0,24},{8,16},{16,8},{24,0},{1,25},{9,17},{17,9},{25,1},{2,26},{10... | collective-permute-start | bytes 196616 | tf_op jit(solution)/shard_map/ppermute | solution.py:17
  14.7 0.8 %collective-permute-start.8 = (bf16[256,128]{1,0:T(8,128)(2,1)S(1)}, bf16[256,128]{1,0:T(8,128)(2,1)S(1)}, u32[]{:S(2)}, u32[]{:S(2)}) collective-permute-start(bf16[256,128]{1,0:T(8,128)(2,1)S(1)} %get-tuple-element.35), channel_id=1, source_target_pairs={{0,16},{8,24},{16,0},{24,8},{1,17},{9,25},{17,1},{25,9},{2,18},{10... | collective-permute-start | bytes 196616 | tf_op jit(solution)/shard_map/ppermute | solution.py:17
  15.4 2.3 %collective-permute-done.6.b_ref = bf16[256,128]{1,0:T(8,128)(2,1)S(1)} collective-permute-done((bf16[256,128]{1,0:T(8,128)(2,1)S(1)}, bf16[256,128]{1,0:T(8,128)(2,1)S(1)}, u32[]{:S(2)}, u32[]{:S(2)}) %collective-permute-start.6) | collective-permute-done | bytes 65568 | tf_op jit(solution)/shard_map/ppermute | solution.py:17
  17.8 1.9 %collective-permute-done.7.b_ref = bf16[256,128]{1,0:T(8,128)(2,1)S(1)} collective-permute-done((bf16[256,128]{1,0:T(8,128)(2,1)S(1)}, bf16[256,128]{1,0:T(8,128)(2,1)S(1)}, u32[]{:S(2)}, u32[]{:S(2)}) %collective-permute-start.7) | collective-permute-done | bytes 65568 | tf_op jit(solution)/shard_map/ppermute | solution.py:17
  19.8 0.7 %collective-permute-done.8.b_ref = bf16[256,128]{1,0:T(8,128)(2,1)S(1)} collective-permute-done((bf16[256,128]{1,0:T(8,128)(2,1)S(1)}, bf16[256,128]{1,0:T(8,128)(2,1)S(1)}, u32[]{:S(2)}, u32[]{:S(2)}) %collective-permute-start.8) | collective-permute-done | bytes 65568 | tf_op jit(solution)/shard_map/ppermute | solution.py:17
  20.5 2.3 %collective-permute-start.9 = (bf16[256,128]{1,0:T(8,128)(2,1)S(1)}, bf16[256,128]{1,0:T(8,128)(2,1)S(1)}, u32[]{:S(2)}, u32[]{:S(2)}) collective-permute-start(bf16[256,128]{1,0:T(8,128)(2,1)S(1)} %shard_map.93.refs_0_), channel_id=1, source_target_pairs={{0,24},{8,16},{16,8},{24,0},{1,25},{9,17},{17,9},{25,1},{2,26},{10... | collective-permute-start | bytes 196616 | tf_op jit(solution)/shard_map/ppermute | solution.py:17
  23.2 1.8 %collective-permute-start.11 = (bf16[256,128]{1,0:T(8,128)(2,1)S(1)}, bf16[256,128]{1,0:T(8,128)(2,1)S(1)}, u32[]{:S(2)}, u32[]{:S(2)}) collective-permute-start(bf16[256,128]{1,0:T(8,128)(2,1)S(1)} %shard_map.93.refs_0_), channel_id=1, source_target_pairs={{0,16},{8,24},{16,0},{24,8},{1,17},{9,25},{17,1},{25,9},{2,18},{10... | collective-permute-start | bytes 196616 | tf_op jit(solution)/shard_map/ppermute | solution.py:17
  25.0 0.6 %copy-done.4 = f32[128]{0:T(128)S(1)} copy-done((f32[128]{0:T(128)S(1)}, f32[128]{0:T(128)}, u32[]{:S(2)}) %copy-start.4) | copy-done | bytes 536
  26.2 0.7 %collective-permute-done.9.refs_0_ = bf16[256,128]{1,0:T(8,128)(2,1)S(1)} collective-permute-done((bf16[256,128]{1,0:T(8,128)(2,1)S(1)}, bf16[256,128]{1,0:T(8,128)(2,1)S(1)}, u32[]{:S(2)}, u32[]{:S(2)}) %collective-permute-start.9) | collective-permute-done | bytes 65568 | tf_op jit(solution)/shard_map/ppermute | solution.py:17
  28.5 0.6 %shard_map.97 = (bf16[256,128]{1,0:T(8,128)(2,1)S(1)}, f32[16,128,128]{2,1,0:T(8,128)S(1)}, bf16[640,128]{1,0:T(8,128)(2,1)S(1)}, bf16[896,128]{1,0:T(8,128)(2,1)S(1)}) custom-call(s32[16,128]{1,0:T(8,128)S(1)} %shard_map.87.place_ref, bf16[8,256,128]{2,1,0:T(8,128)(2,1)S(1)} %get-tuple-element.30.flipped_ref, ...), custom_call_target="tpu_custom_call", output_to_operand_aliasing={{1}: (6, {})} | custom-call | tf_op jit(solution)/shard_map/pallas_call | solution.py:270
  29.1 1.6 %collective-permute-start.13 = (bf16[640,128]{1,0:T(8,128)(2,1)S(1)}, bf16[640,128]{1,0:T(8,128)(2,1)S(1)}, u32[]{:S(2)}, u32[]{:S(2)}) collective-permute-start(bf16[640,128]{1,0:T(8,128)(2,1)S(1)} %get-tuple-element.49), channel_id=1, source_target_pairs={{0,7},{1,6},{2,5},{3,4},{4,3},{5,2},{6,1},{7,0},{8,15},{9,14},{10,... | collective-permute-start | bytes 491528 | tf_op jit(solution)/shard_map/ppermute | solution.py:17
  30.8 1.3 %collective-permute-start.14 = (bf16[384,128]{1,0:T(8,128)(2,1)S(1)}, bf16[384,128]{1,0:T(8,128)(2,1)S(1)}, u32[]{:S(2)}, u32[]{:S(2)}) collective-permute-start(bf16[384,128]{1,0:T(8,128)(2,1)S(1)} %get-tuple-element.50), channel_id=1, source_target_pairs={{0,5},{1,4},{2,7},{3,6},{4,1},{5,0},{6,3},{7,2},{8,13},{9,12},{10,... | collective-permute-start | bytes 294920 | tf_op jit(solution)/shard_map/ppermute | solution.py:17
  32.6 3.5 %collective-permute-done.13.across_ref.got_ref = bf16[640,128]{1,0:T(8,128)(2,1)S(1)} collective-permute-done((bf16[640,128]{1,0:T(8,128)(2,1)S(1)}, bf16[640,128]{1,0:T(8,128)(2,1)S(1)}, u32[]{:S(2)}, u32[]{:S(2)}) %collective-permute-start.13) | collective-permute-done | bytes 163872 | tf_op jit(solution)/shard_map/ppermute | solution.py:17
  36.1 1.0 %collective-permute-start.16 = (bf16[384,128]{1,0:T(8,128)(2,1)S(1)}, bf16[384,128]{1,0:T(8,128)(2,1)S(1)}, u32[]{:S(2)}, u32[]{:S(2)}) collective-permute-start(bf16[384,128]{1,0:T(8,128)(2,1)S(1)} %shard_map.101), channel_id=1, source_target_pairs={{0,1},{1,0},{2,3},{3,2},{4,5},{5,4},{6,7},{7,6},{8,9},{9,8},{10,11... | collective-permute-start | bytes 294920 | tf_op jit(solution)/shard_map/ppermute | solution.py:17
  37.1 0.7 %shard_map.98 = bf16[1024,128]{1,0:T(8,128)(2,1)} custom-call(bf16[256,128]{1,0:T(8,128)(2,1)S(1)} %get-tuple-element.36.refs_0_, bf16[256,128]{1,0:T(8,128)(2,1)S(1)} %get-tuple-element.39.refs_1_, bf16[256,128]{1,0:T(8,128)(2,1)S(1)} %get-tuple-element.42.refs_2_, bf16[256,128]{1,0:T(8,128)(2,1)S(1)} %get-tuple-element.45.refs_3_), custom_call_target="tpu_custom_call" | custom-call | tf_op jit(solution)/shard_map/pallas_call | solution.py:289
  37.8 0.9 %collective-permute-done.14.refs_0_.refs_1_ = bf16[384,128]{1,0:T(8,128)(2,1)S(1)} collective-permute-done((bf16[384,128]{1,0:T(8,128)(2,1)S(1)}, bf16[384,128]{1,0:T(8,128)(2,1)S(1)}, u32[]{:S(2)}, u32[]{:S(2)}) %collective-permute-start.14) | collective-permute-done | bytes 98336 | tf_op jit(solution)/shard_map/ppermute | solution.py:17
  38.7 0.7 %shard_map.102 = (f32[256,128]{1,0:T(8,128)}, f32[128,128]{1,0:T(8,128)}) custom-call(f32[256,128]{1,0:T(8,128)S(1)} %shard_map.100.early_ref, bf16[128,128]{1,0:T(8,128)(2,1)S(1)} %get-tuple-element.52.weight_ref, bf16[640,128]{1,0:T(8,128)(2,1)S(1)} %collective-permute-done.13.across_ref.got_ref, bf16[384,128]{1,0:T(8,128)(2,1)S(1)} %collective-permute-done.16.passed_ref, ...), custom_call_target="tpu_custom_call" | custom-call | tf_op jit(solution)/shard_map/pallas_call | solution.py:295
  (40 shorter events, 4.9 us)
Async XLA Ops:
  0.6 6.4 %collective-permute-start = (bf16[256,128]{1,0:T(8,128)(2,1)}, bf16[256,128]{1,0:T(8,128)(2,1)S(1)}, u32[]{:S(2)}, u32[]{:S(2)}) collective-permute-start(bf16[256,128]{1,0:T(8,128)(2,1)} %features_ref.1), channel_id=1, source_target_pairs={{0,7},{1,6},{2,5},{3,4},{4,3},{5,2},{6,1},{7,0},{8,15},{9,14},{10,... | collective-permute-start | bytes 196616 | tf_op jit(solution)/shard_map/ppermute | solution.py:17
  4.0 4.2 %collective-permute-start.2 = (bf16[256,128]{1,0:T(8,128)(2,1)}, bf16[256,128]{1,0:T(8,128)(2,1)S(1)}, u32[]{:S(2)}, u32[]{:S(2)}) collective-permute-start(bf16[256,128]{1,0:T(8,128)(2,1)} %features_ref.1), channel_id=1, source_target_pairs={{0,5},{1,4},{2,7},{3,6},{4,1},{5,0},{6,3},{7,2},{8,13},{9,12},{10,... | collective-permute-start | bytes 196616 | tf_op jit(solution)/shard_map/ppermute | solution.py:17
  4.8 4.5 %collective-permute-start.1 = (bf16[256,128]{1,0:T(8,128)(2,1)}, bf16[256,128]{1,0:T(8,128)(2,1)S(1)}, u32[]{:S(2)}, u32[]{:S(2)}) collective-permute-start(bf16[256,128]{1,0:T(8,128)(2,1)} %features_ref.1), channel_id=1, source_target_pairs={{0,3},{1,2},{2,1},{3,0},{4,7},{5,6},{6,5},{7,4},{8,11},{9,10},{10,... | collective-permute-start | bytes 196616 | tf_op jit(solution)/shard_map/ppermute | solution.py:17
  5.0 1.0 %copy-start.2 = (bf16[8,2,128,128]{3,2,1,0:T(8,128)(2,1)S(1)}, bf16[8,2,128,128]{3,2,1,0:T(8,128)(2,1)}, u32[]{:S(2)}) copy-start(bf16[8,2,128,128]{3,2,1,0:T(8,128)(2,1)} %vals_ref.1) | copy-start | bytes 1572868
  6.0 0.8 %copy-start.3 = (bf16[256,128]{1,0:T(8,128)(2,1)S(1)}, bf16[256,128]{1,0:T(8,128)(2,1)}, u32[]{:S(2)}) copy-start(bf16[256,128]{1,0:T(8,128)(2,1)} %features_ref.1) | copy-start | bytes 196612
  7.1 2.4 %copy-start.5 = (s32[8,2]{0,1:T(2,128)S(1)}, s32[8,2]{0,1:T(2,128)}, u32[]{:S(2)}) copy-start(s32[8,2]{0,1:T(2,128)} %param.6) | copy-start | bytes 196
  7.1 3.5 %collective-permute-start.3 = (bf16[512,128]{1,0:T(8,128)(2,1)S(1)}, bf16[512,128]{1,0:T(8,128)(2,1)S(1)}, u32[]{:S(2)}, u32[]{:S(2)}) collective-permute-start(bf16[512,128]{1,0:T(8,128)(2,1)S(1)} %shard_map.86._.ends_ref), channel_id=1, source_target_pairs={{0,1},{1,0},{2,3},{3,2},{4,5},{5,4},{6,7},{7,6},{8,9},{9,8},{10,11... | collective-permute-start | bytes 393224 | tf_op jit(solution)/shard_map/ppermute | solution.py:17
  8.2 1.6 %collective-permute-start.5 = (bf16[256,128]{1,0:T(8,128)(2,1)S(1)}, bf16[256,128]{1,0:T(8,128)(2,1)S(1)}, u32[]{:S(2)}, u32[]{:S(2)}) collective-permute-start(bf16[256,128]{1,0:T(8,128)(2,1)S(1)} %collective-permute-done.2.refs_1_), channel_id=1, source_target_pairs={{0,1},{1,0},{2,3},{3,2},{4,5},{5,4},{6,7},{7,6},{8,9},{9,8},{10,11... | collective-permute-start | bytes 196616 | tf_op jit(solution)/shard_map/ppermute | solution.py:17
  9.3 1.3 %collective-permute-start.4 = (bf16[256,128]{1,0:T(8,128)(2,1)S(1)}, bf16[256,128]{1,0:T(8,128)(2,1)S(1)}, u32[]{:S(2)}, u32[]{:S(2)}) collective-permute-start(bf16[256,128]{1,0:T(8,128)(2,1)S(1)} %collective-permute-done.1.refs_0_), channel_id=1, source_target_pairs={{0,1},{1,0},{2,3},{3,2},{4,5},{5,4},{6,7},{7,6},{8,9},{9,8},{10,11... | collective-permute-start | bytes 196616 | tf_op jit(solution)/shard_map/ppermute | solution.py:17
  11.0 6.8 %collective-permute-start.6 = (bf16[256,128]{1,0:T(8,128)(2,1)S(1)}, bf16[256,128]{1,0:T(8,128)(2,1)S(1)}, u32[]{:S(2)}, u32[]{:S(2)}) collective-permute-start(bf16[256,128]{1,0:T(8,128)(2,1)S(1)} %get-tuple-element.33), channel_id=1, source_target_pairs={{0,24},{8,16},{16,8},{24,0},{1,25},{9,17},{17,9},{25,1},{2,26},{10... | collective-permute-start | bytes 196616 | tf_op jit(solution)/shard_map/ppermute | solution.py:17
  14.7 5.1 %collective-permute-start.7 = (bf16[256,128]{1,0:T(8,128)(2,1)S(1)}, bf16[256,128]{1,0:T(8,128)(2,1)S(1)}, u32[]{:S(2)}, u32[]{:S(2)}) collective-permute-start(bf16[256,128]{1,0:T(8,128)(2,1)S(1)} %get-tuple-element.34), channel_id=1, source_target_pairs={{0,8},{8,0},{16,24},{24,16},{1,9},{9,1},{17,25},{25,17},{2,10},{10... | collective-permute-start | bytes 196616 | tf_op jit(solution)/shard_map/ppermute | solution.py:17
  14.7 5.9 %collective-permute-start.8 = (bf16[256,128]{1,0:T(8,128)(2,1)S(1)}, bf16[256,128]{1,0:T(8,128)(2,1)S(1)}, u32[]{:S(2)}, u32[]{:S(2)}) collective-permute-start(bf16[256,128]{1,0:T(8,128)(2,1)S(1)} %get-tuple-element.35), channel_id=1, source_target_pairs={{0,16},{8,24},{16,0},{24,8},{1,17},{9,25},{17,1},{25,9},{2,18},{10... | collective-permute-start | bytes 196616 | tf_op jit(solution)/shard_map/ppermute | solution.py:17
  17.8 7.2 %copy-start = (bf16[1024,128]{1,0:T(8,128)(2,1)S(1)}, bf16[1024,128]{1,0:T(8,128)(2,1)}, u32[]{:S(2)}) copy-start(bf16[1024,128]{1,0:T(8,128)(2,1)} %cotangent_ref.7) | copy-start | bytes 786436
  19.8 5.2 %copy-start.1 = (bf16[128,128]{1,0:T(8,128)(2,1)S(1)}, bf16[128,128]{1,0:T(8,128)(2,1)}, u32[]{:S(2)}) copy-start(bf16[128,128]{1,0:T(8,128)(2,1)} %weight_ref.7) | copy-start | bytes 98308
  20.5 6.3 %collective-permute-start.9 = (bf16[256,128]{1,0:T(8,128)(2,1)S(1)}, bf16[256,128]{1,0:T(8,128)(2,1)S(1)}, u32[]{:S(2)}, u32[]{:S(2)}) collective-permute-start(bf16[256,128]{1,0:T(8,128)(2,1)S(1)} %shard_map.93.refs_0_), channel_id=1, source_target_pairs={{0,24},{8,16},{16,8},{24,0},{1,25},{9,17},{17,9},{25,1},{2,26},{10... | collective-permute-start | bytes 196616 | tf_op jit(solution)/shard_map/ppermute | solution.py:17
  22.8 5.0 %collective-permute-start.10 = (bf16[256,128]{1,0:T(8,128)(2,1)S(1)}, bf16[256,128]{1,0:T(8,128)(2,1)S(1)}, u32[]{:S(2)}, u32[]{:S(2)}) collective-permute-start(bf16[256,128]{1,0:T(8,128)(2,1)S(1)} %shard_map.93.refs_0_), channel_id=1, source_target_pairs={{0,8},{8,0},{16,24},{24,16},{1,9},{9,1},{17,25},{25,17},{2,10},{10... | collective-permute-start | bytes 196616 | tf_op jit(solution)/shard_map/ppermute | solution.py:17
  23.2 5.3 %collective-permute-start.11 = (bf16[256,128]{1,0:T(8,128)(2,1)S(1)}, bf16[256,128]{1,0:T(8,128)(2,1)S(1)}, u32[]{:S(2)}, u32[]{:S(2)}) collective-permute-start(bf16[256,128]{1,0:T(8,128)(2,1)S(1)} %shard_map.93.refs_0_), channel_id=1, source_target_pairs={{0,16},{8,24},{16,0},{24,8},{1,17},{9,25},{17,1},{25,9},{2,18},{10... | collective-permute-start | bytes 196616 | tf_op jit(solution)/shard_map/ppermute | solution.py:17
  25.0 0.7 %copy-start.4 = (f32[128]{0:T(128)S(1)}, f32[128]{0:T(128)}, u32[]{:S(2)}) copy-start(f32[128]{0:T(128)} %param.10) | copy-start | bytes 1540
  29.1 1.7 %collective-permute-start.12 = (bf16[896,128]{1,0:T(8,128)(2,1)S(1)}, bf16[896,128]{1,0:T(8,128)(2,1)S(1)}, u32[]{:S(2)}, u32[]{:S(2)}) collective-permute-start(bf16[896,128]{1,0:T(8,128)(2,1)S(1)} %get-tuple-element.47.sent_ref), channel_id=1, source_target_pairs={{0,1},{1,0},{2,3},{3,2},{4,5},{5,4},{6,7},{7,6},{8,9},{9,8},{10,11... | collective-permute-start | bytes 688136 | tf_op jit(solution)/shard_map/ppermute | solution.py:17
  29.1 7.0 %collective-permute-start.13 = (bf16[640,128]{1,0:T(8,128)(2,1)S(1)}, bf16[640,128]{1,0:T(8,128)(2,1)S(1)}, u32[]{:S(2)}, u32[]{:S(2)}) collective-permute-start(bf16[640,128]{1,0:T(8,128)(2,1)S(1)} %get-tuple-element.49), channel_id=1, source_target_pairs={{0,7},{1,6},{2,5},{3,4},{4,3},{5,2},{6,1},{7,0},{8,15},{9,14},{10,... | collective-permute-start | bytes 491528 | tf_op jit(solution)/shard_map/ppermute | solution.py:17
  30.8 7.9 %collective-permute-start.14 = (bf16[384,128]{1,0:T(8,128)(2,1)S(1)}, bf16[384,128]{1,0:T(8,128)(2,1)S(1)}, u32[]{:S(2)}, u32[]{:S(2)}) collective-permute-start(bf16[384,128]{1,0:T(8,128)(2,1)S(1)} %get-tuple-element.50), channel_id=1, source_target_pairs={{0,5},{1,4},{2,7},{3,6},{4,1},{5,0},{6,3},{7,2},{8,13},{9,12},{10,... | collective-permute-start | bytes 294920 | tf_op jit(solution)/shard_map/ppermute | solution.py:17
  32.1 6.6 %collective-permute-start.15 = (bf16[384,128]{1,0:T(8,128)(2,1)S(1)}, bf16[384,128]{1,0:T(8,128)(2,1)S(1)}, u32[]{:S(2)}, u32[]{:S(2)}) collective-permute-start(bf16[384,128]{1,0:T(8,128)(2,1)S(1)} %get-tuple-element.51), channel_id=1, source_target_pairs={{0,3},{1,2},{2,1},{3,0},{4,7},{5,6},{6,5},{7,4},{8,11},{9,10},{10,... | collective-permute-start | bytes 294920 | tf_op jit(solution)/shard_map/ppermute | solution.py:17
  36.1 2.6 %collective-permute-start.16 = (bf16[384,128]{1,0:T(8,128)(2,1)S(1)}, bf16[384,128]{1,0:T(8,128)(2,1)S(1)}, u32[]{:S(2)}, u32[]{:S(2)}) collective-permute-start(bf16[384,128]{1,0:T(8,128)(2,1)S(1)} %shard_map.101), channel_id=1, source_target_pairs={{0,1},{1,0},{2,3},{3,2},{4,5},{5,4},{6,7},{7,6},{8,9},{9,8},{10,11... | collective-permute-start | bytes 294920 | tf_op jit(solution)/shard_map/ppermute | solution.py:17

commit v21 on v20

--- a/solution.py
+++ b/solution.py
@@ -121,16 +121,17 @@
         refs[0][0] = sums_in[0] + part_sum
         refs[0][1] = sums_in[1]
     else:
-        across_ref, beside_ref = refs
+        across_ref, beside_ref, others_ref = refs
         half = quarter_blocks // 2
         rest = quarter_blocks * size // 2 - nodes
         weight = (sums_in[0] + (sums_in[1] + part_sum)).astype(BF16)
-        across_ref[:nodes] = contrib[half - own_blocks : half].reshape(nodes, -1).astype(BF16)
+        away = contrib[half:].reshape(half * size, -1).astype(BF16)
+        across_ref[:nodes] = away[rest:]
+        across_ref[nodes : 2 * nodes] = contrib[half - own_blocks : half].reshape(nodes, -1).astype(BF16)
         across_ref[2 * nodes :] = weight
-        beside_ref[rest:] = weight
-        away = contrib[half:].reshape(half * size, -1).astype(BF16)
-        across_ref[nodes : 2 * nodes] = away[rest:]
-        beside_ref[:rest] = away[:rest]
+        beside_ref[:nodes] = away[:nodes]
+        beside_ref[nodes:] = weight
+        others_ref[...] = away[nodes:rest]
 
 
 def add_kernel(a_ref, b_ref, out_ref):
@@ -145,18 +146,15 @@
         out_ref[pl.ds(pl.multiple_of(target * part, part), part), :] = piece[...]
 
 
-def pair_kernel(contrib_ref, sent_ref, got_ref, own_ref, *outs):
+def pair_kernel(contrib_ref, sent_ref, got_ref, others_ref, own_ref, *outs):
     size, nodes = contrib_ref.shape[1], own_ref.shape[0]
-    rest = nodes * len(outs)
-    weight = (sent_ref[rest:].astype(F32) + got_ref[rest:].astype(F32)).astype(BF16)
-    for chip in range(len(outs)):
+    weight = (sent_ref[nodes:].astype(F32) + got_ref[nodes:].astype(F32)).astype(BF16)
+    own_ref[...] = contrib_ref[: nodes // size].reshape(nodes, -1) + got_ref[:nodes].astype(F32)
+    for chip in range(1, len(outs)):
         mine = contrib_ref[chip * nodes // size : (chip + 1) * nodes // size].reshape(nodes, -1)
-        total = mine + got_ref[chip * nodes : (chip + 1) * nodes].astype(F32)
-        if chip == 0:
-            own_ref[...] = total
-        else:
-            outs[chip - 1][:nodes] = total.astype(BF16)
-            outs[chip - 1][nodes:] = weight
+        total = mine + others_ref[(chip - 1) * nodes : chip * nodes].astype(F32)
+        outs[chip - 1][:nodes] = total.astype(BF16)
+        outs[chip - 1][nodes:] = weight
     outs[-1][...] = weight
 
 
@@ -265,7 +263,8 @@
         else:
             outs += [
                 shape((2 * nodes + width, width), BF16),
-                shape(((chips - 1) * nodes + width, width), BF16),
+                shape((nodes + width, width), BF16),
+                shape(((chips - 2) * nodes, width), BF16),
             ]
         output, *carried = call(
             functools.partial(layer_kernel, rep, count, own_blocks, j),
@@ -274,16 +273,16 @@
             aliases={6: 1} if carried else {},
         )(place, flipped, cotangent, weight, bias.reshape(1, width), piece, *carried)
         outputs.append(output)
-    contrib, across, beside = carried
+    contrib, across, beside, others = carried
 
     last = chips - 1
     message = shape((nodes + width, width), BF16)
-    got_across = swap(across, "dom", 2 * last + 1)
+    got_across = swap(across, "dom", 2 * last)
     own, *sends, pair_weight = call(
         pair_kernel,
         [shape((nodes, width), F32)] + [message] * (last - 1) + [shape((width, width), BF16)],
-        [VMEM] * 3,
-    )(contrib, beside, swap(beside, "dom", 1))
+        [VMEM] * 4,
+    )(contrib, beside, swap(beside, "dom", 1), swap(others, "dom", 1))
     got = {chip: swap(sends[chip - 1], "dom", 2 * chip + 1) for chip in range(last - 1, 0, -1)}
     passed = swap(call(pass_kernel, message, [VMEM])(got_across), "dom", 1)
     output = call(

time: 39.6 us -> 39.5 us (level)
  starting transfers between devices: 18.5 us -> 18 us
    ppermute x17 -> x18, starting transfers between devices: 18.5 us -> 18 us  [swap(): return lax.ppermute(value, axis, [(i, i ^ distance) for i in range(size)])]
    ppermute x17 -> x18, waiting for transfers between devices: 13.1 us -> 13.4 us  [swap(): return lax.ppermute(value, axis, [(i, i ^ distance) for i in range(size)])]
  transfers between devices with their start and end apart: 17 -> 18, of which waited for: 12 -> 14; matrix products, arithmetic and copies ran while one was open for 0% -> 0% of each run, Pallas kernels for 7% -> 7%
where the time goes in v21:
time: 39.5 us; the launch traced here: 39.3 us
  starting transfers between devices  18 us (46%)
  waiting for transfers between devices  13.4 us (34%)
  Pallas kernels  4.45 us (11%)
  local copies, waits for them, and re-layouts  2.55 us (6%)
  between operations  0.8 us (2%)
    ppermute x18, starting transfers between devices, swap(): return lax.ppermute(value, axis, [(i, i ^ distance) for i in range(size)])  18 us
    ppermute x18, waiting for transfers between devices, swap(): return lax.ppermute(value, axis, [(i, i ^ distance) for i in range(size)])  13.4 us
    unnamed x12, local copies, waits for them, and re-layouts  2.55 us
    pallas_call x4, Pallas kernels, body(): call(functools.partial(layer_kernel, rep, count, own_blocks, j), outs, [V...  2.11 us
  transfers between devices with their start and end apart: 18, of which 14 were waited for; matrix products, arithmetic and copies ran while one was open for 0% of the time, Pallas kernels for 7%

profile of v21, /device:TPU:0, one launch (start us, length us, event | category | flops | bytes accessed | tf_op | source)
XLA Modules:
  0.0 39.3 jit_solution(5938264498802659198)
XLA Ops:
  0.6 3.4 %collective-permute-start = (bf16[256,128]{1,0:T(8,128)(2,1)}, bf16[256,128]{1,0:T(8,128)(2,1)S(1)}, u32[]{:S(2)}, u32[]{:S(2)}) collective-permute-start(bf16[256,128]{1,0:T(8,128)(2,1)} %features_ref.1), channel_id=1, source_target_pairs={{0,7},{1,6},{2,5},{3,4},{4,3},{5,2},{6,1},{7,0},{8,15},{9,14},{10,... | collective-permute-start | bytes 196616 | tf_op jit(solution)/shard_map/ppermute | solution.py:17
  4.0 0.8 %collective-permute-start.2 = (bf16[256,128]{1,0:T(8,128)(2,1)}, bf16[256,128]{1,0:T(8,128)(2,1)S(1)}, u32[]{:S(2)}, u32[]{:S(2)}) collective-permute-start(bf16[256,128]{1,0:T(8,128)(2,1)} %features_ref.1), channel_id=1, source_target_pairs={{0,5},{1,4},{2,7},{3,6},{4,1},{5,0},{6,3},{7,2},{8,13},{9,12},{10,... | collective-permute-start | bytes 196616 | tf_op jit(solution)/shard_map/ppermute | solution.py:17
  5.0 1.0 %copy-done.2 = bf16[8,2,128,128]{3,2,1,0:T(8,128)(2,1)S(1)} copy-done((bf16[8,2,128,128]{3,2,1,0:T(8,128)(2,1)S(1)}, bf16[8,2,128,128]{3,2,1,0:T(8,128)(2,1)}, u32[]{:S(2)}) %copy-start.2) | copy-done | bytes 524312
  6.0 0.8 %copy-done.3 = bf16[256,128]{1,0:T(8,128)(2,1)S(1)} copy-done((bf16[256,128]{1,0:T(8,128)(2,1)S(1)}, bf16[256,128]{1,0:T(8,128)(2,1)}, u32[]{:S(2)}) %copy-start.3) | copy-done | bytes 65560
  7.2 1.0 %collective-permute-done.2.refs_1_ = bf16[256,128]{1,0:T(8,128)(2,1)S(1)} collective-permute-done((bf16[256,128]{1,0:T(8,128)(2,1)}, bf16[256,128]{1,0:T(8,128)(2,1)S(1)}, u32[]{:S(2)}, u32[]{:S(2)}) %collective-permute-start.2) | collective-permute-done | bytes 65568 | tf_op jit(solution)/shard_map/ppermute | solution.py:17
  8.2 0.7 %collective-permute-start.5 = (bf16[256,128]{1,0:T(8,128)(2,1)S(1)}, bf16[256,128]{1,0:T(8,128)(2,1)S(1)}, u32[]{:S(2)}, u32[]{:S(2)}) collective-permute-start(bf16[256,128]{1,0:T(8,128)(2,1)S(1)} %collective-permute-done.2.refs_1_), channel_id=1, source_target_pairs={{0,1},{1,0},{2,3},{3,2},{4,5},{5,4},{6,7},{7,6},{8,9},{9,8},{10,11... | collective-permute-start | bytes 196616 | tf_op jit(solution)/shard_map/ppermute | solution.py:17
  9.8 0.8 %collective-permute-done.4.refs_0_ = bf16[256,128]{1,0:T(8,128)(2,1)S(1)} collective-permute-done((bf16[256,128]{1,0:T(8,128)(2,1)S(1)}, bf16[256,128]{1,0:T(8,128)(2,1)S(1)}, u32[]{:S(2)}, u32[]{:S(2)}) %collective-permute-start.4) | collective-permute-done | bytes 65568 | tf_op jit(solution)/shard_map/ppermute | solution.py:17
  11.0 3.7 %collective-permute-start.6 = (bf16[256,128]{1,0:T(8,128)(2,1)S(1)}, bf16[256,128]{1,0:T(8,128)(2,1)S(1)}, u32[]{:S(2)}, u32[]{:S(2)}) collective-permute-start(bf16[256,128]{1,0:T(8,128)(2,1)S(1)} %get-tuple-element.34), channel_id=1, source_target_pairs={{0,24},{8,16},{16,8},{24,0},{1,25},{9,17},{17,9},{25,1},{2,26},{10... | collective-permute-start | bytes 196616 | tf_op jit(solution)/shard_map/ppermute | solution.py:17
  14.7 0.8 %collective-permute-start.8 = (bf16[256,128]{1,0:T(8,128)(2,1)S(1)}, bf16[256,128]{1,0:T(8,128)(2,1)S(1)}, u32[]{:S(2)}, u32[]{:S(2)}) collective-permute-start(bf16[256,128]{1,0:T(8,128)(2,1)S(1)} %get-tuple-element.36), channel_id=1, source_target_pairs={{0,16},{8,24},{16,0},{24,8},{1,17},{9,25},{17,1},{25,9},{2,18},{10... | collective-permute-start | bytes 196616 | tf_op jit(solution)/shard_map/ppermute | solution.py:17
  15.4 2.3 %collective-permute-done.6.b_ref = bf16[256,128]{1,0:T(8,128)(2,1)S(1)} collective-permute-done((bf16[256,128]{1,0:T(8,128)(2,1)S(1)}, bf16[256,128]{1,0:T(8,128)(2,1)S(1)}, u32[]{:S(2)}, u32[]{:S(2)}) %collective-permute-start.6) | collective-permute-done | bytes 65568 | tf_op jit(solution)/shard_map/ppermute | solution.py:17
  17.8 1.9 %collective-permute-done.7.b_ref = bf16[256,128]{1,0:T(8,128)(2,1)S(1)} collective-permute-done((bf16[256,128]{1,0:T(8,128)(2,1)S(1)}, bf16[256,128]{1,0:T(8,128)(2,1)S(1)}, u32[]{:S(2)}, u32[]{:S(2)}) %collective-permute-start.7) | collective-permute-done | bytes 65568 | tf_op jit(solution)/shard_map/ppermute | solution.py:17
  19.8 0.7 %collective-permute-done.8.b_ref = bf16[256,128]{1,0:T(8,128)(2,1)S(1)} collective-permute-done((bf16[256,128]{1,0:T(8,128)(2,1)S(1)}, bf16[256,128]{1,0:T(8,128)(2,1)S(1)}, u32[]{:S(2)}, u32[]{:S(2)}) %collective-permute-start.8) | collective-permute-done | bytes 65568 | tf_op jit(solution)/shard_map/ppermute | solution.py:17
  20.5 2.3 %collective-permute-start.9 = (bf16[256,128]{1,0:T(8,128)(2,1)S(1)}, bf16[256,128]{1,0:T(8,128)(2,1)S(1)}, u32[]{:S(2)}, u32[]{:S(2)}) collective-permute-start(bf16[256,128]{1,0:T(8,128)(2,1)S(1)} %shard_map.93.refs_0_), channel_id=1, source_target_pairs={{0,24},{8,16},{16,8},{24,0},{1,25},{9,17},{17,9},{25,1},{2,26},{10... | collective-permute-start | bytes 196616 | tf_op jit(solution)/shard_map/ppermute | solution.py:17
  23.2 1.8 %collective-permute-start.11 = (bf16[256,128]{1,0:T(8,128)(2,1)S(1)}, bf16[256,128]{1,0:T(8,128)(2,1)S(1)}, u32[]{:S(2)}, u32[]{:S(2)}) collective-permute-start(bf16[256,128]{1,0:T(8,128)(2,1)S(1)} %shard_map.93.refs_0_), channel_id=1, source_target_pairs={{0,16},{8,24},{16,0},{24,8},{1,17},{9,25},{17,1},{25,9},{2,18},{10... | collective-permute-start | bytes 196616 | tf_op jit(solution)/shard_map/ppermute | solution.py:17
  25.0 0.6 %copy-done.4 = f32[128]{0:T(128)S(1)} copy-done((f32[128]{0:T(128)S(1)}, f32[128]{0:T(128)}, u32[]{:S(2)}) %copy-start.4) | copy-done | bytes 536
  26.2 0.7 %collective-permute-done.9.refs_0_ = bf16[256,128]{1,0:T(8,128)(2,1)S(1)} collective-permute-done((bf16[256,128]{1,0:T(8,128)(2,1)S(1)}, bf16[256,128]{1,0:T(8,128)(2,1)S(1)}, u32[]{:S(2)}, u32[]{:S(2)}) %collective-permute-start.9) | collective-permute-done | bytes 65568 | tf_op jit(solution)/shard_map/ppermute | solution.py:17
  29.1 1.6 %collective-permute-start.14 = (bf16[640,128]{1,0:T(8,128)(2,1)S(1)}, bf16[640,128]{1,0:T(8,128)(2,1)S(1)}, u32[]{:S(2)}, u32[]{:S(2)}) collective-permute-start(bf16[640,128]{1,0:T(8,128)(2,1)S(1)} %get-tuple-element.51), channel_id=1, source_target_pairs={{0,6},{1,7},{2,4},{3,5},{4,2},{5,3},{6,0},{7,1},{8,14},{9,15},{10,... | collective-permute-start | bytes 491528 | tf_op jit(solution)/shard_map/ppermute | solution.py:17
  31.1 1.0 %collective-permute-done.12.got_ref = bf16[384,128]{1,0:T(8,128)(2,1)S(1)} collective-permute-done((bf16[384,128]{1,0:T(8,128)(2,1)S(1)}, bf16[384,128]{1,0:T(8,128)(2,1)S(1)}, u32[]{:S(2)}, u32[]{:S(2)}) %collective-permute-start.12) | collective-permute-done | bytes 98336 | tf_op jit(solution)/shard_map/ppermute | solution.py:17
  32.2 1.5 %collective-permute-start.15 = (bf16[384,128]{1,0:T(8,128)(2,1)S(1)}, bf16[384,128]{1,0:T(8,128)(2,1)S(1)}, u32[]{:S(2)}, u32[]{:S(2)}) collective-permute-start(bf16[384,128]{1,0:T(8,128)(2,1)S(1)} %get-tuple-element.52), channel_id=1, source_target_pairs={{0,5},{1,4},{2,7},{3,6},{4,1},{5,0},{6,3},{7,2},{8,13},{9,12},{10,... | collective-permute-start | bytes 294920 | tf_op jit(solution)/shard_map/ppermute | solution.py:17
  33.9 1.4 %collective-permute-done.14.across_ref.got_ref = bf16[640,128]{1,0:T(8,128)(2,1)S(1)} collective-permute-done((bf16[640,128]{1,0:T(8,128)(2,1)S(1)}, bf16[640,128]{1,0:T(8,128)(2,1)S(1)}, u32[]{:S(2)}, u32[]{:S(2)}) %collective-permute-start.14) | collective-permute-done | bytes 163872 | tf_op jit(solution)/shard_map/ppermute | solution.py:17
  35.4 0.7 %shard_map.98 = bf16[1024,128]{1,0:T(8,128)(2,1)} custom-call(bf16[256,128]{1,0:T(8,128)(2,1)S(1)} %get-tuple-element.37.refs_0_, bf16[256,128]{1,0:T(8,128)(2,1)S(1)} %get-tuple-element.40.refs_1_, bf16[256,128]{1,0:T(8,128)(2,1)S(1)} %get-tuple-element.43.refs_2_, bf16[256,128]{1,0:T(8,128)(2,1)S(1)} %get-tuple-element.46.refs_3_), custom_call_target="tpu_custom_call" | custom-call | tf_op jit(solution)/shard_map/pallas_call | solution.py:288
  36.2 1.0 %collective-permute-done.15.refs_0_.refs_1_ = bf16[384,128]{1,0:T(8,128)(2,1)S(1)} collective-permute-done((bf16[384,128]{1,0:T(8,128)(2,1)S(1)}, bf16[384,128]{1,0:T(8,128)(2,1)S(1)}, u32[]{:S(2)}, u32[]{:S(2)}) %collective-permute-start.15) | collective-permute-done | bytes 98336 | tf_op jit(solution)/shard_map/ppermute | solution.py:17
  37.1 1.4 %collective-permute-done.16.refs_1_.refs_0_ = bf16[384,128]{1,0:T(8,128)(2,1)S(1)} collective-permute-done((bf16[384,128]{1,0:T(8,128)(2,1)S(1)}, bf16[384,128]{1,0:T(8,128)(2,1)S(1)}, u32[]{:S(2)}, u32[]{:S(2)}) %collective-permute-start.16) | collective-permute-done | bytes 98336 | tf_op jit(solution)/shard_map/ppermute | solution.py:17
  38.6 0.7 %shard_map.102 = (f32[256,128]{1,0:T(8,128)}, f32[128,128]{1,0:T(8,128)}) custom-call(f32[256,128]{1,0:T(8,128)S(1)} %shard_map.100.early_ref, bf16[128,128]{1,0:T(8,128)(2,1)S(1)} %get-tuple-element.54.weight_ref, bf16[640,128]{1,0:T(8,128)(2,1)S(1)} %collective-permute-done.14.across_ref.got_ref, bf16[384,128]{1,0:T(8,128)(2,1)S(1)} %collective-permute-done.17.passed_ref, ...), custom_call_target="tpu_custom_call" | custom-call | tf_op jit(solution)/shard_map/pallas_call | solution.py:294
  (42 shorter events, 5.7 us)
Async XLA Ops:
  0.6 6.4 %collective-permute-start = (bf16[256,128]{1,0:T(8,128)(2,1)}, bf16[256,128]{1,0:T(8,128)(2,1)S(1)}, u32[]{:S(2)}, u32[]{:S(2)}) collective-permute-start(bf16[256,128]{1,0:T(8,128)(2,1)} %features_ref.1), channel_id=1, source_target_pairs={{0,7},{1,6},{2,5},{3,4},{4,3},{5,2},{6,1},{7,0},{8,15},{9,14},{10,... | collective-permute-start | bytes 196616 | tf_op jit(solution)/shard_map/ppermute | solution.py:17
  4.0 4.2 %collective-permute-start.2 = (bf16[256,128]{1,0:T(8,128)(2,1)}, bf16[256,128]{1,0:T(8,128)(2,1)S(1)}, u32[]{:S(2)}, u32[]{:S(2)}) collective-permute-start(bf16[256,128]{1,0:T(8,128)(2,1)} %features_ref.1), channel_id=1, source_target_pairs={{0,5},{1,4},{2,7},{3,6},{4,1},{5,0},{6,3},{7,2},{8,13},{9,12},{10,... | collective-permute-start | bytes 196616 | tf_op jit(solution)/shard_map/ppermute | solution.py:17
  4.8 4.5 %collective-permute-start.1 = (bf16[256,128]{1,0:T(8,128)(2,1)}, bf16[256,128]{1,0:T(8,128)(2,1)S(1)}, u32[]{:S(2)}, u32[]{:S(2)}) collective-permute-start(bf16[256,128]{1,0:T(8,128)(2,1)} %features_ref.1), channel_id=1, source_target_pairs={{0,3},{1,2},{2,1},{3,0},{4,7},{5,6},{6,5},{7,4},{8,11},{9,10},{10,... | collective-permute-start | bytes 196616 | tf_op jit(solution)/shard_map/ppermute | solution.py:17
  5.0 1.0 %copy-start.2 = (bf16[8,2,128,128]{3,2,1,0:T(8,128)(2,1)S(1)}, bf16[8,2,128,128]{3,2,1,0:T(8,128)(2,1)}, u32[]{:S(2)}) copy-start(bf16[8,2,128,128]{3,2,1,0:T(8,128)(2,1)} %vals_ref.1) | copy-start | bytes 1572868
  6.0 0.8 %copy-start.3 = (bf16[256,128]{1,0:T(8,128)(2,1)S(1)}, bf16[256,128]{1,0:T(8,128)(2,1)}, u32[]{:S(2)}) copy-start(bf16[256,128]{1,0:T(8,128)(2,1)} %features_ref.1) | copy-start | bytes 196612
  7.1 2.4 %copy-start.5 = (s32[8,2]{0,1:T(2,128)S(1)}, s32[8,2]{0,1:T(2,128)}, u32[]{:S(2)}) copy-start(s32[8,2]{0,1:T(2,128)} %param.6) | copy-start | bytes 196
  7.1 3.5 %collective-permute-start.3 = (bf16[512,128]{1,0:T(8,128)(2,1)S(1)}, bf16[512,128]{1,0:T(8,128)(2,1)S(1)}, u32[]{:S(2)}, u32[]{:S(2)}) collective-permute-start(bf16[512,128]{1,0:T(8,128)(2,1)S(1)} %shard_map.86._.ends_ref), channel_id=1, source_target_pairs={{0,1},{1,0},{2,3},{3,2},{4,5},{5,4},{6,7},{7,6},{8,9},{9,8},{10,11... | collective-permute-start | bytes 393224 | tf_op jit(solution)/shard_map/ppermute | solution.py:17
  8.2 1.6 %collective-permute-start.5 = (bf16[256,128]{1,0:T(8,128)(2,1)S(1)}, bf16[256,128]{1,0:T(8,128)(2,1)S(1)}, u32[]{:S(2)}, u32[]{:S(2)}) collective-permute-start(bf16[256,128]{1,0:T(8,128)(2,1)S(1)} %collective-permute-done.2.refs_1_), channel_id=1, source_target_pairs={{0,1},{1,0},{2,3},{3,2},{4,5},{5,4},{6,7},{7,6},{8,9},{9,8},{10,11... | collective-permute-start | bytes 196616 | tf_op jit(solution)/shard_map/ppermute | solution.py:17
  9.3 1.3 %collective-permute-start.4 = (bf16[256,128]{1,0:T(8,128)(2,1)S(1)}, bf16[256,128]{1,0:T(8,128)(2,1)S(1)}, u32[]{:S(2)}, u32[]{:S(2)}) collective-permute-start(bf16[256,128]{1,0:T(8,128)(2,1)S(1)} %collective-permute-done.1.refs_0_), channel_id=1, source_target_pairs={{0,1},{1,0},{2,3},{3,2},{4,5},{5,4},{6,7},{7,6},{8,9},{9,8},{10,11... | collective-permute-start | bytes 196616 | tf_op jit(solution)/shard_map/ppermute | solution.py:17
  11.0 6.8 %collective-permute-start.6 = (bf16[256,128]{1,0:T(8,128)(2,1)S(1)}, bf16[256,128]{1,0:T(8,128)(2,1)S(1)}, u32[]{:S(2)}, u32[]{:S(2)}) collective-permute-start(bf16[256,128]{1,0:T(8,128)(2,1)S(1)} %get-tuple-element.34), channel_id=1, source_target_pairs={{0,24},{8,16},{16,8},{24,0},{1,25},{9,17},{17,9},{25,1},{2,26},{10... | collective-permute-start | bytes 196616 | tf_op jit(solution)/shard_map/ppermute | solution.py:17
  14.7 5.1 %collective-permute-start.7 = (bf16[256,128]{1,0:T(8,128)(2,1)S(1)}, bf16[256,128]{1,0:T(8,128)(2,1)S(1)}, u32[]{:S(2)}, u32[]{:S(2)}) collective-permute-start(bf16[256,128]{1,0:T(8,128)(2,1)S(1)} %get-tuple-element.35), channel_id=1, source_target_pairs={{0,8},{8,0},{16,24},{24,16},{1,9},{9,1},{17,25},{25,17},{2,10},{10... | collective-permute-start | bytes 196616 | tf_op jit(solution)/shard_map/ppermute | solution.py:17
  14.7 5.9 %collective-permute-start.8 = (bf16[256,128]{1,0:T(8,128)(2,1)S(1)}, bf16[256,128]{1,0:T(8,128)(2,1)S(1)}, u32[]{:S(2)}, u32[]{:S(2)}) collective-permute-start(bf16[256,128]{1,0:T(8,128)(2,1)S(1)} %get-tuple-element.36), channel_id=1, source_target_pairs={{0,16},{8,24},{16,0},{24,8},{1,17},{9,25},{17,1},{25,9},{2,18},{10... | collective-permute-start | bytes 196616 | tf_op jit(solution)/shard_map/ppermute | solution.py:17
  17.8 7.2 %copy-start = (bf16[1024,128]{1,0:T(8,128)(2,1)S(1)}, bf16[1024,128]{1,0:T(8,128)(2,1)}, u32[]{:S(2)}) copy-start(bf16[1024,128]{1,0:T(8,128)(2,1)} %cotangent_ref.7) | copy-start | bytes 786436
  19.8 5.2 %copy-start.1 = (bf16[128,128]{1,0:T(8,128)(2,1)S(1)}, bf16[128,128]{1,0:T(8,128)(2,1)}, u32[]{:S(2)}) copy-start(bf16[128,128]{1,0:T(8,128)(2,1)} %weight_ref.7) | copy-start | bytes 98308
  20.5 6.3 %collective-permute-start.9 = (bf16[256,128]{1,0:T(8,128)(2,1)S(1)}, bf16[256,128]{1,0:T(8,128)(2,1)S(1)}, u32[]{:S(2)}, u32[]{:S(2)}) collective-permute-start(bf16[256,128]{1,0:T(8,128)(2,1)S(1)} %shard_map.93.refs_0_), channel_id=1, source_target_pairs={{0,24},{8,16},{16,8},{24,0},{1,25},{9,17},{17,9},{25,1},{2,26},{10... | collective-permute-start | bytes 196616 | tf_op jit(solution)/shard_map/ppermute | solution.py:17
  22.8 5.0 %collective-permute-start.10 = (bf16[256,128]{1,0:T(8,128)(2,1)S(1)}, bf16[256,128]{1,0:T(8,128)(2,1)S(1)}, u32[]{:S(2)}, u32[]{:S(2)}) collective-permute-start(bf16[256,128]{1,0:T(8,128)(2,1)S(1)} %shard_map.93.refs_0_), channel_id=1, source_target_pairs={{0,8},{8,0},{16,24},{24,16},{1,9},{9,1},{17,25},{25,17},{2,10},{10... | collective-permute-start | bytes 196616 | tf_op jit(solution)/shard_map/ppermute | solution.py:17
  23.2 5.3 %collective-permute-start.11 = (bf16[256,128]{1,0:T(8,128)(2,1)S(1)}, bf16[256,128]{1,0:T(8,128)(2,1)S(1)}, u32[]{:S(2)}, u32[]{:S(2)}) collective-permute-start(bf16[256,128]{1,0:T(8,128)(2,1)S(1)} %shard_map.93.refs_0_), channel_id=1, source_target_pairs={{0,16},{8,24},{16,0},{24,8},{1,17},{9,25},{17,1},{25,9},{2,18},{10... | collective-permute-start | bytes 196616 | tf_op jit(solution)/shard_map/ppermute | solution.py:17
  25.0 0.7 %copy-start.4 = (f32[128]{0:T(128)S(1)}, f32[128]{0:T(128)}, u32[]{:S(2)}) copy-start(f32[128]{0:T(128)} %param.10) | copy-start | bytes 1540
  29.1 6.3 %collective-permute-start.14 = (bf16[640,128]{1,0:T(8,128)(2,1)S(1)}, bf16[640,128]{1,0:T(8,128)(2,1)S(1)}, u32[]{:S(2)}, u32[]{:S(2)}) collective-permute-start(bf16[640,128]{1,0:T(8,128)(2,1)S(1)} %get-tuple-element.51), channel_id=1, source_target_pairs={{0,6},{1,7},{2,4},{3,5},{4,2},{5,3},{6,0},{7,1},{8,14},{9,15},{10,... | collective-permute-start | bytes 491528 | tf_op jit(solution)/shard_map/ppermute | solution.py:17
  30.6 1.5 %collective-permute-start.13 = (bf16[512,128]{1,0:T(8,128)(2,1)S(1)}, bf16[512,128]{1,0:T(8,128)(2,1)S(1)}, u32[]{:S(2)}, u32[]{:S(2)}) collective-permute-start(bf16[512,128]{1,0:T(8,128)(2,1)S(1)} %get-tuple-element.49), channel_id=1, source_target_pairs={{0,1},{1,0},{2,3},{3,2},{4,5},{5,4},{6,7},{7,6},{8,9},{9,8},{10,11... | collective-permute-start | bytes 393224 | tf_op jit(solution)/shard_map/ppermute | solution.py:17
  30.6 1.5 %collective-permute-start.12 = (bf16[384,128]{1,0:T(8,128)(2,1)S(1)}, bf16[384,128]{1,0:T(8,128)(2,1)S(1)}, u32[]{:S(2)}, u32[]{:S(2)}) collective-permute-start(bf16[384,128]{1,0:T(8,128)(2,1)S(1)} %get-tuple-element.48.sent_ref), channel_id=1, source_target_pairs={{0,1},{1,0},{2,3},{3,2},{4,5},{5,4},{6,7},{7,6},{8,9},{9,8},{10,11... | collective-permute-start | bytes 294920 | tf_op jit(solution)/shard_map/ppermute | solution.py:17
  32.2 5.0 %collective-permute-start.15 = (bf16[384,128]{1,0:T(8,128)(2,1)S(1)}, bf16[384,128]{1,0:T(8,128)(2,1)S(1)}, u32[]{:S(2)}, u32[]{:S(2)}) collective-permute-start(bf16[384,128]{1,0:T(8,128)(2,1)S(1)} %get-tuple-element.52), channel_id=1, source_target_pairs={{0,5},{1,4},{2,7},{3,6},{4,1},{5,0},{6,3},{7,2},{8,13},{9,12},{10,... | collective-permute-start | bytes 294920 | tf_op jit(solution)/shard_map/ppermute | solution.py:17
  33.7 4.8 %collective-permute-start.16 = (bf16[384,128]{1,0:T(8,128)(2,1)S(1)}, bf16[384,128]{1,0:T(8,128)(2,1)S(1)}, u32[]{:S(2)}, u32[]{:S(2)}) collective-permute-start(bf16[384,128]{1,0:T(8,128)(2,1)S(1)} %get-tuple-element.53), channel_id=1, source_target_pairs={{0,3},{1,2},{2,1},{3,0},{4,7},{5,6},{6,5},{7,4},{8,11},{9,10},{10,... | collective-permute-start | bytes 294920 | tf_op jit(solution)/shard_map/ppermute | solution.py:17
  35.4 3.2 %collective-permute-start.17 = (bf16[384,128]{1,0:T(8,128)(2,1)S(1)}, bf16[384,128]{1,0:T(8,128)(2,1)S(1)}, u32[]{:S(2)}, u32[]{:S(2)}) collective-permute-start(bf16[384,128]{1,0:T(8,128)(2,1)S(1)} %shard_map.101), channel_id=1, source_target_pairs={{0,1},{1,0},{2,3},{3,2},{4,5},{5,4},{6,7},{7,6},{8,9},{9,8},{10,11... | collective-permute-start | bytes 294920 | tf_op jit(solution)/shard_map/ppermute | solution.py:17

commit v22 on v21

--- a/solution.py
+++ b/solution.py
@@ -15,6 +15,11 @@
 def swap(value, axis, distance):
     size = lax.axis_size(axis)
     return lax.ppermute(value, axis, [(i, i ^ distance) for i in range(size)])
+
+
+def swap_some(value, distance, core):
+    pairs = [(i, i ^ distance) for i in range(lax.axis_size("dom")) if i % 2 == core]
+    return lax.ppermute(value, "dom", pairs)
 
 
 def matmul(a, b, contract):
@@ -158,8 +163,14 @@
     outs[-1][...] = weight
 
 
-def pass_kernel(got_ref, out_ref):
-    out_ref[...] = got_ref[got_ref.shape[0] - out_ref.shape[0] :]
+def copy_kernel(value_ref, out_ref):
+    out_ref[...] = value_ref[...]
+
+
+def pass_kernel(odd_ref, even_ref, across_ref, out_ref):
+    across = odd_ref[...] + even_ref[...]
+    across_ref[...] = across
+    out_ref[...] = across[across.shape[0] - out_ref.shape[0] :]
 
 
 def total_of(values):
@@ -277,14 +288,16 @@
 
     last = chips - 1
     message = shape((nodes + width, width), BF16)
-    got_across = swap(across, "dom", 2 * last)
+    odd, even = (swap_some(across, 2 * last, core) for core in (1, 0))
     own, *sends, pair_weight = call(
         pair_kernel,
         [shape((nodes, width), F32)] + [message] * (last - 1) + [shape((width, width), BF16)],
         [VMEM] * 4,
     )(contrib, beside, swap(beside, "dom", 1), swap(others, "dom", 1))
     got = {chip: swap(sends[chip - 1], "dom", 2 * chip + 1) for chip in range(last - 1, 0, -1)}
-    passed = swap(call(pass_kernel, message, [VMEM])(got_across), "dom", 1)
+    odd = call(copy_kernel, shape(odd.shape, BF16), [VMEM], cost=10**9)(odd)
+    got_across, passed = call(pass_kernel, [shape(odd.shape, BF16), message], [VMEM] * 2)(odd, even)
+    passed = swap(passed, "dom", 1)
     output = call(
         functools.partial(order_kernel, list(pieces)), shape((rows * size, width), BF16), [VMEM] * rep
     )(*outputs)

time: 39.5 us -> 42.4 us (1.073)
  starting transfers between devices: 18 us -> 21.5 us
  waiting for transfers between devices: 13.4 us -> 12.8 us
    ppermute x0 -> x2, starting transfers between devices: none -> 4.01 us  [swap_some(): return lax.ppermute(value, 'dom', pairs)]
    ppermute x18 -> x17, waiting for transfers between devices: 13.4 us -> 9.44 us  [swap(): return lax.ppermute(value, axis, [(i, i ^ distance) for i in range(size)])]
    ppermute x0 -> x2, waiting for transfers between devices: none -> 3.33 us  [swap_some(): return lax.ppermute(value, 'dom', pairs)]
    ppermute x18 -> x17, starting transfers between devices: 18 us -> 17.4 us  [swap(): return lax.ppermute(value, axis, [(i, i ^ distance) for i in range(size)])]
  transfers between devices with their start and end apart: 18 -> 19, of which waited for: 14 -> 12; matrix products, arithmetic and copies ran while one was open for 0% -> 0% of each run, Pallas kernels for 7% -> 7%
where the time goes in v22:
time: 42.4 us; the launch traced here: 42.1 us
  starting transfers between devices  21.5 us (51%)
  waiting for transfers between devices  12.8 us (30%)
  Pallas kernels  4.49 us (11%)
  local copies, waits for them, and re-layouts  2.55 us (6%)
  between operations  0.84 us (2%)
    ppermute x17, starting transfers between devices, swap(): return lax.ppermute(value, axis, [(i, i ^ distance) for i in range(size)])  17.4 us
    ppermute x17, waiting for transfers between devices, swap(): return lax.ppermute(value, axis, [(i, i ^ distance) for i in range(size)])  9.44 us
    ppermute x2, starting transfers between devices, swap_some(): return lax.ppermute(value, 'dom', pairs)  4.01 us
    ppermute x2, waiting for transfers between devices, swap_some(): return lax.ppermute(value, 'dom', pairs)  3.33 us
    unnamed x12, local copies, waits for them, and re-layouts  2.55 us
    pallas_call x4, Pallas kernels, body(): call(functools.partial(layer_kernel, rep, count, own_blocks, j), outs, [V...  2.11 us
  transfers between devices with their start and end apart: 19, of which 12 were waited for; matrix products, arithmetic and copies ran while one was open for 0% of the time, Pallas kernels for 7%

profile of v22, /device:TPU:0, one launch (start us, length us, event | category | flops | bytes accessed | tf_op | source)
XLA Modules:
  0.0 42.1 jit_solution(891644815093713459)
XLA Ops:
  0.6 3.4 %collective-permute-start = (bf16[256,128]{1,0:T(8,128)(2,1)}, bf16[256,128]{1,0:T(8,128)(2,1)S(1)}, u32[]{:S(2)}, u32[]{:S(2)}) collective-permute-start(bf16[256,128]{1,0:T(8,128)(2,1)} %features_ref.1), channel_id=1, source_target_pairs={{0,7},{1,6},{2,5},{3,4},{4,3},{5,2},{6,1},{7,0},{8,15},{9,14},{10,... | collective-permute-start | bytes 196616 | tf_op jit(solution)/shard_map/ppermute | solution.py:17
  4.0 0.8 %collective-permute-start.2 = (bf16[256,128]{1,0:T(8,128)(2,1)}, bf16[256,128]{1,0:T(8,128)(2,1)S(1)}, u32[]{:S(2)}, u32[]{:S(2)}) collective-permute-start(bf16[256,128]{1,0:T(8,128)(2,1)} %features_ref.1), channel_id=1, source_target_pairs={{0,5},{1,4},{2,7},{3,6},{4,1},{5,0},{6,3},{7,2},{8,13},{9,12},{10,... | collective-permute-start | bytes 196616 | tf_op jit(solution)/shard_map/ppermute | solution.py:17
  5.0 1.0 %copy-done.2 = bf16[8,2,128,128]{3,2,1,0:T(8,128)(2,1)S(1)} copy-done((bf16[8,2,128,128]{3,2,1,0:T(8,128)(2,1)S(1)}, bf16[8,2,128,128]{3,2,1,0:T(8,128)(2,1)}, u32[]{:S(2)}) %copy-start.2) | copy-done | bytes 524312
  6.0 0.8 %copy-done.3 = bf16[256,128]{1,0:T(8,128)(2,1)S(1)} copy-done((bf16[256,128]{1,0:T(8,128)(2,1)S(1)}, bf16[256,128]{1,0:T(8,128)(2,1)}, u32[]{:S(2)}) %copy-start.3) | copy-done | bytes 65560
  7.2 1.0 %collective-permute-done.2.refs_1_ = bf16[256,128]{1,0:T(8,128)(2,1)S(1)} collective-permute-done((bf16[256,128]{1,0:T(8,128)(2,1)}, bf16[256,128]{1,0:T(8,128)(2,1)S(1)}, u32[]{:S(2)}, u32[]{:S(2)}) %collective-permute-start.2) | collective-permute-done | bytes 65568 | tf_op jit(solution)/shard_map/ppermute | solution.py:17
  8.2 0.7 %collective-permute-start.5 = (bf16[256,128]{1,0:T(8,128)(2,1)S(1)}, bf16[256,128]{1,0:T(8,128)(2,1)S(1)}, u32[]{:S(2)}, u32[]{:S(2)}) collective-permute-start(bf16[256,128]{1,0:T(8,128)(2,1)S(1)} %collective-permute-done.2.refs_1_), channel_id=1, source_target_pairs={{0,1},{1,0},{2,3},{3,2},{4,5},{5,4},{6,7},{7,6},{8,9},{9,8},{10,11... | collective-permute-start | bytes 196616 | tf_op jit(solution)/shard_map/ppermute | solution.py:17
  9.8 0.8 %collective-permute-done.4.refs_0_ = bf16[256,128]{1,0:T(8,128)(2,1)S(1)} collective-permute-done((bf16[256,128]{1,0:T(8,128)(2,1)S(1)}, bf16[256,128]{1,0:T(8,128)(2,1)S(1)}, u32[]{:S(2)}, u32[]{:S(2)}) %collective-permute-start.4) | collective-permute-done | bytes 65568 | tf_op jit(solution)/shard_map/ppermute | solution.py:17
  11.0 3.7 %collective-permute-start.6 = (bf16[256,128]{1,0:T(8,128)(2,1)S(1)}, bf16[256,128]{1,0:T(8,128)(2,1)S(1)}, u32[]{:S(2)}, u32[]{:S(2)}) collective-permute-start(bf16[256,128]{1,0:T(8,128)(2,1)S(1)} %get-tuple-element.36), channel_id=1, source_target_pairs={{0,24},{8,16},{16,8},{24,0},{1,25},{9,17},{17,9},{25,1},{2,26},{10... | collective-permute-start | bytes 196616 | tf_op jit(solution)/shard_map/ppermute | solution.py:17
  14.7 0.8 %collective-permute-start.8 = (bf16[256,128]{1,0:T(8,128)(2,1)S(1)}, bf16[256,128]{1,0:T(8,128)(2,1)S(1)}, u32[]{:S(2)}, u32[]{:S(2)}) collective-permute-start(bf16[256,128]{1,0:T(8,128)(2,1)S(1)} %get-tuple-element.38), channel_id=1, source_target_pairs={{0,16},{8,24},{16,0},{24,8},{1,17},{9,25},{17,1},{25,9},{2,18},{10... | collective-permute-start | bytes 196616 | tf_op jit(solution)/shard_map/ppermute | solution.py:17
  15.4 2.3 %collective-permute-done.6.b_ref = bf16[256,128]{1,0:T(8,128)(2,1)S(1)} collective-permute-done((bf16[256,128]{1,0:T(8,128)(2,1)S(1)}, bf16[256,128]{1,0:T(8,128)(2,1)S(1)}, u32[]{:S(2)}, u32[]{:S(2)}) %collective-permute-start.6) | collective-permute-done | bytes 65568 | tf_op jit(solution)/shard_map/ppermute | solution.py:17
  17.8 1.9 %collective-permute-done.7.b_ref = bf16[256,128]{1,0:T(8,128)(2,1)S(1)} collective-permute-done((bf16[256,128]{1,0:T(8,128)(2,1)S(1)}, bf16[256,128]{1,0:T(8,128)(2,1)S(1)}, u32[]{:S(2)}, u32[]{:S(2)}) %collective-permute-start.7) | collective-permute-done | bytes 65568 | tf_op jit(solution)/shard_map/ppermute | solution.py:17
  19.8 0.7 %collective-permute-done.8.b_ref = bf16[256,128]{1,0:T(8,128)(2,1)S(1)} collective-permute-done((bf16[256,128]{1,0:T(8,128)(2,1)S(1)}, bf16[256,128]{1,0:T(8,128)(2,1)S(1)}, u32[]{:S(2)}, u32[]{:S(2)}) %collective-permute-start.8) | collective-permute-done | bytes 65568 | tf_op jit(solution)/shard_map/ppermute | solution.py:17
  20.5 2.3 %collective-permute-start.9 = (bf16[256,128]{1,0:T(8,128)(2,1)S(1)}, bf16[256,128]{1,0:T(8,128)(2,1)S(1)}, u32[]{:S(2)}, u32[]{:S(2)}) collective-permute-start(bf16[256,128]{1,0:T(8,128)(2,1)S(1)} %shard_map.93.refs_0_), channel_id=1, source_target_pairs={{0,24},{8,16},{16,8},{24,0},{1,25},{9,17},{17,9},{25,1},{2,26},{10... | collective-permute-start | bytes 196616 | tf_op jit(solution)/shard_map/ppermute | solution.py:17
  23.2 1.8 %collective-permute-start.11 = (bf16[256,128]{1,0:T(8,128)(2,1)S(1)}, bf16[256,128]{1,0:T(8,128)(2,1)S(1)}, u32[]{:S(2)}, u32[]{:S(2)}) collective-permute-start(bf16[256,128]{1,0:T(8,128)(2,1)S(1)} %shard_map.93.refs_0_), channel_id=1, source_target_pairs={{0,16},{8,24},{16,0},{24,8},{1,17},{9,25},{17,1},{25,9},{2,18},{10... | collective-permute-start | bytes 196616 | tf_op jit(solution)/shard_map/ppermute | solution.py:17
  25.0 0.6 %copy-done.4 = f32[128]{0:T(128)S(1)} copy-done((f32[128]{0:T(128)S(1)}, f32[128]{0:T(128)}, u32[]{:S(2)}) %copy-start.4) | copy-done | bytes 536
  26.2 0.7 %collective-permute-done.9.refs_0_ = bf16[256,128]{1,0:T(8,128)(2,1)S(1)} collective-permute-done((bf16[256,128]{1,0:T(8,128)(2,1)S(1)}, bf16[256,128]{1,0:T(8,128)(2,1)S(1)}, u32[]{:S(2)}, u32[]{:S(2)}) %collective-permute-start.9) | collective-permute-done | bytes 65568 | tf_op jit(solution)/shard_map/ppermute | solution.py:17
  29.1 0.7 %collective-permute-start.14 = (bf16[640,128]{1,0:T(8,128)(2,1)S(1)}, bf16[640,128]{1,0:T(8,128)(2,1)S(1)}, u32[]{:S(2)}, u32[]{:S(2)}) collective-permute-start(bf16[640,128]{1,0:T(8,128)(2,1)S(1)} %get-tuple-element.53), channel_id=1, source_target_pairs={{1,7},{3,5},{5,3},{7,1},{9,15},{11,13},{13,11},{15,9},{17,23},{19,... | collective-permute-start | bytes 491528 | tf_op jit(solution)/shard_map/ppermute | solution.py:22
  29.7 1.3 %collective-permute-start.13 = (bf16[512,128]{1,0:T(8,128)(2,1)S(1)}, bf16[512,128]{1,0:T(8,128)(2,1)S(1)}, u32[]{:S(2)}, u32[]{:S(2)}) collective-permute-start(bf16[512,128]{1,0:T(8,128)(2,1)S(1)} %get-tuple-element.51), channel_id=1, source_target_pairs={{0,1},{1,0},{2,3},{3,2},{4,5},{5,4},{6,7},{7,6},{8,9},{9,8},{10,11... | collective-permute-start | bytes 393224 | tf_op jit(solution)/shard_map/ppermute | solution.py:17
  31.2 3.3 %collective-permute-start.15 = (bf16[640,128]{1,0:T(8,128)(2,1)S(1)}, bf16[640,128]{1,0:T(8,128)(2,1)S(1)}, u32[]{:S(2)}, u32[]{:S(2)}) collective-permute-start(bf16[640,128]{1,0:T(8,128)(2,1)S(1)} %get-tuple-element.53), channel_id=1, source_target_pairs={{0,6},{2,4},{4,2},{6,0},{8,14},{10,12},{12,10},{14,8},{16,22},{18,... | collective-permute-start | bytes 491528 | tf_op jit(solution)/shard_map/ppermute | solution.py:22
  34.7 1.8 %collective-permute-start.17 = (bf16[384,128]{1,0:T(8,128)(2,1)S(1)}, bf16[384,128]{1,0:T(8,128)(2,1)S(1)}, u32[]{:S(2)}, u32[]{:S(2)}) collective-permute-start(bf16[384,128]{1,0:T(8,128)(2,1)S(1)} %get-tuple-element.56), channel_id=1, source_target_pairs={{0,3},{1,2},{2,1},{3,0},{4,7},{5,6},{6,5},{7,4},{8,11},{9,10},{10,... | collective-permute-start | bytes 294920 | tf_op jit(solution)/shard_map/ppermute | solution.py:17
  36.4 3.3 %collective-permute-done.15.even_ref = bf16[640,128]{1,0:T(8,128)(2,1)S(1)} collective-permute-done((bf16[640,128]{1,0:T(8,128)(2,1)S(1)}, bf16[640,128]{1,0:T(8,128)(2,1)S(1)}, u32[]{:S(2)}, u32[]{:S(2)}) %collective-permute-start.15) | collective-permute-done | bytes 163872 | tf_op jit(solution)/shard_map/ppermute | solution.py:22
  39.9 0.7 %shard_map.98 = bf16[1024,128]{1,0:T(8,128)(2,1)} custom-call(bf16[256,128]{1,0:T(8,128)(2,1)S(1)} %get-tuple-element.39.refs_0_, bf16[256,128]{1,0:T(8,128)(2,1)S(1)} %get-tuple-element.42.refs_1_, bf16[256,128]{1,0:T(8,128)(2,1)S(1)} %get-tuple-element.45.refs_2_, bf16[256,128]{1,0:T(8,128)(2,1)S(1)} %get-tuple-element.48.refs_3_), custom_call_target="tpu_custom_call" | custom-call | tf_op jit(solution)/shard_map/pallas_call | solution.py:301
  40.6 0.7 %collective-permute-done.16.refs_0_.refs_1_ = bf16[384,128]{1,0:T(8,128)(2,1)S(1)} collective-permute-done((bf16[384,128]{1,0:T(8,128)(2,1)S(1)}, bf16[384,128]{1,0:T(8,128)(2,1)S(1)}, u32[]{:S(2)}, u32[]{:S(2)}) %collective-permute-start.16) | collective-permute-done | bytes 98336 | tf_op jit(solution)/shard_map/ppermute | solution.py:17
  41.4 0.7 %shard_map.103 = (f32[256,128]{1,0:T(8,128)}, f32[128,128]{1,0:T(8,128)}) custom-call(f32[256,128]{1,0:T(8,128)S(1)} %shard_map.102.early_ref, bf16[128,128]{1,0:T(8,128)(2,1)S(1)} %get-tuple-element.57.weight_ref, bf16[640,128]{1,0:T(8,128)(2,1)S(1)} %get-tuple-element.54.across_ref, bf16[384,128]{1,0:T(8,128)(2,1)S(1)} %collective-permute-done.18.passed_ref, ...), custom_call_target="tpu_custom_call" | custom-call | tf_op jit(solution)/shard_map/pallas_call | solution.py:307
  (45 shorter events, 5.1 us)
Async XLA Ops:
  0.6 6.4 %collective-permute-start = (bf16[256,128]{1,0:T(8,128)(2,1)}, bf16[256,128]{1,0:T(8,128)(2,1)S(1)}, u32[]{:S(2)}, u32[]{:S(2)}) collective-permute-start(bf16[256,128]{1,0:T(8,128)(2,1)} %features_ref.1), channel_id=1, source_target_pairs={{0,7},{1,6},{2,5},{3,4},{4,3},{5,2},{6,1},{7,0},{8,15},{9,14},{10,... | collective-permute-start | bytes 196616 | tf_op jit(solution)/shard_map/ppermute | solution.py:17
  4.0 4.2 %collective-permute-start.2 = (bf16[256,128]{1,0:T(8,128)(2,1)}, bf16[256,128]{1,0:T(8,128)(2,1)S(1)}, u32[]{:S(2)}, u32[]{:S(2)}) collective-permute-start(bf16[256,128]{1,0:T(8,128)(2,1)} %features_ref.1), channel_id=1, source_target_pairs={{0,5},{1,4},{2,7},{3,6},{4,1},{5,0},{6,3},{7,2},{8,13},{9,12},{10,... | collective-permute-start | bytes 196616 | tf_op jit(solution)/shard_map/ppermute | solution.py:17
  4.8 4.5 %collective-permute-start.1 = (bf16[256,128]{1,0:T(8,128)(2,1)}, bf16[256,128]{1,0:T(8,128)(2,1)S(1)}, u32[]{:S(2)}, u32[]{:S(2)}) collective-permute-start(bf16[256,128]{1,0:T(8,128)(2,1)} %features_ref.1), channel_id=1, source_target_pairs={{0,3},{1,2},{2,1},{3,0},{4,7},{5,6},{6,5},{7,4},{8,11},{9,10},{10,... | collective-permute-start | bytes 196616 | tf_op jit(solution)/shard_map/ppermute | solution.py:17
  5.0 1.0 %copy-start.2 = (bf16[8,2,128,128]{3,2,1,0:T(8,128)(2,1)S(1)}, bf16[8,2,128,128]{3,2,1,0:T(8,128)(2,1)}, u32[]{:S(2)}) copy-start(bf16[8,2,128,128]{3,2,1,0:T(8,128)(2,1)} %vals_ref.1) | copy-start | bytes 1572868
  6.0 0.8 %copy-start.3 = (bf16[256,128]{1,0:T(8,128)(2,1)S(1)}, bf16[256,128]{1,0:T(8,128)(2,1)}, u32[]{:S(2)}) copy-start(bf16[256,128]{1,0:T(8,128)(2,1)} %features_ref.1) | copy-start | bytes 196612
  7.1 2.4 %copy-start.5 = (s32[8,2]{0,1:T(2,128)S(1)}, s32[8,2]{0,1:T(2,128)}, u32[]{:S(2)}) copy-start(s32[8,2]{0,1:T(2,128)} %param.6) | copy-start | bytes 196
  7.1 3.5 %collective-permute-start.3 = (bf16[512,128]{1,0:T(8,128)(2,1)S(1)}, bf16[512,128]{1,0:T(8,128)(2,1)S(1)}, u32[]{:S(2)}, u32[]{:S(2)}) collective-permute-start(bf16[512,128]{1,0:T(8,128)(2,1)S(1)} %shard_map.86._.ends_ref), channel_id=1, source_target_pairs={{0,1},{1,0},{2,3},{3,2},{4,5},{5,4},{6,7},{7,6},{8,9},{9,8},{10,11... | collective-permute-start | bytes 393224 | tf_op jit(solution)/shard_map/ppermute | solution.py:17
  8.2 1.6 %collective-permute-start.5 = (bf16[256,128]{1,0:T(8,128)(2,1)S(1)}, bf16[256,128]{1,0:T(8,128)(2,1)S(1)}, u32[]{:S(2)}, u32[]{:S(2)}) collective-permute-start(bf16[256,128]{1,0:T(8,128)(2,1)S(1)} %collective-permute-done.2.refs_1_), channel_id=1, source_target_pairs={{0,1},{1,0},{2,3},{3,2},{4,5},{5,4},{6,7},{7,6},{8,9},{9,8},{10,11... | collective-permute-start | bytes 196616 | tf_op jit(solution)/shard_map/ppermute | solution.py:17
  9.3 1.3 %collective-permute-start.4 = (bf16[256,128]{1,0:T(8,128)(2,1)S(1)}, bf16[256,128]{1,0:T(8,128)(2,1)S(1)}, u32[]{:S(2)}, u32[]{:S(2)}) collective-permute-start(bf16[256,128]{1,0:T(8,128)(2,1)S(1)} %collective-permute-done.1.refs_0_), channel_id=1, source_target_pairs={{0,1},{1,0},{2,3},{3,2},{4,5},{5,4},{6,7},{7,6},{8,9},{9,8},{10,11... | collective-permute-start | bytes 196616 | tf_op jit(solution)/shard_map/ppermute | solution.py:17
  11.0 6.8 %collective-permute-start.6 = (bf16[256,128]{1,0:T(8,128)(2,1)S(1)}, bf16[256,128]{1,0:T(8,128)(2,1)S(1)}, u32[]{:S(2)}, u32[]{:S(2)}) collective-permute-start(bf16[256,128]{1,0:T(8,128)(2,1)S(1)} %get-tuple-element.36), channel_id=1, source_target_pairs={{0,24},{8,16},{16,8},{24,0},{1,25},{9,17},{17,9},{25,1},{2,26},{10... | collective-permute-start | bytes 196616 | tf_op jit(solution)/shard_map/ppermute | solution.py:17
  14.7 5.1 %collective-permute-start.7 = (bf16[256,128]{1,0:T(8,128)(2,1)S(1)}, bf16[256,128]{1,0:T(8,128)(2,1)S(1)}, u32[]{:S(2)}, u32[]{:S(2)}) collective-permute-start(bf16[256,128]{1,0:T(8,128)(2,1)S(1)} %get-tuple-element.37), channel_id=1, source_target_pairs={{0,8},{8,0},{16,24},{24,16},{1,9},{9,1},{17,25},{25,17},{2,10},{10... | collective-permute-start | bytes 196616 | tf_op jit(solution)/shard_map/ppermute | solution.py:17
  14.7 5.9 %collective-permute-start.8 = (bf16[256,128]{1,0:T(8,128)(2,1)S(1)}, bf16[256,128]{1,0:T(8,128)(2,1)S(1)}, u32[]{:S(2)}, u32[]{:S(2)}) collective-permute-start(bf16[256,128]{1,0:T(8,128)(2,1)S(1)} %get-tuple-element.38), channel_id=1, source_target_pairs={{0,16},{8,24},{16,0},{24,8},{1,17},{9,25},{17,1},{25,9},{2,18},{10... | collective-permute-start | bytes 196616 | tf_op jit(solution)/shard_map/ppermute | solution.py:17
  17.8 7.2 %copy-start = (bf16[1024,128]{1,0:T(8,128)(2,1)S(1)}, bf16[1024,128]{1,0:T(8,128)(2,1)}, u32[]{:S(2)}) copy-start(bf16[1024,128]{1,0:T(8,128)(2,1)} %cotangent_ref.7) | copy-start | bytes 786436
  19.8 5.2 %copy-start.1 = (bf16[128,128]{1,0:T(8,128)(2,1)S(1)}, bf16[128,128]{1,0:T(8,128)(2,1)}, u32[]{:S(2)}) copy-start(bf16[128,128]{1,0:T(8,128)(2,1)} %weight_ref.7) | copy-start | bytes 98308
  20.5 6.3 %collective-permute-start.9 = (bf16[256,128]{1,0:T(8,128)(2,1)S(1)}, bf16[256,128]{1,0:T(8,128)(2,1)S(1)}, u32[]{:S(2)}, u32[]{:S(2)}) collective-permute-start(bf16[256,128]{1,0:T(8,128)(2,1)S(1)} %shard_map.93.refs_0_), channel_id=1, source_target_pairs={{0,24},{8,16},{16,8},{24,0},{1,25},{9,17},{17,9},{25,1},{2,26},{10... | collective-permute-start | bytes 196616 | tf_op jit(solution)/shard_map/ppermute | solution.py:17
  22.8 5.0 %collective-permute-start.10 = (bf16[256,128]{1,0:T(8,128)(2,1)S(1)}, bf16[256,128]{1,0:T(8,128)(2,1)S(1)}, u32[]{:S(2)}, u32[]{:S(2)}) collective-permute-start(bf16[256,128]{1,0:T(8,128)(2,1)S(1)} %shard_map.93.refs_0_), channel_id=1, source_target_pairs={{0,8},{8,0},{16,24},{24,16},{1,9},{9,1},{17,25},{25,17},{2,10},{10... | collective-permute-start | bytes 196616 | tf_op jit(solution)/shard_map/ppermute | solution.py:17
  23.2 5.3 %collective-permute-start.11 = (bf16[256,128]{1,0:T(8,128)(2,1)S(1)}, bf16[256,128]{1,0:T(8,128)(2,1)S(1)}, u32[]{:S(2)}, u32[]{:S(2)}) collective-permute-start(bf16[256,128]{1,0:T(8,128)(2,1)S(1)} %shard_map.93.refs_0_), channel_id=1, source_target_pairs={{0,16},{8,24},{16,0},{24,8},{1,17},{9,25},{17,1},{25,9},{2,18},{10... | collective-permute-start | bytes 196616 | tf_op jit(solution)/shard_map/ppermute | solution.py:17
  29.1 7.4 %collective-permute-start.14 = (bf16[640,128]{1,0:T(8,128)(2,1)S(1)}, bf16[640,128]{1,0:T(8,128)(2,1)S(1)}, u32[]{:S(2)}, u32[]{:S(2)}) collective-permute-start(bf16[640,128]{1,0:T(8,128)(2,1)S(1)} %get-tuple-element.53), channel_id=1, source_target_pairs={{1,7},{3,5},{5,3},{7,1},{9,15},{11,13},{13,11},{15,9},{17,23},{19,... | collective-permute-start | bytes 491528 | tf_op jit(solution)/shard_map/ppermute | solution.py:22
  29.7 4.8 %collective-permute-start.13 = (bf16[512,128]{1,0:T(8,128)(2,1)S(1)}, bf16[512,128]{1,0:T(8,128)(2,1)S(1)}, u32[]{:S(2)}, u32[]{:S(2)}) collective-permute-start(bf16[512,128]{1,0:T(8,128)(2,1)S(1)} %get-tuple-element.51), channel_id=1, source_target_pairs={{0,1},{1,0},{2,3},{3,2},{4,5},{5,4},{6,7},{7,6},{8,9},{9,8},{10,11... | collective-permute-start | bytes 393224 | tf_op jit(solution)/shard_map/ppermute | solution.py:17
  31.1 3.4 %collective-permute-start.12 = (bf16[384,128]{1,0:T(8,128)(2,1)S(1)}, bf16[384,128]{1,0:T(8,128)(2,1)S(1)}, u32[]{:S(2)}, u32[]{:S(2)}) collective-permute-start(bf16[384,128]{1,0:T(8,128)(2,1)S(1)} %get-tuple-element.50.sent_ref), channel_id=1, source_target_pairs={{0,1},{1,0},{2,3},{3,2},{4,5},{5,4},{6,7},{7,6},{8,9},{9,8},{10,11... | collective-permute-start | bytes 294920 | tf_op jit(solution)/shard_map/ppermute | solution.py:17
  31.2 8.6 %collective-permute-start.15 = (bf16[640,128]{1,0:T(8,128)(2,1)S(1)}, bf16[640,128]{1,0:T(8,128)(2,1)S(1)}, u32[]{:S(2)}, u32[]{:S(2)}) collective-permute-start(bf16[640,128]{1,0:T(8,128)(2,1)S(1)} %get-tuple-element.53), channel_id=1, source_target_pairs={{0,6},{2,4},{4,2},{6,0},{8,14},{10,12},{12,10},{14,8},{16,22},{18,... | collective-permute-start | bytes 491528 | tf_op jit(solution)/shard_map/ppermute | solution.py:22
  34.6 6.8 %collective-permute-start.16 = (bf16[384,128]{1,0:T(8,128)(2,1)S(1)}, bf16[384,128]{1,0:T(8,128)(2,1)S(1)}, u32[]{:S(2)}, u32[]{:S(2)}) collective-permute-start(bf16[384,128]{1,0:T(8,128)(2,1)S(1)} %get-tuple-element.55), channel_id=1, source_target_pairs={{0,5},{1,4},{2,7},{3,6},{4,1},{5,0},{6,3},{7,2},{8,13},{9,12},{10,... | collective-permute-start | bytes 294920 | tf_op jit(solution)/shard_map/ppermute | solution.py:17
  34.7 6.7 %collective-permute-start.17 = (bf16[384,128]{1,0:T(8,128)(2,1)S(1)}, bf16[384,128]{1,0:T(8,128)(2,1)S(1)}, u32[]{:S(2)}, u32[]{:S(2)}) collective-permute-start(bf16[384,128]{1,0:T(8,128)(2,1)S(1)} %get-tuple-element.56), channel_id=1, source_target_pairs={{0,3},{1,2},{2,1},{3,0},{4,7},{5,6},{6,5},{7,4},{8,11},{9,10},{10,... | collective-permute-start | bytes 294920 | tf_op jit(solution)/shard_map/ppermute | solution.py:17
  39.8 1.6 %collective-permute-start.18 = (bf16[384,128]{1,0:T(8,128)(2,1)S(1)}, bf16[384,128]{1,0:T(8,128)(2,1)S(1)}, u32[]{:S(2)}, u32[]{:S(2)}) collective-permute-start(bf16[384,128]{1,0:T(8,128)(2,1)S(1)} %get-tuple-element.58), channel_id=1, source_target_pairs={{0,1},{1,0},{2,3},{3,2},{4,5},{5,4},{6,7},{7,6},{8,9},{9,8},{10,11... | collective-permute-start | bytes 294920 | tf_op jit(solution)/shard_map/ppermute | solution.py:17
  (1 other events, 0.7 us)

commit v23 on v21

--- a/solution.py
+++ b/solution.py
@@ -129,9 +129,9 @@
         across_ref[:nodes] = away[rest:]
         across_ref[nodes : 2 * nodes] = contrib[half - own_blocks : half].reshape(nodes, -1).astype(BF16)
         across_ref[2 * nodes :] = weight
-        beside_ref[:nodes] = away[:nodes]
+        beside_ref[:nodes] = away[rest - nodes : rest]
         beside_ref[nodes:] = weight
-        others_ref[...] = away[nodes:rest]
+        others_ref[...] = away[: rest - nodes]
 
 
 def add_kernel(a_ref, b_ref, out_ref):
@@ -146,16 +146,25 @@
         out_ref[pl.ds(pl.multiple_of(target * part, part), part), :] = piece[...]
 
 
-def pair_kernel(contrib_ref, sent_ref, got_ref, others_ref, own_ref, *outs):
+def first_pair_kernel(contrib_ref, sent_ref, got_ref, out_ref):
+    blocks, size, _ = contrib_ref.shape
+    nodes = out_ref.shape[0] - sent_ref.shape[1]
+    own_blocks = nodes // size
+    mine = contrib_ref[blocks // 2 - 2 * own_blocks : blocks // 2 - own_blocks].reshape(nodes, -1)
+    out_ref[:nodes] = (mine + got_ref[:nodes].astype(F32)).astype(BF16)
+    out_ref[nodes:] = (sent_ref[nodes:].astype(F32) + got_ref[nodes:].astype(F32)).astype(BF16)
+
+
+def rest_pair_kernel(contrib_ref, first_ref, got_ref, own_ref, *outs):
     size, nodes = contrib_ref.shape[1], own_ref.shape[0]
-    weight = (sent_ref[nodes:].astype(F32) + got_ref[nodes:].astype(F32)).astype(BF16)
-    own_ref[...] = contrib_ref[: nodes // size].reshape(nodes, -1) + got_ref[:nodes].astype(F32)
-    for chip in range(1, len(outs)):
+    for chip in range(len(outs) + 1):
         mine = contrib_ref[chip * nodes // size : (chip + 1) * nodes // size].reshape(nodes, -1)
-        total = mine + others_ref[(chip - 1) * nodes : chip * nodes].astype(F32)
-        outs[chip - 1][:nodes] = total.astype(BF16)
-        outs[chip - 1][nodes:] = weight
-    outs[-1][...] = weight
+        total = mine + got_ref[chip * nodes : (chip + 1) * nodes].astype(F32)
+        if chip == 0:
+            own_ref[...] = total
+        else:
+            outs[chip - 1][:nodes] = total.astype(BF16)
+            outs[chip - 1][nodes:] = first_ref[nodes:]
 
 
 def pass_kernel(got_ref, out_ref):
@@ -168,20 +177,14 @@
     return values[0]
 
 
-def early_sum_kernel(own_ref, across_ref, *refs):
-    got, out_ref = refs[:-1], refs[-1]
-    nodes = own_ref.shape[0]
-    total = own_ref[...] + across_ref[:nodes].astype(F32)
+def final_kernel(own_ref, sent_ref, across_ref, passed_ref, *refs):
+    got, (feature_ref, grad_ref) = refs[:-2], refs[-2:]
+    nodes = feature_ref.shape[0]
+    total = own_ref[...] + across_ref[:nodes].astype(F32) + passed_ref[:nodes].astype(F32)
     for g in got:
         total += g[:nodes].astype(F32)
-    out_ref[...] = total
-
-
-def final_kernel(early_ref, weight_ref, across_ref, passed_ref, *refs):
-    got, (feature_ref, grad_ref) = refs[:-2], refs[-2:]
-    nodes = feature_ref.shape[0]
-    feature_ref[...] = early_ref[...] + passed_ref[:nodes].astype(F32)
-    weights = [weight_ref[...].astype(F32)] + [g[nodes:].astype(F32) for g in got]
+    feature_ref[...] = total
+    weights = [sent_ref[nodes:].astype(F32)] + [g[nodes:].astype(F32) for g in got]
     across = across_ref[2 * nodes :].astype(F32) + passed_ref[nodes:].astype(F32)
     grad_ref[...] = total_of(weights + [across.astype(BF16).astype(F32)])
 
@@ -200,7 +203,7 @@
     part = rows * size // rep
     params = pltpu.CompilerParams(vmem_limit_bytes=(8 + dom // 2) * 1024 * 1024)
 
-    def call(kernel, out_shape, in_specs, aliases={}, cost=0):
+    def call(kernel, out_shape, in_specs, aliases={}):
         single = not isinstance(out_shape, list)
         return pl.pallas_call(
             kernel,
@@ -209,7 +212,7 @@
             out_specs=VMEM if single else [VMEM] * len(out_shape),
             input_output_aliases=aliases,
             compiler_params=params,
-            cost_estimate=pl.CostEstimate(flops=cost, bytes_accessed=0, transcendentals=0),
+            cost_estimate=pl.CostEstimate(flops=0, bytes_accessed=0, transcendentals=0),
         )
 
     flipped, own, vals = call(
@@ -278,24 +281,24 @@
     last = chips - 1
     message = shape((nodes + width, width), BF16)
     got_across = swap(across, "dom", 2 * last)
-    own, *sends, pair_weight = call(
-        pair_kernel,
-        [shape((nodes, width), F32)] + [message] * (last - 1) + [shape((width, width), BF16)],
-        [VMEM] * 4,
-    )(contrib, beside, swap(beside, "dom", 1), swap(others, "dom", 1))
+    got_beside, got_others = swap(beside, "dom", 1), swap(others, "dom", 1)
+    first = call(first_pair_kernel, message, [VMEM] * 3)(contrib, beside, got_beside)
+    own, *sends = call(
+        rest_pair_kernel,
+        [shape((nodes, width), F32)] + [message] * (last - 2),
+        [VMEM] * 3,
+    )(contrib, first, got_others)
+    sends.append(first)
     got = {chip: swap(sends[chip - 1], "dom", 2 * chip + 1) for chip in range(last - 1, 0, -1)}
     passed = swap(call(pass_kernel, message, [VMEM])(got_across), "dom", 1)
     output = call(
         functools.partial(order_kernel, list(pieces)), shape((rows * size, width), BF16), [VMEM] * rep
     )(*outputs)
-    early = call(early_sum_kernel, shape((nodes, width), F32), [VMEM] * chips)(
-        own, got_across, *[got[chip] for chip in range(last - 1, 0, -1)]
-    )
     feature_grad, weight_grad = call(
         final_kernel,
         [shape((nodes, width), F32), shape((width, width), F32)],
         [VMEM] * (chips + 2),
-    )(early, pair_weight, got_across, passed, *[got[chip] for chip in range(1, last)])
+    )(own, first, got_across, passed, *[got[chip] for chip in range(1, last)])
     return output, feature_grad, weight_grad
 
 

time: 39.5 us -> 39.5 us (level)
  no operation moved by 1% of the time
where the time goes in v23:
time: 39.5 us; the launch traced here: 39.3 us
  starting transfers between devices  18.1 us (46%)
  waiting for transfers between devices  13.4 us (34%)
  Pallas kernels  4.43 us (11%)
  local copies, waits for them, and re-layouts  2.55 us (6%)
  between operations  0.79 us (2%)
    ppermute x18, starting transfers between devices, swap(): return lax.ppermute(value, axis, [(i, i ^ distance) for i in range(size)])  18.1 us
    ppermute x18, waiting for transfers between devices, swap(): return lax.ppermute(value, axis, [(i, i ^ distance) for i in range(size)])  13.4 us
    unnamed x12, local copies, waits for them, and re-layouts  2.55 us
    pallas_call x4, Pallas kernels, body(): call(functools.partial(layer_kernel, rep, count, own_blocks, j), outs, [V...  2.11 us
  transfers between devices with their start and end apart: 18, of which 14 were waited for; matrix products, arithmetic and copies ran while one was open for 0% of the time, Pallas kernels for 7%

profile of v23, /device:TPU:0, one launch (start us, length us, event | category | flops | bytes accessed | tf_op | source)
XLA Modules:
  0.0 39.3 jit_solution(3643025633430935301)
XLA Ops:
  0.6 3.4 %collective-permute-start = (bf16[256,128]{1,0:T(8,128)(2,1)}, bf16[256,128]{1,0:T(8,128)(2,1)S(1)}, u32[]{:S(2)}, u32[]{:S(2)}) collective-permute-start(bf16[256,128]{1,0:T(8,128)(2,1)} %features_ref.1), channel_id=1, source_target_pairs={{0,7},{1,6},{2,5},{3,4},{4,3},{5,2},{6,1},{7,0},{8,15},{9,14},{10,... | collective-permute-start | bytes 196616 | tf_op jit(solution)/shard_map/ppermute | solution.py:17
  4.0 0.8 %collective-permute-start.2 = (bf16[256,128]{1,0:T(8,128)(2,1)}, bf16[256,128]{1,0:T(8,128)(2,1)S(1)}, u32[]{:S(2)}, u32[]{:S(2)}) collective-permute-start(bf16[256,128]{1,0:T(8,128)(2,1)} %features_ref.1), channel_id=1, source_target_pairs={{0,5},{1,4},{2,7},{3,6},{4,1},{5,0},{6,3},{7,2},{8,13},{9,12},{10,... | collective-permute-start | bytes 196616 | tf_op jit(solution)/shard_map/ppermute | solution.py:17
  5.0 1.0 %copy-done.2 = bf16[8,2,128,128]{3,2,1,0:T(8,128)(2,1)S(1)} copy-done((bf16[8,2,128,128]{3,2,1,0:T(8,128)(2,1)S(1)}, bf16[8,2,128,128]{3,2,1,0:T(8,128)(2,1)}, u32[]{:S(2)}) %copy-start.2) | copy-done | bytes 524312
  6.0 0.8 %copy-done.3 = bf16[256,128]{1,0:T(8,128)(2,1)S(1)} copy-done((bf16[256,128]{1,0:T(8,128)(2,1)S(1)}, bf16[256,128]{1,0:T(8,128)(2,1)}, u32[]{:S(2)}) %copy-start.3) | copy-done | bytes 65560
  7.2 1.0 %collective-permute-done.2.refs_1_ = bf16[256,128]{1,0:T(8,128)(2,1)S(1)} collective-permute-done((bf16[256,128]{1,0:T(8,128)(2,1)}, bf16[256,128]{1,0:T(8,128)(2,1)S(1)}, u32[]{:S(2)}, u32[]{:S(2)}) %collective-permute-start.2) | collective-permute-done | bytes 65568 | tf_op jit(solution)/shard_map/ppermute | solution.py:17
  8.2 0.7 %collective-permute-start.5 = (bf16[256,128]{1,0:T(8,128)(2,1)S(1)}, bf16[256,128]{1,0:T(8,128)(2,1)S(1)}, u32[]{:S(2)}, u32[]{:S(2)}) collective-permute-start(bf16[256,128]{1,0:T(8,128)(2,1)S(1)} %collective-permute-done.2.refs_1_), channel_id=1, source_target_pairs={{0,1},{1,0},{2,3},{3,2},{4,5},{5,4},{6,7},{7,6},{8,9},{9,8},{10,11... | collective-permute-start | bytes 196616 | tf_op jit(solution)/shard_map/ppermute | solution.py:17
  9.8 0.8 %collective-permute-done.4.refs_0_ = bf16[256,128]{1,0:T(8,128)(2,1)S(1)} collective-permute-done((bf16[256,128]{1,0:T(8,128)(2,1)S(1)}, bf16[256,128]{1,0:T(8,128)(2,1)S(1)}, u32[]{:S(2)}, u32[]{:S(2)}) %collective-permute-start.4) | collective-permute-done | bytes 65568 | tf_op jit(solution)/shard_map/ppermute | solution.py:17
  11.0 3.7 %collective-permute-start.6 = (bf16[256,128]{1,0:T(8,128)(2,1)S(1)}, bf16[256,128]{1,0:T(8,128)(2,1)S(1)}, u32[]{:S(2)}, u32[]{:S(2)}) collective-permute-start(bf16[256,128]{1,0:T(8,128)(2,1)S(1)} %get-tuple-element.32), channel_id=1, source_target_pairs={{0,24},{8,16},{16,8},{24,0},{1,25},{9,17},{17,9},{25,1},{2,26},{10... | collective-permute-start | bytes 196616 | tf_op jit(solution)/shard_map/ppermute | solution.py:17
  14.7 0.8 %collective-permute-start.8 = (bf16[256,128]{1,0:T(8,128)(2,1)S(1)}, bf16[256,128]{1,0:T(8,128)(2,1)S(1)}, u32[]{:S(2)}, u32[]{:S(2)}) collective-permute-start(bf16[256,128]{1,0:T(8,128)(2,1)S(1)} %get-tuple-element.34), channel_id=1, source_target_pairs={{0,16},{8,24},{16,0},{24,8},{1,17},{9,25},{17,1},{25,9},{2,18},{10... | collective-permute-start | bytes 196616 | tf_op jit(solution)/shard_map/ppermute | solution.py:17
  15.4 2.3 %collective-permute-done.6.b_ref = bf16[256,128]{1,0:T(8,128)(2,1)S(1)} collective-permute-done((bf16[256,128]{1,0:T(8,128)(2,1)S(1)}, bf16[256,128]{1,0:T(8,128)(2,1)S(1)}, u32[]{:S(2)}, u32[]{:S(2)}) %collective-permute-start.6) | collective-permute-done | bytes 65568 | tf_op jit(solution)/shard_map/ppermute | solution.py:17
  17.8 1.9 %collective-permute-done.7.b_ref = bf16[256,128]{1,0:T(8,128)(2,1)S(1)} collective-permute-done((bf16[256,128]{1,0:T(8,128)(2,1)S(1)}, bf16[256,128]{1,0:T(8,128)(2,1)S(1)}, u32[]{:S(2)}, u32[]{:S(2)}) %collective-permute-start.7) | collective-permute-done | bytes 65568 | tf_op jit(solution)/shard_map/ppermute | solution.py:17
  19.8 0.7 %collective-permute-done.8.b_ref = bf16[256,128]{1,0:T(8,128)(2,1)S(1)} collective-permute-done((bf16[256,128]{1,0:T(8,128)(2,1)S(1)}, bf16[256,128]{1,0:T(8,128)(2,1)S(1)}, u32[]{:S(2)}, u32[]{:S(2)}) %collective-permute-start.8) | collective-permute-done | bytes 65568 | tf_op jit(solution)/shard_map/ppermute | solution.py:17
  20.5 2.3 %collective-permute-start.9 = (bf16[256,128]{1,0:T(8,128)(2,1)S(1)}, bf16[256,128]{1,0:T(8,128)(2,1)S(1)}, u32[]{:S(2)}, u32[]{:S(2)}) collective-permute-start(bf16[256,128]{1,0:T(8,128)(2,1)S(1)} %shard_map.93.refs_0_), channel_id=1, source_target_pairs={{0,24},{8,16},{16,8},{24,0},{1,25},{9,17},{17,9},{25,1},{2,26},{10... | collective-permute-start | bytes 196616 | tf_op jit(solution)/shard_map/ppermute | solution.py:17
  23.2 1.8 %collective-permute-start.11 = (bf16[256,128]{1,0:T(8,128)(2,1)S(1)}, bf16[256,128]{1,0:T(8,128)(2,1)S(1)}, u32[]{:S(2)}, u32[]{:S(2)}) collective-permute-start(bf16[256,128]{1,0:T(8,128)(2,1)S(1)} %shard_map.93.refs_0_), channel_id=1, source_target_pairs={{0,16},{8,24},{16,0},{24,8},{1,17},{9,25},{17,1},{25,9},{2,18},{10... | collective-permute-start | bytes 196616 | tf_op jit(solution)/shard_map/ppermute | solution.py:17
  25.0 0.6 %copy-done.4 = f32[128]{0:T(128)S(1)} copy-done((f32[128]{0:T(128)S(1)}, f32[128]{0:T(128)}, u32[]{:S(2)}) %copy-start.4) | copy-done | bytes 536
  26.2 0.7 %collective-permute-done.9.refs_0_ = bf16[256,128]{1,0:T(8,128)(2,1)S(1)} collective-permute-done((bf16[256,128]{1,0:T(8,128)(2,1)S(1)}, bf16[256,128]{1,0:T(8,128)(2,1)S(1)}, u32[]{:S(2)}, u32[]{:S(2)}) %collective-permute-start.9) | collective-permute-done | bytes 65568 | tf_op jit(solution)/shard_map/ppermute | solution.py:17
  29.1 1.6 %collective-permute-start.14 = (bf16[640,128]{1,0:T(8,128)(2,1)S(1)}, bf16[640,128]{1,0:T(8,128)(2,1)S(1)}, u32[]{:S(2)}, u32[]{:S(2)}) collective-permute-start(bf16[640,128]{1,0:T(8,128)(2,1)S(1)} %get-tuple-element.49), channel_id=1, source_target_pairs={{0,6},{1,7},{2,4},{3,5},{4,2},{5,3},{6,0},{7,1},{8,14},{9,15},{10,... | collective-permute-start | bytes 491528 | tf_op jit(solution)/shard_map/ppermute | solution.py:17
  31.1 1.0 %collective-permute-done.12.got_ref = bf16[384,128]{1,0:T(8,128)(2,1)S(1)} collective-permute-done((bf16[384,128]{1,0:T(8,128)(2,1)S(1)}, bf16[384,128]{1,0:T(8,128)(2,1)S(1)}, u32[]{:S(2)}, u32[]{:S(2)}) %collective-permute-start.12) | collective-permute-done | bytes 98336 | tf_op jit(solution)/shard_map/ppermute | solution.py:17
  32.1 1.5 %collective-permute-start.17 = (bf16[384,128]{1,0:T(8,128)(2,1)S(1)}, bf16[384,128]{1,0:T(8,128)(2,1)S(1)}, u32[]{:S(2)}, u32[]{:S(2)}) collective-permute-start(bf16[384,128]{1,0:T(8,128)(2,1)S(1)} %shard_map.99.first_ref.sent_ref), channel_id=1, source_target_pairs={{0,5},{1,4},{2,7},{3,6},{4,1},{5,0},{6,3},{7,2},{8,13},{9,12},{10,... | collective-permute-start | bytes 294920 | tf_op jit(solution)/shard_map/ppermute | solution.py:17
  34.0 1.3 %collective-permute-done.14.got_ref.across_ref = bf16[640,128]{1,0:T(8,128)(2,1)S(1)} collective-permute-done((bf16[640,128]{1,0:T(8,128)(2,1)S(1)}, bf16[640,128]{1,0:T(8,128)(2,1)S(1)}, u32[]{:S(2)}, u32[]{:S(2)}) %collective-permute-start.14) | collective-permute-done | bytes 163872 | tf_op jit(solution)/shard_map/ppermute | solution.py:17
  35.4 0.7 %shard_map.98 = bf16[1024,128]{1,0:T(8,128)(2,1)} custom-call(bf16[256,128]{1,0:T(8,128)(2,1)S(1)} %get-tuple-element.35.refs_0_, bf16[256,128]{1,0:T(8,128)(2,1)S(1)} %get-tuple-element.38.refs_1_, bf16[256,128]{1,0:T(8,128)(2,1)S(1)} %get-tuple-element.41.refs_2_, bf16[256,128]{1,0:T(8,128)(2,1)S(1)} %get-tuple-element.44.refs_3_), custom_call_target="tpu_custom_call" | custom-call | tf_op jit(solution)/shard_map/pallas_call | solution.py:294
  36.2 0.9 %collective-permute-done.17.refs_1_ = bf16[384,128]{1,0:T(8,128)(2,1)S(1)} collective-permute-done((bf16[384,128]{1,0:T(8,128)(2,1)S(1)}, bf16[384,128]{1,0:T(8,128)(2,1)S(1)}, u32[]{:S(2)}, u32[]{:S(2)}) %collective-permute-start.17) | collective-permute-done | bytes 98336 | tf_op jit(solution)/shard_map/ppermute | solution.py:17
  37.1 1.5 %collective-permute-done.16.refs_0_ = bf16[384,128]{1,0:T(8,128)(2,1)S(1)} collective-permute-done((bf16[384,128]{1,0:T(8,128)(2,1)S(1)}, bf16[384,128]{1,0:T(8,128)(2,1)S(1)}, u32[]{:S(2)}, u32[]{:S(2)}) %collective-permute-start.16) | collective-permute-done | bytes 98336 | tf_op jit(solution)/shard_map/ppermute | solution.py:17
  38.6 0.7 %shard_map.102 = (f32[256,128]{1,0:T(8,128)}, f32[128,128]{1,0:T(8,128)}) custom-call(f32[256,128]{1,0:T(8,128)S(1)} %get-tuple-element.48.own_ref, bf16[384,128]{1,0:T(8,128)(2,1)S(1)} %shard_map.99.first_ref.sent_ref, bf16[640,128]{1,0:T(8,128)(2,1)S(1)} %collective-permute-done.14.got_ref.across_ref, ...), custom_call_target="tpu_custom_call" | custom-call | tf_op jit(solution)/shard_map/pallas_call | solution.py:297
  (42 shorter events, 5.7 us)
Async XLA Ops:
  0.6 6.4 %collective-permute-start = (bf16[256,128]{1,0:T(8,128)(2,1)}, bf16[256,128]{1,0:T(8,128)(2,1)S(1)}, u32[]{:S(2)}, u32[]{:S(2)}) collective-permute-start(bf16[256,128]{1,0:T(8,128)(2,1)} %features_ref.1), channel_id=1, source_target_pairs={{0,7},{1,6},{2,5},{3,4},{4,3},{5,2},{6,1},{7,0},{8,15},{9,14},{10,... | collective-permute-start | bytes 196616 | tf_op jit(solution)/shard_map/ppermute | solution.py:17
  4.0 4.2 %collective-permute-start.2 = (bf16[256,128]{1,0:T(8,128)(2,1)}, bf16[256,128]{1,0:T(8,128)(2,1)S(1)}, u32[]{:S(2)}, u32[]{:S(2)}) collective-permute-start(bf16[256,128]{1,0:T(8,128)(2,1)} %features_ref.1), channel_id=1, source_target_pairs={{0,5},{1,4},{2,7},{3,6},{4,1},{5,0},{6,3},{7,2},{8,13},{9,12},{10,... | collective-permute-start | bytes 196616 | tf_op jit(solution)/shard_map/ppermute | solution.py:17
  4.8 4.5 %collective-permute-start.1 = (bf16[256,128]{1,0:T(8,128)(2,1)}, bf16[256,128]{1,0:T(8,128)(2,1)S(1)}, u32[]{:S(2)}, u32[]{:S(2)}) collective-permute-start(bf16[256,128]{1,0:T(8,128)(2,1)} %features_ref.1), channel_id=1, source_target_pairs={{0,3},{1,2},{2,1},{3,0},{4,7},{5,6},{6,5},{7,4},{8,11},{9,10},{10,... | collective-permute-start | bytes 196616 | tf_op jit(solution)/shard_map/ppermute | solution.py:17
  5.0 1.0 %copy-start.2 = (bf16[8,2,128,128]{3,2,1,0:T(8,128)(2,1)S(1)}, bf16[8,2,128,128]{3,2,1,0:T(8,128)(2,1)}, u32[]{:S(2)}) copy-start(bf16[8,2,128,128]{3,2,1,0:T(8,128)(2,1)} %vals_ref.1) | copy-start | bytes 1572868
  6.0 0.8 %copy-start.3 = (bf16[256,128]{1,0:T(8,128)(2,1)S(1)}, bf16[256,128]{1,0:T(8,128)(2,1)}, u32[]{:S(2)}) copy-start(bf16[256,128]{1,0:T(8,128)(2,1)} %features_ref.1) | copy-start | bytes 196612
  7.1 2.4 %copy-start.5 = (s32[8,2]{0,1:T(2,128)S(1)}, s32[8,2]{0,1:T(2,128)}, u32[]{:S(2)}) copy-start(s32[8,2]{0,1:T(2,128)} %param.6) | copy-start | bytes 196
  7.1 3.5 %collective-permute-start.3 = (bf16[512,128]{1,0:T(8,128)(2,1)S(1)}, bf16[512,128]{1,0:T(8,128)(2,1)S(1)}, u32[]{:S(2)}, u32[]{:S(2)}) collective-permute-start(bf16[512,128]{1,0:T(8,128)(2,1)S(1)} %shard_map.86._.ends_ref), channel_id=1, source_target_pairs={{0,1},{1,0},{2,3},{3,2},{4,5},{5,4},{6,7},{7,6},{8,9},{9,8},{10,11... | collective-permute-start | bytes 393224 | tf_op jit(solution)/shard_map/ppermute | solution.py:17
  8.2 1.6 %collective-permute-start.5 = (bf16[256,128]{1,0:T(8,128)(2,1)S(1)}, bf16[256,128]{1,0:T(8,128)(2,1)S(1)}, u32[]{:S(2)}, u32[]{:S(2)}) collective-permute-start(bf16[256,128]{1,0:T(8,128)(2,1)S(1)} %collective-permute-done.2.refs_1_), channel_id=1, source_target_pairs={{0,1},{1,0},{2,3},{3,2},{4,5},{5,4},{6,7},{7,6},{8,9},{9,8},{10,11... | collective-permute-start | bytes 196616 | tf_op jit(solution)/shard_map/ppermute | solution.py:17
  9.3 1.3 %collective-permute-start.4 = (bf16[256,128]{1,0:T(8,128)(2,1)S(1)}, bf16[256,128]{1,0:T(8,128)(2,1)S(1)}, u32[]{:S(2)}, u32[]{:S(2)}) collective-permute-start(bf16[256,128]{1,0:T(8,128)(2,1)S(1)} %collective-permute-done.1.refs_0_), channel_id=1, source_target_pairs={{0,1},{1,0},{2,3},{3,2},{4,5},{5,4},{6,7},{7,6},{8,9},{9,8},{10,11... | collective-permute-start | bytes 196616 | tf_op jit(solution)/shard_map/ppermute | solution.py:17
  11.0 6.8 %collective-permute-start.6 = (bf16[256,128]{1,0:T(8,128)(2,1)S(1)}, bf16[256,128]{1,0:T(8,128)(2,1)S(1)}, u32[]{:S(2)}, u32[]{:S(2)}) collective-permute-start(bf16[256,128]{1,0:T(8,128)(2,1)S(1)} %get-tuple-element.32), channel_id=1, source_target_pairs={{0,24},{8,16},{16,8},{24,0},{1,25},{9,17},{17,9},{25,1},{2,26},{10... | collective-permute-start | bytes 196616 | tf_op jit(solution)/shard_map/ppermute | solution.py:17
  14.7 5.1 %collective-permute-start.7 = (bf16[256,128]{1,0:T(8,128)(2,1)S(1)}, bf16[256,128]{1,0:T(8,128)(2,1)S(1)}, u32[]{:S(2)}, u32[]{:S(2)}) collective-permute-start(bf16[256,128]{1,0:T(8,128)(2,1)S(1)} %get-tuple-element.33), channel_id=1, source_target_pairs={{0,8},{8,0},{16,24},{24,16},{1,9},{9,1},{17,25},{25,17},{2,10},{10... | collective-permute-start | bytes 196616 | tf_op jit(solution)/shard_map/ppermute | solution.py:17
  14.7 5.9 %collective-permute-start.8 = (bf16[256,128]{1,0:T(8,128)(2,1)S(1)}, bf16[256,128]{1,0:T(8,128)(2,1)S(1)}, u32[]{:S(2)}, u32[]{:S(2)}) collective-permute-start(bf16[256,128]{1,0:T(8,128)(2,1)S(1)} %get-tuple-element.34), channel_id=1, source_target_pairs={{0,16},{8,24},{16,0},{24,8},{1,17},{9,25},{17,1},{25,9},{2,18},{10... | collective-permute-start | bytes 196616 | tf_op jit(solution)/shard_map/ppermute | solution.py:17
  17.8 7.2 %copy-start = (bf16[1024,128]{1,0:T(8,128)(2,1)S(1)}, bf16[1024,128]{1,0:T(8,128)(2,1)}, u32[]{:S(2)}) copy-start(bf16[1024,128]{1,0:T(8,128)(2,1)} %cotangent_ref.7) | copy-start | bytes 786436
  19.8 5.2 %copy-start.1 = (bf16[128,128]{1,0:T(8,128)(2,1)S(1)}, bf16[128,128]{1,0:T(8,128)(2,1)}, u32[]{:S(2)}) copy-start(bf16[128,128]{1,0:T(8,128)(2,1)} %weight_ref.7) | copy-start | bytes 98308
  20.5 6.3 %collective-permute-start.9 = (bf16[256,128]{1,0:T(8,128)(2,1)S(1)}, bf16[256,128]{1,0:T(8,128)(2,1)S(1)}, u32[]{:S(2)}, u32[]{:S(2)}) collective-permute-start(bf16[256,128]{1,0:T(8,128)(2,1)S(1)} %shard_map.93.refs_0_), channel_id=1, source_target_pairs={{0,24},{8,16},{16,8},{24,0},{1,25},{9,17},{17,9},{25,1},{2,26},{10... | collective-permute-start | bytes 196616 | tf_op jit(solution)/shard_map/ppermute | solution.py:17
  22.8 5.0 %collective-permute-start.10 = (bf16[256,128]{1,0:T(8,128)(2,1)S(1)}, bf16[256,128]{1,0:T(8,128)(2,1)S(1)}, u32[]{:S(2)}, u32[]{:S(2)}) collective-permute-start(bf16[256,128]{1,0:T(8,128)(2,1)S(1)} %shard_map.93.refs_0_), channel_id=1, source_target_pairs={{0,8},{8,0},{16,24},{24,16},{1,9},{9,1},{17,25},{25,17},{2,10},{10... | collective-permute-start | bytes 196616 | tf_op jit(solution)/shard_map/ppermute | solution.py:17
  23.2 5.3 %collective-permute-start.11 = (bf16[256,128]{1,0:T(8,128)(2,1)S(1)}, bf16[256,128]{1,0:T(8,128)(2,1)S(1)}, u32[]{:S(2)}, u32[]{:S(2)}) collective-permute-start(bf16[256,128]{1,0:T(8,128)(2,1)S(1)} %shard_map.93.refs_0_), channel_id=1, source_target_pairs={{0,16},{8,24},{16,0},{24,8},{1,17},{9,25},{17,1},{25,9},{2,18},{10... | collective-permute-start | bytes 196616 | tf_op jit(solution)/shard_map/ppermute | solution.py:17
  25.0 0.7 %copy-start.4 = (f32[128]{0:T(128)S(1)}, f32[128]{0:T(128)}, u32[]{:S(2)}) copy-start(f32[128]{0:T(128)} %param.10) | copy-start | bytes 1540
  29.1 6.3 %collective-permute-start.14 = (bf16[640,128]{1,0:T(8,128)(2,1)S(1)}, bf16[640,128]{1,0:T(8,128)(2,1)S(1)}, u32[]{:S(2)}, u32[]{:S(2)}) collective-permute-start(bf16[640,128]{1,0:T(8,128)(2,1)S(1)} %get-tuple-element.49), channel_id=1, source_target_pairs={{0,6},{1,7},{2,4},{3,5},{4,2},{5,3},{6,0},{7,1},{8,14},{9,15},{10,... | collective-permute-start | bytes 491528 | tf_op jit(solution)/shard_map/ppermute | solution.py:17
  30.6 3.1 %collective-permute-start.13 = (bf16[512,128]{1,0:T(8,128)(2,1)S(1)}, bf16[512,128]{1,0:T(8,128)(2,1)S(1)}, u32[]{:S(2)}, u32[]{:S(2)}) collective-permute-start(bf16[512,128]{1,0:T(8,128)(2,1)S(1)} %get-tuple-element.47), channel_id=1, source_target_pairs={{0,1},{1,0},{2,3},{3,2},{4,5},{5,4},{6,7},{7,6},{8,9},{9,8},{10,11... | collective-permute-start | bytes 393224 | tf_op jit(solution)/shard_map/ppermute | solution.py:17
  30.6 1.5 %collective-permute-start.12 = (bf16[384,128]{1,0:T(8,128)(2,1)S(1)}, bf16[384,128]{1,0:T(8,128)(2,1)S(1)}, u32[]{:S(2)}, u32[]{:S(2)}) collective-permute-start(bf16[384,128]{1,0:T(8,128)(2,1)S(1)} %get-tuple-element.46.sent_ref), channel_id=1, source_target_pairs={{0,1},{1,0},{2,3},{3,2},{4,5},{5,4},{6,7},{7,6},{8,9},{9,8},{10,11... | collective-permute-start | bytes 294920 | tf_op jit(solution)/shard_map/ppermute | solution.py:17
  32.1 5.0 %collective-permute-start.17 = (bf16[384,128]{1,0:T(8,128)(2,1)S(1)}, bf16[384,128]{1,0:T(8,128)(2,1)S(1)}, u32[]{:S(2)}, u32[]{:S(2)}) collective-permute-start(bf16[384,128]{1,0:T(8,128)(2,1)S(1)} %shard_map.99.first_ref.sent_ref), channel_id=1, source_target_pairs={{0,5},{1,4},{2,7},{3,6},{4,1},{5,0},{6,3},{7,2},{8,13},{9,12},{10,... | collective-permute-start | bytes 294920 | tf_op jit(solution)/shard_map/ppermute | solution.py:17
  33.7 4.9 %collective-permute-start.16 = (bf16[384,128]{1,0:T(8,128)(2,1)S(1)}, bf16[384,128]{1,0:T(8,128)(2,1)S(1)}, u32[]{:S(2)}, u32[]{:S(2)}) collective-permute-start(bf16[384,128]{1,0:T(8,128)(2,1)S(1)} %get-tuple-element.50), channel_id=1, source_target_pairs={{0,3},{1,2},{2,1},{3,0},{4,7},{5,6},{6,5},{7,4},{8,11},{9,10},{10,... | collective-permute-start | bytes 294920 | tf_op jit(solution)/shard_map/ppermute | solution.py:17
  35.4 3.2 %collective-permute-start.15 = (bf16[384,128]{1,0:T(8,128)(2,1)S(1)}, bf16[384,128]{1,0:T(8,128)(2,1)S(1)}, u32[]{:S(2)}, u32[]{:S(2)}) collective-permute-start(bf16[384,128]{1,0:T(8,128)(2,1)S(1)} %shard_map.101), channel_id=1, source_target_pairs={{0,1},{1,0},{2,3},{3,2},{4,5},{5,4},{6,7},{7,6},{8,9},{9,8},{10,11... | collective-permute-start | bytes 294920 | tf_op jit(solution)/shard_map/ppermute | solution.py:17

commit v24 on v23

--- a/solution.py
+++ b/solution.py
@@ -203,7 +203,7 @@
     part = rows * size // rep
     params = pltpu.CompilerParams(vmem_limit_bytes=(8 + dom // 2) * 1024 * 1024)
 
-    def call(kernel, out_shape, in_specs, aliases={}):
+    def call(kernel, out_shape, in_specs, aliases={}, cost=0):
         single = not isinstance(out_shape, list)
         return pl.pallas_call(
             kernel,
@@ -212,7 +212,7 @@
             out_specs=VMEM if single else [VMEM] * len(out_shape),
             input_output_aliases=aliases,
             compiler_params=params,
-            cost_estimate=pl.CostEstimate(flops=0, bytes_accessed=0, transcendentals=0),
+            cost_estimate=pl.CostEstimate(flops=cost, bytes_accessed=0, transcendentals=0),
         )
 
     flipped, own, vals = call(
@@ -282,11 +282,12 @@
     message = shape((nodes + width, width), BF16)
     got_across = swap(across, "dom", 2 * last)
     got_beside, got_others = swap(beside, "dom", 1), swap(others, "dom", 1)
-    first = call(first_pair_kernel, message, [VMEM] * 3)(contrib, beside, got_beside)
+    first = call(first_pair_kernel, message, [VMEM] * 3, cost=5 * 10**9)(contrib, beside, got_beside)
     own, *sends = call(
         rest_pair_kernel,
         [shape((nodes, width), F32)] + [message] * (last - 2),
         [VMEM] * 3,
+        cost=10**9,
     )(contrib, first, got_others)
     sends.append(first)
     got = {chip: swap(sends[chip - 1], "dom", 2 * chip + 1) for chip in range(last - 1, 0, -1)}

time: 39.5 us -> 39.9 us (1.010)
  waiting for transfers between devices: 13.4 us -> 13.8 us
  transfers between devices with their start and end apart: 18 -> 18, of which waited for: 14 -> 13; matrix products, arithmetic and copies ran while one was open for 0% -> 0% of each run, Pallas kernels for 7% -> 7%
where the time goes in v24:
time: 39.9 us; the launch traced here: 39.7 us
  starting transfers between devices  18.1 us (45%)
  waiting for transfers between devices  13.8 us (35%)
  Pallas kernels  4.43 us (11%)
  local copies, waits for them, and re-layouts  2.55 us (6%)
  between operations  0.8 us (2%)
    ppermute x18, starting transfers between devices, swap(): return lax.ppermute(value, axis, [(i, i ^ distance) for i in range(size)])  18.1 us
    ppermute x18, waiting for transfers between devices, swap(): return lax.ppermute(value, axis, [(i, i ^ distance) for i in range(size)])  13.8 us
    unnamed x12, local copies, waits for them, and re-layouts  2.55 us
    pallas_call x4, Pallas kernels, body(): call(functools.partial(layer_kernel, rep, count, own_blocks, j), outs, [V...  2.11 us
  transfers between devices with their start and end apart: 18, of which 13 were waited for; matrix products, arithmetic and copies ran while one was open for 0% of the time, Pallas kernels for 7%

profile of v24, /device:TPU:0, one launch (start us, length us, event | category | flops | bytes accessed | tf_op | source)
XLA Modules:
  0.0 39.7 jit_solution(14696211891790624860)
XLA Ops:
  0.6 3.4 %collective-permute-start = (bf16[256,128]{1,0:T(8,128)(2,1)}, bf16[256,128]{1,0:T(8,128)(2,1)S(1)}, u32[]{:S(2)}, u32[]{:S(2)}) collective-permute-start(bf16[256,128]{1,0:T(8,128)(2,1)} %features_ref.1), channel_id=1, source_target_pairs={{0,7},{1,6},{2,5},{3,4},{4,3},{5,2},{6,1},{7,0},{8,15},{9,14},{10,... | collective-permute-start | bytes 196616 | tf_op jit(solution)/shard_map/ppermute | solution.py:17
  4.0 0.8 %collective-permute-start.2 = (bf16[256,128]{1,0:T(8,128)(2,1)}, bf16[256,128]{1,0:T(8,128)(2,1)S(1)}, u32[]{:S(2)}, u32[]{:S(2)}) collective-permute-start(bf16[256,128]{1,0:T(8,128)(2,1)} %features_ref.1), channel_id=1, source_target_pairs={{0,5},{1,4},{2,7},{3,6},{4,1},{5,0},{6,3},{7,2},{8,13},{9,12},{10,... | collective-permute-start | bytes 196616 | tf_op jit(solution)/shard_map/ppermute | solution.py:17
  5.0 1.0 %copy-done.2 = bf16[8,2,128,128]{3,2,1,0:T(8,128)(2,1)S(1)} copy-done((bf16[8,2,128,128]{3,2,1,0:T(8,128)(2,1)S(1)}, bf16[8,2,128,128]{3,2,1,0:T(8,128)(2,1)}, u32[]{:S(2)}) %copy-start.2) | copy-done | bytes 524312
  6.0 0.8 %copy-done.3 = bf16[256,128]{1,0:T(8,128)(2,1)S(1)} copy-done((bf16[256,128]{1,0:T(8,128)(2,1)S(1)}, bf16[256,128]{1,0:T(8,128)(2,1)}, u32[]{:S(2)}) %copy-start.3) | copy-done | bytes 65560
  7.2 1.0 %collective-permute-done.2.refs_1_ = bf16[256,128]{1,0:T(8,128)(2,1)S(1)} collective-permute-done((bf16[256,128]{1,0:T(8,128)(2,1)}, bf16[256,128]{1,0:T(8,128)(2,1)S(1)}, u32[]{:S(2)}, u32[]{:S(2)}) %collective-permute-start.2) | collective-permute-done | bytes 65568 | tf_op jit(solution)/shard_map/ppermute | solution.py:17
  8.2 0.7 %collective-permute-start.5 = (bf16[256,128]{1,0:T(8,128)(2,1)S(1)}, bf16[256,128]{1,0:T(8,128)(2,1)S(1)}, u32[]{:S(2)}, u32[]{:S(2)}) collective-permute-start(bf16[256,128]{1,0:T(8,128)(2,1)S(1)} %collective-permute-done.2.refs_1_), channel_id=1, source_target_pairs={{0,1},{1,0},{2,3},{3,2},{4,5},{5,4},{6,7},{7,6},{8,9},{9,8},{10,11... | collective-permute-start | bytes 196616 | tf_op jit(solution)/shard_map/ppermute | solution.py:17
  9.8 0.8 %collective-permute-done.4.refs_0_ = bf16[256,128]{1,0:T(8,128)(2,1)S(1)} collective-permute-done((bf16[256,128]{1,0:T(8,128)(2,1)S(1)}, bf16[256,128]{1,0:T(8,128)(2,1)S(1)}, u32[]{:S(2)}, u32[]{:S(2)}) %collective-permute-start.4) | collective-permute-done | bytes 65568 | tf_op jit(solution)/shard_map/ppermute | solution.py:17
  11.0 3.7 %collective-permute-start.6 = (bf16[256,128]{1,0:T(8,128)(2,1)S(1)}, bf16[256,128]{1,0:T(8,128)(2,1)S(1)}, u32[]{:S(2)}, u32[]{:S(2)}) collective-permute-start(bf16[256,128]{1,0:T(8,128)(2,1)S(1)} %get-tuple-element.32), channel_id=1, source_target_pairs={{0,24},{8,16},{16,8},{24,0},{1,25},{9,17},{17,9},{25,1},{2,26},{10... | collective-permute-start | bytes 196616 | tf_op jit(solution)/shard_map/ppermute | solution.py:17
  14.7 0.8 %collective-permute-start.8 = (bf16[256,128]{1,0:T(8,128)(2,1)S(1)}, bf16[256,128]{1,0:T(8,128)(2,1)S(1)}, u32[]{:S(2)}, u32[]{:S(2)}) collective-permute-start(bf16[256,128]{1,0:T(8,128)(2,1)S(1)} %get-tuple-element.34), channel_id=1, source_target_pairs={{0,16},{8,24},{16,0},{24,8},{1,17},{9,25},{17,1},{25,9},{2,18},{10... | collective-permute-start | bytes 196616 | tf_op jit(solution)/shard_map/ppermute | solution.py:17
  15.4 2.3 %collective-permute-done.6.b_ref = bf16[256,128]{1,0:T(8,128)(2,1)S(1)} collective-permute-done((bf16[256,128]{1,0:T(8,128)(2,1)S(1)}, bf16[256,128]{1,0:T(8,128)(2,1)S(1)}, u32[]{:S(2)}, u32[]{:S(2)}) %collective-permute-start.6) | collective-permute-done | bytes 65568 | tf_op jit(solution)/shard_map/ppermute | solution.py:17
  17.8 1.9 %collective-permute-done.7.b_ref = bf16[256,128]{1,0:T(8,128)(2,1)S(1)} collective-permute-done((bf16[256,128]{1,0:T(8,128)(2,1)S(1)}, bf16[256,128]{1,0:T(8,128)(2,1)S(1)}, u32[]{:S(2)}, u32[]{:S(2)}) %collective-permute-start.7) | collective-permute-done | bytes 65568 | tf_op jit(solution)/shard_map/ppermute | solution.py:17
  19.8 0.7 %collective-permute-done.8.b_ref = bf16[256,128]{1,0:T(8,128)(2,1)S(1)} collective-permute-done((bf16[256,128]{1,0:T(8,128)(2,1)S(1)}, bf16[256,128]{1,0:T(8,128)(2,1)S(1)}, u32[]{:S(2)}, u32[]{:S(2)}) %collective-permute-start.8) | collective-permute-done | bytes 65568 | tf_op jit(solution)/shard_map/ppermute | solution.py:17
  20.5 2.3 %collective-permute-start.9 = (bf16[256,128]{1,0:T(8,128)(2,1)S(1)}, bf16[256,128]{1,0:T(8,128)(2,1)S(1)}, u32[]{:S(2)}, u32[]{:S(2)}) collective-permute-start(bf16[256,128]{1,0:T(8,128)(2,1)S(1)} %shard_map.93.refs_0_), channel_id=1, source_target_pairs={{0,24},{8,16},{16,8},{24,0},{1,25},{9,17},{17,9},{25,1},{2,26},{10... | collective-permute-start | bytes 196616 | tf_op jit(solution)/shard_map/ppermute | solution.py:17
  23.2 1.8 %collective-permute-start.11 = (bf16[256,128]{1,0:T(8,128)(2,1)S(1)}, bf16[256,128]{1,0:T(8,128)(2,1)S(1)}, u32[]{:S(2)}, u32[]{:S(2)}) collective-permute-start(bf16[256,128]{1,0:T(8,128)(2,1)S(1)} %shard_map.93.refs_0_), channel_id=1, source_target_pairs={{0,16},{8,24},{16,0},{24,8},{1,17},{9,25},{17,1},{25,9},{2,18},{10... | collective-permute-start | bytes 196616 | tf_op jit(solution)/shard_map/ppermute | solution.py:17
  25.0 0.6 %copy-done.4 = f32[128]{0:T(128)S(1)} copy-done((f32[128]{0:T(128)S(1)}, f32[128]{0:T(128)}, u32[]{:S(2)}) %copy-start.4) | copy-done | bytes 536
  26.2 0.7 %collective-permute-done.9.refs_0_ = bf16[256,128]{1,0:T(8,128)(2,1)S(1)} collective-permute-done((bf16[256,128]{1,0:T(8,128)(2,1)S(1)}, bf16[256,128]{1,0:T(8,128)(2,1)S(1)}, u32[]{:S(2)}, u32[]{:S(2)}) %collective-permute-start.9) | collective-permute-done | bytes 65568 | tf_op jit(solution)/shard_map/ppermute | solution.py:17
  27.8 0.5 %shard_map.96 = (bf16[256,128]{1,0:T(8,128)(2,1)S(1)}, f32[16,128,128]{2,1,0:T(8,128)S(1)}, f32[2,128,128]{2,1,0:T(8,128)S(1)}) custom-call(s32[16,128]{1,0:T(8,128)S(1)} %shard_map.87.place_ref, bf16[8,256,128]{2,1,0:T(8,128)(2,1)S(1)} %get-tuple-element.29.flipped_ref, bf16[1024,128]{1,0:T(8,128)(2,1)S(1)} %copy-done, ...), custom_call_target="tpu_custom_call", output_to_operand_aliasing={{1}: (6, {})} | custom-call | tf_op jit(solution)/shard_map/pallas_call | solution.py:272
  28.5 0.6 %shard_map.97 = (bf16[256,128]{1,0:T(8,128)(2,1)S(1)}, f32[16,128,128]{2,1,0:T(8,128)S(1)}, bf16[640,128]{1,0:T(8,128)(2,1)S(1)}, bf16[384,128]{1,0:T(8,128)(2,1)S(1)}, bf16[512,128]{1,0:T(8,128)(2,1)S(1)}) custom-call(s32[16,128]{1,0:T(8,128)S(1)} %shard_map.87.place_ref, ...), custom_call_target="tpu_custom_call", output_to_operand_aliasing={{1}: (6, {})} | custom-call | tf_op jit(solution)/shard_map/pallas_call | solution.py:272
  29.6 1.5 %collective-permute-start.14 = (bf16[640,128]{1,0:T(8,128)(2,1)S(1)}, bf16[640,128]{1,0:T(8,128)(2,1)S(1)}, u32[]{:S(2)}, u32[]{:S(2)}) collective-permute-start(bf16[640,128]{1,0:T(8,128)(2,1)S(1)} %get-tuple-element.49), channel_id=1, source_target_pairs={{0,6},{1,7},{2,4},{3,5},{4,2},{5,3},{6,0},{7,1},{8,14},{9,15},{10,... | collective-permute-start | bytes 491528 | tf_op jit(solution)/shard_map/ppermute | solution.py:17
  31.2 1.0 %collective-permute-start.17 = (bf16[384,128]{1,0:T(8,128)(2,1)S(1)}, bf16[384,128]{1,0:T(8,128)(2,1)S(1)}, u32[]{:S(2)}, u32[]{:S(2)}) collective-permute-start(bf16[384,128]{1,0:T(8,128)(2,1)S(1)} %shard_map.99.first_ref.sent_ref), channel_id=1, source_target_pairs={{0,5},{1,4},{2,7},{3,6},{4,1},{5,0},{6,3},{7,2},{8,13},{9,12},{10,... | collective-permute-start | bytes 294920 | tf_op jit(solution)/shard_map/ppermute | solution.py:17
  32.2 0.8 %collective-permute-start.16 = (bf16[384,128]{1,0:T(8,128)(2,1)S(1)}, bf16[384,128]{1,0:T(8,128)(2,1)S(1)}, u32[]{:S(2)}, u32[]{:S(2)}) collective-permute-start(bf16[384,128]{1,0:T(8,128)(2,1)S(1)} %get-tuple-element.50), channel_id=1, source_target_pairs={{0,3},{1,2},{2,1},{3,0},{4,7},{5,6},{6,5},{7,4},{8,11},{9,10},{10,... | collective-permute-start | bytes 294920 | tf_op jit(solution)/shard_map/ppermute | solution.py:17
  33.0 4.6 %collective-permute-done.14.got_ref.across_ref = bf16[640,128]{1,0:T(8,128)(2,1)S(1)} collective-permute-done((bf16[640,128]{1,0:T(8,128)(2,1)S(1)}, bf16[640,128]{1,0:T(8,128)(2,1)S(1)}, u32[]{:S(2)}, u32[]{:S(2)}) %collective-permute-start.14) | collective-permute-done | bytes 163872 | tf_op jit(solution)/shard_map/ppermute | solution.py:17
  37.7 0.7 %shard_map.98 = bf16[1024,128]{1,0:T(8,128)(2,1)} custom-call(bf16[256,128]{1,0:T(8,128)(2,1)S(1)} %get-tuple-element.35.refs_0_, bf16[256,128]{1,0:T(8,128)(2,1)S(1)} %get-tuple-element.38.refs_1_, bf16[256,128]{1,0:T(8,128)(2,1)S(1)} %get-tuple-element.41.refs_2_, bf16[256,128]{1,0:T(8,128)(2,1)S(1)} %get-tuple-element.44.refs_3_), custom_call_target="tpu_custom_call" | custom-call | tf_op jit(solution)/shard_map/pallas_call | solution.py:295
  39.0 0.7 %shard_map.102 = (f32[256,128]{1,0:T(8,128)}, f32[128,128]{1,0:T(8,128)}) custom-call(f32[256,128]{1,0:T(8,128)S(1)} %get-tuple-element.48.own_ref, bf16[384,128]{1,0:T(8,128)(2,1)S(1)} %shard_map.99.first_ref.sent_ref, bf16[640,128]{1,0:T(8,128)(2,1)S(1)} %collective-permute-done.14.got_ref.across_ref, ...), custom_call_target="tpu_custom_call" | custom-call | tf_op jit(solution)/shard_map/pallas_call | solution.py:298
  (42 shorter events, 4.9 us)
Async XLA Ops:
  0.6 6.4 %collective-permute-start = (bf16[256,128]{1,0:T(8,128)(2,1)}, bf16[256,128]{1,0:T(8,128)(2,1)S(1)}, u32[]{:S(2)}, u32[]{:S(2)}) collective-permute-start(bf16[256,128]{1,0:T(8,128)(2,1)} %features_ref.1), channel_id=1, source_target_pairs={{0,7},{1,6},{2,5},{3,4},{4,3},{5,2},{6,1},{7,0},{8,15},{9,14},{10,... | collective-permute-start | bytes 196616 | tf_op jit(solution)/shard_map/ppermute | solution.py:17
  4.0 4.2 %collective-permute-start.2 = (bf16[256,128]{1,0:T(8,128)(2,1)}, bf16[256,128]{1,0:T(8,128)(2,1)S(1)}, u32[]{:S(2)}, u32[]{:S(2)}) collective-permute-start(bf16[256,128]{1,0:T(8,128)(2,1)} %features_ref.1), channel_id=1, source_target_pairs={{0,5},{1,4},{2,7},{3,6},{4,1},{5,0},{6,3},{7,2},{8,13},{9,12},{10,... | collective-permute-start | bytes 196616 | tf_op jit(solution)/shard_map/ppermute | solution.py:17
  4.8 4.5 %collective-permute-start.1 = (bf16[256,128]{1,0:T(8,128)(2,1)}, bf16[256,128]{1,0:T(8,128)(2,1)S(1)}, u32[]{:S(2)}, u32[]{:S(2)}) collective-permute-start(bf16[256,128]{1,0:T(8,128)(2,1)} %features_ref.1), channel_id=1, source_target_pairs={{0,3},{1,2},{2,1},{3,0},{4,7},{5,6},{6,5},{7,4},{8,11},{9,10},{10,... | collective-permute-start | bytes 196616 | tf_op jit(solution)/shard_map/ppermute | solution.py:17
  5.0 1.0 %copy-start.2 = (bf16[8,2,128,128]{3,2,1,0:T(8,128)(2,1)S(1)}, bf16[8,2,128,128]{3,2,1,0:T(8,128)(2,1)}, u32[]{:S(2)}) copy-start(bf16[8,2,128,128]{3,2,1,0:T(8,128)(2,1)} %vals_ref.1) | copy-start | bytes 1572868
  6.0 0.8 %copy-start.3 = (bf16[256,128]{1,0:T(8,128)(2,1)S(1)}, bf16[256,128]{1,0:T(8,128)(2,1)}, u32[]{:S(2)}) copy-start(bf16[256,128]{1,0:T(8,128)(2,1)} %features_ref.1) | copy-start | bytes 196612
  7.1 2.4 %copy-start.5 = (s32[8,2]{0,1:T(2,128)S(1)}, s32[8,2]{0,1:T(2,128)}, u32[]{:S(2)}) copy-start(s32[8,2]{0,1:T(2,128)} %param.6) | copy-start | bytes 196
  7.1 3.5 %collective-permute-start.3 = (bf16[512,128]{1,0:T(8,128)(2,1)S(1)}, bf16[512,128]{1,0:T(8,128)(2,1)S(1)}, u32[]{:S(2)}, u32[]{:S(2)}) collective-permute-start(bf16[512,128]{1,0:T(8,128)(2,1)S(1)} %shard_map.86._.ends_ref), channel_id=1, source_target_pairs={{0,1},{1,0},{2,3},{3,2},{4,5},{5,4},{6,7},{7,6},{8,9},{9,8},{10,11... | collective-permute-start | bytes 393224 | tf_op jit(solution)/shard_map/ppermute | solution.py:17
  8.2 1.6 %collective-permute-start.5 = (bf16[256,128]{1,0:T(8,128)(2,1)S(1)}, bf16[256,128]{1,0:T(8,128)(2,1)S(1)}, u32[]{:S(2)}, u32[]{:S(2)}) collective-permute-start(bf16[256,128]{1,0:T(8,128)(2,1)S(1)} %collective-permute-done.2.refs_1_), channel_id=1, source_target_pairs={{0,1},{1,0},{2,3},{3,2},{4,5},{5,4},{6,7},{7,6},{8,9},{9,8},{10,11... | collective-permute-start | bytes 196616 | tf_op jit(solution)/shard_map/ppermute | solution.py:17
  9.3 1.3 %collective-permute-start.4 = (bf16[256,128]{1,0:T(8,128)(2,1)S(1)}, bf16[256,128]{1,0:T(8,128)(2,1)S(1)}, u32[]{:S(2)}, u32[]{:S(2)}) collective-permute-start(bf16[256,128]{1,0:T(8,128)(2,1)S(1)} %collective-permute-done.1.refs_0_), channel_id=1, source_target_pairs={{0,1},{1,0},{2,3},{3,2},{4,5},{5,4},{6,7},{7,6},{8,9},{9,8},{10,11... | collective-permute-start | bytes 196616 | tf_op jit(solution)/shard_map/ppermute | solution.py:17
  11.0 6.8 %collective-permute-start.6 = (bf16[256,128]{1,0:T(8,128)(2,1)S(1)}, bf16[256,128]{1,0:T(8,128)(2,1)S(1)}, u32[]{:S(2)}, u32[]{:S(2)}) collective-permute-start(bf16[256,128]{1,0:T(8,128)(2,1)S(1)} %get-tuple-element.32), channel_id=1, source_target_pairs={{0,24},{8,16},{16,8},{24,0},{1,25},{9,17},{17,9},{25,1},{2,26},{10... | collective-permute-start | bytes 196616 | tf_op jit(solution)/shard_map/ppermute | solution.py:17
  14.7 5.1 %collective-permute-start.7 = (bf16[256,128]{1,0:T(8,128)(2,1)S(1)}, bf16[256,128]{1,0:T(8,128)(2,1)S(1)}, u32[]{:S(2)}, u32[]{:S(2)}) collective-permute-start(bf16[256,128]{1,0:T(8,128)(2,1)S(1)} %get-tuple-element.33), channel_id=1, source_target_pairs={{0,8},{8,0},{16,24},{24,16},{1,9},{9,1},{17,25},{25,17},{2,10},{10... | collective-permute-start | bytes 196616 | tf_op jit(solution)/shard_map/ppermute | solution.py:17
  14.7 5.9 %collective-permute-start.8 = (bf16[256,128]{1,0:T(8,128)(2,1)S(1)}, bf16[256,128]{1,0:T(8,128)(2,1)S(1)}, u32[]{:S(2)}, u32[]{:S(2)}) collective-permute-start(bf16[256,128]{1,0:T(8,128)(2,1)S(1)} %get-tuple-element.34), channel_id=1, source_target_pairs={{0,16},{8,24},{16,0},{24,8},{1,17},{9,25},{17,1},{25,9},{2,18},{10... | collective-permute-start | bytes 196616 | tf_op jit(solution)/shard_map/ppermute | solution.py:17
  17.8 7.2 %copy-start = (bf16[1024,128]{1,0:T(8,128)(2,1)S(1)}, bf16[1024,128]{1,0:T(8,128)(2,1)}, u32[]{:S(2)}) copy-start(bf16[1024,128]{1,0:T(8,128)(2,1)} %cotangent_ref.7) | copy-start | bytes 786436
  19.8 5.2 %copy-start.1 = (bf16[128,128]{1,0:T(8,128)(2,1)S(1)}, bf16[128,128]{1,0:T(8,128)(2,1)}, u32[]{:S(2)}) copy-start(bf16[128,128]{1,0:T(8,128)(2,1)} %weight_ref.7) | copy-start | bytes 98308
  20.5 6.3 %collective-permute-start.9 = (bf16[256,128]{1,0:T(8,128)(2,1)S(1)}, bf16[256,128]{1,0:T(8,128)(2,1)S(1)}, u32[]{:S(2)}, u32[]{:S(2)}) collective-permute-start(bf16[256,128]{1,0:T(8,128)(2,1)S(1)} %shard_map.93.refs_0_), channel_id=1, source_target_pairs={{0,24},{8,16},{16,8},{24,0},{1,25},{9,17},{17,9},{25,1},{2,26},{10... | collective-permute-start | bytes 196616 | tf_op jit(solution)/shard_map/ppermute | solution.py:17
  22.8 5.0 %collective-permute-start.10 = (bf16[256,128]{1,0:T(8,128)(2,1)S(1)}, bf16[256,128]{1,0:T(8,128)(2,1)S(1)}, u32[]{:S(2)}, u32[]{:S(2)}) collective-permute-start(bf16[256,128]{1,0:T(8,128)(2,1)S(1)} %shard_map.93.refs_0_), channel_id=1, source_target_pairs={{0,8},{8,0},{16,24},{24,16},{1,9},{9,1},{17,25},{25,17},{2,10},{10... | collective-permute-start | bytes 196616 | tf_op jit(solution)/shard_map/ppermute | solution.py:17
  23.2 5.3 %collective-permute-start.11 = (bf16[256,128]{1,0:T(8,128)(2,1)S(1)}, bf16[256,128]{1,0:T(8,128)(2,1)S(1)}, u32[]{:S(2)}, u32[]{:S(2)}) collective-permute-start(bf16[256,128]{1,0:T(8,128)(2,1)S(1)} %shard_map.93.refs_0_), channel_id=1, source_target_pairs={{0,16},{8,24},{16,0},{24,8},{1,17},{9,25},{17,1},{25,9},{2,18},{10... | collective-permute-start | bytes 196616 | tf_op jit(solution)/shard_map/ppermute | solution.py:17
  25.0 0.7 %copy-start.4 = (f32[128]{0:T(128)S(1)}, f32[128]{0:T(128)}, u32[]{:S(2)}) copy-start(f32[128]{0:T(128)} %param.10) | copy-start | bytes 1540
  29.1 2.1 %collective-permute-start.12 = (bf16[384,128]{1,0:T(8,128)(2,1)S(1)}, bf16[384,128]{1,0:T(8,128)(2,1)S(1)}, u32[]{:S(2)}, u32[]{:S(2)}) collective-permute-start(bf16[384,128]{1,0:T(8,128)(2,1)S(1)} %get-tuple-element.46.sent_ref), channel_id=1, source_target_pairs={{0,1},{1,0},{2,3},{3,2},{4,5},{5,4},{6,7},{7,6},{8,9},{9,8},{10,11... | collective-permute-start | bytes 294920 | tf_op jit(solution)/shard_map/ppermute | solution.py:17
  29.1 3.0 %collective-permute-start.13 = (bf16[512,128]{1,0:T(8,128)(2,1)S(1)}, bf16[512,128]{1,0:T(8,128)(2,1)S(1)}, u32[]{:S(2)}, u32[]{:S(2)}) collective-permute-start(bf16[512,128]{1,0:T(8,128)(2,1)S(1)} %get-tuple-element.47), channel_id=1, source_target_pairs={{0,1},{1,0},{2,3},{3,2},{4,5},{5,4},{6,7},{7,6},{8,9},{9,8},{10,11... | collective-permute-start | bytes 393224 | tf_op jit(solution)/shard_map/ppermute | solution.py:17
  29.6 8.0 %collective-permute-start.14 = (bf16[640,128]{1,0:T(8,128)(2,1)S(1)}, bf16[640,128]{1,0:T(8,128)(2,1)S(1)}, u32[]{:S(2)}, u32[]{:S(2)}) collective-permute-start(bf16[640,128]{1,0:T(8,128)(2,1)S(1)} %get-tuple-element.49), channel_id=1, source_target_pairs={{0,6},{1,7},{2,4},{3,5},{4,2},{5,3},{6,0},{7,1},{8,14},{9,15},{10,... | collective-permute-start | bytes 491528 | tf_op jit(solution)/shard_map/ppermute | solution.py:17
  31.2 7.7 %collective-permute-start.17 = (bf16[384,128]{1,0:T(8,128)(2,1)S(1)}, bf16[384,128]{1,0:T(8,128)(2,1)S(1)}, u32[]{:S(2)}, u32[]{:S(2)}) collective-permute-start(bf16[384,128]{1,0:T(8,128)(2,1)S(1)} %shard_map.99.first_ref.sent_ref), channel_id=1, source_target_pairs={{0,5},{1,4},{2,7},{3,6},{4,1},{5,0},{6,3},{7,2},{8,13},{9,12},{10,... | collective-permute-start | bytes 294920 | tf_op jit(solution)/shard_map/ppermute | solution.py:17
  32.2 6.6 %collective-permute-start.16 = (bf16[384,128]{1,0:T(8,128)(2,1)S(1)}, bf16[384,128]{1,0:T(8,128)(2,1)S(1)}, u32[]{:S(2)}, u32[]{:S(2)}) collective-permute-start(bf16[384,128]{1,0:T(8,128)(2,1)S(1)} %get-tuple-element.50), channel_id=1, source_target_pairs={{0,3},{1,2},{2,1},{3,0},{4,7},{5,6},{6,5},{7,4},{8,11},{9,10},{10,... | collective-permute-start | bytes 294920 | tf_op jit(solution)/shard_map/ppermute | solution.py:17
  37.6 1.4 %collective-permute-start.15 = (bf16[384,128]{1,0:T(8,128)(2,1)S(1)}, bf16[384,128]{1,0:T(8,128)(2,1)S(1)}, u32[]{:S(2)}, u32[]{:S(2)}) collective-permute-start(bf16[384,128]{1,0:T(8,128)(2,1)S(1)} %shard_map.101), channel_id=1, source_target_pairs={{0,1},{1,0},{2,3},{3,2},{4,5},{5,4},{6,7},{7,6},{8,9},{9,8},{10,11... | collective-permute-start | bytes 294920 | tf_op jit(solution)/shard_map/ppermute | solution.py:17
